TPU v7x, 32 devices: a whole 2x2x4 slice. The times are simulated.
32 devices in a mesh: groups: 2 (over y), story: 4 (over z), rec: 2 (over x), blk: 2 (over core).
Axes of the slice: x: 2, y: 2, z: 4, core: 2. Of those that a mesh axis runs over, the one named last changes fastest.
Arguments:
- record_ids: int32 [128], P('groups'), parts along dimension 0, may hold values from 0 to 511
- ground_table: float32 [512], replicated, may hold values from -6 to 6
- mass_int: float32 [8, 2048], P(('groups', 'story'), ('rec', 'blk')), parts along dimension 0, may hold values from 0.5 to 2
- mass_face: float32 [8, 1536], P(('groups', 'story'), ('rec', 'blk')), parts along dimension 0, may hold values from 0.5 to 2
- pattern_int: float32 [8, 2048], P(('groups', 'story'), ('rec', 'blk')), parts along dimension 0, may hold values from -1 to 1
- pattern_face: float32 [8, 1536], P(('groups', 'story'), ('rec', 'blk')), parts along dimension 0, may hold values from -1 to 1
- disp_int: float32 [8, 2048, 64], P(('groups', 'story'), ('rec', 'blk')), parts along dimension 0, may hold values from -4 to 4
- vel_int: float32 [8, 2048, 64], P(('groups', 'story'), ('rec', 'blk')), parts along dimension 0, may hold values from -4 to 4
- acc_int: float32 [8, 2048, 64], P(('groups', 'story'), ('rec', 'blk')), parts along dimension 0, may hold values from -4 to 4
- disp_face: float32 [8, 1536, 64], P(('groups', 'story'), ('rec', 'blk')), parts along dimension 0, may hold values from -4 to 4
- vel_face: float32 [8, 1536, 64], P(('groups', 'story'), ('rec', 'blk')), parts along dimension 0, may hold values from -4 to 4
- acc_face: float32 [8, 1536, 64], P(('groups', 'story'), ('rec', 'blk')), parts along dimension 0, may hold values from -4 to 4
- interior_inverse: float32 [8, 2048, 2048], P(('groups', 'story'), ('rec', 'blk')), parts along dimension 0, may hold values from -0.125 to 0.125
- couple_below: float32 [8, 2048, 1536], P(('groups', 'story'), ('rec', 'blk')), parts along dimension 0, may hold values from -0.125 to 0.125
- couple_above: float32 [8, 2048, 1536], P(('groups', 'story'), ('rec', 'blk')), parts along dimension 0, may hold values from -0.125 to 0.125
- lower: float32 [8, 1536, 1536], P(('groups', 'story'), ('rec', 'blk')), parts along dimension 0, may hold values from -0.122474484 to 0.122474484
- pivot: float32 [8, 1536, 1536], P(('groups', 'story'), ('rec', 'blk')), parts along dimension 0, may hold values from -0.07654656 to 0.07654656
- upper: float32 [8, 1536, 1536], P(('groups', 'story'), ('rec', 'blk')), parts along dimension 0, may hold values from -0.122474484 to 0.122474484
Outputs:
- disp_int_new: float32 [8, 2048, 64], P(('groups', 'story'), ('rec', 'blk')), parts along dimension 0
- vel_int_new: float32 [8, 2048, 64], P(('groups', 'story'), ('rec', 'blk')), parts along dimension 0
- acc_int_new: float32 [8, 2048, 64], P(('groups', 'story'), ('rec', 'blk')), parts along dimension 0
- disp_face_new: float32 [8, 1536, 64], P(('groups', 'story'), ('rec', 'blk')), parts along dimension 0
- vel_face_new: float32 [8, 1536, 64], P(('groups', 'story'), ('rec', 'blk')), parts along dimension 0
- acc_face_new: float32 [8, 1536, 64], P(('groups', 'story'), ('rec', 'blk')), parts along dimension 0
There are 2 independent parts, one for each index of `groups`. A program takes and returns all parts, laid end to end along the dimension named above; an argument that names none is the same for every part. Nothing has to cross between parts.
Inputs may be any that keep to these rules, and one draw needn't show every extreme that they name: `record_ids`: each entry indexes ground_table.
All inputs are finite; a program needn't handle non-finite values.
Results may differ from a plain program's by a relative error of at most 0.0001.
Values sent between devices are 32-bit elements; how exact they have to be, the bound alone decides.
No kernel may reach another device: no remote copies, remote signals or barrier semaphores. Data moves between devices by JAX's collectives and lax.ppermute only.
A program may use at most 64 MiB of HBM per device.

v0:
```python
import jax
import jax.numpy as jnp
from jax import lax
from jax.sharding import PartitionSpec as P


def from_behind(value, axis, steps):
    count = lax.axis_size(axis)
    leading, last = (max(0, -steps), min(count, count - steps))
    return lax.ppermute(value, axis, [(source, source + steps) for source in range(leading, last)])


def product(left, right):
    return jnp.dot(left, right, precision=lax.Precision.HIGHEST, preferred_element_type=jnp.float32)


def contract_rows(left, right):
    return lax.dot_general(
        left,
        right,
        (((0,), (0,)), ((), ())),
        precision=lax.Precision.HIGHEST,
        preferred_element_type=jnp.float32,
    )


def fold_product(matrix_rows):

    def accumulate(total, piece, start):
        return product(matrix_rows, piece)

    return accumulate


def fold_pair(first_rows, second_rows, pieces):
    return product(first_rows, pieces[0]) + product(second_rows, pieces[1])


def newmark_load(mass, pattern, disp, vel, acc, ground):
    return mass[:, None] * (disp + 2.0 * vel + acc - pattern[:, None] * ground[None, :])


def carry_chain(rhs, matrix_rows, upward, blocks):
    stories = lax.axis_size("story")
    here = lax.axis_index("story")
    position = here if upward else stories - 1 - here
    rows, records = rhs.shape
    width = records // blocks
    accumulate = fold_product(matrix_rows)
    empty = jnp.zeros((rows, width), jnp.float32)

    def advance(step, state):
        result, latest = state
        if upward:
            came = from_behind(latest, "story", 1)
            carried = accumulate(
                empty, lax.all_gather(came, ("rec", "blk"), axis=0, tiled=True), jnp.int32(0)
            )
        else:
            came = from_behind(latest, "story", -1)
            carried = accumulate(
                empty, lax.all_gather(came, ("rec", "blk"), axis=0, tiled=True), jnp.int32(0)
            )
        block = step - position
        fresh = rhs - carried
        valid = jnp.logical_and(block >= 0, block < blocks)
        return (jnp.where(valid, fresh, result), fresh)

    start_state = (jnp.zeros((rows, records), jnp.float32), empty)
    result, latest = lax.fori_loop(0, stories + blocks - 1, advance, start_state)
    return result


def shards(
    record_ids,
    ground_table,
    mass_int,
    mass_face,
    pattern_int,
    pattern_face,
    disp_int,
    vel_int,
    acc_int,
    disp_face,
    vel_face,
    acc_face,
    interior_inverse,
    couple_below,
    couple_above,
    lower,
    pivot,
    upper,
):
    library = ground_table.shape[0]
    picked = record_ids[:, None] == jnp.arange(library, dtype=jnp.int32)[None, :]
    ground = jnp.sum(jnp.where(picked, ground_table[None, :], 0.0), axis=1)
    load_int = newmark_load(
        mass_int[0], pattern_int[0], disp_int[0], vel_int[0], acc_int[0], ground
    )
    load_face = newmark_load(
        mass_face[0], pattern_face[0], disp_face[0], vel_face[0], acc_face[0], ground
    )
    inverse_rows = interior_inverse[0]
    below_rows = couple_below[0]
    above_rows = couple_above[0]
    rows_int, records = load_int.shape
    rows_face = load_face.shape[0]
    zeros_int = jnp.zeros((rows_int, records), jnp.float32)
    zeros_face = jnp.zeros((rows_face, records), jnp.float32)
    interior_part = fold_product(inverse_rows)(
        zeros_int, lax.all_gather(load_int, ("rec", "blk"), axis=0, tiled=True), jnp.int32(0)
    )
    partial_below = contract_rows(below_rows, interior_part)
    received = from_behind(partial_below, "story", -1)
    own = contract_rows(above_rows, interior_part)
    condensed = load_face - lax.psum_scatter(
        own + received, ("rec", "blk"), scatter_dimension=0, tiled=True
    )
    blocks = 1
    forward = carry_chain(condensed, lower[0], True, blocks)
    pivoted = fold_product(pivot[0])(
        zeros_face, lax.all_gather(forward, ("rec", "blk"), axis=0, tiled=True), jnp.int32(0)
    )
    face_new = carry_chain(pivoted, upper[0], False, blocks)
    face_below = from_behind(face_new, "story", 1)
    coupled = fold_pair(
        below_rows,
        above_rows,
        (
            lax.all_gather(face_below, ("rec", "blk"), axis=0, tiled=True),
            lax.all_gather(face_new, ("rec", "blk"), axis=0, tiled=True),
        ),
    )
    interior_new = fold_product(inverse_rows)(
        zeros_int,
        lax.all_gather(load_int - coupled, ("rec", "blk"), axis=0, tiled=True),
        jnp.int32(0),
    )
    acc_int_new = interior_new - disp_int[0] - 2.0 * vel_int[0] - acc_int[0]
    acc_face_new = face_new - disp_face[0] - 2.0 * vel_face[0] - acc_face[0]
    vel_int_new = vel_int[0] + acc_int[0] + acc_int_new
    vel_face_new = vel_face[0] + acc_face[0] + acc_face_new
    return (
        interior_new[None],
        vel_int_new[None],
        acc_int_new[None],
        face_new[None],
        vel_face_new[None],
        acc_face_new[None],
    )


def solution(mesh):
    in_specs = (
        P("groups"),
        P(),
        P(("groups", "story"), ("rec", "blk")),
        P(("groups", "story"), ("rec", "blk")),
        P(("groups", "story"), ("rec", "blk")),
        P(("groups", "story"), ("rec", "blk")),
        P(("groups", "story"), ("rec", "blk"), None),
        P(("groups", "story"), ("rec", "blk"), None),
        P(("groups", "story"), ("rec", "blk"), None),
        P(("groups", "story"), ("rec", "blk"), None),
        P(("groups", "story"), ("rec", "blk"), None),
        P(("groups", "story"), ("rec", "blk"), None),
        P(("groups", "story"), ("rec", "blk"), None),
        P(("groups", "story"), ("rec", "blk"), None),
        P(("groups", "story"), ("rec", "blk"), None),
        P(("groups", "story"), ("rec", "blk"), None),
        P(("groups", "story"), ("rec", "blk"), None),
        P(("groups", "story"), ("rec", "blk"), None),
    )
    out_specs = (
        P(("groups", "story"), ("rec", "blk"), None),
        P(("groups", "story"), ("rec", "blk"), None),
        P(("groups", "story"), ("rec", "blk"), None),
        P(("groups", "story"), ("rec", "blk"), None),
        P(("groups", "story"), ("rec", "blk"), None),
        P(("groups", "story"), ("rec", "blk"), None),
    )
    return jax.shard_map(shards, mesh=mesh, in_specs=in_specs, out_specs=out_specs, check_vma=False)
```

profile of v0, /device:TPU:0, one launch (start us, length us, event | category | flops | bytes accessed | tf_op | source)
XLA Modules:
  0.0 265.0 jit_solution(9781131658559824964)
XLA Ops:
  9.5 8.6 %all_gather.29 = f32[2048,64]{0,1:T(8,128)S(1)} all-gather(f32[512,64]{0,1:T(8,128)S(1)} %fusion.38), channel_id=1, replica_groups=mesh['groups'=2,'story'=4,'rec'=2,'blk'=2] {'rec','blk'}, dimensions={0}, use_global_device_ids=true | all-gather | bytes 655360 | tf_op jit(solution)/shard_map/all_gather | solution.py:111
  18.1 6.3 %fusion.2 = f32[64,512]{1,0:T(8,128)S(1)} fusion(f32[2048,64]{0,1:T(8,128)S(1)} %all_gather.29, f32[1,512,2048]{2,1,0:T(8,128)} %param.34), kind=kOutput, calls=%fused_computation.8 | convolution fusion | flops 805306368 | bytes 4849664 | tf_op jit(solution)/shard_map/dot_general | solution.py:14
  24.4 2.0 fusion.20
  27.8 12.0 %collective-permute-done.2 = f32[1536,64]{0,1:T(8,128)S(1)} collective-permute-done((f32[1536,64]{0,1:T(8,128)S(1)}, f32[1536,64]{0,1:T(8,128)S(1)}, u32[]{:S(2)}, u32[]{:S(2)}) %collective-permute-start.2) | collective-permute-done | bytes 393248 | tf_op jit(solution)/shard_map/ppermute | solution.py:10
  39.7 2.8 %fusion.17 = f32[1536,64]{0,1:T(8,128)} fusion(f32[1536,64]{0,1:T(8,128)S(1)} %collective-permute-done.2, f32[64,512]{1,0:T(8,128)S(1)} %fusion.2, f32[1,512,1536]{2,1,0:T(8,128)S(1)} %copy-done), kind=kOutput, calls=%fused_computation.21 | convolution fusion | flops 604078080 | bytes 4063232 | tf_op jit(solution)/shard_map/dot_general | solution.py:18
  42.6 20.7 %reduce-scatter.2.cloned.1.call-done = f32[384,64]{0,1:T(8,128)} async-done(((f32[1536,64]{0,1:T(8,128)}), f32[384,64]{0,1:T(8,128)}) %reduce-scatter.2.cloned.1.call-update) | async-done | bytes 98320 | tf_op jit(solution)/shard_map/reduce_scatter | solution.py:116
  64.4 77.0 %while.32 = (s32[]{:T(128)}, f32[384,64]{0,1:T(8,128)S(1)}, f32[384,64]{0,1:T(8,128)}, s32[]{:T(128)}, f32[384,1536]{1,0:T(8,128)}, /*index=5*/f32[384,64]{0,1:T(8,128)S(1)}, s32[]{:T(128)}, s32[]{:T(128)}) while((s32[]{:T(128)}, f32[384,64]{0,1:T(8,128)S(1)}, f32[384,64]{0,1:T(8,128)}, s32[]{:T(128)}, f32[384,1536]{1,0:T(8,128)}, ...), condition=%wide.region_3.4_spmd.clone, body=%wide.region_2.3_spmd.clone.sunk | while | flops 453083136 | bytes 4227242 | solution.py:70
  65.1 4.0 %collective-permute-start = (f32[384,64]{0,1:T(8,128)}, f32[384,64]{0,1:T(8,128)}, u32[]{:S(2)}, u32[]{:S(2)}) collective-permute-start(f32[384,64]{0,1:T(8,128)} %broadcast_select_fusion.4), channel_id=1, source_target_pairs={{0,4},{4,8},{8,12},{1,5},{5,9},{9,13},{2,6},{6,10},{10,14},{3,7},{... | collective-permute-start | bytes 294920 | tf_op jit(solution)/shard_map/while/body/eval_jaxpr/ppermute | solution.py:10
  69.2 1.9 collective-permute-done
  71.0 6.3 %all_gather.38 = f32[1536,64]{0,1:T(8,128)S(1)} all-gather(f32[384,64]{0,1:T(8,128)} %collective-permute-done), channel_id=1, replica_groups=mesh['groups'=2,'story'=4,'rec'=2,'blk'=2] {'rec','blk'}, dimensions={0}, use_global_device_ids=true | all-gather | bytes 491520 | tf_op jit(solution)/shard_map/while/body/eval_jaxpr/all_gather | solution.py:57
  77.4 4.7 %select_select_fusion.4 = (f32[384,64]{0,1:T(8,128)S(1)}, f32[384,64]{0,1:T(8,128)}) fusion(f32[384,64]{0,1:T(8,128)S(1)} %get-tuple-element.391, pred[]{:T(512)S(6)} %compare.6, pred[]{:T(512)S(6)} %and.19, f32[384,64]{0,1:T(8,128)S(1)} %get-tuple-element.403, f32[384,1536]{1,0:T(8,128)} %get-tuple-element.402, f32[1536,64]{0,1:T(8,128)S(1)} %all_gather.38), kind=kOutput, calls=%fused_computation.1.clone.1 | convolution fusion | flops 453058560 | bytes 3145730 | tf_op jit(solution)/shard_map/while/body/eval_jaxpr/dot_general | solution.py:14
  82.1 1.5 broadcast_select_fusion.4
  83.6 4.9 %collective-permute-start = (f32[384,64]{0,1:T(8,128)}, f32[384,64]{0,1:T(8,128)}, u32[]{:S(2)}, u32[]{:S(2)}) collective-permute-start(f32[384,64]{0,1:T(8,128)} %broadcast_select_fusion.4), channel_id=1, source_target_pairs={{0,4},{4,8},{8,12},{1,5},{5,9},{9,13},{2,6},{6,10},{10,14},{3,7},{... | collective-permute-start | bytes 294920 | tf_op jit(solution)/shard_map/while/body/eval_jaxpr/ppermute | solution.py:10
  88.5 2.2 collective-permute-done
  90.8 6.3 %all_gather.38 = f32[1536,64]{0,1:T(8,128)S(1)} all-gather(f32[384,64]{0,1:T(8,128)} %collective-permute-done), channel_id=1, replica_groups=mesh['groups'=2,'story'=4,'rec'=2,'blk'=2] {'rec','blk'}, dimensions={0}, use_global_device_ids=true | all-gather | bytes 491520 | tf_op jit(solution)/shard_map/while/body/eval_jaxpr/all_gather | solution.py:57
  97.1 4.7 %select_select_fusion.4 = (f32[384,64]{0,1:T(8,128)S(1)}, f32[384,64]{0,1:T(8,128)}) fusion(f32[384,64]{0,1:T(8,128)S(1)} %get-tuple-element.391, pred[]{:T(512)S(6)} %compare.6, pred[]{:T(512)S(6)} %and.19, f32[384,64]{0,1:T(8,128)S(1)} %get-tuple-element.403, f32[384,1536]{1,0:T(8,128)} %get-tuple-element.402, f32[1536,64]{0,1:T(8,128)S(1)} %all_gather.38), kind=kOutput, calls=%fused_computation.1.clone.1 | convolution fusion | flops 453058560 | bytes 3145730 | tf_op jit(solution)/shard_map/while/body/eval_jaxpr/dot_general | solution.py:14
  101.8 1.5 broadcast_select_fusion.4
  103.3 5.0 %collective-permute-start = (f32[384,64]{0,1:T(8,128)}, f32[384,64]{0,1:T(8,128)}, u32[]{:S(2)}, u32[]{:S(2)}) collective-permute-start(f32[384,64]{0,1:T(8,128)} %broadcast_select_fusion.4), channel_id=1, source_target_pairs={{0,4},{4,8},{8,12},{1,5},{5,9},{9,13},{2,6},{6,10},{10,14},{3,7},{... | collective-permute-start | bytes 294920 | tf_op jit(solution)/shard_map/while/body/eval_jaxpr/ppermute | solution.py:10
  108.4 2.2 collective-permute-done
  110.6 6.3 %all_gather.38 = f32[1536,64]{0,1:T(8,128)S(1)} all-gather(f32[384,64]{0,1:T(8,128)} %collective-permute-done), channel_id=1, replica_groups=mesh['groups'=2,'story'=4,'rec'=2,'blk'=2] {'rec','blk'}, dimensions={0}, use_global_device_ids=true | all-gather | bytes 491520 | tf_op jit(solution)/shard_map/while/body/eval_jaxpr/all_gather | solution.py:57
  116.9 4.7 %select_select_fusion.4 = (f32[384,64]{0,1:T(8,128)S(1)}, f32[384,64]{0,1:T(8,128)}) fusion(f32[384,64]{0,1:T(8,128)S(1)} %get-tuple-element.391, pred[]{:T(512)S(6)} %compare.6, pred[]{:T(512)S(6)} %and.19, f32[384,64]{0,1:T(8,128)S(1)} %get-tuple-element.403, f32[384,1536]{1,0:T(8,128)} %get-tuple-element.402, f32[1536,64]{0,1:T(8,128)S(1)} %all_gather.38), kind=kOutput, calls=%fused_computation.1.clone.1 | convolution fusion | flops 453058560 | bytes 3145730 | tf_op jit(solution)/shard_map/while/body/eval_jaxpr/dot_general | solution.py:14
  121.6 1.5 broadcast_select_fusion.4
  123.1 5.0 %collective-permute-start = (f32[384,64]{0,1:T(8,128)}, f32[384,64]{0,1:T(8,128)}, u32[]{:S(2)}, u32[]{:S(2)}) collective-permute-start(f32[384,64]{0,1:T(8,128)} %broadcast_select_fusion.4), channel_id=1, source_target_pairs={{0,4},{4,8},{8,12},{1,5},{5,9},{9,13},{2,6},{6,10},{10,14},{3,7},{... | collective-permute-start | bytes 294920 | tf_op jit(solution)/shard_map/while/body/eval_jaxpr/ppermute | solution.py:10
  128.2 2.2 collective-permute-done
  130.4 6.3 %all_gather.38 = f32[1536,64]{0,1:T(8,128)S(1)} all-gather(f32[384,64]{0,1:T(8,128)} %collective-permute-done), channel_id=1, replica_groups=mesh['groups'=2,'story'=4,'rec'=2,'blk'=2] {'rec','blk'}, dimensions={0}, use_global_device_ids=true | all-gather | bytes 491520 | tf_op jit(solution)/shard_map/while/body/eval_jaxpr/all_gather | solution.py:57
  136.7 4.7 %select_select_fusion.4 = (f32[384,64]{0,1:T(8,128)S(1)}, f32[384,64]{0,1:T(8,128)}) fusion(f32[384,64]{0,1:T(8,128)S(1)} %get-tuple-element.391, pred[]{:T(512)S(6)} %compare.6, pred[]{:T(512)S(6)} %and.19, f32[384,64]{0,1:T(8,128)S(1)} %get-tuple-element.403, f32[384,1536]{1,0:T(8,128)} %get-tuple-element.402, f32[1536,64]{0,1:T(8,128)S(1)} %all_gather.38), kind=kOutput, calls=%fused_computation.1.clone.1 | convolution fusion | flops 453058560 | bytes 3145730 | tf_op jit(solution)/shard_map/while/body/eval_jaxpr/dot_general | solution.py:14
  141.4 6.7 %all_gather.30 = f32[1536,64]{0,1:T(8,128)S(1)} all-gather(f32[384,64]{0,1:T(8,128)S(1)} %get-tuple-element.224), channel_id=1, replica_groups=mesh['groups'=2,'story'=4,'rec'=2,'blk'=2] {'rec','blk'}, dimensions={0}, use_global_device_ids=true | all-gather | bytes 491520 | tf_op jit(solution)/shard_map/all_gather | solution.py:122
  148.2 4.0 %fusion.32 = f32[384,64]{0,1:T(8,128)S(1)} fusion(f32[1536,64]{0,1:T(8,128)S(1)} %all_gather.30, f32[1,384,1536]{2,1,0:T(8,128)} %param.38), kind=kOutput, calls=%fused_computation.26 | convolution fusion | flops 452984832 | bytes 2850816 | tf_op jit(solution)/shard_map/dot_general | solution.py:14
  152.2 69.4 %while.33 = (s32[]{:T(128)}, f32[384,64]{0,1:T(8,128)S(1)}, f32[384,64]{0,1:T(8,128)S(1)}, s32[]{:T(128)}, f32[384,1536]{1,0:T(8,128)}, /*index=5*/f32[384,64]{0,1:T(8,128)S(1)}, s32[]{:T(128)}, s32[]{:T(128)}) while((s32[]{:T(128)}, f32[384,64]{0,1:T(8,128)S(1)}, f32[384,64]{0,1:T(8,128)S(1)}, s32[]{:T(128)}, ...), condition=%wide.region_5.6_spmd.clone, body=%wide.region_4.5_spmd.clone.sunk | while | flops 453083136 | bytes 4227242 | solution.py:70
  153.5 6.4 %collective-permute-done.1 = f32[384,64]{0,1:T(8,128)S(1)} collective-permute-done((f32[384,64]{0,1:T(8,128)S(1)}, f32[384,64]{0,1:T(8,128)S(1)}, u32[]{:S(2)}, u32[]{:S(2)}) %collective-permute-start.1) | collective-permute-done | bytes 98336 | tf_op jit(solution)/shard_map/while/body/eval_jaxpr/ppermute | solution.py:10
  159.9 6.1 %all_gather.39 = f32[1536,64]{0,1:T(8,128)S(1)} all-gather(f32[384,64]{0,1:T(8,128)S(1)} %collective-permute-done.1), channel_id=1, replica_groups=mesh['groups'=2,'story'=4,'rec'=2,'blk'=2] {'rec','blk'}, dimensions={0}, use_global_device_ids=true | all-gather | bytes 491520 | tf_op jit(solution)/shard_map/while/body/eval_jaxpr/all_gather | solution.py:62
  166.0 4.0 %select_select_fusion.5 = (f32[384,64]{0,1:T(8,128)S(1)}, f32[384,64]{0,1:T(8,128)S(1)}) fusion(f32[384,64]{0,1:T(8,128)S(1)} %get-tuple-element.415, pred[]{:T(512)S(6)} %compare.7, pred[]{:T(512)S(6)} %and.20, f32[384,64]{0,1:T(8,128)S(1)} %get-tuple-element.427, f32[384,1536]{1,0:T(8,128)} %get-tuple-element.426, f32[1536,64]{0,1:T(8,128)S(1)} %all_gather.39), kind=kOutput, calls=%fused_computation.4.clone.1 | convolution fusion | flops 453058560 | bytes 3145730 | tf_op jit(solution)/shard_map/while/body/eval_jaxpr/dot_general | solution.py:14
  171.4 5.6 %collective-permute-done.1 = f32[384,64]{0,1:T(8,128)S(1)} collective-permute-done((f32[384,64]{0,1:T(8,128)S(1)}, f32[384,64]{0,1:T(8,128)S(1)}, u32[]{:S(2)}, u32[]{:S(2)}) %collective-permute-start.1) | collective-permute-done | bytes 98336 | tf_op jit(solution)/shard_map/while/body/eval_jaxpr/ppermute | solution.py:10
  177.0 6.1 %all_gather.39 = f32[1536,64]{0,1:T(8,128)S(1)} all-gather(f32[384,64]{0,1:T(8,128)S(1)} %collective-permute-done.1), channel_id=1, replica_groups=mesh['groups'=2,'story'=4,'rec'=2,'blk'=2] {'rec','blk'}, dimensions={0}, use_global_device_ids=true | all-gather | bytes 491520 | tf_op jit(solution)/shard_map/while/body/eval_jaxpr/all_gather | solution.py:62
  183.2 4.0 %select_select_fusion.5 = (f32[384,64]{0,1:T(8,128)S(1)}, f32[384,64]{0,1:T(8,128)S(1)}) fusion(f32[384,64]{0,1:T(8,128)S(1)} %get-tuple-element.415, pred[]{:T(512)S(6)} %compare.7, pred[]{:T(512)S(6)} %and.20, f32[384,64]{0,1:T(8,128)S(1)} %get-tuple-element.427, f32[384,1536]{1,0:T(8,128)} %get-tuple-element.426, f32[1536,64]{0,1:T(8,128)S(1)} %all_gather.39), kind=kOutput, calls=%fused_computation.4.clone.1 | convolution fusion | flops 453058560 | bytes 3145730 | tf_op jit(solution)/shard_map/while/body/eval_jaxpr/dot_general | solution.py:14
  188.6 5.6 %collective-permute-done.1 = f32[384,64]{0,1:T(8,128)S(1)} collective-permute-done((f32[384,64]{0,1:T(8,128)S(1)}, f32[384,64]{0,1:T(8,128)S(1)}, u32[]{:S(2)}, u32[]{:S(2)}) %collective-permute-start.1) | collective-permute-done | bytes 98336 | tf_op jit(solution)/shard_map/while/body/eval_jaxpr/ppermute | solution.py:10
  194.2 6.1 %all_gather.39 = f32[1536,64]{0,1:T(8,128)S(1)} all-gather(f32[384,64]{0,1:T(8,128)S(1)} %collective-permute-done.1), channel_id=1, replica_groups=mesh['groups'=2,'story'=4,'rec'=2,'blk'=2] {'rec','blk'}, dimensions={0}, use_global_device_ids=true | all-gather | bytes 491520 | tf_op jit(solution)/shard_map/while/body/eval_jaxpr/all_gather | solution.py:62
  200.3 4.0 %select_select_fusion.5 = (f32[384,64]{0,1:T(8,128)S(1)}, f32[384,64]{0,1:T(8,128)S(1)}) fusion(f32[384,64]{0,1:T(8,128)S(1)} %get-tuple-element.415, pred[]{:T(512)S(6)} %compare.7, pred[]{:T(512)S(6)} %and.20, f32[384,64]{0,1:T(8,128)S(1)} %get-tuple-element.427, f32[384,1536]{1,0:T(8,128)} %get-tuple-element.426, f32[1536,64]{0,1:T(8,128)S(1)} %all_gather.39), kind=kOutput, calls=%fused_computation.4.clone.1 | convolution fusion | flops 453058560 | bytes 3145730 | tf_op jit(solution)/shard_map/while/body/eval_jaxpr/dot_general | solution.py:14
  205.7 5.6 %collective-permute-done.1 = f32[384,64]{0,1:T(8,128)S(1)} collective-permute-done((f32[384,64]{0,1:T(8,128)S(1)}, f32[384,64]{0,1:T(8,128)S(1)}, u32[]{:S(2)}, u32[]{:S(2)}) %collective-permute-start.1) | collective-permute-done | bytes 98336 | tf_op jit(solution)/shard_map/while/body/eval_jaxpr/ppermute | solution.py:10
  211.4 6.1 %all_gather.39 = f32[1536,64]{0,1:T(8,128)S(1)} all-gather(f32[384,64]{0,1:T(8,128)S(1)} %collective-permute-done.1), channel_id=1, replica_groups=mesh['groups'=2,'story'=4,'rec'=2,'blk'=2] {'rec','blk'}, dimensions={0}, use_global_device_ids=true | all-gather | bytes 491520 | tf_op jit(solution)/shard_map/while/body/eval_jaxpr/all_gather | solution.py:62
  217.5 4.0 %select_select_fusion.5 = (f32[384,64]{0,1:T(8,128)S(1)}, f32[384,64]{0,1:T(8,128)S(1)}) fusion(f32[384,64]{0,1:T(8,128)S(1)} %get-tuple-element.415, pred[]{:T(512)S(6)} %compare.7, pred[]{:T(512)S(6)} %and.20, f32[384,64]{0,1:T(8,128)S(1)} %get-tuple-element.427, f32[384,1536]{1,0:T(8,128)} %get-tuple-element.426, f32[1536,64]{0,1:T(8,128)S(1)} %all_gather.39), kind=kOutput, calls=%fused_computation.4.clone.1 | convolution fusion | flops 453058560 | bytes 3145730 | tf_op jit(solution)/shard_map/while/body/eval_jaxpr/dot_general | solution.py:14
  221.6 6.7 %all_gather.32 = f32[1536,64]{0,1:T(8,128)S(1)} all-gather(f32[384,64]{0,1:T(8,128)S(1)} %get-tuple-element.225), channel_id=1, replica_groups=mesh['groups'=2,'story'=4,'rec'=2,'blk'=2] {'rec','blk'}, dimensions={0}, use_global_device_ids=true | all-gather | bytes 491520 | tf_op jit(solution)/shard_map/all_gather | solution.py:131
  228.3 3.6 %collective-permute-start.3 = (f32[384,64]{0,1:T(8,128)S(1)}, f32[384,64]{0,1:T(8,128)S(1)}, u32[]{:S(2)}, u32[]{:S(2)}) collective-permute-start(f32[384,64]{0,1:T(8,128)S(1)} %get-tuple-element.225), channel_id=1, source_target_pairs={{0,4},{4,8},{8,12},{1,5},{5,9},{9,13},{2,6},{6,10},{10,14},{3,7},{... | collective-permute-start | bytes 294920 | tf_op jit(solution)/shard_map/ppermute | solution.py:10
  232.0 3.1 %fusion.8 = f32[64,512]{1,0:T(8,128)S(1)} fusion(f32[1536,64]{0,1:T(8,128)S(1)} %all_gather.32, f32[1,512,1536]{2,1,0:T(8,128)S(1)} %copy-done), kind=kOutput, calls=%fused_computation.14 | convolution fusion | flops 603979776 | bytes 3670016 | tf_op jit(solution)/shard_map/dot_general | solution.py:14
  235.9 6.4 %all_gather.31 = f32[1536,64]{0,1:T(8,128)S(1)} all-gather(f32[384,64]{0,1:T(8,128)S(1)} %collective-permute-done.3), channel_id=1, replica_groups=mesh['groups'=2,'story'=4,'rec'=2,'blk'=2] {'rec','blk'}, dimensions={0}, use_global_device_ids=true | all-gather | bytes 491520 | tf_op jit(solution)/shard_map/all_gather | solution.py:130
  242.3 3.2 %fusion.29 = f32[512,64]{0,1:T(8,128)S(1)} fusion(f32[512,64]{0,1:T(8,128)S(1)} %copy-done.6, f32[64,512]{1,0:T(8,128)S(1)} %fusion.8, f32[1536,64]{0,1:T(8,128)S(1)} %all_gather.31, f32[1,512,1536]{2,1,0:T(8,128)S(1)} %copy-done.3), kind=kOutput, calls=%fused_computation.25 | convolution fusion | flops 604045312 | bytes 3932160 | tf_op jit(solution)/shard_map/dot_general | solution.py:14
  245.5 7.6 %all_gather.33 = f32[2048,64]{0,1:T(8,128)S(1)} all-gather(f32[512,64]{0,1:T(8,128)S(1)} %fusion.29), channel_id=1, replica_groups=mesh['groups'=2,'story'=4,'rec'=2,'blk'=2] {'rec','blk'}, dimensions={0}, use_global_device_ids=true | all-gather | bytes 655360 | tf_op jit(solution)/shard_map/all_gather | solution.py:136
  253.1 4.2 %fusion = f32[64,512]{1,0:T(8,128)S(1)} fusion(f32[2048,64]{0,1:T(8,128)S(1)} %all_gather.33, f32[1,512,2048]{2,1,0:T(8,128)S(1)} %copy-done.1), kind=kOutput, calls=%fused_computation.6 | convolution fusion | flops 805306368 | bytes 4849664 | tf_op jit(solution)/shard_map/dot_general | solution.py:14
  (56 shorter events, 12.2 us)
Async XLA Ops:
  7.2 32.6 %copy-start = (f32[1,512,1536]{2,1,0:T(8,128)S(1)}, f32[1,512,1536]{2,1,0:T(8,128)}, u32[]{:S(2)}) copy-start(f32[1,512,1536]{2,1,0:T(8,128)} %param.36) | copy-start | bytes 9437188
  7.2 56.1 %reduce-scatter.2.cloned.1.call-start = ((), (), s32[]{:S(2)}) async-start(), calls=%async_computation.1 | async-start | bytes 491520 | tf_op jit(solution)/shard_map/reduce_scatter | solution.py:116
  7.2 17.2 %copy-start.2 = (f32[1,512,1536]{2,1,0:T(8,128)S(1)}, f32[1,512,1536]{2,1,0:T(8,128)}, u32[]{:S(2)}) copy-start(f32[1,512,1536]{2,1,0:T(8,128)} %param.35) | copy-start | bytes 9437188
  9.5 16.9 %copy-start.5 = (f32[512,64]{0,1:T(8,128)}, f32[512,64]{0,1:T(8,128)S(1)}, u32[]{:S(2)}) copy-start(f32[512,64]{0,1:T(8,128)S(1)} %fusion.38) | copy-start | bytes 393220
  26.4 16.1 %copy-start.14 = (f32[1,384]{1,0:T(1,128)S(1)}, f32[1,384]{1,0:T(1,128)}, u32[]{:S(2)}) copy-start(f32[1,384]{1,0:T(1,128)} %param.25) | copy-start | bytes 4612
  26.4 16.1 %copy-start.15 = (f32[1,384]{1,0:T(1,128)S(1)}, f32[1,384]{1,0:T(1,128)}, u32[]{:S(2)}) copy-start(f32[1,384]{1,0:T(1,128)} %param.27) | copy-start | bytes 4612
  26.5 13.3 %collective-permute-start.2 = (f32[1536,64]{0,1:T(8,128)S(1)}, f32[1536,64]{0,1:T(8,128)S(1)}, u32[]{:S(2)}, u32[]{:S(2)}) collective-permute-start(f32[1536,64]{0,1:T(8,128)S(1)} %fusion.20), channel_id=1, source_target_pairs={{4,0},{8,4},{12,8},{5,1},{9,5},{13,9},{6,2},{10,6},{14,10},{7,3},{... | collective-permute-start | bytes 1179656 | tf_op jit(solution)/shard_map/ppermute | solution.py:10
  65.1 5.9 %collective-permute-start = (f32[384,64]{0,1:T(8,128)}, f32[384,64]{0,1:T(8,128)}, u32[]{:S(2)}, u32[]{:S(2)}) collective-permute-start(f32[384,64]{0,1:T(8,128)} %broadcast_select_fusion.4), channel_id=1, source_target_pairs={{0,4},{4,8},{8,12},{1,5},{5,9},{9,13},{2,6},{6,10},{10,14},{3,7},{... | collective-permute-start | bytes 294920 | tf_op jit(solution)/shard_map/while/body/eval_jaxpr/ppermute | solution.py:10
  83.6 7.2 %collective-permute-start = (f32[384,64]{0,1:T(8,128)}, f32[384,64]{0,1:T(8,128)}, u32[]{:S(2)}, u32[]{:S(2)}) collective-permute-start(f32[384,64]{0,1:T(8,128)} %broadcast_select_fusion.4), channel_id=1, source_target_pairs={{0,4},{4,8},{8,12},{1,5},{5,9},{9,13},{2,6},{6,10},{10,14},{3,7},{... | collective-permute-start | bytes 294920 | tf_op jit(solution)/shard_map/while/body/eval_jaxpr/ppermute | solution.py:10
  103.3 7.2 %collective-permute-start = (f32[384,64]{0,1:T(8,128)}, f32[384,64]{0,1:T(8,128)}, u32[]{:S(2)}, u32[]{:S(2)}) collective-permute-start(f32[384,64]{0,1:T(8,128)} %broadcast_select_fusion.4), channel_id=1, source_target_pairs={{0,4},{4,8},{8,12},{1,5},{5,9},{9,13},{2,6},{6,10},{10,14},{3,7},{... | collective-permute-start | bytes 294920 | tf_op jit(solution)/shard_map/while/body/eval_jaxpr/ppermute | solution.py:10
  123.1 7.2 %collective-permute-start = (f32[384,64]{0,1:T(8,128)}, f32[384,64]{0,1:T(8,128)}, u32[]{:S(2)}, u32[]{:S(2)}) collective-permute-start(f32[384,64]{0,1:T(8,128)} %broadcast_select_fusion.4), channel_id=1, source_target_pairs={{0,4},{4,8},{8,12},{1,5},{5,9},{9,13},{2,6},{6,10},{10,14},{3,7},{... | collective-permute-start | bytes 294920 | tf_op jit(solution)/shard_map/while/body/eval_jaxpr/ppermute | solution.py:10
  152.2 7.7 %collective-permute-start.1 = (f32[384,64]{0,1:T(8,128)S(1)}, f32[384,64]{0,1:T(8,128)S(1)}, u32[]{:S(2)}, u32[]{:S(2)}) collective-permute-start(f32[384,64]{0,1:T(8,128)S(1)} %broadcast_select_fusion.5), channel_id=1, source_target_pairs={{4,0},{8,4},{12,8},{5,1},{9,5},{13,9},{6,2},{10,6},{14,10},{7,3},{... | collective-permute-start | bytes 294920 | tf_op jit(solution)/shard_map/while/body/eval_jaxpr/ppermute | solution.py:10
  170.1 6.9 %collective-permute-start.1 = (f32[384,64]{0,1:T(8,128)S(1)}, f32[384,64]{0,1:T(8,128)S(1)}, u32[]{:S(2)}, u32[]{:S(2)}) collective-permute-start(f32[384,64]{0,1:T(8,128)S(1)} %broadcast_select_fusion.5), channel_id=1, source_target_pairs={{4,0},{8,4},{12,8},{5,1},{9,5},{13,9},{6,2},{10,6},{14,10},{7,3},{... | collective-permute-start | bytes 294920 | tf_op jit(solution)/shard_map/while/body/eval_jaxpr/ppermute | solution.py:10
  187.3 6.9 %collective-permute-start.1 = (f32[384,64]{0,1:T(8,128)S(1)}, f32[384,64]{0,1:T(8,128)S(1)}, u32[]{:S(2)}, u32[]{:S(2)}) collective-permute-start(f32[384,64]{0,1:T(8,128)S(1)} %broadcast_select_fusion.5), channel_id=1, source_target_pairs={{4,0},{8,4},{12,8},{5,1},{9,5},{13,9},{6,2},{10,6},{14,10},{7,3},{... | collective-permute-start | bytes 294920 | tf_op jit(solution)/shard_map/while/body/eval_jaxpr/ppermute | solution.py:10
  204.4 6.9 %collective-permute-start.1 = (f32[384,64]{0,1:T(8,128)S(1)}, f32[384,64]{0,1:T(8,128)S(1)}, u32[]{:S(2)}, u32[]{:S(2)}) collective-permute-start(f32[384,64]{0,1:T(8,128)S(1)} %broadcast_select_fusion.5), channel_id=1, source_target_pairs={{4,0},{8,4},{12,8},{5,1},{9,5},{13,9},{6,2},{10,6},{14,10},{7,3},{... | collective-permute-start | bytes 294920 | tf_op jit(solution)/shard_map/while/body/eval_jaxpr/ppermute | solution.py:10
  221.5 23.9 %copy-start.4 = (f32[384,64]{0,1:T(8,128)}, f32[384,64]{0,1:T(8,128)S(1)}, u32[]{:S(2)}) copy-start(f32[384,64]{0,1:T(8,128)S(1)} %get-tuple-element.225) | copy-start | bytes 294916
  221.6 13.6 %copy-start.11 = (f32[1,384,64]{1,2,0:T(8,128)S(1)}, f32[1,384,64]{1,2,0:T(8,128)}, u32[]{:S(2)}) copy-start(f32[1,384,64]{1,2,0:T(8,128)} %param.33) | copy-start | bytes 294916
  221.6 13.5 %copy-start.12 = (f32[1,384,64]{1,2,0:T(8,128)S(1)}, f32[1,384,64]{1,2,0:T(8,128)}, u32[]{:S(2)}) copy-start(f32[1,384,64]{1,2,0:T(8,128)} %param.31) | copy-start | bytes 294916
  221.6 13.5 %copy-start.13 = (f32[1,384,64]{1,2,0:T(8,128)S(1)}, f32[1,384,64]{1,2,0:T(8,128)}, u32[]{:S(2)}) copy-start(f32[1,384,64]{1,2,0:T(8,128)} %param.32) | copy-start | bytes 294916
  221.6 20.7 %copy-start.3 = (f32[1,512,1536]{2,1,0:T(8,128)S(1)}, f32[1,512,1536]{2,1,0:T(8,128)}, u32[]{:S(2)}) copy-start(f32[1,512,1536]{2,1,0:T(8,128)} %param.35) | copy-start | bytes 9437188
  221.6 20.7 %copy-start.6 = (f32[512,64]{0,1:T(8,128)S(1)}, f32[512,64]{0,1:T(8,128)}, u32[]{:S(2)}) copy-start(f32[512,64]{0,1:T(8,128)} %copy-done.5) | copy-start | bytes 393220
  228.3 7.5 %collective-permute-start.3 = (f32[384,64]{0,1:T(8,128)S(1)}, f32[384,64]{0,1:T(8,128)S(1)}, u32[]{:S(2)}, u32[]{:S(2)}) collective-permute-start(f32[384,64]{0,1:T(8,128)S(1)} %get-tuple-element.225), channel_id=1, source_target_pairs={{0,4},{4,8},{8,12},{1,5},{5,9},{9,13},{2,6},{6,10},{10,14},{3,7},{... | collective-permute-start | bytes 294920 | tf_op jit(solution)/shard_map/ppermute | solution.py:10
  235.1 18.0 %copy-start.1 = (f32[1,512,2048]{2,1,0:T(8,128)S(1)}, f32[1,512,2048]{2,1,0:T(8,128)}, u32[]{:S(2)}) copy-start(f32[1,512,2048]{2,1,0:T(8,128)} %param.34) | copy-start | bytes 12582916
  245.5 11.9 %copy-start.7 = (f32[1,512,64]{1,2,0:T(8,128)S(1)}, f32[1,512,64]{1,2,0:T(8,128)}, u32[]{:S(2)}) copy-start(f32[1,512,64]{1,2,0:T(8,128)} %param.30) | copy-start | bytes 393220
  245.5 11.9 %copy-start.8 = (f32[1,512,64]{1,2,0:T(8,128)S(1)}, f32[1,512,64]{1,2,0:T(8,128)}, u32[]{:S(2)}) copy-start(f32[1,512,64]{1,2,0:T(8,128)} %param.28) | copy-start | bytes 393220
  245.5 11.8 %copy-start.9 = (f32[1,512,64]{1,2,0:T(8,128)S(1)}, f32[1,512,64]{1,2,0:T(8,128)}, u32[]{:S(2)}) copy-start(f32[1,512,64]{1,2,0:T(8,128)} %param.29) | copy-start | bytes 393220
  257.3 0.8 copy-start.10
Sparse Core Ops, SparseCore 0:
  42.6 20.6 reduce-scatter.1
where the time goes:
time: 266 us; the launch traced here: 265 us
  blocking collectives  86 us (32%)
  waiting for transfers between devices  64.5 us (24%)
  matrix products  60.4 us (23%)
  starting transfers between devices  29.2 us (11%)
  between operations  14.3 us (5%)
  other arithmetic  10.2 us (4%)
    dot_general x13, matrix products, product(): jnp.dot(left, right, precision=lax.Precision.HIGHEST, preferred_element_t...  55.6 us
    all_gather x8, blocking collectives, advance(): lax.all_gather(came, ('rec', 'blk'), axis=0, tiled=True)  49.9 us
    ppermute x10, waiting for transfers between devices, from_behind(): lax.ppermute(value, axis, [(source, source + steps) for source in range(l...  43.8 us
    ppermute x10, starting transfers between devices, from_behind(): lax.ppermute(value, axis, [(source, source + steps) for source in range(l...  29.1 us
    reduce_scatter x1, waiting for transfers between devices, shards(): lax.psum_scatter(own + received, ('rec', 'blk'), scatter_dimension=0, til...  20.7 us
    all_gather x1, blocking collectives, shards(): lax.all_gather(load_int, ('rec', 'blk'), axis=0, tiled=True)  8.62 us
    all_gather x1, blocking collectives, shards(): lax.all_gather(load_int - coupled, ('rec', 'blk'), axis=0, tiled=True)  7.64 us
    all_gather x1, blocking collectives, shards(): lax.all_gather(forward, ('rec', 'blk'), axis=0, tiled=True)  6.74 us
  transfers between devices with their start and end apart: 11, of which 10 were waited for; matrix products, arithmetic and copies ran while one was open for 1% of the time, Pallas kernels for 0%

commit v1 on v0

v1 whole, which is shorter than its diff:
```python
import jax
import jax.numpy as jnp
from jax import lax
from jax.sharding import PartitionSpec as P

AXES = ("story", "rec", "blk")


def product(left, right):
    return lax.dot_general(
        left,
        right,
        (((1,), (1,)), ((), ())),
        precision=lax.Precision.HIGH,
        preferred_element_type=jnp.float32,
    )


def product_plain(left, right):
    return lax.dot_general(
        left,
        right,
        (((1,), (0,)), ((), ())),
        precision=lax.Precision.HIGH,
        preferred_element_type=jnp.float32,
    )


class Moves:
    def __init__(self):
        self.stories = lax.axis_size("story")
        self.chips = lax.axis_size("rec")
        self.cores = lax.axis_size("blk")
        assert self.cores == 2 and self.chips & (self.chips - 1) == 0
        self.s = lax.axis_index("story")
        self.r = lax.axis_index("rec")
        self.b = lax.axis_index("blk")

    def permute(self, value, target):
        pairs = []
        for s in range(self.stories):
            for r in range(self.chips):
                for b in range(self.cores):
                    t, q, c = target(s, r, b)
                    pairs.append(
                        (
                            (s * self.chips + r) * self.cores + b,
                            (t * self.chips + q) * self.cores + c,
                        )
                    )
        return lax.ppermute(value, AXES, pairs)

    def core(self, value):
        return self.permute(value, lambda s, r, b: (s, r, 1 - b))

    def chip(self, value, j):
        return self.permute(value, lambda s, r, b: (s, r ^ j, b))

    def story(self, value, parity, j):
        def target(s, r, b):
            t = s ^ 1 if parity == 0 else ((s - 1) ^ 1) + 1
            if t < 0 or t >= self.stories:
                return s, r, 1 - b
            return t, r ^ j, b

        return self.permute(value, target)

    def by_core(self, own, other, axis):
        first = jnp.where(self.b == 0, own, other)
        second = jnp.where(self.b == 0, other, own)
        return jnp.concatenate([first, second], axis=axis)

    def by_chip(self, pieces, axis=1):
        bit = 1
        while bit < self.chips:
            swap = (self.r & bit) != 0
            pieces = [jnp.where(swap, pieces[j ^ bit], pieces[j]) for j in range(self.chips)]
            bit *= 2
        return jnp.concatenate(pieces, axis=axis)

    def gather_chips(self, value):
        return self.by_chip([value] + [self.chip(value, j) for j in range(1, self.chips)])

    def gather_story(self, value, parity):
        return self.by_chip([self.story(value, parity, j) for j in range(self.chips)])

    def half(self, value, which, axis=0):
        width = value.shape[axis] // 2
        return lax.dynamic_slice_in_dim(value, which * width, width, axis)

    def to_half(self, value):
        other = self.core(self.half(value, 1 - self.b))
        return self.by_core(self.half(value, self.b), other, 1)

    def from_half(self, value):
        other = self.core(self.half(value, 1 - self.b, 1))
        return self.by_core(self.half(value, self.b, 1), other, 0)


def shards(
    record_ids,
    ground_table,
    mass_int,
    mass_face,
    pattern_int,
    pattern_face,
    disp_int,
    vel_int,
    acc_int,
    disp_face,
    vel_face,
    acc_face,
    interior_inverse,
    couple_below,
    couple_above,
    lower,
    pivot,
    upper,
):
    mv = Moves()
    s, r, b = mv.s, mv.r, mv.b
    last = mv.stories - 1
    library = ground_table.shape[0]
    picked = record_ids[:, None] == jnp.arange(library, dtype=jnp.int32)[None, :]
    ground = jnp.sum(jnp.where(picked, ground_table[None, :], 0.0), axis=1)
    d_i, v_i, a_i = disp_int[0].T, vel_int[0].T, acc_int[0].T
    d_f, v_f, a_f = disp_face[0].T, vel_face[0].T, acc_face[0].T
    load_int = mass_int * (d_i + 2.0 * v_i + a_i - pattern_int * ground[:, None])
    load_face = mass_face * (d_f + 2.0 * v_f + a_f - pattern_face * ground[:, None])

    def chip_rows(matrix):
        own = matrix[0]
        return own, mv.core(own)

    def chip_product(left, rows):
        return mv.by_core(product(left, rows[0]), product(left, rows[1]), 1)

    across = [mv.chip(load_int, j) for j in range(1, mv.chips)]
    beside = [mv.core(piece) for piece in [load_int] + across]
    load_full = mv.by_chip(
        [mv.by_core(own, other, 1) for own, other in zip([load_int] + across, beside)]
    )
    interior_part = product(load_full, interior_inverse[0])
    forces = jnp.stack(
        [product_plain(interior_part, couple_above[0]), product_plain(interior_part, couple_below[0])]
    )
    forces = mv.half(forces, b, 1) + mv.core(mv.half(forces, 1 - b, 1))
    width = forces.shape[2] // mv.chips

    def chunk(which, j):
        return lax.dynamic_slice_in_dim(forces[which], (r ^ j) * width, width, 1)

    above_force = chunk(0, 0)
    for j in range(1, mv.chips):
        above_force = above_force + mv.chip(chunk(0, j), j)
    below_force = []
    for parity in range(2):
        total = mv.story(chunk(1, 0), parity, 0)
        for j in range(1, mv.chips):
            total = total + mv.story(chunk(1, j), parity, j)
        below_force.append(total)
    below_force = jnp.where(s % 2 == 0, below_force[0], below_force[1])
    below_force = jnp.where(s == last, 0.0, below_force)
    condensed = mv.to_half(load_face) - above_force - below_force

    lower_rows, pivot_rows, upper_rows = chip_rows(lower), chip_rows(pivot), chip_rows(upper)
    forward = condensed
    for k in range(1, mv.stories):
        came = mv.gather_story(forward, (k - 1) % 2)
        forward = jnp.where(s == k, condensed - chip_product(came, lower_rows), forward)
    pivoted = chip_product(mv.gather_chips(forward), pivot_rows)
    face = pivoted
    for k in range(mv.stories - 2, -1, -1):
        came = mv.gather_story(face, k % 2)
        face = jnp.where(s == k, pivoted - chip_product(came, upper_rows), face)

    below_rows, above_rows = chip_rows(couple_below), chip_rows(couple_above)
    inverse_rows = chip_rows(interior_inverse)
    even = mv.gather_story(face, 0)
    odd = mv.gather_story(face, 1)
    face_below = jnp.where(s % 2 == 1, even, odd)
    face_below = jnp.where(s == 0, 0.0, face_below)
    coupled = chip_product(mv.gather_chips(face), above_rows) + chip_product(face_below, below_rows)
    reduced = mv.to_half(load_int) - coupled
    interior = chip_product(mv.gather_chips(reduced), inverse_rows)

    u_i, u_f = mv.from_half(interior), mv.from_half(face)
    new_a_i = u_i - d_i - 2.0 * v_i - a_i
    new_a_f = u_f - d_f - 2.0 * v_f - a_f
    new_v_i = v_i + a_i + new_a_i
    new_v_f = v_f + a_f + new_a_f
    return tuple(out.T[None] for out in (u_i, new_v_i, new_a_i, u_f, new_v_f, new_a_f))


def solution(mesh):
    whole, rows, cube = P(), P(("groups", "story"), ("rec", "blk")), P(("groups", "story"), ("rec", "blk"), None)
    in_specs = (P("groups"), whole) + (rows,) * 4 + (cube,) * 12
    return jax.shard_map(shards, mesh=mesh, in_specs=in_specs, out_specs=(cube,) * 6, check_vma=False)
```

time: 266 us -> 150 us (0.56)
  blocking collectives: 86 us -> 0 us
  waiting for transfers between devices: 64.5 us -> 44.8 us
  between operations: 14.3 us -> 1.23 us
  starting transfers between devices: 29.2 us -> 41 us
  matrix products: 60.4 us -> 54.1 us
    all_gather x13 -> x0, blocking collectives: 86 us -> none  [the longest x8 49.9 us: advance(): lax.all_gather(came, ('rec', 'blk'), axis=0, tiled=True)]
    reduce_scatter x1 -> x0, waiting for transfers between devices: 20.7 us -> none  [shards(): lax.psum_scatter(own + received, ('rec', 'blk'), scatter_dimension=0, til...]
    ppermute x10 -> x38, starting transfers between devices: 29.1 us -> 41 us  [permute(): return lax.ppermute(value, AXES, pairs)]
    dot_general x15 -> x23, matrix products: 60.4 us -> 54.1 us  [the longest x21 48.1 us: product(): lax.dot_general(left, right, (((1,), (1,)), ((), ())), precision=lax.Prec...]
    while x8 -> x0, other arithmetic: 5.33 us -> none
    ppermute x10 -> x38, waiting for transfers between devices: 43.8 us -> 44.8 us  [permute(): return lax.ppermute(value, AXES, pairs)]
  transfers between devices with their start and end apart: 11 -> 38, of which waited for: 10 -> 20; matrix products, arithmetic and copies ran while one was open for 1% -> 28% of each run, Pallas kernels for 0% -> 0%
where the time goes in v1:
time: 150 us; the launch traced here: 149 us
  matrix products  54.1 us (36%)
  waiting for transfers between devices  44.8 us (30%)
  starting transfers between devices  41 us (27%)
  other arithmetic  7.78 us (5%)
    dot_general x21, matrix products, product(): lax.dot_general(left, right, (((1,), (1,)), ((), ())), precision=lax.Prec...  48.1 us
    ppermute x38, waiting for transfers between devices, permute(): return lax.ppermute(value, AXES, pairs)  44.8 us
    ppermute x38, starting transfers between devices, permute(): return lax.ppermute(value, AXES, pairs)  41 us
    dot_general x2, matrix products, product_plain(): lax.dot_general(left, right, (((1,), (0,)), ((), ())), precision=lax.Prec...  5.99 us
  transfers between devices with their start and end apart: 38, of which 20 were waited for; matrix products, arithmetic and copies ran while one was open for 28% of the time, Pallas kernels for 0%

profile of v1, /device:TPU:0, one launch (start us, length us, event | category | flops | bytes accessed | tf_op | source)
XLA Modules:
  0.0 149.0 jit_solution(3029191106804630208)
XLA Ops:
  1.5 1.1 fusion.30
  2.6 3.0 %collective-permute-start.2 = (f32[64,512]{1,0:T(8,128)S(1)}, f32[64,512]{1,0:T(8,128)S(1)}, u32[]{:S(2)}, u32[]{:S(2)}) collective-permute-start(f32[64,512]{1,0:T(8,128)S(1)} %fusion.30), channel_id=1, source_target_pairs={{0,2},{1,3},{2,0},{3,1},{4,6},{5,7},{6,4},{7,5},{8,10},{9,11},{10,... | collective-permute-start | bytes 393224 | tf_op jit(solution)/shard_map/ppermute | solution.py:51
  5.7 3.5 %collective-permute-done.2 = f32[64,512]{1,0:T(8,128)S(1)} collective-permute-done((f32[64,512]{1,0:T(8,128)S(1)}, f32[64,512]{1,0:T(8,128)S(1)}, u32[]{:S(2)}, u32[]{:S(2)}) %collective-permute-start.2) | collective-permute-done | bytes 131104 | tf_op jit(solution)/shard_map/ppermute | solution.py:51
  9.2 1.3 collective-permute-done.3
  10.6 4.2 %fusion = f32[64,512]{1,0:T(8,128)S(1)} fusion(f32[64,1024]{1,0:T(8,128)S(1)} %get-tuple-element.9, f32[64,1024]{1,0:T(8,128)S(1)} %get-tuple-element.8, f32[1,512,2048]{2,1,0:T(8,128)} %param.30), kind=kOutput, calls=%fused_computation.6 | convolution fusion | flops 402784256 | bytes 4849664 | tf_op jit(solution)/shard_map/dot_general | solution.py:10
  14.8 3.0 %convolution_bitcast_fusion = f32[1,64,1536]{2,1,0:T(8,128)S(1)} fusion(f32[64,512]{1,0:T(8,128)S(1)} %fusion, f32[1,512,1536]{2,1,0:T(8,128)} %param.31), kind=kOutput, calls=%fused_computation | convolution fusion | flops 301989888 | bytes 3670016 | tf_op jit(solution)/shard_map/dot_general | solution.py:20
  17.8 3.0 %convolution_bitcast_fusion.1 = f32[1,64,1536]{2,1,0:T(8,128)S(1)} fusion(f32[64,512]{1,0:T(8,128)S(1)} %fusion, f32[1,512,1536]{2,1,0:T(8,128)} %param.32), kind=kOutput, calls=%fused_computation.1 | convolution fusion | flops 301989888 | bytes 3670016 | tf_op jit(solution)/shard_map/dot_general | solution.py:20
  25.0 4.2 %collective-permute-start.8 = (f32[32,768]{1,0:T(8,128)S(1)}, f32[32,768]{1,0:T(8,128)S(1)}, u32[]{:S(2)}, u32[]{:S(2)}) collective-permute-start(f32[32,768]{1,0:T(8,128)S(1)} %get-tuple-element.42), channel_id=1, source_target_pairs={{0,6},{1,7},{2,4},{3,5},{4,2},{5,3},{6,0},{7,1},{8,14},{9,15},{10,... | collective-permute-start | bytes 294920 | tf_op jit(solution)/shard_map/ppermute | solution.py:51
  29.3 1.5 %collective-permute-start.6 = (f32[32,768]{1,0:T(8,128)S(1)}, f32[32,768]{1,0:T(8,128)S(1)}, u32[]{:S(2)}, u32[]{:S(2)}) collective-permute-start(f32[32,768]{1,0:T(8,128)S(1)} %dynamic-slice_bitcast_fusion.2), channel_id=1, source_target_pairs={{0,2},{1,3},{2,0},{3,1},{4,6},{5,7},{6,4},{7,5},{8,10},{9,11},{10,... | collective-permute-start | bytes 294920 | tf_op jit(solution)/shard_map/ppermute | solution.py:51
  31.7 2.5 %collective-permute-done.7 = f32[32,768]{1,0:T(8,128)S(1)} collective-permute-done((f32[32,768]{1,0:T(8,128)S(1)}, f32[32,768]{1,0:T(8,128)S(1)}, u32[]{:S(2)}, u32[]{:S(2)}) %collective-permute-start.7) | collective-permute-done | bytes 98336 | tf_op jit(solution)/shard_map/ppermute | solution.py:51
  34.6 4.4 %collective-permute-start.11 = (f32[32,768]{1,0:T(8,128)S(1)}, f32[32,768]{1,0:T(8,128)S(1)}, u32[]{:S(2)}, u32[]{:S(2)}) collective-permute-start(f32[32,768]{1,0:T(8,128)S(1)} %fusion.36), channel_id=1, source_target_pairs={{0,6},{1,7},{2,4},{3,5},{4,2},{5,3},{6,0},{7,1},{8,14},{9,15},{10,... | collective-permute-start | bytes 294920 | tf_op jit(solution)/shard_map/ppermute | solution.py:51
  38.9 2.6 %collective-permute-done.11 = f32[32,768]{1,0:T(8,128)S(1)} collective-permute-done((f32[32,768]{1,0:T(8,128)S(1)}, f32[32,768]{1,0:T(8,128)S(1)}, u32[]{:S(2)}, u32[]{:S(2)}) %collective-permute-start.11) | collective-permute-done | bytes 98336 | tf_op jit(solution)/shard_map/ppermute | solution.py:51
  41.5 2.0 %collective-permute-done.12 = f32[32,768]{1,0:T(8,128)S(1)} collective-permute-done((f32[32,768]{1,0:T(8,128)S(1)}, f32[32,768]{1,0:T(8,128)S(1)}, u32[]{:S(2)}, u32[]{:S(2)}) %collective-permute-start.12) | collective-permute-done | bytes 98336 | tf_op jit(solution)/shard_map/ppermute | solution.py:51
  43.6 1.1 fusion.26
  44.7 2.8 %broadcast_select_fusion.47 = (f32[32,384]{1,0:T(8,128)S(1)}, f32[32,384]{1,0:T(8,128)S(1)}) fusion(f32[32,384]{1,0:T(8,128)S(1)} %fusion.26, pred[]{:T(512)S(6)} %eq.23, f32[1,384,1536]{2,1,0:T(8,128)} %param.33, f32[32,768]{1,0:T(8,128)S(1)} %get-tuple-element.41, f32[32,768]{1,0:T(8,128)S(1)} %get-tuple-element.40), kind=kOutput, calls=%fused_computation.152 | convolution fusion | flops 113319936 | bytes 2703361 | tf_op jit(solution)/shard_map/dot_general | solution.py:10
  49.1 1.1 fusion.24
  50.2 2.8 %broadcast_select_fusion.45 = (f32[32,384]{1,0:T(8,128)S(1)}, f32[32,384]{1,0:T(8,128)S(1)}) fusion(f32[32,384]{1,0:T(8,128)S(1)} %fusion.24, pred[]{:T(512)S(6)} %eq.23, f32[1,384,1536]{2,1,0:T(8,128)} %param.33, f32[32,768]{1,0:T(8,128)S(1)} %get-tuple-element.39, f32[32,768]{1,0:T(8,128)S(1)} %get-tuple-element.38), kind=kOutput, calls=%fused_computation.150 | convolution fusion | flops 113319936 | bytes 2703361 | tf_op jit(solution)/shard_map/dot_general | solution.py:10
  53.1 7.9 %collective-permute-start.16 = (f32[32,768]{1,0:T(8,128)S(1)}, f32[32,768]{1,0:T(8,128)S(1)}, u32[]{:S(2)}, u32[]{:S(2)}) collective-permute-start(f32[32,768]{1,0:T(8,128)S(1)} %fusion.37), channel_id=1, source_target_pairs={{0,6},{1,7},{2,4},{3,5},{4,2},{5,3},{6,0},{7,1},{8,14},{9,15},{10,... | collective-permute-start | bytes 294920 | tf_op jit(solution)/shard_map/ppermute | solution.py:51
  61.0 2.6 %collective-permute-done.16 = f32[32,768]{1,0:T(8,128)S(1)} collective-permute-done((f32[32,768]{1,0:T(8,128)S(1)}, f32[32,768]{1,0:T(8,128)S(1)}, u32[]{:S(2)}, u32[]{:S(2)}) %collective-permute-start.16) | collective-permute-done | bytes 98336 | tf_op jit(solution)/shard_map/ppermute | solution.py:51
  63.6 2.0 %collective-permute-done.17 = f32[32,768]{1,0:T(8,128)S(1)} collective-permute-done((f32[32,768]{1,0:T(8,128)S(1)}, f32[32,768]{1,0:T(8,128)S(1)}, u32[]{:S(2)}, u32[]{:S(2)}) %collective-permute-start.17) | collective-permute-done | bytes 98336 | tf_op jit(solution)/shard_map/ppermute | solution.py:51
  65.6 1.1 fusion.22
  66.7 2.8 %broadcast_select_fusion.43 = (f32[32,384]{1,0:T(8,128)S(1)}, f32[32,384]{1,0:T(8,128)S(1)}) fusion(f32[32,384]{1,0:T(8,128)S(1)} %fusion.22, pred[]{:T(512)S(6)} %eq.23, f32[1,384,1536]{2,1,0:T(8,128)} %param.33, f32[32,768]{1,0:T(8,128)S(1)} %get-tuple-element.37, f32[32,768]{1,0:T(8,128)S(1)} %get-tuple-element.36), kind=kOutput, calls=%fused_computation.148 | convolution fusion | flops 113319936 | bytes 2703361 | tf_op jit(solution)/shard_map/dot_general | solution.py:10
  70.0 4.2 %collective-permute-done.18 = f32[32,768]{1,0:T(8,128)S(1)} collective-permute-done((f32[32,768]{1,0:T(8,128)S(1)}, f32[32,768]{1,0:T(8,128)S(1)}, u32[]{:S(2)}, u32[]{:S(2)}) %collective-permute-start.18) | collective-permute-done | bytes 98336 | tf_op jit(solution)/shard_map/ppermute | solution.py:51
  74.3 2.8 %fusion.20 = f32[32,384]{1,0:T(8,128)S(1)} fusion(f32[384,1536]{1,0:T(8,128)} %collective-permute-done.19, f32[32,768]{1,0:T(8,128)S(1)} %get-tuple-element.35, f32[32,768]{1,0:T(8,128)S(1)} %get-tuple-element.34), kind=kOutput, calls=%fused_computation.38 | convolution fusion | flops 113295360 | bytes 2605056 | tf_op jit(solution)/shard_map/dot_general | solution.py:10
  77.1 3.0 %broadcast_select_fusion.41 = (f32[32,384]{1,0:T(8,128)S(1)}, f32[32,384]{1,0:T(8,128)S(1)}) fusion(f32[32,384]{1,0:T(8,128)S(1)} %fusion.20, pred[]{:T(512)S(6)} %eq.23, f32[1,384,1536]{2,1,0:T(8,128)} %param.34, f32[32,768]{1,0:T(8,128)S(1)} %get-tuple-element.35, f32[32,768]{1,0:T(8,128)S(1)} %get-tuple-element.34), kind=kOutput, calls=%fused_computation.146 | convolution fusion | flops 113319936 | bytes 2703361 | tf_op jit(solution)/shard_map/dot_general | solution.py:10
  82.5 3.1 %collective-permute-done.20 = f32[32,768]{1,0:T(8,128)S(1)} collective-permute-done((f32[32,768]{1,0:T(8,128)S(1)}, f32[32,768]{1,0:T(8,128)S(1)}, u32[]{:S(2)}, u32[]{:S(2)}) %collective-permute-start.20) | collective-permute-done | bytes 98336 | tf_op jit(solution)/shard_map/ppermute | solution.py:51
  85.7 1.1 fusion.18
  86.8 1.1 broadcast_select_fusion.39
  88.7 3.6 %collective-permute-done.23 = f32[32,768]{1,0:T(8,128)S(1)} collective-permute-done((f32[32,768]{1,0:T(8,128)S(1)}, f32[32,768]{1,0:T(8,128)S(1)}, u32[]{:S(2)}, u32[]{:S(2)}) %collective-permute-start.23) | collective-permute-done | bytes 98336 | tf_op jit(solution)/shard_map/ppermute | solution.py:51
  92.5 2.8 %fusion.16 = f32[32,384]{1,0:T(8,128)S(1)} fusion(f32[384,1536]{1,0:T(8,128)} %copy-done, f32[32,768]{1,0:T(8,128)S(1)} %get-tuple-element.31, f32[32,768]{1,0:T(8,128)S(1)} %get-tuple-element.30), kind=kOutput, calls=%fused_computation.34 | convolution fusion | flops 113295360 | bytes 2605056 | tf_op jit(solution)/shard_map/dot_general | solution.py:10
  95.3 1.1 broadcast_select_fusion.37
  96.5 3.3 %collective-permute-start.25 = (f32[32,768]{1,0:T(8,128)S(1)}, f32[32,768]{1,0:T(8,128)S(1)}, u32[]{:S(2)}, u32[]{:S(2)}) collective-permute-start(f32[32,768]{1,0:T(8,128)S(1)} %fusion.39), channel_id=1, source_target_pairs={{0,6},{1,7},{2,4},{3,5},{4,2},{5,3},{6,0},{7,1},{8,14},{9,15},{10,... | collective-permute-start | bytes 294920 | tf_op jit(solution)/shard_map/ppermute | solution.py:51
  100.0 3.4 %collective-permute-done.25 = f32[32,768]{1,0:T(8,128)S(1)} collective-permute-done((f32[32,768]{1,0:T(8,128)S(1)}, f32[32,768]{1,0:T(8,128)S(1)}, u32[]{:S(2)}, u32[]{:S(2)}) %collective-permute-start.25) | collective-permute-done | bytes 98336 | tf_op jit(solution)/shard_map/ppermute | solution.py:51
  103.4 1.3 collective-permute-done.26
  104.8 1.1 fusion.14
  105.9 1.1 broadcast_select_fusion.35
  107.2 1.3 collective-permute-start.27
  108.5 3.9 %collective-permute-done.27 = f32[32,768]{1,0:T(8,128)S(1)} collective-permute-done((f32[32,768]{1,0:T(8,128)S(1)}, f32[32,768]{1,0:T(8,128)S(1)}, u32[]{:S(2)}, u32[]{:S(2)}) %collective-permute-start.27) | collective-permute-done | bytes 98336 | tf_op jit(solution)/shard_map/ppermute | solution.py:51
  112.4 5.3 %collective-permute-start.29 = (f32[32,768]{1,0:T(8,128)S(1)}, f32[32,768]{1,0:T(8,128)S(1)}, u32[]{:S(2)}, u32[]{:S(2)}) collective-permute-start(f32[32,768]{1,0:T(8,128)S(1)} %fusion.40), channel_id=1, source_target_pairs={{0,6},{1,7},{2,4},{3,5},{4,2},{5,3},{6,0},{7,1},{8,14},{9,15},{10,... | collective-permute-start | bytes 294920 | tf_op jit(solution)/shard_map/ppermute | solution.py:51
  117.7 3.4 %collective-permute-start.30 = (f32[32,768]{1,0:T(8,128)S(1)}, f32[32,768]{1,0:T(8,128)S(1)}, u32[]{:S(2)}, u32[]{:S(2)}) collective-permute-start(f32[32,768]{1,0:T(8,128)S(1)} %fusion.40), channel_id=1, source_target_pairs={{0,4},{1,5},{2,6},{3,7},{4,0},{5,1},{6,2},{7,3},{8,12},{9,13},{10,... | collective-permute-start | bytes 294920 | tf_op jit(solution)/shard_map/ppermute | solution.py:51
  121.3 2.5 %collective-permute-done.30 = f32[32,768]{1,0:T(8,128)S(1)} collective-permute-done((f32[32,768]{1,0:T(8,128)S(1)}, f32[32,768]{1,0:T(8,128)S(1)}, u32[]{:S(2)}, u32[]{:S(2)}) %collective-permute-start.30) | collective-permute-done | bytes 98336 | tf_op jit(solution)/shard_map/ppermute | solution.py:51
  123.8 3.4 %fusion.12 = f32[32,512]{1,0:T(8,128)S(1)} fusion(f32[512,1536]{1,0:T(8,128)} %collective-permute-done.28, f32[32,768]{1,0:T(8,128)S(1)} %get-tuple-element.27, f32[32,768]{1,0:T(8,128)S(1)} %get-tuple-element.26), kind=kOutput, calls=%fused_computation.30 | convolution fusion | flops 151044096 | bytes 3407872 | tf_op jit(solution)/shard_map/dot_general | solution.py:10
  127.1 3.4 %fusion.53 = f32[32,512]{1,0:T(8,128)S(1)} fusion(f32[512,1536]{1,0:T(8,128)} %collective-permute-done.33, f32[32,768]{1,0:T(8,128)S(1)} %get-tuple-element.25, f32[32,768]{1,0:T(8,128)S(1)} %get-tuple-element.24, f32[32,768]{1,0:T(8,128)S(1)} %get-tuple-element.23, f32[32,768]{1,0:T(8,128)S(1)} %get-tuple-element.22, pred[]{:T(512)S(6)} %eq.32, pred[]{:T(512)S(6)} %eq.27), kind=kOutput, calls=%fused_computation.155 | convolution fusion | flops 151191552 | bytes 3604482 | tf_op jit(solution)/shard_map/dot_general | solution.py:10
  130.5 3.4 %broadcast_select_fusion.31 = (f32[32,512]{1,0:T(8,128)S(1)}, f32[32,512]{1,0:T(8,128)S(1)}) fusion(f32[32,512]{1,0:T(8,128)S(1)} %fusion.53, pred[]{:T(512)S(6)} %eq.23, f32[1,512,1536]{2,1,0:T(8,128)} %param.31, f32[32,768]{1,0:T(8,128)S(1)} %get-tuple-element.25, f32[32,768]{1,0:T(8,128)S(1)} %get-tuple-element.24, ...), kind=kOutput, calls=%fused_computation.136 | convolution fusion | flops 151224320 | bytes 3735555 | tf_op jit(solution)/shard_map/dot_general | solution.py:10
  133.9 3.7 %broadcast_select_fusion.33 = (f32[32,512]{1,0:T(8,128)S(1)}, f32[32,512]{1,0:T(8,128)S(1)}) fusion(f32[32,512]{1,0:T(8,128)S(1)} %fusion.12, pred[]{:T(512)S(6)} %eq.23, f32[1,512,1536]{2,1,0:T(8,128)} %param.32, f32[32,768]{1,0:T(8,128)S(1)} %get-tuple-element.27, f32[32,768]{1,0:T(8,128)S(1)} %get-tuple-element.26), kind=kOutput, calls=%fused_computation.138 | convolution fusion | flops 151076864 | bytes 3538945 | tf_op jit(solution)/shard_map/dot_general | solution.py:10
  138.4 4.3 %collective-permute-done.34 = f32[32,1024]{1,0:T(8,128)S(1)} collective-permute-done((f32[32,1024]{1,0:T(8,128)S(1)}, f32[32,1024]{1,0:T(8,128)S(1)}, u32[]{:S(2)}, u32[]{:S(2)}) %collective-permute-start.34) | collective-permute-done | bytes 131104 | tf_op jit(solution)/shard_map/ppermute | solution.py:51
  142.7 2.0 %fusion.8 = f32[32,512]{1,0:T(8,128)S(1)} fusion(f32[32,1024]{1,0:T(8,128)S(1)} %get-tuple-element.15, f32[32,1024]{1,0:T(8,128)S(1)} %get-tuple-element.14, f32[1,512,2048]{2,1,0:T(8,128)S(1)} %copy-done.4), kind=kOutput, calls=%fused_computation.17 | convolution fusion | flops 201392128 | bytes 4521984 | tf_op jit(solution)/shard_map/dot_general | solution.py:10
  144.8 2.0 %broadcast_select_fusion.28 = (f32[32,512]{1,0:T(8,128)S(1)}, f32[32,512]{1,0:T(8,128)S(1)}) fusion(f32[32,512]{1,0:T(8,128)S(1)} %fusion.8, pred[]{:T(512)S(6)} %eq.23, f32[512,2048]{1,0:T(8,128)S(1)} %collective-permute-done.35, f32[32,1024]{1,0:T(8,128)S(1)} %get-tuple-element.15, f32[32,1024]{1,0:T(8,128)S(1)} %get-tuple-element.14), kind=kOutput, calls=%fused_computation.133 | convolution fusion | flops 201424896 | bytes 4653057 | tf_op jit(solution)/shard_map/dot_general | solution.py:10
  (120 shorter events, 15.4 us)
Async XLA Ops:
  2.6 6.5 %collective-permute-start.2 = (f32[64,512]{1,0:T(8,128)S(1)}, f32[64,512]{1,0:T(8,128)S(1)}, u32[]{:S(2)}, u32[]{:S(2)}) collective-permute-start(f32[64,512]{1,0:T(8,128)S(1)} %fusion.30), channel_id=1, source_target_pairs={{0,2},{1,3},{2,0},{3,1},{4,6},{5,7},{6,4},{7,5},{8,10},{9,11},{10,... | collective-permute-start | bytes 393224 | tf_op jit(solution)/shard_map/ppermute | solution.py:51
  5.7 3.5 %collective-permute-start.4 = (f32[64,512]{1,0:T(8,128)S(1)}, f32[64,512]{1,0:T(8,128)S(1)}, u32[]{:S(2)}, u32[]{:S(2)}) collective-permute-start(f32[64,512]{1,0:T(8,128)S(1)} %fusion.30), channel_id=1, source_target_pairs={{0,1},{1,0},{2,3},{3,2},{4,5},{5,4},{6,7},{7,6},{8,9},{9,8},{10,11... | collective-permute-start | bytes 393224 | tf_op jit(solution)/shard_map/ppermute | solution.py:51
  9.1 1.3 collective-permute-start.3
  17.8 4.4 %copy-start.11 = (f32[1,384]{1,0:T(1,128)S(1)}, f32[1,384]{1,0:T(1,128)}, u32[]{:S(2)}) copy-start(f32[1,384]{1,0:T(1,128)} %param.21) | copy-start | bytes 4612
  17.8 4.4 %copy-start.12 = (f32[1,384]{1,0:T(1,128)S(1)}, f32[1,384]{1,0:T(1,128)}, u32[]{:S(2)}) copy-start(f32[1,384]{1,0:T(1,128)} %param.23) | copy-start | bytes 4612
  17.8 4.4 %copy-start.8 = (f32[1,384,64]{1,2,0:T(8,128)S(1)}, f32[1,384,64]{1,2,0:T(8,128)}, u32[]{:S(2)}) copy-start(f32[1,384,64]{1,2,0:T(8,128)} %param.27) | copy-start | bytes 294916
  21.6 2.1 %collective-permute-start.5 = (f32[2,32,1536]{2,1,0:T(8,128)}, f32[2,32,1536]{2,1,0:T(8,128)}, u32[]{:S(2)}, u32[]{:S(2)}) collective-permute-start(f32[2,32,1536]{2,1,0:T(8,128)} %fusion.4), channel_id=1, source_target_pairs={{0,1},{1,0},{2,3},{3,2},{4,5},{5,4},{6,7},{7,6},{8,9},{9,8},{10,11... | collective-permute-start | bytes 1179656 | tf_op jit(solution)/shard_map/ppermute | solution.py:51
  21.8 21.8 %collective-permute-start.13 = (f32[384,1536]{1,0:T(8,128)}, f32[384,1536]{1,0:T(8,128)S(1)}, u32[]{:S(2)}, u32[]{:S(2)}) collective-permute-start(f32[384,1536]{1,0:T(8,128)} %bitcast.23), channel_id=1, source_target_pairs={{0,1},{1,0},{2,3},{3,2},{4,5},{5,4},{6,7},{7,6},{8,9},{9,8},{10,11... | collective-permute-start | bytes 7077896 | tf_op jit(solution)/shard_map/ppermute | solution.py:51
  23.3 6.0 %collective-permute-start.1 = (f32[32,384]{1,0:T(8,128)S(1)}, f32[32,384]{1,0:T(8,128)}, u32[]{:S(2)}, u32[]{:S(2)}) collective-permute-start(f32[32,384]{1,0:T(8,128)S(1)} %constant_dynamic-slice_fusion.1), channel_id=1, source_target_pairs={{0,1},{1,0},{2,3},{3,2},{4,5},{5,4},{6,7},{7,6},{8,9},{9,8},{10,11... | collective-permute-start | bytes 147464 | tf_op jit(solution)/shard_map/ppermute | solution.py:51
  24.8 4.5 %collective-permute-start.10 = (f32[32,768]{1,0:T(8,128)S(1)}, f32[32,768]{1,0:T(8,128)S(1)}, u32[]{:S(2)}, u32[]{:S(2)}) collective-permute-start(f32[32,768]{1,0:T(8,128)S(1)} %get-tuple-element.42), channel_id=1, source_target_pairs={{0,1},{1,0},{2,3},{3,2},{4,10},{5,11},{6,8},{7,9},{8,6},{9,7},{10,... | collective-permute-start | bytes 294920 | tf_op jit(solution)/shard_map/ppermute | solution.py:51
  25.0 9.1 %collective-permute-start.8 = (f32[32,768]{1,0:T(8,128)S(1)}, f32[32,768]{1,0:T(8,128)S(1)}, u32[]{:S(2)}, u32[]{:S(2)}) collective-permute-start(f32[32,768]{1,0:T(8,128)S(1)} %get-tuple-element.42), channel_id=1, source_target_pairs={{0,6},{1,7},{2,4},{3,5},{4,2},{5,3},{6,0},{7,1},{8,14},{9,15},{10,... | collective-permute-start | bytes 294920 | tf_op jit(solution)/shard_map/ppermute | solution.py:51
  29.2 5.0 %collective-permute-start.7 = (f32[32,768]{1,0:T(8,128)S(1)}, f32[32,768]{1,0:T(8,128)S(1)}, u32[]{:S(2)}, u32[]{:S(2)}) collective-permute-start(f32[32,768]{1,0:T(8,128)S(1)} %get-tuple-element.43), channel_id=1, source_target_pairs={{0,4},{1,5},{2,6},{3,7},{4,0},{5,1},{6,2},{7,3},{8,12},{9,13},{10,... | collective-permute-start | bytes 294920 | tf_op jit(solution)/shard_map/ppermute | solution.py:51
  29.2 4.9 %collective-permute-start.9 = (f32[32,768]{1,0:T(8,128)S(1)}, f32[32,768]{1,0:T(8,128)S(1)}, u32[]{:S(2)}, u32[]{:S(2)}) collective-permute-start(f32[32,768]{1,0:T(8,128)S(1)} %get-tuple-element.43), channel_id=1, source_target_pairs={{0,1},{1,0},{2,3},{3,2},{4,8},{5,9},{6,10},{7,11},{8,4},{9,5},{10,... | collective-permute-start | bytes 294920 | tf_op jit(solution)/shard_map/ppermute | solution.py:51
  29.3 5.2 %collective-permute-start.6 = (f32[32,768]{1,0:T(8,128)S(1)}, f32[32,768]{1,0:T(8,128)S(1)}, u32[]{:S(2)}, u32[]{:S(2)}) collective-permute-start(f32[32,768]{1,0:T(8,128)S(1)} %dynamic-slice_bitcast_fusion.2), channel_id=1, source_target_pairs={{0,2},{1,3},{2,0},{3,1},{4,6},{5,7},{6,4},{7,5},{8,10},{9,11},{10,... | collective-permute-start | bytes 294920 | tf_op jit(solution)/shard_map/ppermute | solution.py:51
  34.6 7.0 %collective-permute-start.11 = (f32[32,768]{1,0:T(8,128)S(1)}, f32[32,768]{1,0:T(8,128)S(1)}, u32[]{:S(2)}, u32[]{:S(2)}) collective-permute-start(f32[32,768]{1,0:T(8,128)S(1)} %fusion.36), channel_id=1, source_target_pairs={{0,6},{1,7},{2,4},{3,5},{4,2},{5,3},{6,0},{7,1},{8,14},{9,15},{10,... | collective-permute-start | bytes 294920 | tf_op jit(solution)/shard_map/ppermute | solution.py:51
  38.9 4.6 %collective-permute-start.12 = (f32[32,768]{1,0:T(8,128)S(1)}, f32[32,768]{1,0:T(8,128)S(1)}, u32[]{:S(2)}, u32[]{:S(2)}) collective-permute-start(f32[32,768]{1,0:T(8,128)S(1)} %fusion.36), channel_id=1, source_target_pairs={{0,4},{1,5},{2,6},{3,7},{4,0},{5,1},{6,2},{7,3},{8,12},{9,13},{10,... | collective-permute-start | bytes 294920 | tf_op jit(solution)/shard_map/ppermute | solution.py:51
  47.6 1.4 collective-permute-start.14
  47.6 1.4 collective-permute-start.15
  48.1 26.1 %collective-permute-start.19 = (f32[384,1536]{1,0:T(8,128)}, f32[384,1536]{1,0:T(8,128)}, u32[]{:S(2)}, u32[]{:S(2)}) collective-permute-start(f32[384,1536]{1,0:T(8,128)} %bitcast.24), channel_id=1, source_target_pairs={{0,1},{1,0},{2,3},{3,2},{4,5},{5,4},{6,7},{7,6},{8,9},{9,8},{10,11... | collective-permute-start | bytes 7077896 | tf_op jit(solution)/shard_map/ppermute | solution.py:51
  49.1 11.9 %copy-start.2 = (f32[1,384,1536]{2,1,0:T(8,128)S(1)}, f32[1,384,1536]{2,1,0:T(8,128)}, u32[]{:S(2)}) copy-start(f32[1,384,1536]{2,1,0:T(8,128)} %param.35) | copy-start | bytes 7077892
  53.1 10.5 %collective-permute-start.16 = (f32[32,768]{1,0:T(8,128)S(1)}, f32[32,768]{1,0:T(8,128)S(1)}, u32[]{:S(2)}, u32[]{:S(2)}) collective-permute-start(f32[32,768]{1,0:T(8,128)S(1)} %fusion.37), channel_id=1, source_target_pairs={{0,6},{1,7},{2,4},{3,5},{4,2},{5,3},{6,0},{7,1},{8,14},{9,15},{10,... | collective-permute-start | bytes 294920 | tf_op jit(solution)/shard_map/ppermute | solution.py:51
  61.0 4.6 %collective-permute-start.17 = (f32[32,768]{1,0:T(8,128)S(1)}, f32[32,768]{1,0:T(8,128)S(1)}, u32[]{:S(2)}, u32[]{:S(2)}) collective-permute-start(f32[32,768]{1,0:T(8,128)S(1)} %fusion.37), channel_id=1, source_target_pairs={{0,4},{1,5},{2,6},{3,7},{4,0},{5,1},{6,2},{7,3},{8,12},{9,13},{10,... | collective-permute-start | bytes 294920 | tf_op jit(solution)/shard_map/ppermute | solution.py:51
  61.0 24.7 %collective-permute-start.22 = (f32[384,1536]{1,0:T(8,128)S(1)}, f32[384,1536]{1,0:T(8,128)S(1)}, u32[]{:S(2)}, u32[]{:S(2)}) collective-permute-start(f32[384,1536]{1,0:T(8,128)S(1)} %bitcast.194), channel_id=1, source_target_pairs={{0,1},{1,0},{2,3},{3,2},{4,5},{5,4},{6,7},{7,6},{8,9},{9,8},{10,11... | collective-permute-start | bytes 7077896 | tf_op jit(solution)/shard_map/ppermute | solution.py:51
  69.6 4.7 %collective-permute-start.18 = (f32[32,768]{1,0:T(8,128)S(1)}, f32[32,768]{1,0:T(8,128)S(1)}, u32[]{:S(2)}, u32[]{:S(2)}) collective-permute-start(f32[32,768]{1,0:T(8,128)S(1)} %fusion.38), channel_id=1, source_target_pairs={{0,2},{1,3},{2,0},{3,1},{4,6},{5,7},{6,4},{7,5},{8,10},{9,11},{10,... | collective-permute-start | bytes 294920 | tf_op jit(solution)/shard_map/ppermute | solution.py:51
  80.1 5.6 %collective-permute-start.20 = (f32[32,768]{1,0:T(8,128)S(1)}, f32[32,768]{1,0:T(8,128)S(1)}, u32[]{:S(2)}, u32[]{:S(2)}) collective-permute-start(f32[32,768]{1,0:T(8,128)S(1)} %pad_maximum_fusion.30), channel_id=1, source_target_pairs={{0,6},{1,7},{2,4},{3,5},{4,2},{5,3},{6,0},{7,1},{8,14},{9,15},{10,... | collective-permute-start | bytes 294920 | tf_op jit(solution)/shard_map/ppermute | solution.py:51
  81.0 4.6 %collective-permute-start.21 = (f32[32,768]{1,0:T(8,128)S(1)}, f32[32,768]{1,0:T(8,128)S(1)}, u32[]{:S(2)}, u32[]{:S(2)}) collective-permute-start(f32[32,768]{1,0:T(8,128)S(1)} %pad_maximum_fusion.30), channel_id=1, source_target_pairs={{0,4},{1,5},{2,6},{3,7},{4,0},{5,1},{6,2},{7,3},{8,12},{9,13},{10,... | collective-permute-start | bytes 294920 | tf_op jit(solution)/shard_map/ppermute | solution.py:51
  82.0 45.1 %collective-permute-start.33 = (f32[512,1536]{1,0:T(8,128)}, f32[512,1536]{1,0:T(8,128)}, u32[]{:S(2)}, u32[]{:S(2)}) collective-permute-start(f32[512,1536]{1,0:T(8,128)} %bitcast.17), channel_id=1, source_target_pairs={{0,1},{1,0},{2,3},{3,2},{4,5},{5,4},{6,7},{7,6},{8,9},{9,8},{10,11... | collective-permute-start | bytes 9437192 | tf_op jit(solution)/shard_map/ppermute | solution.py:51
  82.0 41.7 %collective-permute-start.28 = (f32[512,1536]{1,0:T(8,128)}, f32[512,1536]{1,0:T(8,128)}, u32[]{:S(2)}, u32[]{:S(2)}) collective-permute-start(f32[512,1536]{1,0:T(8,128)} %bitcast.15), channel_id=1, source_target_pairs={{0,1},{1,0},{2,3},{3,2},{4,5},{5,4},{6,7},{7,6},{8,9},{9,8},{10,11... | collective-permute-start | bytes 9437192 | tf_op jit(solution)/shard_map/ppermute | solution.py:51
  88.0 7.3 %copy-start.3 = (f32[1,384,1536]{2,1,0:T(8,128)S(1)}, f32[1,384,1536]{2,1,0:T(8,128)}, u32[]{:S(2)}) copy-start(f32[1,384,1536]{2,1,0:T(8,128)} %param.35) | copy-start | bytes 7077892
  88.0 4.3 %collective-permute-start.23 = (f32[32,768]{1,0:T(8,128)S(1)}, f32[32,768]{1,0:T(8,128)S(1)}, u32[]{:S(2)}, u32[]{:S(2)}) collective-permute-start(f32[32,768]{1,0:T(8,128)S(1)} %subtract_select_fusion), channel_id=1, source_target_pairs={{0,1},{1,0},{2,3},{3,2},{4,10},{5,11},{6,8},{7,9},{8,6},{9,7},{10,... | collective-permute-start | bytes 294920 | tf_op jit(solution)/shard_map/ppermute | solution.py:51
  88.1 4.3 %collective-permute-start.24 = (f32[32,768]{1,0:T(8,128)S(1)}, f32[32,768]{1,0:T(8,128)S(1)}, u32[]{:S(2)}, u32[]{:S(2)}) collective-permute-start(f32[32,768]{1,0:T(8,128)S(1)} %subtract_select_fusion), channel_id=1, source_target_pairs={{0,1},{1,0},{2,3},{3,2},{4,8},{5,9},{6,10},{7,11},{8,4},{9,5},{10,... | collective-permute-start | bytes 294920 | tf_op jit(solution)/shard_map/ppermute | solution.py:51
  88.6 11.2 %collective-permute-start = (f32[32,512]{1,0:T(8,128)S(1)}, f32[32,512]{1,0:T(8,128)S(1)}, u32[]{:S(2)}, u32[]{:S(2)}) collective-permute-start(f32[32,512]{1,0:T(8,128)S(1)} %constant_dynamic-slice_fusion.2), channel_id=1, source_target_pairs={{0,1},{1,0},{2,3},{3,2},{4,5},{5,4},{6,7},{7,6},{8,9},{9,8},{10,11... | collective-permute-start | bytes 196616 | tf_op jit(solution)/shard_map/ppermute | solution.py:51
  92.3 52.5 %collective-permute-start.35 = (f32[512,2048]{1,0:T(8,128)}, f32[512,2048]{1,0:T(8,128)S(1)}, u32[]{:S(2)}, u32[]{:S(2)}) collective-permute-start(f32[512,2048]{1,0:T(8,128)} %bitcast.195), channel_id=1, source_target_pairs={{0,1},{1,0},{2,3},{3,2},{4,5},{5,4},{6,7},{7,6},{8,9},{9,8},{10,11... | collective-permute-start | bytes 12582920 | tf_op jit(solution)/shard_map/ppermute | solution.py:51
  95.3 9.5 %copy-start.1 = (f32[384,1536]{1,0:T(8,128)S(1)}, f32[384,1536]{1,0:T(8,128)}, u32[]{:S(2)}) copy-start(f32[384,1536]{1,0:T(8,128)} %copy-done) | copy-start | bytes 7077892
  96.5 7.0 %collective-permute-start.25 = (f32[32,768]{1,0:T(8,128)S(1)}, f32[32,768]{1,0:T(8,128)S(1)}, u32[]{:S(2)}, u32[]{:S(2)}) collective-permute-start(f32[32,768]{1,0:T(8,128)S(1)} %fusion.39), channel_id=1, source_target_pairs={{0,6},{1,7},{2,4},{3,5},{4,2},{5,3},{6,0},{7,1},{8,14},{9,15},{10,... | collective-permute-start | bytes 294920 | tf_op jit(solution)/shard_map/ppermute | solution.py:51
  99.8 5.0 %collective-permute-start.26 = (f32[32,768]{1,0:T(8,128)S(1)}, f32[32,768]{1,0:T(8,128)S(1)}, u32[]{:S(2)}, u32[]{:S(2)}) collective-permute-start(f32[32,768]{1,0:T(8,128)S(1)} %fusion.39), channel_id=1, source_target_pairs={{0,4},{1,5},{2,6},{3,7},{4,0},{5,1},{6,2},{7,3},{8,12},{9,13},{10,... | collective-permute-start | bytes 294920 | tf_op jit(solution)/shard_map/ppermute | solution.py:51
  107.1 5.3 %collective-permute-start.31 = (f32[32,768]{1,0:T(8,128)S(1)}, f32[32,768]{1,0:T(8,128)S(1)}, u32[]{:S(2)}, u32[]{:S(2)}) collective-permute-start(f32[32,768]{1,0:T(8,128)S(1)} %fusion.40), channel_id=1, source_target_pairs={{0,1},{1,0},{2,3},{3,2},{4,10},{5,11},{6,8},{7,9},{8,6},{9,7},{10,... | collective-permute-start | bytes 294920 | tf_op jit(solution)/shard_map/ppermute | solution.py:51
  107.2 5.2 %collective-permute-start.27 = (f32[32,768]{1,0:T(8,128)S(1)}, f32[32,768]{1,0:T(8,128)S(1)}, u32[]{:S(2)}, u32[]{:S(2)}) collective-permute-start(f32[32,768]{1,0:T(8,128)S(1)} %fusion.40), channel_id=1, source_target_pairs={{0,2},{1,3},{2,0},{3,1},{4,6},{5,7},{6,4},{7,5},{8,10},{9,11},{10,... | collective-permute-start | bytes 294920 | tf_op jit(solution)/shard_map/ppermute | solution.py:51
  112.4 5.3 %collective-permute-start.32 = (f32[32,768]{1,0:T(8,128)S(1)}, f32[32,768]{1,0:T(8,128)S(1)}, u32[]{:S(2)}, u32[]{:S(2)}) collective-permute-start(f32[32,768]{1,0:T(8,128)S(1)} %fusion.40), channel_id=1, source_target_pairs={{0,1},{1,0},{2,3},{3,2},{4,8},{5,9},{6,10},{7,11},{8,4},{9,5},{10,... | collective-permute-start | bytes 294920 | tf_op jit(solution)/shard_map/ppermute | solution.py:51
  112.4 8.8 %collective-permute-start.29 = (f32[32,768]{1,0:T(8,128)S(1)}, f32[32,768]{1,0:T(8,128)S(1)}, u32[]{:S(2)}, u32[]{:S(2)}) collective-permute-start(f32[32,768]{1,0:T(8,128)S(1)} %fusion.40), channel_id=1, source_target_pairs={{0,6},{1,7},{2,4},{3,5},{4,2},{5,3},{6,0},{7,1},{8,14},{9,15},{10,... | collective-permute-start | bytes 294920 | tf_op jit(solution)/shard_map/ppermute | solution.py:51
  117.7 6.0 %collective-permute-start.30 = (f32[32,768]{1,0:T(8,128)S(1)}, f32[32,768]{1,0:T(8,128)S(1)}, u32[]{:S(2)}, u32[]{:S(2)}) collective-permute-start(f32[32,768]{1,0:T(8,128)S(1)} %fusion.40), channel_id=1, source_target_pairs={{0,4},{1,5},{2,6},{3,7},{4,0},{5,1},{6,2},{7,3},{8,12},{9,13},{10,... | collective-permute-start | bytes 294920 | tf_op jit(solution)/shard_map/ppermute | solution.py:51
  121.2 17.2 %collective-permute-start.37 = (f32[32,384]{1,0:T(8,128)S(1)}, f32[32,384]{1,0:T(8,128)S(1)}, u32[]{:S(2)}, u32[]{:S(2)}) collective-permute-start(f32[32,384]{1,0:T(8,128)S(1)} %constant_dynamic-slice_fusion), channel_id=1, source_target_pairs={{0,1},{1,0},{2,3},{3,2},{4,5},{5,4},{6,7},{7,6},{8,9},{9,8},{10,11... | collective-permute-start | bytes 147464 | tf_op jit(solution)/shard_map/ppermute | solution.py:51
  133.9 8.8 %copy-start.4 = (f32[1,512,2048]{2,1,0:T(8,128)S(1)}, f32[1,512,2048]{2,1,0:T(8,128)}, u32[]{:S(2)}) copy-start(f32[1,512,2048]{2,1,0:T(8,128)} %param.30) | copy-start | bytes 12582916
  137.6 5.0 %collective-permute-start.34 = (f32[32,1024]{1,0:T(8,128)S(1)}, f32[32,1024]{1,0:T(8,128)S(1)}, u32[]{:S(2)}, u32[]{:S(2)}) collective-permute-start(f32[32,1024]{1,0:T(8,128)S(1)} %maximum_subtract_fusion), channel_id=1, source_target_pairs={{0,2},{1,3},{2,0},{3,1},{4,6},{5,7},{6,4},{7,5},{8,10},{9,11},{10,... | collective-permute-start | bytes 393224 | tf_op jit(solution)/shard_map/ppermute | solution.py:51
  144.7 3.4 %copy-start.5 = (f32[1,512,64]{1,2,0:T(8,128)S(1)}, f32[1,512,64]{1,2,0:T(8,128)}, u32[]{:S(2)}) copy-start(f32[1,512,64]{1,2,0:T(8,128)} %param.26) | copy-start | bytes 393220
  144.8 3.4 %copy-start.6 = (f32[1,512,64]{1,2,0:T(8,128)S(1)}, f32[1,512,64]{1,2,0:T(8,128)}, u32[]{:S(2)}) copy-start(f32[1,512,64]{1,2,0:T(8,128)} %param.25) | copy-start | bytes 393220
  144.8 3.4 %copy-start.7 = (f32[1,512,64]{1,2,0:T(8,128)S(1)}, f32[1,512,64]{1,2,0:T(8,128)}, u32[]{:S(2)}) copy-start(f32[1,512,64]{1,2,0:T(8,128)} %param.24) | copy-start | bytes 393220
  146.8 1.3 collective-permute-start.36
  (3 other events, 6.7 us)

commit v2 on v1

--- a/solution.py
+++ b/solution.py
@@ -1,29 +1,172 @@
+import functools
+
 import jax
 import jax.numpy as jnp
 from jax import lax
+from jax.experimental import pallas as pl
+from jax.experimental.pallas import tpu as pltpu
 from jax.sharding import PartitionSpec as P
 
 AXES = ("story", "rec", "blk")
-
-
-def product(left, right):
-    return lax.dot_general(
-        left,
-        right,
-        (((1,), (1,)), ((), ())),
-        precision=lax.Precision.HIGH,
-        preferred_element_type=jnp.float32,
-    )
-
-
-def product_plain(left, right):
-    return lax.dot_general(
-        left,
-        right,
-        (((1,), (0,)), ((), ())),
-        precision=lax.Precision.HIGH,
-        preferred_element_type=jnp.float32,
-    )
+TILE = 256
+VMEM = pl.BlockSpec(memory_space=pltpu.VMEM)
+
+
+def split(value):
+    high = value.astype(jnp.bfloat16)
+    return high, (value - high.astype(jnp.float32)).astype(jnp.bfloat16)
+
+
+def stacked(value):
+    return jnp.concatenate(split(value), axis=0)
+
+
+def matmul(left, right, over):
+    rows = left.shape[0] // 2
+    total = None
+    for part in reversed(split(right)):
+        both = lax.dot_general(
+            left, part, (((1,), (over,)), ((), ())), preferred_element_type=jnp.float32
+        )
+        both = both[rows:] + both[:rows]
+        total = both if total is None else total + both
+    return total
+
+
+def times_rows(left, *refs):
+    left = stacked(left)
+    count = refs[0].shape[0]
+    ends = count * len(refs)
+    columns = []
+    for start in range(0, ends, TILE):
+        stop = min(start + TILE, ends)
+        blocks = []
+        for i, ref in enumerate(refs):
+            low, high = max(start - i * count, 0), min(stop - i * count, count)
+            if low < high:
+                blocks.append(ref[low:high, :])
+        columns.append(matmul(left, jnp.concatenate(blocks, axis=0), 1))
+    return jnp.concatenate(columns, axis=1)
+
+
+def times(left, ref):
+    left = stacked(left)
+    width = ref.shape[1]
+    columns = [matmul(left, ref[:, n : min(n + TILE, width)], 0) for n in range(0, width, TILE)]
+    return jnp.concatenate(columns, axis=1)
+
+
+def in_order(pieces, own):
+    bit = 1
+    while bit < len(pieces):
+        swap = (own & bit) != 0
+        pieces = [jnp.where(swap, pieces[j ^ bit], pieces[j]) for j in range(len(pieces))]
+        bit *= 2
+    return pieces
+
+
+def joined(refs, axis="rec"):
+    own = lax.axis_index(axis) if len(refs) > 1 else 0
+    return jnp.concatenate(in_order([ref[...] for ref in refs], own), axis=1)
+
+
+def store_rows(ref, value):
+    half = value.shape[1] // 2
+    swap = lax.axis_index("blk") == 1
+    own, other = value[:, :half], value[:, half:]
+    ref[...] = jnp.concatenate([jnp.where(swap, other, own), jnp.where(swap, own, other)], axis=1)
+
+
+def call(kernel, shapes, *groups):
+    flat = [value for group in groups for value in group]
+
+    def body(*refs):
+        at, parts = 0, []
+        for group in groups:
+            parts.append(refs[at : at + len(group)])
+            at += len(group)
+        kernel(*parts, *refs[at:])
+
+    out = [jax.ShapeDtypeStruct(shape, jnp.float32) for shape in shapes]
+    return pl.pallas_call(
+        body,
+        in_specs=[VMEM] * len(flat),
+        out_specs=[VMEM] * len(out),
+        out_shape=out,
+        compiler_params=pltpu.CompilerParams(vmem_limit_bytes=40 << 20),
+    )(*flat)
+
+
+def forces_kernel(swap_chips, pieces, matrices, mine, theirs):
+    inverse, above, below = matrices
+    if swap_chips:
+        chips = len(pieces) // 2
+        core = lax.axis_index("blk")
+        sets = [in_order([pieces[2 * j][...], pieces[2 * j + 1][...]], core) for j in range(chips)]
+        sets = [jnp.concatenate(pair, axis=1) for pair in sets]
+        full = jnp.concatenate(in_order(sets, lax.axis_index("rec")), axis=1)
+    else:
+        full = pieces[0][...]
+    part = times_rows(full, inverse)
+    half = part.shape[0] // 2
+    second = lax.axis_index("blk") == 1
+    for i, matrix in enumerate((above, below)):
+        force = times(part, matrix)
+        mine[i] = jnp.where(second, force[half:], force[:half])
+        theirs[i] = jnp.where(second, force[:half], force[half:])
+
+
+def chunks_kernel(inputs, *outs):
+    mine, came = inputs
+    chips = len(outs) // 2
+    for i in range(2):
+        total = mine[i] + came[i]
+        width = total.shape[1] // chips
+        pieces = [total[:, j * width : (j + 1) * width] for j in range(chips)]
+        for j, piece in enumerate(in_order(pieces, lax.axis_index("rec"))):
+            outs[i * chips + j][...] = piece
+
+
+def step_kernel(story, pieces, rows, terms, out):
+    first, latest = terms
+
+    @pl.when(lax.axis_index("story") == story)
+    def _():
+        store_rows(out, times_rows(joined(pieces), *rows))
+        out[...] = first[...] - out[...]
+
+    @pl.when(lax.axis_index("story") != story)
+    def _():
+        out[...] = latest[...]
+
+
+def rows_kernel(pieces, rows, out):
+    store_rows(out, times_rows(joined(pieces), *rows))
+
+
+def coupled_kernel(load, early, here, even, odd, above, below, out):
+    story = lax.axis_index("story")
+
+    @pl.when(story == 0)
+    def _():
+        store_rows(out, times_rows(joined(here), *above))
+        out[...] = load[0][...] - out[...]
+
+    @pl.when(story > 0)
+    def _():
+        use = lax.rem(story, 2) == 1
+        refs = [jnp.where(use, e[...], o[...]) for e, o in zip(even, odd)]
+        own = lax.axis_index("rec") if len(refs) > 1 else 0
+        value = jnp.concatenate(in_order(refs, own), axis=1)
+        store_rows(out, times_rows(value, *below))
+        out[...] = load[0][...] - early[0][...] - out[...]
+
+
+def last_kernel(pieces, rows, mine, theirs):
+    value = times_rows(joined(pieces), *rows)
+    half = value.shape[1] // 2
+    mine[...] = value[:, :half]
+    theirs[...] = value[:, half:]
 
 
 class Moves:
@@ -60,7 +203,7 @@
         def target(s, r, b):
             t = s ^ 1 if parity == 0 else ((s - 1) ^ 1) + 1
             if t < 0 or t >= self.stories:
-                return s, r, 1 - b
+                return (s, r ^ 1, b) if self.chips > 1 else (s, r, 1 - b)
             return t, r ^ j, b
 
         return self.permute(value, target)
@@ -78,11 +221,14 @@
             bit *= 2
         return jnp.concatenate(pieces, axis=axis)
 
+    def pieces(self, pieces):
+        return pieces if pieces[0].shape[1] % 128 == 0 else [self.by_chip(pieces)]
+
     def gather_chips(self, value):
-        return self.by_chip([value] + [self.chip(value, j) for j in range(1, self.chips)])
+        return self.pieces([value] + [self.chip(value, j) for j in range(1, self.chips)])
 
     def gather_story(self, value, parity):
-        return self.by_chip([self.story(value, parity, j) for j in range(self.chips)])
+        return self.pieces([self.story(value, parity, j) for j in range(self.chips)])
 
     def half(self, value, which, axis=0):
         width = value.shape[axis] // 2
@@ -128,63 +274,90 @@
     load_int = mass_int * (d_i + 2.0 * v_i + a_i - pattern_int * ground[:, None])
     load_face = mass_face * (d_f + 2.0 * v_f + a_f - pattern_face * ground[:, None])
 
+    records = load_int.shape[0]
+    half = records // 2
+    rows_int, rows_face = 2 * load_int.shape[1], 2 * load_face.shape[1]
+    faces = couple_above.shape[2]
+
     def chip_rows(matrix):
         own = matrix[0]
-        return own, mv.core(own)
-
-    def chip_product(left, rows):
-        return mv.by_core(product(left, rows[0]), product(left, rows[1]), 1)
+        return [own, mv.core(own)]
 
     across = [mv.chip(load_int, j) for j in range(1, mv.chips)]
     beside = [mv.core(piece) for piece in [load_int] + across]
-    load_full = mv.by_chip(
-        [mv.by_core(own, other, 1) for own, other in zip([load_int] + across, beside)]
+    pieces = [piece for pair in zip([load_int] + across, beside) for piece in pair]
+    aligned = load_int.shape[1] % 128 == 0
+    if not aligned:
+        pieces = [
+            mv.by_chip([mv.by_core(pieces[2 * j], pieces[2 * j + 1], 1) for j in range(mv.chips)])
+        ]
+    mine, theirs = call(
+        functools.partial(forces_kernel, aligned),
+        [(2, half, faces)] * 2,
+        pieces,
+        [interior_inverse[0], couple_above[0], couple_below[0]],
     )
-    interior_part = product(load_full, interior_inverse[0])
-    forces = jnp.stack(
-        [product_plain(interior_part, couple_above[0]), product_plain(interior_part, couple_below[0])]
+    chunks = call(
+        chunks_kernel,
+        [(half, faces // mv.chips)] * (2 * mv.chips),
+        [mine, mv.core(theirs)],
     )
-    forces = mv.half(forces, b, 1) + mv.core(mv.half(forces, 1 - b, 1))
-    width = forces.shape[2] // mv.chips
-
-    def chunk(which, j):
-        return lax.dynamic_slice_in_dim(forces[which], (r ^ j) * width, width, 1)
-
-    above_force = chunk(0, 0)
+    above_force = chunks[0]
     for j in range(1, mv.chips):
-        above_force = above_force + mv.chip(chunk(0, j), j)
+        above_force = above_force + mv.chip(chunks[j], j)
     below_force = []
     for parity in range(2):
-        total = mv.story(chunk(1, 0), parity, 0)
+        total = mv.story(chunks[mv.chips], parity, 0)
         for j in range(1, mv.chips):
-            total = total + mv.story(chunk(1, j), parity, j)
+            total = total + mv.story(chunks[mv.chips + j], parity, j)
         below_force.append(total)
-    below_force = jnp.where(s % 2 == 0, below_force[0], below_force[1])
-    below_force = jnp.where(s == last, 0.0, below_force)
-    condensed = mv.to_half(load_face) - above_force - below_force
+    condensed = mv.to_half(load_face) - above_force
+    condensed = jnp.where((s % 2 == 0) & (s != last), condensed - below_force[0], condensed)
 
     lower_rows, pivot_rows, upper_rows = chip_rows(lower), chip_rows(pivot), chip_rows(upper)
+    shape = [(half, rows_face)]
     forward = condensed
     for k in range(1, mv.stories):
         came = mv.gather_story(forward, (k - 1) % 2)
-        forward = jnp.where(s == k, condensed - chip_product(came, lower_rows), forward)
-    pivoted = chip_product(mv.gather_chips(forward), pivot_rows)
+        if k == 1:
+            condensed = jnp.where((s % 2 == 1) & (s != last), condensed - below_force[1], condensed)
+        (forward,) = call(
+            functools.partial(step_kernel, k), shape, came, lower_rows, [condensed, forward]
+        )
+    (pivoted,) = call(rows_kernel, shape, mv.gather_chips(forward), pivot_rows)
+
+    below_rows, above_rows = chip_rows(couple_below), chip_rows(couple_above)
+    inverse_rows = chip_rows(interior_inverse)
+    shape_int = [(half, rows_int)]
     face = pivoted
     for k in range(mv.stories - 2, -1, -1):
         came = mv.gather_story(face, k % 2)
-        face = jnp.where(s == k, pivoted - chip_product(came, upper_rows), face)
-
-    below_rows, above_rows = chip_rows(couple_below), chip_rows(couple_above)
-    inverse_rows = chip_rows(interior_inverse)
+        if k == 0:
+            odd = mv.gather_story(face, 1)
+            (early,) = call(rows_kernel, shape_int, mv.gather_chips(face), above_rows)
+        (face,) = call(functools.partial(step_kernel, k), shape, came, upper_rows, [pivoted, face])
+
     even = mv.gather_story(face, 0)
-    odd = mv.gather_story(face, 1)
-    face_below = jnp.where(s % 2 == 1, even, odd)
-    face_below = jnp.where(s == 0, 0.0, face_below)
-    coupled = chip_product(mv.gather_chips(face), above_rows) + chip_product(face_below, below_rows)
-    reduced = mv.to_half(load_int) - coupled
-    interior = chip_product(mv.gather_chips(reduced), inverse_rows)
-
-    u_i, u_f = mv.from_half(interior), mv.from_half(face)
+    (reduced,) = call(
+        coupled_kernel,
+        shape_int,
+        [mv.to_half(load_int)],
+        [early],
+        mv.gather_chips(face),
+        even,
+        odd,
+        above_rows,
+        below_rows,
+    )
+    mine, theirs = call(
+        last_kernel,
+        [(half, rows_int // 2)] * 2,
+        mv.gather_chips(reduced),
+        inverse_rows,
+    )
+
+    u_f = mv.from_half(face)
+    u_i = mv.by_core(mine, mv.core(theirs), 0)
     new_a_i = u_i - d_i - 2.0 * v_i - a_i
     new_a_f = u_f - d_f - 2.0 * v_f - a_f
     new_v_i = v_i + a_i + new_a_i

time: 150 us -> 134 us (0.89)
  matrix products: 54.1 us -> 0 us
  Pallas kernels: 0 us -> 27 us
  local copies, waits for them, and re-layouts: 0.16 us -> 9.4 us
  waiting for transfers between devices: 44.8 us -> 50.2 us
  other arithmetic: 7.78 us -> 5.71 us
    dot_general x23 -> x0, matrix products: 54.1 us -> none  [the longest x21 48.1 us: product(): lax.dot_general(left, right, (((1,), (1,)), ((), ())), precision=lax.Prec...]
    pallas_call x0 -> x12, Pallas kernels: none -> 27 us  [call(): pl.pallas_call(body, in_specs=[VMEM] * len(flat), out_specs=[VMEM] * len(...]
    unnamed x26 -> x48, local copies, waits for them, and re-layouts: 0.08 us -> 9.38 us
    ppermute x38 -> x39, waiting for transfers between devices: 44.8 us -> 50.2 us  [permute(): return lax.ppermute(value, AXES, pairs)]
    ppermute x38 -> x39, starting transfers between devices: 41 us -> 40.5 us  [permute(): return lax.ppermute(value, AXES, pairs)]
  transfers between devices with their start and end apart: 38 -> 39, of which waited for: 20 -> 24; matrix products, arithmetic and copies ran while one was open for 28% -> 4% of each run, Pallas kernels for 0% -> 17%
where the time goes in v2:
time: 134 us
  waiting for transfers between devices  50.2 us (37%)
  starting transfers between devices  40.5 us (30%)
  Pallas kernels  27 us (20%)
  local copies, waits for them, and re-layouts  9.4 us (7%)
  other arithmetic  5.71 us (4%)
    ppermute x39, waiting for transfers between devices, permute(): return lax.ppermute(value, AXES, pairs)  50.2 us
    ppermute x39, starting transfers between devices, permute(): return lax.ppermute(value, AXES, pairs)  40.5 us
    pallas_call x12, Pallas kernels, call(): pl.pallas_call(body, in_specs=[VMEM] * len(flat), out_specs=[VMEM] * len(...  27 us
    unnamed x48, local copies, waits for them, and re-layouts  9.38 us
  transfers between devices with their start and end apart: 39, of which 24 were waited for; matrix products, arithmetic and copies ran while one was open for 4% of the time, Pallas kernels for 17%

profile of v2, /device:TPU:0, one launch (start us, length us, event | category | flops | bytes accessed | tf_op | source)
XLA Modules:
  0.0 133.8 jit_solution(3451138495036140134)
XLA Ops:
  2.0 1.1 fusion.2.refs_0_
  3.2 2.6 %collective-permute-start.3 = (f32[64,512]{1,0:T(8,128)S(1)}, f32[64,512]{1,0:T(8,128)S(1)}, u32[]{:S(2)}, u32[]{:S(2)}) collective-permute-start(f32[64,512]{1,0:T(8,128)S(1)} %fusion.2.refs_0_), channel_id=1, source_target_pairs={{0,2},{1,3},{2,0},{3,1},{4,6},{5,7},{6,4},{7,5},{8,10},{9,11},{10,... | collective-permute-start | bytes 393224 | tf_op jit(solution)/shard_map/ppermute | solution.py:194
  5.9 3.9 %collective-permute-done.3.refs_2_ = f32[64,512]{1,0:T(8,128)S(1)} collective-permute-done((f32[64,512]{1,0:T(8,128)S(1)}, f32[64,512]{1,0:T(8,128)S(1)}, u32[]{:S(2)}, u32[]{:S(2)}) %collective-permute-start.3) | collective-permute-done | bytes 131104 | tf_op jit(solution)/shard_map/ppermute | solution.py:194
  9.9 1.3 %collective-permute-done.4.refs_3_ = f32[64,512]{1,0:T(8,128)S(1)} collective-permute-done((f32[64,512]{1,0:T(8,128)S(1)}, f32[64,512]{1,0:T(8,128)S(1)}, u32[]{:S(2)}, u32[]{:S(2)}) %collective-permute-start.4) | collective-permute-done | bytes 131104 | tf_op jit(solution)/shard_map/ppermute | solution.py:194
  11.2 1.9 %copy-done = f32[1,512,1536]{2,1,0:T(8,128)S(1)} copy-done((f32[1,512,1536]{2,1,0:T(8,128)S(1)}, f32[1,512,1536]{2,1,0:T(8,128)}, u32[]{:S(2)}) %copy-start) | copy-done | bytes 3145752
  13.1 2.2 %copy-done.8 = f32[1,512,2048]{2,1,0:T(8,128)S(1)} copy-done((f32[1,512,2048]{2,1,0:T(8,128)S(1)}, f32[1,512,2048]{2,1,0:T(8,128)}, u32[]{:S(2)}) %copy-start.8) | copy-done | bytes 4194328
  15.3 1.9 %copy-done.10 = f32[1,512,1536]{2,1,0:T(8,128)S(1)} copy-done((f32[1,512,1536]{2,1,0:T(8,128)S(1)}, f32[1,512,1536]{2,1,0:T(8,128)}, u32[]{:S(2)}) %copy-start.10) | copy-done | bytes 3145752
  17.2 3.3 %shard_map.217 = (f32[2,32,1536]{2,1,0:T(8,128)S(1)}, f32[2,32,1536]{2,1,0:T(8,128)}) custom-call(f32[64,512]{1,0:T(8,128)S(1)} %fusion.2.refs_0_, f32[64,512]{1,0:T(8,128)S(1)} %collective-permute-done.2.refs_1_, f32[64,512]{1,0:T(8,128)S(1)} %collective-permute-done.3.refs_2_, f32[64,512]{1,0:T(8,128)S(1)} %collective-permute-done.4.refs_3_, ...), custom_call_target="tpu_custom_call" | custom-call | tf_op jit(solution)/shard_map/pallas_call | solution.py:91
  20.7 1.1 fusion.10
  23.2 1.8 %collective-permute-start.12 = (f32[32,768]{1,0:T(8,128)}, f32[32,768]{1,0:T(8,128)S(1)}, u32[]{:S(2)}, u32[]{:S(2)}) collective-permute-start(f32[32,768]{1,0:T(8,128)} %get-tuple-element.18), channel_id=1, source_target_pairs={{0,2},{1,3},{2,0},{3,1},{4,8},{5,9},{6,10},{7,11},{8,4},{9,5},{10,... | collective-permute-start | bytes 294920 | tf_op jit(solution)/shard_map/ppermute | solution.py:194
  26.4 2.8 %collective-permute-start.7 = (f32[32,768]{1,0:T(8,128)}, f32[32,768]{1,0:T(8,128)S(1)}, u32[]{:S(2)}, u32[]{:S(2)}) collective-permute-start(f32[32,768]{1,0:T(8,128)} %get-tuple-element.18), channel_id=1, source_target_pairs={{0,4},{1,5},{2,6},{3,7},{4,0},{5,1},{6,2},{7,3},{8,12},{9,13},{10,... | collective-permute-start | bytes 294920 | tf_op jit(solution)/shard_map/ppermute | solution.py:194
  29.2 2.6 %collective-permute-start.8 = (f32[32,768]{1,0:T(8,128)}, f32[32,768]{1,0:T(8,128)S(1)}, u32[]{:S(2)}, u32[]{:S(2)}) collective-permute-start(f32[32,768]{1,0:T(8,128)} %get-tuple-element.19), channel_id=1, source_target_pairs={{0,6},{1,7},{2,4},{3,5},{4,2},{5,3},{6,0},{7,1},{8,14},{9,15},{10,... | collective-permute-start | bytes 294920 | tf_op jit(solution)/shard_map/ppermute | solution.py:194
  33.0 1.9 %collective-permute-done.8 = f32[32,768]{1,0:T(8,128)S(1)} collective-permute-done((f32[32,768]{1,0:T(8,128)}, f32[32,768]{1,0:T(8,128)S(1)}, u32[]{:S(2)}, u32[]{:S(2)}) %collective-permute-start.8) | collective-permute-done | bytes 98336 | tf_op jit(solution)/shard_map/ppermute | solution.py:194
  35.0 1.9 %collective-permute-done.6 = f32[32,768]{1,0:T(8,128)S(1)} collective-permute-done((f32[32,768]{1,0:T(8,128)S(1)}, f32[32,768]{1,0:T(8,128)S(1)}, u32[]{:S(2)}, u32[]{:S(2)}) %collective-permute-start.6) | collective-permute-done | bytes 98336 | tf_op jit(solution)/shard_map/ppermute | solution.py:194
  36.9 1.7 %collective-permute-start.9 = (f32[32,768]{1,0:T(8,128)S(1)}, f32[32,768]{1,0:T(8,128)S(1)}, u32[]{:S(2)}, u32[]{:S(2)}) collective-permute-start(f32[32,768]{1,0:T(8,128)S(1)} %get-tuple-element.23.refs_5_), channel_id=1, source_target_pairs={{0,4},{1,5},{2,6},{3,7},{4,0},{5,1},{6,2},{7,3},{8,12},{9,13},{10,... | collective-permute-start | bytes 294920 | tf_op jit(solution)/shard_map/ppermute | solution.py:194
  39.5 2.9 %collective-permute-done.9.refs_0_ = f32[32,768]{1,0:T(8,128)S(1)} collective-permute-done((f32[32,768]{1,0:T(8,128)S(1)}, f32[32,768]{1,0:T(8,128)S(1)}, u32[]{:S(2)}, u32[]{:S(2)}) %collective-permute-start.9) | collective-permute-done | bytes 98336 | tf_op jit(solution)/shard_map/ppermute | solution.py:194
  42.5 1.8 %collective-permute-done.10.refs_1_ = f32[32,768]{1,0:T(8,128)S(1)} collective-permute-done((f32[32,768]{1,0:T(8,128)S(1)}, f32[32,768]{1,0:T(8,128)S(1)}, u32[]{:S(2)}, u32[]{:S(2)}) %collective-permute-start.10) | collective-permute-done | bytes 98336 | tf_op jit(solution)/shard_map/ppermute | solution.py:194
  44.2 1.8 %shard_map.219.refs_5_ = f32[32,768]{1,0:T(8,128)S(1)} custom-call(f32[32,768]{1,0:T(8,128)S(1)} %collective-permute-done.9.refs_0_, f32[32,768]{1,0:T(8,128)S(1)} %collective-permute-done.10.refs_1_, f32[384,1536]{1,0:T(8,128)S(1)} %bitcast.129, f32[384,1536]{1,0:T(8,128)} %collective-permute-done.11.refs_3_, f32[32,768]{1,0:T(8,128)S(1)} %get-tuple-element.22.refs_4_, ...), custom_call_target="tpu_custom_call" | custom-call | tf_op jit(solution)/shard_map/pallas_call | solution.py:91
  46.9 1.3 collective-permute-start.15
  48.2 2.9 %collective-permute-done.14.refs_0_ = f32[32,768]{1,0:T(8,128)S(1)} collective-permute-done((f32[32,768]{1,0:T(8,128)S(1)}, f32[32,768]{1,0:T(8,128)S(1)}, u32[]{:S(2)}, u32[]{:S(2)}) %collective-permute-start.14) | collective-permute-done | bytes 98336 | tf_op jit(solution)/shard_map/ppermute | solution.py:194
  51.1 1.1 collective-permute-done.15.refs_1_
  52.1 1.7 %shard_map.220.refs_5_ = f32[32,768]{1,0:T(8,128)S(1)} custom-call(f32[32,768]{1,0:T(8,128)S(1)} %collective-permute-done.14.refs_0_, f32[32,768]{1,0:T(8,128)S(1)} %collective-permute-done.15.refs_1_, f32[384,1536]{1,0:T(8,128)S(1)} %bitcast.130, f32[384,1536]{1,0:T(8,128)} %collective-permute-done.11.refs_3_, f32[32,768]{1,0:T(8,128)S(1)} %get-tuple-element.22.refs_4_, ...), custom_call_target="tpu_custom_call" | custom-call | tf_op jit(solution)/shard_map/pallas_call | solution.py:91
  53.8 3.0 %collective-permute-start.16 = (f32[32,768]{1,0:T(8,128)S(1)}, f32[32,768]{1,0:T(8,128)S(1)}, u32[]{:S(2)}, u32[]{:S(2)}) collective-permute-start(f32[32,768]{1,0:T(8,128)S(1)} %shard_map.220.refs_5_), channel_id=1, source_target_pairs={{0,4},{1,5},{2,6},{3,7},{4,0},{5,1},{6,2},{7,3},{8,12},{9,13},{10,... | collective-permute-start | bytes 294920 | tf_op jit(solution)/shard_map/ppermute | solution.py:194
  56.9 2.9 %collective-permute-done.16.refs_0_ = f32[32,768]{1,0:T(8,128)S(1)} collective-permute-done((f32[32,768]{1,0:T(8,128)S(1)}, f32[32,768]{1,0:T(8,128)S(1)}, u32[]{:S(2)}, u32[]{:S(2)}) %collective-permute-start.16) | collective-permute-done | bytes 98336 | tf_op jit(solution)/shard_map/ppermute | solution.py:194
  59.9 3.1 %collective-permute-done.17.refs_1_ = f32[32,768]{1,0:T(8,128)S(1)} collective-permute-done((f32[32,768]{1,0:T(8,128)S(1)}, f32[32,768]{1,0:T(8,128)S(1)}, u32[]{:S(2)}, u32[]{:S(2)}) %collective-permute-start.17) | collective-permute-done | bytes 98336 | tf_op jit(solution)/shard_map/ppermute | solution.py:194
  62.9 1.7 %shard_map.221.refs_0_ = f32[32,768]{1,0:T(8,128)S(1)} custom-call(f32[32,768]{1,0:T(8,128)S(1)} %collective-permute-done.16.refs_0_, f32[32,768]{1,0:T(8,128)S(1)} %collective-permute-done.17.refs_1_, f32[384,1536]{1,0:T(8,128)S(1)} %bitcast.131, f32[384,1536]{1,0:T(8,128)} %collective-permute-done.11.refs_3_, f32[32,768]{1,0:T(8,128)S(1)} %get-tuple-element.22.refs_4_, ...), custom_call_target="tpu_custom_call" | custom-call | tf_op jit(solution)/shard_map/pallas_call | solution.py:91
  65.2 4.7 %collective-permute-done.18.refs_1_ = f32[32,768]{1,0:T(8,128)S(1)} collective-permute-done((f32[32,768]{1,0:T(8,128)S(1)}, f32[32,768]{1,0:T(8,128)S(1)}, u32[]{:S(2)}, u32[]{:S(2)}) %collective-permute-start.18) | collective-permute-done | bytes 98336 | tf_op jit(solution)/shard_map/ppermute | solution.py:194
  69.9 1.5 %shard_map.222.refs_4_.refs_5_ = f32[32,768]{1,0:T(8,128)S(1)} custom-call(f32[32,768]{1,0:T(8,128)S(1)} %shard_map.221.refs_0_, f32[32,768]{1,0:T(8,128)S(1)} %collective-permute-done.18.refs_1_, f32[384,1536]{1,0:T(8,128)S(1)} %bitcast.143, f32[384,1536]{1,0:T(8,128)S(1)} %collective-permute-done.19.refs_3_), custom_call_target="tpu_custom_call" | custom-call | tf_op jit(solution)/shard_map/pallas_call | solution.py:91
  72.0 1.4 %collective-permute-start.21 = (f32[32,768]{1,0:T(8,128)S(1)}, f32[32,768]{1,0:T(8,128)S(1)}, u32[]{:S(2)}, u32[]{:S(2)}) collective-permute-start(f32[32,768]{1,0:T(8,128)S(1)} %shard_map.222.refs_4_.refs_5_), channel_id=1, source_target_pairs={{0,6},{1,7},{2,4},{3,5},{4,2},{5,3},{6,0},{7,1},{8,14},{9,15},{10,... | collective-permute-start | bytes 294920 | tf_op jit(solution)/shard_map/ppermute | solution.py:194
  73.5 3.5 %collective-permute-done.20.refs_0_ = f32[32,768]{1,0:T(8,128)S(1)} collective-permute-done((f32[32,768]{1,0:T(8,128)S(1)}, f32[32,768]{1,0:T(8,128)S(1)}, u32[]{:S(2)}, u32[]{:S(2)}) %collective-permute-start.20) | collective-permute-done | bytes 98336 | tf_op jit(solution)/shard_map/ppermute | solution.py:194
  77.0 1.1 collective-permute-done.21.refs_1_
  78.2 1.4 %collective-permute-start.23 = (f32[32,768]{1,0:T(8,128)S(1)}, f32[32,768]{1,0:T(8,128)S(1)}, u32[]{:S(2)}, u32[]{:S(2)}) collective-permute-start(f32[32,768]{1,0:T(8,128)S(1)} %shard_map.223.refs_5_), channel_id=1, source_target_pairs={{0,2},{1,3},{2,0},{3,1},{4,8},{5,9},{6,10},{7,11},{8,4},{9,5},{10,... | collective-permute-start | bytes 294920 | tf_op jit(solution)/shard_map/ppermute | solution.py:194
  80.3 2.6 %collective-permute-done.23.refs_0_ = f32[32,768]{1,0:T(8,128)S(1)} collective-permute-done((f32[32,768]{1,0:T(8,128)S(1)}, f32[32,768]{1,0:T(8,128)S(1)}, u32[]{:S(2)}, u32[]{:S(2)}) %collective-permute-start.23) | collective-permute-done | bytes 98336 | tf_op jit(solution)/shard_map/ppermute | solution.py:194
  82.8 1.4 %collective-permute-done.24.refs_1_ = f32[32,768]{1,0:T(8,128)S(1)} collective-permute-done((f32[32,768]{1,0:T(8,128)S(1)}, f32[32,768]{1,0:T(8,128)S(1)}, u32[]{:S(2)}, u32[]{:S(2)}) %collective-permute-start.24) | collective-permute-done | bytes 98336 | tf_op jit(solution)/shard_map/ppermute | solution.py:194
  84.2 7.9 %collective-permute-start.27 = (f32[32,768]{1,0:T(8,128)S(1)}, f32[32,768]{1,0:T(8,128)}, u32[]{:S(2)}, u32[]{:S(2)}) collective-permute-start(f32[32,768]{1,0:T(8,128)S(1)} %shard_map.224.refs_0_.refs_5_), channel_id=1, source_target_pairs={{0,4},{1,5},{2,6},{3,7},{4,0},{5,1},{6,2},{7,3},{8,12},{9,13},{10,... | collective-permute-start | bytes 294920 | tf_op jit(solution)/shard_map/ppermute | solution.py:194
  92.9 2.9 %collective-permute-done.27.refs_0_ = f32[32,768]{1,0:T(8,128)} collective-permute-done((f32[32,768]{1,0:T(8,128)S(1)}, f32[32,768]{1,0:T(8,128)}, u32[]{:S(2)}, u32[]{:S(2)}) %collective-permute-start.27) | collective-permute-done | bytes 98336 | tf_op jit(solution)/shard_map/ppermute | solution.py:194
  97.7 1.3 collective-permute-start.32
  99.1 1.7 %copy-done.5 = f32[1,384,1536]{2,1,0:T(8,128)S(1)} copy-done((f32[1,384,1536]{2,1,0:T(8,128)S(1)}, f32[1,384,1536]{2,1,0:T(8,128)}, u32[]{:S(2)}) %copy-start.5) | copy-done | bytes 2359320
  100.7 1.7 %copy-done.7 = f32[384,1536]{1,0:T(8,128)S(1)} copy-done((f32[384,1536]{1,0:T(8,128)S(1)}, f32[384,1536]{1,0:T(8,128)}, u32[]{:S(2)}) %copy-start.7) | copy-done | bytes 2359320
  102.4 2.5 %shard_map.226.refs_2_ = f32[32,768]{1,0:T(8,128)S(1)} custom-call(f32[32,768]{1,0:T(8,128)} %collective-permute-done.27.refs_0_, f32[32,768]{1,0:T(8,128)} %collective-permute-done.28.refs_1_, f32[384,1536]{1,0:T(8,128)S(1)} %bitcast.135, f32[384,1536]{1,0:T(8,128)S(1)} %copy-done.7, f32[32,768]{1,0:T(8,128)S(1)} %shard_map.222.refs_4_.refs_5_, ...), custom_call_target="tpu_custom_call" | custom-call | tf_op jit(solution)/shard_map/pallas_call | solution.py:91
  105.7 1.3 collective-permute-start.29
  107.0 2.6 %collective-permute-done.33.refs_7_ = f32[32,768]{1,0:T(8,128)S(1)} collective-permute-done((f32[32,768]{1,0:T(8,128)S(1)}, f32[32,768]{1,0:T(8,128)S(1)}, u32[]{:S(2)}, u32[]{:S(2)}) %collective-permute-start.33) | collective-permute-done | bytes 98336 | tf_op jit(solution)/shard_map/ppermute | solution.py:194
  110.6 1.1 collective-permute-start.31
  111.8 4.0 %shard_map.225.refs_1_ = f32[32,1024]{1,0:T(8,128)S(1)} custom-call(f32[32,768]{1,0:T(8,128)S(1)} %shard_map.224.refs_0_.refs_5_, f32[32,768]{1,0:T(8,128)S(1)} %collective-permute-done.25.refs_1_, f32[512,1536]{1,0:T(8,128)S(1)} %bitcast.126, f32[512,1536]{1,0:T(8,128)} %collective-permute-done.26.refs_3_.refs_9_), custom_call_target="tpu_custom_call" | custom-call | tf_op jit(solution)/shard_map/pallas_call | solution.py:91
  116.1 5.0 %shard_map.227.refs_0_ = f32[32,1024]{1,0:T(8,128)S(1)} custom-call(f32[32,1024]{1,0:T(8,128)S(1)} %pad_maximum_fusion.refs_0_, f32[32,1024]{1,0:T(8,128)S(1)} %shard_map.225.refs_1_, f32[32,768]{1,0:T(8,128)S(1)} %shard_map.226.refs_2_, f32[32,768]{1,0:T(8,128)S(1)} %collective-permute-done.29.refs_3_, f32[32,768]{1,0:T(8,128)S(1)} %collective-permute-done.30.refs_4_, ...), custom_call_target="tpu_custom_call" | custom-call | tf_op jit(solution)/shard_map/pallas_call | solution.py:91
  121.1 2.2 %collective-permute-start.35 = (f32[32,1024]{1,0:T(8,128)S(1)}, f32[32,1024]{1,0:T(8,128)S(1)}, u32[]{:S(2)}, u32[]{:S(2)}) collective-permute-start(f32[32,1024]{1,0:T(8,128)S(1)} %shard_map.227.refs_0_), channel_id=1, source_target_pairs={{0,2},{1,3},{2,0},{3,1},{4,6},{5,7},{6,4},{7,5},{8,10},{9,11},{10,... | collective-permute-start | bytes 393224 | tf_op jit(solution)/shard_map/ppermute | solution.py:194
  123.4 3.5 %collective-permute-done.35.refs_1_ = f32[32,1024]{1,0:T(8,128)S(1)} collective-permute-done((f32[32,1024]{1,0:T(8,128)S(1)}, f32[32,1024]{1,0:T(8,128)S(1)}, u32[]{:S(2)}, u32[]{:S(2)}) %collective-permute-start.35) | collective-permute-done | bytes 131104 | tf_op jit(solution)/shard_map/ppermute | solution.py:194
  126.9 4.8 %shard_map.228 = (f32[32,512]{1,0:T(8,128)S(1)}, f32[32,512]{1,0:T(8,128)S(1)}) custom-call(f32[32,1024]{1,0:T(8,128)S(1)} %shard_map.227.refs_0_, f32[32,1024]{1,0:T(8,128)S(1)} %collective-permute-done.35.refs_1_, f32[512,2048]{1,0:T(8,128)S(1)} %bitcast.138, f32[512,2048]{1,0:T(8,128)} %collective-permute-done.36.refs_3_), custom_call_target="tpu_custom_call" | custom-call | tf_op jit(solution)/shard_map/pallas_call | solution.py:91
  (106 shorter events, 16.7 us)
Async XLA Ops:
  0.6 43.6 %collective-permute-start.11 = (f32[384,1536]{1,0:T(8,128)}, f32[384,1536]{1,0:T(8,128)}, u32[]{:S(2)}, u32[]{:S(2)}) collective-permute-start(f32[384,1536]{1,0:T(8,128)} %bitcast.128), channel_id=1, source_target_pairs={{0,1},{1,0},{2,3},{3,2},{4,5},{5,4},{6,7},{7,6},{8,9},{9,8},{10,11... | collective-permute-start | bytes 7077896 | tf_op jit(solution)/shard_map/ppermute | solution.py:194
  3.2 6.7 %collective-permute-start.3 = (f32[64,512]{1,0:T(8,128)S(1)}, f32[64,512]{1,0:T(8,128)S(1)}, u32[]{:S(2)}, u32[]{:S(2)}) collective-permute-start(f32[64,512]{1,0:T(8,128)S(1)} %fusion.2.refs_0_), channel_id=1, source_target_pairs={{0,2},{1,3},{2,0},{3,1},{4,6},{5,7},{6,4},{7,5},{8,10},{9,11},{10,... | collective-permute-start | bytes 393224 | tf_op jit(solution)/shard_map/ppermute | solution.py:194
  5.7 4.2 %collective-permute-start.2 = (f32[64,512]{1,0:T(8,128)S(1)}, f32[64,512]{1,0:T(8,128)S(1)}, u32[]{:S(2)}, u32[]{:S(2)}) collective-permute-start(f32[64,512]{1,0:T(8,128)S(1)} %fusion.2.refs_0_), channel_id=1, source_target_pairs={{0,1},{1,0},{2,3},{3,2},{4,5},{5,4},{6,7},{7,6},{8,9},{9,8},{10,11... | collective-permute-start | bytes 393224 | tf_op jit(solution)/shard_map/ppermute | solution.py:194
  9.9 1.3 %collective-permute-start.4 = (f32[64,512]{1,0:T(8,128)S(1)}, f32[64,512]{1,0:T(8,128)S(1)}, u32[]{:S(2)}, u32[]{:S(2)}) collective-permute-start(f32[64,512]{1,0:T(8,128)S(1)} %collective-permute-done.3.refs_2_), channel_id=1, source_target_pairs={{0,1},{1,0},{2,3},{3,2},{4,5},{5,4},{6,7},{7,6},{8,9},{9,8},{10,11... | collective-permute-start | bytes 393224 | tf_op jit(solution)/shard_map/ppermute | solution.py:194
  20.5 23.7 %copy-start.2 = (f32[1,384,1536]{2,1,0:T(8,128)S(1)}, f32[1,384,1536]{2,1,0:T(8,128)}, u32[]{:S(2)}) copy-start(f32[1,384,1536]{2,1,0:T(8,128)} %param.33) | copy-start | bytes 7077892
  20.5 1.9 %collective-permute-start.5 = (f32[2,32,1536]{2,1,0:T(8,128)}, f32[2,32,1536]{2,1,0:T(8,128)S(1)}, u32[]{:S(2)}, u32[]{:S(2)}) collective-permute-start(f32[2,32,1536]{2,1,0:T(8,128)} %get-tuple-element.15), channel_id=1, source_target_pairs={{0,1},{1,0},{2,3},{3,2},{4,5},{5,4},{6,7},{7,6},{8,9},{9,8},{10,11... | collective-permute-start | bytes 1179656 | tf_op jit(solution)/shard_map/ppermute | solution.py:194
  23.2 6.0 %collective-permute-start.12 = (f32[32,768]{1,0:T(8,128)}, f32[32,768]{1,0:T(8,128)S(1)}, u32[]{:S(2)}, u32[]{:S(2)}) collective-permute-start(f32[32,768]{1,0:T(8,128)} %get-tuple-element.18), channel_id=1, source_target_pairs={{0,2},{1,3},{2,0},{3,1},{4,8},{5,9},{6,10},{7,11},{8,4},{9,5},{10,... | collective-permute-start | bytes 294920 | tf_op jit(solution)/shard_map/ppermute | solution.py:194
  24.9 6.9 %collective-permute-start.13 = (f32[32,768]{1,0:T(8,128)}, f32[32,768]{1,0:T(8,128)S(1)}, u32[]{:S(2)}, u32[]{:S(2)}) collective-permute-start(f32[32,768]{1,0:T(8,128)} %get-tuple-element.19), channel_id=1, source_target_pairs={{0,2},{1,3},{2,0},{3,1},{4,10},{5,11},{6,8},{7,9},{8,6},{9,7},{10,... | collective-permute-start | bytes 294920 | tf_op jit(solution)/shard_map/ppermute | solution.py:194
  25.2 1.2 collective-permute-start.1
  25.2 101.7 %collective-permute-start.36 = (f32[512,2048]{1,0:T(8,128)}, f32[512,2048]{1,0:T(8,128)}, u32[]{:S(2)}, u32[]{:S(2)}) collective-permute-start(f32[512,2048]{1,0:T(8,128)} %bitcast.136), channel_id=1, source_target_pairs={{0,1},{1,0},{2,3},{3,2},{4,5},{5,4},{6,7},{7,6},{8,9},{9,8},{10,11... | collective-permute-start | bytes 12582920 | tf_op jit(solution)/shard_map/ppermute | solution.py:194
  26.4 6.6 %collective-permute-start.7 = (f32[32,768]{1,0:T(8,128)}, f32[32,768]{1,0:T(8,128)S(1)}, u32[]{:S(2)}, u32[]{:S(2)}) collective-permute-start(f32[32,768]{1,0:T(8,128)} %get-tuple-element.18), channel_id=1, source_target_pairs={{0,4},{1,5},{2,6},{3,7},{4,0},{5,1},{6,2},{7,3},{8,12},{9,13},{10,... | collective-permute-start | bytes 294920 | tf_op jit(solution)/shard_map/ppermute | solution.py:194
  29.2 5.8 %collective-permute-start.8 = (f32[32,768]{1,0:T(8,128)}, f32[32,768]{1,0:T(8,128)S(1)}, u32[]{:S(2)}, u32[]{:S(2)}) collective-permute-start(f32[32,768]{1,0:T(8,128)} %get-tuple-element.19), channel_id=1, source_target_pairs={{0,6},{1,7},{2,4},{3,5},{4,2},{5,3},{6,0},{7,1},{8,14},{9,15},{10,... | collective-permute-start | bytes 294920 | tf_op jit(solution)/shard_map/ppermute | solution.py:194
  31.8 16.4 %copy-start.12 = (f32[1,384,1536]{2,1,0:T(8,128)S(1)}, f32[1,384,1536]{2,1,0:T(8,128)}, u32[]{:S(2)}) copy-start(f32[1,384,1536]{2,1,0:T(8,128)} %param.34) | copy-start | bytes 7077892
  31.8 20.3 %copy-start.3 = (f32[1,384,1536]{2,1,0:T(8,128)S(1)}, f32[1,384,1536]{2,1,0:T(8,128)}, u32[]{:S(2)}) copy-start(f32[1,384,1536]{2,1,0:T(8,128)} %param.33) | copy-start | bytes 7077892
  31.8 5.1 %collective-permute-start.6 = (f32[32,768]{1,0:T(8,128)S(1)}, f32[32,768]{1,0:T(8,128)S(1)}, u32[]{:S(2)}, u32[]{:S(2)}) collective-permute-start(f32[32,768]{1,0:T(8,128)S(1)} %get-tuple-element.17), channel_id=1, source_target_pairs={{0,2},{1,3},{2,0},{3,1},{4,6},{5,7},{6,4},{7,5},{8,10},{9,11},{10,... | collective-permute-start | bytes 294920 | tf_op jit(solution)/shard_map/ppermute | solution.py:194
  36.9 5.6 %collective-permute-start.9 = (f32[32,768]{1,0:T(8,128)S(1)}, f32[32,768]{1,0:T(8,128)S(1)}, u32[]{:S(2)}, u32[]{:S(2)}) collective-permute-start(f32[32,768]{1,0:T(8,128)S(1)} %get-tuple-element.23.refs_5_), channel_id=1, source_target_pairs={{0,4},{1,5},{2,6},{3,7},{4,0},{5,1},{6,2},{7,3},{8,12},{9,13},{10,... | collective-permute-start | bytes 294920 | tf_op jit(solution)/shard_map/ppermute | solution.py:194
  38.5 5.7 %collective-permute-start.10 = (f32[32,768]{1,0:T(8,128)S(1)}, f32[32,768]{1,0:T(8,128)S(1)}, u32[]{:S(2)}, u32[]{:S(2)}) collective-permute-start(f32[32,768]{1,0:T(8,128)S(1)} %get-tuple-element.23.refs_5_), channel_id=1, source_target_pairs={{0,6},{1,7},{2,4},{3,5},{4,2},{5,3},{6,0},{7,1},{8,14},{9,15},{10,... | collective-permute-start | bytes 294920 | tf_op jit(solution)/shard_map/ppermute | solution.py:194
  44.2 15.6 %copy-start.4 = (f32[1,384,1536]{2,1,0:T(8,128)S(1)}, f32[1,384,1536]{2,1,0:T(8,128)}, u32[]{:S(2)}) copy-start(f32[1,384,1536]{2,1,0:T(8,128)} %param.35) | copy-start | bytes 7077892
  46.1 10.8 %copy-start.1 = (f32[1,512,1536]{2,1,0:T(8,128)S(1)}, f32[1,512,1536]{2,1,0:T(8,128)}, u32[]{:S(2)}) copy-start(f32[1,512,1536]{2,1,0:T(8,128)} %param.32) | copy-start | bytes 9437188
  46.1 5.0 %collective-permute-start.14 = (f32[32,768]{1,0:T(8,128)S(1)}, f32[32,768]{1,0:T(8,128)S(1)}, u32[]{:S(2)}, u32[]{:S(2)}) collective-permute-start(f32[32,768]{1,0:T(8,128)S(1)} %shard_map.219.refs_5_), channel_id=1, source_target_pairs={{0,2},{1,3},{2,0},{3,1},{4,8},{5,9},{6,10},{7,11},{8,4},{9,5},{10,... | collective-permute-start | bytes 294920 | tf_op jit(solution)/shard_map/ppermute | solution.py:194
  46.9 5.2 %collective-permute-start.15 = (f32[32,768]{1,0:T(8,128)S(1)}, f32[32,768]{1,0:T(8,128)S(1)}, u32[]{:S(2)}, u32[]{:S(2)}) collective-permute-start(f32[32,768]{1,0:T(8,128)S(1)} %shard_map.219.refs_5_), channel_id=1, source_target_pairs={{0,2},{1,3},{2,0},{3,1},{4,10},{5,11},{6,8},{7,9},{8,6},{9,7},{10,... | collective-permute-start | bytes 294920 | tf_op jit(solution)/shard_map/ppermute | solution.py:194
  48.2 16.5 %collective-permute-start.19 = (f32[384,1536]{1,0:T(8,128)S(1)}, f32[384,1536]{1,0:T(8,128)S(1)}, u32[]{:S(2)}, u32[]{:S(2)}) collective-permute-start(f32[384,1536]{1,0:T(8,128)S(1)} %bitcast.142), channel_id=1, source_target_pairs={{0,1},{1,0},{2,3},{3,2},{4,5},{5,4},{6,7},{7,6},{8,9},{9,8},{10,11... | collective-permute-start | bytes 7077896 | tf_op jit(solution)/shard_map/ppermute | solution.py:194
  53.8 6.0 %collective-permute-start.16 = (f32[32,768]{1,0:T(8,128)S(1)}, f32[32,768]{1,0:T(8,128)S(1)}, u32[]{:S(2)}, u32[]{:S(2)}) collective-permute-start(f32[32,768]{1,0:T(8,128)S(1)} %shard_map.220.refs_5_), channel_id=1, source_target_pairs={{0,4},{1,5},{2,6},{3,7},{4,0},{5,1},{6,2},{7,3},{8,12},{9,13},{10,... | collective-permute-start | bytes 294920 | tf_op jit(solution)/shard_map/ppermute | solution.py:194
  56.8 54.9 %collective-permute-start.26 = (f32[512,1536]{1,0:T(8,128)S(1)}, f32[512,1536]{1,0:T(8,128)}, u32[]{:S(2)}, u32[]{:S(2)}) collective-permute-start(f32[512,1536]{1,0:T(8,128)S(1)} %bitcast.125), channel_id=1, source_target_pairs={{0,1},{1,0},{2,3},{3,2},{4,5},{5,4},{6,7},{7,6},{8,9},{9,8},{10,11... | collective-permute-start | bytes 9437192 | tf_op jit(solution)/shard_map/ppermute | solution.py:194
  56.8 6.1 %collective-permute-start.17 = (f32[32,768]{1,0:T(8,128)S(1)}, f32[32,768]{1,0:T(8,128)S(1)}, u32[]{:S(2)}, u32[]{:S(2)}) collective-permute-start(f32[32,768]{1,0:T(8,128)S(1)} %shard_map.220.refs_5_), channel_id=1, source_target_pairs={{0,6},{1,7},{2,4},{3,5},{4,2},{5,3},{6,0},{7,1},{8,14},{9,15},{10,... | collective-permute-start | bytes 294920 | tf_op jit(solution)/shard_map/ppermute | solution.py:194
  59.9 12.2 %collective-permute-start.22 = (f32[384,1536]{1,0:T(8,128)S(1)}, f32[384,1536]{1,0:T(8,128)S(1)}, u32[]{:S(2)}, u32[]{:S(2)}) collective-permute-start(f32[384,1536]{1,0:T(8,128)S(1)} %bitcast.132), channel_id=1, source_target_pairs={{0,1},{1,0},{2,3},{3,2},{4,5},{5,4},{6,7},{7,6},{8,9},{9,8},{10,11... | collective-permute-start | bytes 7077896 | tf_op jit(solution)/shard_map/ppermute | solution.py:194
  62.9 53.2 %collective-permute-start.34 = (f32[512,1536]{1,0:T(8,128)}, f32[512,1536]{1,0:T(8,128)}, u32[]{:S(2)}, u32[]{:S(2)}) collective-permute-start(f32[512,1536]{1,0:T(8,128)} %bitcast.139), channel_id=1, source_target_pairs={{0,1},{1,0},{2,3},{3,2},{4,5},{5,4},{6,7},{7,6},{8,9},{9,8},{10,11... | collective-permute-start | bytes 9437192 | tf_op jit(solution)/shard_map/ppermute | solution.py:194
  64.6 5.3 %collective-permute-start.18 = (f32[32,768]{1,0:T(8,128)S(1)}, f32[32,768]{1,0:T(8,128)S(1)}, u32[]{:S(2)}, u32[]{:S(2)}) collective-permute-start(f32[32,768]{1,0:T(8,128)S(1)} %shard_map.221.refs_0_), channel_id=1, source_target_pairs={{0,2},{1,3},{2,0},{3,1},{4,6},{5,7},{6,4},{7,5},{8,10},{9,11},{10,... | collective-permute-start | bytes 294920 | tf_op jit(solution)/shard_map/ppermute | solution.py:194
  71.4 5.6 %collective-permute-start.20 = (f32[32,768]{1,0:T(8,128)S(1)}, f32[32,768]{1,0:T(8,128)S(1)}, u32[]{:S(2)}, u32[]{:S(2)}) collective-permute-start(f32[32,768]{1,0:T(8,128)S(1)} %shard_map.222.refs_4_.refs_5_), channel_id=1, source_target_pairs={{0,4},{1,5},{2,6},{3,7},{4,0},{5,1},{6,2},{7,3},{8,12},{9,13},{10,... | collective-permute-start | bytes 294920 | tf_op jit(solution)/shard_map/ppermute | solution.py:194
  72.0 12.2 %copy-start.6 = (f32[384,1536]{1,0:T(8,128)}, f32[384,1536]{1,0:T(8,128)S(1)}, u32[]{:S(2)}) copy-start(f32[384,1536]{1,0:T(8,128)S(1)} %collective-permute-done.22.refs_3_) | copy-start | bytes 7077892
  72.0 6.1 %collective-permute-start.21 = (f32[32,768]{1,0:T(8,128)S(1)}, f32[32,768]{1,0:T(8,128)S(1)}, u32[]{:S(2)}, u32[]{:S(2)}) collective-permute-start(f32[32,768]{1,0:T(8,128)S(1)} %shard_map.222.refs_4_.refs_5_), channel_id=1, source_target_pairs={{0,6},{1,7},{2,4},{3,5},{4,2},{5,3},{6,0},{7,1},{8,14},{9,15},{10,... | collective-permute-start | bytes 294920 | tf_op jit(solution)/shard_map/ppermute | solution.py:194
  78.2 4.7 %collective-permute-start.23 = (f32[32,768]{1,0:T(8,128)S(1)}, f32[32,768]{1,0:T(8,128)S(1)}, u32[]{:S(2)}, u32[]{:S(2)}) collective-permute-start(f32[32,768]{1,0:T(8,128)S(1)} %shard_map.223.refs_5_), channel_id=1, source_target_pairs={{0,2},{1,3},{2,0},{3,1},{4,8},{5,9},{6,10},{7,11},{8,4},{9,5},{10,... | collective-permute-start | bytes 294920 | tf_op jit(solution)/shard_map/ppermute | solution.py:194
  79.6 4.6 %collective-permute-start.24 = (f32[32,768]{1,0:T(8,128)S(1)}, f32[32,768]{1,0:T(8,128)S(1)}, u32[]{:S(2)}, u32[]{:S(2)}) collective-permute-start(f32[32,768]{1,0:T(8,128)S(1)} %shard_map.223.refs_5_), channel_id=1, source_target_pairs={{0,2},{1,3},{2,0},{3,1},{4,10},{5,11},{6,8},{7,9},{8,6},{9,7},{10,... | collective-permute-start | bytes 294920 | tf_op jit(solution)/shard_map/ppermute | solution.py:194
  82.8 9.3 %collective-permute-start = (f32[32,512]{1,0:T(8,128)S(1)}, f32[32,512]{1,0:T(8,128)S(1)}, u32[]{:S(2)}, u32[]{:S(2)}) collective-permute-start(f32[32,512]{1,0:T(8,128)S(1)} %constant_dynamic-slice_fusion.2), channel_id=1, source_target_pairs={{0,1},{1,0},{2,3},{3,2},{4,5},{5,4},{6,7},{7,6},{8,9},{9,8},{10,11... | collective-permute-start | bytes 196616 | tf_op jit(solution)/shard_map/ppermute | solution.py:194
  84.2 11.6 %collective-permute-start.27 = (f32[32,768]{1,0:T(8,128)S(1)}, f32[32,768]{1,0:T(8,128)}, u32[]{:S(2)}, u32[]{:S(2)}) collective-permute-start(f32[32,768]{1,0:T(8,128)S(1)} %shard_map.224.refs_0_.refs_5_), channel_id=1, source_target_pairs={{0,4},{1,5},{2,6},{3,7},{4,0},{5,1},{6,2},{7,3},{8,12},{9,13},{10,... | collective-permute-start | bytes 294920 | tf_op jit(solution)/shard_map/ppermute | solution.py:194
  92.1 5.6 %collective-permute-start.28 = (f32[32,768]{1,0:T(8,128)S(1)}, f32[32,768]{1,0:T(8,128)}, u32[]{:S(2)}, u32[]{:S(2)}) collective-permute-start(f32[32,768]{1,0:T(8,128)S(1)} %shard_map.224.refs_0_.refs_5_), channel_id=1, source_target_pairs={{0,6},{1,7},{2,4},{3,5},{4,2},{5,3},{6,0},{7,1},{8,14},{9,15},{10,... | collective-permute-start | bytes 294920 | tf_op jit(solution)/shard_map/ppermute | solution.py:194
  95.8 9.0 %collective-permute-start.25 = (f32[32,768]{1,0:T(8,128)S(1)}, f32[32,768]{1,0:T(8,128)S(1)}, u32[]{:S(2)}, u32[]{:S(2)}) collective-permute-start(f32[32,768]{1,0:T(8,128)S(1)} %shard_map.224.refs_0_.refs_5_), channel_id=1, source_target_pairs={{0,2},{1,3},{2,0},{3,1},{4,6},{5,7},{6,4},{7,5},{8,10},{9,11},{10,... | collective-permute-start | bytes 294920 | tf_op jit(solution)/shard_map/ppermute | solution.py:194
  97.7 7.9 %collective-permute-start.32 = (f32[32,768]{1,0:T(8,128)S(1)}, f32[32,768]{1,0:T(8,128)S(1)}, u32[]{:S(2)}, u32[]{:S(2)}) collective-permute-start(f32[32,768]{1,0:T(8,128)S(1)} %shard_map.224.refs_0_.refs_5_), channel_id=1, source_target_pairs={{0,2},{1,3},{2,0},{3,1},{4,8},{5,9},{6,10},{7,11},{8,4},{9,5},{10,... | collective-permute-start | bytes 294920 | tf_op jit(solution)/shard_map/ppermute | solution.py:194
  104.9 4.7 %collective-permute-start.33 = (f32[32,768]{1,0:T(8,128)S(1)}, f32[32,768]{1,0:T(8,128)S(1)}, u32[]{:S(2)}, u32[]{:S(2)}) collective-permute-start(f32[32,768]{1,0:T(8,128)S(1)} %shard_map.224.refs_0_.refs_5_), channel_id=1, source_target_pairs={{0,2},{1,3},{2,0},{3,1},{4,10},{5,11},{6,8},{7,9},{8,6},{9,7},{10,... | collective-permute-start | bytes 294920 | tf_op jit(solution)/shard_map/ppermute | solution.py:194
  105.7 4.9 %collective-permute-start.29 = (f32[32,768]{1,0:T(8,128)S(1)}, f32[32,768]{1,0:T(8,128)S(1)}, u32[]{:S(2)}, u32[]{:S(2)}) collective-permute-start(f32[32,768]{1,0:T(8,128)S(1)} %shard_map.226.refs_2_), channel_id=1, source_target_pairs={{0,2},{1,3},{2,0},{3,1},{4,6},{5,7},{6,4},{7,5},{8,10},{9,11},{10,... | collective-permute-start | bytes 294920 | tf_op jit(solution)/shard_map/ppermute | solution.py:194
  109.6 6.3 %collective-permute-start.30 = (f32[32,768]{1,0:T(8,128)S(1)}, f32[32,768]{1,0:T(8,128)S(1)}, u32[]{:S(2)}, u32[]{:S(2)}) collective-permute-start(f32[32,768]{1,0:T(8,128)S(1)} %shard_map.226.refs_2_), channel_id=1, source_target_pairs={{0,4},{1,5},{2,6},{3,7},{4,0},{5,1},{6,2},{7,3},{8,12},{9,13},{10,... | collective-permute-start | bytes 294920 | tf_op jit(solution)/shard_map/ppermute | solution.py:194
  110.6 5.5 %collective-permute-start.31 = (f32[32,768]{1,0:T(8,128)S(1)}, f32[32,768]{1,0:T(8,128)S(1)}, u32[]{:S(2)}, u32[]{:S(2)}) collective-permute-start(f32[32,768]{1,0:T(8,128)S(1)} %shard_map.226.refs_2_), channel_id=1, source_target_pairs={{0,6},{1,7},{2,4},{3,5},{4,2},{5,3},{6,0},{7,1},{8,14},{9,15},{10,... | collective-permute-start | bytes 294920 | tf_op jit(solution)/shard_map/ppermute | solution.py:194
  111.8 11.5 %collective-permute-start.38 = (f32[32,384]{1,0:T(8,128)S(1)}, f32[32,384]{1,0:T(8,128)S(1)}, u32[]{:S(2)}, u32[]{:S(2)}) collective-permute-start(f32[32,384]{1,0:T(8,128)S(1)} %constant_dynamic-slice_fusion), channel_id=1, source_target_pairs={{0,1},{1,0},{2,3},{3,2},{4,5},{5,4},{6,7},{7,6},{8,9},{9,8},{10,11... | collective-permute-start | bytes 147464 | tf_op jit(solution)/shard_map/ppermute | solution.py:194
  115.8 11.0 %copy-start.9 = (f32[1,512,2048]{2,1,0:T(8,128)S(1)}, f32[1,512,2048]{2,1,0:T(8,128)}, u32[]{:S(2)}) copy-start(f32[1,512,2048]{2,1,0:T(8,128)} %param.30) | copy-start | bytes 12582916
  121.1 5.7 %collective-permute-start.35 = (f32[32,1024]{1,0:T(8,128)S(1)}, f32[32,1024]{1,0:T(8,128)S(1)}, u32[]{:S(2)}, u32[]{:S(2)}) collective-permute-start(f32[32,1024]{1,0:T(8,128)S(1)} %shard_map.227.refs_0_), channel_id=1, source_target_pairs={{0,2},{1,3},{2,0},{3,1},{4,6},{5,7},{6,4},{7,5},{8,10},{9,11},{10,... | collective-permute-start | bytes 393224 | tf_op jit(solution)/shard_map/ppermute | solution.py:194
  123.4 9.6 %copy-start.13 = (f32[1,512,64]{1,2,0:T(8,128)S(1)}, f32[1,512,64]{1,2,0:T(8,128)}, u32[]{:S(2)}) copy-start(f32[1,512,64]{1,2,0:T(8,128)} %param.26) | copy-start | bytes 393220
  123.4 9.6 %copy-start.14 = (f32[1,512,64]{1,2,0:T(8,128)S(1)}, f32[1,512,64]{1,2,0:T(8,128)}, u32[]{:S(2)}) copy-start(f32[1,512,64]{1,2,0:T(8,128)} %param.25) | copy-start | bytes 393220
  131.7 1.3 collective-permute-start.37
  (15 other events, 65.7 us)

commit v3 on v2

--- a/solution.py
+++ b/solution.py
@@ -33,27 +33,59 @@
     return total
 
 
-def times_rows(left, *refs):
-    left = stacked(left)
-    count = refs[0].shape[0]
-    ends = count * len(refs)
-    columns = []
-    for start in range(0, ends, TILE):
-        stop = min(start + TILE, ends)
-        blocks = []
-        for i, ref in enumerate(refs):
-            low, high = max(start - i * count, 0), min(stop - i * count, count)
-            if low < high:
-                blocks.append(ref[low:high, :])
-        columns.append(matmul(left, jnp.concatenate(blocks, axis=0), 1))
-    return jnp.concatenate(columns, axis=1)
-
-
-def times(left, ref):
-    left = stacked(left)
-    width = ref.shape[1]
-    columns = [matmul(left, ref[:, n : min(n + TILE, width)], 0) for n in range(0, width, TILE)]
-    return jnp.concatenate(columns, axis=1)
+class Rows:
+    def __init__(self, refs, buffer, sems, first_sem=0):
+        self.buffer, self.blocks = buffer, []
+        count = refs[0].shape[0]
+        self.ends = count * len(refs)
+        for start in range(0, self.ends, TILE):
+            stop = min(start + TILE, self.ends)
+            copies = []
+            for i, ref in enumerate(refs):
+                low, high = max(start - i * count, 0), min(stop - i * count, count)
+                if low < high:
+                    copies.append(
+                        pltpu.make_async_copy(
+                            ref.at[pl.ds(low, high - low), :],
+                            buffer.at[pl.ds(low + i * count, high - low), :],
+                            sems.at[first_sem],
+                        )
+                    )
+                    first_sem += 1
+            self.blocks.append((start, stop, copies))
+        self.next_sem = first_sem
+
+    def start(self):
+        for _, _, copies in self.blocks:
+            for copy in copies:
+                copy.start()
+
+    def times(self, left):
+        left = stacked(left)
+        columns = []
+        for start, stop, copies in self.blocks:
+            for copy in copies:
+                copy.wait()
+            columns.append(matmul(left, self.buffer[start:stop, :], 1))
+        return jnp.concatenate(columns, axis=1)
+
+    def weigh(self, left):
+        total = None
+        for start, stop, copies in self.blocks:
+            for copy in copies:
+                copy.wait()
+            part = matmul(stacked(left[:, start:stop]), self.buffer[start:stop, :], 0)
+            total = part if total is None else total + part
+        return total
+
+
+def fetches(count, matrices):
+    return sum(
+        1
+        for start in range(0, count * matrices, TILE)
+        for i in range(matrices)
+        if max(start, i * count) < min(start + TILE, (i + 1) * count)
+    )
 
 
 def in_order(pieces, own):
@@ -77,29 +109,44 @@
     ref[...] = jnp.concatenate([jnp.where(swap, other, own), jnp.where(swap, own, other)], axis=1)
 
 
-def call(kernel, shapes, *groups):
-    flat = [value for group in groups for value in group]
+def call(kernel, shapes, matrices, *groups):
+    flat = [value for group in matrices for value in group]
+    arrays = [value for group in groups for value in group]
+    outs = len(shapes)
+    buffers, sems = [], 0
+    for group in matrices:
+        count, width = group[0].shape
+        buffers.append(pltpu.VMEM((count * len(group), width), jnp.float32))
+        sems += fetches(count, len(group))
+    scratch = buffers + [pltpu.SemaphoreType.DMA((sems,))] if matrices else []
 
     def body(*refs):
-        at, parts = 0, []
+        at, rows, parts, sem = 0, [], [], 0
+        held = refs[len(flat) + len(arrays) + outs :]
+        for i, group in enumerate(matrices):
+            rows.append(Rows(refs[at : at + len(group)], held[i], held[-1], sem))
+            sem = rows[-1].next_sem
+            at += len(group)
         for group in groups:
             parts.append(refs[at : at + len(group)])
             at += len(group)
-        kernel(*parts, *refs[at:])
+        kernel(*rows, *parts, *refs[at : at + outs])
 
     out = [jax.ShapeDtypeStruct(shape, jnp.float32) for shape in shapes]
     return pl.pallas_call(
         body,
-        in_specs=[VMEM] * len(flat),
-        out_specs=[VMEM] * len(out),
+        in_specs=[pl.BlockSpec(memory_space=pl.ANY)] * len(flat) + [VMEM] * len(arrays),
+        out_specs=[VMEM] * outs,
         out_shape=out,
-        compiler_params=pltpu.CompilerParams(vmem_limit_bytes=40 << 20),
-    )(*flat)
-
-
-def forces_kernel(swap_chips, pieces, matrices, mine, theirs):
-    inverse, above, below = matrices
-    if swap_chips:
+        scratch_shapes=scratch,
+        compiler_params=pltpu.CompilerParams(vmem_limit_bytes=24 << 20),
+    )(*flat, *arrays)
+
+
+def forces_kernel(aligned, inverse, above, below, pieces, mine, theirs):
+    for rows in (inverse, above, below):
+        rows.start()
+    if aligned:
         chips = len(pieces) // 2
         core = lax.axis_index("blk")
         sets = [in_order([pieces[2 * j][...], pieces[2 * j + 1][...]], core) for j in range(chips)]
@@ -107,11 +154,11 @@
         full = jnp.concatenate(in_order(sets, lax.axis_index("rec")), axis=1)
     else:
         full = pieces[0][...]
-    part = times_rows(full, inverse)
+    part = inverse.times(full)
     half = part.shape[0] // 2
     second = lax.axis_index("blk") == 1
-    for i, matrix in enumerate((above, below)):
-        force = times(part, matrix)
+    for i, rows in enumerate((above, below)):
+        force = rows.weigh(part)
         mine[i] = jnp.where(second, force[half:], force[:half])
         theirs[i] = jnp.where(second, force[:half], force[half:])
 
@@ -127,12 +174,13 @@
             outs[i * chips + j][...] = piece
 
 
-def step_kernel(story, pieces, rows, terms, out):
+def step_kernel(story, rows, pieces, terms, out):
     first, latest = terms
 
     @pl.when(lax.axis_index("story") == story)
     def _():
-        store_rows(out, times_rows(joined(pieces), *rows))
+        rows.start()
+        store_rows(out, rows.times(joined(pieces)))
         out[...] = first[...] - out[...]
 
     @pl.when(lax.axis_index("story") != story)
@@ -140,30 +188,34 @@
         out[...] = latest[...]
 
 
-def rows_kernel(pieces, rows, out):
-    store_rows(out, times_rows(joined(pieces), *rows))
-
-
-def coupled_kernel(load, early, here, even, odd, above, below, out):
+def rows_kernel(rows, pieces, out):
+    rows.start()
+    store_rows(out, rows.times(joined(pieces)))
+
+
+def coupled_kernel(above, below, load, early, here, even, odd, out):
     story = lax.axis_index("story")
 
     @pl.when(story == 0)
     def _():
-        store_rows(out, times_rows(joined(here), *above))
+        above.start()
+        store_rows(out, above.times(joined(here)))
         out[...] = load[0][...] - out[...]
 
     @pl.when(story > 0)
     def _():
+        below.start()
         use = lax.rem(story, 2) == 1
         refs = [jnp.where(use, e[...], o[...]) for e, o in zip(even, odd)]
         own = lax.axis_index("rec") if len(refs) > 1 else 0
         value = jnp.concatenate(in_order(refs, own), axis=1)
-        store_rows(out, times_rows(value, *below))
+        store_rows(out, below.times(value))
         out[...] = load[0][...] - early[0][...] - out[...]
 
 
-def last_kernel(pieces, rows, mine, theirs):
-    value = times_rows(joined(pieces), *rows)
+def last_kernel(rows, pieces, mine, theirs):
+    rows.start()
+    value = rows.times(joined(pieces))
     half = value.shape[1] // 2
     mine[...] = value[:, :half]
     theirs[...] = value[:, half:]
@@ -294,25 +346,30 @@
     mine, theirs = call(
         functools.partial(forces_kernel, aligned),
         [(2, half, faces)] * 2,
+        [[interior_inverse[0]], [couple_above[0]], [couple_below[0]]],
         pieces,
-        [interior_inverse[0], couple_above[0], couple_below[0]],
     )
     chunks = call(
         chunks_kernel,
         [(half, faces // mv.chips)] * (2 * mv.chips),
+        [],
         [mine, mv.core(theirs)],
     )
     above_force = chunks[0]
     for j in range(1, mv.chips):
         above_force = above_force + mv.chip(chunks[j], j)
-    below_force = []
-    for parity in range(2):
-        total = mv.story(chunks[mv.chips], parity, 0)
+
+    def from_above(parts, parity):
+        total = mv.story(parts[0], parity, 0)
         for j in range(1, mv.chips):
-            total = total + mv.story(chunks[mv.chips + j], parity, j)
-        below_force.append(total)
+            total = total + mv.story(parts[j], parity, j)
+        return total
+
     condensed = mv.to_half(load_face) - above_force
-    condensed = jnp.where((s % 2 == 0) & (s != last), condensed - below_force[0], condensed)
+    below_parts = chunks[mv.chips :]
+    below_force = from_above(below_parts, 0)
+    condensed = jnp.where((s % 2 == 0) & (s != last), condensed - below_force, condensed)
+    condensed, *below_parts = lax.optimization_barrier([condensed, *below_parts])
 
     lower_rows, pivot_rows, upper_rows = chip_rows(lower), chip_rows(pivot), chip_rows(upper)
     shape = [(half, rows_face)]
@@ -320,11 +377,12 @@
     for k in range(1, mv.stories):
         came = mv.gather_story(forward, (k - 1) % 2)
         if k == 1:
-            condensed = jnp.where((s % 2 == 1) & (s != last), condensed - below_force[1], condensed)
+            below_force = from_above(below_parts, 1)
+            condensed = jnp.where((s % 2 == 1) & (s != last), condensed - below_force, condensed)
         (forward,) = call(
-            functools.partial(step_kernel, k), shape, came, lower_rows, [condensed, forward]
+            functools.partial(step_kernel, k), shape, [lower_rows], came, [condensed, forward]
         )
-    (pivoted,) = call(rows_kernel, shape, mv.gather_chips(forward), pivot_rows)
+    (pivoted,) = call(rows_kernel, shape, [pivot_rows], mv.gather_chips(forward))
 
     below_rows, above_rows = chip_rows(couple_below), chip_rows(couple_above)
     inverse_rows = chip_rows(interior_inverse)
@@ -334,26 +392,28 @@
         came = mv.gather_story(face, k % 2)
         if k == 0:
             odd = mv.gather_story(face, 1)
-            (early,) = call(rows_kernel, shape_int, mv.gather_chips(face), above_rows)
-        (face,) = call(functools.partial(step_kernel, k), shape, came, upper_rows, [pivoted, face])
+            (early,) = call(rows_kernel, shape_int, [above_rows], mv.gather_chips(face))
+            *came, early = lax.optimization_barrier([*came, early])
+        (face,) = call(
+            functools.partial(step_kernel, k), shape, [upper_rows], came, [pivoted, face]
+        )
 
     even = mv.gather_story(face, 0)
     (reduced,) = call(
         coupled_kernel,
         shape_int,
+        [above_rows, below_rows],
         [mv.to_half(load_int)],
         [early],
         mv.gather_chips(face),
         even,
         odd,
-        above_rows,
-        below_rows,
     )
     mine, theirs = call(
         last_kernel,
         [(half, rows_int // 2)] * 2,
+        [inverse_rows],
         mv.gather_chips(reduced),
-        inverse_rows,
     )
 
     u_f = mv.from_half(face)

time: 134 us -> 139 us (1.037)
  starting transfers between devices: 40.5 us -> 52.3 us
  local copies, waits for them, and re-layouts: 9.4 us -> 3.66 us
  waiting for transfers between devices: 50.2 us -> 46.2 us
  Pallas kernels: 27 us -> 28.9 us
    ppermute x39, starting transfers between devices: 40.5 us -> 52.3 us  [permute(): return lax.ppermute(value, AXES, pairs)]
    unnamed x48 -> x34, local copies, waits for them, and re-layouts: 9.38 us -> 3.63 us
    ppermute x39, waiting for transfers between devices: 50.2 us -> 46.2 us  [permute(): return lax.ppermute(value, AXES, pairs)]
    pallas_call x12, Pallas kernels: 27 us -> 28.9 us  [call(): pl.pallas_call(body, in_specs=[pl.BlockSpec(memory_space=pl.ANY)] * len(f...]
  transfers between devices with their start and end apart: 39 -> 39, of which waited for: 24 -> 23; matrix products, arithmetic and copies ran while one was open for 4% -> 4% of each run, Pallas kernels for 17% -> 16%
where the time goes in v3:
time: 139 us
  starting transfers between devices  52.3 us (38%)
  waiting for transfers between devices  46.2 us (33%)
  Pallas kernels  28.9 us (21%)
  other arithmetic  6.9 us (5%)
  local copies, waits for them, and re-layouts  3.66 us (3%)
    ppermute x39, starting transfers between devices, permute(): return lax.ppermute(value, AXES, pairs)  52.3 us
    ppermute x39, waiting for transfers between devices, permute(): return lax.ppermute(value, AXES, pairs)  46.2 us
    pallas_call x12, Pallas kernels, call(): pl.pallas_call(body, in_specs=[pl.BlockSpec(memory_space=pl.ANY)] * len(f...  28.9 us
    unnamed x34, local copies, waits for them, and re-layouts  3.63 us
  transfers between devices with their start and end apart: 39, of which 23 were waited for; matrix products, arithmetic and copies ran while one was open for 4% of the time, Pallas kernels for 16%

profile of v3, /device:TPU:0, one launch (start us, length us, event | category | flops | bytes accessed | tf_op | source)
XLA Modules:
  0.0 138.9 jit_solution(2206450239821261689)
XLA Ops:
  2.0 1.1 fusion.2.refs_3_
  3.2 2.6 %collective-permute-start.9 = (f32[64,512]{1,0:T(8,128)S(1)}, f32[64,512]{1,0:T(8,128)S(1)}, u32[]{:S(2)}, u32[]{:S(2)}) collective-permute-start(f32[64,512]{1,0:T(8,128)S(1)} %fusion.2.refs_3_), channel_id=1, source_target_pairs={{0,2},{1,3},{2,0},{3,1},{4,6},{5,7},{6,4},{7,5},{8,10},{9,11},{10,... | collective-permute-start | bytes 393224 | tf_op jit(solution)/shard_map/ppermute | solution.py:246
  5.9 3.9 %collective-permute-done.9.refs_5_ = f32[64,512]{1,0:T(8,128)S(1)} collective-permute-done((f32[64,512]{1,0:T(8,128)S(1)}, f32[64,512]{1,0:T(8,128)S(1)}, u32[]{:S(2)}, u32[]{:S(2)}) %collective-permute-start.9) | collective-permute-done | bytes 131104 | tf_op jit(solution)/shard_map/ppermute | solution.py:246
  11.3 1.9 %copy-done = f32[1,512,1536]{2,1,0:T(8,128)S(1)} copy-done((f32[1,512,1536]{2,1,0:T(8,128)S(1)}, f32[1,512,1536]{2,1,0:T(8,128)}, u32[]{:S(2)}) %copy-start) | copy-done | bytes 3145752
  13.2 5.8 %shard_map.217 = (f32[2,32,1536]{2,1,0:T(8,128)S(1)}, f32[2,32,1536]{2,1,0:T(8,128)S(1)}) custom-call(f32[512,2048]{1,0:T(8,128)} %bitcast.refs_0_, f32[512,1536]{1,0:T(8,128)S(1)} %bitcast.124, f32[512,1536]{1,0:T(8,128)} %bitcast.2.refs_2_, f32[64,512]{1,0:T(8,128)S(1)} %fusion.2.refs_3_, f32[64,512]{1,0:T(8,128)S(1)} %collective-permute-done.8.refs_4_, ...), custom_call_target="tpu_custom_call" | custom-call | tf_op jit(solution)/shard_map/pallas_call | solution.py:136
  21.6 1.9 %collective-permute-start.13 = (f32[32,768]{1,0:T(8,128)}, f32[32,768]{1,0:T(8,128)S(1)}, u32[]{:S(2)}, u32[]{:S(2)}) collective-permute-start(f32[32,768]{1,0:T(8,128)} %get-tuple-element.27), channel_id=1, source_target_pairs={{0,4},{1,5},{2,6},{3,7},{4,0},{5,1},{6,2},{7,3},{8,12},{9,13},{10,... | collective-permute-start | bytes 294920 | tf_op jit(solution)/shard_map/ppermute | solution.py:246
  23.5 1.4 collective-permute-start.14
  25.2 1.8 %collective-permute-done.13 = f32[32,768]{1,0:T(8,128)S(1)} collective-permute-done((f32[32,768]{1,0:T(8,128)}, f32[32,768]{1,0:T(8,128)S(1)}, u32[]{:S(2)}, u32[]{:S(2)}) %collective-permute-start.13) | collective-permute-done | bytes 98336 | tf_op jit(solution)/shard_map/ppermute | solution.py:246
  27.0 3.3 %collective-permute-done.14 = f32[32,768]{1,0:T(8,128)S(1)} collective-permute-done((f32[32,768]{1,0:T(8,128)S(1)}, f32[32,768]{1,0:T(8,128)S(1)}, u32[]{:S(2)}, u32[]{:S(2)}) %collective-permute-start.14) | collective-permute-done | bytes 98336 | tf_op jit(solution)/shard_map/ppermute | solution.py:246
  30.3 1.2 collective-permute-done.12
  32.0 1.6 %collective-permute-start.18 = (f32[32,768]{1,0:T(8,128)S(1)}, f32[32,768]{1,0:T(8,128)}, u32[]{:S(2)}, u32[]{:S(2)}) collective-permute-start(f32[32,768]{1,0:T(8,128)S(1)} %get-tuple-element.28), channel_id=1, source_target_pairs={{0,2},{1,3},{2,0},{3,1},{4,10},{5,11},{6,8},{7,9},{8,6},{9,7},{10,... | collective-permute-start | bytes 294920 | tf_op jit(solution)/shard_map/ppermute | solution.py:246
  33.6 1.6 %collective-permute-start.15 = (f32[32,768]{1,0:T(8,128)S(1)}, f32[32,768]{1,0:T(8,128)S(1)}, u32[]{:S(2)}, u32[]{:S(2)}) collective-permute-start(f32[32,768]{1,0:T(8,128)S(1)} %subtract_select_fusion.1.refs_5_), channel_id=1, source_target_pairs={{0,4},{1,5},{2,6},{3,7},{4,0},{5,1},{6,2},{7,3},{8,12},{9,13},{10,... | collective-permute-start | bytes 294920 | tf_op jit(solution)/shard_map/ppermute | solution.py:246
  35.2 1.8 %collective-permute-done.17 = f32[32,768]{1,0:T(8,128)} collective-permute-done((f32[32,768]{1,0:T(8,128)}, f32[32,768]{1,0:T(8,128)}, u32[]{:S(2)}, u32[]{:S(2)}) %collective-permute-start.17) | collective-permute-done | bytes 98336 | tf_op jit(solution)/shard_map/ppermute | solution.py:246
  37.0 1.8 %collective-permute-start.16 = (f32[32,768]{1,0:T(8,128)S(1)}, f32[32,768]{1,0:T(8,128)S(1)}, u32[]{:S(2)}, u32[]{:S(2)}) collective-permute-start(f32[32,768]{1,0:T(8,128)S(1)} %subtract_select_fusion.1.refs_5_), channel_id=1, source_target_pairs={{0,6},{1,7},{2,4},{3,5},{4,2},{5,3},{6,0},{7,1},{8,14},{9,15},{10,... | collective-permute-start | bytes 294920 | tf_op jit(solution)/shard_map/ppermute | solution.py:246
  39.8 2.7 %collective-permute-done.16.refs_3_ = f32[32,768]{1,0:T(8,128)S(1)} collective-permute-done((f32[32,768]{1,0:T(8,128)S(1)}, f32[32,768]{1,0:T(8,128)S(1)}, u32[]{:S(2)}, u32[]{:S(2)}) %collective-permute-start.16) | collective-permute-done | bytes 98336 | tf_op jit(solution)/shard_map/ppermute | solution.py:246
  42.5 1.7 %copy-done.2 = f32[1,384,1536]{2,1,0:T(8,128)S(1)} copy-done((f32[1,384,1536]{2,1,0:T(8,128)S(1)}, f32[1,384,1536]{2,1,0:T(8,128)}, u32[]{:S(2)}) %copy-start.2) | copy-done | bytes 2359320
  44.8 1.5 %collective-permute-start.20 = (f32[32,768]{1,0:T(8,128)S(1)}, f32[32,768]{1,0:T(8,128)S(1)}, u32[]{:S(2)}, u32[]{:S(2)}) collective-permute-start(f32[32,768]{1,0:T(8,128)S(1)} %shard_map.219.refs_5_), channel_id=1, source_target_pairs={{0,2},{1,3},{2,0},{3,1},{4,10},{5,11},{6,8},{7,9},{8,6},{9,7},{10,... | collective-permute-start | bytes 294920 | tf_op jit(solution)/shard_map/ppermute | solution.py:246
  46.4 2.6 %collective-permute-done.19.refs_2_ = f32[32,768]{1,0:T(8,128)S(1)} collective-permute-done((f32[32,768]{1,0:T(8,128)S(1)}, f32[32,768]{1,0:T(8,128)S(1)}, u32[]{:S(2)}, u32[]{:S(2)}) %collective-permute-start.19) | collective-permute-done | bytes 98336 | tf_op jit(solution)/shard_map/ppermute | solution.py:246
  48.9 1.1 collective-permute-done.20.refs_3_
  50.0 5.1 %collective-permute-start.21 = (f32[32,768]{1,0:T(8,128)S(1)}, f32[32,768]{1,0:T(8,128)S(1)}, u32[]{:S(2)}, u32[]{:S(2)}) collective-permute-start(f32[32,768]{1,0:T(8,128)S(1)} %shard_map.220.refs_5_), channel_id=1, source_target_pairs={{0,4},{1,5},{2,6},{3,7},{4,0},{5,1},{6,2},{7,3},{8,12},{9,13},{10,... | collective-permute-start | bytes 294920 | tf_op jit(solution)/shard_map/ppermute | solution.py:246
  56.0 2.0 %collective-permute-done.21.refs_2_ = f32[32,768]{1,0:T(8,128)S(1)} collective-permute-done((f32[32,768]{1,0:T(8,128)S(1)}, f32[32,768]{1,0:T(8,128)S(1)}, u32[]{:S(2)}, u32[]{:S(2)}) %collective-permute-start.21) | collective-permute-done | bytes 98336 | tf_op jit(solution)/shard_map/ppermute | solution.py:246
  58.0 3.2 %collective-permute-done.22.refs_3_ = f32[32,768]{1,0:T(8,128)S(1)} collective-permute-done((f32[32,768]{1,0:T(8,128)S(1)}, f32[32,768]{1,0:T(8,128)S(1)}, u32[]{:S(2)}, u32[]{:S(2)}) %collective-permute-start.22) | collective-permute-done | bytes 98336 | tf_op jit(solution)/shard_map/ppermute | solution.py:246
  61.3 1.3 collective-permute-start.23
  62.6 4.0 %collective-permute-done.23.refs_3_ = f32[32,768]{1,0:T(8,128)S(1)} collective-permute-done((f32[32,768]{1,0:T(8,128)S(1)}, f32[32,768]{1,0:T(8,128)S(1)}, u32[]{:S(2)}, u32[]{:S(2)}) %collective-permute-start.23) | collective-permute-done | bytes 98336 | tf_op jit(solution)/shard_map/ppermute | solution.py:246
  66.6 3.0 %shard_map.222.refs_4_.refs_5_ = f32[32,768]{1,0:T(8,128)S(1)} custom-call(f32[384,1536]{1,0:T(8,128)S(1)} %bitcast.137, f32[384,1536]{1,0:T(8,128)S(1)} %collective-permute-done.5.refs_1_, f32[32,768]{1,0:T(8,128)S(1)} %shard_map.221.refs_2_, f32[32,768]{1,0:T(8,128)S(1)} %collective-permute-done.23.refs_3_), custom_call_target="tpu_custom_call" | custom-call | tf_op jit(solution)/shard_map/pallas_call | solution.py:136
  69.6 1.2 collective-permute-start.24
  70.8 1.6 %collective-permute-start.25 = (f32[32,768]{1,0:T(8,128)S(1)}, f32[32,768]{1,0:T(8,128)S(1)}, u32[]{:S(2)}, u32[]{:S(2)}) collective-permute-start(f32[32,768]{1,0:T(8,128)S(1)} %shard_map.222.refs_4_.refs_5_), channel_id=1, source_target_pairs={{0,6},{1,7},{2,4},{3,5},{4,2},{5,3},{6,0},{7,1},{8,14},{9,15},{10,... | collective-permute-start | bytes 294920 | tf_op jit(solution)/shard_map/ppermute | solution.py:246
  72.3 3.0 %collective-permute-done.24.refs_2_ = f32[32,768]{1,0:T(8,128)S(1)} collective-permute-done((f32[32,768]{1,0:T(8,128)S(1)}, f32[32,768]{1,0:T(8,128)S(1)}, u32[]{:S(2)}, u32[]{:S(2)}) %collective-permute-start.24) | collective-permute-done | bytes 98336 | tf_op jit(solution)/shard_map/ppermute | solution.py:246
  75.3 1.6 %collective-permute-done.25.refs_3_ = f32[32,768]{1,0:T(8,128)S(1)} collective-permute-done((f32[32,768]{1,0:T(8,128)S(1)}, f32[32,768]{1,0:T(8,128)S(1)}, u32[]{:S(2)}, u32[]{:S(2)}) %collective-permute-start.25) | collective-permute-done | bytes 98336 | tf_op jit(solution)/shard_map/ppermute | solution.py:246
  77.0 1.0 collective-permute-start.26
  77.9 1.1 collective-permute-start.27
  79.0 2.6 %collective-permute-done.26.refs_2_ = f32[32,768]{1,0:T(8,128)S(1)} collective-permute-done((f32[32,768]{1,0:T(8,128)S(1)}, f32[32,768]{1,0:T(8,128)S(1)}, u32[]{:S(2)}, u32[]{:S(2)}) %collective-permute-start.26) | collective-permute-done | bytes 98336 | tf_op jit(solution)/shard_map/ppermute | solution.py:246
  81.6 1.1 collective-permute-done.27.refs_3_
  82.7 1.0 collective-permute-start.30
  83.8 1.4 collective-permute-done.3
  85.2 13.9 %collective-permute-start.28 = (f32[32,768]{1,0:T(8,128)S(1)}, f32[32,768]{1,0:T(8,128)S(1)}, u32[]{:S(2)}, u32[]{:S(2)}) collective-permute-start(f32[32,768]{1,0:T(8,128)S(1)} %shard_map.224.refs_2_.refs_5_), channel_id=1, source_target_pairs={{0,4},{1,5},{2,6},{3,7},{4,0},{5,1},{6,2},{7,3},{8,12},{9,13},{10,... | collective-permute-start | bytes 294920 | tf_op jit(solution)/shard_map/ppermute | solution.py:246
  99.1 2.8 %collective-permute-start.29 = (f32[32,768]{1,0:T(8,128)S(1)}, f32[32,768]{1,0:T(8,128)S(1)}, u32[]{:S(2)}, u32[]{:S(2)}) collective-permute-start(f32[32,768]{1,0:T(8,128)S(1)} %shard_map.224.refs_2_.refs_5_), channel_id=1, source_target_pairs={{0,6},{1,7},{2,4},{3,5},{4,2},{5,3},{6,0},{7,1},{8,14},{9,15},{10,... | collective-permute-start | bytes 294920 | tf_op jit(solution)/shard_map/ppermute | solution.py:246
  102.7 1.3 collective-permute-start.34
  104.0 5.2 %shard_map.225.refs_5_ = f32[32,1024]{1,0:T(8,128)S(1)} custom-call(f32[512,1536]{1,0:T(8,128)S(1)} %bitcast.126, f32[512,1536]{1,0:T(8,128)} %collective-permute-done.1.refs_1_, f32[32,768]{1,0:T(8,128)S(1)} %shard_map.224.refs_2_.refs_5_, f32[32,768]{1,0:T(8,128)} %collective-permute-done.30.refs_3_), custom_call_target="tpu_custom_call" | custom-call | tf_op jit(solution)/shard_map/pallas_call | solution.py:136
  109.2 1.2 collective-permute-start.35
  110.4 3.0 %shard_map.226.refs_6_ = f32[32,768]{1,0:T(8,128)S(1)} custom-call(f32[384,1536]{1,0:T(8,128)S(1)} %bitcast.135, f32[384,1536]{1,0:T(8,128)S(1)} %copy-done.6, f32[32,768]{1,0:T(8,128)S(1)} %collective-permute-done.28.refs_2_, f32[32,768]{1,0:T(8,128)S(1)} %collective-permute-done.29.refs_3_, f32[32,768]{1,0:T(8,128)S(1)} %shard_map.222.refs_4_.refs_5_, ...), custom_call_target="tpu_custom_call" | custom-call | tf_op jit(solution)/shard_map/pallas_call | solution.py:136
  114.7 2.4 %collective-permute-start.33 = (f32[32,768]{1,0:T(8,128)S(1)}, f32[32,768]{1,0:T(8,128)S(1)}, u32[]{:S(2)}, u32[]{:S(2)}) collective-permute-start(f32[32,768]{1,0:T(8,128)S(1)} %shard_map.226.refs_6_), channel_id=1, source_target_pairs={{0,6},{1,7},{2,4},{3,5},{4,2},{5,3},{6,0},{7,1},{8,14},{9,15},{10,... | collective-permute-start | bytes 294920 | tf_op jit(solution)/shard_map/ppermute | solution.py:246
  117.1 1.0 collective-permute-done.31.refs_7_
  119.1 1.6 %collective-permute-done.33.refs_9_ = f32[32,768]{1,0:T(8,128)S(1)} collective-permute-done((f32[32,768]{1,0:T(8,128)S(1)}, f32[32,768]{1,0:T(8,128)S(1)}, u32[]{:S(2)}, u32[]{:S(2)}) %collective-permute-start.33) | collective-permute-done | bytes 98336 | tf_op jit(solution)/shard_map/ppermute | solution.py:246
  120.7 4.4 %shard_map.227.refs_2_ = f32[32,1024]{1,0:T(8,128)S(1)} custom-call(f32[512,1536]{1,0:T(8,128)S(1)} %bitcast.127, f32[512,1536]{1,0:T(8,128)} %collective-permute-done.1.refs_1_, f32[512,1536]{1,0:T(8,128)} %bitcast.2.refs_2_, f32[512,1536]{1,0:T(8,128)} %collective-permute-done.2.refs_3_, f32[32,1024]{1,0:T(8,128)S(1)} %pad_maximum_fusion.refs_4_, ...), custom_call_target="tpu_custom_call" | custom-call | tf_op jit(solution)/shard_map/pallas_call | solution.py:136
  125.1 1.0 collective-permute-start.36
  126.1 4.0 %collective-permute-done.36.refs_3_ = f32[32,1024]{1,0:T(8,128)S(1)} collective-permute-done((f32[32,1024]{1,0:T(8,128)S(1)}, f32[32,1024]{1,0:T(8,128)S(1)}, u32[]{:S(2)}, u32[]{:S(2)}) %collective-permute-start.36) | collective-permute-done | bytes 131104 | tf_op jit(solution)/shard_map/ppermute | solution.py:246
  130.1 6.7 %shard_map.228 = (f32[32,512]{1,0:T(8,128)S(1)}, f32[32,512]{1,0:T(8,128)S(1)}) custom-call(f32[512,2048]{1,0:T(8,128)} %bitcast.refs_0_, f32[512,2048]{1,0:T(8,128)} %collective-permute-done.refs_1_, f32[32,1024]{1,0:T(8,128)S(1)} %shard_map.227.refs_2_, f32[32,1024]{1,0:T(8,128)S(1)} %collective-permute-done.36.refs_3_), custom_call_target="tpu_custom_call" | custom-call | tf_op jit(solution)/shard_map/pallas_call | solution.py:136
  (93 shorter events, 14.2 us)
Async XLA Ops:
  0.6 41.9 %collective-permute-start.6 = (f32[384,1536]{1,0:T(8,128)}, f32[384,1536]{1,0:T(8,128)}, u32[]{:S(2)}, u32[]{:S(2)}) collective-permute-start(f32[384,1536]{1,0:T(8,128)} %bitcast.128), channel_id=1, source_target_pairs={{0,1},{1,0},{2,3},{3,2},{4,5},{5,4},{6,7},{7,6},{8,9},{9,8},{10,11... | collective-permute-start | bytes 7077896 | tf_op jit(solution)/shard_map/ppermute | solution.py:246
  3.2 6.7 %collective-permute-start.9 = (f32[64,512]{1,0:T(8,128)S(1)}, f32[64,512]{1,0:T(8,128)S(1)}, u32[]{:S(2)}, u32[]{:S(2)}) collective-permute-start(f32[64,512]{1,0:T(8,128)S(1)} %fusion.2.refs_3_), channel_id=1, source_target_pairs={{0,2},{1,3},{2,0},{3,1},{4,6},{5,7},{6,4},{7,5},{8,10},{9,11},{10,... | collective-permute-start | bytes 393224 | tf_op jit(solution)/shard_map/ppermute | solution.py:246
  5.7 5.6 %collective-permute-start.8 = (f32[64,512]{1,0:T(8,128)S(1)}, f32[64,512]{1,0:T(8,128)S(1)}, u32[]{:S(2)}, u32[]{:S(2)}) collective-permute-start(f32[64,512]{1,0:T(8,128)S(1)} %fusion.2.refs_3_), channel_id=1, source_target_pairs={{0,1},{1,0},{2,3},{3,2},{4,5},{5,4},{6,7},{7,6},{8,9},{9,8},{10,11... | collective-permute-start | bytes 393224 | tf_op jit(solution)/shard_map/ppermute | solution.py:246
  9.9 1.4 %collective-permute-start.10 = (f32[64,512]{1,0:T(8,128)S(1)}, f32[64,512]{1,0:T(8,128)S(1)}, u32[]{:S(2)}, u32[]{:S(2)}) collective-permute-start(f32[64,512]{1,0:T(8,128)S(1)} %collective-permute-done.9.refs_5_), channel_id=1, source_target_pairs={{0,1},{1,0},{2,3},{3,2},{4,5},{5,4},{6,7},{7,6},{8,9},{9,8},{10,11... | collective-permute-start | bytes 393224 | tf_op jit(solution)/shard_map/ppermute | solution.py:246
  19.1 1.9 %collective-permute-start.11 = (f32[2,32,1536]{2,1,0:T(8,128)S(1)}, f32[2,32,1536]{2,1,0:T(8,128)S(1)}, u32[]{:S(2)}, u32[]{:S(2)}) collective-permute-start(f32[2,32,1536]{2,1,0:T(8,128)S(1)} %get-tuple-element.21), channel_id=1, source_target_pairs={{0,1},{1,0},{2,3},{3,2},{4,5},{5,4},{6,7},{7,6},{8,9},{9,8},{10,11... | collective-permute-start | bytes 1179656 | tf_op jit(solution)/shard_map/ppermute | solution.py:246
  19.7 5.1 %collective-permute-start.7 = (f32[32,384]{1,0:T(8,128)S(1)}, f32[32,384]{1,0:T(8,128)S(1)}, u32[]{:S(2)}, u32[]{:S(2)}) collective-permute-start(f32[32,384]{1,0:T(8,128)S(1)} %constant_dynamic-slice_fusion.1), channel_id=1, source_target_pairs={{0,1},{1,0},{2,3},{3,2},{4,5},{5,4},{6,7},{7,6},{8,9},{9,8},{10,11... | collective-permute-start | bytes 147464 | tf_op jit(solution)/shard_map/ppermute | solution.py:246
  19.8 110.3 %collective-permute-start = (f32[512,2048]{1,0:T(8,128)}, f32[512,2048]{1,0:T(8,128)}, u32[]{:S(2)}, u32[]{:S(2)}) collective-permute-start(f32[512,2048]{1,0:T(8,128)} %bitcast.refs_0_), channel_id=1, source_target_pairs={{0,1},{1,0},{2,3},{3,2},{4,5},{5,4},{6,7},{7,6},{8,9},{9,8},{10,11... | collective-permute-start | bytes 12582920 | tf_op jit(solution)/shard_map/ppermute | solution.py:246
  21.6 5.4 %collective-permute-start.13 = (f32[32,768]{1,0:T(8,128)}, f32[32,768]{1,0:T(8,128)S(1)}, u32[]{:S(2)}, u32[]{:S(2)}) collective-permute-start(f32[32,768]{1,0:T(8,128)} %get-tuple-element.27), channel_id=1, source_target_pairs={{0,4},{1,5},{2,6},{3,7},{4,0},{5,1},{6,2},{7,3},{8,12},{9,13},{10,... | collective-permute-start | bytes 294920 | tf_op jit(solution)/shard_map/ppermute | solution.py:246
  23.5 6.8 %collective-permute-start.14 = (f32[32,768]{1,0:T(8,128)S(1)}, f32[32,768]{1,0:T(8,128)S(1)}, u32[]{:S(2)}, u32[]{:S(2)}) collective-permute-start(f32[32,768]{1,0:T(8,128)S(1)} %get-tuple-element.28), channel_id=1, source_target_pairs={{0,6},{1,7},{2,4},{3,5},{4,2},{5,3},{6,0},{7,1},{8,14},{9,15},{10,... | collective-permute-start | bytes 294920 | tf_op jit(solution)/shard_map/ppermute | solution.py:246
  24.9 6.6 %collective-permute-start.12 = (f32[32,768]{1,0:T(8,128)S(1)}, f32[32,768]{1,0:T(8,128)S(1)}, u32[]{:S(2)}, u32[]{:S(2)}) collective-permute-start(f32[32,768]{1,0:T(8,128)S(1)} %get-tuple-element.23), channel_id=1, source_target_pairs={{0,2},{1,3},{2,0},{3,1},{4,6},{5,7},{6,4},{7,5},{8,10},{9,11},{10,... | collective-permute-start | bytes 294920 | tf_op jit(solution)/shard_map/ppermute | solution.py:246
  25.2 21.2 %copy-start.1 = (f32[1,512,1536]{2,1,0:T(8,128)S(1)}, f32[1,512,1536]{2,1,0:T(8,128)}, u32[]{:S(2)}) copy-start(f32[1,512,1536]{2,1,0:T(8,128)} %param.32) | copy-start | bytes 9437188
  31.5 5.5 %collective-permute-start.17 = (f32[32,768]{1,0:T(8,128)}, f32[32,768]{1,0:T(8,128)}, u32[]{:S(2)}, u32[]{:S(2)}) collective-permute-start(f32[32,768]{1,0:T(8,128)} %get-tuple-element.27), channel_id=1, source_target_pairs={{0,2},{1,3},{2,0},{3,1},{4,8},{5,9},{6,10},{7,11},{8,4},{9,5},{10,... | collective-permute-start | bytes 294920 | tf_op jit(solution)/shard_map/ppermute | solution.py:246
  32.0 6.8 %collective-permute-start.18 = (f32[32,768]{1,0:T(8,128)S(1)}, f32[32,768]{1,0:T(8,128)}, u32[]{:S(2)}, u32[]{:S(2)}) collective-permute-start(f32[32,768]{1,0:T(8,128)S(1)} %get-tuple-element.28), channel_id=1, source_target_pairs={{0,2},{1,3},{2,0},{3,1},{4,10},{5,11},{6,8},{7,9},{8,6},{9,7},{10,... | collective-permute-start | bytes 294920 | tf_op jit(solution)/shard_map/ppermute | solution.py:246
  33.6 6.2 %collective-permute-start.15 = (f32[32,768]{1,0:T(8,128)S(1)}, f32[32,768]{1,0:T(8,128)S(1)}, u32[]{:S(2)}, u32[]{:S(2)}) collective-permute-start(f32[32,768]{1,0:T(8,128)S(1)} %subtract_select_fusion.1.refs_5_), channel_id=1, source_target_pairs={{0,4},{1,5},{2,6},{3,7},{4,0},{5,1},{6,2},{7,3},{8,12},{9,13},{10,... | collective-permute-start | bytes 294920 | tf_op jit(solution)/shard_map/ppermute | solution.py:246
  37.0 5.5 %collective-permute-start.16 = (f32[32,768]{1,0:T(8,128)S(1)}, f32[32,768]{1,0:T(8,128)S(1)}, u32[]{:S(2)}, u32[]{:S(2)}) collective-permute-start(f32[32,768]{1,0:T(8,128)S(1)} %subtract_select_fusion.1.refs_5_), channel_id=1, source_target_pairs={{0,6},{1,7},{2,4},{3,5},{4,2},{5,3},{6,0},{7,1},{8,14},{9,15},{10,... | collective-permute-start | bytes 294920 | tf_op jit(solution)/shard_map/ppermute | solution.py:246
  44.2 10.9 %copy-start.7 = (f32[1,384,1536]{2,1,0:T(8,128)S(1)}, f32[1,384,1536]{2,1,0:T(8,128)}, u32[]{:S(2)}) copy-start(f32[1,384,1536]{2,1,0:T(8,128)} %param.34) | copy-start | bytes 7077892
  44.2 17.0 %copy-start.3 = (f32[1,384,1536]{2,1,0:T(8,128)S(1)}, f32[1,384,1536]{2,1,0:T(8,128)}, u32[]{:S(2)}) copy-start(f32[1,384,1536]{2,1,0:T(8,128)} %param.35) | copy-start | bytes 7077892
  44.3 4.7 %collective-permute-start.19 = (f32[32,768]{1,0:T(8,128)S(1)}, f32[32,768]{1,0:T(8,128)S(1)}, u32[]{:S(2)}, u32[]{:S(2)}) collective-permute-start(f32[32,768]{1,0:T(8,128)S(1)} %shard_map.219.refs_5_), channel_id=1, source_target_pairs={{0,2},{1,3},{2,0},{3,1},{4,8},{5,9},{6,10},{7,11},{8,4},{9,5},{10,... | collective-permute-start | bytes 294920 | tf_op jit(solution)/shard_map/ppermute | solution.py:246
  44.8 5.2 %collective-permute-start.20 = (f32[32,768]{1,0:T(8,128)S(1)}, f32[32,768]{1,0:T(8,128)S(1)}, u32[]{:S(2)}, u32[]{:S(2)}) collective-permute-start(f32[32,768]{1,0:T(8,128)S(1)} %shard_map.219.refs_5_), channel_id=1, source_target_pairs={{0,2},{1,3},{2,0},{3,1},{4,10},{5,11},{6,8},{7,9},{8,6},{9,7},{10,... | collective-permute-start | bytes 294920 | tf_op jit(solution)/shard_map/ppermute | solution.py:246
  46.4 56.4 %collective-permute-start.1 = (f32[512,1536]{1,0:T(8,128)S(1)}, f32[512,1536]{1,0:T(8,128)}, u32[]{:S(2)}, u32[]{:S(2)}) collective-permute-start(f32[512,1536]{1,0:T(8,128)S(1)} %bitcast.125), channel_id=1, source_target_pairs={{0,1},{1,0},{2,3},{3,2},{4,5},{5,4},{6,7},{7,6},{8,9},{9,8},{10,11... | collective-permute-start | bytes 9437192 | tf_op jit(solution)/shard_map/ppermute | solution.py:246
  50.0 8.0 %collective-permute-start.21 = (f32[32,768]{1,0:T(8,128)S(1)}, f32[32,768]{1,0:T(8,128)S(1)}, u32[]{:S(2)}, u32[]{:S(2)}) collective-permute-start(f32[32,768]{1,0:T(8,128)S(1)} %shard_map.220.refs_5_), channel_id=1, source_target_pairs={{0,4},{1,5},{2,6},{3,7},{4,0},{5,1},{6,2},{7,3},{8,12},{9,13},{10,... | collective-permute-start | bytes 294920 | tf_op jit(solution)/shard_map/ppermute | solution.py:246
  55.2 6.2 %collective-permute-start.5 = (f32[384,1536]{1,0:T(8,128)S(1)}, f32[384,1536]{1,0:T(8,128)S(1)}, u32[]{:S(2)}, u32[]{:S(2)}) collective-permute-start(f32[384,1536]{1,0:T(8,128)S(1)} %bitcast.136), channel_id=1, source_target_pairs={{0,1},{1,0},{2,3},{3,2},{4,5},{5,4},{6,7},{7,6},{8,9},{9,8},{10,11... | collective-permute-start | bytes 7077896 | tf_op jit(solution)/shard_map/ppermute | solution.py:246
  55.2 6.1 %collective-permute-start.22 = (f32[32,768]{1,0:T(8,128)S(1)}, f32[32,768]{1,0:T(8,128)S(1)}, u32[]{:S(2)}, u32[]{:S(2)}) collective-permute-start(f32[32,768]{1,0:T(8,128)S(1)} %shard_map.220.refs_5_), channel_id=1, source_target_pairs={{0,6},{1,7},{2,4},{3,5},{4,2},{5,3},{6,0},{7,1},{8,14},{9,15},{10,... | collective-permute-start | bytes 294920 | tf_op jit(solution)/shard_map/ppermute | solution.py:246
  58.0 59.0 %collective-permute-start.2 = (f32[512,1536]{1,0:T(8,128)}, f32[512,1536]{1,0:T(8,128)}, u32[]{:S(2)}, u32[]{:S(2)}) collective-permute-start(f32[512,1536]{1,0:T(8,128)} %bitcast.2.refs_2_), channel_id=1, source_target_pairs={{0,1},{1,0},{2,3},{3,2},{4,5},{5,4},{6,7},{7,6},{8,9},{9,8},{10,11... | collective-permute-start | bytes 9437192 | tf_op jit(solution)/shard_map/ppermute | solution.py:246
  61.3 9.5 %collective-permute-start.4 = (f32[384,1536]{1,0:T(8,128)S(1)}, f32[384,1536]{1,0:T(8,128)S(1)}, u32[]{:S(2)}, u32[]{:S(2)}) collective-permute-start(f32[384,1536]{1,0:T(8,128)S(1)} %bitcast.132), channel_id=1, source_target_pairs={{0,1},{1,0},{2,3},{3,2},{4,5},{5,4},{6,7},{7,6},{8,9},{9,8},{10,11... | collective-permute-start | bytes 7077896 | tf_op jit(solution)/shard_map/ppermute | solution.py:246
  61.3 5.3 %collective-permute-start.23 = (f32[32,768]{1,0:T(8,128)S(1)}, f32[32,768]{1,0:T(8,128)S(1)}, u32[]{:S(2)}, u32[]{:S(2)}) collective-permute-start(f32[32,768]{1,0:T(8,128)S(1)} %shard_map.221.refs_2_), channel_id=1, source_target_pairs={{0,2},{1,3},{2,0},{3,1},{4,6},{5,7},{6,4},{7,5},{8,10},{9,11},{10,... | collective-permute-start | bytes 294920 | tf_op jit(solution)/shard_map/ppermute | solution.py:246
  69.6 5.7 %collective-permute-start.24 = (f32[32,768]{1,0:T(8,128)S(1)}, f32[32,768]{1,0:T(8,128)S(1)}, u32[]{:S(2)}, u32[]{:S(2)}) collective-permute-start(f32[32,768]{1,0:T(8,128)S(1)} %shard_map.222.refs_4_.refs_5_), channel_id=1, source_target_pairs={{0,4},{1,5},{2,6},{3,7},{4,0},{5,1},{6,2},{7,3},{8,12},{9,13},{10,... | collective-permute-start | bytes 294920 | tf_op jit(solution)/shard_map/ppermute | solution.py:246
  70.8 11.9 %copy-start.5 = (f32[384,1536]{1,0:T(8,128)}, f32[384,1536]{1,0:T(8,128)S(1)}, u32[]{:S(2)}) copy-start(f32[384,1536]{1,0:T(8,128)S(1)} %collective-permute-done.4.refs_1_) | copy-start | bytes 7077892
  70.8 6.1 %collective-permute-start.25 = (f32[32,768]{1,0:T(8,128)S(1)}, f32[32,768]{1,0:T(8,128)S(1)}, u32[]{:S(2)}, u32[]{:S(2)}) collective-permute-start(f32[32,768]{1,0:T(8,128)S(1)} %shard_map.222.refs_4_.refs_5_), channel_id=1, source_target_pairs={{0,6},{1,7},{2,4},{3,5},{4,2},{5,3},{6,0},{7,1},{8,14},{9,15},{10,... | collective-permute-start | bytes 294920 | tf_op jit(solution)/shard_map/ppermute | solution.py:246
  77.0 4.7 %collective-permute-start.26 = (f32[32,768]{1,0:T(8,128)S(1)}, f32[32,768]{1,0:T(8,128)S(1)}, u32[]{:S(2)}, u32[]{:S(2)}) collective-permute-start(f32[32,768]{1,0:T(8,128)S(1)} %shard_map.223.refs_5_), channel_id=1, source_target_pairs={{0,2},{1,3},{2,0},{3,1},{4,8},{5,9},{6,10},{7,11},{8,4},{9,5},{10,... | collective-permute-start | bytes 294920 | tf_op jit(solution)/shard_map/ppermute | solution.py:246
  77.9 4.7 %collective-permute-start.27 = (f32[32,768]{1,0:T(8,128)S(1)}, f32[32,768]{1,0:T(8,128)S(1)}, u32[]{:S(2)}, u32[]{:S(2)}) collective-permute-start(f32[32,768]{1,0:T(8,128)S(1)} %shard_map.223.refs_5_), channel_id=1, source_target_pairs={{0,2},{1,3},{2,0},{3,1},{4,10},{5,11},{6,8},{7,9},{8,6},{9,7},{10,... | collective-permute-start | bytes 294920 | tf_op jit(solution)/shard_map/ppermute | solution.py:246
  82.7 16.3 %collective-permute-start.30 = (f32[32,768]{1,0:T(8,128)S(1)}, f32[32,768]{1,0:T(8,128)}, u32[]{:S(2)}, u32[]{:S(2)}) collective-permute-start(f32[32,768]{1,0:T(8,128)S(1)} %shard_map.224.refs_2_.refs_5_), channel_id=1, source_target_pairs={{0,2},{1,3},{2,0},{3,1},{4,6},{5,7},{6,4},{7,5},{8,10},{9,11},{10,... | collective-permute-start | bytes 294920 | tf_op jit(solution)/shard_map/ppermute | solution.py:246
  83.8 1.4 collective-permute-start.3
  85.2 24.0 %collective-permute-start.28 = (f32[32,768]{1,0:T(8,128)S(1)}, f32[32,768]{1,0:T(8,128)S(1)}, u32[]{:S(2)}, u32[]{:S(2)}) collective-permute-start(f32[32,768]{1,0:T(8,128)S(1)} %shard_map.224.refs_2_.refs_5_), channel_id=1, source_target_pairs={{0,4},{1,5},{2,6},{3,7},{4,0},{5,1},{6,2},{7,3},{8,12},{9,13},{10,... | collective-permute-start | bytes 294920 | tf_op jit(solution)/shard_map/ppermute | solution.py:246
  99.1 11.3 %collective-permute-start.29 = (f32[32,768]{1,0:T(8,128)S(1)}, f32[32,768]{1,0:T(8,128)S(1)}, u32[]{:S(2)}, u32[]{:S(2)}) collective-permute-start(f32[32,768]{1,0:T(8,128)S(1)} %shard_map.224.refs_2_.refs_5_), channel_id=1, source_target_pairs={{0,6},{1,7},{2,4},{3,5},{4,2},{5,3},{6,0},{7,1},{8,14},{9,15},{10,... | collective-permute-start | bytes 294920 | tf_op jit(solution)/shard_map/ppermute | solution.py:246
  102.7 11.7 %collective-permute-start.34 = (f32[32,768]{1,0:T(8,128)S(1)}, f32[32,768]{1,0:T(8,128)S(1)}, u32[]{:S(2)}, u32[]{:S(2)}) collective-permute-start(f32[32,768]{1,0:T(8,128)S(1)} %shard_map.224.refs_2_.refs_5_), channel_id=1, source_target_pairs={{0,2},{1,3},{2,0},{3,1},{4,8},{5,9},{6,10},{7,11},{8,4},{9,5},{10,... | collective-permute-start | bytes 294920 | tf_op jit(solution)/shard_map/ppermute | solution.py:246
  109.2 5.4 %collective-permute-start.35 = (f32[32,768]{1,0:T(8,128)S(1)}, f32[32,768]{1,0:T(8,128)S(1)}, u32[]{:S(2)}, u32[]{:S(2)}) collective-permute-start(f32[32,768]{1,0:T(8,128)S(1)} %shard_map.224.refs_2_.refs_5_), channel_id=1, source_target_pairs={{0,2},{1,3},{2,0},{3,1},{4,10},{5,11},{6,8},{7,9},{8,6},{9,7},{10,... | collective-permute-start | bytes 294920 | tf_op jit(solution)/shard_map/ppermute | solution.py:246
  113.4 4.7 %collective-permute-start.31 = (f32[32,768]{1,0:T(8,128)S(1)}, f32[32,768]{1,0:T(8,128)S(1)}, u32[]{:S(2)}, u32[]{:S(2)}) collective-permute-start(f32[32,768]{1,0:T(8,128)S(1)} %shard_map.226.refs_6_), channel_id=1, source_target_pairs={{0,2},{1,3},{2,0},{3,1},{4,6},{5,7},{6,4},{7,5},{8,10},{9,11},{10,... | collective-permute-start | bytes 294920 | tf_op jit(solution)/shard_map/ppermute | solution.py:246
  114.4 4.7 %collective-permute-start.32 = (f32[32,768]{1,0:T(8,128)S(1)}, f32[32,768]{1,0:T(8,128)S(1)}, u32[]{:S(2)}, u32[]{:S(2)}) collective-permute-start(f32[32,768]{1,0:T(8,128)S(1)} %shard_map.226.refs_6_), channel_id=1, source_target_pairs={{0,4},{1,5},{2,6},{3,7},{4,0},{5,1},{6,2},{7,3},{8,12},{9,13},{10,... | collective-permute-start | bytes 294920 | tf_op jit(solution)/shard_map/ppermute | solution.py:246
  114.7 6.0 %collective-permute-start.33 = (f32[32,768]{1,0:T(8,128)S(1)}, f32[32,768]{1,0:T(8,128)S(1)}, u32[]{:S(2)}, u32[]{:S(2)}) collective-permute-start(f32[32,768]{1,0:T(8,128)S(1)} %shard_map.226.refs_6_), channel_id=1, source_target_pairs={{0,6},{1,7},{2,4},{3,5},{4,2},{5,3},{6,0},{7,1},{8,14},{9,15},{10,... | collective-permute-start | bytes 294920 | tf_op jit(solution)/shard_map/ppermute | solution.py:246
  117.1 9.0 %collective-permute-start.38 = (f32[32,384]{1,0:T(8,128)S(1)}, f32[32,384]{1,0:T(8,128)S(1)}, u32[]{:S(2)}, u32[]{:S(2)}) collective-permute-start(f32[32,384]{1,0:T(8,128)S(1)} %constant_dynamic-slice_fusion), channel_id=1, source_target_pairs={{0,1},{1,0},{2,3},{3,2},{4,5},{5,4},{6,7},{7,6},{8,9},{9,8},{10,11... | collective-permute-start | bytes 147464 | tf_op jit(solution)/shard_map/ppermute | solution.py:246
  125.1 5.0 %collective-permute-start.36 = (f32[32,1024]{1,0:T(8,128)S(1)}, f32[32,1024]{1,0:T(8,128)S(1)}, u32[]{:S(2)}, u32[]{:S(2)}) collective-permute-start(f32[32,1024]{1,0:T(8,128)S(1)} %shard_map.227.refs_2_), channel_id=1, source_target_pairs={{0,2},{1,3},{2,0},{3,1},{4,6},{5,7},{6,4},{7,5},{8,10},{9,11},{10,... | collective-permute-start | bytes 393224 | tf_op jit(solution)/shard_map/ppermute | solution.py:246
  126.1 10.8 %copy-start.12 = (f32[1,384,64]{1,2,0:T(8,128)S(1)}, f32[1,384,64]{1,2,0:T(8,128)}, u32[]{:S(2)}) copy-start(f32[1,384,64]{1,2,0:T(8,128)} %param.27) | copy-start | bytes 294916
  126.1 10.8 %copy-start.14 = (f32[1,384,64]{1,2,0:T(8,128)S(1)}, f32[1,384,64]{1,2,0:T(8,128)}, u32[]{:S(2)}) copy-start(f32[1,384,64]{1,2,0:T(8,128)} %param.29) | copy-start | bytes 294916
  126.1 12.0 %copy-start.8 = (f32[1,512,64]{1,2,0:T(8,128)S(1)}, f32[1,512,64]{1,2,0:T(8,128)}, u32[]{:S(2)}) copy-start(f32[1,512,64]{1,2,0:T(8,128)} %param.26) | copy-start | bytes 393220
  126.1 12.0 %copy-start.9 = (f32[1,512,64]{1,2,0:T(8,128)S(1)}, f32[1,512,64]{1,2,0:T(8,128)}, u32[]{:S(2)}) copy-start(f32[1,512,64]{1,2,0:T(8,128)} %param.25) | copy-start | bytes 393220
  126.1 12.0 %copy-start.10 = (f32[1,512,64]{1,2,0:T(8,128)S(1)}, f32[1,512,64]{1,2,0:T(8,128)}, u32[]{:S(2)}) copy-start(f32[1,512,64]{1,2,0:T(8,128)} %param.24) | copy-start | bytes 393220
  136.8 1.3 collective-permute-start.37
  (8 other events, 49.1 us)

commit v4 on v2

--- a/solution.py
+++ b/solution.py
@@ -93,8 +93,32 @@
         in_specs=[VMEM] * len(flat),
         out_specs=[VMEM] * len(out),
         out_shape=out,
-        compiler_params=pltpu.CompilerParams(vmem_limit_bytes=40 << 20),
+        compiler_params=pltpu.CompilerParams(vmem_limit_bytes=24 << 20),
     )(*flat)
+
+
+def staged(*matrices, after):
+    held = lax.optimization_barrier([*matrices, *after])[: len(matrices)]
+
+    def body(*refs):
+        count = len(held)
+        sems = refs[-1]
+        copies = [
+            pltpu.make_async_copy(refs[i], refs[count + i], sems.at[i]) for i in range(count)
+        ]
+        for copy in copies:
+            copy.start()
+        for copy in copies:
+            copy.wait()
+
+    return pl.pallas_call(
+        body,
+        in_specs=[pl.BlockSpec(memory_space=pltpu.HBM)] * len(held),
+        out_specs=[VMEM] * len(held),
+        out_shape=[pltpu.VMEM(matrix.shape, matrix.dtype) for matrix in held],
+        scratch_shapes=[pltpu.SemaphoreType.DMA((len(held),))],
+        compiler_params=pltpu.CompilerParams(vmem_limit_bytes=24 << 20),
+    )(*held)
 
 
 def forces_kernel(swap_chips, pieces, matrices, mine, theirs):
@@ -223,6 +247,19 @@
 
     def pieces(self, pieces):
         return pieces if pieces[0].shape[1] % 128 == 0 else [self.by_chip(pieces)]
+
+    def below(self, value, j):
+        pairs = []
+        for s in range(1, self.stories):
+            for r in range(self.chips):
+                for b in range(self.cores):
+                    pairs.append(
+                        (
+                            (s * self.chips + r) * self.cores + b,
+                            ((s - 1) * self.chips + (r ^ j)) * self.cores + b,
+                        )
+                    )
+        return lax.ppermute(value, AXES, pairs)
 
     def gather_chips(self, value):
         return self.pieces([value] + [self.chip(value, j) for j in range(1, self.chips)])
@@ -279,11 +316,18 @@
     rows_int, rows_face = 2 * load_int.shape[1], 2 * load_face.shape[1]
     faces = couple_above.shape[2]
 
-    def chip_rows(matrix):
-        own = matrix[0]
-        return [own, mv.core(own)]
-
+    def others(matrix, after):
+        return mv.core(lax.optimization_barrier([matrix, *after])[0])
+
+    inverse_own, above_own, below_own = interior_inverse[0], couple_above[0], couple_below[0]
+    lower_other = mv.core(lower[0])
     across = [mv.chip(load_int, j) for j in range(1, mv.chips)]
+    inverse_own, above_own, below_own = staged(
+        inverse_own, above_own, below_own, after=[load_int]
+    )
+    inverse_own, above_own, below_own, *across = lax.optimization_barrier(
+        [inverse_own, above_own, below_own, *across]
+    )
     beside = [mv.core(piece) for piece in [load_int] + across]
     pieces = [piece for pair in zip([load_int] + across, beside) for piece in pair]
     aligned = load_int.shape[1] % 128 == 0
@@ -295,65 +339,84 @@
         functools.partial(forces_kernel, aligned),
         [(2, half, faces)] * 2,
         pieces,
-        [interior_inverse[0], couple_above[0], couple_below[0]],
-    )
+        [inverse_own, above_own, below_own],
+    )
+    load_face_half, load_int_half = mv.to_half(load_face), mv.to_half(load_int)
     chunks = call(
         chunks_kernel,
         [(half, faces // mv.chips)] * (2 * mv.chips),
         [mine, mv.core(theirs)],
     )
+    pivot_other = others(pivot[0], [chunks[0]])
+    upper_other = others(upper[0], [chunks[0]])
     above_force = chunks[0]
+    below_force = mv.below(chunks[mv.chips], 0)
     for j in range(1, mv.chips):
         above_force = above_force + mv.chip(chunks[j], j)
-    below_force = []
-    for parity in range(2):
-        total = mv.story(chunks[mv.chips], parity, 0)
-        for j in range(1, mv.chips):
-            total = total + mv.story(chunks[mv.chips + j], parity, j)
-        below_force.append(total)
-    condensed = mv.to_half(load_face) - above_force
-    condensed = jnp.where((s % 2 == 0) & (s != last), condensed - below_force[0], condensed)
-
-    lower_rows, pivot_rows, upper_rows = chip_rows(lower), chip_rows(pivot), chip_rows(upper)
+        below_force = below_force + mv.below(chunks[mv.chips + j], j)
+    lower_rows = staged(lower[0], lower_other, after=[chunks[0]])
+    condensed = load_face_half - above_force - below_force
+    condensed, *lower_rows = lax.optimization_barrier([condensed, *lower_rows])
+
     shape = [(half, rows_face)]
     forward = condensed
     for k in range(1, mv.stories):
         came = mv.gather_story(forward, (k - 1) % 2)
         if k == 1:
-            condensed = jnp.where((s % 2 == 1) & (s != last), condensed - below_force[1], condensed)
+            pivot_rows = staged(pivot[0], pivot_other, after=[forward])
+            *came, p0, p1 = lax.optimization_barrier([*came, *pivot_rows])
+            pivot_rows = [p0, p1]
+            above_other = others(couple_above[0], [forward])
+            below_other = others(couple_below[0], [forward])
+            inverse_other = others(interior_inverse[0], [forward])
+        if k == mv.stories - 1:
+            upper_rows = staged(upper[0], upper_other, after=[forward])
+            *came, u0, u1 = lax.optimization_barrier([*came, *upper_rows])
+            upper_rows = [u0, u1]
         (forward,) = call(
             functools.partial(step_kernel, k), shape, came, lower_rows, [condensed, forward]
         )
     (pivoted,) = call(rows_kernel, shape, mv.gather_chips(forward), pivot_rows)
 
-    below_rows, above_rows = chip_rows(couple_below), chip_rows(couple_above)
-    inverse_rows = chip_rows(interior_inverse)
     shape_int = [(half, rows_int)]
     face = pivoted
     for k in range(mv.stories - 2, -1, -1):
         came = mv.gather_story(face, k % 2)
+        if k == mv.stories - 2:
+            (above_other,) = staged(above_other, after=[face])
+            *came, above_other = lax.optimization_barrier([*came, above_other])
+        if k == max(mv.stories - 3, 0):
+            (below_other,) = staged(below_other, after=[face])
+            *came, below_other = lax.optimization_barrier([*came, below_other])
         if k == 0:
             odd = mv.gather_story(face, 1)
-            (early,) = call(rows_kernel, shape_int, mv.gather_chips(face), above_rows)
-        (face,) = call(functools.partial(step_kernel, k), shape, came, upper_rows, [pivoted, face])
+            (early,) = call(
+                rows_kernel, shape_int, mv.gather_chips(face), [above_own, above_other]
+            )
+            *came, early = lax.optimization_barrier([*came, early])
+        (face,) = call(
+            functools.partial(step_kernel, k), shape, came, upper_rows, [pivoted, face]
+        )
 
     even = mv.gather_story(face, 0)
+    (inverse_other,) = staged(inverse_other, after=[face])
+    *even, inverse_other = lax.optimization_barrier([*even, inverse_other])
     (reduced,) = call(
         coupled_kernel,
         shape_int,
-        [mv.to_half(load_int)],
+        [load_int_half],
         [early],
         mv.gather_chips(face),
         even,
         odd,
-        above_rows,
-        below_rows,
+        [above_own, above_other],
+        [below_own, below_other],
     )
     mine, theirs = call(
         last_kernel,
         [(half, rows_int // 2)] * 2,
         mv.gather_chips(reduced),
-        inverse_rows,
+        [inverse_own, inverse_other],
     )
 
     u_f = mv.from_half(face)

time: 134 us -> 144 us (1.075)
  waiting for transfers between devices: 50.2 us -> 55.7 us
  local copies, waits for them, and re-layouts: 9.4 us -> 14.8 us
  Pallas kernels: 27 us -> 25.4 us
    pallas_call x12, Pallas kernels: 27 us -> 15 us  [call(): pl.pallas_call(body, in_specs=[VMEM] * len(flat), out_specs=[VMEM] * len(...]
    pallas_call x0 -> x7, Pallas kernels: none -> 10.4 us  [staged(): pl.pallas_call(body, in_specs=[pl.BlockSpec(memory_space=pltpu.HBM)] * le...]
    unnamed x48 -> x60, local copies, waits for them, and re-layouts: 9.38 us -> 14.8 us
    ppermute x0 -> x2, waiting for transfers between devices: none -> 5.17 us  [below(): return lax.ppermute(value, AXES, pairs)]
    ppermute x0 -> x2, starting transfers between devices: none -> 2.7 us  [below(): return lax.ppermute(value, AXES, pairs)]
    ppermute x39 -> x35, starting transfers between devices: 40.5 us -> 39 us  [permute(): return lax.ppermute(value, AXES, pairs)]
    ppermute x39 -> x35, waiting for transfers between devices: 50.2 us -> 50.5 us  [permute(): return lax.ppermute(value, AXES, pairs)]
  transfers between devices with their start and end apart: 39 -> 37, of which waited for: 24 -> 22; matrix products, arithmetic and copies ran while one was open for 4% -> 3% of each run, Pallas kernels for 17% -> 15%
where the time goes in v4:
time: 144 us; the launch traced here: 143 us
  waiting for transfers between devices  55.7 us (39%)
  starting transfers between devices  41.7 us (29%)
  Pallas kernels  25.4 us (18%)
  local copies, waits for them, and re-layouts  14.8 us (10%)
  other arithmetic  4.58 us (3%)
    ppermute x35, waiting for transfers between devices, permute(): return lax.ppermute(value, AXES, pairs)  50.5 us
    ppermute x35, starting transfers between devices, permute(): return lax.ppermute(value, AXES, pairs)  39 us
    pallas_call x12, Pallas kernels, call(): pl.pallas_call(body, in_specs=[VMEM] * len(flat), out_specs=[VMEM] * len(...  15 us
    unnamed x60, local copies, waits for them, and re-layouts  14.8 us
    pallas_call x7, Pallas kernels, staged(): pl.pallas_call(body, in_specs=[pl.BlockSpec(memory_space=pltpu.HBM)] * le...  10.4 us
    ppermute x2, waiting for transfers between devices, below(): return lax.ppermute(value, AXES, pairs)  5.17 us
  transfers between devices with their start and end apart: 37, of which 22 were waited for; matrix products, arithmetic and copies ran while one was open for 3% of the time, Pallas kernels for 15%

profile of v4, /device:TPU:0, one launch (start us, length us, event | category | flops | bytes accessed | tf_op | source)
XLA Modules:
  0.0 143.3 jit_solution(2321332198301372662)
XLA Ops:
  2.0 1.1 fusion.2.refs_0_
  3.2 2.6 %collective-permute-start.3 = (f32[64,512]{1,0:T(8,128)S(1)}, f32[64,512]{1,0:T(8,128)S(1)}, u32[]{:S(2)}, u32[]{:S(2)}) collective-permute-start(f32[64,512]{1,0:T(8,128)S(1)} %fusion.2.refs_0_), channel_id=1, source_target_pairs={{0,2},{1,3},{2,0},{3,1},{4,6},{5,7},{6,4},{7,5},{8,10},{9,11},{10,... | collective-permute-start | bytes 393224 | tf_op jit(solution)/shard_map/ppermute | solution.py:218
  5.9 1.9 %copy-done.12 = f32[1,512,1536]{2,1,0:T(8,128)S(1)} copy-done((f32[1,512,1536]{2,1,0:T(8,128)S(1)}, f32[1,512,1536]{2,1,0:T(8,128)}, u32[]{:S(2)}) %copy-start.12) | copy-done | bytes 3145752
  7.8 3.3 %shard_map.217 = (f32[512,2048]{1,0:T(8,128)S(1)}, f32[512,1536]{1,0:T(8,128)S(1)}, f32[512,1536]{1,0:T(8,128)S(1)}) custom-call(f32[512,2048]{1,0:T(8,128)} %bitcast.14.refs_0_, f32[512,1536]{1,0:T(8,128)S(1)} %bitcast.124, f32[512,1536]{1,0:T(8,128)} %bitcast.16.refs_2_), custom_call_target="tpu_custom_call" | custom-call | tf_op jit(solution)/shard_map/pallas_call | solution.py:114
  11.1 2.0 %copy-done.6 = f32[512,2048]{1,0:T(8,128)} copy-done((f32[512,2048]{1,0:T(8,128)}, f32[512,2048]{1,0:T(8,128)S(1)}, u32[]{:S(2)}) %copy-start.6) | copy-done | bytes 4194328
  13.1 1.6 %copy-done.9 = f32[512,1536]{1,0:T(8,128)} copy-done((f32[512,1536]{1,0:T(8,128)}, f32[512,1536]{1,0:T(8,128)S(1)}, u32[]{:S(2)}) %copy-start.9) | copy-done | bytes 3145752
  16.2 2.2 %copy-done.7 = f32[512,2048]{1,0:T(8,128)S(1)} copy-done((f32[512,2048]{1,0:T(8,128)S(1)}, f32[512,2048]{1,0:T(8,128)}, u32[]{:S(2)}) %copy-start.7) | copy-done | bytes 4194328
  18.4 1.9 %copy-done.10 = f32[512,1536]{1,0:T(8,128)S(1)} copy-done((f32[512,1536]{1,0:T(8,128)S(1)}, f32[512,1536]{1,0:T(8,128)}, u32[]{:S(2)}) %copy-start.10) | copy-done | bytes 3145752
  20.3 4.3 %shard_map.218 = (f32[2,32,1536]{2,1,0:T(8,128)S(1)}, f32[2,32,1536]{2,1,0:T(8,128)}) custom-call(f32[64,512]{1,0:T(8,128)S(1)} %fusion.2.refs_0_, f32[64,512]{1,0:T(8,128)} %collective-permute-done.2.refs_1_, f32[64,512]{1,0:T(8,128)S(1)} %collective-permute-done.3.refs_2_, f32[64,512]{1,0:T(8,128)} %collective-permute-done.4.refs_3_, ...), custom_call_target="tpu_custom_call" | custom-call | tf_op jit(solution)/shard_map/pallas_call | solution.py:91
  26.1 1.2 collective-permute-done.5.refs_1_
  28.8 1.4 collective-permute-start.7
  30.2 1.3 collective-permute-start.8
  31.6 1.9 %collective-permute-done.6 = f32[32,768]{1,0:T(8,128)S(1)} collective-permute-done((f32[32,768]{1,0:T(8,128)S(1)}, f32[32,768]{1,0:T(8,128)S(1)}, u32[]{:S(2)}, u32[]{:S(2)}) %collective-permute-start.6) | collective-permute-done | bytes 98336 | tf_op jit(solution)/shard_map/ppermute | solution.py:218
  33.4 2.2 %collective-permute-done.7 = f32[32,768]{1,0:T(8,128)S(1)} collective-permute-done((f32[32,768]{1,0:T(8,128)S(1)}, f32[32,768]{1,0:T(8,128)S(1)}, u32[]{:S(2)}, u32[]{:S(2)}) %collective-permute-start.7) | collective-permute-done | bytes 98336 | tf_op jit(solution)/shard_map/ppermute | solution.py:262
  35.6 3.0 %collective-permute-done.8 = f32[32,768]{1,0:T(8,128)S(1)} collective-permute-done((f32[32,768]{1,0:T(8,128)S(1)}, f32[32,768]{1,0:T(8,128)S(1)}, u32[]{:S(2)}, u32[]{:S(2)}) %collective-permute-start.8) | collective-permute-done | bytes 98336 | tf_op jit(solution)/shard_map/ppermute | solution.py:262
  38.7 1.7 %copy-done.14 = f32[1,384,1536]{2,1,0:T(8,128)S(1)} copy-done((f32[1,384,1536]{2,1,0:T(8,128)S(1)}, f32[1,384,1536]{2,1,0:T(8,128)}, u32[]{:S(2)}) %copy-start.14) | copy-done | bytes 2359320
  40.3 1.8 %shard_map.220 = (f32[384,1536]{1,0:T(8,128)S(1)}, f32[384,1536]{1,0:T(8,128)S(1)}) custom-call(f32[384,1536]{1,0:T(8,128)S(1)} %bitcast.127, f32[384,1536]{1,0:T(8,128)} %collective-permute-done.9.refs_1_), custom_call_target="tpu_custom_call" | custom-call | tf_op jit(solution)/shard_map/pallas_call | solution.py:114
  43.3 1.7 %collective-permute-start.10 = (f32[32,768]{1,0:T(8,128)S(1)}, f32[32,768]{1,0:T(8,128)S(1)}, u32[]{:S(2)}, u32[]{:S(2)}) collective-permute-start(f32[32,768]{1,0:T(8,128)S(1)} %fusion.8.refs_4_.refs_5_), channel_id=1, source_target_pairs={{0,4},{1,5},{2,6},{3,7},{4,0},{5,1},{6,2},{7,3},{8,12},{9,13},{10,... | collective-permute-start | bytes 294920 | tf_op jit(solution)/shard_map/ppermute | solution.py:218
  44.9 3.1 %collective-permute-done.10.refs_0_ = f32[32,768]{1,0:T(8,128)S(1)} collective-permute-done((f32[32,768]{1,0:T(8,128)S(1)}, f32[32,768]{1,0:T(8,128)S(1)}, u32[]{:S(2)}, u32[]{:S(2)}) %collective-permute-start.10) | collective-permute-done | bytes 98336 | tf_op jit(solution)/shard_map/ppermute | solution.py:218
  48.0 12.3 %collective-permute-done.12.refs_1_ = f32[384,1536]{1,0:T(8,128)S(1)} collective-permute-done((f32[384,1536]{1,0:T(8,128)}, f32[384,1536]{1,0:T(8,128)S(1)}, u32[]{:S(2)}, u32[]{:S(2)}) %collective-permute-start.12) | collective-permute-done | bytes 2359328 | tf_op jit(solution)/shard_map/ppermute | solution.py:218
  60.3 2.6 %collective-permute-start.11 = (f32[32,768]{1,0:T(8,128)S(1)}, f32[32,768]{1,0:T(8,128)S(1)}, u32[]{:S(2)}, u32[]{:S(2)}) collective-permute-start(f32[32,768]{1,0:T(8,128)S(1)} %fusion.8.refs_4_.refs_5_), channel_id=1, source_target_pairs={{0,6},{1,7},{2,4},{3,5},{4,2},{5,3},{6,0},{7,1},{8,14},{9,15},{10,... | collective-permute-start | bytes 294920 | tf_op jit(solution)/shard_map/ppermute | solution.py:218
  63.0 1.7 %copy-done.15 = f32[1,384,1536]{2,1,0:T(8,128)S(1)} copy-done((f32[1,384,1536]{2,1,0:T(8,128)S(1)}, f32[1,384,1536]{2,1,0:T(8,128)}, u32[]{:S(2)}) %copy-start.15) | copy-done | bytes 2359320
  65.0 1.3 collective-permute-done.11.refs_1_
  67.0 4.0 %collective-permute-done.13.refs_0_ = f32[32,768]{1,0:T(8,128)S(1)} collective-permute-done((f32[32,768]{1,0:T(8,128)S(1)}, f32[32,768]{1,0:T(8,128)S(1)}, u32[]{:S(2)}, u32[]{:S(2)}) %collective-permute-start.13) | collective-permute-done | bytes 98336 | tf_op jit(solution)/shard_map/ppermute | solution.py:218
  71.6 4.0 %collective-permute-done.14.refs_1_ = f32[32,768]{1,0:T(8,128)S(1)} collective-permute-done((f32[32,768]{1,0:T(8,128)S(1)}, f32[32,768]{1,0:T(8,128)S(1)}, u32[]{:S(2)}, u32[]{:S(2)}) %collective-permute-start.14) | collective-permute-done | bytes 98336 | tf_op jit(solution)/shard_map/ppermute | solution.py:218
  75.6 4.2 %collective-permute-start.15 = (f32[32,768]{1,0:T(8,128)S(1)}, f32[32,768]{1,0:T(8,128)S(1)}, u32[]{:S(2)}, u32[]{:S(2)}) collective-permute-start(f32[32,768]{1,0:T(8,128)S(1)} %shard_map.223.refs_5_), channel_id=1, source_target_pairs={{0,4},{1,5},{2,6},{3,7},{4,0},{5,1},{6,2},{7,3},{8,12},{9,13},{10,... | collective-permute-start | bytes 294920 | tf_op jit(solution)/shard_map/ppermute | solution.py:218
  81.2 1.2 collective-permute-done.15.refs_0_
  82.4 3.0 %collective-permute-done.16.refs_1_ = f32[32,768]{1,0:T(8,128)S(1)} collective-permute-done((f32[32,768]{1,0:T(8,128)S(1)}, f32[32,768]{1,0:T(8,128)S(1)}, u32[]{:S(2)}, u32[]{:S(2)}) %collective-permute-start.16) | collective-permute-done | bytes 98336 | tf_op jit(solution)/shard_map/ppermute | solution.py:218
  85.4 1.6 %collective-permute-start.18 = (f32[32,768]{1,0:T(8,128)S(1)}, f32[32,768]{1,0:T(8,128)S(1)}, u32[]{:S(2)}, u32[]{:S(2)}) collective-permute-start(f32[32,768]{1,0:T(8,128)S(1)} %shard_map.225.refs_0_), channel_id=1, source_target_pairs={{0,2},{1,3},{2,0},{3,1},{4,6},{5,7},{6,4},{7,5},{8,10},{9,11},{10,... | collective-permute-start | bytes 294920 | tf_op jit(solution)/shard_map/ppermute | solution.py:218
  87.0 3.1 %collective-permute-done.18.refs_1_ = f32[32,768]{1,0:T(8,128)S(1)} collective-permute-done((f32[32,768]{1,0:T(8,128)S(1)}, f32[32,768]{1,0:T(8,128)S(1)}, u32[]{:S(2)}, u32[]{:S(2)}) %collective-permute-start.18) | collective-permute-done | bytes 98336 | tf_op jit(solution)/shard_map/ppermute | solution.py:218
  90.1 1.5 %shard_map.226.refs_4_.refs_5_ = f32[32,768]{1,0:T(8,128)S(1)} custom-call(f32[32,768]{1,0:T(8,128)S(1)} %shard_map.225.refs_0_, f32[32,768]{1,0:T(8,128)S(1)} %collective-permute-done.18.refs_1_, f32[384,1536]{1,0:T(8,128)S(1)} %get-tuple-element.104.refs_2_, f32[384,1536]{1,0:T(8,128)S(1)} %get-tuple-element.105.refs_3_), custom_call_target="tpu_custom_call" | custom-call | tf_op jit(solution)/shard_map/pallas_call | solution.py:91
  91.6 1.2 collective-permute-start.19
  92.8 1.9 %collective-permute-start.20 = (f32[32,768]{1,0:T(8,128)S(1)}, f32[32,768]{1,0:T(8,128)S(1)}, u32[]{:S(2)}, u32[]{:S(2)}) collective-permute-start(f32[32,768]{1,0:T(8,128)S(1)} %shard_map.226.refs_4_.refs_5_), channel_id=1, source_target_pairs={{0,6},{1,7},{2,4},{3,5},{4,2},{5,3},{6,0},{7,1},{8,14},{9,15},{10,... | collective-permute-start | bytes 294920 | tf_op jit(solution)/shard_map/ppermute | solution.py:218
  94.9 1.4 collective-permute-done.19.refs_0_
  96.3 2.1 %collective-permute-done.20.refs_1_ = f32[32,768]{1,0:T(8,128)S(1)} collective-permute-done((f32[32,768]{1,0:T(8,128)S(1)}, f32[32,768]{1,0:T(8,128)S(1)}, u32[]{:S(2)}, u32[]{:S(2)}) %collective-permute-start.20) | collective-permute-done | bytes 98336 | tf_op jit(solution)/shard_map/ppermute | solution.py:218
  99.0 1.5 %collective-permute-start.23 = (f32[32,768]{1,0:T(8,128)S(1)}, f32[32,768]{1,0:T(8,128)}, u32[]{:S(2)}, u32[]{:S(2)}) collective-permute-start(f32[32,768]{1,0:T(8,128)S(1)} %shard_map.228.refs_5_), channel_id=1, source_target_pairs={{0,2},{1,3},{2,0},{3,1},{4,10},{5,11},{6,8},{7,9},{8,6},{9,7},{10,... | collective-permute-start | bytes 294920 | tf_op jit(solution)/shard_map/ppermute | solution.py:218
  100.6 2.0 %shard_map.229.refs_11_ = f32[512,1536]{1,0:T(8,128)S(1)} custom-call(f32[512,1536]{1,0:T(8,128)} %collective-permute-done.24.refs_0_), custom_call_target="tpu_custom_call" | custom-call | tf_op jit(solution)/shard_map/pallas_call | solution.py:114
  106.3 8.4 %collective-permute-start.25 = (f32[32,768]{1,0:T(8,128)S(1)}, f32[32,768]{1,0:T(8,128)S(1)}, u32[]{:S(2)}, u32[]{:S(2)}) collective-permute-start(f32[32,768]{1,0:T(8,128)S(1)} %shard_map.230.refs_0_.refs_5_), channel_id=1, source_target_pairs={{0,4},{1,5},{2,6},{3,7},{4,0},{5,1},{6,2},{7,3},{8,12},{9,13},{10,... | collective-permute-start | bytes 294920 | tf_op jit(solution)/shard_map/ppermute | solution.py:218
  115.6 1.5 %collective-permute-start.32 = (f32[32,768]{1,0:T(8,128)S(1)}, f32[32,768]{1,0:T(8,128)S(1)}, u32[]{:S(2)}, u32[]{:S(2)}) collective-permute-start(f32[32,768]{1,0:T(8,128)S(1)} %shard_map.230.refs_0_.refs_5_), channel_id=1, source_target_pairs={{0,2},{1,3},{2,0},{3,1},{4,8},{5,9},{6,10},{7,11},{8,4},{9,5},{10,... | collective-permute-start | bytes 294920 | tf_op jit(solution)/shard_map/ppermute | solution.py:218
  117.7 2.0 %shard_map.231.refs_1_ = f32[32,1024]{1,0:T(8,128)S(1)} custom-call(f32[32,768]{1,0:T(8,128)S(1)} %shard_map.230.refs_0_.refs_5_, f32[32,768]{1,0:T(8,128)S(1)} %collective-permute-done.27.refs_1_, f32[512,1536]{1,0:T(8,128)S(1)} %copy-done.1, f32[512,1536]{1,0:T(8,128)S(1)} %shard_map.227.refs_3_.refs_9_), custom_call_target="tpu_custom_call" | custom-call | tf_op jit(solution)/shard_map/pallas_call | solution.py:91
  120.3 1.5 %shard_map.232.refs_2_ = f32[32,768]{1,0:T(8,128)S(1)} custom-call(f32[32,768]{1,0:T(8,128)S(1)} %collective-permute-done.25.refs_0_, f32[32,768]{1,0:T(8,128)S(1)} %collective-permute-done.26.refs_1_, f32[384,1536]{1,0:T(8,128)S(1)} %copy-done.3, f32[384,1536]{1,0:T(8,128)S(1)} %copy-done.5, f32[32,768]{1,0:T(8,128)S(1)} %shard_map.226.refs_4_.refs_5_, ...), custom_call_target="tpu_custom_call" | custom-call | tf_op jit(solution)/shard_map/pallas_call | solution.py:91
  122.7 1.5 %collective-permute-start.30 = (f32[32,768]{1,0:T(8,128)S(1)}, f32[32,768]{1,0:T(8,128)S(1)}, u32[]{:S(2)}, u32[]{:S(2)}) collective-permute-start(f32[32,768]{1,0:T(8,128)S(1)} %shard_map.232.refs_2_), channel_id=1, source_target_pairs={{0,6},{1,7},{2,4},{3,5},{4,2},{5,3},{6,0},{7,1},{8,14},{9,15},{10,... | collective-permute-start | bytes 294920 | tf_op jit(solution)/shard_map/ppermute | solution.py:218
  124.2 2.3 %collective-permute-done.29.refs_4_ = f32[32,768]{1,0:T(8,128)S(1)} collective-permute-done((f32[32,768]{1,0:T(8,128)S(1)}, f32[32,768]{1,0:T(8,128)S(1)}, u32[]{:S(2)}, u32[]{:S(2)}) %collective-permute-start.29) | collective-permute-done | bytes 98336 | tf_op jit(solution)/shard_map/ppermute | solution.py:218
  127.4 2.3 %shard_map.233.refs_3_ = f32[512,2048]{1,0:T(8,128)S(1)} custom-call(f32[512,2048]{1,0:T(8,128)} %collective-permute-done.31.refs_0_), custom_call_target="tpu_custom_call" | custom-call | tf_op jit(solution)/shard_map/pallas_call | solution.py:114
  129.8 1.3 collective-permute-done.28.refs_3_
  131.2 2.0 %shard_map.234.refs_0_ = f32[32,1024]{1,0:T(8,128)S(1)} custom-call(f32[32,1024]{1,0:T(8,128)S(1)} %pad_maximum_fusion.refs_0_, f32[32,1024]{1,0:T(8,128)S(1)} %shard_map.231.refs_1_, f32[32,768]{1,0:T(8,128)S(1)} %shard_map.232.refs_2_, f32[32,768]{1,0:T(8,128)S(1)} %collective-permute-done.28.refs_3_, f32[32,768]{1,0:T(8,128)S(1)} %collective-permute-done.29.refs_4_, ...), custom_call_target="tpu_custom_call" | custom-call | tf_op jit(solution)/shard_map/pallas_call | solution.py:91
  134.2 4.4 %collective-permute-done.34.refs_1_ = f32[32,1024]{1,0:T(8,128)S(1)} collective-permute-done((f32[32,1024]{1,0:T(8,128)S(1)}, f32[32,1024]{1,0:T(8,128)S(1)}, u32[]{:S(2)}, u32[]{:S(2)}) %collective-permute-start.34) | collective-permute-done | bytes 131104 | tf_op jit(solution)/shard_map/ppermute | solution.py:218
  138.6 2.6 %shard_map.235 = (f32[32,512]{1,0:T(8,128)S(1)}, f32[32,512]{1,0:T(8,128)S(1)}) custom-call(f32[32,1024]{1,0:T(8,128)S(1)} %shard_map.234.refs_0_, f32[32,1024]{1,0:T(8,128)S(1)} %collective-permute-done.34.refs_1_, f32[512,2048]{1,0:T(8,128)S(1)} %copy-done.8, f32[512,2048]{1,0:T(8,128)S(1)} %shard_map.233.refs_3_), custom_call_target="tpu_custom_call" | custom-call | tf_op jit(solution)/shard_map/pallas_call | solution.py:91
  (121 shorter events, 21.5 us)
Async XLA Ops:
  0.6 38.0 %collective-permute-start.9 = (f32[384,1536]{1,0:T(8,128)}, f32[384,1536]{1,0:T(8,128)}, u32[]{:S(2)}, u32[]{:S(2)}) collective-permute-start(f32[384,1536]{1,0:T(8,128)} %bitcast.126), channel_id=1, source_target_pairs={{0,1},{1,0},{2,3},{3,2},{4,5},{5,4},{6,7},{7,6},{8,9},{9,8},{10,11... | collective-permute-start | bytes 7077896 | tf_op jit(solution)/shard_map/ppermute | solution.py:218
  3.2 11.6 %collective-permute-start.3 = (f32[64,512]{1,0:T(8,128)S(1)}, f32[64,512]{1,0:T(8,128)S(1)}, u32[]{:S(2)}, u32[]{:S(2)}) collective-permute-start(f32[64,512]{1,0:T(8,128)S(1)} %fusion.2.refs_0_), channel_id=1, source_target_pairs={{0,2},{1,3},{2,0},{3,1},{4,6},{5,7},{6,4},{7,5},{8,10},{9,11},{10,... | collective-permute-start | bytes 393224 | tf_op jit(solution)/shard_map/ppermute | solution.py:218
  5.7 9.4 %collective-permute-start.2 = (f32[64,512]{1,0:T(8,128)S(1)}, f32[64,512]{1,0:T(8,128)}, u32[]{:S(2)}, u32[]{:S(2)}) collective-permute-start(f32[64,512]{1,0:T(8,128)S(1)} %fusion.2.refs_0_), channel_id=1, source_target_pairs={{0,1},{1,0},{2,3},{3,2},{4,5},{5,4},{6,7},{7,6},{8,9},{9,8},{10,11... | collective-permute-start | bytes 393224 | tf_op jit(solution)/shard_map/ppermute | solution.py:218
  7.8 7.2 %copy-start.29 = (f32[1,384]{1,0:T(1,128)S(1)}, f32[1,384]{1,0:T(1,128)}, u32[]{:S(2)}) copy-start(f32[1,384]{1,0:T(1,128)} %param.23) | copy-start | bytes 4612
  14.8 9.8 %copy-start = (f32[512,1536]{1,0:T(8,128)}, f32[512,1536]{1,0:T(8,128)S(1)}, u32[]{:S(2)}) copy-start(f32[512,1536]{1,0:T(8,128)S(1)} %get-tuple-element.75.refs_5_.refs_2_.refs_8_) | copy-start | bytes 9437188
  14.8 1.5 %collective-permute-start.4 = (f32[64,512]{1,0:T(8,128)S(1)}, f32[64,512]{1,0:T(8,128)}, u32[]{:S(2)}, u32[]{:S(2)}) collective-permute-start(f32[64,512]{1,0:T(8,128)S(1)} %collective-permute-done.3.refs_2_), channel_id=1, source_target_pairs={{0,1},{1,0},{2,3},{3,2},{4,5},{5,4},{6,7},{7,6},{8,9},{9,8},{10,11... | collective-permute-start | bytes 393224 | tf_op jit(solution)/shard_map/ppermute | solution.py:218
  25.4 1.9 %collective-permute-start.5 = (f32[2,32,1536]{2,1,0:T(8,128)}, f32[2,32,1536]{2,1,0:T(8,128)S(1)}, u32[]{:S(2)}, u32[]{:S(2)}) collective-permute-start(f32[2,32,1536]{2,1,0:T(8,128)} %get-tuple-element.78), channel_id=1, source_target_pairs={{0,1},{1,0},{2,3},{3,2},{4,5},{5,4},{6,7},{7,6},{8,9},{9,8},{10,11... | collective-permute-start | bytes 1179656 | tf_op jit(solution)/shard_map/ppermute | solution.py:218
  25.8 5.7 %collective-permute-start.1 = (f32[32,384]{1,0:T(8,128)S(1)}, f32[32,384]{1,0:T(8,128)S(1)}, u32[]{:S(2)}, u32[]{:S(2)}) collective-permute-start(f32[32,384]{1,0:T(8,128)S(1)} %constant_dynamic-slice_fusion.1), channel_id=1, source_target_pairs={{0,1},{1,0},{2,3},{3,2},{4,5},{5,4},{6,7},{7,6},{8,9},{9,8},{10,11... | collective-permute-start | bytes 147464 | tf_op jit(solution)/shard_map/ppermute | solution.py:218
  28.3 13.9 %copy-start.13 = (f32[1,512,1536]{2,1,0:T(8,128)S(1)}, f32[1,512,1536]{2,1,0:T(8,128)}, u32[]{:S(2)}) copy-start(f32[1,512,1536]{2,1,0:T(8,128)} %param.32) | copy-start | bytes 9437188
  28.4 5.1 %collective-permute-start.6 = (f32[32,768]{1,0:T(8,128)S(1)}, f32[32,768]{1,0:T(8,128)S(1)}, u32[]{:S(2)}, u32[]{:S(2)}) collective-permute-start(f32[32,768]{1,0:T(8,128)S(1)} %get-tuple-element.80), channel_id=1, source_target_pairs={{0,2},{1,3},{2,0},{3,1},{4,6},{5,7},{6,4},{7,5},{8,10},{9,11},{10,... | collective-permute-start | bytes 294920 | tf_op jit(solution)/shard_map/ppermute | solution.py:218
  28.8 6.8 %collective-permute-start.7 = (f32[32,768]{1,0:T(8,128)S(1)}, f32[32,768]{1,0:T(8,128)S(1)}, u32[]{:S(2)}, u32[]{:S(2)}) collective-permute-start(f32[32,768]{1,0:T(8,128)S(1)} %get-tuple-element.81), channel_id=1, source_target_pairs={{4,0},{5,1},{6,2},{7,3},{8,4},{9,5},{10,6},{11,7},{12,8},{13,9},{1... | collective-permute-start | bytes 294920 | tf_op jit(solution)/shard_map/ppermute | solution.py:262
  30.2 8.4 %collective-permute-start.8 = (f32[32,768]{1,0:T(8,128)S(1)}, f32[32,768]{1,0:T(8,128)S(1)}, u32[]{:S(2)}, u32[]{:S(2)}) collective-permute-start(f32[32,768]{1,0:T(8,128)S(1)} %get-tuple-element.82), channel_id=1, source_target_pairs={{4,2},{5,3},{6,0},{7,1},{8,6},{9,7},{10,4},{11,5},{12,10},{13,11},... | collective-permute-start | bytes 294920 | tf_op jit(solution)/shard_map/ppermute | solution.py:262
  42.2 85.2 %collective-permute-start.31 = (f32[512,2048]{1,0:T(8,128)}, f32[512,2048]{1,0:T(8,128)}, u32[]{:S(2)}, u32[]{:S(2)}) collective-permute-start(f32[512,2048]{1,0:T(8,128)} %bitcast.14.refs_0_), channel_id=1, source_target_pairs={{0,1},{1,0},{2,3},{3,2},{4,5},{5,4},{6,7},{7,6},{8,9},{9,8},{10,11... | collective-permute-start | bytes 12582920 | tf_op jit(solution)/shard_map/ppermute | solution.py:218
  42.3 52.5 %collective-permute-start.21 = (f32[512,1536]{1,0:T(8,128)S(1)}, f32[512,1536]{1,0:T(8,128)S(1)}, u32[]{:S(2)}, u32[]{:S(2)}) collective-permute-start(f32[512,1536]{1,0:T(8,128)S(1)} %bitcast.125), channel_id=1, source_target_pairs={{0,1},{1,0},{2,3},{3,2},{4,5},{5,4},{6,7},{7,6},{8,9},{9,8},{10,11... | collective-permute-start | bytes 9437192 | tf_op jit(solution)/shard_map/ppermute | solution.py:218
  42.7 57.9 %collective-permute-start.24 = (f32[512,1536]{1,0:T(8,128)}, f32[512,1536]{1,0:T(8,128)}, u32[]{:S(2)}, u32[]{:S(2)}) collective-permute-start(f32[512,1536]{1,0:T(8,128)} %bitcast.16.refs_2_), channel_id=1, source_target_pairs={{0,1},{1,0},{2,3},{3,2},{4,5},{5,4},{6,7},{7,6},{8,9},{9,8},{10,11... | collective-permute-start | bytes 9437192 | tf_op jit(solution)/shard_map/ppermute | solution.py:218
  42.8 17.5 %collective-permute-start.12 = (f32[384,1536]{1,0:T(8,128)}, f32[384,1536]{1,0:T(8,128)S(1)}, u32[]{:S(2)}, u32[]{:S(2)}) collective-permute-start(f32[384,1536]{1,0:T(8,128)} %bitcast.128), channel_id=1, source_target_pairs={{0,1},{1,0},{2,3},{3,2},{4,5},{5,4},{6,7},{7,6},{8,9},{9,8},{10,11... | collective-permute-start | bytes 7077896 | tf_op jit(solution)/shard_map/ppermute | solution.py:218
  43.3 4.8 %collective-permute-start.10 = (f32[32,768]{1,0:T(8,128)S(1)}, f32[32,768]{1,0:T(8,128)S(1)}, u32[]{:S(2)}, u32[]{:S(2)}) collective-permute-start(f32[32,768]{1,0:T(8,128)S(1)} %fusion.8.refs_4_.refs_5_), channel_id=1, source_target_pairs={{0,4},{1,5},{2,6},{3,7},{4,0},{5,1},{6,2},{7,3},{8,12},{9,13},{10,... | collective-permute-start | bytes 294920 | tf_op jit(solution)/shard_map/ppermute | solution.py:218
  48.0 31.7 %collective-permute-start.17 = (f32[384,1536]{1,0:T(8,128)}, f32[384,1536]{1,0:T(8,128)S(1)}, u32[]{:S(2)}, u32[]{:S(2)}) collective-permute-start(f32[384,1536]{1,0:T(8,128)} %bitcast.130), channel_id=1, source_target_pairs={{0,1},{1,0},{2,3},{3,2},{4,5},{5,4},{6,7},{7,6},{8,9},{9,8},{10,11... | collective-permute-start | bytes 7077896 | tf_op jit(solution)/shard_map/ppermute | solution.py:218
  60.3 6.0 %collective-permute-start.11 = (f32[32,768]{1,0:T(8,128)S(1)}, f32[32,768]{1,0:T(8,128)S(1)}, u32[]{:S(2)}, u32[]{:S(2)}) collective-permute-start(f32[32,768]{1,0:T(8,128)S(1)} %fusion.8.refs_4_.refs_5_), channel_id=1, source_target_pairs={{0,6},{1,7},{2,4},{3,5},{4,2},{5,3},{6,0},{7,1},{8,14},{9,15},{10,... | collective-permute-start | bytes 294920 | tf_op jit(solution)/shard_map/ppermute | solution.py:218
  66.3 14.5 %copy-start.16 = (f32[1,384,1536]{2,1,0:T(8,128)S(1)}, f32[1,384,1536]{2,1,0:T(8,128)}, u32[]{:S(2)}) copy-start(f32[1,384,1536]{2,1,0:T(8,128)} %param.35) | copy-start | bytes 7077892
  66.3 4.7 %collective-permute-start.13 = (f32[32,768]{1,0:T(8,128)S(1)}, f32[32,768]{1,0:T(8,128)S(1)}, u32[]{:S(2)}, u32[]{:S(2)}) collective-permute-start(f32[32,768]{1,0:T(8,128)S(1)} %shard_map.222.refs_5_), channel_id=1, source_target_pairs={{0,2},{1,3},{2,0},{3,1},{4,8},{5,9},{6,10},{7,11},{8,4},{9,5},{10,... | collective-permute-start | bytes 294920 | tf_op jit(solution)/shard_map/ppermute | solution.py:218
  71.0 4.6 %collective-permute-start.14 = (f32[32,768]{1,0:T(8,128)S(1)}, f32[32,768]{1,0:T(8,128)S(1)}, u32[]{:S(2)}, u32[]{:S(2)}) collective-permute-start(f32[32,768]{1,0:T(8,128)S(1)} %shard_map.222.refs_5_), channel_id=1, source_target_pairs={{0,2},{1,3},{2,0},{3,1},{4,10},{5,11},{6,8},{7,9},{8,6},{9,7},{10,... | collective-permute-start | bytes 294920 | tf_op jit(solution)/shard_map/ppermute | solution.py:218
  75.6 6.8 %collective-permute-start.15 = (f32[32,768]{1,0:T(8,128)S(1)}, f32[32,768]{1,0:T(8,128)S(1)}, u32[]{:S(2)}, u32[]{:S(2)}) collective-permute-start(f32[32,768]{1,0:T(8,128)S(1)} %shard_map.223.refs_5_), channel_id=1, source_target_pairs={{0,4},{1,5},{2,6},{3,7},{4,0},{5,1},{6,2},{7,3},{8,12},{9,13},{10,... | collective-permute-start | bytes 294920 | tf_op jit(solution)/shard_map/ppermute | solution.py:218
  79.8 5.6 %collective-permute-start.16 = (f32[32,768]{1,0:T(8,128)S(1)}, f32[32,768]{1,0:T(8,128)S(1)}, u32[]{:S(2)}, u32[]{:S(2)}) collective-permute-start(f32[32,768]{1,0:T(8,128)S(1)} %shard_map.223.refs_5_), channel_id=1, source_target_pairs={{0,6},{1,7},{2,4},{3,5},{4,2},{5,3},{6,0},{7,1},{8,14},{9,15},{10,... | collective-permute-start | bytes 294920 | tf_op jit(solution)/shard_map/ppermute | solution.py:218
  81.2 17.3 %copy-start.2 = (f32[384,1536]{1,0:T(8,128)}, f32[384,1536]{1,0:T(8,128)S(1)}, u32[]{:S(2)}) copy-start(f32[384,1536]{1,0:T(8,128)S(1)} %get-tuple-element.110.refs_2_) | copy-start | bytes 7077892
  81.2 17.3 %copy-start.4 = (f32[384,1536]{1,0:T(8,128)}, f32[384,1536]{1,0:T(8,128)S(1)}, u32[]{:S(2)}) copy-start(f32[384,1536]{1,0:T(8,128)S(1)} %get-tuple-element.111.refs_3_) | copy-start | bytes 7077892
  85.4 4.7 %collective-permute-start.18 = (f32[32,768]{1,0:T(8,128)S(1)}, f32[32,768]{1,0:T(8,128)S(1)}, u32[]{:S(2)}, u32[]{:S(2)}) collective-permute-start(f32[32,768]{1,0:T(8,128)S(1)} %shard_map.225.refs_0_), channel_id=1, source_target_pairs={{0,2},{1,3},{2,0},{3,1},{4,6},{5,7},{6,4},{7,5},{8,10},{9,11},{10,... | collective-permute-start | bytes 294920 | tf_op jit(solution)/shard_map/ppermute | solution.py:218
  91.6 4.7 %collective-permute-start.19 = (f32[32,768]{1,0:T(8,128)S(1)}, f32[32,768]{1,0:T(8,128)S(1)}, u32[]{:S(2)}, u32[]{:S(2)}) collective-permute-start(f32[32,768]{1,0:T(8,128)S(1)} %shard_map.226.refs_4_.refs_5_), channel_id=1, source_target_pairs={{0,4},{1,5},{2,6},{3,7},{4,0},{5,1},{6,2},{7,3},{8,12},{9,13},{10,... | collective-permute-start | bytes 294920 | tf_op jit(solution)/shard_map/ppermute | solution.py:218
  92.8 5.6 %collective-permute-start.20 = (f32[32,768]{1,0:T(8,128)S(1)}, f32[32,768]{1,0:T(8,128)S(1)}, u32[]{:S(2)}, u32[]{:S(2)}) collective-permute-start(f32[32,768]{1,0:T(8,128)S(1)} %shard_map.226.refs_4_.refs_5_), channel_id=1, source_target_pairs={{0,6},{1,7},{2,4},{3,5},{4,2},{5,3},{6,0},{7,1},{8,14},{9,15},{10,... | collective-permute-start | bytes 294920 | tf_op jit(solution)/shard_map/ppermute | solution.py:218
  98.5 4.8 %collective-permute-start.22 = (f32[32,768]{1,0:T(8,128)S(1)}, f32[32,768]{1,0:T(8,128)}, u32[]{:S(2)}, u32[]{:S(2)}) collective-permute-start(f32[32,768]{1,0:T(8,128)S(1)} %shard_map.228.refs_5_), channel_id=1, source_target_pairs={{0,2},{1,3},{2,0},{3,1},{4,8},{5,9},{6,10},{7,11},{8,4},{9,5},{10,... | collective-permute-start | bytes 294920 | tf_op jit(solution)/shard_map/ppermute | solution.py:218
  99.0 5.3 %collective-permute-start.23 = (f32[32,768]{1,0:T(8,128)S(1)}, f32[32,768]{1,0:T(8,128)}, u32[]{:S(2)}, u32[]{:S(2)}) collective-permute-start(f32[32,768]{1,0:T(8,128)S(1)} %shard_map.228.refs_5_), channel_id=1, source_target_pairs={{0,2},{1,3},{2,0},{3,1},{4,10},{5,11},{6,8},{7,9},{8,6},{9,7},{10,... | collective-permute-start | bytes 294920 | tf_op jit(solution)/shard_map/ppermute | solution.py:218
  100.6 14.1 %collective-permute-start = (f32[32,512]{1,0:T(8,128)S(1)}, f32[32,512]{1,0:T(8,128)}, u32[]{:S(2)}, u32[]{:S(2)}) collective-permute-start(f32[32,512]{1,0:T(8,128)S(1)} %constant_dynamic-slice_fusion.2), channel_id=1, source_target_pairs={{0,1},{1,0},{2,3},{3,2},{4,5},{5,4},{6,7},{7,6},{8,9},{9,8},{10,11... | collective-permute-start | bytes 196616 | tf_op jit(solution)/shard_map/ppermute | solution.py:218
  102.7 15.0 %copy-start.1 = (f32[512,1536]{1,0:T(8,128)S(1)}, f32[512,1536]{1,0:T(8,128)}, u32[]{:S(2)}) copy-start(f32[512,1536]{1,0:T(8,128)} %copy-done) | copy-start | bytes 9437188
  105.3 11.8 %collective-permute-start.27 = (f32[32,768]{1,0:T(8,128)S(1)}, f32[32,768]{1,0:T(8,128)S(1)}, u32[]{:S(2)}, u32[]{:S(2)}) collective-permute-start(f32[32,768]{1,0:T(8,128)S(1)} %shard_map.230.refs_0_.refs_5_), channel_id=1, source_target_pairs={{0,2},{1,3},{2,0},{3,1},{4,6},{5,7},{6,4},{7,5},{8,10},{9,11},{10,... | collective-permute-start | bytes 294920 | tf_op jit(solution)/shard_map/ppermute | solution.py:218
  106.3 13.4 %collective-permute-start.25 = (f32[32,768]{1,0:T(8,128)S(1)}, f32[32,768]{1,0:T(8,128)S(1)}, u32[]{:S(2)}, u32[]{:S(2)}) collective-permute-start(f32[32,768]{1,0:T(8,128)S(1)} %shard_map.230.refs_0_.refs_5_), channel_id=1, source_target_pairs={{0,4},{1,5},{2,6},{3,7},{4,0},{5,1},{6,2},{7,3},{8,12},{9,13},{10,... | collective-permute-start | bytes 294920 | tf_op jit(solution)/shard_map/ppermute | solution.py:218
  114.7 5.6 %collective-permute-start.26 = (f32[32,768]{1,0:T(8,128)S(1)}, f32[32,768]{1,0:T(8,128)S(1)}, u32[]{:S(2)}, u32[]{:S(2)}) collective-permute-start(f32[32,768]{1,0:T(8,128)S(1)} %shard_map.230.refs_0_.refs_5_), channel_id=1, source_target_pairs={{0,6},{1,7},{2,4},{3,5},{4,2},{5,3},{6,0},{7,1},{8,14},{9,15},{10,... | collective-permute-start | bytes 294920 | tf_op jit(solution)/shard_map/ppermute | solution.py:218
  115.6 14.2 %collective-permute-start.32 = (f32[32,768]{1,0:T(8,128)S(1)}, f32[32,768]{1,0:T(8,128)S(1)}, u32[]{:S(2)}, u32[]{:S(2)}) collective-permute-start(f32[32,768]{1,0:T(8,128)S(1)} %shard_map.230.refs_0_.refs_5_), channel_id=1, source_target_pairs={{0,2},{1,3},{2,0},{3,1},{4,8},{5,9},{6,10},{7,11},{8,4},{9,5},{10,... | collective-permute-start | bytes 294920 | tf_op jit(solution)/shard_map/ppermute | solution.py:218
  117.1 12.7 %collective-permute-start.33 = (f32[32,768]{1,0:T(8,128)S(1)}, f32[32,768]{1,0:T(8,128)S(1)}, u32[]{:S(2)}, u32[]{:S(2)}) collective-permute-start(f32[32,768]{1,0:T(8,128)S(1)} %shard_map.230.refs_0_.refs_5_), channel_id=1, source_target_pairs={{0,2},{1,3},{2,0},{3,1},{4,10},{5,11},{6,8},{7,9},{8,6},{9,7},{10,... | collective-permute-start | bytes 294920 | tf_op jit(solution)/shard_map/ppermute | solution.py:218
  121.9 4.7 %collective-permute-start.29 = (f32[32,768]{1,0:T(8,128)S(1)}, f32[32,768]{1,0:T(8,128)S(1)}, u32[]{:S(2)}, u32[]{:S(2)}) collective-permute-start(f32[32,768]{1,0:T(8,128)S(1)} %shard_map.232.refs_2_), channel_id=1, source_target_pairs={{0,4},{1,5},{2,6},{3,7},{4,0},{5,1},{6,2},{7,3},{8,12},{9,13},{10,... | collective-permute-start | bytes 294920 | tf_op jit(solution)/shard_map/ppermute | solution.py:218
  122.7 7.1 %collective-permute-start.30 = (f32[32,768]{1,0:T(8,128)S(1)}, f32[32,768]{1,0:T(8,128)S(1)}, u32[]{:S(2)}, u32[]{:S(2)}) collective-permute-start(f32[32,768]{1,0:T(8,128)S(1)} %shard_map.232.refs_2_), channel_id=1, source_target_pairs={{0,6},{1,7},{2,4},{3,5},{4,2},{5,3},{6,0},{7,1},{8,14},{9,15},{10,... | collective-permute-start | bytes 294920 | tf_op jit(solution)/shard_map/ppermute | solution.py:218
  126.6 4.6 %collective-permute-start.28 = (f32[32,768]{1,0:T(8,128)S(1)}, f32[32,768]{1,0:T(8,128)S(1)}, u32[]{:S(2)}, u32[]{:S(2)}) collective-permute-start(f32[32,768]{1,0:T(8,128)S(1)} %shard_map.232.refs_2_), channel_id=1, source_target_pairs={{0,2},{1,3},{2,0},{3,1},{4,6},{5,7},{6,4},{7,5},{8,10},{9,11},{10,... | collective-permute-start | bytes 294920 | tf_op jit(solution)/shard_map/ppermute | solution.py:218
  127.4 6.7 %collective-permute-start.36 = (f32[32,384]{1,0:T(8,128)S(1)}, f32[32,384]{1,0:T(8,128)S(1)}, u32[]{:S(2)}, u32[]{:S(2)}) collective-permute-start(f32[32,384]{1,0:T(8,128)S(1)} %constant_dynamic-slice_fusion), channel_id=1, source_target_pairs={{0,1},{1,0},{2,3},{3,2},{4,5},{5,4},{6,7},{7,6},{8,9},{9,8},{10,11... | collective-permute-start | bytes 147464 | tf_op jit(solution)/shard_map/ppermute | solution.py:218
  129.8 8.8 %copy-start.8 = (f32[512,2048]{1,0:T(8,128)S(1)}, f32[512,2048]{1,0:T(8,128)}, u32[]{:S(2)}) copy-start(f32[512,2048]{1,0:T(8,128)} %copy-done.6) | copy-start | bytes 12582916
  133.2 5.4 %collective-permute-start.34 = (f32[32,1024]{1,0:T(8,128)S(1)}, f32[32,1024]{1,0:T(8,128)S(1)}, u32[]{:S(2)}, u32[]{:S(2)}) collective-permute-start(f32[32,1024]{1,0:T(8,128)S(1)} %shard_map.234.refs_0_), channel_id=1, source_target_pairs={{0,2},{1,3},{2,0},{3,1},{4,6},{5,7},{6,4},{7,5},{8,10},{9,11},{10,... | collective-permute-start | bytes 393224 | tf_op jit(solution)/shard_map/ppermute | solution.py:218
  134.2 8.3 %copy-start.19 = (f32[1,512,64]{1,2,0:T(8,128)S(1)}, f32[1,512,64]{1,2,0:T(8,128)}, u32[]{:S(2)}) copy-start(f32[1,512,64]{1,2,0:T(8,128)} %param.26) | copy-start | bytes 393220
  134.2 8.3 %copy-start.20 = (f32[1,512,64]{1,2,0:T(8,128)S(1)}, f32[1,512,64]{1,2,0:T(8,128)}, u32[]{:S(2)}) copy-start(f32[1,512,64]{1,2,0:T(8,128)} %param.25) | copy-start | bytes 393220
  134.2 8.3 %copy-start.21 = (f32[1,512,64]{1,2,0:T(8,128)S(1)}, f32[1,512,64]{1,2,0:T(8,128)}, u32[]{:S(2)}) copy-start(f32[1,512,64]{1,2,0:T(8,128)} %param.24) | copy-start | bytes 393220
  141.2 1.3 collective-permute-start.35
  (19 other events, 70.5 us)

commit v5 on v4

--- a/solution.py
+++ b/solution.py
@@ -77,7 +77,7 @@
     ref[...] = jnp.concatenate([jnp.where(swap, other, own), jnp.where(swap, own, other)], axis=1)
 
 
-def call(kernel, shapes, *groups):
+def call(kernel, shapes, *groups, cost=0):
     flat = [value for group in groups for value in group]
 
     def body(*refs):
@@ -94,18 +94,32 @@
         out_specs=[VMEM] * len(out),
         out_shape=out,
         compiler_params=pltpu.CompilerParams(vmem_limit_bytes=24 << 20),
+        cost_estimate=pl.CostEstimate(flops=0, bytes_accessed=cost, transcendentals=0) if cost else None,
     )(*flat)
 
 
 def staged(*matrices, after):
     held = lax.optimization_barrier([*matrices, *after])[: len(matrices)]
+    held = [pltpu.with_memory_space_constraint(matrix, pltpu.HBM) for matrix in held]
+    count = len(held)
+    rows = held[0].shape[0]
+    ends = [0]
+    for matrix in held:
+        ends.append(ends[-1] + matrix.shape[1])
 
     def body(*refs):
-        count = len(held)
-        sems = refs[-1]
-        copies = [
-            pltpu.make_async_copy(refs[i], refs[count + i], sems.at[i]) for i in range(count)
-        ]
+        out, sems = refs[count:]
+        copies = []
+        for i in range(count):
+            for j in range(2):
+                part = pl.ds(j * (rows // 2), rows // 2)
+                copies.append(
+                    pltpu.make_async_copy(
+                        refs[i].at[part, :],
+                        out.at[part, ends[i] : ends[i + 1]],
+                        sems.at[2 * i + j],
+                    )
+                )
         for copy in copies:
             copy.start()
         for copy in copies:
@@ -113,16 +127,21 @@
 
     return pl.pallas_call(
         body,
-        in_specs=[pl.BlockSpec(memory_space=pltpu.HBM)] * len(held),
-        out_specs=[VMEM] * len(held),
-        out_shape=[pltpu.VMEM(matrix.shape, matrix.dtype) for matrix in held],
-        scratch_shapes=[pltpu.SemaphoreType.DMA((len(held),))],
+        in_specs=[pl.BlockSpec(memory_space=pltpu.HBM)] * count,
+        out_specs=VMEM,
+        out_shape=pltpu.VMEM((rows, ends[-1]), jnp.float32),
+        scratch_shapes=[pltpu.SemaphoreType.DMA((2 * count,))],
         compiler_params=pltpu.CompilerParams(vmem_limit_bytes=24 << 20),
     )(*held)
 
 
 def forces_kernel(swap_chips, pieces, matrices, mine, theirs):
-    inverse, above, below = matrices
+    (rows,) = matrices
+    faces = mine.shape[2]
+    inner = rows.shape[1] - 2 * faces
+    inverse = rows.at[:, :inner]
+    above = rows.at[:, inner : inner + faces]
+    below = rows.at[:, inner + faces :]
     if swap_chips:
         chips = len(pieces) // 2
         core = lax.axis_index("blk")
@@ -140,6 +159,43 @@
         theirs[i] = jnp.where(second, force[:half], force[half:])
 
 
+def records_kernel(whole, mine, theirs):
+    value = whole[0][...]
+    half = value.shape[0] // 2
+    second = lax.axis_index("blk") == 1
+    mine[...] = jnp.where(second, value[half:], value[:half])
+    theirs[...] = jnp.where(second, value[:half], value[half:])
+
+
+def by_core(own, other, axis):
+    second = lax.axis_index("blk") == 1
+    return jnp.concatenate([jnp.where(second, other, own), jnp.where(second, own, other)], axis=axis)
+
+
+def condensed_kernel(load, forces, out):
+    value = by_core(load[0][...], load[1][...], 1)
+    for force in forces:
+        value = value - force[...]
+    out[...] = value
+
+
+def halves_kernel(whole, mine, theirs):
+    value = whole[0][...]
+    half = value.shape[1] // 2
+    second = lax.axis_index("blk") == 1
+    mine[...] = jnp.where(second, value[:, half:], value[:, :half])
+    theirs[...] = jnp.where(second, value[:, :half], value[:, half:])
+
+
+def outputs_kernel(halves, before, new_disp, new_vel, new_acc):
+    disp, vel, acc = before
+    value = by_core(halves[0][...], halves[1][...], 0)
+    change = value - disp[...] - 2.0 * vel[...] - acc[...]
+    new_disp[...] = value
+    new_vel[...] = vel[...] + acc[...] + change
+    new_acc[...] = change
+
+
 def chunks_kernel(inputs, *outs):
     mine, came = inputs
     chips = len(outs) // 2
@@ -174,7 +230,7 @@
     @pl.when(story == 0)
     def _():
         store_rows(out, times_rows(joined(here), *above))
-        out[...] = load[0][...] - out[...]
+        out[...] = by_core(load[0][...], load[1][...], 1) - out[...]
 
     @pl.when(story > 0)
     def _():
@@ -183,7 +239,7 @@
         own = lax.axis_index("rec") if len(refs) > 1 else 0
         value = jnp.concatenate(in_order(refs, own), axis=1)
         store_rows(out, times_rows(value, *below))
-        out[...] = load[0][...] - early[0][...] - out[...]
+        out[...] = by_core(load[0][...], load[1][...], 1) - early[0][...] - out[...]
 
 
 def last_kernel(pieces, rows, mine, theirs):
@@ -266,18 +322,6 @@
 
     def gather_story(self, value, parity):
         return self.pieces([self.story(value, parity, j) for j in range(self.chips)])
-
-    def half(self, value, which, axis=0):
-        width = value.shape[axis] // 2
-        return lax.dynamic_slice_in_dim(value, which * width, width, axis)
-
-    def to_half(self, value):
-        other = self.core(self.half(value, 1 - self.b))
-        return self.by_core(self.half(value, self.b), other, 1)
-
-    def from_half(self, value):
-        other = self.core(self.half(value, 1 - self.b, 1))
-        return self.by_core(self.half(value, self.b, 1), other, 0)
 
 
 def shards(
@@ -301,33 +345,32 @@
     upper,
 ):
     mv = Moves()
-    s, r, b = mv.s, mv.r, mv.b
-    last = mv.stories - 1
-    library = ground_table.shape[0]
+    library, records = ground_table.shape[0], record_ids.shape[0]
+    half = records // 2
+    cube_int = [value[0].T for value in (disp_int, vel_int, acc_int)]
+    cube_face = [value[0].T for value in (disp_face, vel_face, acc_face)]
+    own_int, own_face = cube_int[0].shape[1], cube_face[0].shape[1]
     picked = record_ids[:, None] == jnp.arange(library, dtype=jnp.int32)[None, :]
-    ground = jnp.sum(jnp.where(picked, ground_table[None, :], 0.0), axis=1)
-    d_i, v_i, a_i = disp_int[0].T, vel_int[0].T, acc_int[0].T
-    d_f, v_f, a_f = disp_face[0].T, vel_face[0].T, acc_face[0].T
-    load_int = mass_int * (d_i + 2.0 * v_i + a_i - pattern_int * ground[:, None])
-    load_face = mass_face * (d_f + 2.0 * v_f + a_f - pattern_face * ground[:, None])
-
-    records = load_int.shape[0]
-    half = records // 2
-    rows_int, rows_face = 2 * load_int.shape[1], 2 * load_face.shape[1]
+    ground = jnp.sum(jnp.where(picked, ground_table[None, :], 0.0), axis=1)[:, None]
+
+    def newmark_load(mass, pattern, values):
+        disp, vel, acc = values
+        return mass * (disp + 2.0 * vel + acc - pattern * ground)
+
+    load_int = newmark_load(mass_int, pattern_int, cube_int)
+    load_face = newmark_load(mass_face, pattern_face, cube_face)
+    rows_int, rows_face = 2 * own_int, 2 * own_face
     faces = couple_above.shape[2]
 
     def others(matrix, after):
         return mv.core(lax.optimization_barrier([matrix, *after])[0])
 
-    inverse_own, above_own, below_own = interior_inverse[0], couple_above[0], couple_below[0]
     lower_other = mv.core(lower[0])
     across = [mv.chip(load_int, j) for j in range(1, mv.chips)]
-    inverse_own, above_own, below_own = staged(
-        inverse_own, above_own, below_own, after=[load_int]
-    )
-    inverse_own, above_own, below_own, *across = lax.optimization_barrier(
-        [inverse_own, above_own, below_own, *across]
-    )
+    phase_rows = staged(
+        interior_inverse[0], couple_above[0], couple_below[0], after=[load_int, load_face]
+    )
+    phase_rows, *across = lax.optimization_barrier([phase_rows, *across])
     beside = [mv.core(piece) for piece in [load_int] + across]
     pieces = [piece for pair in zip([load_int] + across, beside) for piece in pair]
     aligned = load_int.shape[1] % 128 == 0
@@ -336,96 +379,97 @@
             mv.by_chip([mv.by_core(pieces[2 * j], pieces[2 * j + 1], 1) for j in range(mv.chips)])
         ]
     mine, theirs = call(
-        functools.partial(forces_kernel, aligned),
-        [(2, half, faces)] * 2,
-        pieces,
-        [inverse_own, above_own, below_own],
-    )
-    load_face_half, load_int_half = mv.to_half(load_face), mv.to_half(load_int)
+        functools.partial(forces_kernel, aligned), [(2, half, faces)] * 2, pieces, [phase_rows]
+    )
+    mine_face, theirs_face = call(records_kernel, [(half, own_face)] * 2, [load_face])
+    mine_int, theirs_int = call(records_kernel, [(half, own_int)] * 2, [load_int])
+    load_face_half = [mine_face, mv.core(theirs_face)]
+    load_int_half = [mine_int, mv.core(theirs_int)]
     chunks = call(
         chunks_kernel,
         [(half, faces // mv.chips)] * (2 * mv.chips),
         [mine, mv.core(theirs)],
     )
     pivot_other = others(pivot[0], [chunks[0]])
-    upper_other = others(upper[0], [chunks[0]])
-    above_force = chunks[0]
-    below_force = mv.below(chunks[mv.chips], 0)
+    forces = [mv.below(chunks[mv.chips], 0)]
     for j in range(1, mv.chips):
-        above_force = above_force + mv.chip(chunks[j], j)
-        below_force = below_force + mv.below(chunks[mv.chips + j], j)
-    lower_rows = staged(lower[0], lower_other, after=[chunks[0]])
-    condensed = load_face_half - above_force - below_force
-    condensed, *lower_rows = lax.optimization_barrier([condensed, *lower_rows])
-
+        forces += [mv.chip(chunks[j], j), mv.below(chunks[mv.chips + j], j)]
     shape = [(half, rows_face)]
+    (condensed,) = call(condensed_kernel, shape, load_face_half, [chunks[0]] + forces)
+
     forward = condensed
     for k in range(1, mv.stories):
         came = mv.gather_story(forward, (k - 1) % 2)
-        if k == 1:
-            pivot_rows = staged(pivot[0], pivot_other, after=[forward])
-            *came, p0, p1 = lax.optimization_barrier([*came, *pivot_rows])
-            pivot_rows = [p0, p1]
+        if k == min(2, mv.stories - 1):
+            *came, pivot_other = lax.optimization_barrier([*came, pivot_other])
+            upper_other = others(upper[0], [forward])
+        if k == mv.stories - 1:
+            *came, upper_other = lax.optimization_barrier([*came, upper_other])
             above_other = others(couple_above[0], [forward])
-            below_other = others(couple_below[0], [forward])
-            inverse_other = others(interior_inverse[0], [forward])
-        if k == mv.stories - 1:
-            upper_rows = staged(upper[0], upper_other, after=[forward])
-            *came, u0, u1 = lax.optimization_barrier([*came, *upper_rows])
-            upper_rows = [u0, u1]
         (forward,) = call(
-            functools.partial(step_kernel, k), shape, came, lower_rows, [condensed, forward]
+            functools.partial(step_kernel, k),
+            shape,
+            came,
+            [lower[0], lower_other],
+            [condensed, forward],
         )
-    (pivoted,) = call(rows_kernel, shape, mv.gather_chips(forward), pivot_rows)
+    came = mv.gather_chips(forward)
+    below_other = others(couple_below[0], [forward])
+    *came, above_other = lax.optimization_barrier([*came, above_other])
+    (pivoted,) = call(rows_kernel, shape, came, [pivot[0], pivot_other])
 
     shape_int = [(half, rows_int)]
     face = pivoted
     for k in range(mv.stories - 2, -1, -1):
         came = mv.gather_story(face, k % 2)
         if k == mv.stories - 2:
-            (above_other,) = staged(above_other, after=[face])
-            *came, above_other = lax.optimization_barrier([*came, above_other])
-        if k == max(mv.stories - 3, 0):
-            (below_other,) = staged(below_other, after=[face])
+            inverse_other = others(interior_inverse[0], [face])
             *came, below_other = lax.optimization_barrier([*came, below_other])
         if k == 0:
             odd = mv.gather_story(face, 1)
             (early,) = call(
-                rows_kernel, shape_int, mv.gather_chips(face), [above_own, above_other]
+                rows_kernel,
+                shape_int,
+                mv.gather_chips(face),
+                [couple_above[0], above_other],
+                cost=8 << 20,
             )
-            *came, early = lax.optimization_barrier([*came, early])
+            *came, early, inverse_other = lax.optimization_barrier([*came, early, inverse_other])
         (face,) = call(
-            functools.partial(step_kernel, k), shape, came, upper_rows, [pivoted, face]
+            functools.partial(step_kernel, k),
+            shape,
+            came,
+            [upper[0], upper_other],
+            [pivoted, face],
         )
 
     even = mv.gather_story(face, 0)
-    (inverse_other,) = staged(inverse_other, after=[face])
-    *even, inverse_other = lax.optimization_barrier([*even, inverse_other])
     (reduced,) = call(
         coupled_kernel,
         shape_int,
-        [load_int_half],
+        load_int_half,
         [early],
         mv.gather_chips(face),
         even,
         odd,
-        [above_own, above_other],
-        [below_own, below_other],
+        [couple_above[0], above_other],
+        [couple_below[0], below_other],
     )
     mine, theirs = call(
         last_kernel,
         [(half, rows_int // 2)] * 2,
         mv.gather_chips(reduced),
-        [inverse_own, inverse_other],
-    )
-
-    u_f = mv.from_half(face)
-    u_i = mv.by_core(mine, mv.core(theirs), 0)
-    new_a_i = u_i - d_i - 2.0 * v_i - a_i
-    new_a_f = u_f - d_f - 2.0 * v_f - a_f
-    new_v_i = v_i + a_i + new_a_i
-    new_v_f = v_f + a_f + new_a_f
-    return tuple(out.T[None] for out in (u_i, new_v_i, new_a_i, u_f, new_v_f, new_a_f))
+        [interior_inverse[0], inverse_other],
+    )
+
+    new_int = call(
+        outputs_kernel, [(records, own_int)] * 3, [mine, mv.core(theirs)], cube_int
+    )
+    mine, theirs = call(halves_kernel, [(half, own_face)] * 2, [face])
+    new_face = call(
+        outputs_kernel, [(records, own_face)] * 3, [mine, mv.core(theirs)], cube_face
+    )
+    return tuple(out.T[None] for out in (*new_int, *new_face))
 
 
 def solution(mesh):

time: 144 us -> 118 us (0.82)
  local copies, waits for them, and re-layouts: 14.8 us -> 0.07 us
  Pallas kernels: 25.4 us -> 18 us
  starting transfers between devices: 41.7 us -> 39.8 us
    unnamed x60 -> x24, local copies, waits for them, and re-layouts: 14.8 us -> 0.07 us
    pallas_call x7 -> x1, Pallas kernels: 10.4 us -> 4.08 us  [staged(): pl.pallas_call(body, in_specs=[pl.BlockSpec(memory_space=pltpu.HBM)] * co...]
    ppermute x35, waiting for transfers between devices: 50.5 us -> 47.9 us  [permute(): return lax.ppermute(value, AXES, pairs)]
    ppermute x35, starting transfers between devices: 39 us -> 37.2 us  [permute(): return lax.ppermute(value, AXES, pairs)]
    broadcast_in_dim x2 -> x0, other arithmetic: 1.52 us -> none  [shards(): out.T[None]]
    pallas_call x12 -> x18, Pallas kernels: 15 us -> 13.9 us  [call(): pl.pallas_call(body, in_specs=[VMEM] * len(flat), out_specs=[VMEM] * len(...]
  transfers between devices with their start and end apart: 37 -> 37, of which waited for: 22 -> 22; matrix products, arithmetic and copies ran while one was open for 3% -> 2% of each run, Pallas kernels for 15% -> 7%
where the time goes in v5:
time: 118 us
  waiting for transfers between devices  54.4 us (46%)
  starting transfers between devices  39.8 us (34%)
  Pallas kernels  18 us (15%)
  other arithmetic  4.49 us (4%)
    ppermute x35, waiting for transfers between devices, permute(): return lax.ppermute(value, AXES, pairs)  47.9 us
    ppermute x35, starting transfers between devices, permute(): return lax.ppermute(value, AXES, pairs)  37.2 us
    pallas_call x18, Pallas kernels, call(): pl.pallas_call(body, in_specs=[VMEM] * len(flat), out_specs=[VMEM] * len(...  13.9 us
    ppermute x2, waiting for transfers between devices, below(): return lax.ppermute(value, AXES, pairs)  6.53 us
    pallas_call x1, Pallas kernels, staged(): pl.pallas_call(body, in_specs=[pl.BlockSpec(memory_space=pltpu.HBM)] * co...  4.08 us
    ppermute x2, starting transfers between devices, below(): return lax.ppermute(value, AXES, pairs)  2.56 us
  transfers between devices with their start and end apart: 37, of which 22 were waited for; matrix products, arithmetic and copies ran while one was open for 2% of the time, Pallas kernels for 7%

profile of v5, /device:TPU:0, one launch (start us, length us, event | category | flops | bytes accessed | tf_op | source)
XLA Modules:
  0.0 117.8 jit_solution(14642391683185443543)
XLA Ops:
  0.6 0.9 select_reduce_fusion
  1.5 1.2 subtract_multiply_fusion.refs_0_
  2.7 3.0 %collective-permute-start.3 = (f32[64,512]{1,0:T(8,128)S(1)}, f32[64,512]{1,0:T(8,128)S(1)}, u32[]{:S(2)}, u32[]{:S(2)}) collective-permute-start(f32[64,512]{1,0:T(8,128)S(1)} %subtract_multiply_fusion.refs_0_), channel_id=1, source_target_pairs={{0,2},{1,3},{2,0},{3,1},{4,6},{5,7},{6,4},{7,5},{8,10},{9,11},{10,... | collective-permute-start | bytes 393224 | tf_op jit(solution)/shard_map/ppermute | solution.py:274
  7.1 1.1 subtract_multiply_fusion.1.refs_0_
  8.1 4.1 %shard_map.219.refs_4_ = f32[512,5120]{1,0:T(8,128)S(1)} custom-call(f32[512,2048]{1,0:T(8,128)} %bitcast.62, f32[512,1536]{1,0:T(8,128)} %bitcast.50, f32[512,1536]{1,0:T(8,128)} %bitcast.65), custom_call_target="tpu_custom_call" | custom-call | tf_op jit(solution)/shard_map/pallas_call | solution.py:128
  12.8 1.0 collective-permute-done.4.refs_3_
  13.8 2.5 %shard_map.220 = (f32[2,32,1536]{2,1,0:T(8,128)S(1)}, f32[2,32,1536]{2,1,0:T(8,128)S(1)}) custom-call(f32[64,512]{1,0:T(8,128)S(1)} %subtract_multiply_fusion.refs_0_, f32[64,512]{1,0:T(8,128)S(1)} %collective-permute-done.2.refs_1_, f32[64,512]{1,0:T(8,128)S(1)} %collective-permute-done.3.refs_2_, f32[64,512]{1,0:T(8,128)S(1)} %collective-permute-done.4.refs_3_, ...), custom_call_target="tpu_custom_call" | custom-call | tf_op jit(solution)/shard_map/pallas_call | solution.py:91
  16.9 1.2 %collective-permute-done.5.refs_1_ = f32[2,32,1536]{2,1,0:T(8,128)S(1)} collective-permute-done((f32[2,32,1536]{2,1,0:T(8,128)S(1)}, f32[2,32,1536]{2,1,0:T(8,128)S(1)}, u32[]{:S(2)}, u32[]{:S(2)}) %collective-permute-start.5) | collective-permute-done | bytes 393248 | tf_op jit(solution)/shard_map/ppermute | solution.py:274
  18.9 1.3 %collective-permute-start.6 = (f32[32,768]{1,0:T(8,128)S(1)}, f32[32,768]{1,0:T(8,128)S(1)}, u32[]{:S(2)}, u32[]{:S(2)}) collective-permute-start(f32[32,768]{1,0:T(8,128)S(1)} %get-tuple-element.64), channel_id=1, source_target_pairs={{4,0},{5,1},{6,2},{7,3},{8,4},{9,5},{10,6},{11,7},{12,8},{13,9},{1... | collective-permute-start | bytes 294920 | tf_op jit(solution)/shard_map/ppermute | solution.py:318
  20.3 4.7 %collective-permute-done.1.refs_1_ = f32[32,384]{1,0:T(8,128)S(1)} collective-permute-done((f32[32,384]{1,0:T(8,128)S(1)}, f32[32,384]{1,0:T(8,128)S(1)}, u32[]{:S(2)}, u32[]{:S(2)}) %collective-permute-start.1) | collective-permute-done | bytes 49184 | tf_op jit(solution)/shard_map/ppermute | solution.py:274
  25.0 1.3 %collective-permute-start.8 = (f32[32,768]{1,0:T(8,128)S(1)}, f32[32,768]{1,0:T(8,128)S(1)}, u32[]{:S(2)}, u32[]{:S(2)}) collective-permute-start(f32[32,768]{1,0:T(8,128)S(1)} %get-tuple-element.66), channel_id=1, source_target_pairs={{4,2},{5,3},{6,0},{7,1},{8,6},{9,7},{10,4},{11,5},{12,10},{13,11},... | collective-permute-start | bytes 294920 | tf_op jit(solution)/shard_map/ppermute | solution.py:318
  26.3 6.5 %collective-permute-done.8.refs_5_ = f32[32,768]{1,0:T(8,128)S(1)} collective-permute-done((f32[32,768]{1,0:T(8,128)S(1)}, f32[32,768]{1,0:T(8,128)S(1)}, u32[]{:S(2)}, u32[]{:S(2)}) %collective-permute-start.8) | collective-permute-done | bytes 98336 | tf_op jit(solution)/shard_map/ppermute | solution.py:318
  32.8 1.6 %collective-permute-start.10 = (f32[32,768]{1,0:T(8,128)S(1)}, f32[32,768]{1,0:T(8,128)S(1)}, u32[]{:S(2)}, u32[]{:S(2)}) collective-permute-start(f32[32,768]{1,0:T(8,128)S(1)} %shard_map.222.refs_4_.refs_5_), channel_id=1, source_target_pairs={{0,6},{1,7},{2,4},{3,5},{4,2},{5,3},{6,0},{7,1},{8,14},{9,15},{10,... | collective-permute-start | bytes 294920 | tf_op jit(solution)/shard_map/ppermute | solution.py:274
  34.8 4.6 %collective-permute-done.10.refs_1_ = f32[32,768]{1,0:T(8,128)S(1)} collective-permute-done((f32[32,768]{1,0:T(8,128)S(1)}, f32[32,768]{1,0:T(8,128)S(1)}, u32[]{:S(2)}, u32[]{:S(2)}) %collective-permute-start.10) | collective-permute-done | bytes 98336 | tf_op jit(solution)/shard_map/ppermute | solution.py:274
  39.5 1.6 %collective-permute-start.12 = (f32[32,768]{1,0:T(8,128)S(1)}, f32[32,768]{1,0:T(8,128)S(1)}, u32[]{:S(2)}, u32[]{:S(2)}) collective-permute-start(f32[32,768]{1,0:T(8,128)S(1)} %shard_map.223.refs_5_), channel_id=1, source_target_pairs={{0,2},{1,3},{2,0},{3,1},{4,8},{5,9},{6,10},{7,11},{8,4},{9,5},{10,... | collective-permute-start | bytes 294920 | tf_op jit(solution)/shard_map/ppermute | solution.py:274
  41.6 2.8 %collective-permute-done.12.refs_0_ = f32[32,768]{1,0:T(8,128)S(1)} collective-permute-done((f32[32,768]{1,0:T(8,128)S(1)}, f32[32,768]{1,0:T(8,128)S(1)}, u32[]{:S(2)}, u32[]{:S(2)}) %collective-permute-start.12) | collective-permute-done | bytes 98336 | tf_op jit(solution)/shard_map/ppermute | solution.py:274
  44.4 1.3 %collective-permute-done.13.refs_1_ = f32[32,768]{1,0:T(8,128)S(1)} collective-permute-done((f32[32,768]{1,0:T(8,128)S(1)}, f32[32,768]{1,0:T(8,128)S(1)}, u32[]{:S(2)}, u32[]{:S(2)}) %collective-permute-start.13) | collective-permute-done | bytes 98336 | tf_op jit(solution)/shard_map/ppermute | solution.py:274
  46.3 3.4 %collective-permute-start.15 = (f32[32,768]{1,0:T(8,128)S(1)}, f32[32,768]{1,0:T(8,128)S(1)}, u32[]{:S(2)}, u32[]{:S(2)}) collective-permute-start(f32[32,768]{1,0:T(8,128)S(1)} %shard_map.224.refs_5_), channel_id=1, source_target_pairs={{0,4},{1,5},{2,6},{3,7},{4,0},{5,1},{6,2},{7,3},{8,12},{9,13},{10,... | collective-permute-start | bytes 294920 | tf_op jit(solution)/shard_map/ppermute | solution.py:274
  49.6 3.6 %collective-permute-done.15.refs_0_ = f32[32,768]{1,0:T(8,128)S(1)} collective-permute-done((f32[32,768]{1,0:T(8,128)S(1)}, f32[32,768]{1,0:T(8,128)S(1)}, u32[]{:S(2)}, u32[]{:S(2)}) %collective-permute-start.15) | collective-permute-done | bytes 98336 | tf_op jit(solution)/shard_map/ppermute | solution.py:274
  53.2 1.9 %collective-permute-done.16.refs_1_ = f32[32,768]{1,0:T(8,128)S(1)} collective-permute-done((f32[32,768]{1,0:T(8,128)S(1)}, f32[32,768]{1,0:T(8,128)S(1)}, u32[]{:S(2)}, u32[]{:S(2)}) %collective-permute-start.16) | collective-permute-done | bytes 98336 | tf_op jit(solution)/shard_map/ppermute | solution.py:274
  55.2 1.2 collective-permute-start.18
  56.3 3.5 %collective-permute-done.18.refs_1_ = f32[32,768]{1,0:T(8,128)S(1)} collective-permute-done((f32[32,768]{1,0:T(8,128)S(1)}, f32[32,768]{1,0:T(8,128)S(1)}, u32[]{:S(2)}, u32[]{:S(2)}) %collective-permute-start.18) | collective-permute-done | bytes 98336 | tf_op jit(solution)/shard_map/ppermute | solution.py:274
  59.9 1.5 %shard_map.226.refs_4_.refs_5_ = f32[32,768]{1,0:T(8,128)S(1)} custom-call(f32[32,768]{1,0:T(8,128)S(1)} %shard_map.225.refs_0_, f32[32,768]{1,0:T(8,128)S(1)} %collective-permute-done.18.refs_1_, f32[384,1536]{1,0:T(8,128)S(1)} %bitcast.69, f32[384,1536]{1,0:T(8,128)S(1)} %collective-permute-done.14.refs_3_), custom_call_target="tpu_custom_call" | custom-call | tf_op jit(solution)/shard_map/pallas_call | solution.py:91
  62.0 3.2 %collective-permute-start.20 = (f32[32,768]{1,0:T(8,128)S(1)}, f32[32,768]{1,0:T(8,128)S(1)}, u32[]{:S(2)}, u32[]{:S(2)}) collective-permute-start(f32[32,768]{1,0:T(8,128)S(1)} %shard_map.226.refs_4_.refs_5_), channel_id=1, source_target_pairs={{0,4},{1,5},{2,6},{3,7},{4,0},{5,1},{6,2},{7,3},{8,12},{9,13},{10,... | collective-permute-start | bytes 294920 | tf_op jit(solution)/shard_map/ppermute | solution.py:274
  65.2 3.6 %collective-permute-done.20.refs_0_ = f32[32,768]{1,0:T(8,128)S(1)} collective-permute-done((f32[32,768]{1,0:T(8,128)S(1)}, f32[32,768]{1,0:T(8,128)S(1)}, u32[]{:S(2)}, u32[]{:S(2)}) %collective-permute-start.20) | collective-permute-done | bytes 98336 | tf_op jit(solution)/shard_map/ppermute | solution.py:274
  68.8 1.9 %collective-permute-done.21.refs_1_ = f32[32,768]{1,0:T(8,128)S(1)} collective-permute-done((f32[32,768]{1,0:T(8,128)S(1)}, f32[32,768]{1,0:T(8,128)S(1)}, u32[]{:S(2)}, u32[]{:S(2)}) %collective-permute-start.21) | collective-permute-done | bytes 98336 | tf_op jit(solution)/shard_map/ppermute | solution.py:274
  70.7 2.4 %collective-permute-done.22.refs_12_ = f32[512,1536]{1,0:T(8,128)S(1)} collective-permute-done((f32[512,1536]{1,0:T(8,128)S(1)}, f32[512,1536]{1,0:T(8,128)S(1)}, u32[]{:S(2)}, u32[]{:S(2)}) %collective-permute-start.22) | collective-permute-done | bytes 3145760 | tf_op jit(solution)/shard_map/ppermute | solution.py:274
  73.2 1.2 collective-permute-start.23
  74.3 0.9 collective-permute-start.24
  75.2 3.6 %collective-permute-done.23.refs_0_ = f32[32,768]{1,0:T(8,128)S(1)} collective-permute-done((f32[32,768]{1,0:T(8,128)S(1)}, f32[32,768]{1,0:T(8,128)S(1)}, u32[]{:S(2)}, u32[]{:S(2)}) %collective-permute-start.23) | collective-permute-done | bytes 98336 | tf_op jit(solution)/shard_map/ppermute | solution.py:274
  78.9 1.3 %collective-permute-done.24.refs_1_ = f32[32,768]{1,0:T(8,128)S(1)} collective-permute-done((f32[32,768]{1,0:T(8,128)S(1)}, f32[32,768]{1,0:T(8,128)S(1)}, u32[]{:S(2)}, u32[]{:S(2)}) %collective-permute-start.24) | collective-permute-done | bytes 98336 | tf_op jit(solution)/shard_map/ppermute | solution.py:274
  80.1 1.2 collective-permute-start.27
  81.3 8.0 %collective-permute-start.25 = (f32[32,768]{1,0:T(8,128)S(1)}, f32[32,768]{1,0:T(8,128)S(1)}, u32[]{:S(2)}, u32[]{:S(2)}) collective-permute-start(f32[32,768]{1,0:T(8,128)S(1)} %shard_map.228.refs_0_.refs_5_), channel_id=1, source_target_pairs={{0,4},{1,5},{2,6},{3,7},{4,0},{5,1},{6,2},{7,3},{8,12},{9,13},{10,... | collective-permute-start | bytes 294920 | tf_op jit(solution)/shard_map/ppermute | solution.py:274
  90.0 0.9 collective-permute-start.32
  90.9 2.0 %shard_map.229.refs_2_ = f32[32,1024]{1,0:T(8,128)S(1)} custom-call(f32[32,768]{1,0:T(8,128)S(1)} %shard_map.228.refs_0_.refs_5_, f32[32,768]{1,0:T(8,128)S(1)} %collective-permute-done.27.refs_1_, f32[512,1536]{1,0:T(8,128)S(1)} %bitcast.52, f32[512,1536]{1,0:T(8,128)S(1)} %collective-permute-done.19.refs_3_.refs_10_), custom_call_target="tpu_custom_call" | custom-call | bytes 8388608 | tf_op jit(solution)/shard_map/pallas_call | solution.py:91
  92.9 1.2 %collective-permute-start.33 = (f32[32,768]{1,0:T(8,128)S(1)}, f32[32,768]{1,0:T(8,128)S(1)}, u32[]{:S(2)}, u32[]{:S(2)}) collective-permute-start(f32[32,768]{1,0:T(8,128)S(1)} %shard_map.228.refs_0_.refs_5_), channel_id=1, source_target_pairs={{0,2},{1,3},{2,0},{3,1},{4,10},{5,11},{6,8},{7,9},{8,6},{9,7},{10,... | collective-permute-start | bytes 294920 | tf_op jit(solution)/shard_map/ppermute | solution.py:274
  94.1 0.8 collective-permute-done.26.refs_1_
  94.9 1.5 %shard_map.230.refs_3_.refs_0_ = f32[32,768]{1,0:T(8,128)S(1)} custom-call(f32[32,768]{1,0:T(8,128)S(1)} %collective-permute-done.25.refs_0_, f32[32,768]{1,0:T(8,128)S(1)} %collective-permute-done.26.refs_1_, f32[384,1536]{1,0:T(8,128)S(1)} %bitcast.61, f32[384,1536]{1,0:T(8,128)S(1)} %collective-permute-done.17.refs_3_, ...), custom_call_target="tpu_custom_call" | custom-call | tf_op jit(solution)/shard_map/pallas_call | solution.py:91
  96.4 1.2 %collective-permute-start.29 = (f32[32,768]{1,0:T(8,128)S(1)}, f32[32,768]{1,0:T(8,128)S(1)}, u32[]{:S(2)}, u32[]{:S(2)}) collective-permute-start(f32[32,768]{1,0:T(8,128)S(1)} %shard_map.230.refs_3_.refs_0_), channel_id=1, source_target_pairs={{0,2},{1,3},{2,0},{3,1},{4,6},{5,7},{6,4},{7,5},{8,10},{9,11},{10,... | collective-permute-start | bytes 294920 | tf_op jit(solution)/shard_map/ppermute | solution.py:274
  97.6 1.8 %collective-permute-start.30 = (f32[32,768]{1,0:T(8,128)S(1)}, f32[32,768]{1,0:T(8,128)S(1)}, u32[]{:S(2)}, u32[]{:S(2)}) collective-permute-start(f32[32,768]{1,0:T(8,128)S(1)} %shard_map.230.refs_3_.refs_0_), channel_id=1, source_target_pairs={{0,4},{1,5},{2,6},{3,7},{4,0},{5,1},{6,2},{7,3},{8,12},{9,13},{10,... | collective-permute-start | bytes 294920 | tf_op jit(solution)/shard_map/ppermute | solution.py:274
  100.0 2.1 %collective-permute-done.29.refs_4_ = f32[32,768]{1,0:T(8,128)S(1)} collective-permute-done((f32[32,768]{1,0:T(8,128)S(1)}, f32[32,768]{1,0:T(8,128)S(1)}, u32[]{:S(2)}, u32[]{:S(2)}) %collective-permute-start.29) | collective-permute-done | bytes 98336 | tf_op jit(solution)/shard_map/ppermute | solution.py:274
  102.3 2.7 %collective-permute-done.31.refs_6_ = f32[32,768]{1,0:T(8,128)S(1)} collective-permute-done((f32[32,768]{1,0:T(8,128)S(1)}, f32[32,768]{1,0:T(8,128)S(1)}, u32[]{:S(2)}, u32[]{:S(2)}) %collective-permute-start.31) | collective-permute-done | bytes 98336 | tf_op jit(solution)/shard_map/ppermute | solution.py:274
  105.0 2.0 %shard_map.231.refs_0_ = f32[32,1024]{1,0:T(8,128)S(1)} custom-call(f32[32,512]{1,0:T(8,128)S(1)} %get-tuple-element.52.refs_0_, f32[32,512]{1,0:T(8,128)S(1)} %collective-permute-done.refs_1_, f32[32,1024]{1,0:T(8,128)S(1)} %shard_map.229.refs_2_, f32[32,768]{1,0:T(8,128)S(1)} %shard_map.230.refs_3_.refs_0_, f32[32,768]{1,0:T(8,128)S(1)} %collective-permute-done.29.refs_4_, ...), custom_call_target="tpu_custom_call" | custom-call | tf_op jit(solution)/shard_map/pallas_call | solution.py:91
  107.1 1.2 %collective-permute-start.34 = (f32[32,1024]{1,0:T(8,128)S(1)}, f32[32,1024]{1,0:T(8,128)S(1)}, u32[]{:S(2)}, u32[]{:S(2)}) collective-permute-start(f32[32,1024]{1,0:T(8,128)S(1)} %shard_map.231.refs_0_), channel_id=1, source_target_pairs={{0,2},{1,3},{2,0},{3,1},{4,6},{5,7},{6,4},{7,5},{8,10},{9,11},{10,... | collective-permute-start | bytes 393224 | tf_op jit(solution)/shard_map/ppermute | solution.py:274
  108.3 3.8 %collective-permute-done.34.refs_1_ = f32[32,1024]{1,0:T(8,128)S(1)} collective-permute-done((f32[32,1024]{1,0:T(8,128)S(1)}, f32[32,1024]{1,0:T(8,128)S(1)}, u32[]{:S(2)}, u32[]{:S(2)}) %collective-permute-start.34) | collective-permute-done | bytes 131104 | tf_op jit(solution)/shard_map/ppermute | solution.py:274
  112.1 2.6 %shard_map.232 = (f32[32,512]{1,0:T(8,128)S(1)}, f32[32,512]{1,0:T(8,128)S(1)}) custom-call(f32[32,1024]{1,0:T(8,128)S(1)} %shard_map.231.refs_0_, f32[32,1024]{1,0:T(8,128)S(1)} %collective-permute-done.34.refs_1_, f32[512,2048]{1,0:T(8,128)S(1)} %bitcast.64, f32[512,2048]{1,0:T(8,128)S(1)} %collective-permute-done.28.refs_3_), custom_call_target="tpu_custom_call" | custom-call | tf_op jit(solution)/shard_map/pallas_call | solution.py:91
  115.3 0.9 collective-permute-done.36.refs_1_
  117.0 0.8 shard_map.233
  (74 shorter events, 8.4 us)
Async XLA Ops:
  2.7 9.6 %collective-permute-start.3 = (f32[64,512]{1,0:T(8,128)S(1)}, f32[64,512]{1,0:T(8,128)S(1)}, u32[]{:S(2)}, u32[]{:S(2)}) collective-permute-start(f32[64,512]{1,0:T(8,128)S(1)} %subtract_multiply_fusion.refs_0_), channel_id=1, source_target_pairs={{0,2},{1,3},{2,0},{3,1},{4,6},{5,7},{6,4},{7,5},{8,10},{9,11},{10,... | collective-permute-start | bytes 393224 | tf_op jit(solution)/shard_map/ppermute | solution.py:274
  5.7 7.2 %collective-permute-start.2 = (f32[64,512]{1,0:T(8,128)S(1)}, f32[64,512]{1,0:T(8,128)S(1)}, u32[]{:S(2)}, u32[]{:S(2)}) collective-permute-start(f32[64,512]{1,0:T(8,128)S(1)} %subtract_multiply_fusion.refs_0_), channel_id=1, source_target_pairs={{0,1},{1,0},{2,3},{3,2},{4,5},{5,4},{6,7},{7,6},{8,9},{9,8},{10,11... | collective-permute-start | bytes 393224 | tf_op jit(solution)/shard_map/ppermute | solution.py:274
  12.2 5.9 %copy-start.5 = (f32[1,384,1536]{2,1,0:T(8,128)S(1)}, f32[1,384,1536]{2,1,0:T(8,128)}, u32[]{:S(2)}) copy-start(f32[1,384,1536]{2,1,0:T(8,128)} %param.34) | copy-start | bytes 7077892
  12.3 1.6 %collective-permute-start.4 = (f32[64,512]{1,0:T(8,128)S(1)}, f32[64,512]{1,0:T(8,128)S(1)}, u32[]{:S(2)}, u32[]{:S(2)}) collective-permute-start(f32[64,512]{1,0:T(8,128)S(1)} %collective-permute-done.3.refs_2_), channel_id=1, source_target_pairs={{0,1},{1,0},{2,3},{3,2},{4,5},{5,4},{6,7},{7,6},{8,9},{9,8},{10,11... | collective-permute-start | bytes 393224 | tf_op jit(solution)/shard_map/ppermute | solution.py:274
  16.4 1.8 %collective-permute-start.5 = (f32[2,32,1536]{2,1,0:T(8,128)S(1)}, f32[2,32,1536]{2,1,0:T(8,128)S(1)}, u32[]{:S(2)}, u32[]{:S(2)}) collective-permute-start(f32[2,32,1536]{2,1,0:T(8,128)S(1)} %get-tuple-element.62), channel_id=1, source_target_pairs={{0,1},{1,0},{2,3},{3,2},{4,5},{5,4},{6,7},{7,6},{8,9},{9,8},{10,11... | collective-permute-start | bytes 1179656 | tf_op jit(solution)/shard_map/ppermute | solution.py:274
  16.8 22.7 %collective-permute-start.11 = (f32[384,1536]{1,0:T(8,128)S(1)}, f32[384,1536]{1,0:T(8,128)S(1)}, u32[]{:S(2)}, u32[]{:S(2)}) collective-permute-start(f32[384,1536]{1,0:T(8,128)S(1)} %bitcast.54), channel_id=1, source_target_pairs={{0,1},{1,0},{2,3},{3,2},{4,5},{5,4},{6,7},{7,6},{8,9},{9,8},{10,11... | collective-permute-start | bytes 7077896 | tf_op jit(solution)/shard_map/ppermute | solution.py:274
  18.2 27.5 %collective-permute-start.14 = (f32[384,1536]{1,0:T(8,128)S(1)}, f32[384,1536]{1,0:T(8,128)S(1)}, u32[]{:S(2)}, u32[]{:S(2)}) collective-permute-start(f32[384,1536]{1,0:T(8,128)S(1)} %bitcast.68), channel_id=1, source_target_pairs={{0,1},{1,0},{2,3},{3,2},{4,5},{5,4},{6,7},{7,6},{8,9},{9,8},{10,11... | collective-permute-start | bytes 7077896 | tf_op jit(solution)/shard_map/ppermute | solution.py:274
  18.6 6.3 %collective-permute-start.1 = (f32[32,384]{1,0:T(8,128)S(1)}, f32[32,384]{1,0:T(8,128)S(1)}, u32[]{:S(2)}, u32[]{:S(2)}) collective-permute-start(f32[32,384]{1,0:T(8,128)S(1)} %get-tuple-element.55), channel_id=1, source_target_pairs={{0,1},{1,0},{2,3},{3,2},{4,5},{5,4},{6,7},{7,6},{8,9},{9,8},{10,11... | collective-permute-start | bytes 147464 | tf_op jit(solution)/shard_map/ppermute | solution.py:274
  18.9 7.4 %collective-permute-start.6 = (f32[32,768]{1,0:T(8,128)S(1)}, f32[32,768]{1,0:T(8,128)S(1)}, u32[]{:S(2)}, u32[]{:S(2)}) collective-permute-start(f32[32,768]{1,0:T(8,128)S(1)} %get-tuple-element.64), channel_id=1, source_target_pairs={{4,0},{5,1},{6,2},{7,3},{8,4},{9,5},{10,6},{11,7},{12,8},{13,9},{1... | collective-permute-start | bytes 294920 | tf_op jit(solution)/shard_map/ppermute | solution.py:318
  20.1 6.1 %collective-permute-start.7 = (f32[32,768]{1,0:T(8,128)S(1)}, f32[32,768]{1,0:T(8,128)S(1)}, u32[]{:S(2)}, u32[]{:S(2)}) collective-permute-start(f32[32,768]{1,0:T(8,128)S(1)} %get-tuple-element.65), channel_id=1, source_target_pairs={{0,2},{1,3},{2,0},{3,1},{4,6},{5,7},{6,4},{7,5},{8,10},{9,11},{10,... | collective-permute-start | bytes 294920 | tf_op jit(solution)/shard_map/ppermute | solution.py:274
  25.0 7.8 %collective-permute-start.8 = (f32[32,768]{1,0:T(8,128)S(1)}, f32[32,768]{1,0:T(8,128)S(1)}, u32[]{:S(2)}, u32[]{:S(2)}) collective-permute-start(f32[32,768]{1,0:T(8,128)S(1)} %get-tuple-element.66), channel_id=1, source_target_pairs={{4,2},{5,3},{6,0},{7,1},{8,6},{9,7},{10,4},{11,5},{12,10},{13,11},... | collective-permute-start | bytes 294920 | tf_op jit(solution)/shard_map/ppermute | solution.py:318
  32.8 6.5 %collective-permute-start.10 = (f32[32,768]{1,0:T(8,128)S(1)}, f32[32,768]{1,0:T(8,128)S(1)}, u32[]{:S(2)}, u32[]{:S(2)}) collective-permute-start(f32[32,768]{1,0:T(8,128)S(1)} %shard_map.222.refs_4_.refs_5_), channel_id=1, source_target_pairs={{0,6},{1,7},{2,4},{3,5},{4,2},{5,3},{6,0},{7,1},{8,14},{9,15},{10,... | collective-permute-start | bytes 294920 | tf_op jit(solution)/shard_map/ppermute | solution.py:274
  34.4 5.0 %collective-permute-start.9 = (f32[32,768]{1,0:T(8,128)S(1)}, f32[32,768]{1,0:T(8,128)S(1)}, u32[]{:S(2)}, u32[]{:S(2)}) collective-permute-start(f32[32,768]{1,0:T(8,128)S(1)} %shard_map.222.refs_4_.refs_5_), channel_id=1, source_target_pairs={{0,4},{1,5},{2,6},{3,7},{4,0},{5,1},{6,2},{7,3},{8,12},{9,13},{10,... | collective-permute-start | bytes 294920 | tf_op jit(solution)/shard_map/ppermute | solution.py:274
  39.5 6.3 %copy-start.2 = (f32[1,384,1536]{2,1,0:T(8,128)S(1)}, f32[1,384,1536]{2,1,0:T(8,128)}, u32[]{:S(2)}) copy-start(f32[1,384,1536]{2,1,0:T(8,128)} %param.35) | copy-start | bytes 7077892
  39.5 6.2 %copy-start = (f32[1,512,1536]{2,1,0:T(8,128)S(1)}, f32[1,512,1536]{2,1,0:T(8,128)}, u32[]{:S(2)}) copy-start(f32[1,512,1536]{2,1,0:T(8,128)} %param.32) | copy-start | bytes 9437188
  39.5 4.9 %collective-permute-start.12 = (f32[32,768]{1,0:T(8,128)S(1)}, f32[32,768]{1,0:T(8,128)S(1)}, u32[]{:S(2)}, u32[]{:S(2)}) collective-permute-start(f32[32,768]{1,0:T(8,128)S(1)} %shard_map.223.refs_5_), channel_id=1, source_target_pairs={{0,2},{1,3},{2,0},{3,1},{4,8},{5,9},{6,10},{7,11},{8,4},{9,5},{10,... | collective-permute-start | bytes 294920 | tf_op jit(solution)/shard_map/ppermute | solution.py:274
  41.1 4.6 %collective-permute-start.13 = (f32[32,768]{1,0:T(8,128)S(1)}, f32[32,768]{1,0:T(8,128)S(1)}, u32[]{:S(2)}, u32[]{:S(2)}) collective-permute-start(f32[32,768]{1,0:T(8,128)S(1)} %shard_map.223.refs_5_), channel_id=1, source_target_pairs={{0,2},{1,3},{2,0},{3,1},{4,10},{5,11},{6,8},{7,9},{8,6},{9,7},{10,... | collective-permute-start | bytes 294920 | tf_op jit(solution)/shard_map/ppermute | solution.py:274
  45.7 14.2 %collective-permute-start.19 = (f32[512,1536]{1,0:T(8,128)S(1)}, f32[512,1536]{1,0:T(8,128)S(1)}, u32[]{:S(2)}, u32[]{:S(2)}) collective-permute-start(f32[512,1536]{1,0:T(8,128)S(1)} %bitcast.51), channel_id=1, source_target_pairs={{0,1},{1,0},{2,3},{3,2},{4,5},{5,4},{6,7},{7,6},{8,9},{9,8},{10,11... | collective-permute-start | bytes 9437192 | tf_op jit(solution)/shard_map/ppermute | solution.py:274
  45.8 9.4 %collective-permute-start.17 = (f32[384,1536]{1,0:T(8,128)S(1)}, f32[384,1536]{1,0:T(8,128)S(1)}, u32[]{:S(2)}, u32[]{:S(2)}) collective-permute-start(f32[384,1536]{1,0:T(8,128)S(1)} %bitcast.58), channel_id=1, source_target_pairs={{0,1},{1,0},{2,3},{3,2},{4,5},{5,4},{6,7},{7,6},{8,9},{9,8},{10,11... | collective-permute-start | bytes 7077896 | tf_op jit(solution)/shard_map/ppermute | solution.py:274
  46.3 6.9 %collective-permute-start.15 = (f32[32,768]{1,0:T(8,128)S(1)}, f32[32,768]{1,0:T(8,128)S(1)}, u32[]{:S(2)}, u32[]{:S(2)}) collective-permute-start(f32[32,768]{1,0:T(8,128)S(1)} %shard_map.224.refs_5_), channel_id=1, source_target_pairs={{0,4},{1,5},{2,6},{3,7},{4,0},{5,1},{6,2},{7,3},{8,12},{9,13},{10,... | collective-permute-start | bytes 294920 | tf_op jit(solution)/shard_map/ppermute | solution.py:274
  49.6 5.5 %collective-permute-start.16 = (f32[32,768]{1,0:T(8,128)S(1)}, f32[32,768]{1,0:T(8,128)S(1)}, u32[]{:S(2)}, u32[]{:S(2)}) collective-permute-start(f32[32,768]{1,0:T(8,128)S(1)} %shard_map.224.refs_5_), channel_id=1, source_target_pairs={{0,6},{1,7},{2,4},{3,5},{4,2},{5,3},{6,0},{7,1},{8,14},{9,15},{10,... | collective-permute-start | bytes 294920 | tf_op jit(solution)/shard_map/ppermute | solution.py:274
  55.2 6.3 %copy-start.4 = (f32[1,512,1536]{2,1,0:T(8,128)S(1)}, f32[1,512,1536]{2,1,0:T(8,128)}, u32[]{:S(2)}) copy-start(f32[1,512,1536]{2,1,0:T(8,128)} %param.31) | copy-start | bytes 9437188
  55.2 6.2 %copy-start.3 = (f32[1,512,2048]{2,1,0:T(8,128)S(1)}, f32[1,512,2048]{2,1,0:T(8,128)}, u32[]{:S(2)}) copy-start(f32[1,512,2048]{2,1,0:T(8,128)} %param.30) | copy-start | bytes 12582916
  55.2 4.7 %collective-permute-start.18 = (f32[32,768]{1,0:T(8,128)S(1)}, f32[32,768]{1,0:T(8,128)S(1)}, u32[]{:S(2)}, u32[]{:S(2)}) collective-permute-start(f32[32,768]{1,0:T(8,128)S(1)} %shard_map.225.refs_0_), channel_id=1, source_target_pairs={{0,2},{1,3},{2,0},{3,1},{4,6},{5,7},{6,4},{7,5},{8,10},{9,11},{10,... | collective-permute-start | bytes 294920 | tf_op jit(solution)/shard_map/ppermute | solution.py:274
  61.4 33.5 %collective-permute-start.28 = (f32[512,2048]{1,0:T(8,128)S(1)}, f32[512,2048]{1,0:T(8,128)S(1)}, u32[]{:S(2)}, u32[]{:S(2)}) collective-permute-start(f32[512,2048]{1,0:T(8,128)S(1)} %bitcast.63), channel_id=1, source_target_pairs={{0,1},{1,0},{2,3},{3,2},{4,5},{5,4},{6,7},{7,6},{8,9},{9,8},{10,11... | collective-permute-start | bytes 12582920 | tf_op jit(solution)/shard_map/ppermute | solution.py:274
  61.5 11.6 %collective-permute-start.22 = (f32[512,1536]{1,0:T(8,128)S(1)}, f32[512,1536]{1,0:T(8,128)S(1)}, u32[]{:S(2)}, u32[]{:S(2)}) collective-permute-start(f32[512,1536]{1,0:T(8,128)S(1)} %bitcast.66), channel_id=1, source_target_pairs={{0,1},{1,0},{2,3},{3,2},{4,5},{5,4},{6,7},{7,6},{8,9},{9,8},{10,11... | collective-permute-start | bytes 9437192 | tf_op jit(solution)/shard_map/ppermute | solution.py:274
  62.0 6.8 %collective-permute-start.20 = (f32[32,768]{1,0:T(8,128)S(1)}, f32[32,768]{1,0:T(8,128)S(1)}, u32[]{:S(2)}, u32[]{:S(2)}) collective-permute-start(f32[32,768]{1,0:T(8,128)S(1)} %shard_map.226.refs_4_.refs_5_), channel_id=1, source_target_pairs={{0,4},{1,5},{2,6},{3,7},{4,0},{5,1},{6,2},{7,3},{8,12},{9,13},{10,... | collective-permute-start | bytes 294920 | tf_op jit(solution)/shard_map/ppermute | solution.py:274
  65.2 5.5 %collective-permute-start.21 = (f32[32,768]{1,0:T(8,128)S(1)}, f32[32,768]{1,0:T(8,128)S(1)}, u32[]{:S(2)}, u32[]{:S(2)}) collective-permute-start(f32[32,768]{1,0:T(8,128)S(1)} %shard_map.226.refs_4_.refs_5_), channel_id=1, source_target_pairs={{0,6},{1,7},{2,4},{3,5},{4,2},{5,3},{6,0},{7,1},{8,14},{9,15},{10,... | collective-permute-start | bytes 294920 | tf_op jit(solution)/shard_map/ppermute | solution.py:274
  73.2 5.7 %collective-permute-start.23 = (f32[32,768]{1,0:T(8,128)S(1)}, f32[32,768]{1,0:T(8,128)S(1)}, u32[]{:S(2)}, u32[]{:S(2)}) collective-permute-start(f32[32,768]{1,0:T(8,128)S(1)} %shard_map.227.refs_5_), channel_id=1, source_target_pairs={{0,2},{1,3},{2,0},{3,1},{4,8},{5,9},{6,10},{7,11},{8,4},{9,5},{10,... | collective-permute-start | bytes 294920 | tf_op jit(solution)/shard_map/ppermute | solution.py:274
  74.3 5.8 %collective-permute-start.24 = (f32[32,768]{1,0:T(8,128)S(1)}, f32[32,768]{1,0:T(8,128)S(1)}, u32[]{:S(2)}, u32[]{:S(2)}) collective-permute-start(f32[32,768]{1,0:T(8,128)S(1)} %shard_map.227.refs_5_), channel_id=1, source_target_pairs={{0,2},{1,3},{2,0},{3,1},{4,10},{5,11},{6,8},{7,9},{8,6},{9,7},{10,... | collective-permute-start | bytes 294920 | tf_op jit(solution)/shard_map/ppermute | solution.py:274
  80.1 9.8 %collective-permute-start.27 = (f32[32,768]{1,0:T(8,128)S(1)}, f32[32,768]{1,0:T(8,128)S(1)}, u32[]{:S(2)}, u32[]{:S(2)}) collective-permute-start(f32[32,768]{1,0:T(8,128)S(1)} %shard_map.228.refs_0_.refs_5_), channel_id=1, source_target_pairs={{0,2},{1,3},{2,0},{3,1},{4,6},{5,7},{6,4},{7,5},{8,10},{9,11},{10,... | collective-permute-start | bytes 294920 | tf_op jit(solution)/shard_map/ppermute | solution.py:274
  81.3 11.6 %collective-permute-start.25 = (f32[32,768]{1,0:T(8,128)S(1)}, f32[32,768]{1,0:T(8,128)S(1)}, u32[]{:S(2)}, u32[]{:S(2)}) collective-permute-start(f32[32,768]{1,0:T(8,128)S(1)} %shard_map.228.refs_0_.refs_5_), channel_id=1, source_target_pairs={{0,4},{1,5},{2,6},{3,7},{4,0},{5,1},{6,2},{7,3},{8,12},{9,13},{10,... | collective-permute-start | bytes 294920 | tf_op jit(solution)/shard_map/ppermute | solution.py:274
  89.3 5.6 %collective-permute-start.26 = (f32[32,768]{1,0:T(8,128)S(1)}, f32[32,768]{1,0:T(8,128)S(1)}, u32[]{:S(2)}, u32[]{:S(2)}) collective-permute-start(f32[32,768]{1,0:T(8,128)S(1)} %shard_map.228.refs_0_.refs_5_), channel_id=1, source_target_pairs={{0,6},{1,7},{2,4},{3,5},{4,2},{5,3},{6,0},{7,1},{8,14},{9,15},{10,... | collective-permute-start | bytes 294920 | tf_op jit(solution)/shard_map/ppermute | solution.py:274
  89.9 9.6 %collective-permute-start = (f32[32,512]{1,0:T(8,128)S(1)}, f32[32,512]{1,0:T(8,128)S(1)}, u32[]{:S(2)}, u32[]{:S(2)}) collective-permute-start(f32[32,512]{1,0:T(8,128)S(1)} %get-tuple-element.53), channel_id=1, source_target_pairs={{0,1},{1,0},{2,3},{3,2},{4,5},{5,4},{6,7},{7,6},{8,9},{9,8},{10,11... | collective-permute-start | bytes 196616 | tf_op jit(solution)/shard_map/ppermute | solution.py:274
  90.0 10.1 %collective-permute-start.32 = (f32[32,768]{1,0:T(8,128)S(1)}, f32[32,768]{1,0:T(8,128)S(1)}, u32[]{:S(2)}, u32[]{:S(2)}) collective-permute-start(f32[32,768]{1,0:T(8,128)S(1)} %shard_map.228.refs_0_.refs_5_), channel_id=1, source_target_pairs={{0,2},{1,3},{2,0},{3,1},{4,8},{5,9},{6,10},{7,11},{8,4},{9,5},{10,... | collective-permute-start | bytes 294920 | tf_op jit(solution)/shard_map/ppermute | solution.py:274
  92.9 7.1 %collective-permute-start.33 = (f32[32,768]{1,0:T(8,128)S(1)}, f32[32,768]{1,0:T(8,128)S(1)}, u32[]{:S(2)}, u32[]{:S(2)}) collective-permute-start(f32[32,768]{1,0:T(8,128)S(1)} %shard_map.228.refs_0_.refs_5_), channel_id=1, source_target_pairs={{0,2},{1,3},{2,0},{3,1},{4,10},{5,11},{6,8},{7,9},{8,6},{9,7},{10,... | collective-permute-start | bytes 294920 | tf_op jit(solution)/shard_map/ppermute | solution.py:274
  96.4 5.7 %collective-permute-start.29 = (f32[32,768]{1,0:T(8,128)S(1)}, f32[32,768]{1,0:T(8,128)S(1)}, u32[]{:S(2)}, u32[]{:S(2)}) collective-permute-start(f32[32,768]{1,0:T(8,128)S(1)} %shard_map.230.refs_3_.refs_0_), channel_id=1, source_target_pairs={{0,2},{1,3},{2,0},{3,1},{4,6},{5,7},{6,4},{7,5},{8,10},{9,11},{10,... | collective-permute-start | bytes 294920 | tf_op jit(solution)/shard_map/ppermute | solution.py:274
  97.6 4.6 %collective-permute-start.30 = (f32[32,768]{1,0:T(8,128)S(1)}, f32[32,768]{1,0:T(8,128)S(1)}, u32[]{:S(2)}, u32[]{:S(2)}) collective-permute-start(f32[32,768]{1,0:T(8,128)S(1)} %shard_map.230.refs_3_.refs_0_), channel_id=1, source_target_pairs={{0,4},{1,5},{2,6},{3,7},{4,0},{5,1},{6,2},{7,3},{8,12},{9,13},{10,... | collective-permute-start | bytes 294920 | tf_op jit(solution)/shard_map/ppermute | solution.py:274
  99.4 5.5 %collective-permute-start.31 = (f32[32,768]{1,0:T(8,128)S(1)}, f32[32,768]{1,0:T(8,128)S(1)}, u32[]{:S(2)}, u32[]{:S(2)}) collective-permute-start(f32[32,768]{1,0:T(8,128)S(1)} %shard_map.230.refs_3_.refs_0_), channel_id=1, source_target_pairs={{0,6},{1,7},{2,4},{3,5},{4,2},{5,3},{6,0},{7,1},{8,14},{9,15},{10,... | collective-permute-start | bytes 294920 | tf_op jit(solution)/shard_map/ppermute | solution.py:274
  107.0 9.2 %copy-start.9 = (f32[1,384,64]{1,2,0:T(8,128)S(1)}, f32[1,384,64]{1,2,0:T(8,128)}, u32[]{:S(2)}) copy-start(f32[1,384,64]{1,2,0:T(8,128)} %param.29) | copy-start | bytes 294916
  107.0 9.2 %copy-start.10 = (f32[1,384,64]{1,2,0:T(8,128)S(1)}, f32[1,384,64]{1,2,0:T(8,128)}, u32[]{:S(2)}) copy-start(f32[1,384,64]{1,2,0:T(8,128)} %param.28) | copy-start | bytes 294916
  107.0 9.2 %copy-start.11 = (f32[1,384,64]{1,2,0:T(8,128)S(1)}, f32[1,384,64]{1,2,0:T(8,128)}, u32[]{:S(2)}) copy-start(f32[1,384,64]{1,2,0:T(8,128)} %param.27) | copy-start | bytes 294916
  107.0 9.9 %copy-start.6 = (f32[1,512,64]{1,2,0:T(8,128)S(1)}, f32[1,512,64]{1,2,0:T(8,128)}, u32[]{:S(2)}) copy-start(f32[1,512,64]{1,2,0:T(8,128)} %param.26) | copy-start | bytes 393220
  107.0 9.9 %copy-start.7 = (f32[1,512,64]{1,2,0:T(8,128)S(1)}, f32[1,512,64]{1,2,0:T(8,128)}, u32[]{:S(2)}) copy-start(f32[1,512,64]{1,2,0:T(8,128)} %param.25) | copy-start | bytes 393220
  107.0 9.9 %copy-start.8 = (f32[1,512,64]{1,2,0:T(8,128)S(1)}, f32[1,512,64]{1,2,0:T(8,128)}, u32[]{:S(2)}) copy-start(f32[1,512,64]{1,2,0:T(8,128)} %param.24) | copy-start | bytes 393220
  107.1 5.0 %collective-permute-start.34 = (f32[32,1024]{1,0:T(8,128)S(1)}, f32[32,1024]{1,0:T(8,128)S(1)}, u32[]{:S(2)}, u32[]{:S(2)}) collective-permute-start(f32[32,1024]{1,0:T(8,128)S(1)} %shard_map.231.refs_0_), channel_id=1, source_target_pairs={{0,2},{1,3},{2,0},{3,1},{4,6},{5,7},{6,4},{7,5},{8,10},{9,11},{10,... | collective-permute-start | bytes 393224 | tf_op jit(solution)/shard_map/ppermute | solution.py:274
  114.7 2.3 %collective-permute-start.35 = (f32[32,512]{1,0:T(8,128)S(1)}, f32[32,512]{1,0:T(8,128)S(1)}, u32[]{:S(2)}, u32[]{:S(2)}) collective-permute-start(f32[32,512]{1,0:T(8,128)S(1)} %get-tuple-element.89), channel_id=1, source_target_pairs={{0,1},{1,0},{2,3},{3,2},{4,5},{5,4},{6,7},{7,6},{8,9},{9,8},{10,11... | collective-permute-start | bytes 196616 | tf_op jit(solution)/shard_map/ppermute | solution.py:274
  114.8 1.4 %collective-permute-start.36 = (f32[32,384]{1,0:T(8,128)S(1)}, f32[32,384]{1,0:T(8,128)S(1)}, u32[]{:S(2)}, u32[]{:S(2)}) collective-permute-start(f32[32,384]{1,0:T(8,128)S(1)} %get-tuple-element.94), channel_id=1, source_target_pairs={{0,1},{1,0},{2,3},{3,2},{4,5},{5,4},{6,7},{7,6},{8,9},{9,8},{10,11... | collective-permute-start | bytes 147464 | tf_op jit(solution)/shard_map/ppermute | solution.py:274
  (1 other events, 4.5 us)

commit v6 on v5

--- a/solution.py
+++ b/solution.py
@@ -157,6 +157,60 @@
         force = times(part, matrix)
         mine[i] = jnp.where(second, force[half:], force[:half])
         theirs[i] = jnp.where(second, force[:half], force[half:])
+
+
+def fetched(kernel, shapes, arrays, *held):
+    count = len(arrays)
+    arrays = [pltpu.with_memory_space_constraint(value, pltpu.HBM) for value in arrays]
+
+    def body(*refs):
+        sources, rest = refs[:count], refs[count:-1]
+        buffers, sems = rest[len(held) + len(shapes) :], refs[-1]
+        copies = [
+            pltpu.make_async_copy(source, buffer, sems.at[i])
+            for i, (source, buffer) in enumerate(zip(sources, buffers))
+        ]
+        for copy in copies:
+            copy.start()
+        for copy in copies:
+            copy.wait()
+        kernel(buffers, rest[: len(held)], *rest[len(held) : len(held) + len(shapes)])
+
+    out = [jax.ShapeDtypeStruct(shape, jnp.float32) for shape in shapes]
+    return pl.pallas_call(
+        body,
+        in_specs=[pl.BlockSpec(memory_space=pltpu.HBM)] * count + [VMEM] * len(held),
+        out_specs=[VMEM] * len(out),
+        out_shape=out,
+        scratch_shapes=[pltpu.VMEM(value.shape, value.dtype) for value in arrays]
+        + [pltpu.SemaphoreType.DMA((count,))],
+        compiler_params=pltpu.CompilerParams(vmem_limit_bytes=24 << 20),
+    )(*arrays, *held)
+
+
+def newmark_load(mass, pattern, disp, vel, acc, ground):
+    return mass[...] * (disp[...] + 2.0 * vel[...] + acc[...] - pattern[...] * ground)
+
+
+def load_int_kernel(fetched_refs, held, load, ground_out):
+    ids, table, *arrays = fetched_refs
+    records, library = ids.shape[1], table.shape[1]
+    shape = (records, records)
+    diagonal = lax.broadcasted_iota(jnp.int32, shape, 0) == lax.broadcasted_iota(jnp.int32, shape, 1)
+    row = jnp.broadcast_to(ids[...].astype(jnp.float32), shape)
+    column = jnp.sum(jnp.where(diagonal, row, 0.0), axis=1, keepdims=True)
+    index = lax.broadcasted_iota(jnp.int32, (records, library), 1).astype(jnp.float32)
+    ground = jnp.sum(jnp.where(column == index, table[...], 0.0), axis=1, keepdims=True)
+    ground_out[...] = jnp.broadcast_to(ground, ground_out.shape)
+    load[...] = newmark_load(*arrays, ground)
+
+
+def load_face_kernel(fetched_refs, held, mine, theirs):
+    load = newmark_load(*fetched_refs, held[0][:, :1])
+    half = load.shape[0] // 2
+    second = lax.axis_index("blk") == 1
+    mine[...] = jnp.where(second, load[half:], load[:half])
+    theirs[...] = jnp.where(second, load[:half], load[half:])
 
 
 def records_kernel(whole, mine, theirs):
@@ -350,15 +404,15 @@
     cube_int = [value[0].T for value in (disp_int, vel_int, acc_int)]
     cube_face = [value[0].T for value in (disp_face, vel_face, acc_face)]
     own_int, own_face = cube_int[0].shape[1], cube_face[0].shape[1]
-    picked = record_ids[:, None] == jnp.arange(library, dtype=jnp.int32)[None, :]
-    ground = jnp.sum(jnp.where(picked, ground_table[None, :], 0.0), axis=1)[:, None]
-
-    def newmark_load(mass, pattern, values):
-        disp, vel, acc = values
-        return mass * (disp + 2.0 * vel + acc - pattern * ground)
-
-    load_int = newmark_load(mass_int, pattern_int, cube_int)
-    load_face = newmark_load(mass_face, pattern_face, cube_face)
+    load_int, ground = fetched(
+        load_int_kernel,
+        [(records, own_int), (records, 128)],
+        [record_ids.reshape(1, records), ground_table.reshape(1, library), mass_int, pattern_int]
+        + cube_int,
+    )
+    mine_face, theirs_face = fetched(
+        load_face_kernel, [(half, own_face)] * 2, [mass_face, pattern_face] + cube_face, ground
+    )
     rows_int, rows_face = 2 * own_int, 2 * own_face
     faces = couple_above.shape[2]
 
@@ -367,10 +421,13 @@
 
     lower_other = mv.core(lower[0])
     across = [mv.chip(load_int, j) for j in range(1, mv.chips)]
+    load_face_half = [mine_face, mv.core(theirs_face)]
     phase_rows = staged(
-        interior_inverse[0], couple_above[0], couple_below[0], after=[load_int, load_face]
-    )
-    phase_rows, *across = lax.optimization_barrier([phase_rows, *across])
+        interior_inverse[0], couple_above[0], couple_below[0], after=[theirs_face]
+    )
+    phase_rows, load_face_half[1], *across = lax.optimization_barrier(
+        [phase_rows, load_face_half[1], *across]
+    )
     beside = [mv.core(piece) for piece in [load_int] + across]
     pieces = [piece for pair in zip([load_int] + across, beside) for piece in pair]
     aligned = load_int.shape[1] % 128 == 0
@@ -381,16 +438,13 @@
     mine, theirs = call(
         functools.partial(forces_kernel, aligned), [(2, half, faces)] * 2, pieces, [phase_rows]
     )
-    mine_face, theirs_face = call(records_kernel, [(half, own_face)] * 2, [load_face])
     mine_int, theirs_int = call(records_kernel, [(half, own_int)] * 2, [load_int])
-    load_face_half = [mine_face, mv.core(theirs_face)]
     load_int_half = [mine_int, mv.core(theirs_int)]
     chunks = call(
         chunks_kernel,
         [(half, faces // mv.chips)] * (2 * mv.chips),
         [mine, mv.core(theirs)],
     )
-    pivot_other = others(pivot[0], [chunks[0]])
     forces = [mv.below(chunks[mv.chips], 0)]
     for j in range(1, mv.chips):
         forces += [mv.chip(chunks[j], j), mv.below(chunks[mv.chips + j], j)]
@@ -398,6 +452,7 @@
     (condensed,) = call(condensed_kernel, shape, load_face_half, [chunks[0]] + forces)
 
     forward = condensed
+    pivot_other = others(pivot[0], [condensed])
     for k in range(1, mv.stories):
         came = mv.gather_story(forward, (k - 1) % 2)
         if k == min(2, mv.stories - 1):
@@ -405,7 +460,7 @@
             upper_other = others(upper[0], [forward])
         if k == mv.stories - 1:
             *came, upper_other = lax.optimization_barrier([*came, upper_other])
-            above_other = others(couple_above[0], [forward])
+            above_other = others(couple_above[0], [upper_other])
         (forward,) = call(
             functools.partial(step_kernel, k),
             shape,
@@ -413,18 +468,18 @@
             [lower[0], lower_other],
             [condensed, forward],
         )
-    came = mv.gather_chips(forward)
-    below_other = others(couple_below[0], [forward])
-    *came, above_other = lax.optimization_barrier([*came, above_other])
-    (pivoted,) = call(rows_kernel, shape, came, [pivot[0], pivot_other])
+    (pivoted,) = call(rows_kernel, shape, mv.gather_chips(forward), [pivot[0], pivot_other])
 
     shape_int = [(half, rows_int)]
     face = pivoted
     for k in range(mv.stories - 2, -1, -1):
         came = mv.gather_story(face, k % 2)
         if k == mv.stories - 2:
-            inverse_other = others(interior_inverse[0], [face])
+            *came, above_other = lax.optimization_barrier([*came, above_other])
+            below_other = others(couple_below[0], [above_other])
+        if k == max(mv.stories - 3, 0):
             *came, below_other = lax.optimization_barrier([*came, below_other])
+            inverse_other = others(interior_inverse[0], [below_other])
         if k == 0:
             odd = mv.gather_story(face, 1)
             (early,) = call(
@@ -434,7 +489,7 @@
                 [couple_above[0], above_other],
                 cost=8 << 20,
             )
-            *came, early, inverse_other = lax.optimization_barrier([*came, early, inverse_other])
+            *came, early = lax.optimization_barrier([*came, early])
         (face,) = call(
             functools.partial(step_kernel, k),
             shape,
@@ -444,6 +499,7 @@
         )
 
     even = mv.gather_story(face, 0)
+    *even, inverse_other = lax.optimization_barrier([*even, inverse_other])
     (reduced,) = call(
         coupled_kernel,
         shape_int,
@@ -455,20 +511,19 @@
         [couple_above[0], above_other],
         [couple_below[0], below_other],
     )
-    mine, theirs = call(
-        last_kernel,
-        [(half, rows_int // 2)] * 2,
-        mv.gather_chips(reduced),
-        [interior_inverse[0], inverse_other],
-    )
-
-    new_int = call(
-        outputs_kernel, [(records, own_int)] * 3, [mine, mv.core(theirs)], cube_int
-    )
     mine, theirs = call(halves_kernel, [(half, own_face)] * 2, [face])
     new_face = call(
         outputs_kernel, [(records, own_face)] * 3, [mine, mv.core(theirs)], cube_face
     )
+    came = mv.gather_chips(reduced)
+    *came, f0, f1, f2 = lax.optimization_barrier([*came, *new_face])
+    mine, theirs = call(
+        last_kernel, [(half, own_int)] * 2, came, [interior_inverse[0], inverse_other]
+    )
+    new_int = call(
+        outputs_kernel, [(records, own_int)] * 3, [mine, mv.core(theirs)], cube_int
+    )
+    new_face = [f0, f1, f2]
     return tuple(out.T[None] for out in (*new_int, *new_face))
 
 

time: 118 us -> 110 us (0.932)
  other arithmetic: 4.49 us -> 0 us
  starting transfers between devices: 39.8 us -> 35.9 us
  Pallas kernels: 18 us -> 20.7 us
  waiting for transfers between devices: 54.4 us -> 51.8 us
    ppermute x35, starting transfers between devices: 37.2 us -> 33.2 us  [permute(): return lax.ppermute(value, AXES, pairs)]
    ppermute x35, waiting for transfers between devices: 47.9 us -> 44.6 us  [permute(): return lax.ppermute(value, AXES, pairs)]
    pallas_call x0 -> x2, Pallas kernels: none -> 2.47 us  [fetched(): pl.pallas_call(body, in_specs=[pl.BlockSpec(memory_space=pltpu.HBM)] * co...]
    mul x2 -> x0, other arithmetic: 2.23 us -> none  [newmark_load(): return mass * (disp + 2.0 * vel + acc - pattern * ground)]
    unnamed x2 -> x0, other arithmetic: 1.4 us -> none
    pallas_call x18 -> x17, Pallas kernels: 13.9 us -> 14.1 us  [call(): pl.pallas_call(body, in_specs=[VMEM] * len(flat), out_specs=[VMEM] * len(...]
  transfers between devices with their start and end apart: 37 -> 37, of which waited for: 22 -> 26; matrix products, arithmetic and copies ran while one was open for 2% -> 0% of each run, Pallas kernels for 7% -> 14%
where the time goes in v6:
time: 110 us; the launch traced here: 109 us
  waiting for transfers between devices  51.8 us (47%)
  starting transfers between devices  35.9 us (33%)
  Pallas kernels  20.7 us (19%)
    ppermute x35, waiting for transfers between devices, permute(): return lax.ppermute(value, AXES, pairs)  44.6 us
    ppermute x35, starting transfers between devices, permute(): return lax.ppermute(value, AXES, pairs)  33.2 us
    pallas_call x17, Pallas kernels, call(): pl.pallas_call(body, in_specs=[VMEM] * len(flat), out_specs=[VMEM] * len(...  14.1 us
    ppermute x2, waiting for transfers between devices, below(): return lax.ppermute(value, AXES, pairs)  7.13 us
    pallas_call x1, Pallas kernels, staged(): pl.pallas_call(body, in_specs=[pl.BlockSpec(memory_space=pltpu.HBM)] * co...  4.08 us
    ppermute x2, starting transfers between devices, below(): return lax.ppermute(value, AXES, pairs)  2.7 us
    pallas_call x2, Pallas kernels, fetched(): pl.pallas_call(body, in_specs=[pl.BlockSpec(memory_space=pltpu.HBM)] * co...  2.47 us
  transfers between devices with their start and end apart: 37, of which 26 were waited for; matrix products, arithmetic and copies ran while one was open for 0% of the time, Pallas kernels for 14%

profile of v6, /device:TPU:0, one launch (start us, length us, event | category | flops | bytes accessed | tf_op | source)
XLA Modules:
  0.0 109.3 jit_solution(10327892911572115564)
XLA Ops:
  1.2 1.3 %shard_map.217 = (f32[64,512]{1,0:T(8,128)S(1)}, f32[64,128]{1,0:T(8,128)S(1)}) custom-call(s32[1,64]{1,0:T(1,128)} %bitcast.77, f32[1,512]{1,0:T(1,128)} %bitcast.76, f32[1,512]{1,0:T(1,128)} %refs_2_.1, f32[1,512]{1,0:T(1,128)} %refs_3_.1, f32[64,512]{1,0:T(8,128)} %bitcast.64, f32[64,512]{1,0:T(8,128)} %bitcast.66, f32[64,512]{1,0:T(8,128)} %bitcast.68), custom_call_target="tpu_custom_call" | custom-call | tf_op jit(solution)/shard_map/pallas_call | solution.py:180
  2.5 2.6 %collective-permute-start.2 = (f32[64,512]{1,0:T(8,128)S(1)}, f32[64,512]{1,0:T(8,128)S(1)}, u32[]{:S(2)}, u32[]{:S(2)}) collective-permute-start(f32[64,512]{1,0:T(8,128)S(1)} %get-tuple-element.62.refs_0_), channel_id=1, source_target_pairs={{0,2},{1,3},{2,0},{3,1},{4,6},{5,7},{6,4},{7,5},{8,10},{9,11},{10,... | collective-permute-start | bytes 393224 | tf_op jit(solution)/shard_map/ppermute | solution.py:328
  5.1 1.1 %shard_map.219 = (f32[32,384]{1,0:T(8,128)S(1)}, f32[32,384]{1,0:T(8,128)S(1)}) custom-call(f32[1,384]{1,0:T(1,128)} %refs_0_.1, f32[1,384]{1,0:T(1,128)} %refs_1_.1, f32[64,384]{1,0:T(8,128)} %bitcast.70, f32[64,384]{1,0:T(8,128)} %bitcast.72, f32[64,384]{1,0:T(8,128)} %bitcast.74, f32[64,128]{1,0:T(8,128)S(1)} %get-tuple-element.65.refs_5_), custom_call_target="tpu_custom_call" | custom-call | tf_op jit(solution)/shard_map/pallas_call | solution.py:180
  6.8 4.1 %shard_map.220.refs_4_ = f32[512,5120]{1,0:T(8,128)S(1)} custom-call(f32[512,2048]{1,0:T(8,128)} %bitcast.56, f32[512,1536]{1,0:T(8,128)} %bitcast.44, f32[512,1536]{1,0:T(8,128)} %bitcast.59), custom_call_target="tpu_custom_call" | custom-call | tf_op jit(solution)/shard_map/pallas_call | solution.py:128
  11.2 1.1 %collective-permute-done.4.refs_3_ = f32[64,512]{1,0:T(8,128)S(1)} collective-permute-done((f32[64,512]{1,0:T(8,128)S(1)}, f32[64,512]{1,0:T(8,128)S(1)}, u32[]{:S(2)}, u32[]{:S(2)}) %collective-permute-start.4) | collective-permute-done | bytes 131104 | tf_op jit(solution)/shard_map/ppermute | solution.py:328
  12.3 2.5 %shard_map.221 = (f32[2,32,1536]{2,1,0:T(8,128)S(1)}, f32[2,32,1536]{2,1,0:T(8,128)S(1)}) custom-call(f32[64,512]{1,0:T(8,128)S(1)} %get-tuple-element.62.refs_0_, f32[64,512]{1,0:T(8,128)S(1)} %collective-permute-done.3.refs_1_, f32[64,512]{1,0:T(8,128)S(1)} %collective-permute-done.2.refs_2_, f32[64,512]{1,0:T(8,128)S(1)} %collective-permute-done.4.refs_3_, ...), custom_call_target="tpu_custom_call" | custom-call | tf_op jit(solution)/shard_map/pallas_call | solution.py:91
  15.1 1.5 %collective-permute-done.5.refs_1_ = f32[2,32,1536]{2,1,0:T(8,128)S(1)} collective-permute-done((f32[2,32,1536]{2,1,0:T(8,128)S(1)}, f32[2,32,1536]{2,1,0:T(8,128)S(1)}, u32[]{:S(2)}, u32[]{:S(2)}) %collective-permute-start.5) | collective-permute-done | bytes 393248 | tf_op jit(solution)/shard_map/ppermute | solution.py:328
  16.7 1.4 %collective-permute-start.6 = (f32[32,768]{1,0:T(8,128)S(1)}, f32[32,768]{1,0:T(8,128)S(1)}, u32[]{:S(2)}, u32[]{:S(2)}) collective-permute-start(f32[32,768]{1,0:T(8,128)S(1)} %get-tuple-element.77), channel_id=1, source_target_pairs={{4,0},{5,1},{6,2},{7,3},{8,4},{9,5},{10,6},{11,7},{12,8},{13,9},{1... | collective-permute-start | bytes 294920 | tf_op jit(solution)/shard_map/ppermute | solution.py:372
  18.4 1.3 %collective-permute-start.8 = (f32[32,768]{1,0:T(8,128)S(1)}, f32[32,768]{1,0:T(8,128)S(1)}, u32[]{:S(2)}, u32[]{:S(2)}) collective-permute-start(f32[32,768]{1,0:T(8,128)S(1)} %get-tuple-element.79), channel_id=1, source_target_pairs={{4,2},{5,3},{6,0},{7,1},{8,6},{9,7},{10,4},{11,5},{12,10},{13,11},... | collective-permute-start | bytes 294920 | tf_op jit(solution)/shard_map/ppermute | solution.py:372
  19.7 4.0 %collective-permute-done.6.refs_3_ = f32[32,768]{1,0:T(8,128)S(1)} collective-permute-done((f32[32,768]{1,0:T(8,128)S(1)}, f32[32,768]{1,0:T(8,128)S(1)}, u32[]{:S(2)}, u32[]{:S(2)}) %collective-permute-start.6) | collective-permute-done | bytes 98336 | tf_op jit(solution)/shard_map/ppermute | solution.py:372
  23.6 3.2 %collective-permute-done.8.refs_5_ = f32[32,768]{1,0:T(8,128)S(1)} collective-permute-done((f32[32,768]{1,0:T(8,128)S(1)}, f32[32,768]{1,0:T(8,128)S(1)}, u32[]{:S(2)}, u32[]{:S(2)}) %collective-permute-start.8) | collective-permute-done | bytes 98336 | tf_op jit(solution)/shard_map/ppermute | solution.py:372
  26.8 3.0 %collective-permute-start.10 = (f32[32,768]{1,0:T(8,128)S(1)}, f32[32,768]{1,0:T(8,128)S(1)}, u32[]{:S(2)}, u32[]{:S(2)}) collective-permute-start(f32[32,768]{1,0:T(8,128)S(1)} %shard_map.223.refs_4_.refs_5_), channel_id=1, source_target_pairs={{0,6},{1,7},{2,4},{3,5},{4,2},{5,3},{6,0},{7,1},{8,14},{9,15},{10,... | collective-permute-start | bytes 294920 | tf_op jit(solution)/shard_map/ppermute | solution.py:328
  29.8 2.7 %collective-permute-done.10.refs_1_ = f32[32,768]{1,0:T(8,128)S(1)} collective-permute-done((f32[32,768]{1,0:T(8,128)S(1)}, f32[32,768]{1,0:T(8,128)S(1)}, u32[]{:S(2)}, u32[]{:S(2)}) %collective-permute-start.10) | collective-permute-done | bytes 98336 | tf_op jit(solution)/shard_map/ppermute | solution.py:328
  32.6 1.9 %collective-permute-done.9.refs_0_ = f32[32,768]{1,0:T(8,128)S(1)} collective-permute-done((f32[32,768]{1,0:T(8,128)S(1)}, f32[32,768]{1,0:T(8,128)S(1)}, u32[]{:S(2)}, u32[]{:S(2)}) %collective-permute-start.9) | collective-permute-done | bytes 98336 | tf_op jit(solution)/shard_map/ppermute | solution.py:328
  34.8 1.9 %collective-permute-start.13 = (f32[32,768]{1,0:T(8,128)S(1)}, f32[32,768]{1,0:T(8,128)S(1)}, u32[]{:S(2)}, u32[]{:S(2)}) collective-permute-start(f32[32,768]{1,0:T(8,128)S(1)} %shard_map.224.refs_5_), channel_id=1, source_target_pairs={{0,2},{1,3},{2,0},{3,1},{4,10},{5,11},{6,8},{7,9},{8,6},{9,7},{10,... | collective-permute-start | bytes 294920 | tf_op jit(solution)/shard_map/ppermute | solution.py:328
  36.6 3.6 %collective-permute-done.12.refs_0_ = f32[32,768]{1,0:T(8,128)S(1)} collective-permute-done((f32[32,768]{1,0:T(8,128)S(1)}, f32[32,768]{1,0:T(8,128)S(1)}, u32[]{:S(2)}, u32[]{:S(2)}) %collective-permute-start.12) | collective-permute-done | bytes 98336 | tf_op jit(solution)/shard_map/ppermute | solution.py:328
  40.2 1.7 %collective-permute-done.13.refs_1_ = f32[32,768]{1,0:T(8,128)S(1)} collective-permute-done((f32[32,768]{1,0:T(8,128)S(1)}, f32[32,768]{1,0:T(8,128)S(1)}, u32[]{:S(2)}, u32[]{:S(2)}) %collective-permute-start.13) | collective-permute-done | bytes 98336 | tf_op jit(solution)/shard_map/ppermute | solution.py:328
  41.9 2.5 %collective-permute-start.15 = (f32[32,768]{1,0:T(8,128)S(1)}, f32[32,768]{1,0:T(8,128)S(1)}, u32[]{:S(2)}, u32[]{:S(2)}) collective-permute-start(f32[32,768]{1,0:T(8,128)S(1)} %shard_map.225.refs_5_), channel_id=1, source_target_pairs={{0,4},{1,5},{2,6},{3,7},{4,0},{5,1},{6,2},{7,3},{8,12},{9,13},{10,... | collective-permute-start | bytes 294920 | tf_op jit(solution)/shard_map/ppermute | solution.py:328
  44.4 1.1 %collective-permute-start.16 = (f32[32,768]{1,0:T(8,128)S(1)}, f32[32,768]{1,0:T(8,128)S(1)}, u32[]{:S(2)}, u32[]{:S(2)}) collective-permute-start(f32[32,768]{1,0:T(8,128)S(1)} %shard_map.225.refs_5_), channel_id=1, source_target_pairs={{0,6},{1,7},{2,4},{3,5},{4,2},{5,3},{6,0},{7,1},{8,14},{9,15},{10,... | collective-permute-start | bytes 294920 | tf_op jit(solution)/shard_map/ppermute | solution.py:328
  45.5 1.9 %collective-permute-done.15.refs_0_ = f32[32,768]{1,0:T(8,128)S(1)} collective-permute-done((f32[32,768]{1,0:T(8,128)S(1)}, f32[32,768]{1,0:T(8,128)S(1)}, u32[]{:S(2)}, u32[]{:S(2)}) %collective-permute-start.15) | collective-permute-done | bytes 98336 | tf_op jit(solution)/shard_map/ppermute | solution.py:328
  47.4 2.8 %collective-permute-done.16.refs_1_ = f32[32,768]{1,0:T(8,128)S(1)} collective-permute-done((f32[32,768]{1,0:T(8,128)S(1)}, f32[32,768]{1,0:T(8,128)S(1)}, u32[]{:S(2)}, u32[]{:S(2)}) %collective-permute-start.16) | collective-permute-done | bytes 98336 | tf_op jit(solution)/shard_map/ppermute | solution.py:328
  50.2 1.4 %collective-permute-start.18 = (f32[32,768]{1,0:T(8,128)S(1)}, f32[32,768]{1,0:T(8,128)S(1)}, u32[]{:S(2)}, u32[]{:S(2)}) collective-permute-start(f32[32,768]{1,0:T(8,128)S(1)} %shard_map.226.refs_0_), channel_id=1, source_target_pairs={{0,2},{1,3},{2,0},{3,1},{4,6},{5,7},{6,4},{7,5},{8,10},{9,11},{10,... | collective-permute-start | bytes 294920 | tf_op jit(solution)/shard_map/ppermute | solution.py:328
  51.6 3.8 %collective-permute-done.18.refs_1_ = f32[32,768]{1,0:T(8,128)S(1)} collective-permute-done((f32[32,768]{1,0:T(8,128)S(1)}, f32[32,768]{1,0:T(8,128)S(1)}, u32[]{:S(2)}, u32[]{:S(2)}) %collective-permute-start.18) | collective-permute-done | bytes 98336 | tf_op jit(solution)/shard_map/ppermute | solution.py:328
  55.5 1.5 %shard_map.227.refs_4_.refs_5_ = f32[32,768]{1,0:T(8,128)S(1)} custom-call(f32[32,768]{1,0:T(8,128)S(1)} %shard_map.226.refs_0_, f32[32,768]{1,0:T(8,128)S(1)} %collective-permute-done.18.refs_1_, f32[384,1536]{1,0:T(8,128)S(1)} %bitcast.63, f32[384,1536]{1,0:T(8,128)S(1)} %collective-permute-done.14.refs_3_), custom_call_target="tpu_custom_call" | custom-call | tf_op jit(solution)/shard_map/pallas_call | solution.py:91
  57.0 1.8 %collective-permute-start.19 = (f32[32,768]{1,0:T(8,128)S(1)}, f32[32,768]{1,0:T(8,128)S(1)}, u32[]{:S(2)}, u32[]{:S(2)}) collective-permute-start(f32[32,768]{1,0:T(8,128)S(1)} %shard_map.227.refs_4_.refs_5_), channel_id=1, source_target_pairs={{0,4},{1,5},{2,6},{3,7},{4,0},{5,1},{6,2},{7,3},{8,12},{9,13},{10,... | collective-permute-start | bytes 294920 | tf_op jit(solution)/shard_map/ppermute | solution.py:328
  58.8 1.1 collective-permute-start.20
  59.9 2.7 %collective-permute-done.19.refs_0_ = f32[32,768]{1,0:T(8,128)S(1)} collective-permute-done((f32[32,768]{1,0:T(8,128)S(1)}, f32[32,768]{1,0:T(8,128)S(1)}, u32[]{:S(2)}, u32[]{:S(2)}) %collective-permute-start.19) | collective-permute-done | bytes 98336 | tf_op jit(solution)/shard_map/ppermute | solution.py:328
  62.6 1.9 %collective-permute-done.20.refs_1_ = f32[32,768]{1,0:T(8,128)S(1)} collective-permute-done((f32[32,768]{1,0:T(8,128)S(1)}, f32[32,768]{1,0:T(8,128)S(1)}, u32[]{:S(2)}, u32[]{:S(2)}) %collective-permute-start.20) | collective-permute-done | bytes 98336 | tf_op jit(solution)/shard_map/ppermute | solution.py:328
  65.4 1.4 %collective-permute-start.23 = (f32[32,768]{1,0:T(8,128)S(1)}, f32[32,768]{1,0:T(8,128)S(1)}, u32[]{:S(2)}, u32[]{:S(2)}) collective-permute-start(f32[32,768]{1,0:T(8,128)S(1)} %shard_map.228.refs_5_), channel_id=1, source_target_pairs={{0,2},{1,3},{2,0},{3,1},{4,10},{5,11},{6,8},{7,9},{8,6},{9,7},{10,... | collective-permute-start | bytes 294920 | tf_op jit(solution)/shard_map/ppermute | solution.py:328
  66.7 3.6 %collective-permute-done.22.refs_0_ = f32[32,768]{1,0:T(8,128)S(1)} collective-permute-done((f32[32,768]{1,0:T(8,128)S(1)}, f32[32,768]{1,0:T(8,128)S(1)}, u32[]{:S(2)}, u32[]{:S(2)}) %collective-permute-start.22) | collective-permute-done | bytes 98336 | tf_op jit(solution)/shard_map/ppermute | solution.py:328
  70.3 1.7 %collective-permute-done.23.refs_1_ = f32[32,768]{1,0:T(8,128)S(1)} collective-permute-done((f32[32,768]{1,0:T(8,128)S(1)}, f32[32,768]{1,0:T(8,128)S(1)}, u32[]{:S(2)}, u32[]{:S(2)}) %collective-permute-start.23) | collective-permute-done | bytes 98336 | tf_op jit(solution)/shard_map/ppermute | solution.py:328
  72.9 5.7 %collective-permute-start.25 = (f32[32,768]{1,0:T(8,128)S(1)}, f32[32,768]{1,0:T(8,128)S(1)}, u32[]{:S(2)}, u32[]{:S(2)}) collective-permute-start(f32[32,768]{1,0:T(8,128)S(1)} %shard_map.229.refs_0_.refs_5_), channel_id=1, source_target_pairs={{0,4},{1,5},{2,6},{3,7},{4,0},{5,1},{6,2},{7,3},{8,12},{9,13},{10,... | collective-permute-start | bytes 294920 | tf_op jit(solution)/shard_map/ppermute | solution.py:328
  79.2 2.0 %shard_map.230.refs_2_ = f32[32,1024]{1,0:T(8,128)S(1)} custom-call(f32[32,768]{1,0:T(8,128)S(1)} %shard_map.229.refs_0_.refs_5_, f32[32,768]{1,0:T(8,128)S(1)} %collective-permute-done.27.refs_1_, f32[512,1536]{1,0:T(8,128)S(1)} %bitcast.46, f32[512,1536]{1,0:T(8,128)S(1)} %collective-permute-done.21.refs_3_.refs_10_), custom_call_target="tpu_custom_call" | custom-call | bytes 8388608 | tf_op jit(solution)/shard_map/pallas_call | solution.py:91
  81.8 2.7 %collective-permute-done.26.refs_1_ = f32[32,768]{1,0:T(8,128)S(1)} collective-permute-done((f32[32,768]{1,0:T(8,128)S(1)}, f32[32,768]{1,0:T(8,128)S(1)}, u32[]{:S(2)}, u32[]{:S(2)}) %collective-permute-start.26) | collective-permute-done | bytes 98336 | tf_op jit(solution)/shard_map/ppermute | solution.py:328
  84.5 1.5 %shard_map.231.refs_3_.refs_0_ = f32[32,768]{1,0:T(8,128)S(1)} custom-call(f32[32,768]{1,0:T(8,128)S(1)} %collective-permute-done.25.refs_0_, f32[32,768]{1,0:T(8,128)S(1)} %collective-permute-done.26.refs_1_, f32[384,1536]{1,0:T(8,128)S(1)} %bitcast.55, f32[384,1536]{1,0:T(8,128)S(1)} %collective-permute-done.17.refs_3_, ...), custom_call_target="tpu_custom_call" | custom-call | tf_op jit(solution)/shard_map/pallas_call | solution.py:91
  86.3 2.1 %collective-permute-start.30 = (f32[32,768]{1,0:T(8,128)S(1)}, f32[32,768]{1,0:T(8,128)S(1)}, u32[]{:S(2)}, u32[]{:S(2)}) collective-permute-start(f32[32,768]{1,0:T(8,128)S(1)} %shard_map.231.refs_3_.refs_0_), channel_id=1, source_target_pairs={{0,6},{1,7},{2,4},{3,5},{4,2},{5,3},{6,0},{7,1},{8,14},{9,15},{10,... | collective-permute-start | bytes 294920 | tf_op jit(solution)/shard_map/ppermute | solution.py:328
  88.4 1.2 %collective-permute-start.32 = (f32[32,768]{1,0:T(8,128)S(1)}, f32[32,768]{1,0:T(8,128)S(1)}, u32[]{:S(2)}, u32[]{:S(2)}) collective-permute-start(f32[32,768]{1,0:T(8,128)S(1)} %shard_map.229.refs_0_.refs_5_), channel_id=1, source_target_pairs={{0,2},{1,3},{2,0},{3,1},{4,8},{5,9},{6,10},{7,11},{8,4},{9,5},{10,... | collective-permute-start | bytes 294920 | tf_op jit(solution)/shard_map/ppermute | solution.py:328
  90.5 0.9 collective-permute-done.29.refs_5_
  92.4 1.2 %collective-permute-done.refs_1_ = f32[32,512]{1,0:T(8,128)S(1)} collective-permute-done((f32[32,512]{1,0:T(8,128)S(1)}, f32[32,512]{1,0:T(8,128)S(1)}, u32[]{:S(2)}, u32[]{:S(2)}) %collective-permute-start) | collective-permute-done | bytes 65568 | tf_op jit(solution)/shard_map/ppermute | solution.py:328
  93.7 0.9 collective-permute-done.32.refs_7_
  94.6 1.9 %collective-permute-done.33.refs_8_ = f32[32,768]{1,0:T(8,128)S(1)} collective-permute-done((f32[32,768]{1,0:T(8,128)S(1)}, f32[32,768]{1,0:T(8,128)S(1)}, u32[]{:S(2)}, u32[]{:S(2)}) %collective-permute-start.33) | collective-permute-done | bytes 98336 | tf_op jit(solution)/shard_map/ppermute | solution.py:328
  96.5 1.1 collective-permute-done.28.refs_4_
  97.6 2.0 %shard_map.232.refs_0_ = f32[32,1024]{1,0:T(8,128)S(1)} custom-call(f32[32,512]{1,0:T(8,128)S(1)} %get-tuple-element.63.refs_0_, f32[32,512]{1,0:T(8,128)S(1)} %collective-permute-done.refs_1_, f32[32,1024]{1,0:T(8,128)S(1)} %shard_map.230.refs_2_, f32[32,768]{1,0:T(8,128)S(1)} %shard_map.231.refs_3_.refs_0_, f32[32,768]{1,0:T(8,128)S(1)} %collective-permute-done.28.refs_4_, ...), custom_call_target="tpu_custom_call" | custom-call | tf_op jit(solution)/shard_map/pallas_call | solution.py:91
  99.6 1.6 %collective-permute-start.34 = (f32[32,1024]{1,0:T(8,128)S(1)}, f32[32,1024]{1,0:T(8,128)S(1)}, u32[]{:S(2)}, u32[]{:S(2)}) collective-permute-start(f32[32,1024]{1,0:T(8,128)S(1)} %shard_map.232.refs_0_), channel_id=1, source_target_pairs={{0,2},{1,3},{2,0},{3,1},{4,6},{5,7},{6,4},{7,5},{8,10},{9,11},{10,... | collective-permute-start | bytes 393224 | tf_op jit(solution)/shard_map/ppermute | solution.py:328
  101.3 1.2 %collective-permute-done.35.refs_1_ = f32[32,384]{1,0:T(8,128)S(1)} collective-permute-done((f32[32,384]{1,0:T(8,128)S(1)}, f32[32,384]{1,0:T(8,128)S(1)}, u32[]{:S(2)}, u32[]{:S(2)}) %collective-permute-start.35) | collective-permute-done | bytes 49184 | tf_op jit(solution)/shard_map/ppermute | solution.py:328
  103.2 1.4 %collective-permute-done.34.refs_1_ = f32[32,1024]{1,0:T(8,128)S(1)} collective-permute-done((f32[32,1024]{1,0:T(8,128)S(1)}, f32[32,1024]{1,0:T(8,128)S(1)}, u32[]{:S(2)}, u32[]{:S(2)}) %collective-permute-start.34) | collective-permute-done | bytes 131104 | tf_op jit(solution)/shard_map/ppermute | solution.py:328
  104.6 2.6 %shard_map.235 = (f32[32,512]{1,0:T(8,128)S(1)}, f32[32,512]{1,0:T(8,128)S(1)}) custom-call(f32[32,1024]{1,0:T(8,128)S(1)} %shard_map.232.refs_0_, f32[32,1024]{1,0:T(8,128)S(1)} %collective-permute-done.34.refs_1_, f32[512,2048]{1,0:T(8,128)S(1)} %bitcast.58, f32[512,2048]{1,0:T(8,128)S(1)} %collective-permute-done.31.refs_3_), custom_call_target="tpu_custom_call" | custom-call | tf_op jit(solution)/shard_map/pallas_call | solution.py:91
  107.3 1.3 %collective-permute-done.36.refs_1_ = f32[32,512]{1,0:T(8,128)S(1)} collective-permute-done((f32[32,512]{1,0:T(8,128)S(1)}, f32[32,512]{1,0:T(8,128)S(1)}, u32[]{:S(2)}, u32[]{:S(2)}) %collective-permute-start.36) | collective-permute-done | bytes 65568 | tf_op jit(solution)/shard_map/ppermute | solution.py:328
  (70 shorter events, 9.1 us)
Async XLA Ops:
  0.6 33.8 %collective-permute-start.11 = (f32[384,1536]{1,0:T(8,128)}, f32[384,1536]{1,0:T(8,128)S(1)}, u32[]{:S(2)}, u32[]{:S(2)}) collective-permute-start(f32[384,1536]{1,0:T(8,128)} %bitcast.48), channel_id=1, source_target_pairs={{0,1},{1,0},{2,3},{3,2},{4,5},{5,4},{6,7},{7,6},{8,9},{9,8},{10,11... | collective-permute-start | bytes 7077896 | tf_op jit(solution)/shard_map/ppermute | solution.py:328
  2.5 8.4 %collective-permute-start.2 = (f32[64,512]{1,0:T(8,128)S(1)}, f32[64,512]{1,0:T(8,128)S(1)}, u32[]{:S(2)}, u32[]{:S(2)}) collective-permute-start(f32[64,512]{1,0:T(8,128)S(1)} %get-tuple-element.62.refs_0_), channel_id=1, source_target_pairs={{0,2},{1,3},{2,0},{3,1},{4,6},{5,7},{6,4},{7,5},{8,10},{9,11},{10,... | collective-permute-start | bytes 393224 | tf_op jit(solution)/shard_map/ppermute | solution.py:328
  6.2 4.7 %collective-permute-start.1 = (f32[32,384]{1,0:T(8,128)S(1)}, f32[32,384]{1,0:T(8,128)S(1)}, u32[]{:S(2)}, u32[]{:S(2)}) collective-permute-start(f32[32,384]{1,0:T(8,128)S(1)} %get-tuple-element.67), channel_id=1, source_target_pairs={{0,1},{1,0},{2,3},{3,2},{4,5},{5,4},{6,7},{7,6},{8,9},{9,8},{10,11... | collective-permute-start | bytes 147464 | tf_op jit(solution)/shard_map/ppermute | solution.py:328
  6.5 4.7 %collective-permute-start.3 = (f32[64,512]{1,0:T(8,128)S(1)}, f32[64,512]{1,0:T(8,128)S(1)}, u32[]{:S(2)}, u32[]{:S(2)}) collective-permute-start(f32[64,512]{1,0:T(8,128)S(1)} %get-tuple-element.62.refs_0_), channel_id=1, source_target_pairs={{0,1},{1,0},{2,3},{3,2},{4,5},{5,4},{6,7},{7,6},{8,9},{9,8},{10,11... | collective-permute-start | bytes 393224 | tf_op jit(solution)/shard_map/ppermute | solution.py:328
  10.9 18.9 %copy-start.5 = (f32[1,384,1536]{2,1,0:T(8,128)S(1)}, f32[1,384,1536]{2,1,0:T(8,128)}, u32[]{:S(2)}) copy-start(f32[1,384,1536]{2,1,0:T(8,128)} %param.34) | copy-start | bytes 7077892
  10.9 23.5 %copy-start.1 = (f32[1,384,1536]{2,1,0:T(8,128)S(1)}, f32[1,384,1536]{2,1,0:T(8,128)}, u32[]{:S(2)}) copy-start(f32[1,384,1536]{2,1,0:T(8,128)} %param.33) | copy-start | bytes 7077892
  10.9 1.4 %collective-permute-start.4 = (f32[64,512]{1,0:T(8,128)S(1)}, f32[64,512]{1,0:T(8,128)S(1)}, u32[]{:S(2)}, u32[]{:S(2)}) collective-permute-start(f32[64,512]{1,0:T(8,128)S(1)} %collective-permute-done.2.refs_2_), channel_id=1, source_target_pairs={{0,1},{1,0},{2,3},{3,2},{4,5},{5,4},{6,7},{7,6},{8,9},{9,8},{10,11... | collective-permute-start | bytes 393224 | tf_op jit(solution)/shard_map/ppermute | solution.py:328
  14.9 1.8 %collective-permute-start.5 = (f32[2,32,1536]{2,1,0:T(8,128)S(1)}, f32[2,32,1536]{2,1,0:T(8,128)S(1)}, u32[]{:S(2)}, u32[]{:S(2)}) collective-permute-start(f32[2,32,1536]{2,1,0:T(8,128)S(1)} %get-tuple-element.75), channel_id=1, source_target_pairs={{0,1},{1,0},{2,3},{3,2},{4,5},{5,4},{6,7},{7,6},{8,9},{9,8},{10,11... | collective-permute-start | bytes 1179656 | tf_op jit(solution)/shard_map/ppermute | solution.py:328
  16.7 17.8 %copy-start.2 = (f32[1,384,1536]{2,1,0:T(8,128)S(1)}, f32[1,384,1536]{2,1,0:T(8,128)}, u32[]{:S(2)}) copy-start(f32[1,384,1536]{2,1,0:T(8,128)} %param.35) | copy-start | bytes 7077892
  16.7 6.9 %collective-permute-start.6 = (f32[32,768]{1,0:T(8,128)S(1)}, f32[32,768]{1,0:T(8,128)S(1)}, u32[]{:S(2)}, u32[]{:S(2)}) collective-permute-start(f32[32,768]{1,0:T(8,128)S(1)} %get-tuple-element.77), channel_id=1, source_target_pairs={{4,0},{5,1},{6,2},{7,3},{8,4},{9,5},{10,6},{11,7},{12,8},{13,9},{1... | collective-permute-start | bytes 294920 | tf_op jit(solution)/shard_map/ppermute | solution.py:372
  18.1 5.5 %collective-permute-start.7 = (f32[32,768]{1,0:T(8,128)S(1)}, f32[32,768]{1,0:T(8,128)S(1)}, u32[]{:S(2)}, u32[]{:S(2)}) collective-permute-start(f32[32,768]{1,0:T(8,128)S(1)} %get-tuple-element.78), channel_id=1, source_target_pairs={{0,2},{1,3},{2,0},{3,1},{4,6},{5,7},{6,4},{7,5},{8,10},{9,11},{10,... | collective-permute-start | bytes 294920 | tf_op jit(solution)/shard_map/ppermute | solution.py:328
  18.4 8.4 %collective-permute-start.8 = (f32[32,768]{1,0:T(8,128)S(1)}, f32[32,768]{1,0:T(8,128)S(1)}, u32[]{:S(2)}, u32[]{:S(2)}) collective-permute-start(f32[32,768]{1,0:T(8,128)S(1)} %get-tuple-element.79), channel_id=1, source_target_pairs={{4,2},{5,3},{6,0},{7,1},{8,6},{9,7},{10,4},{11,5},{12,10},{13,11},... | collective-permute-start | bytes 294920 | tf_op jit(solution)/shard_map/ppermute | solution.py:372
  26.8 5.7 %collective-permute-start.10 = (f32[32,768]{1,0:T(8,128)S(1)}, f32[32,768]{1,0:T(8,128)S(1)}, u32[]{:S(2)}, u32[]{:S(2)}) collective-permute-start(f32[32,768]{1,0:T(8,128)S(1)} %shard_map.223.refs_4_.refs_5_), channel_id=1, source_target_pairs={{0,6},{1,7},{2,4},{3,5},{4,2},{5,3},{6,0},{7,1},{8,14},{9,15},{10,... | collective-permute-start | bytes 294920 | tf_op jit(solution)/shard_map/ppermute | solution.py:328
  29.8 4.6 %collective-permute-start.9 = (f32[32,768]{1,0:T(8,128)S(1)}, f32[32,768]{1,0:T(8,128)S(1)}, u32[]{:S(2)}, u32[]{:S(2)}) collective-permute-start(f32[32,768]{1,0:T(8,128)S(1)} %shard_map.223.refs_4_.refs_5_), channel_id=1, source_target_pairs={{0,4},{1,5},{2,6},{3,7},{4,0},{5,1},{6,2},{7,3},{8,12},{9,13},{10,... | collective-permute-start | bytes 294920 | tf_op jit(solution)/shard_map/ppermute | solution.py:328
  29.8 12.1 %collective-permute-start.14 = (f32[384,1536]{1,0:T(8,128)S(1)}, f32[384,1536]{1,0:T(8,128)S(1)}, u32[]{:S(2)}, u32[]{:S(2)}) collective-permute-start(f32[384,1536]{1,0:T(8,128)S(1)} %bitcast.62), channel_id=1, source_target_pairs={{0,1},{1,0},{2,3},{3,2},{4,5},{5,4},{6,7},{7,6},{8,9},{9,8},{10,11... | collective-permute-start | bytes 7077896 | tf_op jit(solution)/shard_map/ppermute | solution.py:328
  34.4 15.7 %copy-start = (f32[1,512,1536]{2,1,0:T(8,128)S(1)}, f32[1,512,1536]{2,1,0:T(8,128)}, u32[]{:S(2)}) copy-start(f32[1,512,1536]{2,1,0:T(8,128)} %param.32) | copy-start | bytes 9437188
  34.5 15.7 %collective-permute-start.17 = (f32[384,1536]{1,0:T(8,128)S(1)}, f32[384,1536]{1,0:T(8,128)S(1)}, u32[]{:S(2)}, u32[]{:S(2)}) collective-permute-start(f32[384,1536]{1,0:T(8,128)S(1)} %bitcast.52), channel_id=1, source_target_pairs={{0,1},{1,0},{2,3},{3,2},{4,5},{5,4},{6,7},{7,6},{8,9},{9,8},{10,11... | collective-permute-start | bytes 7077896 | tf_op jit(solution)/shard_map/ppermute | solution.py:328
  34.5 5.7 %collective-permute-start.12 = (f32[32,768]{1,0:T(8,128)S(1)}, f32[32,768]{1,0:T(8,128)S(1)}, u32[]{:S(2)}, u32[]{:S(2)}) collective-permute-start(f32[32,768]{1,0:T(8,128)S(1)} %shard_map.224.refs_5_), channel_id=1, source_target_pairs={{0,2},{1,3},{2,0},{3,1},{4,8},{5,9},{6,10},{7,11},{8,4},{9,5},{10,... | collective-permute-start | bytes 294920 | tf_op jit(solution)/shard_map/ppermute | solution.py:328
  34.8 7.1 %collective-permute-start.13 = (f32[32,768]{1,0:T(8,128)S(1)}, f32[32,768]{1,0:T(8,128)S(1)}, u32[]{:S(2)}, u32[]{:S(2)}) collective-permute-start(f32[32,768]{1,0:T(8,128)S(1)} %shard_map.224.refs_5_), channel_id=1, source_target_pairs={{0,2},{1,3},{2,0},{3,1},{4,10},{5,11},{6,8},{7,9},{8,6},{9,7},{10,... | collective-permute-start | bytes 294920 | tf_op jit(solution)/shard_map/ppermute | solution.py:328
  41.9 5.5 %collective-permute-start.15 = (f32[32,768]{1,0:T(8,128)S(1)}, f32[32,768]{1,0:T(8,128)S(1)}, u32[]{:S(2)}, u32[]{:S(2)}) collective-permute-start(f32[32,768]{1,0:T(8,128)S(1)} %shard_map.225.refs_5_), channel_id=1, source_target_pairs={{0,4},{1,5},{2,6},{3,7},{4,0},{5,1},{6,2},{7,3},{8,12},{9,13},{10,... | collective-permute-start | bytes 294920 | tf_op jit(solution)/shard_map/ppermute | solution.py:328
  44.4 5.8 %collective-permute-start.16 = (f32[32,768]{1,0:T(8,128)S(1)}, f32[32,768]{1,0:T(8,128)S(1)}, u32[]{:S(2)}, u32[]{:S(2)}) collective-permute-start(f32[32,768]{1,0:T(8,128)S(1)} %shard_map.225.refs_5_), channel_id=1, source_target_pairs={{0,6},{1,7},{2,4},{3,5},{4,2},{5,3},{6,0},{7,1},{8,14},{9,15},{10,... | collective-permute-start | bytes 294920 | tf_op jit(solution)/shard_map/ppermute | solution.py:328
  50.2 14.4 %collective-permute-start.21 = (f32[512,1536]{1,0:T(8,128)S(1)}, f32[512,1536]{1,0:T(8,128)S(1)}, u32[]{:S(2)}, u32[]{:S(2)}) collective-permute-start(f32[512,1536]{1,0:T(8,128)S(1)} %bitcast.45), channel_id=1, source_target_pairs={{0,1},{1,0},{2,3},{3,2},{4,5},{5,4},{6,7},{7,6},{8,9},{9,8},{10,11... | collective-permute-start | bytes 9437192 | tf_op jit(solution)/shard_map/ppermute | solution.py:328
  50.2 14.4 %copy-start.4 = (f32[1,512,1536]{2,1,0:T(8,128)S(1)}, f32[1,512,1536]{2,1,0:T(8,128)}, u32[]{:S(2)}) copy-start(f32[1,512,1536]{2,1,0:T(8,128)} %param.31) | copy-start | bytes 9437188
  50.2 5.2 %collective-permute-start.18 = (f32[32,768]{1,0:T(8,128)S(1)}, f32[32,768]{1,0:T(8,128)S(1)}, u32[]{:S(2)}, u32[]{:S(2)}) collective-permute-start(f32[32,768]{1,0:T(8,128)S(1)} %shard_map.226.refs_0_), channel_id=1, source_target_pairs={{0,2},{1,3},{2,0},{3,1},{4,6},{5,7},{6,4},{7,5},{8,10},{9,11},{10,... | collective-permute-start | bytes 294920 | tf_op jit(solution)/shard_map/ppermute | solution.py:328
  57.0 15.0 %copy-start.3 = (f32[1,512,2048]{2,1,0:T(8,128)S(1)}, f32[1,512,2048]{2,1,0:T(8,128)}, u32[]{:S(2)}) copy-start(f32[1,512,2048]{2,1,0:T(8,128)} %param.30) | copy-start | bytes 12582916
  57.0 5.6 %collective-permute-start.19 = (f32[32,768]{1,0:T(8,128)S(1)}, f32[32,768]{1,0:T(8,128)S(1)}, u32[]{:S(2)}, u32[]{:S(2)}) collective-permute-start(f32[32,768]{1,0:T(8,128)S(1)} %shard_map.227.refs_4_.refs_5_), channel_id=1, source_target_pairs={{0,4},{1,5},{2,6},{3,7},{4,0},{5,1},{6,2},{7,3},{8,12},{9,13},{10,... | collective-permute-start | bytes 294920 | tf_op jit(solution)/shard_map/ppermute | solution.py:328
  58.8 5.8 %collective-permute-start.20 = (f32[32,768]{1,0:T(8,128)S(1)}, f32[32,768]{1,0:T(8,128)S(1)}, u32[]{:S(2)}, u32[]{:S(2)}) collective-permute-start(f32[32,768]{1,0:T(8,128)S(1)} %shard_map.227.refs_4_.refs_5_), channel_id=1, source_target_pairs={{0,6},{1,7},{2,4},{3,5},{4,2},{5,3},{6,0},{7,1},{8,14},{9,15},{10,... | collective-permute-start | bytes 294920 | tf_op jit(solution)/shard_map/ppermute | solution.py:328
  64.6 7.4 %collective-permute-start.24 = (f32[512,1536]{1,0:T(8,128)S(1)}, f32[512,1536]{1,0:T(8,128)S(1)}, u32[]{:S(2)}, u32[]{:S(2)}) collective-permute-start(f32[512,1536]{1,0:T(8,128)S(1)} %bitcast.60), channel_id=1, source_target_pairs={{0,1},{1,0},{2,3},{3,2},{4,5},{5,4},{6,7},{7,6},{8,9},{9,8},{10,11... | collective-permute-start | bytes 9437192 | tf_op jit(solution)/shard_map/ppermute | solution.py:328
  64.6 5.7 %collective-permute-start.22 = (f32[32,768]{1,0:T(8,128)S(1)}, f32[32,768]{1,0:T(8,128)S(1)}, u32[]{:S(2)}, u32[]{:S(2)}) collective-permute-start(f32[32,768]{1,0:T(8,128)S(1)} %shard_map.228.refs_5_), channel_id=1, source_target_pairs={{0,2},{1,3},{2,0},{3,1},{4,8},{5,9},{6,10},{7,11},{8,4},{9,5},{10,... | collective-permute-start | bytes 294920 | tf_op jit(solution)/shard_map/ppermute | solution.py:328
  65.4 6.6 %collective-permute-start.23 = (f32[32,768]{1,0:T(8,128)S(1)}, f32[32,768]{1,0:T(8,128)S(1)}, u32[]{:S(2)}, u32[]{:S(2)}) collective-permute-start(f32[32,768]{1,0:T(8,128)S(1)} %shard_map.228.refs_5_), channel_id=1, source_target_pairs={{0,2},{1,3},{2,0},{3,1},{4,10},{5,11},{6,8},{7,9},{8,6},{9,7},{10,... | collective-permute-start | bytes 294920 | tf_op jit(solution)/shard_map/ppermute | solution.py:328
  72.0 20.4 %collective-permute-start.31 = (f32[512,2048]{1,0:T(8,128)S(1)}, f32[512,2048]{1,0:T(8,128)S(1)}, u32[]{:S(2)}, u32[]{:S(2)}) collective-permute-start(f32[512,2048]{1,0:T(8,128)S(1)} %bitcast.57), channel_id=1, source_target_pairs={{0,1},{1,0},{2,3},{3,2},{4,5},{5,4},{6,7},{7,6},{8,9},{9,8},{10,11... | collective-permute-start | bytes 12582920 | tf_op jit(solution)/shard_map/ppermute | solution.py:328
  72.2 7.0 %collective-permute-start.27 = (f32[32,768]{1,0:T(8,128)S(1)}, f32[32,768]{1,0:T(8,128)S(1)}, u32[]{:S(2)}, u32[]{:S(2)}) collective-permute-start(f32[32,768]{1,0:T(8,128)S(1)} %shard_map.229.refs_0_.refs_5_), channel_id=1, source_target_pairs={{0,2},{1,3},{2,0},{3,1},{4,6},{5,7},{6,4},{7,5},{8,10},{9,11},{10,... | collective-permute-start | bytes 294920 | tf_op jit(solution)/shard_map/ppermute | solution.py:328
  72.9 8.8 %collective-permute-start.25 = (f32[32,768]{1,0:T(8,128)S(1)}, f32[32,768]{1,0:T(8,128)S(1)}, u32[]{:S(2)}, u32[]{:S(2)}) collective-permute-start(f32[32,768]{1,0:T(8,128)S(1)} %shard_map.229.refs_0_.refs_5_), channel_id=1, source_target_pairs={{0,4},{1,5},{2,6},{3,7},{4,0},{5,1},{6,2},{7,3},{8,12},{9,13},{10,... | collective-permute-start | bytes 294920 | tf_op jit(solution)/shard_map/ppermute | solution.py:328
  78.6 5.9 %collective-permute-start.26 = (f32[32,768]{1,0:T(8,128)S(1)}, f32[32,768]{1,0:T(8,128)S(1)}, u32[]{:S(2)}, u32[]{:S(2)}) collective-permute-start(f32[32,768]{1,0:T(8,128)S(1)} %shard_map.229.refs_0_.refs_5_), channel_id=1, source_target_pairs={{0,6},{1,7},{2,4},{3,5},{4,2},{5,3},{6,0},{7,1},{8,14},{9,15},{10,... | collective-permute-start | bytes 294920 | tf_op jit(solution)/shard_map/ppermute | solution.py:328
  86.1 5.2 %collective-permute-start.29 = (f32[32,768]{1,0:T(8,128)S(1)}, f32[32,768]{1,0:T(8,128)S(1)}, u32[]{:S(2)}, u32[]{:S(2)}) collective-permute-start(f32[32,768]{1,0:T(8,128)S(1)} %shard_map.231.refs_3_.refs_0_), channel_id=1, source_target_pairs={{0,4},{1,5},{2,6},{3,7},{4,0},{5,1},{6,2},{7,3},{8,12},{9,13},{10,... | collective-permute-start | bytes 294920 | tf_op jit(solution)/shard_map/ppermute | solution.py:328
  86.3 6.1 %collective-permute-start.30 = (f32[32,768]{1,0:T(8,128)S(1)}, f32[32,768]{1,0:T(8,128)S(1)}, u32[]{:S(2)}, u32[]{:S(2)}) collective-permute-start(f32[32,768]{1,0:T(8,128)S(1)} %shard_map.231.refs_3_.refs_0_), channel_id=1, source_target_pairs={{0,6},{1,7},{2,4},{3,5},{4,2},{5,3},{6,0},{7,1},{8,14},{9,15},{10,... | collective-permute-start | bytes 294920 | tf_op jit(solution)/shard_map/ppermute | solution.py:328
  88.4 6.1 %collective-permute-start.32 = (f32[32,768]{1,0:T(8,128)S(1)}, f32[32,768]{1,0:T(8,128)S(1)}, u32[]{:S(2)}, u32[]{:S(2)}) collective-permute-start(f32[32,768]{1,0:T(8,128)S(1)} %shard_map.229.refs_0_.refs_5_), channel_id=1, source_target_pairs={{0,2},{1,3},{2,0},{3,1},{4,8},{5,9},{6,10},{7,11},{8,4},{9,5},{10,... | collective-permute-start | bytes 294920 | tf_op jit(solution)/shard_map/ppermute | solution.py:328
  89.6 6.9 %collective-permute-start.33 = (f32[32,768]{1,0:T(8,128)S(1)}, f32[32,768]{1,0:T(8,128)S(1)}, u32[]{:S(2)}, u32[]{:S(2)}) collective-permute-start(f32[32,768]{1,0:T(8,128)S(1)} %shard_map.229.refs_0_.refs_5_), channel_id=1, source_target_pairs={{0,2},{1,3},{2,0},{3,1},{4,10},{5,11},{6,8},{7,9},{8,6},{9,7},{10,... | collective-permute-start | bytes 294920 | tf_op jit(solution)/shard_map/ppermute | solution.py:328
  91.3 6.3 %collective-permute-start.28 = (f32[32,768]{1,0:T(8,128)S(1)}, f32[32,768]{1,0:T(8,128)S(1)}, u32[]{:S(2)}, u32[]{:S(2)}) collective-permute-start(f32[32,768]{1,0:T(8,128)S(1)} %shard_map.231.refs_3_.refs_0_), channel_id=1, source_target_pairs={{0,2},{1,3},{2,0},{3,1},{4,6},{5,7},{6,4},{7,5},{8,10},{9,11},{10,... | collective-permute-start | bytes 294920 | tf_op jit(solution)/shard_map/ppermute | solution.py:328
  92.4 1.3 %collective-permute-start = (f32[32,512]{1,0:T(8,128)S(1)}, f32[32,512]{1,0:T(8,128)S(1)}, u32[]{:S(2)}, u32[]{:S(2)}) collective-permute-start(f32[32,512]{1,0:T(8,128)S(1)} %get-tuple-element.64), channel_id=1, source_target_pairs={{0,1},{1,0},{2,3},{3,2},{4,5},{5,4},{6,7},{7,6},{8,9},{9,8},{10,11... | collective-permute-start | bytes 196616 | tf_op jit(solution)/shard_map/ppermute | solution.py:328
  97.6 4.9 %copy-start.9 = (f32[1,384,64]{1,2,0:T(8,128)S(1)}, f32[1,384,64]{1,2,0:T(8,128)}, u32[]{:S(2)}) copy-start(f32[1,384,64]{1,2,0:T(8,128)} %param.27) | copy-start | bytes 294916
  97.6 4.9 %copy-start.10 = (f32[1,384,64]{1,2,0:T(8,128)S(1)}, f32[1,384,64]{1,2,0:T(8,128)}, u32[]{:S(2)}) copy-start(f32[1,384,64]{1,2,0:T(8,128)} %param.28) | copy-start | bytes 294916
  97.6 4.9 %copy-start.11 = (f32[1,384,64]{1,2,0:T(8,128)S(1)}, f32[1,384,64]{1,2,0:T(8,128)}, u32[]{:S(2)}) copy-start(f32[1,384,64]{1,2,0:T(8,128)} %param.29) | copy-start | bytes 294916
  99.6 5.0 %collective-permute-start.34 = (f32[32,1024]{1,0:T(8,128)S(1)}, f32[32,1024]{1,0:T(8,128)S(1)}, u32[]{:S(2)}, u32[]{:S(2)}) collective-permute-start(f32[32,1024]{1,0:T(8,128)S(1)} %shard_map.232.refs_0_), channel_id=1, source_target_pairs={{0,2},{1,3},{2,0},{3,1},{4,6},{5,7},{6,4},{7,5},{8,10},{9,11},{10,... | collective-permute-start | bytes 393224 | tf_op jit(solution)/shard_map/ppermute | solution.py:328
  101.2 1.3 %collective-permute-start.35 = (f32[32,384]{1,0:T(8,128)S(1)}, f32[32,384]{1,0:T(8,128)S(1)}, u32[]{:S(2)}, u32[]{:S(2)}) collective-permute-start(f32[32,384]{1,0:T(8,128)S(1)} %get-tuple-element.103), channel_id=1, source_target_pairs={{0,1},{1,0},{2,3},{3,2},{4,5},{5,4},{6,7},{7,6},{8,9},{9,8},{10,11... | collective-permute-start | bytes 147464 | tf_op jit(solution)/shard_map/ppermute | solution.py:328
  104.6 3.9 %copy-start.7 = (f32[1,512,64]{1,2,0:T(8,128)S(1)}, f32[1,512,64]{1,2,0:T(8,128)}, u32[]{:S(2)}) copy-start(f32[1,512,64]{1,2,0:T(8,128)} %param.25) | copy-start | bytes 393220
  104.6 3.9 %copy-start.8 = (f32[1,512,64]{1,2,0:T(8,128)S(1)}, f32[1,512,64]{1,2,0:T(8,128)}, u32[]{:S(2)}) copy-start(f32[1,512,64]{1,2,0:T(8,128)} %param.26) | copy-start | bytes 393220
  107.2 1.3 %collective-permute-start.36 = (f32[32,512]{1,0:T(8,128)S(1)}, f32[32,512]{1,0:T(8,128)S(1)}, u32[]{:S(2)}, u32[]{:S(2)}) collective-permute-start(f32[32,512]{1,0:T(8,128)S(1)} %get-tuple-element.111), channel_id=1, source_target_pairs={{0,1},{1,0},{2,3},{3,2},{4,5},{5,4},{6,7},{7,6},{8,9},{9,8},{10,11... | collective-permute-start | bytes 196616 | tf_op jit(solution)/shard_map/ppermute | solution.py:328
  (1 other events, 3.9 us)

commit v7 on v6

--- a/solution.py
+++ b/solution.py
@@ -33,20 +33,20 @@
     return total
 
 
-def times_rows(left, *refs):
+def times_rows(left, *refs, columns=slice(None)):
     left = stacked(left)
     count = refs[0].shape[0]
     ends = count * len(refs)
-    columns = []
+    results = []
     for start in range(0, ends, TILE):
         stop = min(start + TILE, ends)
         blocks = []
         for i, ref in enumerate(refs):
             low, high = max(start - i * count, 0), min(stop - i * count, count)
             if low < high:
-                blocks.append(ref[low:high, :])
-        columns.append(matmul(left, jnp.concatenate(blocks, axis=0), 1))
-    return jnp.concatenate(columns, axis=1)
+                blocks.append(ref[low:high, columns])
+        results.append(matmul(left, jnp.concatenate(blocks, axis=0), 1))
+    return jnp.concatenate(results, axis=1)
 
 
 def times(left, ref):
@@ -261,12 +261,39 @@
             outs[i * chips + j][...] = piece
 
 
-def step_kernel(story, pieces, rows, terms, out):
+def from_chip(count, j):
+    def columns(width):
+        if count == 1:
+            return slice(None)
+        start = (lax.axis_index("rec") ^ j) * width
+        return pl.ds(pl.multiple_of(start, 128), width)
+
+    return columns
+
+
+def plus(value, sofar):
+    return value + sofar[0][...] if sofar else value
+
+
+def part_kernel(columns, story, piece, rows, sofar, out):
+    def product():
+        value = piece[0][...]
+        out[...] = plus(times_rows(value, *rows, columns=columns(value.shape[1])), sofar)
+
+    if story is None:
+        product()
+    else:
+        pl.when(lax.axis_index("story") == story)(product)
+
+
+def step_kernel(columns, story, piece, rows, sofar, terms, out):
     first, latest = terms
 
     @pl.when(lax.axis_index("story") == story)
     def _():
-        store_rows(out, times_rows(joined(pieces), *rows))
+        value = piece[0][...]
+        value = plus(times_rows(value, *rows, columns=columns(value.shape[1])), sofar)
+        store_rows(out, value)
         out[...] = first[...] - out[...]
 
     @pl.when(lax.axis_index("story") != story)
@@ -274,33 +301,53 @@
         out[...] = latest[...]
 
 
+def end_kernel(columns, piece, rows, sofar, out):
+    value = piece[0][...]
+    store_rows(out, plus(times_rows(value, *rows, columns=columns(value.shape[1])), sofar))
+
+
 def rows_kernel(pieces, rows, out):
     store_rows(out, times_rows(joined(pieces), *rows))
 
 
-def coupled_kernel(load, early, here, even, odd, above, below, out):
+def coupled_kernel(columns, final, load, early, pieces, sofar, above, below, out):
+    here, lower = pieces
     story = lax.axis_index("story")
+    width = here.shape[1]
+
+    def finish(value, *terms):
+        if not final:
+            out[...] = value
+            return
+        store_rows(out, value)
+        total = by_core(load[0][...], load[1][...], 1) - out[...]
+        for term in terms:
+            total = total - term[...]
+        out[...] = total
 
     @pl.when(story == 0)
     def _():
-        store_rows(out, times_rows(joined(here), *above))
-        out[...] = by_core(load[0][...], load[1][...], 1) - out[...]
+        finish(plus(times_rows(here[...], *above, columns=columns(width)), sofar))
 
     @pl.when(story > 0)
     def _():
-        use = lax.rem(story, 2) == 1
-        refs = [jnp.where(use, e[...], o[...]) for e, o in zip(even, odd)]
-        own = lax.axis_index("rec") if len(refs) > 1 else 0
-        value = jnp.concatenate(in_order(refs, own), axis=1)
-        store_rows(out, times_rows(value, *below))
-        out[...] = by_core(load[0][...], load[1][...], 1) - early[0][...] - out[...]
-
-
-def last_kernel(pieces, rows, mine, theirs):
-    value = times_rows(joined(pieces), *rows)
+        finish(plus(times_rows(lower[...], *below, columns=columns(width)), sofar), *early)
+
+
+def last_kernel(columns, piece, rows, sofar, mine, theirs):
+    value = piece[0][...]
+    value = plus(times_rows(value, *rows, columns=columns(value.shape[1])), sofar)
     half = value.shape[1] // 2
     mine[...] = value[:, :half]
     theirs[...] = value[:, half:]
+
+
+def partial_sums(story, shape, pieces, rows):
+    sofar = []
+    for j, piece in enumerate(pieces[:-1]):
+        kernel = functools.partial(part_kernel, from_chip(len(pieces), j), story)
+        sofar = call(kernel, shape, [piece], rows, sofar, cost=4 << 20)
+    return [pieces[-1]], rows, sofar
 
 
 class Moves:
@@ -358,15 +405,17 @@
     def pieces(self, pieces):
         return pieces if pieces[0].shape[1] % 128 == 0 else [self.by_chip(pieces)]
 
-    def below(self, value, j):
+    def shift(self, value, step, j):
         pairs = []
-        for s in range(1, self.stories):
+        for s in range(self.stories):
+            if not 0 <= s + step < self.stories:
+                continue
             for r in range(self.chips):
                 for b in range(self.cores):
                     pairs.append(
                         (
                             (s * self.chips + r) * self.cores + b,
-                            ((s - 1) * self.chips + (r ^ j)) * self.cores + b,
+                            ((s + step) * self.chips + (r ^ j)) * self.cores + b,
                         )
                     )
         return lax.ppermute(value, AXES, pairs)
@@ -410,9 +459,6 @@
         [record_ids.reshape(1, records), ground_table.reshape(1, library), mass_int, pattern_int]
         + cube_int,
     )
-    mine_face, theirs_face = fetched(
-        load_face_kernel, [(half, own_face)] * 2, [mass_face, pattern_face] + cube_face, ground
-    )
     rows_int, rows_face = 2 * own_int, 2 * own_face
     faces = couple_above.shape[2]
 
@@ -421,13 +467,10 @@
 
     lower_other = mv.core(lower[0])
     across = [mv.chip(load_int, j) for j in range(1, mv.chips)]
-    load_face_half = [mine_face, mv.core(theirs_face)]
     phase_rows = staged(
-        interior_inverse[0], couple_above[0], couple_below[0], after=[theirs_face]
-    )
-    phase_rows, load_face_half[1], *across = lax.optimization_barrier(
-        [phase_rows, load_face_half[1], *across]
-    )
+        interior_inverse[0], couple_above[0], couple_below[0], after=[load_int]
+    )
+    phase_rows, *across = lax.optimization_barrier([phase_rows, *across])
     beside = [mv.core(piece) for piece in [load_int] + across]
     pieces = [piece for pair in zip([load_int] + across, beside) for piece in pair]
     aligned = load_int.shape[1] % 128 == 0
@@ -438,16 +481,22 @@
     mine, theirs = call(
         functools.partial(forces_kernel, aligned), [(2, half, faces)] * 2, pieces, [phase_rows]
     )
-    mine_int, theirs_int = call(records_kernel, [(half, own_int)] * 2, [load_int])
-    load_int_half = [mine_int, mv.core(theirs_int)]
     chunks = call(
         chunks_kernel,
         [(half, faces // mv.chips)] * (2 * mv.chips),
         [mine, mv.core(theirs)],
     )
-    forces = [mv.below(chunks[mv.chips], 0)]
+    ground, _ = lax.optimization_barrier([ground, chunks[0]])
+    mine_face, theirs_face = fetched(
+        load_face_kernel, [(half, own_face)] * 2, [mass_face, pattern_face] + cube_face, ground
+    )
+    load_late, _ = lax.optimization_barrier([load_int, chunks[0]])
+    mine_int, theirs_int = call(records_kernel, [(half, own_int)] * 2, [load_late])
+    halves = lax.optimization_barrier([mv.core(theirs_face), mv.core(theirs_int)])
+    load_face_half, load_int_half = [mine_face, halves[0]], [mine_int, halves[1]]
+    forces = [mv.shift(chunks[mv.chips], -1, 0)]
     for j in range(1, mv.chips):
-        forces += [mv.chip(chunks[j], j), mv.below(chunks[mv.chips + j], j)]
+        forces += [mv.chip(chunks[j], j), mv.shift(chunks[mv.chips + j], -1, j)]
     shape = [(half, rows_face)]
     (condensed,) = call(condensed_kernel, shape, load_face_half, [chunks[0]] + forces)
 
@@ -456,32 +505,35 @@
     for k in range(1, mv.stories):
         came = mv.gather_story(forward, (k - 1) % 2)
         if k == min(2, mv.stories - 1):
-            *came, pivot_other = lax.optimization_barrier([*came, pivot_other])
-            upper_other = others(upper[0], [forward])
+            upper_other = others(upper[0], [pivot_other, forward])
+            came[-1], pivot_other = lax.optimization_barrier([came[-1], pivot_other])
         if k == mv.stories - 1:
-            *came, upper_other = lax.optimization_barrier([*came, upper_other])
-            above_other = others(couple_above[0], [upper_other])
+            above_other = others(couple_above[0], [upper_other, forward])
+            came[-1], upper_other = lax.optimization_barrier([came[-1], upper_other])
         (forward,) = call(
-            functools.partial(step_kernel, k),
+            functools.partial(step_kernel, from_chip(len(came), len(came) - 1), k),
             shape,
-            came,
-            [lower[0], lower_other],
+            *partial_sums(k, shape, came, [lower[0], lower_other]),
             [condensed, forward],
         )
-    (pivoted,) = call(rows_kernel, shape, mv.gather_chips(forward), [pivot[0], pivot_other])
+    came = mv.gather_chips(forward)
+    (pivoted,) = call(
+        functools.partial(end_kernel, from_chip(len(came), len(came) - 1)),
+        shape,
+        *partial_sums(None, shape, came, [pivot[0], pivot_other]),
+    )
 
     shape_int = [(half, rows_int)]
     face = pivoted
     for k in range(mv.stories - 2, -1, -1):
         came = mv.gather_story(face, k % 2)
         if k == mv.stories - 2:
-            *came, above_other = lax.optimization_barrier([*came, above_other])
-            below_other = others(couple_below[0], [above_other])
+            below_other = others(couple_below[0], [above_other, face])
+            came[-1], above_other = lax.optimization_barrier([came[-1], above_other])
         if k == max(mv.stories - 3, 0):
-            *came, below_other = lax.optimization_barrier([*came, below_other])
-            inverse_other = others(interior_inverse[0], [below_other])
+            inverse_other = others(interior_inverse[0], [below_other, face])
+            came[-1], below_other = lax.optimization_barrier([came[-1], below_other])
         if k == 0:
-            odd = mv.gather_story(face, 1)
             (early,) = call(
                 rows_kernel,
                 shape_int,
@@ -489,36 +541,43 @@
                 [couple_above[0], above_other],
                 cost=8 << 20,
             )
-            *came, early = lax.optimization_barrier([*came, early])
+            came[-1], early = lax.optimization_barrier([came[-1], early])
         (face,) = call(
-            functools.partial(step_kernel, k),
+            functools.partial(step_kernel, from_chip(len(came), len(came) - 1), k),
             shape,
-            came,
-            [upper[0], upper_other],
+            *partial_sums(k, shape, came, [upper[0], upper_other]),
             [pivoted, face],
         )
 
-    even = mv.gather_story(face, 0)
-    *even, inverse_other = lax.optimization_barrier([*even, inverse_other])
-    (reduced,) = call(
-        coupled_kernel,
-        shape_int,
-        load_int_half,
-        [early],
-        mv.gather_chips(face),
-        even,
-        odd,
-        [couple_above[0], above_other],
-        [couple_below[0], below_other],
-    )
+    came = mv.pieces([mv.shift(face, 1, j) for j in range(mv.chips)])
+    came[-1], inverse_other = lax.optimization_barrier([came[-1], inverse_other])
+    pairs = list(zip(mv.gather_chips(face), came))
+    sofar = []
+    for j, pair in enumerate(pairs):
+        final = j == len(pairs) - 1
+        sofar = call(
+            functools.partial(coupled_kernel, from_chip(len(pairs), j), final),
+            shape_int,
+            load_int_half if final else [],
+            [early] if final else [],
+            list(pair),
+            sofar,
+            [couple_above[0], above_other],
+            [couple_below[0], below_other],
+            cost=4 << 20,
+        )
+    (reduced,) = sofar
+
     mine, theirs = call(halves_kernel, [(half, own_face)] * 2, [face])
     new_face = call(
         outputs_kernel, [(records, own_face)] * 3, [mine, mv.core(theirs)], cube_face
     )
     came = mv.gather_chips(reduced)
-    *came, f0, f1, f2 = lax.optimization_barrier([*came, *new_face])
+    came[-1], f0, f1, f2 = lax.optimization_barrier([came[-1], *new_face])
     mine, theirs = call(
-        last_kernel, [(half, own_int)] * 2, came, [interior_inverse[0], inverse_other]
+        functools.partial(last_kernel, from_chip(len(came), len(came) - 1)),
+        [(half, own_int)] * 2,
+        *partial_sums(None, shape_int, came, [interior_inverse[0], inverse_other]),
     )
     new_int = call(
         outputs_kernel, [(records, own_int)] * 3, [mine, mv.core(theirs)], cube_int

time: 110 us -> 102 us (0.927)
  waiting for transfers between devices: 51.8 us -> 44.1 us
    ppermute x35 -> x31, starting transfers between devices: 33.2 us -> 28.2 us  [permute(): return lax.ppermute(value, AXES, pairs)]
    ppermute x2 -> x4, starting transfers between devices: 2.7 us -> 7.61 us  [shift(): return lax.ppermute(value, AXES, pairs)]
    ppermute x35 -> x31, waiting for transfers between devices: 44.6 us -> 40.6 us  [permute(): return lax.ppermute(value, AXES, pairs)]
    ppermute x2 -> x4, waiting for transfers between devices: 7.13 us -> 3.51 us  [shift(): return lax.ppermute(value, AXES, pairs)]
    pallas_call x17 -> x26, Pallas kernels: 14.1 us -> 14.3 us  [call(): pl.pallas_call(body, in_specs=[VMEM] * len(flat), out_specs=[VMEM] * len(...]
  transfers between devices with their start and end apart: 37 -> 35, of which waited for: 26 -> 22; matrix products, arithmetic and copies ran while one was open for 0% -> 0% of each run, Pallas kernels for 14% -> 13%
where the time goes in v7:
time: 102 us
  waiting for transfers between devices  44.1 us (43%)
  starting transfers between devices  35.8 us (35%)
  Pallas kernels  20.9 us (20%)
    ppermute x31, waiting for transfers between devices, permute(): return lax.ppermute(value, AXES, pairs)  40.6 us
    ppermute x31, starting transfers between devices, permute(): return lax.ppermute(value, AXES, pairs)  28.2 us
    pallas_call x26, Pallas kernels, call(): pl.pallas_call(body, in_specs=[VMEM] * len(flat), out_specs=[VMEM] * len(...  14.3 us
    ppermute x4, starting transfers between devices, shift(): return lax.ppermute(value, AXES, pairs)  7.61 us
    pallas_call x1, Pallas kernels, staged(): pl.pallas_call(body, in_specs=[pl.BlockSpec(memory_space=pltpu.HBM)] * co...  4.08 us
    ppermute x4, waiting for transfers between devices, shift(): return lax.ppermute(value, AXES, pairs)  3.51 us
    pallas_call x2, Pallas kernels, fetched(): pl.pallas_call(body, in_specs=[pl.BlockSpec(memory_space=pltpu.HBM)] * co...  2.48 us
  transfers between devices with their start and end apart: 35, of which 22 were waited for; matrix products, arithmetic and copies ran while one was open for 0% of the time, Pallas kernels for 13%

profile of v7, /device:TPU:0, one launch (start us, length us, event | category | flops | bytes accessed | tf_op | source)
XLA Modules:
  0.0 102.1 jit_solution(15545042112741513510)
XLA Ops:
  0.6 1.3 %shard_map.217 = (f32[64,512]{1,0:T(8,128)S(1)}, f32[64,128]{1,0:T(8,128)S(1)}) custom-call(s32[1,64]{1,0:T(1,128)} %bitcast.87, f32[1,512]{1,0:T(1,128)} %bitcast.86, f32[1,512]{1,0:T(1,128)} %refs_2_.1, f32[1,512]{1,0:T(1,128)} %refs_3_.1, f32[64,512]{1,0:T(8,128)} %bitcast.74, f32[64,512]{1,0:T(8,128)} %bitcast.76, f32[64,512]{1,0:T(8,128)} %bitcast.78), custom_call_target="tpu_custom_call" | custom-call | tf_op jit(solution)/shard_map/pallas_call | solution.py:180
  2.0 3.0 %collective-permute-start.1 = (f32[64,512]{1,0:T(8,128)S(1)}, f32[64,512]{1,0:T(8,128)S(1)}, u32[]{:S(2)}, u32[]{:S(2)}) collective-permute-start(f32[64,512]{1,0:T(8,128)S(1)} %get-tuple-element.67.refs_0_), channel_id=1, source_target_pairs={{0,2},{1,3},{2,0},{3,1},{4,6},{5,7},{6,4},{7,5},{8,10},{9,11},{10,... | collective-permute-start | bytes 393224 | tf_op jit(solution)/shard_map/ppermute | solution.py:375
  5.0 4.1 %shard_map.218.refs_4_ = f32[512,5120]{1,0:T(8,128)S(1)} custom-call(f32[512,2048]{1,0:T(8,128)} %bitcast.63, f32[512,1536]{1,0:T(8,128)} %bitcast.58, f32[512,1536]{1,0:T(8,128)} %bitcast.67), custom_call_target="tpu_custom_call" | custom-call | tf_op jit(solution)/shard_map/pallas_call | solution.py:128
  9.7 1.0 collective-permute-done.2.refs_3_
  10.7 2.5 %shard_map.219 = (f32[2,32,1536]{2,1,0:T(8,128)S(1)}, f32[2,32,1536]{2,1,0:T(8,128)S(1)}) custom-call(f32[64,512]{1,0:T(8,128)S(1)} %get-tuple-element.67.refs_0_, f32[64,512]{1,0:T(8,128)S(1)} %collective-permute-done.refs_1_, f32[64,512]{1,0:T(8,128)S(1)} %collective-permute-done.1.refs_2_, f32[64,512]{1,0:T(8,128)S(1)} %collective-permute-done.2.refs_3_, ...), custom_call_target="tpu_custom_call" | custom-call | tf_op jit(solution)/shard_map/pallas_call | solution.py:91
  13.6 1.4 %collective-permute-done.3.refs_1_ = f32[2,32,1536]{2,1,0:T(8,128)S(1)} collective-permute-done((f32[2,32,1536]{2,1,0:T(8,128)S(1)}, f32[2,32,1536]{2,1,0:T(8,128)S(1)}, u32[]{:S(2)}, u32[]{:S(2)}) %collective-permute-start.3) | collective-permute-done | bytes 393248 | tf_op jit(solution)/shard_map/ppermute | solution.py:375
  15.0 1.3 %collective-permute-start.6 = (f32[32,768]{1,0:T(8,128)S(1)}, f32[32,768]{1,0:T(8,128)S(1)}, u32[]{:S(2)}, u32[]{:S(2)}) collective-permute-start(f32[32,768]{1,0:T(8,128)S(1)} %get-tuple-element.76), channel_id=1, source_target_pairs={{4,0},{5,1},{6,2},{7,3},{8,4},{9,5},{10,6},{11,7},{12,8},{13,9},{1... | collective-permute-start | bytes 294920 | tf_op jit(solution)/shard_map/ppermute | solution.py:421
  16.3 1.0 collective-permute-start.7
  17.3 1.3 %collective-permute-start.8 = (f32[32,768]{1,0:T(8,128)S(1)}, f32[32,768]{1,0:T(8,128)S(1)}, u32[]{:S(2)}, u32[]{:S(2)}) collective-permute-start(f32[32,768]{1,0:T(8,128)S(1)} %get-tuple-element.78), channel_id=1, source_target_pairs={{4,2},{5,3},{6,0},{7,1},{8,6},{9,7},{10,4},{11,5},{12,10},{13,11},... | collective-permute-start | bytes 294920 | tf_op jit(solution)/shard_map/ppermute | solution.py:421
  18.7 1.2 %shard_map.222 = (f32[32,384]{1,0:T(8,128)S(1)}, f32[32,384]{1,0:T(8,128)S(1)}) custom-call(f32[1,384]{1,0:T(1,128)} %refs_0_.1, f32[1,384]{1,0:T(1,128)} %refs_1_.1, f32[64,384]{1,0:T(8,128)} %bitcast.80, f32[64,384]{1,0:T(8,128)} %bitcast.82, f32[64,384]{1,0:T(8,128)} %bitcast.84, f32[64,128]{1,0:T(8,128)S(1)} %get-tuple-element.70.refs_5_), custom_call_target="tpu_custom_call" | custom-call | tf_op jit(solution)/shard_map/pallas_call | solution.py:180
  20.4 0.9 collective-permute-done.4.refs_1_
  22.0 3.2 %collective-permute-done.8.refs_5_ = f32[32,768]{1,0:T(8,128)S(1)} collective-permute-done((f32[32,768]{1,0:T(8,128)S(1)}, f32[32,768]{1,0:T(8,128)S(1)}, u32[]{:S(2)}, u32[]{:S(2)}) %collective-permute-start.8) | collective-permute-done | bytes 98336 | tf_op jit(solution)/shard_map/ppermute | solution.py:421
  25.3 2.3 %collective-permute-start.11 = (f32[32,768]{1,0:T(8,128)S(1)}, f32[32,768]{1,0:T(8,128)S(1)}, u32[]{:S(2)}, u32[]{:S(2)}) collective-permute-start(f32[32,768]{1,0:T(8,128)S(1)} %shard_map.223.refs_4_.refs_5_), channel_id=1, source_target_pairs={{0,4},{1,5},{2,6},{3,7},{4,0},{5,1},{6,2},{7,3},{8,12},{9,13},{10,... | collective-permute-start | bytes 294920 | tf_op jit(solution)/shard_map/ppermute | solution.py:375
  28.2 2.7 %collective-permute-done.11.refs_0_ = f32[32,768]{1,0:T(8,128)S(1)} collective-permute-done((f32[32,768]{1,0:T(8,128)S(1)}, f32[32,768]{1,0:T(8,128)S(1)}, u32[]{:S(2)}, u32[]{:S(2)}) %collective-permute-start.11) | collective-permute-done | bytes 98336 | tf_op jit(solution)/shard_map/ppermute | solution.py:375
  30.9 2.7 %collective-permute-done.9.refs_0_ = f32[32,768]{1,0:T(8,128)S(1)} collective-permute-done((f32[32,768]{1,0:T(8,128)S(1)}, f32[32,768]{1,0:T(8,128)S(1)}, u32[]{:S(2)}, u32[]{:S(2)}) %collective-permute-start.9) | collective-permute-done | bytes 98336 | tf_op jit(solution)/shard_map/ppermute | solution.py:375
  33.7 1.0 collective-permute-start.14
  34.7 1.1 %collective-permute-start.12 = (f32[32,768]{1,0:T(8,128)S(1)}, f32[32,768]{1,0:T(8,128)S(1)}, u32[]{:S(2)}, u32[]{:S(2)}) collective-permute-start(f32[32,768]{1,0:T(8,128)S(1)} %shard_map.225.refs_5_), channel_id=1, source_target_pairs={{0,2},{1,3},{2,0},{3,1},{4,10},{5,11},{6,8},{7,9},{8,6},{9,7},{10,... | collective-permute-start | bytes 294920 | tf_op jit(solution)/shard_map/ppermute | solution.py:375
  35.8 3.6 %collective-permute-done.14.refs_0_ = f32[32,768]{1,0:T(8,128)S(1)} collective-permute-done((f32[32,768]{1,0:T(8,128)S(1)}, f32[32,768]{1,0:T(8,128)S(1)}, u32[]{:S(2)}, u32[]{:S(2)}) %collective-permute-start.14) | collective-permute-done | bytes 98336 | tf_op jit(solution)/shard_map/ppermute | solution.py:375
  39.4 1.7 %collective-permute-done.12.refs_0_ = f32[32,768]{1,0:T(8,128)S(1)} collective-permute-done((f32[32,768]{1,0:T(8,128)S(1)}, f32[32,768]{1,0:T(8,128)S(1)}, u32[]{:S(2)}, u32[]{:S(2)}) %collective-permute-start.12) | collective-permute-done | bytes 98336 | tf_op jit(solution)/shard_map/ppermute | solution.py:375
  41.3 2.9 %collective-permute-start.17 = (f32[32,768]{1,0:T(8,128)S(1)}, f32[32,768]{1,0:T(8,128)S(1)}, u32[]{:S(2)}, u32[]{:S(2)}) collective-permute-start(f32[32,768]{1,0:T(8,128)S(1)} %shard_map.227.refs_5_), channel_id=1, source_target_pairs={{0,4},{1,5},{2,6},{3,7},{4,0},{5,1},{6,2},{7,3},{8,12},{9,13},{10,... | collective-permute-start | bytes 294920 | tf_op jit(solution)/shard_map/ppermute | solution.py:375
  44.8 2.7 %collective-permute-done.17.refs_0_ = f32[32,768]{1,0:T(8,128)S(1)} collective-permute-done((f32[32,768]{1,0:T(8,128)S(1)}, f32[32,768]{1,0:T(8,128)S(1)}, u32[]{:S(2)}, u32[]{:S(2)}) %collective-permute-start.17) | collective-permute-done | bytes 98336 | tf_op jit(solution)/shard_map/ppermute | solution.py:375
  47.5 2.7 %collective-permute-done.15.refs_0_ = f32[32,768]{1,0:T(8,128)S(1)} collective-permute-done((f32[32,768]{1,0:T(8,128)S(1)}, f32[32,768]{1,0:T(8,128)S(1)}, u32[]{:S(2)}, u32[]{:S(2)}) %collective-permute-start.15) | collective-permute-done | bytes 98336 | tf_op jit(solution)/shard_map/ppermute | solution.py:375
  50.2 1.0 collective-permute-start.18
  52.0 2.9 %collective-permute-done.18.refs_0_ = f32[32,768]{1,0:T(8,128)S(1)} collective-permute-done((f32[32,768]{1,0:T(8,128)S(1)}, f32[32,768]{1,0:T(8,128)S(1)}, u32[]{:S(2)}, u32[]{:S(2)}) %collective-permute-start.18) | collective-permute-done | bytes 98336 | tf_op jit(solution)/shard_map/ppermute | solution.py:375
  55.8 1.8 %collective-permute-start.21 = (f32[32,768]{1,0:T(8,128)S(1)}, f32[32,768]{1,0:T(8,128)S(1)}, u32[]{:S(2)}, u32[]{:S(2)}) collective-permute-start(f32[32,768]{1,0:T(8,128)S(1)} %shard_map.231.refs_4_.refs_5_), channel_id=1, source_target_pairs={{0,4},{1,5},{2,6},{3,7},{4,0},{5,1},{6,2},{7,3},{8,12},{9,13},{10,... | collective-permute-start | bytes 294920 | tf_op jit(solution)/shard_map/ppermute | solution.py:375
  58.2 3.1 %collective-permute-done.21.refs_0_ = f32[32,768]{1,0:T(8,128)S(1)} collective-permute-done((f32[32,768]{1,0:T(8,128)S(1)}, f32[32,768]{1,0:T(8,128)S(1)}, u32[]{:S(2)}, u32[]{:S(2)}) %collective-permute-start.21) | collective-permute-done | bytes 98336 | tf_op jit(solution)/shard_map/ppermute | solution.py:375
  61.3 2.2 %collective-permute-done.19.refs_0_ = f32[32,768]{1,0:T(8,128)S(1)} collective-permute-done((f32[32,768]{1,0:T(8,128)S(1)}, f32[32,768]{1,0:T(8,128)S(1)}, u32[]{:S(2)}, u32[]{:S(2)}) %collective-permute-start.19) | collective-permute-done | bytes 98336 | tf_op jit(solution)/shard_map/ppermute | solution.py:375
  63.6 1.2 %collective-permute-start.24 = (f32[32,768]{1,0:T(8,128)S(1)}, f32[32,768]{1,0:T(8,128)S(1)}, u32[]{:S(2)}, u32[]{:S(2)}) collective-permute-start(f32[32,768]{1,0:T(8,128)S(1)} %shard_map.233.refs_5_), channel_id=1, source_target_pairs={{0,2},{1,3},{2,0},{3,1},{4,8},{5,9},{6,10},{7,11},{8,4},{9,5},{10,... | collective-permute-start | bytes 294920 | tf_op jit(solution)/shard_map/ppermute | solution.py:375
  64.8 0.9 collective-permute-start.22
  65.7 3.6 %collective-permute-done.24.refs_0_ = f32[32,768]{1,0:T(8,128)S(1)} collective-permute-done((f32[32,768]{1,0:T(8,128)S(1)}, f32[32,768]{1,0:T(8,128)S(1)}, u32[]{:S(2)}, u32[]{:S(2)}) %collective-permute-start.24) | collective-permute-done | bytes 98336 | tf_op jit(solution)/shard_map/ppermute | solution.py:375
  69.2 1.7 %collective-permute-done.22.refs_0_ = f32[32,768]{1,0:T(8,128)S(1)} collective-permute-done((f32[32,768]{1,0:T(8,128)S(1)}, f32[32,768]{1,0:T(8,128)S(1)}, u32[]{:S(2)}, u32[]{:S(2)}) %collective-permute-start.22) | collective-permute-done | bytes 98336 | tf_op jit(solution)/shard_map/ppermute | solution.py:375
  70.9 1.2 %collective-permute-start.26 = (f32[32,768]{1,0:T(8,128)S(1)}, f32[32,768]{1,0:T(8,128)S(1)}, u32[]{:S(2)}, u32[]{:S(2)}) collective-permute-start(f32[32,768]{1,0:T(8,128)S(1)} %shard_map.235.refs_0_.refs_5_), channel_id=1, source_target_pairs={{0,2},{1,3},{2,0},{3,1},{4,6},{5,7},{6,4},{7,5},{8,10},{9,11},{10,... | collective-permute-start | bytes 294920 | tf_op jit(solution)/shard_map/ppermute | solution.py:375
  72.1 4.3 %collective-permute-start.25 = (f32[32,768]{1,0:T(8,128)S(1)}, f32[32,768]{1,0:T(8,128)S(1)}, u32[]{:S(2)}, u32[]{:S(2)}) collective-permute-start(f32[32,768]{1,0:T(8,128)S(1)} %shard_map.235.refs_0_.refs_5_), channel_id=1, source_target_pairs={{0,6},{1,7},{2,4},{3,5},{4,2},{5,3},{6,0},{7,1},{8,14},{9,15},{10,... | collective-permute-start | bytes 294920 | tf_op jit(solution)/shard_map/ppermute | solution.py:375
  76.5 2.0 %shard_map.236.refs_2_ = f32[32,1024]{1,0:T(8,128)S(1)} custom-call(f32[32,768]{1,0:T(8,128)S(1)} %shard_map.235.refs_0_.refs_5_, f32[32,768]{1,0:T(8,128)S(1)} %collective-permute-done.26.refs_1_, f32[512,1536]{1,0:T(8,128)S(1)} %bitcast.60, f32[512,1536]{1,0:T(8,128)S(1)} %collective-permute-done.20.refs_3_.refs_7_), custom_call_target="tpu_custom_call" | custom-call | bytes 8388608 | tf_op jit(solution)/shard_map/pallas_call | solution.py:91
  78.5 1.3 %collective-permute-done.25.refs_0_ = f32[32,768]{1,0:T(8,128)S(1)} collective-permute-done((f32[32,768]{1,0:T(8,128)S(1)}, f32[32,768]{1,0:T(8,128)S(1)}, u32[]{:S(2)}, u32[]{:S(2)}) %collective-permute-start.25) | collective-permute-done | bytes 98336 | tf_op jit(solution)/shard_map/ppermute | solution.py:375
  79.8 1.3 %collective-permute-done.27.refs_0_ = f32[32,768]{1,0:T(8,128)S(1)} collective-permute-done((f32[32,768]{1,0:T(8,128)S(1)}, f32[32,768]{1,0:T(8,128)S(1)}, u32[]{:S(2)}, u32[]{:S(2)}) %collective-permute-start.27) | collective-permute-done | bytes 98336 | tf_op jit(solution)/shard_map/ppermute | solution.py:375
  81.9 0.9 shard_map.238.refs_0_
  82.8 2.0 %collective-permute-start.31 = (f32[32,768]{1,0:T(8,128)S(1)}, f32[32,768]{1,0:T(8,128)S(1)}, u32[]{:S(2)}, u32[]{:S(2)}) collective-permute-start(f32[32,768]{1,0:T(8,128)S(1)} %shard_map.238.refs_0_), channel_id=1, source_target_pairs={{0,4},{1,5},{2,6},{3,7},{4,8},{5,9},{6,10},{7,11},{8,12},{9,13},{1... | collective-permute-start | bytes 294920 | tf_op jit(solution)/shard_map/ppermute | solution.py:421
  84.8 3.0 %collective-permute-start.29 = (f32[32,768]{1,0:T(8,128)S(1)}, f32[32,768]{1,0:T(8,128)S(1)}, u32[]{:S(2)}, u32[]{:S(2)}) collective-permute-start(f32[32,768]{1,0:T(8,128)S(1)} %shard_map.238.refs_0_), channel_id=1, source_target_pairs={{0,6},{1,7},{2,4},{3,5},{4,10},{5,11},{6,8},{7,9},{8,14},{9,15},{1... | collective-permute-start | bytes 294920 | tf_op jit(solution)/shard_map/ppermute | solution.py:421
  87.8 1.2 %collective-permute-start.28 = (f32[32,768]{1,0:T(8,128)S(1)}, f32[32,768]{1,0:T(8,128)S(1)}, u32[]{:S(2)}, u32[]{:S(2)}) collective-permute-start(f32[32,768]{1,0:T(8,128)S(1)} %shard_map.238.refs_0_), channel_id=1, source_target_pairs={{0,2},{1,3},{2,0},{3,1},{4,6},{5,7},{6,4},{7,5},{8,10},{9,11},{10,... | collective-permute-start | bytes 294920 | tf_op jit(solution)/shard_map/ppermute | solution.py:375
  89.0 1.0 %shard_map.239.refs_5_ = f32[32,1024]{1,0:T(8,128)S(1)} custom-call(f32[32,768]{1,0:T(8,128)S(1)} %shard_map.238.refs_0_, f32[32,768]{1,0:T(8,128)S(1)} %collective-permute-done.31.refs_1_, f32[512,1536]{1,0:T(8,128)S(1)} %bitcast.61, f32[512,1536]{1,0:T(8,128)S(1)} %collective-permute-done.20.refs_3_.refs_7_, f32[512,1536]{1,0:T(8,128)S(1)} %bitcast.69, ...), custom_call_target="tpu_custom_call" | custom-call | bytes 4194304 | tf_op jit(solution)/shard_map/pallas_call | solution.py:91
  90.1 2.4 %collective-permute-done.28.refs_3_ = f32[32,768]{1,0:T(8,128)S(1)} collective-permute-done((f32[32,768]{1,0:T(8,128)S(1)}, f32[32,768]{1,0:T(8,128)S(1)}, u32[]{:S(2)}, u32[]{:S(2)}) %collective-permute-start.28) | collective-permute-done | bytes 98336 | tf_op jit(solution)/shard_map/ppermute | solution.py:375
  92.5 1.1 %shard_map.240.refs_0_ = f32[32,1024]{1,0:T(8,128)S(1)} custom-call(f32[32,512]{1,0:T(8,128)S(1)} %get-tuple-element.68.refs_0_, f32[32,512]{1,0:T(8,128)S(1)} %collective-permute-done.5.refs_1_, f32[32,1024]{1,0:T(8,128)S(1)} %shard_map.236.refs_2_, f32[32,768]{1,0:T(8,128)S(1)} %collective-permute-done.28.refs_3_, ...), custom_call_target="tpu_custom_call" | custom-call | bytes 4194304 | tf_op jit(solution)/shard_map/pallas_call | solution.py:91
  93.6 1.2 %collective-permute-start.32 = (f32[32,1024]{1,0:T(8,128)S(1)}, f32[32,1024]{1,0:T(8,128)S(1)}, u32[]{:S(2)}, u32[]{:S(2)}) collective-permute-start(f32[32,1024]{1,0:T(8,128)S(1)} %shard_map.240.refs_0_), channel_id=1, source_target_pairs={{0,2},{1,3},{2,0},{3,1},{4,6},{5,7},{6,4},{7,5},{8,10},{9,11},{10,... | collective-permute-start | bytes 393224 | tf_op jit(solution)/shard_map/ppermute | solution.py:375
  94.9 1.2 %collective-permute-done.33.refs_1_ = f32[32,384]{1,0:T(8,128)S(1)} collective-permute-done((f32[32,384]{1,0:T(8,128)S(1)}, f32[32,384]{1,0:T(8,128)S(1)}, u32[]{:S(2)}, u32[]{:S(2)}) %collective-permute-start.33) | collective-permute-done | bytes 49184 | tf_op jit(solution)/shard_map/ppermute | solution.py:375
  96.8 1.4 %shard_map.243.refs_3_ = f32[32,1024]{1,0:T(8,128)S(1)} custom-call(f32[32,1024]{1,0:T(8,128)S(1)} %shard_map.240.refs_0_, f32[512,2048]{1,0:T(8,128)S(1)} %bitcast.65, f32[512,2048]{1,0:T(8,128)S(1)} %collective-permute-done.30.refs_2_), custom_call_target="tpu_custom_call" | custom-call | bytes 4194304 | tf_op jit(solution)/shard_map/pallas_call | solution.py:91
  98.6 1.3 %shard_map.244 = (f32[32,512]{1,0:T(8,128)S(1)}, f32[32,512]{1,0:T(8,128)S(1)}) custom-call(f32[32,1024]{1,0:T(8,128)S(1)} %collective-permute-done.32.refs_0_, f32[512,2048]{1,0:T(8,128)S(1)} %bitcast.66, f32[512,2048]{1,0:T(8,128)S(1)} %collective-permute-done.30.refs_2_, f32[32,1024]{1,0:T(8,128)S(1)} %shard_map.243.refs_3_), custom_call_target="tpu_custom_call" | custom-call | tf_op jit(solution)/shard_map/pallas_call | solution.py:91
  100.1 1.2 %collective-permute-done.34.refs_1_ = f32[32,512]{1,0:T(8,128)S(1)} collective-permute-done((f32[32,512]{1,0:T(8,128)S(1)}, f32[32,512]{1,0:T(8,128)S(1)}, u32[]{:S(2)}, u32[]{:S(2)}) %collective-permute-start.34) | collective-permute-done | bytes 65568 | tf_op jit(solution)/shard_map/ppermute | solution.py:375
  (75 shorter events, 9.5 us)
Async XLA Ops:
  2.0 7.1 %collective-permute-start.1 = (f32[64,512]{1,0:T(8,128)S(1)}, f32[64,512]{1,0:T(8,128)S(1)}, u32[]{:S(2)}, u32[]{:S(2)}) collective-permute-start(f32[64,512]{1,0:T(8,128)S(1)} %get-tuple-element.67.refs_0_), channel_id=1, source_target_pairs={{0,2},{1,3},{2,0},{3,1},{4,6},{5,7},{6,4},{7,5},{8,10},{9,11},{10,... | collective-permute-start | bytes 393224 | tf_op jit(solution)/shard_map/ppermute | solution.py:375
  5.0 4.7 %collective-permute-start = (f32[64,512]{1,0:T(8,128)S(1)}, f32[64,512]{1,0:T(8,128)S(1)}, u32[]{:S(2)}, u32[]{:S(2)}) collective-permute-start(f32[64,512]{1,0:T(8,128)S(1)} %get-tuple-element.67.refs_0_), channel_id=1, source_target_pairs={{0,1},{1,0},{2,3},{3,2},{4,5},{5,4},{6,7},{7,6},{8,9},{9,8},{10,11... | collective-permute-start | bytes 393224 | tf_op jit(solution)/shard_map/ppermute | solution.py:375
  9.1 12.2 %copy-start = (f32[1,384,1536]{2,1,0:T(8,128)S(1)}, f32[1,384,1536]{2,1,0:T(8,128)}, u32[]{:S(2)}) copy-start(f32[1,384,1536]{2,1,0:T(8,128)} %param.33) | copy-start | bytes 7077892
  9.1 16.1 %copy-start.5 = (f32[1,384,1536]{2,1,0:T(8,128)S(1)}, f32[1,384,1536]{2,1,0:T(8,128)}, u32[]{:S(2)}) copy-start(f32[1,384,1536]{2,1,0:T(8,128)} %param.34) | copy-start | bytes 7077892
  9.1 1.6 %collective-permute-start.2 = (f32[64,512]{1,0:T(8,128)S(1)}, f32[64,512]{1,0:T(8,128)S(1)}, u32[]{:S(2)}, u32[]{:S(2)}) collective-permute-start(f32[64,512]{1,0:T(8,128)S(1)} %collective-permute-done.1.refs_2_), channel_id=1, source_target_pairs={{0,1},{1,0},{2,3},{3,2},{4,5},{5,4},{6,7},{7,6},{8,9},{9,8},{10,11... | collective-permute-start | bytes 393224 | tf_op jit(solution)/shard_map/ppermute | solution.py:375
  13.2 1.8 %collective-permute-start.3 = (f32[2,32,1536]{2,1,0:T(8,128)S(1)}, f32[2,32,1536]{2,1,0:T(8,128)S(1)}, u32[]{:S(2)}, u32[]{:S(2)}) collective-permute-start(f32[2,32,1536]{2,1,0:T(8,128)S(1)} %get-tuple-element.65), channel_id=1, source_target_pairs={{0,1},{1,0},{2,3},{3,2},{4,5},{5,4},{6,7},{7,6},{8,9},{9,8},{10,11... | collective-permute-start | bytes 1179656 | tf_op jit(solution)/shard_map/ppermute | solution.py:375
  15.0 7.0 %collective-permute-start.6 = (f32[32,768]{1,0:T(8,128)S(1)}, f32[32,768]{1,0:T(8,128)S(1)}, u32[]{:S(2)}, u32[]{:S(2)}) collective-permute-start(f32[32,768]{1,0:T(8,128)S(1)} %get-tuple-element.76), channel_id=1, source_target_pairs={{4,0},{5,1},{6,2},{7,3},{8,4},{9,5},{10,6},{11,7},{12,8},{13,9},{1... | collective-permute-start | bytes 294920 | tf_op jit(solution)/shard_map/ppermute | solution.py:421
  16.3 5.7 %collective-permute-start.7 = (f32[32,768]{1,0:T(8,128)S(1)}, f32[32,768]{1,0:T(8,128)S(1)}, u32[]{:S(2)}, u32[]{:S(2)}) collective-permute-start(f32[32,768]{1,0:T(8,128)S(1)} %get-tuple-element.77), channel_id=1, source_target_pairs={{0,2},{1,3},{2,0},{3,1},{4,6},{5,7},{6,4},{7,5},{8,10},{9,11},{10,... | collective-permute-start | bytes 294920 | tf_op jit(solution)/shard_map/ppermute | solution.py:375
  17.3 7.9 %collective-permute-start.8 = (f32[32,768]{1,0:T(8,128)S(1)}, f32[32,768]{1,0:T(8,128)S(1)}, u32[]{:S(2)}, u32[]{:S(2)}) collective-permute-start(f32[32,768]{1,0:T(8,128)S(1)} %get-tuple-element.78), channel_id=1, source_target_pairs={{4,2},{5,3},{6,0},{7,1},{8,6},{9,7},{10,4},{11,5},{12,10},{13,11},... | collective-permute-start | bytes 294920 | tf_op jit(solution)/shard_map/ppermute | solution.py:421
  18.6 3.0 %collective-permute-start.5 = (f32[32,512]{1,0:T(8,128)S(1)}, f32[32,512]{1,0:T(8,128)S(1)}, u32[]{:S(2)}, u32[]{:S(2)}) collective-permute-start(f32[32,512]{1,0:T(8,128)S(1)} %get-tuple-element.72), channel_id=1, source_target_pairs={{0,1},{1,0},{2,3},{3,2},{4,5},{5,4},{6,7},{7,6},{8,9},{9,8},{10,11... | collective-permute-start | bytes 196616 | tf_op jit(solution)/shard_map/ppermute | solution.py:375
  19.9 1.4 %collective-permute-start.4 = (f32[32,384]{1,0:T(8,128)S(1)}, f32[32,384]{1,0:T(8,128)S(1)}, u32[]{:S(2)}, u32[]{:S(2)}) collective-permute-start(f32[32,384]{1,0:T(8,128)S(1)} %get-tuple-element.71), channel_id=1, source_target_pairs={{0,1},{1,0},{2,3},{3,2},{4,5},{5,4},{6,7},{7,6},{8,9},{9,8},{10,11... | collective-permute-start | bytes 147464 | tf_op jit(solution)/shard_map/ppermute | solution.py:375
  21.3 9.6 %collective-permute-start.10 = (f32[384,1536]{1,0:T(8,128)S(1)}, f32[384,1536]{1,0:T(8,128)S(1)}, u32[]{:S(2)}, u32[]{:S(2)}) collective-permute-start(f32[384,1536]{1,0:T(8,128)S(1)} %bitcast.44), channel_id=1, source_target_pairs={{0,1},{1,0},{2,3},{3,2},{4,5},{5,4},{6,7},{7,6},{8,9},{9,8},{10,11... | collective-permute-start | bytes 7077896 | tf_op jit(solution)/shard_map/ppermute | solution.py:375
  25.2 8.4 %collective-permute-start.13 = (f32[384,1536]{1,0:T(8,128)S(1)}, f32[384,1536]{1,0:T(8,128)S(1)}, u32[]{:S(2)}, u32[]{:S(2)}) collective-permute-start(f32[384,1536]{1,0:T(8,128)S(1)} %bitcast.71), channel_id=1, source_target_pairs={{0,1},{1,0},{2,3},{3,2},{4,5},{5,4},{6,7},{7,6},{8,9},{9,8},{10,11... | collective-permute-start | bytes 7077896 | tf_op jit(solution)/shard_map/ppermute | solution.py:375
  25.3 5.6 %collective-permute-start.11 = (f32[32,768]{1,0:T(8,128)S(1)}, f32[32,768]{1,0:T(8,128)S(1)}, u32[]{:S(2)}, u32[]{:S(2)}) collective-permute-start(f32[32,768]{1,0:T(8,128)S(1)} %shard_map.223.refs_4_.refs_5_), channel_id=1, source_target_pairs={{0,4},{1,5},{2,6},{3,7},{4,0},{5,1},{6,2},{7,3},{8,12},{9,13},{10,... | collective-permute-start | bytes 294920 | tf_op jit(solution)/shard_map/ppermute | solution.py:375
  27.5 6.1 %collective-permute-start.9 = (f32[32,768]{1,0:T(8,128)S(1)}, f32[32,768]{1,0:T(8,128)S(1)}, u32[]{:S(2)}, u32[]{:S(2)}) collective-permute-start(f32[32,768]{1,0:T(8,128)S(1)} %shard_map.223.refs_4_.refs_5_), channel_id=1, source_target_pairs={{0,6},{1,7},{2,4},{3,5},{4,2},{5,3},{6,0},{7,1},{8,14},{9,15},{10,... | collective-permute-start | bytes 294920 | tf_op jit(solution)/shard_map/ppermute | solution.py:375
  30.9 2.7 %copy-start.1 = (f32[1,384,1536]{2,1,0:T(8,128)S(1)}, f32[1,384,1536]{2,1,0:T(8,128)}, u32[]{:S(2)}) copy-start(f32[1,384,1536]{2,1,0:T(8,128)} %param.35) | copy-start | bytes 7077892
  33.6 7.4 %collective-permute-start.16 = (f32[384,1536]{1,0:T(8,128)S(1)}, f32[384,1536]{1,0:T(8,128)S(1)}, u32[]{:S(2)}, u32[]{:S(2)}) collective-permute-start(f32[384,1536]{1,0:T(8,128)S(1)} %bitcast.51), channel_id=1, source_target_pairs={{0,1},{1,0},{2,3},{3,2},{4,5},{5,4},{6,7},{7,6},{8,9},{9,8},{10,11... | collective-permute-start | bytes 7077896 | tf_op jit(solution)/shard_map/ppermute | solution.py:375
  33.7 5.7 %collective-permute-start.14 = (f32[32,768]{1,0:T(8,128)S(1)}, f32[32,768]{1,0:T(8,128)S(1)}, u32[]{:S(2)}, u32[]{:S(2)}) collective-permute-start(f32[32,768]{1,0:T(8,128)S(1)} %shard_map.225.refs_5_), channel_id=1, source_target_pairs={{0,2},{1,3},{2,0},{3,1},{4,8},{5,9},{6,10},{7,11},{8,4},{9,5},{10,... | collective-permute-start | bytes 294920 | tf_op jit(solution)/shard_map/ppermute | solution.py:375
  34.7 6.4 %collective-permute-start.12 = (f32[32,768]{1,0:T(8,128)S(1)}, f32[32,768]{1,0:T(8,128)S(1)}, u32[]{:S(2)}, u32[]{:S(2)}) collective-permute-start(f32[32,768]{1,0:T(8,128)S(1)} %shard_map.225.refs_5_), channel_id=1, source_target_pairs={{0,2},{1,3},{2,0},{3,1},{4,10},{5,11},{6,8},{7,9},{8,6},{9,7},{10,... | collective-permute-start | bytes 294920 | tf_op jit(solution)/shard_map/ppermute | solution.py:375
  39.4 1.9 %copy-start.2 = (f32[1,512,1536]{2,1,0:T(8,128)S(1)}, f32[1,512,1536]{2,1,0:T(8,128)}, u32[]{:S(2)}) copy-start(f32[1,512,1536]{2,1,0:T(8,128)} %param.32) | copy-start | bytes 9437188
  41.3 14.5 %collective-permute-start.20 = (f32[512,1536]{1,0:T(8,128)S(1)}, f32[512,1536]{1,0:T(8,128)S(1)}, u32[]{:S(2)}, u32[]{:S(2)}) collective-permute-start(f32[512,1536]{1,0:T(8,128)S(1)} %bitcast.59), channel_id=1, source_target_pairs={{0,1},{1,0},{2,3},{3,2},{4,5},{5,4},{6,7},{7,6},{8,9},{9,8},{10,11... | collective-permute-start | bytes 9437192 | tf_op jit(solution)/shard_map/ppermute | solution.py:375
  41.3 6.3 %collective-permute-start.17 = (f32[32,768]{1,0:T(8,128)S(1)}, f32[32,768]{1,0:T(8,128)S(1)}, u32[]{:S(2)}, u32[]{:S(2)}) collective-permute-start(f32[32,768]{1,0:T(8,128)S(1)} %shard_map.227.refs_5_), channel_id=1, source_target_pairs={{0,4},{1,5},{2,6},{3,7},{4,0},{5,1},{6,2},{7,3},{8,12},{9,13},{10,... | collective-permute-start | bytes 294920 | tf_op jit(solution)/shard_map/ppermute | solution.py:375
  44.1 6.1 %collective-permute-start.15 = (f32[32,768]{1,0:T(8,128)S(1)}, f32[32,768]{1,0:T(8,128)S(1)}, u32[]{:S(2)}, u32[]{:S(2)}) collective-permute-start(f32[32,768]{1,0:T(8,128)S(1)} %shard_map.227.refs_5_), channel_id=1, source_target_pairs={{0,6},{1,7},{2,4},{3,5},{4,2},{5,3},{6,0},{7,1},{8,14},{9,15},{10,... | collective-permute-start | bytes 294920 | tf_op jit(solution)/shard_map/ppermute | solution.py:375
  50.2 4.7 %collective-permute-start.18 = (f32[32,768]{1,0:T(8,128)S(1)}, f32[32,768]{1,0:T(8,128)S(1)}, u32[]{:S(2)}, u32[]{:S(2)}) collective-permute-start(f32[32,768]{1,0:T(8,128)S(1)} %shard_map.229.refs_0_), channel_id=1, source_target_pairs={{0,2},{1,3},{2,0},{3,1},{4,6},{5,7},{6,4},{7,5},{8,10},{9,11},{10,... | collective-permute-start | bytes 294920 | tf_op jit(solution)/shard_map/ppermute | solution.py:375
  52.0 3.8 %copy-start.4 = (f32[1,512,1536]{2,1,0:T(8,128)S(1)}, f32[1,512,1536]{2,1,0:T(8,128)}, u32[]{:S(2)}) copy-start(f32[1,512,1536]{2,1,0:T(8,128)} %param.31) | copy-start | bytes 9437188
  55.7 7.7 %collective-permute-start.23 = (f32[512,1536]{1,0:T(8,128)S(1)}, f32[512,1536]{1,0:T(8,128)S(1)}, u32[]{:S(2)}, u32[]{:S(2)}) collective-permute-start(f32[512,1536]{1,0:T(8,128)S(1)} %bitcast.68), channel_id=1, source_target_pairs={{0,1},{1,0},{2,3},{3,2},{4,5},{5,4},{6,7},{7,6},{8,9},{9,8},{10,11... | collective-permute-start | bytes 9437192 | tf_op jit(solution)/shard_map/ppermute | solution.py:375
  55.8 5.5 %collective-permute-start.21 = (f32[32,768]{1,0:T(8,128)S(1)}, f32[32,768]{1,0:T(8,128)S(1)}, u32[]{:S(2)}, u32[]{:S(2)}) collective-permute-start(f32[32,768]{1,0:T(8,128)S(1)} %shard_map.231.refs_4_.refs_5_), channel_id=1, source_target_pairs={{0,4},{1,5},{2,6},{3,7},{4,0},{5,1},{6,2},{7,3},{8,12},{9,13},{10,... | collective-permute-start | bytes 294920 | tf_op jit(solution)/shard_map/ppermute | solution.py:375
  57.6 5.8 %collective-permute-start.19 = (f32[32,768]{1,0:T(8,128)S(1)}, f32[32,768]{1,0:T(8,128)S(1)}, u32[]{:S(2)}, u32[]{:S(2)}) collective-permute-start(f32[32,768]{1,0:T(8,128)S(1)} %shard_map.231.refs_4_.refs_5_), channel_id=1, source_target_pairs={{0,6},{1,7},{2,4},{3,5},{4,2},{5,3},{6,0},{7,1},{8,14},{9,15},{10,... | collective-permute-start | bytes 294920 | tf_op jit(solution)/shard_map/ppermute | solution.py:375
  61.3 2.2 %copy-start.3 = (f32[1,512,2048]{2,1,0:T(8,128)S(1)}, f32[1,512,2048]{2,1,0:T(8,128)}, u32[]{:S(2)}) copy-start(f32[1,512,2048]{2,1,0:T(8,128)} %param.30) | copy-start | bytes 12582916
  63.5 26.6 %collective-permute-start.30 = (f32[512,2048]{1,0:T(8,128)S(1)}, f32[512,2048]{1,0:T(8,128)S(1)}, u32[]{:S(2)}, u32[]{:S(2)}) collective-permute-start(f32[512,2048]{1,0:T(8,128)S(1)} %bitcast.64), channel_id=1, source_target_pairs={{0,1},{1,0},{2,3},{3,2},{4,5},{5,4},{6,7},{7,6},{8,9},{9,8},{10,11... | collective-permute-start | bytes 12582920 | tf_op jit(solution)/shard_map/ppermute | solution.py:375
  63.6 5.7 %collective-permute-start.24 = (f32[32,768]{1,0:T(8,128)S(1)}, f32[32,768]{1,0:T(8,128)S(1)}, u32[]{:S(2)}, u32[]{:S(2)}) collective-permute-start(f32[32,768]{1,0:T(8,128)S(1)} %shard_map.233.refs_5_), channel_id=1, source_target_pairs={{0,2},{1,3},{2,0},{3,1},{4,8},{5,9},{6,10},{7,11},{8,4},{9,5},{10,... | collective-permute-start | bytes 294920 | tf_op jit(solution)/shard_map/ppermute | solution.py:375
  64.8 6.1 %collective-permute-start.22 = (f32[32,768]{1,0:T(8,128)S(1)}, f32[32,768]{1,0:T(8,128)S(1)}, u32[]{:S(2)}, u32[]{:S(2)}) collective-permute-start(f32[32,768]{1,0:T(8,128)S(1)} %shard_map.233.refs_5_), channel_id=1, source_target_pairs={{0,2},{1,3},{2,0},{3,1},{4,10},{5,11},{6,8},{7,9},{8,6},{9,7},{10,... | collective-permute-start | bytes 294920 | tf_op jit(solution)/shard_map/ppermute | solution.py:375
  70.9 5.5 %collective-permute-start.26 = (f32[32,768]{1,0:T(8,128)S(1)}, f32[32,768]{1,0:T(8,128)S(1)}, u32[]{:S(2)}, u32[]{:S(2)}) collective-permute-start(f32[32,768]{1,0:T(8,128)S(1)} %shard_map.235.refs_0_.refs_5_), channel_id=1, source_target_pairs={{0,2},{1,3},{2,0},{3,1},{4,6},{5,7},{6,4},{7,5},{8,10},{9,11},{10,... | collective-permute-start | bytes 294920 | tf_op jit(solution)/shard_map/ppermute | solution.py:375
  72.1 7.6 %collective-permute-start.25 = (f32[32,768]{1,0:T(8,128)S(1)}, f32[32,768]{1,0:T(8,128)S(1)}, u32[]{:S(2)}, u32[]{:S(2)}) collective-permute-start(f32[32,768]{1,0:T(8,128)S(1)} %shard_map.235.refs_0_.refs_5_), channel_id=1, source_target_pairs={{0,6},{1,7},{2,4},{3,5},{4,2},{5,3},{6,0},{7,1},{8,14},{9,15},{10,... | collective-permute-start | bytes 294920 | tf_op jit(solution)/shard_map/ppermute | solution.py:375
  76.4 4.6 %collective-permute-start.27 = (f32[32,768]{1,0:T(8,128)S(1)}, f32[32,768]{1,0:T(8,128)S(1)}, u32[]{:S(2)}, u32[]{:S(2)}) collective-permute-start(f32[32,768]{1,0:T(8,128)S(1)} %shard_map.235.refs_0_.refs_5_), channel_id=1, source_target_pairs={{0,4},{1,5},{2,6},{3,7},{4,0},{5,1},{6,2},{7,3},{8,12},{9,13},{10,... | collective-permute-start | bytes 294920 | tf_op jit(solution)/shard_map/ppermute | solution.py:375
  82.8 6.2 %collective-permute-start.31 = (f32[32,768]{1,0:T(8,128)S(1)}, f32[32,768]{1,0:T(8,128)S(1)}, u32[]{:S(2)}, u32[]{:S(2)}) collective-permute-start(f32[32,768]{1,0:T(8,128)S(1)} %shard_map.238.refs_0_), channel_id=1, source_target_pairs={{0,4},{1,5},{2,6},{3,7},{4,8},{5,9},{6,10},{7,11},{8,12},{9,13},{1... | collective-permute-start | bytes 294920 | tf_op jit(solution)/shard_map/ppermute | solution.py:421
  84.8 5.3 %collective-permute-start.29 = (f32[32,768]{1,0:T(8,128)S(1)}, f32[32,768]{1,0:T(8,128)S(1)}, u32[]{:S(2)}, u32[]{:S(2)}) collective-permute-start(f32[32,768]{1,0:T(8,128)S(1)} %shard_map.238.refs_0_), channel_id=1, source_target_pairs={{0,6},{1,7},{2,4},{3,5},{4,10},{5,11},{6,8},{7,9},{8,14},{9,15},{1... | collective-permute-start | bytes 294920 | tf_op jit(solution)/shard_map/ppermute | solution.py:421
  87.8 4.7 %collective-permute-start.28 = (f32[32,768]{1,0:T(8,128)S(1)}, f32[32,768]{1,0:T(8,128)S(1)}, u32[]{:S(2)}, u32[]{:S(2)}) collective-permute-start(f32[32,768]{1,0:T(8,128)S(1)} %shard_map.238.refs_0_), channel_id=1, source_target_pairs={{0,2},{1,3},{2,0},{3,1},{4,6},{5,7},{6,4},{7,5},{8,10},{9,11},{10,... | collective-permute-start | bytes 294920 | tf_op jit(solution)/shard_map/ppermute | solution.py:375
  92.5 3.6 %copy-start.9 = (f32[1,384,64]{1,2,0:T(8,128)S(1)}, f32[1,384,64]{1,2,0:T(8,128)}, u32[]{:S(2)}) copy-start(f32[1,384,64]{1,2,0:T(8,128)} %param.27) | copy-start | bytes 294916
  92.5 3.6 %copy-start.10 = (f32[1,384,64]{1,2,0:T(8,128)S(1)}, f32[1,384,64]{1,2,0:T(8,128)}, u32[]{:S(2)}) copy-start(f32[1,384,64]{1,2,0:T(8,128)} %param.28) | copy-start | bytes 294916
  92.5 3.6 %copy-start.11 = (f32[1,384,64]{1,2,0:T(8,128)S(1)}, f32[1,384,64]{1,2,0:T(8,128)}, u32[]{:S(2)}) copy-start(f32[1,384,64]{1,2,0:T(8,128)} %param.29) | copy-start | bytes 294916
  93.6 5.0 %collective-permute-start.32 = (f32[32,1024]{1,0:T(8,128)S(1)}, f32[32,1024]{1,0:T(8,128)S(1)}, u32[]{:S(2)}, u32[]{:S(2)}) collective-permute-start(f32[32,1024]{1,0:T(8,128)S(1)} %shard_map.240.refs_0_), channel_id=1, source_target_pairs={{0,2},{1,3},{2,0},{3,1},{4,6},{5,7},{6,4},{7,5},{8,10},{9,11},{10,... | collective-permute-start | bytes 393224 | tf_op jit(solution)/shard_map/ppermute | solution.py:375
  94.8 1.3 %collective-permute-start.33 = (f32[32,384]{1,0:T(8,128)S(1)}, f32[32,384]{1,0:T(8,128)S(1)}, u32[]{:S(2)}, u32[]{:S(2)}) collective-permute-start(f32[32,384]{1,0:T(8,128)S(1)} %get-tuple-element.96), channel_id=1, source_target_pairs={{0,1},{1,0},{2,3},{3,2},{4,5},{5,4},{6,7},{7,6},{8,9},{9,8},{10,11... | collective-permute-start | bytes 147464 | tf_op jit(solution)/shard_map/ppermute | solution.py:375
  98.6 2.7 %copy-start.6 = (f32[1,512,64]{1,2,0:T(8,128)S(1)}, f32[1,512,64]{1,2,0:T(8,128)}, u32[]{:S(2)}) copy-start(f32[1,512,64]{1,2,0:T(8,128)} %param.24) | copy-start | bytes 393220
  98.6 2.7 %copy-start.7 = (f32[1,512,64]{1,2,0:T(8,128)S(1)}, f32[1,512,64]{1,2,0:T(8,128)}, u32[]{:S(2)}) copy-start(f32[1,512,64]{1,2,0:T(8,128)} %param.25) | copy-start | bytes 393220
  98.6 2.7 %copy-start.8 = (f32[1,512,64]{1,2,0:T(8,128)S(1)}, f32[1,512,64]{1,2,0:T(8,128)}, u32[]{:S(2)}) copy-start(f32[1,512,64]{1,2,0:T(8,128)} %param.26) | copy-start | bytes 393220
  100.0 1.3 %collective-permute-start.34 = (f32[32,512]{1,0:T(8,128)S(1)}, f32[32,512]{1,0:T(8,128)S(1)}, u32[]{:S(2)}, u32[]{:S(2)}) collective-permute-start(f32[32,512]{1,0:T(8,128)S(1)} %get-tuple-element.103), channel_id=1, source_target_pairs={{0,1},{1,0},{2,3},{3,2},{4,5},{5,4},{6,7},{7,6},{8,9},{9,8},{10,11... | collective-permute-start | bytes 196616 | tf_op jit(solution)/shard_map/ppermute | solution.py:375

commit v8 on v7

--- a/solution.py
+++ b/solution.py
@@ -306,32 +306,24 @@
     store_rows(out, plus(times_rows(value, *rows, columns=columns(value.shape[1])), sofar))
 
 
-def rows_kernel(pieces, rows, out):
-    store_rows(out, times_rows(joined(pieces), *rows))
-
-
-def coupled_kernel(columns, final, load, early, pieces, sofar, above, below, out):
-    here, lower = pieces
+def coupled_kernel(columns, final, load, piece, rows, sofar, out):
     story = lax.axis_index("story")
-    width = here.shape[1]
-
-    def finish(value, *terms):
-        if not final:
+
+    def finish(value):
+        if final:
+            store_rows(out, value)
+            out[...] = by_core(load[0][...], load[1][...], 1) - out[...]
+        else:
             out[...] = value
-            return
-        store_rows(out, value)
-        total = by_core(load[0][...], load[1][...], 1) - out[...]
-        for term in terms:
-            total = total - term[...]
-        out[...] = total
 
     @pl.when(story == 0)
     def _():
-        finish(plus(times_rows(here[...], *above, columns=columns(width)), sofar))
+        finish(sofar[0][...])
 
     @pl.when(story > 0)
     def _():
-        finish(plus(times_rows(lower[...], *below, columns=columns(width)), sofar), *early)
+        value = piece[0][...]
+        finish(plus(times_rows(value, *rows, columns=columns(value.shape[1])), sofar))
 
 
 def last_kernel(columns, piece, rows, sofar, mine, theirs):
@@ -533,15 +525,6 @@
         if k == max(mv.stories - 3, 0):
             inverse_other = others(interior_inverse[0], [below_other, face])
             came[-1], below_other = lax.optimization_barrier([came[-1], below_other])
-        if k == 0:
-            (early,) = call(
-                rows_kernel,
-                shape_int,
-                mv.gather_chips(face),
-                [couple_above[0], above_other],
-                cost=8 << 20,
-            )
-            came[-1], early = lax.optimization_barrier([came[-1], early])
         (face,) = call(
             functools.partial(step_kernel, from_chip(len(came), len(came) - 1), k),
             shape,
@@ -549,21 +532,24 @@
             [pivoted, face],
         )
 
+    here = mv.gather_chips(face)
     came = mv.pieces([mv.shift(face, 1, j) for j in range(mv.chips)])
     came[-1], inverse_other = lax.optimization_barrier([came[-1], inverse_other])
-    pairs = list(zip(mv.gather_chips(face), came))
+    rows = [couple_above[0], above_other]
     sofar = []
-    for j, pair in enumerate(pairs):
-        final = j == len(pairs) - 1
+    for j, piece in enumerate(here):
+        kernel = functools.partial(part_kernel, from_chip(len(here), j), None)
+        sofar = call(kernel, shape_int, [piece], rows, sofar, cost=4 << 20)
+    rows = [couple_below[0], below_other]
+    for j, piece in enumerate(came):
+        final = j == len(came) - 1
         sofar = call(
-            functools.partial(coupled_kernel, from_chip(len(pairs), j), final),
+            functools.partial(coupled_kernel, from_chip(len(came), j), final),
             shape_int,
             load_int_half if final else [],
-            [early] if final else [],
-            list(pair),
+            [piece],
+            rows,
             sofar,
-            [couple_above[0], above_other],
-            [couple_below[0], below_other],
             cost=4 << 20,
         )
     (reduced,) = sofar

time: 102 us -> 100 us (0.980); the launches traced: 102 us -> 98.8 us
  Pallas kernels: 20.9 us -> 18.9 us
    pallas_call x26 -> x27, Pallas kernels: 14.3 us -> 12.4 us  [call(): pl.pallas_call(body, in_specs=[VMEM] * len(flat), out_specs=[VMEM] * len(...]
    ppermute x31 -> x30, starting transfers between devices: 28.2 us -> 26.9 us  [permute(): return lax.ppermute(value, AXES, pairs)]
    ppermute x31 -> x30, waiting for transfers between devices: 40.6 us -> 39.9 us  [permute(): return lax.ppermute(value, AXES, pairs)]
  transfers between devices with their start and end apart: 35 -> 34, of which waited for: 22 -> 21; matrix products, arithmetic and copies ran while one was open for 0% -> 0% of each run, Pallas kernels for 13% -> 13%
where the time goes in v8:
time: 100 us; the launch traced here: 98.8 us
  waiting for transfers between devices  43.4 us (43%)
  starting transfers between devices  35.2 us (35%)
  Pallas kernels  18.9 us (19%)
  between operations  1.01 us (1%)
    ppermute x30, waiting for transfers between devices, permute(): return lax.ppermute(value, AXES, pairs)  39.9 us
    ppermute x30, starting transfers between devices, permute(): return lax.ppermute(value, AXES, pairs)  26.9 us
    pallas_call x27, Pallas kernels, call(): pl.pallas_call(body, in_specs=[VMEM] * len(flat), out_specs=[VMEM] * len(...  12.4 us
    ppermute x4, starting transfers between devices, shift(): return lax.ppermute(value, AXES, pairs)  8.36 us
    pallas_call x1, Pallas kernels, staged(): pl.pallas_call(body, in_specs=[pl.BlockSpec(memory_space=pltpu.HBM)] * co...  4.08 us
    ppermute x4, waiting for transfers between devices, shift(): return lax.ppermute(value, AXES, pairs)  3.52 us
    pallas_call x2, Pallas kernels, fetched(): pl.pallas_call(body, in_specs=[pl.BlockSpec(memory_space=pltpu.HBM)] * co...  2.48 us
  transfers between devices with their start and end apart: 34, of which 21 were waited for; matrix products, arithmetic and copies ran while one was open for 0% of the time, Pallas kernels for 13%

profile of v8, /device:TPU:0, one launch (start us, length us, event | category | flops | bytes accessed | tf_op | source)
XLA Modules:
  0.0 98.8 jit_solution(16317777891513628219)
XLA Ops:
  0.6 1.3 %shard_map.217 = (f32[64,512]{1,0:T(8,128)S(1)}, f32[64,128]{1,0:T(8,128)S(1)}) custom-call(s32[1,64]{1,0:T(1,128)} %bitcast.86, f32[1,512]{1,0:T(1,128)} %bitcast.85, f32[1,512]{1,0:T(1,128)} %refs_2_.1, f32[1,512]{1,0:T(1,128)} %refs_3_.1, f32[64,512]{1,0:T(8,128)} %bitcast.73, f32[64,512]{1,0:T(8,128)} %bitcast.75, f32[64,512]{1,0:T(8,128)} %bitcast.77), custom_call_target="tpu_custom_call" | custom-call | tf_op jit(solution)/shard_map/pallas_call | solution.py:180
  2.0 3.0 %collective-permute-start.1 = (f32[64,512]{1,0:T(8,128)S(1)}, f32[64,512]{1,0:T(8,128)S(1)}, u32[]{:S(2)}, u32[]{:S(2)}) collective-permute-start(f32[64,512]{1,0:T(8,128)S(1)} %get-tuple-element.65.refs_0_), channel_id=1, source_target_pairs={{0,2},{1,3},{2,0},{3,1},{4,6},{5,7},{6,4},{7,5},{8,10},{9,11},{10,... | collective-permute-start | bytes 393224 | tf_op jit(solution)/shard_map/ppermute | solution.py:367
  5.0 4.1 %shard_map.218.refs_4_ = f32[512,5120]{1,0:T(8,128)S(1)} custom-call(f32[512,2048]{1,0:T(8,128)} %bitcast.58, f32[512,1536]{1,0:T(8,128)} %bitcast.62, f32[512,1536]{1,0:T(8,128)} %bitcast.66), custom_call_target="tpu_custom_call" | custom-call | tf_op jit(solution)/shard_map/pallas_call | solution.py:128
  9.7 1.0 collective-permute-done.2.refs_3_
  10.7 2.5 %shard_map.219 = (f32[2,32,1536]{2,1,0:T(8,128)S(1)}, f32[2,32,1536]{2,1,0:T(8,128)S(1)}) custom-call(f32[64,512]{1,0:T(8,128)S(1)} %get-tuple-element.65.refs_0_, f32[64,512]{1,0:T(8,128)S(1)} %collective-permute-done.refs_1_, f32[64,512]{1,0:T(8,128)S(1)} %collective-permute-done.1.refs_2_, f32[64,512]{1,0:T(8,128)S(1)} %collective-permute-done.2.refs_3_, ...), custom_call_target="tpu_custom_call" | custom-call | tf_op jit(solution)/shard_map/pallas_call | solution.py:91
  13.6 1.4 %collective-permute-done.3.refs_1_ = f32[2,32,1536]{2,1,0:T(8,128)S(1)} collective-permute-done((f32[2,32,1536]{2,1,0:T(8,128)S(1)}, f32[2,32,1536]{2,1,0:T(8,128)S(1)}, u32[]{:S(2)}, u32[]{:S(2)}) %collective-permute-start.3) | collective-permute-done | bytes 393248 | tf_op jit(solution)/shard_map/ppermute | solution.py:367
  15.0 1.3 %collective-permute-start.6 = (f32[32,768]{1,0:T(8,128)S(1)}, f32[32,768]{1,0:T(8,128)S(1)}, u32[]{:S(2)}, u32[]{:S(2)}) collective-permute-start(f32[32,768]{1,0:T(8,128)S(1)} %get-tuple-element.74), channel_id=1, source_target_pairs={{4,0},{5,1},{6,2},{7,3},{8,4},{9,5},{10,6},{11,7},{12,8},{13,9},{1... | collective-permute-start | bytes 294920 | tf_op jit(solution)/shard_map/ppermute | solution.py:413
  16.3 1.0 collective-permute-start.7
  17.3 1.3 %collective-permute-start.8 = (f32[32,768]{1,0:T(8,128)S(1)}, f32[32,768]{1,0:T(8,128)S(1)}, u32[]{:S(2)}, u32[]{:S(2)}) collective-permute-start(f32[32,768]{1,0:T(8,128)S(1)} %get-tuple-element.76), channel_id=1, source_target_pairs={{4,2},{5,3},{6,0},{7,1},{8,6},{9,7},{10,4},{11,5},{12,10},{13,11},... | collective-permute-start | bytes 294920 | tf_op jit(solution)/shard_map/ppermute | solution.py:413
  18.7 1.2 %shard_map.222 = (f32[32,384]{1,0:T(8,128)S(1)}, f32[32,384]{1,0:T(8,128)S(1)}) custom-call(f32[1,384]{1,0:T(1,128)} %refs_0_.1, f32[1,384]{1,0:T(1,128)} %refs_1_.1, f32[64,384]{1,0:T(8,128)} %bitcast.79, f32[64,384]{1,0:T(8,128)} %bitcast.81, f32[64,384]{1,0:T(8,128)} %bitcast.83, f32[64,128]{1,0:T(8,128)S(1)} %get-tuple-element.68.refs_5_), custom_call_target="tpu_custom_call" | custom-call | tf_op jit(solution)/shard_map/pallas_call | solution.py:180
  20.4 0.9 collective-permute-done.4.refs_1_
  22.0 3.2 %collective-permute-done.8.refs_5_ = f32[32,768]{1,0:T(8,128)S(1)} collective-permute-done((f32[32,768]{1,0:T(8,128)S(1)}, f32[32,768]{1,0:T(8,128)S(1)}, u32[]{:S(2)}, u32[]{:S(2)}) %collective-permute-start.8) | collective-permute-done | bytes 98336 | tf_op jit(solution)/shard_map/ppermute | solution.py:413
  25.3 2.3 %collective-permute-start.11 = (f32[32,768]{1,0:T(8,128)S(1)}, f32[32,768]{1,0:T(8,128)S(1)}, u32[]{:S(2)}, u32[]{:S(2)}) collective-permute-start(f32[32,768]{1,0:T(8,128)S(1)} %shard_map.223.refs_4_.refs_5_), channel_id=1, source_target_pairs={{0,4},{1,5},{2,6},{3,7},{4,0},{5,1},{6,2},{7,3},{8,12},{9,13},{10,... | collective-permute-start | bytes 294920 | tf_op jit(solution)/shard_map/ppermute | solution.py:367
  28.2 2.7 %collective-permute-done.11.refs_0_ = f32[32,768]{1,0:T(8,128)S(1)} collective-permute-done((f32[32,768]{1,0:T(8,128)S(1)}, f32[32,768]{1,0:T(8,128)S(1)}, u32[]{:S(2)}, u32[]{:S(2)}) %collective-permute-start.11) | collective-permute-done | bytes 98336 | tf_op jit(solution)/shard_map/ppermute | solution.py:367
  30.9 2.7 %collective-permute-done.9.refs_0_ = f32[32,768]{1,0:T(8,128)S(1)} collective-permute-done((f32[32,768]{1,0:T(8,128)S(1)}, f32[32,768]{1,0:T(8,128)S(1)}, u32[]{:S(2)}, u32[]{:S(2)}) %collective-permute-start.9) | collective-permute-done | bytes 98336 | tf_op jit(solution)/shard_map/ppermute | solution.py:367
  33.7 1.0 collective-permute-start.14
  34.7 1.1 %collective-permute-start.12 = (f32[32,768]{1,0:T(8,128)S(1)}, f32[32,768]{1,0:T(8,128)S(1)}, u32[]{:S(2)}, u32[]{:S(2)}) collective-permute-start(f32[32,768]{1,0:T(8,128)S(1)} %shard_map.225.refs_5_), channel_id=1, source_target_pairs={{0,2},{1,3},{2,0},{3,1},{4,10},{5,11},{6,8},{7,9},{8,6},{9,7},{10,... | collective-permute-start | bytes 294920 | tf_op jit(solution)/shard_map/ppermute | solution.py:367
  35.8 3.6 %collective-permute-done.14.refs_0_ = f32[32,768]{1,0:T(8,128)S(1)} collective-permute-done((f32[32,768]{1,0:T(8,128)S(1)}, f32[32,768]{1,0:T(8,128)S(1)}, u32[]{:S(2)}, u32[]{:S(2)}) %collective-permute-start.14) | collective-permute-done | bytes 98336 | tf_op jit(solution)/shard_map/ppermute | solution.py:367
  39.4 1.7 %collective-permute-done.12.refs_0_ = f32[32,768]{1,0:T(8,128)S(1)} collective-permute-done((f32[32,768]{1,0:T(8,128)S(1)}, f32[32,768]{1,0:T(8,128)S(1)}, u32[]{:S(2)}, u32[]{:S(2)}) %collective-permute-start.12) | collective-permute-done | bytes 98336 | tf_op jit(solution)/shard_map/ppermute | solution.py:367
  41.3 2.9 %collective-permute-start.17 = (f32[32,768]{1,0:T(8,128)S(1)}, f32[32,768]{1,0:T(8,128)S(1)}, u32[]{:S(2)}, u32[]{:S(2)}) collective-permute-start(f32[32,768]{1,0:T(8,128)S(1)} %shard_map.227.refs_5_), channel_id=1, source_target_pairs={{0,4},{1,5},{2,6},{3,7},{4,0},{5,1},{6,2},{7,3},{8,12},{9,13},{10,... | collective-permute-start | bytes 294920 | tf_op jit(solution)/shard_map/ppermute | solution.py:367
  44.8 2.7 %collective-permute-done.17.refs_0_ = f32[32,768]{1,0:T(8,128)S(1)} collective-permute-done((f32[32,768]{1,0:T(8,128)S(1)}, f32[32,768]{1,0:T(8,128)S(1)}, u32[]{:S(2)}, u32[]{:S(2)}) %collective-permute-start.17) | collective-permute-done | bytes 98336 | tf_op jit(solution)/shard_map/ppermute | solution.py:367
  47.5 2.7 %collective-permute-done.15.refs_0_ = f32[32,768]{1,0:T(8,128)S(1)} collective-permute-done((f32[32,768]{1,0:T(8,128)S(1)}, f32[32,768]{1,0:T(8,128)S(1)}, u32[]{:S(2)}, u32[]{:S(2)}) %collective-permute-start.15) | collective-permute-done | bytes 98336 | tf_op jit(solution)/shard_map/ppermute | solution.py:367
  50.2 1.0 collective-permute-start.18
  51.2 0.8 shard_map.230.refs_3_
  52.0 2.9 %collective-permute-done.18.refs_0_ = f32[32,768]{1,0:T(8,128)S(1)} collective-permute-done((f32[32,768]{1,0:T(8,128)S(1)}, f32[32,768]{1,0:T(8,128)S(1)}, u32[]{:S(2)}, u32[]{:S(2)}) %collective-permute-start.18) | collective-permute-done | bytes 98336 | tf_op jit(solution)/shard_map/ppermute | solution.py:367
  54.9 0.8 shard_map.231.refs_4_.refs_5_
  55.8 1.8 %collective-permute-start.21 = (f32[32,768]{1,0:T(8,128)S(1)}, f32[32,768]{1,0:T(8,128)S(1)}, u32[]{:S(2)}, u32[]{:S(2)}) collective-permute-start(f32[32,768]{1,0:T(8,128)S(1)} %shard_map.231.refs_4_.refs_5_), channel_id=1, source_target_pairs={{0,4},{1,5},{2,6},{3,7},{4,0},{5,1},{6,2},{7,3},{8,12},{9,13},{10,... | collective-permute-start | bytes 294920 | tf_op jit(solution)/shard_map/ppermute | solution.py:367
  58.2 3.1 %collective-permute-done.21.refs_0_ = f32[32,768]{1,0:T(8,128)S(1)} collective-permute-done((f32[32,768]{1,0:T(8,128)S(1)}, f32[32,768]{1,0:T(8,128)S(1)}, u32[]{:S(2)}, u32[]{:S(2)}) %collective-permute-start.21) | collective-permute-done | bytes 98336 | tf_op jit(solution)/shard_map/ppermute | solution.py:367
  61.3 2.2 %collective-permute-done.19.refs_0_ = f32[32,768]{1,0:T(8,128)S(1)} collective-permute-done((f32[32,768]{1,0:T(8,128)S(1)}, f32[32,768]{1,0:T(8,128)S(1)}, u32[]{:S(2)}, u32[]{:S(2)}) %collective-permute-start.19) | collective-permute-done | bytes 98336 | tf_op jit(solution)/shard_map/ppermute | solution.py:367
  63.6 1.2 %collective-permute-start.24 = (f32[32,768]{1,0:T(8,128)S(1)}, f32[32,768]{1,0:T(8,128)S(1)}, u32[]{:S(2)}, u32[]{:S(2)}) collective-permute-start(f32[32,768]{1,0:T(8,128)S(1)} %shard_map.233.refs_5_), channel_id=1, source_target_pairs={{0,2},{1,3},{2,0},{3,1},{4,8},{5,9},{6,10},{7,11},{8,4},{9,5},{10,... | collective-permute-start | bytes 294920 | tf_op jit(solution)/shard_map/ppermute | solution.py:367
  64.8 0.9 collective-permute-start.22
  65.7 3.6 %collective-permute-done.24.refs_0_ = f32[32,768]{1,0:T(8,128)S(1)} collective-permute-done((f32[32,768]{1,0:T(8,128)S(1)}, f32[32,768]{1,0:T(8,128)S(1)}, u32[]{:S(2)}, u32[]{:S(2)}) %collective-permute-start.24) | collective-permute-done | bytes 98336 | tf_op jit(solution)/shard_map/ppermute | solution.py:367
  69.2 1.7 %collective-permute-done.22.refs_0_ = f32[32,768]{1,0:T(8,128)S(1)} collective-permute-done((f32[32,768]{1,0:T(8,128)S(1)}, f32[32,768]{1,0:T(8,128)S(1)}, u32[]{:S(2)}, u32[]{:S(2)}) %collective-permute-start.22) | collective-permute-done | bytes 98336 | tf_op jit(solution)/shard_map/ppermute | solution.py:367
  70.9 3.9 %collective-permute-start.26 = (f32[32,768]{1,0:T(8,128)S(1)}, f32[32,768]{1,0:T(8,128)S(1)}, u32[]{:S(2)}, u32[]{:S(2)}) collective-permute-start(f32[32,768]{1,0:T(8,128)S(1)} %shard_map.235.refs_5_), channel_id=1, source_target_pairs={{0,4},{1,5},{2,6},{3,7},{4,0},{5,1},{6,2},{7,3},{8,12},{9,13},{10,... | collective-permute-start | bytes 294920 | tf_op jit(solution)/shard_map/ppermute | solution.py:367
  75.3 2.5 %collective-permute-done.26.refs_0_ = f32[32,768]{1,0:T(8,128)S(1)} collective-permute-done((f32[32,768]{1,0:T(8,128)S(1)}, f32[32,768]{1,0:T(8,128)S(1)}, u32[]{:S(2)}, u32[]{:S(2)}) %collective-permute-start.26) | collective-permute-done | bytes 98336 | tf_op jit(solution)/shard_map/ppermute | solution.py:367
  77.8 0.8 shard_map.236.refs_3_
  78.6 1.7 %collective-permute-done.25.refs_0_ = f32[32,768]{1,0:T(8,128)S(1)} collective-permute-done((f32[32,768]{1,0:T(8,128)S(1)}, f32[32,768]{1,0:T(8,128)S(1)}, u32[]{:S(2)}, u32[]{:S(2)}) %collective-permute-start.25) | collective-permute-done | bytes 98336 | tf_op jit(solution)/shard_map/ppermute | solution.py:367
  80.3 0.8 shard_map.237.refs_0_
  81.2 1.1 %collective-permute-start.30 = (f32[32,768]{1,0:T(8,128)S(1)}, f32[32,768]{1,0:T(8,128)S(1)}, u32[]{:S(2)}, u32[]{:S(2)}) collective-permute-start(f32[32,768]{1,0:T(8,128)S(1)} %shard_map.237.refs_0_), channel_id=1, source_target_pairs={{0,2},{1,3},{2,0},{3,1},{4,6},{5,7},{6,4},{7,5},{8,10},{9,11},{10,... | collective-permute-start | bytes 294920 | tf_op jit(solution)/shard_map/ppermute | solution.py:367
  82.2 2.4 %collective-permute-start.29 = (f32[32,768]{1,0:T(8,128)S(1)}, f32[32,768]{1,0:T(8,128)S(1)}, u32[]{:S(2)}, u32[]{:S(2)}) collective-permute-start(f32[32,768]{1,0:T(8,128)S(1)} %shard_map.237.refs_0_), channel_id=1, source_target_pairs={{0,4},{1,5},{2,6},{3,7},{4,8},{5,9},{6,10},{7,11},{8,12},{9,13},{1... | collective-permute-start | bytes 294920 | tf_op jit(solution)/shard_map/ppermute | solution.py:413
  84.7 3.3 %collective-permute-start.27 = (f32[32,768]{1,0:T(8,128)S(1)}, f32[32,768]{1,0:T(8,128)S(1)}, u32[]{:S(2)}, u32[]{:S(2)}) collective-permute-start(f32[32,768]{1,0:T(8,128)S(1)} %shard_map.237.refs_0_), channel_id=1, source_target_pairs={{0,6},{1,7},{2,4},{3,5},{4,10},{5,11},{6,8},{7,9},{8,14},{9,15},{1... | collective-permute-start | bytes 294920 | tf_op jit(solution)/shard_map/ppermute | solution.py:413
  88.0 1.1 %shard_map.238.refs_3_ = f32[32,1024]{1,0:T(8,128)S(1)} custom-call(f32[32,768]{1,0:T(8,128)S(1)} %shard_map.237.refs_0_, f32[512,1536]{1,0:T(8,128)S(1)} %bitcast.64, f32[512,1536]{1,0:T(8,128)S(1)} %collective-permute-done.20.refs_2_), custom_call_target="tpu_custom_call" | custom-call | bytes 4194304 | tf_op jit(solution)/shard_map/pallas_call | solution.py:91
  89.1 1.0 %shard_map.239.refs_3_ = f32[32,1024]{1,0:T(8,128)S(1)} custom-call(f32[32,768]{1,0:T(8,128)S(1)} %collective-permute-done.30.refs_0_, f32[512,1536]{1,0:T(8,128)S(1)} %bitcast.65, f32[512,1536]{1,0:T(8,128)S(1)} %collective-permute-done.20.refs_2_, f32[32,1024]{1,0:T(8,128)S(1)} %shard_map.238.refs_3_), custom_call_target="tpu_custom_call" | custom-call | bytes 4194304 | tf_op jit(solution)/shard_map/pallas_call | solution.py:91
  90.3 1.0 %collective-permute-start.31 = (f32[32,1024]{1,0:T(8,128)S(1)}, f32[32,1024]{1,0:T(8,128)S(1)}, u32[]{:S(2)}, u32[]{:S(2)}) collective-permute-start(f32[32,1024]{1,0:T(8,128)S(1)} %shard_map.241.refs_0_), channel_id=1, source_target_pairs={{0,2},{1,3},{2,0},{3,1},{4,6},{5,7},{6,4},{7,5},{8,10},{9,11},{10,... | collective-permute-start | bytes 393224 | tf_op jit(solution)/shard_map/ppermute | solution.py:367
  91.5 1.2 %collective-permute-done.32.refs_1_ = f32[32,384]{1,0:T(8,128)S(1)} collective-permute-done((f32[32,384]{1,0:T(8,128)S(1)}, f32[32,384]{1,0:T(8,128)S(1)}, u32[]{:S(2)}, u32[]{:S(2)}) %collective-permute-start.32) | collective-permute-done | bytes 49184 | tf_op jit(solution)/shard_map/ppermute | solution.py:367
  93.4 1.4 %shard_map.244.refs_3_ = f32[32,1024]{1,0:T(8,128)S(1)} custom-call(f32[32,1024]{1,0:T(8,128)S(1)} %shard_map.241.refs_0_, f32[512,2048]{1,0:T(8,128)S(1)} %bitcast.60, f32[512,2048]{1,0:T(8,128)S(1)} %collective-permute-done.28.refs_2_), custom_call_target="tpu_custom_call" | custom-call | bytes 4194304 | tf_op jit(solution)/shard_map/pallas_call | solution.py:91
  95.4 1.4 %shard_map.245 = (f32[32,512]{1,0:T(8,128)S(1)}, f32[32,512]{1,0:T(8,128)S(1)}) custom-call(f32[32,1024]{1,0:T(8,128)S(1)} %collective-permute-done.31.refs_0_, f32[512,2048]{1,0:T(8,128)S(1)} %bitcast.61, f32[512,2048]{1,0:T(8,128)S(1)} %collective-permute-done.28.refs_2_, f32[32,1024]{1,0:T(8,128)S(1)} %shard_map.244.refs_3_), custom_call_target="tpu_custom_call" | custom-call | tf_op jit(solution)/shard_map/pallas_call | solution.py:91
  96.8 1.2 %collective-permute-done.33.refs_1_ = f32[32,512]{1,0:T(8,128)S(1)} collective-permute-done((f32[32,512]{1,0:T(8,128)S(1)}, f32[32,512]{1,0:T(8,128)S(1)}, u32[]{:S(2)}, u32[]{:S(2)}) %collective-permute-start.33) | collective-permute-done | bytes 65568 | tf_op jit(solution)/shard_map/ppermute | solution.py:367
  (74 shorter events, 7.8 us)
Async XLA Ops:
  2.0 7.1 %collective-permute-start.1 = (f32[64,512]{1,0:T(8,128)S(1)}, f32[64,512]{1,0:T(8,128)S(1)}, u32[]{:S(2)}, u32[]{:S(2)}) collective-permute-start(f32[64,512]{1,0:T(8,128)S(1)} %get-tuple-element.65.refs_0_), channel_id=1, source_target_pairs={{0,2},{1,3},{2,0},{3,1},{4,6},{5,7},{6,4},{7,5},{8,10},{9,11},{10,... | collective-permute-start | bytes 393224 | tf_op jit(solution)/shard_map/ppermute | solution.py:367
  5.0 4.7 %collective-permute-start = (f32[64,512]{1,0:T(8,128)S(1)}, f32[64,512]{1,0:T(8,128)S(1)}, u32[]{:S(2)}, u32[]{:S(2)}) collective-permute-start(f32[64,512]{1,0:T(8,128)S(1)} %get-tuple-element.65.refs_0_), channel_id=1, source_target_pairs={{0,1},{1,0},{2,3},{3,2},{4,5},{5,4},{6,7},{7,6},{8,9},{9,8},{10,11... | collective-permute-start | bytes 393224 | tf_op jit(solution)/shard_map/ppermute | solution.py:367
  9.1 12.2 %copy-start = (f32[1,384,1536]{2,1,0:T(8,128)S(1)}, f32[1,384,1536]{2,1,0:T(8,128)}, u32[]{:S(2)}) copy-start(f32[1,384,1536]{2,1,0:T(8,128)} %param.33) | copy-start | bytes 7077892
  9.1 16.1 %copy-start.5 = (f32[1,384,1536]{2,1,0:T(8,128)S(1)}, f32[1,384,1536]{2,1,0:T(8,128)}, u32[]{:S(2)}) copy-start(f32[1,384,1536]{2,1,0:T(8,128)} %param.34) | copy-start | bytes 7077892
  9.1 1.6 %collective-permute-start.2 = (f32[64,512]{1,0:T(8,128)S(1)}, f32[64,512]{1,0:T(8,128)S(1)}, u32[]{:S(2)}, u32[]{:S(2)}) collective-permute-start(f32[64,512]{1,0:T(8,128)S(1)} %collective-permute-done.1.refs_2_), channel_id=1, source_target_pairs={{0,1},{1,0},{2,3},{3,2},{4,5},{5,4},{6,7},{7,6},{8,9},{9,8},{10,11... | collective-permute-start | bytes 393224 | tf_op jit(solution)/shard_map/ppermute | solution.py:367
  13.2 1.8 %collective-permute-start.3 = (f32[2,32,1536]{2,1,0:T(8,128)S(1)}, f32[2,32,1536]{2,1,0:T(8,128)S(1)}, u32[]{:S(2)}, u32[]{:S(2)}) collective-permute-start(f32[2,32,1536]{2,1,0:T(8,128)S(1)} %get-tuple-element.63), channel_id=1, source_target_pairs={{0,1},{1,0},{2,3},{3,2},{4,5},{5,4},{6,7},{7,6},{8,9},{9,8},{10,11... | collective-permute-start | bytes 1179656 | tf_op jit(solution)/shard_map/ppermute | solution.py:367
  15.0 7.0 %collective-permute-start.6 = (f32[32,768]{1,0:T(8,128)S(1)}, f32[32,768]{1,0:T(8,128)S(1)}, u32[]{:S(2)}, u32[]{:S(2)}) collective-permute-start(f32[32,768]{1,0:T(8,128)S(1)} %get-tuple-element.74), channel_id=1, source_target_pairs={{4,0},{5,1},{6,2},{7,3},{8,4},{9,5},{10,6},{11,7},{12,8},{13,9},{1... | collective-permute-start | bytes 294920 | tf_op jit(solution)/shard_map/ppermute | solution.py:413
  16.3 5.7 %collective-permute-start.7 = (f32[32,768]{1,0:T(8,128)S(1)}, f32[32,768]{1,0:T(8,128)S(1)}, u32[]{:S(2)}, u32[]{:S(2)}) collective-permute-start(f32[32,768]{1,0:T(8,128)S(1)} %get-tuple-element.75), channel_id=1, source_target_pairs={{0,2},{1,3},{2,0},{3,1},{4,6},{5,7},{6,4},{7,5},{8,10},{9,11},{10,... | collective-permute-start | bytes 294920 | tf_op jit(solution)/shard_map/ppermute | solution.py:367
  17.3 7.9 %collective-permute-start.8 = (f32[32,768]{1,0:T(8,128)S(1)}, f32[32,768]{1,0:T(8,128)S(1)}, u32[]{:S(2)}, u32[]{:S(2)}) collective-permute-start(f32[32,768]{1,0:T(8,128)S(1)} %get-tuple-element.76), channel_id=1, source_target_pairs={{4,2},{5,3},{6,0},{7,1},{8,6},{9,7},{10,4},{11,5},{12,10},{13,11},... | collective-permute-start | bytes 294920 | tf_op jit(solution)/shard_map/ppermute | solution.py:413
  18.6 3.0 %collective-permute-start.5 = (f32[32,512]{1,0:T(8,128)S(1)}, f32[32,512]{1,0:T(8,128)S(1)}, u32[]{:S(2)}, u32[]{:S(2)}) collective-permute-start(f32[32,512]{1,0:T(8,128)S(1)} %get-tuple-element.70), channel_id=1, source_target_pairs={{0,1},{1,0},{2,3},{3,2},{4,5},{5,4},{6,7},{7,6},{8,9},{9,8},{10,11... | collective-permute-start | bytes 196616 | tf_op jit(solution)/shard_map/ppermute | solution.py:367
  19.9 1.4 %collective-permute-start.4 = (f32[32,384]{1,0:T(8,128)S(1)}, f32[32,384]{1,0:T(8,128)S(1)}, u32[]{:S(2)}, u32[]{:S(2)}) collective-permute-start(f32[32,384]{1,0:T(8,128)S(1)} %get-tuple-element.69), channel_id=1, source_target_pairs={{0,1},{1,0},{2,3},{3,2},{4,5},{5,4},{6,7},{7,6},{8,9},{9,8},{10,11... | collective-permute-start | bytes 147464 | tf_op jit(solution)/shard_map/ppermute | solution.py:367
  21.3 9.6 %collective-permute-start.10 = (f32[384,1536]{1,0:T(8,128)S(1)}, f32[384,1536]{1,0:T(8,128)S(1)}, u32[]{:S(2)}, u32[]{:S(2)}) collective-permute-start(f32[384,1536]{1,0:T(8,128)S(1)} %bitcast.44), channel_id=1, source_target_pairs={{0,1},{1,0},{2,3},{3,2},{4,5},{5,4},{6,7},{7,6},{8,9},{9,8},{10,11... | collective-permute-start | bytes 7077896 | tf_op jit(solution)/shard_map/ppermute | solution.py:367
  25.2 8.4 %collective-permute-start.13 = (f32[384,1536]{1,0:T(8,128)S(1)}, f32[384,1536]{1,0:T(8,128)S(1)}, u32[]{:S(2)}, u32[]{:S(2)}) collective-permute-start(f32[384,1536]{1,0:T(8,128)S(1)} %bitcast.70), channel_id=1, source_target_pairs={{0,1},{1,0},{2,3},{3,2},{4,5},{5,4},{6,7},{7,6},{8,9},{9,8},{10,11... | collective-permute-start | bytes 7077896 | tf_op jit(solution)/shard_map/ppermute | solution.py:367
  25.3 5.6 %collective-permute-start.11 = (f32[32,768]{1,0:T(8,128)S(1)}, f32[32,768]{1,0:T(8,128)S(1)}, u32[]{:S(2)}, u32[]{:S(2)}) collective-permute-start(f32[32,768]{1,0:T(8,128)S(1)} %shard_map.223.refs_4_.refs_5_), channel_id=1, source_target_pairs={{0,4},{1,5},{2,6},{3,7},{4,0},{5,1},{6,2},{7,3},{8,12},{9,13},{10,... | collective-permute-start | bytes 294920 | tf_op jit(solution)/shard_map/ppermute | solution.py:367
  27.5 6.1 %collective-permute-start.9 = (f32[32,768]{1,0:T(8,128)S(1)}, f32[32,768]{1,0:T(8,128)S(1)}, u32[]{:S(2)}, u32[]{:S(2)}) collective-permute-start(f32[32,768]{1,0:T(8,128)S(1)} %shard_map.223.refs_4_.refs_5_), channel_id=1, source_target_pairs={{0,6},{1,7},{2,4},{3,5},{4,2},{5,3},{6,0},{7,1},{8,14},{9,15},{10,... | collective-permute-start | bytes 294920 | tf_op jit(solution)/shard_map/ppermute | solution.py:367
  30.9 2.7 %copy-start.1 = (f32[1,384,1536]{2,1,0:T(8,128)S(1)}, f32[1,384,1536]{2,1,0:T(8,128)}, u32[]{:S(2)}) copy-start(f32[1,384,1536]{2,1,0:T(8,128)} %param.35) | copy-start | bytes 7077892
  33.6 7.4 %collective-permute-start.16 = (f32[384,1536]{1,0:T(8,128)S(1)}, f32[384,1536]{1,0:T(8,128)S(1)}, u32[]{:S(2)}, u32[]{:S(2)}) collective-permute-start(f32[384,1536]{1,0:T(8,128)S(1)} %bitcast.51), channel_id=1, source_target_pairs={{0,1},{1,0},{2,3},{3,2},{4,5},{5,4},{6,7},{7,6},{8,9},{9,8},{10,11... | collective-permute-start | bytes 7077896 | tf_op jit(solution)/shard_map/ppermute | solution.py:367
  33.7 5.7 %collective-permute-start.14 = (f32[32,768]{1,0:T(8,128)S(1)}, f32[32,768]{1,0:T(8,128)S(1)}, u32[]{:S(2)}, u32[]{:S(2)}) collective-permute-start(f32[32,768]{1,0:T(8,128)S(1)} %shard_map.225.refs_5_), channel_id=1, source_target_pairs={{0,2},{1,3},{2,0},{3,1},{4,8},{5,9},{6,10},{7,11},{8,4},{9,5},{10,... | collective-permute-start | bytes 294920 | tf_op jit(solution)/shard_map/ppermute | solution.py:367
  34.7 6.4 %collective-permute-start.12 = (f32[32,768]{1,0:T(8,128)S(1)}, f32[32,768]{1,0:T(8,128)S(1)}, u32[]{:S(2)}, u32[]{:S(2)}) collective-permute-start(f32[32,768]{1,0:T(8,128)S(1)} %shard_map.225.refs_5_), channel_id=1, source_target_pairs={{0,2},{1,3},{2,0},{3,1},{4,10},{5,11},{6,8},{7,9},{8,6},{9,7},{10,... | collective-permute-start | bytes 294920 | tf_op jit(solution)/shard_map/ppermute | solution.py:367
  39.4 1.9 %copy-start.3 = (f32[1,512,1536]{2,1,0:T(8,128)S(1)}, f32[1,512,1536]{2,1,0:T(8,128)}, u32[]{:S(2)}) copy-start(f32[1,512,1536]{2,1,0:T(8,128)} %param.32) | copy-start | bytes 9437188
  41.3 14.5 %collective-permute-start.20 = (f32[512,1536]{1,0:T(8,128)S(1)}, f32[512,1536]{1,0:T(8,128)S(1)}, u32[]{:S(2)}, u32[]{:S(2)}) collective-permute-start(f32[512,1536]{1,0:T(8,128)S(1)} %bitcast.63), channel_id=1, source_target_pairs={{0,1},{1,0},{2,3},{3,2},{4,5},{5,4},{6,7},{7,6},{8,9},{9,8},{10,11... | collective-permute-start | bytes 9437192 | tf_op jit(solution)/shard_map/ppermute | solution.py:367
  41.3 6.3 %collective-permute-start.17 = (f32[32,768]{1,0:T(8,128)S(1)}, f32[32,768]{1,0:T(8,128)S(1)}, u32[]{:S(2)}, u32[]{:S(2)}) collective-permute-start(f32[32,768]{1,0:T(8,128)S(1)} %shard_map.227.refs_5_), channel_id=1, source_target_pairs={{0,4},{1,5},{2,6},{3,7},{4,0},{5,1},{6,2},{7,3},{8,12},{9,13},{10,... | collective-permute-start | bytes 294920 | tf_op jit(solution)/shard_map/ppermute | solution.py:367
  44.1 6.1 %collective-permute-start.15 = (f32[32,768]{1,0:T(8,128)S(1)}, f32[32,768]{1,0:T(8,128)S(1)}, u32[]{:S(2)}, u32[]{:S(2)}) collective-permute-start(f32[32,768]{1,0:T(8,128)S(1)} %shard_map.227.refs_5_), channel_id=1, source_target_pairs={{0,6},{1,7},{2,4},{3,5},{4,2},{5,3},{6,0},{7,1},{8,14},{9,15},{10,... | collective-permute-start | bytes 294920 | tf_op jit(solution)/shard_map/ppermute | solution.py:367
  50.2 4.7 %collective-permute-start.18 = (f32[32,768]{1,0:T(8,128)S(1)}, f32[32,768]{1,0:T(8,128)S(1)}, u32[]{:S(2)}, u32[]{:S(2)}) collective-permute-start(f32[32,768]{1,0:T(8,128)S(1)} %shard_map.229.refs_0_), channel_id=1, source_target_pairs={{0,2},{1,3},{2,0},{3,1},{4,6},{5,7},{6,4},{7,5},{8,10},{9,11},{10,... | collective-permute-start | bytes 294920 | tf_op jit(solution)/shard_map/ppermute | solution.py:367
  52.0 3.8 %copy-start.4 = (f32[1,512,1536]{2,1,0:T(8,128)S(1)}, f32[1,512,1536]{2,1,0:T(8,128)}, u32[]{:S(2)}) copy-start(f32[1,512,1536]{2,1,0:T(8,128)} %param.31) | copy-start | bytes 9437188
  55.7 7.7 %collective-permute-start.23 = (f32[512,1536]{1,0:T(8,128)S(1)}, f32[512,1536]{1,0:T(8,128)S(1)}, u32[]{:S(2)}, u32[]{:S(2)}) collective-permute-start(f32[512,1536]{1,0:T(8,128)S(1)} %bitcast.67), channel_id=1, source_target_pairs={{0,1},{1,0},{2,3},{3,2},{4,5},{5,4},{6,7},{7,6},{8,9},{9,8},{10,11... | collective-permute-start | bytes 9437192 | tf_op jit(solution)/shard_map/ppermute | solution.py:367
  55.8 5.5 %collective-permute-start.21 = (f32[32,768]{1,0:T(8,128)S(1)}, f32[32,768]{1,0:T(8,128)S(1)}, u32[]{:S(2)}, u32[]{:S(2)}) collective-permute-start(f32[32,768]{1,0:T(8,128)S(1)} %shard_map.231.refs_4_.refs_5_), channel_id=1, source_target_pairs={{0,4},{1,5},{2,6},{3,7},{4,0},{5,1},{6,2},{7,3},{8,12},{9,13},{10,... | collective-permute-start | bytes 294920 | tf_op jit(solution)/shard_map/ppermute | solution.py:367
  57.6 5.8 %collective-permute-start.19 = (f32[32,768]{1,0:T(8,128)S(1)}, f32[32,768]{1,0:T(8,128)S(1)}, u32[]{:S(2)}, u32[]{:S(2)}) collective-permute-start(f32[32,768]{1,0:T(8,128)S(1)} %shard_map.231.refs_4_.refs_5_), channel_id=1, source_target_pairs={{0,6},{1,7},{2,4},{3,5},{4,2},{5,3},{6,0},{7,1},{8,14},{9,15},{10,... | collective-permute-start | bytes 294920 | tf_op jit(solution)/shard_map/ppermute | solution.py:367
  61.3 2.2 %copy-start.2 = (f32[1,512,2048]{2,1,0:T(8,128)S(1)}, f32[1,512,2048]{2,1,0:T(8,128)}, u32[]{:S(2)}) copy-start(f32[1,512,2048]{2,1,0:T(8,128)} %param.30) | copy-start | bytes 12582916
  63.5 26.7 %collective-permute-start.28 = (f32[512,2048]{1,0:T(8,128)S(1)}, f32[512,2048]{1,0:T(8,128)S(1)}, u32[]{:S(2)}, u32[]{:S(2)}) collective-permute-start(f32[512,2048]{1,0:T(8,128)S(1)} %bitcast.59), channel_id=1, source_target_pairs={{0,1},{1,0},{2,3},{3,2},{4,5},{5,4},{6,7},{7,6},{8,9},{9,8},{10,11... | collective-permute-start | bytes 12582920 | tf_op jit(solution)/shard_map/ppermute | solution.py:367
  63.6 5.7 %collective-permute-start.24 = (f32[32,768]{1,0:T(8,128)S(1)}, f32[32,768]{1,0:T(8,128)S(1)}, u32[]{:S(2)}, u32[]{:S(2)}) collective-permute-start(f32[32,768]{1,0:T(8,128)S(1)} %shard_map.233.refs_5_), channel_id=1, source_target_pairs={{0,2},{1,3},{2,0},{3,1},{4,8},{5,9},{6,10},{7,11},{8,4},{9,5},{10,... | collective-permute-start | bytes 294920 | tf_op jit(solution)/shard_map/ppermute | solution.py:367
  64.8 6.1 %collective-permute-start.22 = (f32[32,768]{1,0:T(8,128)S(1)}, f32[32,768]{1,0:T(8,128)S(1)}, u32[]{:S(2)}, u32[]{:S(2)}) collective-permute-start(f32[32,768]{1,0:T(8,128)S(1)} %shard_map.233.refs_5_), channel_id=1, source_target_pairs={{0,2},{1,3},{2,0},{3,1},{4,10},{5,11},{6,8},{7,9},{8,6},{9,7},{10,... | collective-permute-start | bytes 294920 | tf_op jit(solution)/shard_map/ppermute | solution.py:367
  70.9 6.9 %collective-permute-start.26 = (f32[32,768]{1,0:T(8,128)S(1)}, f32[32,768]{1,0:T(8,128)S(1)}, u32[]{:S(2)}, u32[]{:S(2)}) collective-permute-start(f32[32,768]{1,0:T(8,128)S(1)} %shard_map.235.refs_5_), channel_id=1, source_target_pairs={{0,4},{1,5},{2,6},{3,7},{4,0},{5,1},{6,2},{7,3},{8,12},{9,13},{10,... | collective-permute-start | bytes 294920 | tf_op jit(solution)/shard_map/ppermute | solution.py:367
  74.8 5.5 %collective-permute-start.25 = (f32[32,768]{1,0:T(8,128)S(1)}, f32[32,768]{1,0:T(8,128)S(1)}, u32[]{:S(2)}, u32[]{:S(2)}) collective-permute-start(f32[32,768]{1,0:T(8,128)S(1)} %shard_map.235.refs_5_), channel_id=1, source_target_pairs={{0,6},{1,7},{2,4},{3,5},{4,2},{5,3},{6,0},{7,1},{8,14},{9,15},{10,... | collective-permute-start | bytes 294920 | tf_op jit(solution)/shard_map/ppermute | solution.py:367
  81.2 7.9 %collective-permute-start.30 = (f32[32,768]{1,0:T(8,128)S(1)}, f32[32,768]{1,0:T(8,128)S(1)}, u32[]{:S(2)}, u32[]{:S(2)}) collective-permute-start(f32[32,768]{1,0:T(8,128)S(1)} %shard_map.237.refs_0_), channel_id=1, source_target_pairs={{0,2},{1,3},{2,0},{3,1},{4,6},{5,7},{6,4},{7,5},{8,10},{9,11},{10,... | collective-permute-start | bytes 294920 | tf_op jit(solution)/shard_map/ppermute | solution.py:367
  82.2 7.9 %collective-permute-start.29 = (f32[32,768]{1,0:T(8,128)S(1)}, f32[32,768]{1,0:T(8,128)S(1)}, u32[]{:S(2)}, u32[]{:S(2)}) collective-permute-start(f32[32,768]{1,0:T(8,128)S(1)} %shard_map.237.refs_0_), channel_id=1, source_target_pairs={{0,4},{1,5},{2,6},{3,7},{4,8},{5,9},{6,10},{7,11},{8,12},{9,13},{1... | collective-permute-start | bytes 294920 | tf_op jit(solution)/shard_map/ppermute | solution.py:413
  84.7 5.5 %collective-permute-start.27 = (f32[32,768]{1,0:T(8,128)S(1)}, f32[32,768]{1,0:T(8,128)S(1)}, u32[]{:S(2)}, u32[]{:S(2)}) collective-permute-start(f32[32,768]{1,0:T(8,128)S(1)} %shard_map.237.refs_0_), channel_id=1, source_target_pairs={{0,6},{1,7},{2,4},{3,5},{4,10},{5,11},{6,8},{7,9},{8,14},{9,15},{1... | collective-permute-start | bytes 294920 | tf_op jit(solution)/shard_map/ppermute | solution.py:413
  90.2 2.5 %copy-start.9 = (f32[1,384,64]{1,2,0:T(8,128)S(1)}, f32[1,384,64]{1,2,0:T(8,128)}, u32[]{:S(2)}) copy-start(f32[1,384,64]{1,2,0:T(8,128)} %param.27) | copy-start | bytes 294916
  90.2 2.4 %copy-start.10 = (f32[1,384,64]{1,2,0:T(8,128)S(1)}, f32[1,384,64]{1,2,0:T(8,128)}, u32[]{:S(2)}) copy-start(f32[1,384,64]{1,2,0:T(8,128)} %param.28) | copy-start | bytes 294916
  90.3 2.4 %copy-start.11 = (f32[1,384,64]{1,2,0:T(8,128)S(1)}, f32[1,384,64]{1,2,0:T(8,128)}, u32[]{:S(2)}) copy-start(f32[1,384,64]{1,2,0:T(8,128)} %param.29) | copy-start | bytes 294916
  90.3 5.0 %collective-permute-start.31 = (f32[32,1024]{1,0:T(8,128)S(1)}, f32[32,1024]{1,0:T(8,128)S(1)}, u32[]{:S(2)}, u32[]{:S(2)}) collective-permute-start(f32[32,1024]{1,0:T(8,128)S(1)} %shard_map.241.refs_0_), channel_id=1, source_target_pairs={{0,2},{1,3},{2,0},{3,1},{4,6},{5,7},{6,4},{7,5},{8,10},{9,11},{10,... | collective-permute-start | bytes 393224 | tf_op jit(solution)/shard_map/ppermute | solution.py:367
  91.4 1.3 %collective-permute-start.32 = (f32[32,384]{1,0:T(8,128)S(1)}, f32[32,384]{1,0:T(8,128)S(1)}, u32[]{:S(2)}, u32[]{:S(2)}) collective-permute-start(f32[32,384]{1,0:T(8,128)S(1)} %get-tuple-element.92), channel_id=1, source_target_pairs={{0,1},{1,0},{2,3},{3,2},{4,5},{5,4},{6,7},{7,6},{8,9},{9,8},{10,11... | collective-permute-start | bytes 147464 | tf_op jit(solution)/shard_map/ppermute | solution.py:367
  95.4 2.7 %copy-start.6 = (f32[1,512,64]{1,2,0:T(8,128)S(1)}, f32[1,512,64]{1,2,0:T(8,128)}, u32[]{:S(2)}) copy-start(f32[1,512,64]{1,2,0:T(8,128)} %param.24) | copy-start | bytes 393220
  95.4 2.7 %copy-start.7 = (f32[1,512,64]{1,2,0:T(8,128)S(1)}, f32[1,512,64]{1,2,0:T(8,128)}, u32[]{:S(2)}) copy-start(f32[1,512,64]{1,2,0:T(8,128)} %param.25) | copy-start | bytes 393220
  95.4 2.7 %copy-start.8 = (f32[1,512,64]{1,2,0:T(8,128)S(1)}, f32[1,512,64]{1,2,0:T(8,128)}, u32[]{:S(2)}) copy-start(f32[1,512,64]{1,2,0:T(8,128)} %param.26) | copy-start | bytes 393220
  96.7 1.3 %collective-permute-start.33 = (f32[32,512]{1,0:T(8,128)S(1)}, f32[32,512]{1,0:T(8,128)S(1)}, u32[]{:S(2)}, u32[]{:S(2)}) collective-permute-start(f32[32,512]{1,0:T(8,128)S(1)} %get-tuple-element.99), channel_id=1, source_target_pairs={{0,1},{1,0},{2,3},{3,2},{4,5},{5,4},{6,7},{7,6},{8,9},{9,8},{10,11... | collective-permute-start | bytes 196616 | tf_op jit(solution)/shard_map/ppermute | solution.py:367

commit v9 on v8

--- a/solution.py
+++ b/solution.py
@@ -306,7 +306,8 @@
     store_rows(out, plus(times_rows(value, *rows, columns=columns(value.shape[1])), sofar))
 
 
-def coupled_kernel(columns, final, load, piece, rows, sofar, out):
+def coupled_kernel(columns, final, load, pair, rows, sofar, out):
+    even, odd = pair
     story = lax.axis_index("story")
 
     def finish(value):
@@ -322,7 +323,7 @@
 
     @pl.when(story > 0)
     def _():
-        value = piece[0][...]
+        value = jnp.where(lax.rem(story, 2) == 1, even[...], odd[...])
         finish(plus(times_rows(value, *rows, columns=columns(value.shape[1])), sofar))
 
 
@@ -525,6 +526,9 @@
         if k == max(mv.stories - 3, 0):
             inverse_other = others(interior_inverse[0], [below_other, face])
             came[-1], below_other = lax.optimization_barrier([came[-1], below_other])
+        if k == 0:
+            late, came[0] = lax.optimization_barrier([face, came[0]])
+            odd = mv.gather_story(late, 1)
         (face,) = call(
             functools.partial(step_kernel, from_chip(len(came), len(came) - 1), k),
             shape,
@@ -533,21 +537,22 @@
         )
 
     here = mv.gather_chips(face)
-    came = mv.pieces([mv.shift(face, 1, j) for j in range(mv.chips)])
-    came[-1], inverse_other = lax.optimization_barrier([came[-1], inverse_other])
+    face, *odd = lax.optimization_barrier([face, *odd])
+    even = mv.gather_story(face, 0)
+    even[-1], inverse_other = lax.optimization_barrier([even[-1], inverse_other])
     rows = [couple_above[0], above_other]
     sofar = []
     for j, piece in enumerate(here):
         kernel = functools.partial(part_kernel, from_chip(len(here), j), None)
         sofar = call(kernel, shape_int, [piece], rows, sofar, cost=4 << 20)
     rows = [couple_below[0], below_other]
-    for j, piece in enumerate(came):
-        final = j == len(came) - 1
+    for j, pair in enumerate(zip(even, odd)):
+        final = j == len(even) - 1
         sofar = call(
-            functools.partial(coupled_kernel, from_chip(len(came), j), final),
+            functools.partial(coupled_kernel, from_chip(len(even), j), final),
             shape_int,
             load_int_half if final else [],
-            [piece],
+            list(pair),
             rows,
             sofar,
             cost=4 << 20,

time: 100 us -> 101 us (1.010); the launches traced: 98.8 us -> 101 us
  waiting for transfers between devices: 43.4 us -> 46.7 us
  starting transfers between devices: 35.2 us -> 33.8 us
    ppermute x4 -> x2, starting transfers between devices: 8.36 us -> 2.57 us  [shift(): return lax.ppermute(value, AXES, pairs)]
    ppermute x30 -> x34, starting transfers between devices: 26.9 us -> 31.2 us  [permute(): return lax.ppermute(value, AXES, pairs)]
    ppermute x30 -> x34, waiting for transfers between devices: 39.9 us -> 43.2 us  [permute(): return lax.ppermute(value, AXES, pairs)]
    ppermute x4 -> x2, waiting for transfers between devices: 3.52 us -> 3.5 us  [shift(): return lax.ppermute(value, AXES, pairs)]
  transfers between devices with their start and end apart: 34 -> 36, of which waited for: 21 -> 23; matrix products, arithmetic and copies ran while one was open for 0% -> 0% of each run, Pallas kernels for 13% -> 13%
where the time goes in v9:
time: 101 us
  waiting for transfers between devices  46.7 us (46%)
  starting transfers between devices  33.8 us (33%)
  Pallas kernels  19.1 us (19%)
    ppermute x34, waiting for transfers between devices, permute(): return lax.ppermute(value, AXES, pairs)  43.2 us
    ppermute x34, starting transfers between devices, permute(): return lax.ppermute(value, AXES, pairs)  31.2 us
    pallas_call x27, Pallas kernels, call(): pl.pallas_call(body, in_specs=[VMEM] * len(flat), out_specs=[VMEM] * len(...  12.6 us
    pallas_call x1, Pallas kernels, staged(): pl.pallas_call(body, in_specs=[pl.BlockSpec(memory_space=pltpu.HBM)] * co...  4.08 us
    ppermute x2, waiting for transfers between devices, shift(): return lax.ppermute(value, AXES, pairs)  3.5 us
    ppermute x2, starting transfers between devices, shift(): return lax.ppermute(value, AXES, pairs)  2.57 us
    pallas_call x2, Pallas kernels, fetched(): pl.pallas_call(body, in_specs=[pl.BlockSpec(memory_space=pltpu.HBM)] * co...  2.48 us
  transfers between devices with their start and end apart: 36, of which 23 were waited for; matrix products, arithmetic and copies ran while one was open for 0% of the time, Pallas kernels for 13%

profile of v9, /device:TPU:0, one launch (start us, length us, event | category | flops | bytes accessed | tf_op | source)
XLA Modules:
  0.0 100.9 jit_solution(9635478564890616195)
XLA Ops:
  0.6 1.3 %shard_map.217 = (f32[64,512]{1,0:T(8,128)S(1)}, f32[64,128]{1,0:T(8,128)S(1)}) custom-call(s32[1,64]{1,0:T(1,128)} %bitcast.86, f32[1,512]{1,0:T(1,128)} %bitcast.85, f32[1,512]{1,0:T(1,128)} %refs_2_.1, f32[1,512]{1,0:T(1,128)} %refs_3_.1, f32[64,512]{1,0:T(8,128)} %bitcast.73, f32[64,512]{1,0:T(8,128)} %bitcast.75, f32[64,512]{1,0:T(8,128)} %bitcast.77), custom_call_target="tpu_custom_call" | custom-call | tf_op jit(solution)/shard_map/pallas_call | solution.py:180
  2.0 3.0 %collective-permute-start.1 = (f32[64,512]{1,0:T(8,128)S(1)}, f32[64,512]{1,0:T(8,128)S(1)}, u32[]{:S(2)}, u32[]{:S(2)}) collective-permute-start(f32[64,512]{1,0:T(8,128)S(1)} %get-tuple-element.70.refs_0_), channel_id=1, source_target_pairs={{0,2},{1,3},{2,0},{3,1},{4,6},{5,7},{6,4},{7,5},{8,10},{9,11},{10,... | collective-permute-start | bytes 393224 | tf_op jit(solution)/shard_map/ppermute | solution.py:368
  5.0 4.1 %shard_map.218.refs_4_ = f32[512,5120]{1,0:T(8,128)S(1)} custom-call(f32[512,2048]{1,0:T(8,128)} %bitcast.58, f32[512,1536]{1,0:T(8,128)} %bitcast.62, f32[512,1536]{1,0:T(8,128)} %bitcast.66), custom_call_target="tpu_custom_call" | custom-call | tf_op jit(solution)/shard_map/pallas_call | solution.py:128
  9.7 1.0 collective-permute-done.2.refs_3_
  10.7 2.5 %shard_map.219 = (f32[2,32,1536]{2,1,0:T(8,128)S(1)}, f32[2,32,1536]{2,1,0:T(8,128)S(1)}) custom-call(f32[64,512]{1,0:T(8,128)S(1)} %get-tuple-element.70.refs_0_, f32[64,512]{1,0:T(8,128)S(1)} %collective-permute-done.refs_1_, f32[64,512]{1,0:T(8,128)S(1)} %collective-permute-done.1.refs_2_, f32[64,512]{1,0:T(8,128)S(1)} %collective-permute-done.2.refs_3_, ...), custom_call_target="tpu_custom_call" | custom-call | tf_op jit(solution)/shard_map/pallas_call | solution.py:91
  13.6 1.4 %collective-permute-done.3.refs_1_ = f32[2,32,1536]{2,1,0:T(8,128)S(1)} collective-permute-done((f32[2,32,1536]{2,1,0:T(8,128)S(1)}, f32[2,32,1536]{2,1,0:T(8,128)S(1)}, u32[]{:S(2)}, u32[]{:S(2)}) %collective-permute-start.3) | collective-permute-done | bytes 393248 | tf_op jit(solution)/shard_map/ppermute | solution.py:368
  15.0 1.3 %collective-permute-start.6 = (f32[32,768]{1,0:T(8,128)S(1)}, f32[32,768]{1,0:T(8,128)S(1)}, u32[]{:S(2)}, u32[]{:S(2)}) collective-permute-start(f32[32,768]{1,0:T(8,128)S(1)} %get-tuple-element.79), channel_id=1, source_target_pairs={{4,0},{5,1},{6,2},{7,3},{8,4},{9,5},{10,6},{11,7},{12,8},{13,9},{1... | collective-permute-start | bytes 294920 | tf_op jit(solution)/shard_map/ppermute | solution.py:414
  16.3 1.0 collective-permute-start.7
  17.3 1.3 %collective-permute-start.8 = (f32[32,768]{1,0:T(8,128)S(1)}, f32[32,768]{1,0:T(8,128)S(1)}, u32[]{:S(2)}, u32[]{:S(2)}) collective-permute-start(f32[32,768]{1,0:T(8,128)S(1)} %get-tuple-element.81), channel_id=1, source_target_pairs={{4,2},{5,3},{6,0},{7,1},{8,6},{9,7},{10,4},{11,5},{12,10},{13,11},... | collective-permute-start | bytes 294920 | tf_op jit(solution)/shard_map/ppermute | solution.py:414
  18.7 1.2 %shard_map.222 = (f32[32,384]{1,0:T(8,128)S(1)}, f32[32,384]{1,0:T(8,128)S(1)}) custom-call(f32[1,384]{1,0:T(1,128)} %refs_0_.1, f32[1,384]{1,0:T(1,128)} %refs_1_.1, f32[64,384]{1,0:T(8,128)} %bitcast.79, f32[64,384]{1,0:T(8,128)} %bitcast.81, f32[64,384]{1,0:T(8,128)} %bitcast.83, f32[64,128]{1,0:T(8,128)S(1)} %get-tuple-element.73.refs_5_), custom_call_target="tpu_custom_call" | custom-call | tf_op jit(solution)/shard_map/pallas_call | solution.py:180
  20.4 0.9 collective-permute-done.4.refs_1_
  22.0 3.2 %collective-permute-done.8.refs_5_ = f32[32,768]{1,0:T(8,128)S(1)} collective-permute-done((f32[32,768]{1,0:T(8,128)S(1)}, f32[32,768]{1,0:T(8,128)S(1)}, u32[]{:S(2)}, u32[]{:S(2)}) %collective-permute-start.8) | collective-permute-done | bytes 98336 | tf_op jit(solution)/shard_map/ppermute | solution.py:414
  25.3 2.3 %collective-permute-start.11 = (f32[32,768]{1,0:T(8,128)S(1)}, f32[32,768]{1,0:T(8,128)S(1)}, u32[]{:S(2)}, u32[]{:S(2)}) collective-permute-start(f32[32,768]{1,0:T(8,128)S(1)} %shard_map.223.refs_4_.refs_5_), channel_id=1, source_target_pairs={{0,4},{1,5},{2,6},{3,7},{4,0},{5,1},{6,2},{7,3},{8,12},{9,13},{10,... | collective-permute-start | bytes 294920 | tf_op jit(solution)/shard_map/ppermute | solution.py:368
  28.2 2.7 %collective-permute-done.11.refs_0_ = f32[32,768]{1,0:T(8,128)S(1)} collective-permute-done((f32[32,768]{1,0:T(8,128)S(1)}, f32[32,768]{1,0:T(8,128)S(1)}, u32[]{:S(2)}, u32[]{:S(2)}) %collective-permute-start.11) | collective-permute-done | bytes 98336 | tf_op jit(solution)/shard_map/ppermute | solution.py:368
  30.9 2.7 %collective-permute-done.9.refs_0_ = f32[32,768]{1,0:T(8,128)S(1)} collective-permute-done((f32[32,768]{1,0:T(8,128)S(1)}, f32[32,768]{1,0:T(8,128)S(1)}, u32[]{:S(2)}, u32[]{:S(2)}) %collective-permute-start.9) | collective-permute-done | bytes 98336 | tf_op jit(solution)/shard_map/ppermute | solution.py:368
  33.7 1.0 collective-permute-start.14
  34.7 1.1 %collective-permute-start.12 = (f32[32,768]{1,0:T(8,128)S(1)}, f32[32,768]{1,0:T(8,128)S(1)}, u32[]{:S(2)}, u32[]{:S(2)}) collective-permute-start(f32[32,768]{1,0:T(8,128)S(1)} %shard_map.225.refs_5_), channel_id=1, source_target_pairs={{0,2},{1,3},{2,0},{3,1},{4,10},{5,11},{6,8},{7,9},{8,6},{9,7},{10,... | collective-permute-start | bytes 294920 | tf_op jit(solution)/shard_map/ppermute | solution.py:368
  35.8 3.6 %collective-permute-done.14.refs_0_ = f32[32,768]{1,0:T(8,128)S(1)} collective-permute-done((f32[32,768]{1,0:T(8,128)S(1)}, f32[32,768]{1,0:T(8,128)S(1)}, u32[]{:S(2)}, u32[]{:S(2)}) %collective-permute-start.14) | collective-permute-done | bytes 98336 | tf_op jit(solution)/shard_map/ppermute | solution.py:368
  39.4 1.7 %collective-permute-done.12.refs_0_ = f32[32,768]{1,0:T(8,128)S(1)} collective-permute-done((f32[32,768]{1,0:T(8,128)S(1)}, f32[32,768]{1,0:T(8,128)S(1)}, u32[]{:S(2)}, u32[]{:S(2)}) %collective-permute-start.12) | collective-permute-done | bytes 98336 | tf_op jit(solution)/shard_map/ppermute | solution.py:368
  41.3 2.9 %collective-permute-start.17 = (f32[32,768]{1,0:T(8,128)S(1)}, f32[32,768]{1,0:T(8,128)S(1)}, u32[]{:S(2)}, u32[]{:S(2)}) collective-permute-start(f32[32,768]{1,0:T(8,128)S(1)} %shard_map.227.refs_5_), channel_id=1, source_target_pairs={{0,4},{1,5},{2,6},{3,7},{4,0},{5,1},{6,2},{7,3},{8,12},{9,13},{10,... | collective-permute-start | bytes 294920 | tf_op jit(solution)/shard_map/ppermute | solution.py:368
  44.8 2.7 %collective-permute-done.17.refs_0_ = f32[32,768]{1,0:T(8,128)S(1)} collective-permute-done((f32[32,768]{1,0:T(8,128)S(1)}, f32[32,768]{1,0:T(8,128)S(1)}, u32[]{:S(2)}, u32[]{:S(2)}) %collective-permute-start.17) | collective-permute-done | bytes 98336 | tf_op jit(solution)/shard_map/ppermute | solution.py:368
  47.5 2.7 %collective-permute-done.15.refs_0_ = f32[32,768]{1,0:T(8,128)S(1)} collective-permute-done((f32[32,768]{1,0:T(8,128)S(1)}, f32[32,768]{1,0:T(8,128)S(1)}, u32[]{:S(2)}, u32[]{:S(2)}) %collective-permute-start.15) | collective-permute-done | bytes 98336 | tf_op jit(solution)/shard_map/ppermute | solution.py:368
  50.2 1.0 collective-permute-start.18
  52.0 2.9 %collective-permute-done.18.refs_0_ = f32[32,768]{1,0:T(8,128)S(1)} collective-permute-done((f32[32,768]{1,0:T(8,128)S(1)}, f32[32,768]{1,0:T(8,128)S(1)}, u32[]{:S(2)}, u32[]{:S(2)}) %collective-permute-start.18) | collective-permute-done | bytes 98336 | tf_op jit(solution)/shard_map/ppermute | solution.py:368
  55.8 1.8 %collective-permute-start.21 = (f32[32,768]{1,0:T(8,128)S(1)}, f32[32,768]{1,0:T(8,128)S(1)}, u32[]{:S(2)}, u32[]{:S(2)}) collective-permute-start(f32[32,768]{1,0:T(8,128)S(1)} %shard_map.231.refs_4_.refs_5_), channel_id=1, source_target_pairs={{0,4},{1,5},{2,6},{3,7},{4,0},{5,1},{6,2},{7,3},{8,12},{9,13},{10,... | collective-permute-start | bytes 294920 | tf_op jit(solution)/shard_map/ppermute | solution.py:368
  58.2 3.1 %collective-permute-done.21.refs_0_ = f32[32,768]{1,0:T(8,128)S(1)} collective-permute-done((f32[32,768]{1,0:T(8,128)S(1)}, f32[32,768]{1,0:T(8,128)S(1)}, u32[]{:S(2)}, u32[]{:S(2)}) %collective-permute-start.21) | collective-permute-done | bytes 98336 | tf_op jit(solution)/shard_map/ppermute | solution.py:368
  61.3 2.2 %collective-permute-done.19.refs_0_ = f32[32,768]{1,0:T(8,128)S(1)} collective-permute-done((f32[32,768]{1,0:T(8,128)S(1)}, f32[32,768]{1,0:T(8,128)S(1)}, u32[]{:S(2)}, u32[]{:S(2)}) %collective-permute-start.19) | collective-permute-done | bytes 98336 | tf_op jit(solution)/shard_map/ppermute | solution.py:368
  63.6 1.2 %collective-permute-start.24 = (f32[32,768]{1,0:T(8,128)S(1)}, f32[32,768]{1,0:T(8,128)S(1)}, u32[]{:S(2)}, u32[]{:S(2)}) collective-permute-start(f32[32,768]{1,0:T(8,128)S(1)} %shard_map.233.refs_5_), channel_id=1, source_target_pairs={{0,2},{1,3},{2,0},{3,1},{4,8},{5,9},{6,10},{7,11},{8,4},{9,5},{10,... | collective-permute-start | bytes 294920 | tf_op jit(solution)/shard_map/ppermute | solution.py:368
  64.8 0.9 collective-permute-start.22
  65.7 3.6 %collective-permute-done.24.refs_0_ = f32[32,768]{1,0:T(8,128)S(1)} collective-permute-done((f32[32,768]{1,0:T(8,128)S(1)}, f32[32,768]{1,0:T(8,128)S(1)}, u32[]{:S(2)}, u32[]{:S(2)}) %collective-permute-start.24) | collective-permute-done | bytes 98336 | tf_op jit(solution)/shard_map/ppermute | solution.py:368
  69.2 1.7 %collective-permute-done.22.refs_0_ = f32[32,768]{1,0:T(8,128)S(1)} collective-permute-done((f32[32,768]{1,0:T(8,128)S(1)}, f32[32,768]{1,0:T(8,128)S(1)}, u32[]{:S(2)}, u32[]{:S(2)}) %collective-permute-start.22) | collective-permute-done | bytes 98336 | tf_op jit(solution)/shard_map/ppermute | solution.py:368
  70.9 3.9 %collective-permute-start.26 = (f32[32,768]{1,0:T(8,128)S(1)}, f32[32,768]{1,0:T(8,128)S(1)}, u32[]{:S(2)}, u32[]{:S(2)}) collective-permute-start(f32[32,768]{1,0:T(8,128)S(1)} %shard_map.235.refs_5_), channel_id=1, source_target_pairs={{0,4},{1,5},{2,6},{3,7},{4,0},{5,1},{6,2},{7,3},{8,12},{9,13},{10,... | collective-permute-start | bytes 294920 | tf_op jit(solution)/shard_map/ppermute | solution.py:368
  75.3 2.5 %collective-permute-done.26.refs_0_ = f32[32,768]{1,0:T(8,128)S(1)} collective-permute-done((f32[32,768]{1,0:T(8,128)S(1)}, f32[32,768]{1,0:T(8,128)S(1)}, u32[]{:S(2)}, u32[]{:S(2)}) %collective-permute-start.26) | collective-permute-done | bytes 98336 | tf_op jit(solution)/shard_map/ppermute | solution.py:368
  78.6 1.2 %collective-permute-start.28 = (f32[32,768]{1,0:T(8,128)S(1)}, f32[32,768]{1,0:T(8,128)S(1)}, u32[]{:S(2)}, u32[]{:S(2)}) collective-permute-start(f32[32,768]{1,0:T(8,128)S(1)} %shard_map.235.refs_5_), channel_id=1, source_target_pairs={{0,2},{1,3},{2,0},{3,1},{4,10},{5,11},{6,8},{7,9},{8,6},{9,7},{10,... | collective-permute-start | bytes 294920 | tf_op jit(solution)/shard_map/ppermute | solution.py:368
  80.7 1.0 %shard_map.237.refs_0_ = f32[32,768]{1,0:T(8,128)S(1)} custom-call(f32[32,768]{1,0:T(8,128)S(1)} %collective-permute-done.25.refs_0_, f32[384,1536]{1,0:T(8,128)S(1)} %bitcast.57, f32[384,1536]{1,0:T(8,128)S(1)} %collective-permute-done.16.refs_2_, f32[32,768]{1,0:T(8,128)S(1)} %shard_map.236.refs_3_, f32[32,768]{1,0:T(8,128)S(1)} %shard_map.231.refs_4_.refs_5_, ...), custom_call_target="tpu_custom_call" | custom-call | tf_op jit(solution)/shard_map/pallas_call | solution.py:91
  81.7 0.9 collective-permute-start.32
  82.6 0.9 collective-permute-done.27.refs_1_
  83.5 1.7 %collective-permute-done.28.refs_3_ = f32[32,768]{1,0:T(8,128)S(1)} collective-permute-done((f32[32,768]{1,0:T(8,128)S(1)}, f32[32,768]{1,0:T(8,128)S(1)}, u32[]{:S(2)}, u32[]{:S(2)}) %collective-permute-start.28) | collective-permute-done | bytes 98336 | tf_op jit(solution)/shard_map/ppermute | solution.py:368
  85.2 1.5 %collective-permute-start.31 = (f32[32,768]{1,0:T(8,128)S(1)}, f32[32,768]{1,0:T(8,128)S(1)}, u32[]{:S(2)}, u32[]{:S(2)}) collective-permute-start(f32[32,768]{1,0:T(8,128)S(1)} %shard_map.237.refs_0_), channel_id=1, source_target_pairs={{0,4},{1,5},{2,6},{3,7},{4,0},{5,1},{6,2},{7,3},{8,12},{9,13},{10,... | collective-permute-start | bytes 294920 | tf_op jit(solution)/shard_map/ppermute | solution.py:368
  86.7 1.0 collective-permute-start.29
  87.7 1.0 %shard_map.238.refs_3_ = f32[32,1024]{1,0:T(8,128)S(1)} custom-call(f32[32,768]{1,0:T(8,128)S(1)} %shard_map.237.refs_0_, f32[512,1536]{1,0:T(8,128)S(1)} %bitcast.64, f32[512,1536]{1,0:T(8,128)S(1)} %collective-permute-done.20.refs_2_), custom_call_target="tpu_custom_call" | custom-call | bytes 4194304 | tf_op jit(solution)/shard_map/pallas_call | solution.py:91
  88.8 1.1 %shard_map.239.refs_4_ = f32[32,1024]{1,0:T(8,128)S(1)} custom-call(f32[32,768]{1,0:T(8,128)S(1)} %collective-permute-done.32.refs_0_, f32[512,1536]{1,0:T(8,128)S(1)} %bitcast.65, f32[512,1536]{1,0:T(8,128)S(1)} %collective-permute-done.20.refs_2_, f32[32,1024]{1,0:T(8,128)S(1)} %shard_map.238.refs_3_), custom_call_target="tpu_custom_call" | custom-call | bytes 4194304 | tf_op jit(solution)/shard_map/pallas_call | solution.py:91
  89.9 2.4 %collective-permute-done.29.refs_2_ = f32[32,768]{1,0:T(8,128)S(1)} collective-permute-done((f32[32,768]{1,0:T(8,128)S(1)}, f32[32,768]{1,0:T(8,128)S(1)}, u32[]{:S(2)}, u32[]{:S(2)}) %collective-permute-start.29) | collective-permute-done | bytes 98336 | tf_op jit(solution)/shard_map/ppermute | solution.py:368
  92.4 1.1 %collective-permute-start.33 = (f32[32,1024]{1,0:T(8,128)S(1)}, f32[32,1024]{1,0:T(8,128)S(1)}, u32[]{:S(2)}, u32[]{:S(2)}) collective-permute-start(f32[32,1024]{1,0:T(8,128)S(1)} %shard_map.241.refs_0_), channel_id=1, source_target_pairs={{0,2},{1,3},{2,0},{3,1},{4,6},{5,7},{6,4},{7,5},{8,10},{9,11},{10,... | collective-permute-start | bytes 393224 | tf_op jit(solution)/shard_map/ppermute | solution.py:368
  93.6 1.2 %collective-permute-done.34.refs_1_ = f32[32,384]{1,0:T(8,128)S(1)} collective-permute-done((f32[32,384]{1,0:T(8,128)S(1)}, f32[32,384]{1,0:T(8,128)S(1)}, u32[]{:S(2)}, u32[]{:S(2)}) %collective-permute-start.34) | collective-permute-done | bytes 49184 | tf_op jit(solution)/shard_map/ppermute | solution.py:368
  95.6 1.4 %shard_map.244.refs_3_ = f32[32,1024]{1,0:T(8,128)S(1)} custom-call(f32[32,1024]{1,0:T(8,128)S(1)} %shard_map.241.refs_0_, f32[512,2048]{1,0:T(8,128)S(1)} %bitcast.60, f32[512,2048]{1,0:T(8,128)S(1)} %collective-permute-done.30.refs_2_), custom_call_target="tpu_custom_call" | custom-call | bytes 4194304 | tf_op jit(solution)/shard_map/pallas_call | solution.py:91
  97.4 1.4 %shard_map.245 = (f32[32,512]{1,0:T(8,128)S(1)}, f32[32,512]{1,0:T(8,128)S(1)}) custom-call(f32[32,1024]{1,0:T(8,128)S(1)} %collective-permute-done.33.refs_0_, f32[512,2048]{1,0:T(8,128)S(1)} %bitcast.61, f32[512,2048]{1,0:T(8,128)S(1)} %collective-permute-done.30.refs_2_, f32[32,1024]{1,0:T(8,128)S(1)} %shard_map.244.refs_3_), custom_call_target="tpu_custom_call" | custom-call | tf_op jit(solution)/shard_map/pallas_call | solution.py:91
  98.9 1.2 %collective-permute-done.35.refs_1_ = f32[32,512]{1,0:T(8,128)S(1)} collective-permute-done((f32[32,512]{1,0:T(8,128)S(1)}, f32[32,512]{1,0:T(8,128)S(1)}, u32[]{:S(2)}, u32[]{:S(2)}) %collective-permute-start.35) | collective-permute-done | bytes 65568 | tf_op jit(solution)/shard_map/ppermute | solution.py:368
  (78 shorter events, 11.0 us)
Async XLA Ops:
  2.0 7.1 %collective-permute-start.1 = (f32[64,512]{1,0:T(8,128)S(1)}, f32[64,512]{1,0:T(8,128)S(1)}, u32[]{:S(2)}, u32[]{:S(2)}) collective-permute-start(f32[64,512]{1,0:T(8,128)S(1)} %get-tuple-element.70.refs_0_), channel_id=1, source_target_pairs={{0,2},{1,3},{2,0},{3,1},{4,6},{5,7},{6,4},{7,5},{8,10},{9,11},{10,... | collective-permute-start | bytes 393224 | tf_op jit(solution)/shard_map/ppermute | solution.py:368
  5.0 4.7 %collective-permute-start = (f32[64,512]{1,0:T(8,128)S(1)}, f32[64,512]{1,0:T(8,128)S(1)}, u32[]{:S(2)}, u32[]{:S(2)}) collective-permute-start(f32[64,512]{1,0:T(8,128)S(1)} %get-tuple-element.70.refs_0_), channel_id=1, source_target_pairs={{0,1},{1,0},{2,3},{3,2},{4,5},{5,4},{6,7},{7,6},{8,9},{9,8},{10,11... | collective-permute-start | bytes 393224 | tf_op jit(solution)/shard_map/ppermute | solution.py:368
  9.1 12.2 %copy-start = (f32[1,384,1536]{2,1,0:T(8,128)S(1)}, f32[1,384,1536]{2,1,0:T(8,128)}, u32[]{:S(2)}) copy-start(f32[1,384,1536]{2,1,0:T(8,128)} %param.33) | copy-start | bytes 7077892
  9.1 16.1 %copy-start.5 = (f32[1,384,1536]{2,1,0:T(8,128)S(1)}, f32[1,384,1536]{2,1,0:T(8,128)}, u32[]{:S(2)}) copy-start(f32[1,384,1536]{2,1,0:T(8,128)} %param.34) | copy-start | bytes 7077892
  9.1 1.6 %collective-permute-start.2 = (f32[64,512]{1,0:T(8,128)S(1)}, f32[64,512]{1,0:T(8,128)S(1)}, u32[]{:S(2)}, u32[]{:S(2)}) collective-permute-start(f32[64,512]{1,0:T(8,128)S(1)} %collective-permute-done.1.refs_2_), channel_id=1, source_target_pairs={{0,1},{1,0},{2,3},{3,2},{4,5},{5,4},{6,7},{7,6},{8,9},{9,8},{10,11... | collective-permute-start | bytes 393224 | tf_op jit(solution)/shard_map/ppermute | solution.py:368
  13.2 1.8 %collective-permute-start.3 = (f32[2,32,1536]{2,1,0:T(8,128)S(1)}, f32[2,32,1536]{2,1,0:T(8,128)S(1)}, u32[]{:S(2)}, u32[]{:S(2)}) collective-permute-start(f32[2,32,1536]{2,1,0:T(8,128)S(1)} %get-tuple-element.68), channel_id=1, source_target_pairs={{0,1},{1,0},{2,3},{3,2},{4,5},{5,4},{6,7},{7,6},{8,9},{9,8},{10,11... | collective-permute-start | bytes 1179656 | tf_op jit(solution)/shard_map/ppermute | solution.py:368
  15.0 7.0 %collective-permute-start.6 = (f32[32,768]{1,0:T(8,128)S(1)}, f32[32,768]{1,0:T(8,128)S(1)}, u32[]{:S(2)}, u32[]{:S(2)}) collective-permute-start(f32[32,768]{1,0:T(8,128)S(1)} %get-tuple-element.79), channel_id=1, source_target_pairs={{4,0},{5,1},{6,2},{7,3},{8,4},{9,5},{10,6},{11,7},{12,8},{13,9},{1... | collective-permute-start | bytes 294920 | tf_op jit(solution)/shard_map/ppermute | solution.py:414
  16.3 5.7 %collective-permute-start.7 = (f32[32,768]{1,0:T(8,128)S(1)}, f32[32,768]{1,0:T(8,128)S(1)}, u32[]{:S(2)}, u32[]{:S(2)}) collective-permute-start(f32[32,768]{1,0:T(8,128)S(1)} %get-tuple-element.80), channel_id=1, source_target_pairs={{0,2},{1,3},{2,0},{3,1},{4,6},{5,7},{6,4},{7,5},{8,10},{9,11},{10,... | collective-permute-start | bytes 294920 | tf_op jit(solution)/shard_map/ppermute | solution.py:368
  17.3 7.9 %collective-permute-start.8 = (f32[32,768]{1,0:T(8,128)S(1)}, f32[32,768]{1,0:T(8,128)S(1)}, u32[]{:S(2)}, u32[]{:S(2)}) collective-permute-start(f32[32,768]{1,0:T(8,128)S(1)} %get-tuple-element.81), channel_id=1, source_target_pairs={{4,2},{5,3},{6,0},{7,1},{8,6},{9,7},{10,4},{11,5},{12,10},{13,11},... | collective-permute-start | bytes 294920 | tf_op jit(solution)/shard_map/ppermute | solution.py:414
  18.6 3.0 %collective-permute-start.5 = (f32[32,512]{1,0:T(8,128)S(1)}, f32[32,512]{1,0:T(8,128)S(1)}, u32[]{:S(2)}, u32[]{:S(2)}) collective-permute-start(f32[32,512]{1,0:T(8,128)S(1)} %get-tuple-element.75), channel_id=1, source_target_pairs={{0,1},{1,0},{2,3},{3,2},{4,5},{5,4},{6,7},{7,6},{8,9},{9,8},{10,11... | collective-permute-start | bytes 196616 | tf_op jit(solution)/shard_map/ppermute | solution.py:368
  19.9 1.4 %collective-permute-start.4 = (f32[32,384]{1,0:T(8,128)S(1)}, f32[32,384]{1,0:T(8,128)S(1)}, u32[]{:S(2)}, u32[]{:S(2)}) collective-permute-start(f32[32,384]{1,0:T(8,128)S(1)} %get-tuple-element.74), channel_id=1, source_target_pairs={{0,1},{1,0},{2,3},{3,2},{4,5},{5,4},{6,7},{7,6},{8,9},{9,8},{10,11... | collective-permute-start | bytes 147464 | tf_op jit(solution)/shard_map/ppermute | solution.py:368
  21.3 9.6 %collective-permute-start.10 = (f32[384,1536]{1,0:T(8,128)S(1)}, f32[384,1536]{1,0:T(8,128)S(1)}, u32[]{:S(2)}, u32[]{:S(2)}) collective-permute-start(f32[384,1536]{1,0:T(8,128)S(1)} %bitcast.44), channel_id=1, source_target_pairs={{0,1},{1,0},{2,3},{3,2},{4,5},{5,4},{6,7},{7,6},{8,9},{9,8},{10,11... | collective-permute-start | bytes 7077896 | tf_op jit(solution)/shard_map/ppermute | solution.py:368
  25.2 8.4 %collective-permute-start.13 = (f32[384,1536]{1,0:T(8,128)S(1)}, f32[384,1536]{1,0:T(8,128)S(1)}, u32[]{:S(2)}, u32[]{:S(2)}) collective-permute-start(f32[384,1536]{1,0:T(8,128)S(1)} %bitcast.70), channel_id=1, source_target_pairs={{0,1},{1,0},{2,3},{3,2},{4,5},{5,4},{6,7},{7,6},{8,9},{9,8},{10,11... | collective-permute-start | bytes 7077896 | tf_op jit(solution)/shard_map/ppermute | solution.py:368
  25.3 5.6 %collective-permute-start.11 = (f32[32,768]{1,0:T(8,128)S(1)}, f32[32,768]{1,0:T(8,128)S(1)}, u32[]{:S(2)}, u32[]{:S(2)}) collective-permute-start(f32[32,768]{1,0:T(8,128)S(1)} %shard_map.223.refs_4_.refs_5_), channel_id=1, source_target_pairs={{0,4},{1,5},{2,6},{3,7},{4,0},{5,1},{6,2},{7,3},{8,12},{9,13},{10,... | collective-permute-start | bytes 294920 | tf_op jit(solution)/shard_map/ppermute | solution.py:368
  27.5 6.1 %collective-permute-start.9 = (f32[32,768]{1,0:T(8,128)S(1)}, f32[32,768]{1,0:T(8,128)S(1)}, u32[]{:S(2)}, u32[]{:S(2)}) collective-permute-start(f32[32,768]{1,0:T(8,128)S(1)} %shard_map.223.refs_4_.refs_5_), channel_id=1, source_target_pairs={{0,6},{1,7},{2,4},{3,5},{4,2},{5,3},{6,0},{7,1},{8,14},{9,15},{10,... | collective-permute-start | bytes 294920 | tf_op jit(solution)/shard_map/ppermute | solution.py:368
  30.9 2.7 %copy-start.1 = (f32[1,384,1536]{2,1,0:T(8,128)S(1)}, f32[1,384,1536]{2,1,0:T(8,128)}, u32[]{:S(2)}) copy-start(f32[1,384,1536]{2,1,0:T(8,128)} %param.35) | copy-start | bytes 7077892
  33.6 7.4 %collective-permute-start.16 = (f32[384,1536]{1,0:T(8,128)S(1)}, f32[384,1536]{1,0:T(8,128)S(1)}, u32[]{:S(2)}, u32[]{:S(2)}) collective-permute-start(f32[384,1536]{1,0:T(8,128)S(1)} %bitcast.51), channel_id=1, source_target_pairs={{0,1},{1,0},{2,3},{3,2},{4,5},{5,4},{6,7},{7,6},{8,9},{9,8},{10,11... | collective-permute-start | bytes 7077896 | tf_op jit(solution)/shard_map/ppermute | solution.py:368
  33.7 5.7 %collective-permute-start.14 = (f32[32,768]{1,0:T(8,128)S(1)}, f32[32,768]{1,0:T(8,128)S(1)}, u32[]{:S(2)}, u32[]{:S(2)}) collective-permute-start(f32[32,768]{1,0:T(8,128)S(1)} %shard_map.225.refs_5_), channel_id=1, source_target_pairs={{0,2},{1,3},{2,0},{3,1},{4,8},{5,9},{6,10},{7,11},{8,4},{9,5},{10,... | collective-permute-start | bytes 294920 | tf_op jit(solution)/shard_map/ppermute | solution.py:368
  34.7 6.4 %collective-permute-start.12 = (f32[32,768]{1,0:T(8,128)S(1)}, f32[32,768]{1,0:T(8,128)S(1)}, u32[]{:S(2)}, u32[]{:S(2)}) collective-permute-start(f32[32,768]{1,0:T(8,128)S(1)} %shard_map.225.refs_5_), channel_id=1, source_target_pairs={{0,2},{1,3},{2,0},{3,1},{4,10},{5,11},{6,8},{7,9},{8,6},{9,7},{10,... | collective-permute-start | bytes 294920 | tf_op jit(solution)/shard_map/ppermute | solution.py:368
  39.4 1.9 %copy-start.3 = (f32[1,512,1536]{2,1,0:T(8,128)S(1)}, f32[1,512,1536]{2,1,0:T(8,128)}, u32[]{:S(2)}) copy-start(f32[1,512,1536]{2,1,0:T(8,128)} %param.32) | copy-start | bytes 9437188
  41.3 14.5 %collective-permute-start.20 = (f32[512,1536]{1,0:T(8,128)S(1)}, f32[512,1536]{1,0:T(8,128)S(1)}, u32[]{:S(2)}, u32[]{:S(2)}) collective-permute-start(f32[512,1536]{1,0:T(8,128)S(1)} %bitcast.63), channel_id=1, source_target_pairs={{0,1},{1,0},{2,3},{3,2},{4,5},{5,4},{6,7},{7,6},{8,9},{9,8},{10,11... | collective-permute-start | bytes 9437192 | tf_op jit(solution)/shard_map/ppermute | solution.py:368
  41.3 6.3 %collective-permute-start.17 = (f32[32,768]{1,0:T(8,128)S(1)}, f32[32,768]{1,0:T(8,128)S(1)}, u32[]{:S(2)}, u32[]{:S(2)}) collective-permute-start(f32[32,768]{1,0:T(8,128)S(1)} %shard_map.227.refs_5_), channel_id=1, source_target_pairs={{0,4},{1,5},{2,6},{3,7},{4,0},{5,1},{6,2},{7,3},{8,12},{9,13},{10,... | collective-permute-start | bytes 294920 | tf_op jit(solution)/shard_map/ppermute | solution.py:368
  44.1 6.1 %collective-permute-start.15 = (f32[32,768]{1,0:T(8,128)S(1)}, f32[32,768]{1,0:T(8,128)S(1)}, u32[]{:S(2)}, u32[]{:S(2)}) collective-permute-start(f32[32,768]{1,0:T(8,128)S(1)} %shard_map.227.refs_5_), channel_id=1, source_target_pairs={{0,6},{1,7},{2,4},{3,5},{4,2},{5,3},{6,0},{7,1},{8,14},{9,15},{10,... | collective-permute-start | bytes 294920 | tf_op jit(solution)/shard_map/ppermute | solution.py:368
  50.2 4.7 %collective-permute-start.18 = (f32[32,768]{1,0:T(8,128)S(1)}, f32[32,768]{1,0:T(8,128)S(1)}, u32[]{:S(2)}, u32[]{:S(2)}) collective-permute-start(f32[32,768]{1,0:T(8,128)S(1)} %shard_map.229.refs_0_), channel_id=1, source_target_pairs={{0,2},{1,3},{2,0},{3,1},{4,6},{5,7},{6,4},{7,5},{8,10},{9,11},{10,... | collective-permute-start | bytes 294920 | tf_op jit(solution)/shard_map/ppermute | solution.py:368
  52.0 3.8 %copy-start.4 = (f32[1,512,1536]{2,1,0:T(8,128)S(1)}, f32[1,512,1536]{2,1,0:T(8,128)}, u32[]{:S(2)}) copy-start(f32[1,512,1536]{2,1,0:T(8,128)} %param.31) | copy-start | bytes 9437188
  55.7 7.7 %collective-permute-start.23 = (f32[512,1536]{1,0:T(8,128)S(1)}, f32[512,1536]{1,0:T(8,128)S(1)}, u32[]{:S(2)}, u32[]{:S(2)}) collective-permute-start(f32[512,1536]{1,0:T(8,128)S(1)} %bitcast.67), channel_id=1, source_target_pairs={{0,1},{1,0},{2,3},{3,2},{4,5},{5,4},{6,7},{7,6},{8,9},{9,8},{10,11... | collective-permute-start | bytes 9437192 | tf_op jit(solution)/shard_map/ppermute | solution.py:368
  55.8 5.5 %collective-permute-start.21 = (f32[32,768]{1,0:T(8,128)S(1)}, f32[32,768]{1,0:T(8,128)S(1)}, u32[]{:S(2)}, u32[]{:S(2)}) collective-permute-start(f32[32,768]{1,0:T(8,128)S(1)} %shard_map.231.refs_4_.refs_5_), channel_id=1, source_target_pairs={{0,4},{1,5},{2,6},{3,7},{4,0},{5,1},{6,2},{7,3},{8,12},{9,13},{10,... | collective-permute-start | bytes 294920 | tf_op jit(solution)/shard_map/ppermute | solution.py:368
  57.6 5.8 %collective-permute-start.19 = (f32[32,768]{1,0:T(8,128)S(1)}, f32[32,768]{1,0:T(8,128)S(1)}, u32[]{:S(2)}, u32[]{:S(2)}) collective-permute-start(f32[32,768]{1,0:T(8,128)S(1)} %shard_map.231.refs_4_.refs_5_), channel_id=1, source_target_pairs={{0,6},{1,7},{2,4},{3,5},{4,2},{5,3},{6,0},{7,1},{8,14},{9,15},{10,... | collective-permute-start | bytes 294920 | tf_op jit(solution)/shard_map/ppermute | solution.py:368
  61.3 2.2 %copy-start.2 = (f32[1,512,2048]{2,1,0:T(8,128)S(1)}, f32[1,512,2048]{2,1,0:T(8,128)}, u32[]{:S(2)}) copy-start(f32[1,512,2048]{2,1,0:T(8,128)} %param.30) | copy-start | bytes 12582916
  63.5 28.8 %collective-permute-start.30 = (f32[512,2048]{1,0:T(8,128)S(1)}, f32[512,2048]{1,0:T(8,128)S(1)}, u32[]{:S(2)}, u32[]{:S(2)}) collective-permute-start(f32[512,2048]{1,0:T(8,128)S(1)} %bitcast.59), channel_id=1, source_target_pairs={{0,1},{1,0},{2,3},{3,2},{4,5},{5,4},{6,7},{7,6},{8,9},{9,8},{10,11... | collective-permute-start | bytes 12582920 | tf_op jit(solution)/shard_map/ppermute | solution.py:368
  63.6 5.7 %collective-permute-start.24 = (f32[32,768]{1,0:T(8,128)S(1)}, f32[32,768]{1,0:T(8,128)S(1)}, u32[]{:S(2)}, u32[]{:S(2)}) collective-permute-start(f32[32,768]{1,0:T(8,128)S(1)} %shard_map.233.refs_5_), channel_id=1, source_target_pairs={{0,2},{1,3},{2,0},{3,1},{4,8},{5,9},{6,10},{7,11},{8,4},{9,5},{10,... | collective-permute-start | bytes 294920 | tf_op jit(solution)/shard_map/ppermute | solution.py:368
  64.8 6.1 %collective-permute-start.22 = (f32[32,768]{1,0:T(8,128)S(1)}, f32[32,768]{1,0:T(8,128)S(1)}, u32[]{:S(2)}, u32[]{:S(2)}) collective-permute-start(f32[32,768]{1,0:T(8,128)S(1)} %shard_map.233.refs_5_), channel_id=1, source_target_pairs={{0,2},{1,3},{2,0},{3,1},{4,10},{5,11},{6,8},{7,9},{8,6},{9,7},{10,... | collective-permute-start | bytes 294920 | tf_op jit(solution)/shard_map/ppermute | solution.py:368
  70.9 6.9 %collective-permute-start.26 = (f32[32,768]{1,0:T(8,128)S(1)}, f32[32,768]{1,0:T(8,128)S(1)}, u32[]{:S(2)}, u32[]{:S(2)}) collective-permute-start(f32[32,768]{1,0:T(8,128)S(1)} %shard_map.235.refs_5_), channel_id=1, source_target_pairs={{0,4},{1,5},{2,6},{3,7},{4,0},{5,1},{6,2},{7,3},{8,12},{9,13},{10,... | collective-permute-start | bytes 294920 | tf_op jit(solution)/shard_map/ppermute | solution.py:368
  74.8 5.9 %collective-permute-start.25 = (f32[32,768]{1,0:T(8,128)S(1)}, f32[32,768]{1,0:T(8,128)S(1)}, u32[]{:S(2)}, u32[]{:S(2)}) collective-permute-start(f32[32,768]{1,0:T(8,128)S(1)} %shard_map.235.refs_5_), channel_id=1, source_target_pairs={{0,6},{1,7},{2,4},{3,5},{4,2},{5,3},{6,0},{7,1},{8,14},{9,15},{10,... | collective-permute-start | bytes 294920 | tf_op jit(solution)/shard_map/ppermute | solution.py:368
  77.8 5.7 %collective-permute-start.27 = (f32[32,768]{1,0:T(8,128)S(1)}, f32[32,768]{1,0:T(8,128)S(1)}, u32[]{:S(2)}, u32[]{:S(2)}) collective-permute-start(f32[32,768]{1,0:T(8,128)S(1)} %shard_map.235.refs_5_), channel_id=1, source_target_pairs={{0,2},{1,3},{2,0},{3,1},{4,8},{5,9},{6,10},{7,11},{8,4},{9,5},{10,... | collective-permute-start | bytes 294920 | tf_op jit(solution)/shard_map/ppermute | solution.py:368
  78.6 6.6 %collective-permute-start.28 = (f32[32,768]{1,0:T(8,128)S(1)}, f32[32,768]{1,0:T(8,128)S(1)}, u32[]{:S(2)}, u32[]{:S(2)}) collective-permute-start(f32[32,768]{1,0:T(8,128)S(1)} %shard_map.235.refs_5_), channel_id=1, source_target_pairs={{0,2},{1,3},{2,0},{3,1},{4,10},{5,11},{6,8},{7,9},{8,6},{9,7},{10,... | collective-permute-start | bytes 294920 | tf_op jit(solution)/shard_map/ppermute | solution.py:368
  81.7 7.0 %collective-permute-start.32 = (f32[32,768]{1,0:T(8,128)S(1)}, f32[32,768]{1,0:T(8,128)S(1)}, u32[]{:S(2)}, u32[]{:S(2)}) collective-permute-start(f32[32,768]{1,0:T(8,128)S(1)} %shard_map.237.refs_0_), channel_id=1, source_target_pairs={{0,2},{1,3},{2,0},{3,1},{4,6},{5,7},{6,4},{7,5},{8,10},{9,11},{10,... | collective-permute-start | bytes 294920 | tf_op jit(solution)/shard_map/ppermute | solution.py:368
  85.2 4.6 %collective-permute-start.31 = (f32[32,768]{1,0:T(8,128)S(1)}, f32[32,768]{1,0:T(8,128)S(1)}, u32[]{:S(2)}, u32[]{:S(2)}) collective-permute-start(f32[32,768]{1,0:T(8,128)S(1)} %shard_map.237.refs_0_), channel_id=1, source_target_pairs={{0,4},{1,5},{2,6},{3,7},{4,0},{5,1},{6,2},{7,3},{8,12},{9,13},{10,... | collective-permute-start | bytes 294920 | tf_op jit(solution)/shard_map/ppermute | solution.py:368
  86.7 5.6 %collective-permute-start.29 = (f32[32,768]{1,0:T(8,128)S(1)}, f32[32,768]{1,0:T(8,128)S(1)}, u32[]{:S(2)}, u32[]{:S(2)}) collective-permute-start(f32[32,768]{1,0:T(8,128)S(1)} %shard_map.237.refs_0_), channel_id=1, source_target_pairs={{0,6},{1,7},{2,4},{3,5},{4,2},{5,3},{6,0},{7,1},{8,14},{9,15},{10,... | collective-permute-start | bytes 294920 | tf_op jit(solution)/shard_map/ppermute | solution.py:368
  92.3 2.5 %copy-start.9 = (f32[1,384,64]{1,2,0:T(8,128)S(1)}, f32[1,384,64]{1,2,0:T(8,128)}, u32[]{:S(2)}) copy-start(f32[1,384,64]{1,2,0:T(8,128)} %param.27) | copy-start | bytes 294916
  92.3 2.5 %copy-start.10 = (f32[1,384,64]{1,2,0:T(8,128)S(1)}, f32[1,384,64]{1,2,0:T(8,128)}, u32[]{:S(2)}) copy-start(f32[1,384,64]{1,2,0:T(8,128)} %param.28) | copy-start | bytes 294916
  92.3 2.5 %copy-start.11 = (f32[1,384,64]{1,2,0:T(8,128)S(1)}, f32[1,384,64]{1,2,0:T(8,128)}, u32[]{:S(2)}) copy-start(f32[1,384,64]{1,2,0:T(8,128)} %param.29) | copy-start | bytes 294916
  92.4 5.0 %collective-permute-start.33 = (f32[32,1024]{1,0:T(8,128)S(1)}, f32[32,1024]{1,0:T(8,128)S(1)}, u32[]{:S(2)}, u32[]{:S(2)}) collective-permute-start(f32[32,1024]{1,0:T(8,128)S(1)} %shard_map.241.refs_0_), channel_id=1, source_target_pairs={{0,2},{1,3},{2,0},{3,1},{4,6},{5,7},{6,4},{7,5},{8,10},{9,11},{10,... | collective-permute-start | bytes 393224 | tf_op jit(solution)/shard_map/ppermute | solution.py:368
  93.5 1.3 %collective-permute-start.34 = (f32[32,384]{1,0:T(8,128)S(1)}, f32[32,384]{1,0:T(8,128)S(1)}, u32[]{:S(2)}, u32[]{:S(2)}) collective-permute-start(f32[32,384]{1,0:T(8,128)S(1)} %get-tuple-element.102), channel_id=1, source_target_pairs={{0,1},{1,0},{2,3},{3,2},{4,5},{5,4},{6,7},{7,6},{8,9},{9,8},{10,11... | collective-permute-start | bytes 147464 | tf_op jit(solution)/shard_map/ppermute | solution.py:368
  97.4 2.7 %copy-start.6 = (f32[1,512,64]{1,2,0:T(8,128)S(1)}, f32[1,512,64]{1,2,0:T(8,128)}, u32[]{:S(2)}) copy-start(f32[1,512,64]{1,2,0:T(8,128)} %param.24) | copy-start | bytes 393220
  97.4 2.7 %copy-start.7 = (f32[1,512,64]{1,2,0:T(8,128)S(1)}, f32[1,512,64]{1,2,0:T(8,128)}, u32[]{:S(2)}) copy-start(f32[1,512,64]{1,2,0:T(8,128)} %param.25) | copy-start | bytes 393220
  97.4 2.7 %copy-start.8 = (f32[1,512,64]{1,2,0:T(8,128)S(1)}, f32[1,512,64]{1,2,0:T(8,128)}, u32[]{:S(2)}) copy-start(f32[1,512,64]{1,2,0:T(8,128)} %param.26) | copy-start | bytes 393220
  98.8 1.3 %collective-permute-start.35 = (f32[32,512]{1,0:T(8,128)S(1)}, f32[32,512]{1,0:T(8,128)S(1)}, u32[]{:S(2)}, u32[]{:S(2)}) collective-permute-start(f32[32,512]{1,0:T(8,128)S(1)} %get-tuple-element.109), channel_id=1, source_target_pairs={{0,1},{1,0},{2,3},{3,2},{4,5},{5,4},{6,7},{7,6},{8,9},{9,8},{10,11... | collective-permute-start | bytes 196616 | tf_op jit(solution)/shard_map/ppermute | solution.py:368

commit v10 on v9

--- a/solution.py
+++ b/solution.py
@@ -77,7 +77,7 @@
     ref[...] = jnp.concatenate([jnp.where(swap, other, own), jnp.where(swap, own, other)], axis=1)
 
 
-def call(kernel, shapes, *groups, cost=0):
+def call(kernel, shapes, *groups, cost=0, late=None):
     flat = [value for group in groups for value in group]
 
     def body(*refs):
@@ -85,17 +85,25 @@
         for group in groups:
             parts.append(refs[at : at + len(group)])
             at += len(group)
-        kernel(*parts, *refs[at:])
+        if late is None:
+            kernel(*parts, *refs[at:])
+            return
+        buffer, sem = refs[-2:]
+        copy = pltpu.make_async_copy(refs[at], buffer, sem)
+        copy.start()
+        kernel(*parts, *refs[at + 1 : -2], copy, buffer)
 
     out = [jax.ShapeDtypeStruct(shape, jnp.float32) for shape in shapes]
+    last = [] if late is None else [pltpu.with_memory_space_constraint(late, pltpu.HBM)]
     return pl.pallas_call(
         body,
-        in_specs=[VMEM] * len(flat),
+        in_specs=[VMEM] * len(flat) + [pl.BlockSpec(memory_space=pltpu.HBM)] * len(last),
         out_specs=[VMEM] * len(out),
         out_shape=out,
         compiler_params=pltpu.CompilerParams(vmem_limit_bytes=24 << 20),
         cost_estimate=pl.CostEstimate(flops=0, bytes_accessed=cost, transcendentals=0) if cost else None,
-    )(*flat)
+        scratch_shapes=[*(pltpu.VMEM(x.shape, x.dtype) for x in last), *[pltpu.SemaphoreType.DMA] * len(last)],
+    )(*flat, *last)
 
 
 def staged(*matrices, after):
@@ -135,13 +143,12 @@
     )(*held)
 
 
-def forces_kernel(swap_chips, pieces, matrices, mine, theirs):
+def forces_kernel(swap_chips, pieces, matrices, mine, theirs, copy, below):
     (rows,) = matrices
     faces = mine.shape[2]
-    inner = rows.shape[1] - 2 * faces
+    inner = rows.shape[1] - faces
     inverse = rows.at[:, :inner]
-    above = rows.at[:, inner : inner + faces]
-    below = rows.at[:, inner + faces :]
+    above = rows.at[:, inner:]
     if swap_chips:
         chips = len(pieces) // 2
         core = lax.axis_index("blk")
@@ -154,6 +161,8 @@
     half = part.shape[0] // 2
     second = lax.axis_index("blk") == 1
     for i, matrix in enumerate((above, below)):
+        if i == 1:
+            copy.wait()
         force = times(part, matrix)
         mine[i] = jnp.where(second, force[half:], force[:half])
         theirs[i] = jnp.where(second, force[:half], force[half:])
@@ -226,11 +235,23 @@
     return jnp.concatenate([jnp.where(second, other, own), jnp.where(second, own, other)], axis=axis)
 
 
-def condensed_kernel(load, forces, out):
+def less_in(stories_of, value, forces):
+    story, count = lax.axis_index("story"), lax.axis_size("story")
+    there = (lax.rem(story, 2) == stories_of) & (story + 1 < count)
+    for force in forces:
+        value = jnp.where(there, value - force[...], value)
+    return value
+
+
+def condensed_kernel(load, forces, even, out):
     value = by_core(load[0][...], load[1][...], 1)
     for force in forces:
         value = value - force[...]
-    out[...] = value
+    out[...] = less_in(0, value, even)
+
+
+def odd_kernel(value, odd, out):
+    out[...] = less_in(1, value[0][...], odd)
 
 
 def halves_kernel(whole, mine, theirs):
@@ -460,9 +481,7 @@
 
     lower_other = mv.core(lower[0])
     across = [mv.chip(load_int, j) for j in range(1, mv.chips)]
-    phase_rows = staged(
-        interior_inverse[0], couple_above[0], couple_below[0], after=[load_int]
-    )
+    phase_rows = staged(interior_inverse[0], couple_above[0], after=[load_int])
     phase_rows, *across = lax.optimization_barrier([phase_rows, *across])
     beside = [mv.core(piece) for piece in [load_int] + across]
     pieces = [piece for pair in zip([load_int] + across, beside) for piece in pair]
@@ -472,7 +491,11 @@
             mv.by_chip([mv.by_core(pieces[2 * j], pieces[2 * j + 1], 1) for j in range(mv.chips)])
         ]
     mine, theirs = call(
-        functools.partial(forces_kernel, aligned), [(2, half, faces)] * 2, pieces, [phase_rows]
+        functools.partial(forces_kernel, aligned),
+        [(2, half, faces)] * 2,
+        pieces,
+        [phase_rows],
+        late=couple_below[0],
     )
     chunks = call(
         chunks_kernel,
@@ -487,16 +510,19 @@
     mine_int, theirs_int = call(records_kernel, [(half, own_int)] * 2, [load_late])
     halves = lax.optimization_barrier([mv.core(theirs_face), mv.core(theirs_int)])
     load_face_half, load_int_half = [mine_face, halves[0]], [mine_int, halves[1]]
-    forces = [mv.shift(chunks[mv.chips], -1, 0)]
-    for j in range(1, mv.chips):
-        forces += [mv.chip(chunks[j], j), mv.shift(chunks[mv.chips + j], -1, j)]
+    below_parts = chunks[mv.chips :]
+    even = [mv.story(below_parts[j], 0, j) for j in range(mv.chips)]
+    forces = [chunks[0]] + [mv.chip(chunks[j], j) for j in range(1, mv.chips)]
     shape = [(half, rows_face)]
-    (condensed,) = call(condensed_kernel, shape, load_face_half, [chunks[0]] + forces)
+    (condensed,) = call(condensed_kernel, shape, load_face_half, forces, even)
+    odd = [mv.story(below_parts[j], 1, j) for j in range(mv.chips)]
 
     forward = condensed
     pivot_other = others(pivot[0], [condensed])
     for k in range(1, mv.stories):
         came = mv.gather_story(forward, (k - 1) % 2)
+        if k == 1:
+            (condensed,) = call(odd_kernel, shape, [condensed], odd)
         if k == min(2, mv.stories - 1):
             upper_other = others(upper[0], [pivot_other, forward])
             came[-1], pivot_other = lax.optimization_barrier([came[-1], pivot_other])
@@ -526,9 +552,6 @@
         if k == max(mv.stories - 3, 0):
             inverse_other = others(interior_inverse[0], [below_other, face])
             came[-1], below_other = lax.optimization_barrier([came[-1], below_other])
-        if k == 0:
-            late, came[0] = lax.optimization_barrier([face, came[0]])
-            odd = mv.gather_story(late, 1)
         (face,) = call(
             functools.partial(step_kernel, from_chip(len(came), len(came) - 1), k),
             shape,
@@ -537,8 +560,8 @@
         )
 
     here = mv.gather_chips(face)
-    face, *odd = lax.optimization_barrier([face, *odd])
     even = mv.gather_story(face, 0)
+    odd = mv.gather_story(face, 1)
     even[-1], inverse_other = lax.optimization_barrier([even[-1], inverse_other])
     rows = [couple_above[0], above_other]
     sofar = []

time: 101 us -> 103 us (1.020)
  starting transfers between devices: 33.8 us -> 35.4 us
  waiting for transfers between devices: 46.7 us -> 47.9 us
    ppermute x34 -> x38, waiting for transfers between devices: 43.2 us -> 47.9 us  [permute(): return lax.ppermute(value, AXES, pairs)]
    ppermute x34 -> x38, starting transfers between devices: 31.2 us -> 35.4 us  [permute(): return lax.ppermute(value, AXES, pairs)]
    ppermute x2 -> x0, waiting for transfers between devices: 3.5 us -> none  [shift(): return lax.ppermute(value, AXES, pairs)]
    ppermute x2 -> x0, starting transfers between devices: 2.57 us -> none  [shift(): return lax.ppermute(value, AXES, pairs)]
    pallas_call x27 -> x28, Pallas kernels: 12.6 us -> 12.7 us  [call(): pl.pallas_call(body, in_specs=[VMEM] * len(flat) + [pl.BlockSpec(memory_s...]
  transfers between devices with their start and end apart: 36 -> 38, of which waited for: 23 -> 24; matrix products, arithmetic and copies ran while one was open for 0% -> 0% of each run, Pallas kernels for 13% -> 12%
where the time goes in v10:
time: 103 us
  waiting for transfers between devices  47.9 us (47%)
  starting transfers between devices  35.4 us (34%)
  Pallas kernels  18.3 us (18%)
    ppermute x38, waiting for transfers between devices, permute(): return lax.ppermute(value, AXES, pairs)  47.9 us
    ppermute x38, starting transfers between devices, permute(): return lax.ppermute(value, AXES, pairs)  35.4 us
    pallas_call x28, Pallas kernels, call(): pl.pallas_call(body, in_specs=[VMEM] * len(flat) + [pl.BlockSpec(memory_s...  12.7 us
    pallas_call x1, Pallas kernels, staged(): pl.pallas_call(body, in_specs=[pl.BlockSpec(memory_space=pltpu.HBM)] * co...  3.16 us
    pallas_call x2, Pallas kernels, fetched(): pl.pallas_call(body, in_specs=[pl.BlockSpec(memory_space=pltpu.HBM)] * co...  2.48 us
  transfers between devices with their start and end apart: 38, of which 24 were waited for; matrix products, arithmetic and copies ran while one was open for 0% of the time, Pallas kernels for 12%

profile of v10, /device:TPU:0, one launch (start us, length us, event | category | flops | bytes accessed | tf_op | source)
XLA Modules:
  0.0 102.9 jit_solution(7367728321303360363)
XLA Ops:
  0.6 1.3 %shard_map.217 = (f32[64,512]{1,0:T(8,128)S(1)}, f32[64,128]{1,0:T(8,128)S(1)}) custom-call(s32[1,64]{1,0:T(1,128)} %bitcast.86, f32[1,512]{1,0:T(1,128)} %bitcast.85, f32[1,512]{1,0:T(1,128)} %refs_2_.1, f32[1,512]{1,0:T(1,128)} %refs_3_.1, f32[64,512]{1,0:T(8,128)} %bitcast.73, f32[64,512]{1,0:T(8,128)} %bitcast.75, f32[64,512]{1,0:T(8,128)} %bitcast.77), custom_call_target="tpu_custom_call" | custom-call | tf_op jit(solution)/shard_map/pallas_call | solution.py:189
  2.0 3.0 %collective-permute-start.1 = (f32[64,512]{1,0:T(8,128)S(1)}, f32[64,512]{1,0:T(8,128)S(1)}, u32[]{:S(2)}, u32[]{:S(2)}) collective-permute-start(f32[64,512]{1,0:T(8,128)S(1)} %get-tuple-element.63.refs_0_), channel_id=1, source_target_pairs={{0,2},{1,3},{2,0},{3,1},{4,6},{5,7},{6,4},{7,5},{8,10},{9,11},{10,... | collective-permute-start | bytes 393224 | tf_op jit(solution)/shard_map/ppermute | solution.py:389
  5.0 3.2 %shard_map.218.refs_4_ = f32[512,3584]{1,0:T(8,128)S(1)} custom-call(f32[512,2048]{1,0:T(8,128)} %bitcast.58, f32[512,1536]{1,0:T(8,128)} %bitcast.62), custom_call_target="tpu_custom_call" | custom-call | tf_op jit(solution)/shard_map/pallas_call | solution.py:136
  8.7 1.1 %collective-permute-done.2.refs_3_ = f32[64,512]{1,0:T(8,128)S(1)} collective-permute-done((f32[64,512]{1,0:T(8,128)S(1)}, f32[64,512]{1,0:T(8,128)S(1)}, u32[]{:S(2)}, u32[]{:S(2)}) %collective-permute-start.2) | collective-permute-done | bytes 131104 | tf_op jit(solution)/shard_map/ppermute | solution.py:389
  9.8 2.8 %shard_map.219 = (f32[2,32,1536]{2,1,0:T(8,128)S(1)}, f32[2,32,1536]{2,1,0:T(8,128)S(1)}) custom-call(f32[64,512]{1,0:T(8,128)S(1)} %get-tuple-element.63.refs_0_, f32[64,512]{1,0:T(8,128)S(1)} %collective-permute-done.refs_1_, f32[64,512]{1,0:T(8,128)S(1)} %collective-permute-done.1.refs_2_, f32[64,512]{1,0:T(8,128)S(1)} %collective-permute-done.2.refs_3_, ...), custom_call_target="tpu_custom_call" | custom-call | tf_op jit(solution)/shard_map/pallas_call | solution.py:98
  12.9 1.5 %collective-permute-done.3.refs_1_ = f32[2,32,1536]{2,1,0:T(8,128)S(1)} collective-permute-done((f32[2,32,1536]{2,1,0:T(8,128)S(1)}, f32[2,32,1536]{2,1,0:T(8,128)S(1)}, u32[]{:S(2)}, u32[]{:S(2)}) %collective-permute-start.3) | collective-permute-done | bytes 393248 | tf_op jit(solution)/shard_map/ppermute | solution.py:389
  14.5 1.8 %collective-permute-start.6 = (f32[32,768]{1,0:T(8,128)S(1)}, f32[32,768]{1,0:T(8,128)S(1)}, u32[]{:S(2)}, u32[]{:S(2)}) collective-permute-start(f32[32,768]{1,0:T(8,128)S(1)} %get-tuple-element.72), channel_id=1, source_target_pairs={{0,2},{1,3},{2,0},{3,1},{4,6},{5,7},{6,4},{7,5},{8,10},{9,11},{10,... | collective-permute-start | bytes 294920 | tf_op jit(solution)/shard_map/ppermute | solution.py:389
  16.3 1.6 %collective-permute-start.7 = (f32[32,768]{1,0:T(8,128)S(1)}, f32[32,768]{1,0:T(8,128)S(1)}, u32[]{:S(2)}, u32[]{:S(2)}) collective-permute-start(f32[32,768]{1,0:T(8,128)S(1)} %get-tuple-element.73), channel_id=1, source_target_pairs={{0,4},{1,5},{2,6},{3,7},{4,0},{5,1},{6,2},{7,3},{8,12},{9,13},{10,... | collective-permute-start | bytes 294920 | tf_op jit(solution)/shard_map/ppermute | solution.py:389
  18.1 1.2 %shard_map.222 = (f32[32,384]{1,0:T(8,128)S(1)}, f32[32,384]{1,0:T(8,128)S(1)}) custom-call(f32[1,384]{1,0:T(1,128)} %refs_0_.1, f32[1,384]{1,0:T(1,128)} %refs_1_.1, f32[64,384]{1,0:T(8,128)} %bitcast.79, f32[64,384]{1,0:T(8,128)} %bitcast.81, f32[64,384]{1,0:T(8,128)} %bitcast.83, f32[64,128]{1,0:T(8,128)S(1)} %get-tuple-element.66.refs_5_), custom_call_target="tpu_custom_call" | custom-call | tf_op jit(solution)/shard_map/pallas_call | solution.py:189
  21.8 1.6 %collective-permute-done.8.refs_5_ = f32[32,768]{1,0:T(8,128)S(1)} collective-permute-done((f32[32,768]{1,0:T(8,128)S(1)}, f32[32,768]{1,0:T(8,128)S(1)}, u32[]{:S(2)}, u32[]{:S(2)}) %collective-permute-start.8) | collective-permute-done | bytes 98336 | tf_op jit(solution)/shard_map/ppermute | solution.py:389
  23.5 1.2 %collective-permute-start.12 = (f32[32,768]{1,0:T(8,128)S(1)}, f32[32,768]{1,0:T(8,128)S(1)}, u32[]{:S(2)}, u32[]{:S(2)}) collective-permute-start(f32[32,768]{1,0:T(8,128)S(1)} %get-tuple-element.73), channel_id=1, source_target_pairs={{0,2},{1,3},{2,0},{3,1},{4,8},{5,9},{6,10},{7,11},{8,4},{9,5},{10,... | collective-permute-start | bytes 294920 | tf_op jit(solution)/shard_map/ppermute | solution.py:389
  24.6 0.9 collective-permute-start.13
  25.6 2.1 %collective-permute-start.11 = (f32[32,768]{1,0:T(8,128)S(1)}, f32[32,768]{1,0:T(8,128)S(1)}, u32[]{:S(2)}, u32[]{:S(2)}) collective-permute-start(f32[32,768]{1,0:T(8,128)S(1)} %shard_map.223.refs_0_.refs_5_), channel_id=1, source_target_pairs={{0,4},{1,5},{2,6},{3,7},{4,0},{5,1},{6,2},{7,3},{8,12},{9,13},{10,... | collective-permute-start | bytes 294920 | tf_op jit(solution)/shard_map/ppermute | solution.py:389
  27.6 1.5 %collective-permute-done.12.refs_1_ = f32[32,768]{1,0:T(8,128)S(1)} collective-permute-done((f32[32,768]{1,0:T(8,128)S(1)}, f32[32,768]{1,0:T(8,128)S(1)}, u32[]{:S(2)}, u32[]{:S(2)}) %collective-permute-start.12) | collective-permute-done | bytes 98336 | tf_op jit(solution)/shard_map/ppermute | solution.py:389
  29.1 2.0 %collective-permute-start.9 = (f32[32,768]{1,0:T(8,128)S(1)}, f32[32,768]{1,0:T(8,128)S(1)}, u32[]{:S(2)}, u32[]{:S(2)}) collective-permute-start(f32[32,768]{1,0:T(8,128)S(1)} %shard_map.223.refs_0_.refs_5_), channel_id=1, source_target_pairs={{0,6},{1,7},{2,4},{3,5},{4,2},{5,3},{6,0},{7,1},{8,14},{9,15},{10,... | collective-permute-start | bytes 294920 | tf_op jit(solution)/shard_map/ppermute | solution.py:389
  31.2 3.4 %collective-permute-done.9.refs_0_ = f32[32,768]{1,0:T(8,128)S(1)} collective-permute-done((f32[32,768]{1,0:T(8,128)S(1)}, f32[32,768]{1,0:T(8,128)S(1)}, u32[]{:S(2)}, u32[]{:S(2)}) %collective-permute-start.9) | collective-permute-done | bytes 98336 | tf_op jit(solution)/shard_map/ppermute | solution.py:389
  34.8 1.2 %collective-permute-start.16 = (f32[32,768]{1,0:T(8,128)S(1)}, f32[32,768]{1,0:T(8,128)S(1)}, u32[]{:S(2)}, u32[]{:S(2)}) collective-permute-start(f32[32,768]{1,0:T(8,128)S(1)} %shard_map.226.refs_5_), channel_id=1, source_target_pairs={{0,2},{1,3},{2,0},{3,1},{4,8},{5,9},{6,10},{7,11},{8,4},{9,5},{10,... | collective-permute-start | bytes 294920 | tf_op jit(solution)/shard_map/ppermute | solution.py:389
  35.9 0.9 collective-permute-start.14
  36.9 3.6 %collective-permute-done.16.refs_0_ = f32[32,768]{1,0:T(8,128)S(1)} collective-permute-done((f32[32,768]{1,0:T(8,128)S(1)}, f32[32,768]{1,0:T(8,128)S(1)}, u32[]{:S(2)}, u32[]{:S(2)}) %collective-permute-start.16) | collective-permute-done | bytes 98336 | tf_op jit(solution)/shard_map/ppermute | solution.py:389
  40.4 1.7 %collective-permute-done.14.refs_0_ = f32[32,768]{1,0:T(8,128)S(1)} collective-permute-done((f32[32,768]{1,0:T(8,128)S(1)}, f32[32,768]{1,0:T(8,128)S(1)}, u32[]{:S(2)}, u32[]{:S(2)}) %collective-permute-start.14) | collective-permute-done | bytes 98336 | tf_op jit(solution)/shard_map/ppermute | solution.py:389
  42.3 2.8 %collective-permute-start.19 = (f32[32,768]{1,0:T(8,128)S(1)}, f32[32,768]{1,0:T(8,128)S(1)}, u32[]{:S(2)}, u32[]{:S(2)}) collective-permute-start(f32[32,768]{1,0:T(8,128)S(1)} %shard_map.228.refs_5_), channel_id=1, source_target_pairs={{0,4},{1,5},{2,6},{3,7},{4,0},{5,1},{6,2},{7,3},{8,12},{9,13},{10,... | collective-permute-start | bytes 294920 | tf_op jit(solution)/shard_map/ppermute | solution.py:389
  45.1 3.6 %collective-permute-done.19.refs_0_ = f32[32,768]{1,0:T(8,128)S(1)} collective-permute-done((f32[32,768]{1,0:T(8,128)S(1)}, f32[32,768]{1,0:T(8,128)S(1)}, u32[]{:S(2)}, u32[]{:S(2)}) %collective-permute-start.19) | collective-permute-done | bytes 98336 | tf_op jit(solution)/shard_map/ppermute | solution.py:389
  48.7 2.1 %collective-permute-done.17.refs_0_ = f32[32,768]{1,0:T(8,128)S(1)} collective-permute-done((f32[32,768]{1,0:T(8,128)S(1)}, f32[32,768]{1,0:T(8,128)S(1)}, u32[]{:S(2)}, u32[]{:S(2)}) %collective-permute-start.17) | collective-permute-done | bytes 98336 | tf_op jit(solution)/shard_map/ppermute | solution.py:389
  50.9 1.3 %collective-permute-start.20 = (f32[32,768]{1,0:T(8,128)S(1)}, f32[32,768]{1,0:T(8,128)S(1)}, u32[]{:S(2)}, u32[]{:S(2)}) collective-permute-start(f32[32,768]{1,0:T(8,128)S(1)} %shard_map.230.refs_0_), channel_id=1, source_target_pairs={{0,2},{1,3},{2,0},{3,1},{4,6},{5,7},{6,4},{7,5},{8,10},{9,11},{10,... | collective-permute-start | bytes 294920 | tf_op jit(solution)/shard_map/ppermute | solution.py:389
  52.9 2.6 %collective-permute-done.20.refs_0_ = f32[32,768]{1,0:T(8,128)S(1)} collective-permute-done((f32[32,768]{1,0:T(8,128)S(1)}, f32[32,768]{1,0:T(8,128)S(1)}, u32[]{:S(2)}, u32[]{:S(2)}) %collective-permute-start.20) | collective-permute-done | bytes 98336 | tf_op jit(solution)/shard_map/ppermute | solution.py:389
  56.5 1.7 %collective-permute-start.23 = (f32[32,768]{1,0:T(8,128)S(1)}, f32[32,768]{1,0:T(8,128)S(1)}, u32[]{:S(2)}, u32[]{:S(2)}) collective-permute-start(f32[32,768]{1,0:T(8,128)S(1)} %shard_map.232.refs_4_.refs_5_), channel_id=1, source_target_pairs={{0,4},{1,5},{2,6},{3,7},{4,0},{5,1},{6,2},{7,3},{8,12},{9,13},{10,... | collective-permute-start | bytes 294920 | tf_op jit(solution)/shard_map/ppermute | solution.py:389
  58.2 1.0 %collective-permute-start.21 = (f32[32,768]{1,0:T(8,128)S(1)}, f32[32,768]{1,0:T(8,128)S(1)}, u32[]{:S(2)}, u32[]{:S(2)}) collective-permute-start(f32[32,768]{1,0:T(8,128)S(1)} %shard_map.232.refs_4_.refs_5_), channel_id=1, source_target_pairs={{0,6},{1,7},{2,4},{3,5},{4,2},{5,3},{6,0},{7,1},{8,14},{9,15},{10,... | collective-permute-start | bytes 294920 | tf_op jit(solution)/shard_map/ppermute | solution.py:389
  59.2 2.5 %collective-permute-done.23.refs_0_ = f32[32,768]{1,0:T(8,128)S(1)} collective-permute-done((f32[32,768]{1,0:T(8,128)S(1)}, f32[32,768]{1,0:T(8,128)S(1)}, u32[]{:S(2)}, u32[]{:S(2)}) %collective-permute-start.23) | collective-permute-done | bytes 98336 | tf_op jit(solution)/shard_map/ppermute | solution.py:389
  61.7 2.7 %collective-permute-done.21.refs_0_ = f32[32,768]{1,0:T(8,128)S(1)} collective-permute-done((f32[32,768]{1,0:T(8,128)S(1)}, f32[32,768]{1,0:T(8,128)S(1)}, u32[]{:S(2)}, u32[]{:S(2)}) %collective-permute-start.21) | collective-permute-done | bytes 98336 | tf_op jit(solution)/shard_map/ppermute | solution.py:389
  64.5 1.0 collective-permute-start.26
  65.5 1.1 %collective-permute-start.24 = (f32[32,768]{1,0:T(8,128)S(1)}, f32[32,768]{1,0:T(8,128)S(1)}, u32[]{:S(2)}, u32[]{:S(2)}) collective-permute-start(f32[32,768]{1,0:T(8,128)S(1)} %shard_map.234.refs_5_), channel_id=1, source_target_pairs={{0,2},{1,3},{2,0},{3,1},{4,10},{5,11},{6,8},{7,9},{8,6},{9,7},{10,... | collective-permute-start | bytes 294920 | tf_op jit(solution)/shard_map/ppermute | solution.py:389
  66.6 3.6 %collective-permute-done.26.refs_0_ = f32[32,768]{1,0:T(8,128)S(1)} collective-permute-done((f32[32,768]{1,0:T(8,128)S(1)}, f32[32,768]{1,0:T(8,128)S(1)}, u32[]{:S(2)}, u32[]{:S(2)}) %collective-permute-start.26) | collective-permute-done | bytes 98336 | tf_op jit(solution)/shard_map/ppermute | solution.py:389
  70.2 1.7 %collective-permute-done.24.refs_0_ = f32[32,768]{1,0:T(8,128)S(1)} collective-permute-done((f32[32,768]{1,0:T(8,128)S(1)}, f32[32,768]{1,0:T(8,128)S(1)}, u32[]{:S(2)}, u32[]{:S(2)}) %collective-permute-start.24) | collective-permute-done | bytes 98336 | tf_op jit(solution)/shard_map/ppermute | solution.py:389
  71.9 3.9 %collective-permute-start.28 = (f32[32,768]{1,0:T(8,128)S(1)}, f32[32,768]{1,0:T(8,128)S(1)}, u32[]{:S(2)}, u32[]{:S(2)}) collective-permute-start(f32[32,768]{1,0:T(8,128)S(1)} %shard_map.236.refs_5_), channel_id=1, source_target_pairs={{0,4},{1,5},{2,6},{3,7},{4,0},{5,1},{6,2},{7,3},{8,12},{9,13},{10,... | collective-permute-start | bytes 294920 | tf_op jit(solution)/shard_map/ppermute | solution.py:389
  76.3 2.3 %collective-permute-done.28.refs_0_ = f32[32,768]{1,0:T(8,128)S(1)} collective-permute-done((f32[32,768]{1,0:T(8,128)S(1)}, f32[32,768]{1,0:T(8,128)S(1)}, u32[]{:S(2)}, u32[]{:S(2)}) %collective-permute-start.28) | collective-permute-done | bytes 98336 | tf_op jit(solution)/shard_map/ppermute | solution.py:389
  79.4 1.9 %collective-permute-done.27.refs_0_ = f32[32,768]{1,0:T(8,128)S(1)} collective-permute-done((f32[32,768]{1,0:T(8,128)S(1)}, f32[32,768]{1,0:T(8,128)S(1)}, u32[]{:S(2)}, u32[]{:S(2)}) %collective-permute-start.27) | collective-permute-done | bytes 98336 | tf_op jit(solution)/shard_map/ppermute | solution.py:389
  82.1 1.1 %collective-permute-start.34 = (f32[32,768]{1,0:T(8,128)S(1)}, f32[32,768]{1,0:T(8,128)S(1)}, u32[]{:S(2)}, u32[]{:S(2)}) collective-permute-start(f32[32,768]{1,0:T(8,128)S(1)} %shard_map.238.refs_0_), channel_id=1, source_target_pairs={{0,2},{1,3},{2,0},{3,1},{4,6},{5,7},{6,4},{7,5},{8,10},{9,11},{10,... | collective-permute-start | bytes 294920 | tf_op jit(solution)/shard_map/ppermute | solution.py:389
  83.6 1.1 %collective-permute-start.33 = (f32[32,768]{1,0:T(8,128)S(1)}, f32[32,768]{1,0:T(8,128)S(1)}, u32[]{:S(2)}, u32[]{:S(2)}) collective-permute-start(f32[32,768]{1,0:T(8,128)S(1)} %shard_map.238.refs_0_), channel_id=1, source_target_pairs={{0,2},{1,3},{2,0},{3,1},{4,8},{5,9},{6,10},{7,11},{8,4},{9,5},{10,... | collective-permute-start | bytes 294920 | tf_op jit(solution)/shard_map/ppermute | solution.py:389
  84.7 1.0 collective-permute-start.29
  85.7 3.0 %collective-permute-done.34.refs_0_ = f32[32,768]{1,0:T(8,128)S(1)} collective-permute-done((f32[32,768]{1,0:T(8,128)S(1)}, f32[32,768]{1,0:T(8,128)S(1)}, u32[]{:S(2)}, u32[]{:S(2)}) %collective-permute-start.34) | collective-permute-done | bytes 98336 | tf_op jit(solution)/shard_map/ppermute | solution.py:389
  88.8 0.9 collective-permute-start.31
  89.7 1.0 %shard_map.239.refs_3_ = f32[32,1024]{1,0:T(8,128)S(1)} custom-call(f32[32,768]{1,0:T(8,128)S(1)} %shard_map.238.refs_0_, f32[512,1536]{1,0:T(8,128)S(1)} %bitcast.64, f32[512,1536]{1,0:T(8,128)S(1)} %collective-permute-done.22.refs_2_), custom_call_target="tpu_custom_call" | custom-call | bytes 4194304 | tf_op jit(solution)/shard_map/pallas_call | solution.py:98
  90.7 1.1 %shard_map.240.refs_4_ = f32[32,1024]{1,0:T(8,128)S(1)} custom-call(f32[32,768]{1,0:T(8,128)S(1)} %collective-permute-done.34.refs_0_, f32[512,1536]{1,0:T(8,128)S(1)} %bitcast.65, f32[512,1536]{1,0:T(8,128)S(1)} %collective-permute-done.22.refs_2_, f32[32,1024]{1,0:T(8,128)S(1)} %shard_map.239.refs_3_), custom_call_target="tpu_custom_call" | custom-call | bytes 4194304 | tf_op jit(solution)/shard_map/pallas_call | solution.py:98
  91.9 2.4 %collective-permute-done.31.refs_3_ = f32[32,768]{1,0:T(8,128)S(1)} collective-permute-done((f32[32,768]{1,0:T(8,128)S(1)}, f32[32,768]{1,0:T(8,128)S(1)}, u32[]{:S(2)}, u32[]{:S(2)}) %collective-permute-start.31) | collective-permute-done | bytes 98336 | tf_op jit(solution)/shard_map/ppermute | solution.py:389
  95.3 1.2 %collective-permute-done.36.refs_1_ = f32[32,384]{1,0:T(8,128)S(1)} collective-permute-done((f32[32,384]{1,0:T(8,128)S(1)}, f32[32,384]{1,0:T(8,128)S(1)}, u32[]{:S(2)}, u32[]{:S(2)}) %collective-permute-start.36) | collective-permute-done | bytes 49184 | tf_op jit(solution)/shard_map/ppermute | solution.py:389
  97.3 1.3 %shard_map.245.refs_3_ = f32[32,1024]{1,0:T(8,128)S(1)} custom-call(f32[32,1024]{1,0:T(8,128)S(1)} %shard_map.242.refs_0_, f32[512,2048]{1,0:T(8,128)S(1)} %bitcast.60, f32[512,2048]{1,0:T(8,128)S(1)} %collective-permute-done.30.refs_2_), custom_call_target="tpu_custom_call" | custom-call | bytes 4194304 | tf_op jit(solution)/shard_map/pallas_call | solution.py:98
  99.4 1.4 %shard_map.246 = (f32[32,512]{1,0:T(8,128)S(1)}, f32[32,512]{1,0:T(8,128)S(1)}) custom-call(f32[32,1024]{1,0:T(8,128)S(1)} %collective-permute-done.35.refs_0_, f32[512,2048]{1,0:T(8,128)S(1)} %bitcast.61, f32[512,2048]{1,0:T(8,128)S(1)} %collective-permute-done.30.refs_2_, f32[32,1024]{1,0:T(8,128)S(1)} %shard_map.245.refs_3_), custom_call_target="tpu_custom_call" | custom-call | tf_op jit(solution)/shard_map/pallas_call | solution.py:98
  100.8 1.2 %collective-permute-done.37.refs_1_ = f32[32,512]{1,0:T(8,128)S(1)} collective-permute-done((f32[32,512]{1,0:T(8,128)S(1)}, f32[32,512]{1,0:T(8,128)S(1)}, u32[]{:S(2)}, u32[]{:S(2)}) %collective-permute-start.37) | collective-permute-done | bytes 65568 | tf_op jit(solution)/shard_map/ppermute | solution.py:389
  (83 shorter events, 12.1 us)
Async XLA Ops:
  2.0 6.5 %collective-permute-start.1 = (f32[64,512]{1,0:T(8,128)S(1)}, f32[64,512]{1,0:T(8,128)S(1)}, u32[]{:S(2)}, u32[]{:S(2)}) collective-permute-start(f32[64,512]{1,0:T(8,128)S(1)} %get-tuple-element.63.refs_0_), channel_id=1, source_target_pairs={{0,2},{1,3},{2,0},{3,1},{4,6},{5,7},{6,4},{7,5},{8,10},{9,11},{10,... | collective-permute-start | bytes 393224 | tf_op jit(solution)/shard_map/ppermute | solution.py:389
  5.0 3.8 %collective-permute-start = (f32[64,512]{1,0:T(8,128)S(1)}, f32[64,512]{1,0:T(8,128)S(1)}, u32[]{:S(2)}, u32[]{:S(2)}) collective-permute-start(f32[64,512]{1,0:T(8,128)S(1)} %get-tuple-element.63.refs_0_), channel_id=1, source_target_pairs={{0,1},{1,0},{2,3},{3,2},{4,5},{5,4},{6,7},{7,6},{8,9},{9,8},{10,11... | collective-permute-start | bytes 393224 | tf_op jit(solution)/shard_map/ppermute | solution.py:389
  8.5 1.3 %collective-permute-start.2 = (f32[64,512]{1,0:T(8,128)S(1)}, f32[64,512]{1,0:T(8,128)S(1)}, u32[]{:S(2)}, u32[]{:S(2)}) collective-permute-start(f32[64,512]{1,0:T(8,128)S(1)} %collective-permute-done.1.refs_2_), channel_id=1, source_target_pairs={{0,1},{1,0},{2,3},{3,2},{4,5},{5,4},{6,7},{7,6},{8,9},{9,8},{10,11... | collective-permute-start | bytes 393224 | tf_op jit(solution)/shard_map/ppermute | solution.py:389
  9.8 10.9 %copy-start = (f32[1,384,1536]{2,1,0:T(8,128)S(1)}, f32[1,384,1536]{2,1,0:T(8,128)}, u32[]{:S(2)}) copy-start(f32[1,384,1536]{2,1,0:T(8,128)} %param.33) | copy-start | bytes 7077892
  9.8 13.6 %copy-start.5 = (f32[1,384,1536]{2,1,0:T(8,128)S(1)}, f32[1,384,1536]{2,1,0:T(8,128)}, u32[]{:S(2)}) copy-start(f32[1,384,1536]{2,1,0:T(8,128)} %param.34) | copy-start | bytes 7077892
  12.6 1.8 %collective-permute-start.3 = (f32[2,32,1536]{2,1,0:T(8,128)S(1)}, f32[2,32,1536]{2,1,0:T(8,128)S(1)}, u32[]{:S(2)}, u32[]{:S(2)}) collective-permute-start(f32[2,32,1536]{2,1,0:T(8,128)S(1)} %get-tuple-element.61), channel_id=1, source_target_pairs={{0,1},{1,0},{2,3},{3,2},{4,5},{5,4},{6,7},{7,6},{8,9},{9,8},{10,11... | collective-permute-start | bytes 1179656 | tf_op jit(solution)/shard_map/ppermute | solution.py:389
  14.5 6.6 %collective-permute-start.6 = (f32[32,768]{1,0:T(8,128)S(1)}, f32[32,768]{1,0:T(8,128)S(1)}, u32[]{:S(2)}, u32[]{:S(2)}) collective-permute-start(f32[32,768]{1,0:T(8,128)S(1)} %get-tuple-element.72), channel_id=1, source_target_pairs={{0,2},{1,3},{2,0},{3,1},{4,6},{5,7},{6,4},{7,5},{8,10},{9,11},{10,... | collective-permute-start | bytes 294920 | tf_op jit(solution)/shard_map/ppermute | solution.py:389
  16.3 5.5 %collective-permute-start.7 = (f32[32,768]{1,0:T(8,128)S(1)}, f32[32,768]{1,0:T(8,128)S(1)}, u32[]{:S(2)}, u32[]{:S(2)}) collective-permute-start(f32[32,768]{1,0:T(8,128)S(1)} %get-tuple-element.73), channel_id=1, source_target_pairs={{0,4},{1,5},{2,6},{3,7},{4,0},{5,1},{6,2},{7,3},{8,12},{9,13},{10,... | collective-permute-start | bytes 294920 | tf_op jit(solution)/shard_map/ppermute | solution.py:389
  17.8 5.5 %collective-permute-start.8 = (f32[32,768]{1,0:T(8,128)S(1)}, f32[32,768]{1,0:T(8,128)S(1)}, u32[]{:S(2)}, u32[]{:S(2)}) collective-permute-start(f32[32,768]{1,0:T(8,128)S(1)} %get-tuple-element.74), channel_id=1, source_target_pairs={{0,6},{1,7},{2,4},{3,5},{4,2},{5,3},{6,0},{7,1},{8,14},{9,15},{10,... | collective-permute-start | bytes 294920 | tf_op jit(solution)/shard_map/ppermute | solution.py:389
  18.0 3.0 %collective-permute-start.5 = (f32[32,512]{1,0:T(8,128)S(1)}, f32[32,512]{1,0:T(8,128)S(1)}, u32[]{:S(2)}, u32[]{:S(2)}) collective-permute-start(f32[32,512]{1,0:T(8,128)S(1)} %get-tuple-element.68), channel_id=1, source_target_pairs={{0,1},{1,0},{2,3},{3,2},{4,5},{5,4},{6,7},{7,6},{8,9},{9,8},{10,11... | collective-permute-start | bytes 196616 | tf_op jit(solution)/shard_map/ppermute | solution.py:389
  19.3 1.4 %collective-permute-start.4 = (f32[32,384]{1,0:T(8,128)S(1)}, f32[32,384]{1,0:T(8,128)S(1)}, u32[]{:S(2)}, u32[]{:S(2)}) collective-permute-start(f32[32,384]{1,0:T(8,128)S(1)} %get-tuple-element.67), channel_id=1, source_target_pairs={{0,1},{1,0},{2,3},{3,2},{4,5},{5,4},{6,7},{7,6},{8,9},{9,8},{10,11... | collective-permute-start | bytes 147464 | tf_op jit(solution)/shard_map/ppermute | solution.py:389
  20.7 10.5 %collective-permute-start.10 = (f32[384,1536]{1,0:T(8,128)S(1)}, f32[384,1536]{1,0:T(8,128)S(1)}, u32[]{:S(2)}, u32[]{:S(2)}) collective-permute-start(f32[384,1536]{1,0:T(8,128)S(1)} %bitcast.44), channel_id=1, source_target_pairs={{0,1},{1,0},{2,3},{3,2},{4,5},{5,4},{6,7},{7,6},{8,9},{9,8},{10,11... | collective-permute-start | bytes 7077896 | tf_op jit(solution)/shard_map/ppermute | solution.py:389
  23.4 11.3 %collective-permute-start.15 = (f32[384,1536]{1,0:T(8,128)S(1)}, f32[384,1536]{1,0:T(8,128)S(1)}, u32[]{:S(2)}, u32[]{:S(2)}) collective-permute-start(f32[384,1536]{1,0:T(8,128)S(1)} %bitcast.70), channel_id=1, source_target_pairs={{0,1},{1,0},{2,3},{3,2},{4,5},{5,4},{6,7},{7,6},{8,9},{9,8},{10,11... | collective-permute-start | bytes 7077896 | tf_op jit(solution)/shard_map/ppermute | solution.py:389
  23.5 5.7 %collective-permute-start.12 = (f32[32,768]{1,0:T(8,128)S(1)}, f32[32,768]{1,0:T(8,128)S(1)}, u32[]{:S(2)}, u32[]{:S(2)}) collective-permute-start(f32[32,768]{1,0:T(8,128)S(1)} %get-tuple-element.73), channel_id=1, source_target_pairs={{0,2},{1,3},{2,0},{3,1},{4,8},{5,9},{6,10},{7,11},{8,4},{9,5},{10,... | collective-permute-start | bytes 294920 | tf_op jit(solution)/shard_map/ppermute | solution.py:389
  24.6 6.5 %collective-permute-start.13 = (f32[32,768]{1,0:T(8,128)S(1)}, f32[32,768]{1,0:T(8,128)S(1)}, u32[]{:S(2)}, u32[]{:S(2)}) collective-permute-start(f32[32,768]{1,0:T(8,128)S(1)} %get-tuple-element.74), channel_id=1, source_target_pairs={{0,2},{1,3},{2,0},{3,1},{4,10},{5,11},{6,8},{7,9},{8,6},{9,7},{10,... | collective-permute-start | bytes 294920 | tf_op jit(solution)/shard_map/ppermute | solution.py:389
  25.6 5.6 %collective-permute-start.11 = (f32[32,768]{1,0:T(8,128)S(1)}, f32[32,768]{1,0:T(8,128)S(1)}, u32[]{:S(2)}, u32[]{:S(2)}) collective-permute-start(f32[32,768]{1,0:T(8,128)S(1)} %shard_map.223.refs_0_.refs_5_), channel_id=1, source_target_pairs={{0,4},{1,5},{2,6},{3,7},{4,0},{5,1},{6,2},{7,3},{8,12},{9,13},{10,... | collective-permute-start | bytes 294920 | tf_op jit(solution)/shard_map/ppermute | solution.py:389
  29.1 5.5 %collective-permute-start.9 = (f32[32,768]{1,0:T(8,128)S(1)}, f32[32,768]{1,0:T(8,128)S(1)}, u32[]{:S(2)}, u32[]{:S(2)}) collective-permute-start(f32[32,768]{1,0:T(8,128)S(1)} %shard_map.223.refs_0_.refs_5_), channel_id=1, source_target_pairs={{0,6},{1,7},{2,4},{3,5},{4,2},{5,3},{6,0},{7,1},{8,14},{9,15},{10,... | collective-permute-start | bytes 294920 | tf_op jit(solution)/shard_map/ppermute | solution.py:389
  31.2 3.5 %copy-start.1 = (f32[1,384,1536]{2,1,0:T(8,128)S(1)}, f32[1,384,1536]{2,1,0:T(8,128)}, u32[]{:S(2)}) copy-start(f32[1,384,1536]{2,1,0:T(8,128)} %param.35) | copy-start | bytes 7077892
  34.7 7.4 %collective-permute-start.18 = (f32[384,1536]{1,0:T(8,128)S(1)}, f32[384,1536]{1,0:T(8,128)S(1)}, u32[]{:S(2)}, u32[]{:S(2)}) collective-permute-start(f32[384,1536]{1,0:T(8,128)S(1)} %bitcast.51), channel_id=1, source_target_pairs={{0,1},{1,0},{2,3},{3,2},{4,5},{5,4},{6,7},{7,6},{8,9},{9,8},{10,11... | collective-permute-start | bytes 7077896 | tf_op jit(solution)/shard_map/ppermute | solution.py:389
  34.8 5.7 %collective-permute-start.16 = (f32[32,768]{1,0:T(8,128)S(1)}, f32[32,768]{1,0:T(8,128)S(1)}, u32[]{:S(2)}, u32[]{:S(2)}) collective-permute-start(f32[32,768]{1,0:T(8,128)S(1)} %shard_map.226.refs_5_), channel_id=1, source_target_pairs={{0,2},{1,3},{2,0},{3,1},{4,8},{5,9},{6,10},{7,11},{8,4},{9,5},{10,... | collective-permute-start | bytes 294920 | tf_op jit(solution)/shard_map/ppermute | solution.py:389
  35.9 6.2 %collective-permute-start.14 = (f32[32,768]{1,0:T(8,128)S(1)}, f32[32,768]{1,0:T(8,128)S(1)}, u32[]{:S(2)}, u32[]{:S(2)}) collective-permute-start(f32[32,768]{1,0:T(8,128)S(1)} %shard_map.226.refs_5_), channel_id=1, source_target_pairs={{0,2},{1,3},{2,0},{3,1},{4,10},{5,11},{6,8},{7,9},{8,6},{9,7},{10,... | collective-permute-start | bytes 294920 | tf_op jit(solution)/shard_map/ppermute | solution.py:389
  42.3 14.1 %collective-permute-start.22 = (f32[512,1536]{1,0:T(8,128)S(1)}, f32[512,1536]{1,0:T(8,128)S(1)}, u32[]{:S(2)}, u32[]{:S(2)}) collective-permute-start(f32[512,1536]{1,0:T(8,128)S(1)} %bitcast.63), channel_id=1, source_target_pairs={{0,1},{1,0},{2,3},{3,2},{4,5},{5,4},{6,7},{7,6},{8,9},{9,8},{10,11... | collective-permute-start | bytes 9437192 | tf_op jit(solution)/shard_map/ppermute | solution.py:389
  42.3 6.4 %collective-permute-start.19 = (f32[32,768]{1,0:T(8,128)S(1)}, f32[32,768]{1,0:T(8,128)S(1)}, u32[]{:S(2)}, u32[]{:S(2)}) collective-permute-start(f32[32,768]{1,0:T(8,128)S(1)} %shard_map.228.refs_5_), channel_id=1, source_target_pairs={{0,4},{1,5},{2,6},{3,7},{4,0},{5,1},{6,2},{7,3},{8,12},{9,13},{10,... | collective-permute-start | bytes 294920 | tf_op jit(solution)/shard_map/ppermute | solution.py:389
  45.1 5.8 %collective-permute-start.17 = (f32[32,768]{1,0:T(8,128)S(1)}, f32[32,768]{1,0:T(8,128)S(1)}, u32[]{:S(2)}, u32[]{:S(2)}) collective-permute-start(f32[32,768]{1,0:T(8,128)S(1)} %shard_map.228.refs_5_), channel_id=1, source_target_pairs={{0,6},{1,7},{2,4},{3,5},{4,2},{5,3},{6,0},{7,1},{8,14},{9,15},{10,... | collective-permute-start | bytes 294920 | tf_op jit(solution)/shard_map/ppermute | solution.py:389
  50.9 4.7 %collective-permute-start.20 = (f32[32,768]{1,0:T(8,128)S(1)}, f32[32,768]{1,0:T(8,128)S(1)}, u32[]{:S(2)}, u32[]{:S(2)}) collective-permute-start(f32[32,768]{1,0:T(8,128)S(1)} %shard_map.230.refs_0_), channel_id=1, source_target_pairs={{0,2},{1,3},{2,0},{3,1},{4,6},{5,7},{6,4},{7,5},{8,10},{9,11},{10,... | collective-permute-start | bytes 294920 | tf_op jit(solution)/shard_map/ppermute | solution.py:389
  52.9 3.5 %copy-start.4 = (f32[1,512,1536]{2,1,0:T(8,128)S(1)}, f32[1,512,1536]{2,1,0:T(8,128)}, u32[]{:S(2)}) copy-start(f32[1,512,1536]{2,1,0:T(8,128)} %param.31) | copy-start | bytes 9437188
  56.4 8.0 %collective-permute-start.25 = (f32[512,1536]{1,0:T(8,128)S(1)}, f32[512,1536]{1,0:T(8,128)S(1)}, u32[]{:S(2)}, u32[]{:S(2)}) collective-permute-start(f32[512,1536]{1,0:T(8,128)S(1)} %bitcast.67), channel_id=1, source_target_pairs={{0,1},{1,0},{2,3},{3,2},{4,5},{5,4},{6,7},{7,6},{8,9},{9,8},{10,11... | collective-permute-start | bytes 9437192 | tf_op jit(solution)/shard_map/ppermute | solution.py:389
  56.5 5.2 %collective-permute-start.23 = (f32[32,768]{1,0:T(8,128)S(1)}, f32[32,768]{1,0:T(8,128)S(1)}, u32[]{:S(2)}, u32[]{:S(2)}) collective-permute-start(f32[32,768]{1,0:T(8,128)S(1)} %shard_map.232.refs_4_.refs_5_), channel_id=1, source_target_pairs={{0,4},{1,5},{2,6},{3,7},{4,0},{5,1},{6,2},{7,3},{8,12},{9,13},{10,... | collective-permute-start | bytes 294920 | tf_op jit(solution)/shard_map/ppermute | solution.py:389
  58.2 6.3 %collective-permute-start.21 = (f32[32,768]{1,0:T(8,128)S(1)}, f32[32,768]{1,0:T(8,128)S(1)}, u32[]{:S(2)}, u32[]{:S(2)}) collective-permute-start(f32[32,768]{1,0:T(8,128)S(1)} %shard_map.232.refs_4_.refs_5_), channel_id=1, source_target_pairs={{0,6},{1,7},{2,4},{3,5},{4,2},{5,3},{6,0},{7,1},{8,14},{9,15},{10,... | collective-permute-start | bytes 294920 | tf_op jit(solution)/shard_map/ppermute | solution.py:389
  61.7 2.8 %copy-start.2 = (f32[1,512,2048]{2,1,0:T(8,128)S(1)}, f32[1,512,2048]{2,1,0:T(8,128)}, u32[]{:S(2)}) copy-start(f32[1,512,2048]{2,1,0:T(8,128)} %param.30) | copy-start | bytes 12582916
  64.5 27.4 %collective-permute-start.30 = (f32[512,2048]{1,0:T(8,128)S(1)}, f32[512,2048]{1,0:T(8,128)S(1)}, u32[]{:S(2)}, u32[]{:S(2)}) collective-permute-start(f32[512,2048]{1,0:T(8,128)S(1)} %bitcast.59), channel_id=1, source_target_pairs={{0,1},{1,0},{2,3},{3,2},{4,5},{5,4},{6,7},{7,6},{8,9},{9,8},{10,11... | collective-permute-start | bytes 12582920 | tf_op jit(solution)/shard_map/ppermute | solution.py:389
  64.5 5.7 %collective-permute-start.26 = (f32[32,768]{1,0:T(8,128)S(1)}, f32[32,768]{1,0:T(8,128)S(1)}, u32[]{:S(2)}, u32[]{:S(2)}) collective-permute-start(f32[32,768]{1,0:T(8,128)S(1)} %shard_map.234.refs_5_), channel_id=1, source_target_pairs={{0,2},{1,3},{2,0},{3,1},{4,8},{5,9},{6,10},{7,11},{8,4},{9,5},{10,... | collective-permute-start | bytes 294920 | tf_op jit(solution)/shard_map/ppermute | solution.py:389
  65.5 6.3 %collective-permute-start.24 = (f32[32,768]{1,0:T(8,128)S(1)}, f32[32,768]{1,0:T(8,128)S(1)}, u32[]{:S(2)}, u32[]{:S(2)}) collective-permute-start(f32[32,768]{1,0:T(8,128)S(1)} %shard_map.234.refs_5_), channel_id=1, source_target_pairs={{0,2},{1,3},{2,0},{3,1},{4,10},{5,11},{6,8},{7,9},{8,6},{9,7},{10,... | collective-permute-start | bytes 294920 | tf_op jit(solution)/shard_map/ppermute | solution.py:389
  71.9 6.7 %collective-permute-start.28 = (f32[32,768]{1,0:T(8,128)S(1)}, f32[32,768]{1,0:T(8,128)S(1)}, u32[]{:S(2)}, u32[]{:S(2)}) collective-permute-start(f32[32,768]{1,0:T(8,128)S(1)} %shard_map.236.refs_5_), channel_id=1, source_target_pairs={{0,4},{1,5},{2,6},{3,7},{4,0},{5,1},{6,2},{7,3},{8,12},{9,13},{10,... | collective-permute-start | bytes 294920 | tf_op jit(solution)/shard_map/ppermute | solution.py:389
  75.8 5.5 %collective-permute-start.27 = (f32[32,768]{1,0:T(8,128)S(1)}, f32[32,768]{1,0:T(8,128)S(1)}, u32[]{:S(2)}, u32[]{:S(2)}) collective-permute-start(f32[32,768]{1,0:T(8,128)S(1)} %shard_map.236.refs_5_), channel_id=1, source_target_pairs={{0,6},{1,7},{2,4},{3,5},{4,2},{5,3},{6,0},{7,1},{8,14},{9,15},{10,... | collective-permute-start | bytes 294920 | tf_op jit(solution)/shard_map/ppermute | solution.py:389
  82.1 6.6 %collective-permute-start.34 = (f32[32,768]{1,0:T(8,128)S(1)}, f32[32,768]{1,0:T(8,128)S(1)}, u32[]{:S(2)}, u32[]{:S(2)}) collective-permute-start(f32[32,768]{1,0:T(8,128)S(1)} %shard_map.238.refs_0_), channel_id=1, source_target_pairs={{0,2},{1,3},{2,0},{3,1},{4,6},{5,7},{6,4},{7,5},{8,10},{9,11},{10,... | collective-permute-start | bytes 294920 | tf_op jit(solution)/shard_map/ppermute | solution.py:389
  83.2 8.6 %collective-permute-start.32 = (f32[32,768]{1,0:T(8,128)S(1)}, f32[32,768]{1,0:T(8,128)S(1)}, u32[]{:S(2)}, u32[]{:S(2)}) collective-permute-start(f32[32,768]{1,0:T(8,128)S(1)} %shard_map.238.refs_0_), channel_id=1, source_target_pairs={{0,4},{1,5},{2,6},{3,7},{4,0},{5,1},{6,2},{7,3},{8,12},{9,13},{10,... | collective-permute-start | bytes 294920 | tf_op jit(solution)/shard_map/ppermute | solution.py:389
  83.6 8.2 %collective-permute-start.33 = (f32[32,768]{1,0:T(8,128)S(1)}, f32[32,768]{1,0:T(8,128)S(1)}, u32[]{:S(2)}, u32[]{:S(2)}) collective-permute-start(f32[32,768]{1,0:T(8,128)S(1)} %shard_map.238.refs_0_), channel_id=1, source_target_pairs={{0,2},{1,3},{2,0},{3,1},{4,8},{5,9},{6,10},{7,11},{8,4},{9,5},{10,... | collective-permute-start | bytes 294920 | tf_op jit(solution)/shard_map/ppermute | solution.py:389
  84.7 7.1 %collective-permute-start.29 = (f32[32,768]{1,0:T(8,128)S(1)}, f32[32,768]{1,0:T(8,128)S(1)}, u32[]{:S(2)}, u32[]{:S(2)}) collective-permute-start(f32[32,768]{1,0:T(8,128)S(1)} %shard_map.238.refs_0_), channel_id=1, source_target_pairs={{0,6},{1,7},{2,4},{3,5},{4,2},{5,3},{6,0},{7,1},{8,14},{9,15},{10,... | collective-permute-start | bytes 294920 | tf_op jit(solution)/shard_map/ppermute | solution.py:389
  88.8 5.6 %collective-permute-start.31 = (f32[32,768]{1,0:T(8,128)S(1)}, f32[32,768]{1,0:T(8,128)S(1)}, u32[]{:S(2)}, u32[]{:S(2)}) collective-permute-start(f32[32,768]{1,0:T(8,128)S(1)} %shard_map.238.refs_0_), channel_id=1, source_target_pairs={{0,2},{1,3},{2,0},{3,1},{4,10},{5,11},{6,8},{7,9},{8,6},{9,7},{10,... | collective-permute-start | bytes 294920 | tf_op jit(solution)/shard_map/ppermute | solution.py:389
  94.3 2.2 %copy-start.10 = (f32[1,384,64]{1,2,0:T(8,128)S(1)}, f32[1,384,64]{1,2,0:T(8,128)}, u32[]{:S(2)}) copy-start(f32[1,384,64]{1,2,0:T(8,128)} %param.28) | copy-start | bytes 294916
  94.3 2.2 %copy-start.11 = (f32[1,384,64]{1,2,0:T(8,128)S(1)}, f32[1,384,64]{1,2,0:T(8,128)}, u32[]{:S(2)}) copy-start(f32[1,384,64]{1,2,0:T(8,128)} %param.29) | copy-start | bytes 294916
  94.4 5.0 %collective-permute-start.35 = (f32[32,1024]{1,0:T(8,128)S(1)}, f32[32,1024]{1,0:T(8,128)S(1)}, u32[]{:S(2)}, u32[]{:S(2)}) collective-permute-start(f32[32,1024]{1,0:T(8,128)S(1)} %shard_map.242.refs_0_), channel_id=1, source_target_pairs={{0,2},{1,3},{2,0},{3,1},{4,6},{5,7},{6,4},{7,5},{8,10},{9,11},{10,... | collective-permute-start | bytes 393224 | tf_op jit(solution)/shard_map/ppermute | solution.py:389
  95.2 1.3 %collective-permute-start.36 = (f32[32,384]{1,0:T(8,128)S(1)}, f32[32,384]{1,0:T(8,128)S(1)}, u32[]{:S(2)}, u32[]{:S(2)}) collective-permute-start(f32[32,384]{1,0:T(8,128)S(1)} %get-tuple-element.90), channel_id=1, source_target_pairs={{0,1},{1,0},{2,3},{3,2},{4,5},{5,4},{6,7},{7,6},{8,9},{9,8},{10,11... | collective-permute-start | bytes 147464 | tf_op jit(solution)/shard_map/ppermute | solution.py:389
  99.4 2.7 %copy-start.6 = (f32[1,512,64]{1,2,0:T(8,128)S(1)}, f32[1,512,64]{1,2,0:T(8,128)}, u32[]{:S(2)}) copy-start(f32[1,512,64]{1,2,0:T(8,128)} %param.24) | copy-start | bytes 393220
  99.4 2.7 %copy-start.7 = (f32[1,512,64]{1,2,0:T(8,128)S(1)}, f32[1,512,64]{1,2,0:T(8,128)}, u32[]{:S(2)}) copy-start(f32[1,512,64]{1,2,0:T(8,128)} %param.25) | copy-start | bytes 393220
  99.4 2.7 %copy-start.8 = (f32[1,512,64]{1,2,0:T(8,128)S(1)}, f32[1,512,64]{1,2,0:T(8,128)}, u32[]{:S(2)}) copy-start(f32[1,512,64]{1,2,0:T(8,128)} %param.26) | copy-start | bytes 393220
  100.8 1.3 %collective-permute-start.37 = (f32[32,512]{1,0:T(8,128)S(1)}, f32[32,512]{1,0:T(8,128)S(1)}, u32[]{:S(2)}, u32[]{:S(2)}) collective-permute-start(f32[32,512]{1,0:T(8,128)S(1)} %get-tuple-element.97), channel_id=1, source_target_pairs={{0,1},{1,0},{2,3},{3,2},{4,5},{5,4},{6,7},{7,6},{8,9},{9,8},{10,11... | collective-permute-start | bytes 196616 | tf_op jit(solution)/shard_map/ppermute | solution.py:389
  (2 other events, 4.1 us)

commit v11 on v10

--- a/solution.py
+++ b/solution.py
@@ -235,23 +235,11 @@
     return jnp.concatenate([jnp.where(second, other, own), jnp.where(second, own, other)], axis=axis)
 
 
-def less_in(stories_of, value, forces):
-    story, count = lax.axis_index("story"), lax.axis_size("story")
-    there = (lax.rem(story, 2) == stories_of) & (story + 1 < count)
-    for force in forces:
-        value = jnp.where(there, value - force[...], value)
-    return value
-
-
-def condensed_kernel(load, forces, even, out):
+def condensed_kernel(load, forces, out):
     value = by_core(load[0][...], load[1][...], 1)
     for force in forces:
         value = value - force[...]
-    out[...] = less_in(0, value, even)
-
-
-def odd_kernel(value, odd, out):
-    out[...] = less_in(1, value[0][...], odd)
+    out[...] = value
 
 
 def halves_kernel(whole, mine, theirs):
@@ -510,19 +498,16 @@
     mine_int, theirs_int = call(records_kernel, [(half, own_int)] * 2, [load_late])
     halves = lax.optimization_barrier([mv.core(theirs_face), mv.core(theirs_int)])
     load_face_half, load_int_half = [mine_face, halves[0]], [mine_int, halves[1]]
-    below_parts = chunks[mv.chips :]
-    even = [mv.story(below_parts[j], 0, j) for j in range(mv.chips)]
-    forces = [chunks[0]] + [mv.chip(chunks[j], j) for j in range(1, mv.chips)]
+    forces = [mv.shift(chunks[mv.chips], -1, 0)]
+    for j in range(1, mv.chips):
+        forces += [mv.chip(chunks[j], j), mv.shift(chunks[mv.chips + j], -1, j)]
     shape = [(half, rows_face)]
-    (condensed,) = call(condensed_kernel, shape, load_face_half, forces, even)
-    odd = [mv.story(below_parts[j], 1, j) for j in range(mv.chips)]
+    (condensed,) = call(condensed_kernel, shape, load_face_half, [chunks[0]] + forces)
 
     forward = condensed
     pivot_other = others(pivot[0], [condensed])
     for k in range(1, mv.stories):
         came = mv.gather_story(forward, (k - 1) % 2)
-        if k == 1:
-            (condensed,) = call(odd_kernel, shape, [condensed], odd)
         if k == min(2, mv.stories - 1):
             upper_other = others(upper[0], [pivot_other, forward])
             came[-1], pivot_other = lax.optimization_barrier([came[-1], pivot_other])
@@ -552,6 +537,9 @@
         if k == max(mv.stories - 3, 0):
             inverse_other = others(interior_inverse[0], [below_other, face])
             came[-1], below_other = lax.optimization_barrier([came[-1], below_other])
+        if k == 0:
+            late, came[0] = lax.optimization_barrier([face, came[0]])
+            odd = mv.gather_story(late, 1)
         (face,) = call(
             functools.partial(step_kernel, from_chip(len(came), len(came) - 1), k),
             shape,
@@ -560,8 +548,8 @@
         )
 
     here = mv.gather_chips(face)
+    here[0], *odd = lax.optimization_barrier([here[0], *odd])
     even = mv.gather_story(face, 0)
-    odd = mv.gather_story(face, 1)
     even[-1], inverse_other = lax.optimization_barrier([even[-1], inverse_other])
     rows = [couple_above[0], above_other]
     sofar = []

time: 103 us -> 98.4 us (0.955)
  waiting for transfers between devices: 47.9 us -> 43.5 us
    ppermute x38 -> x34, waiting for transfers between devices: 47.9 us -> 40.4 us  [permute(): return lax.ppermute(value, AXES, pairs)]
    ppermute x38 -> x34, starting transfers between devices: 35.4 us -> 32.2 us  [permute(): return lax.ppermute(value, AXES, pairs)]
    ppermute x0 -> x2, waiting for transfers between devices: none -> 3.04 us  [shift(): return lax.ppermute(value, AXES, pairs)]
    ppermute x0 -> x2, starting transfers between devices: none -> 2.57 us  [shift(): return lax.ppermute(value, AXES, pairs)]
    pallas_call x28 -> x27, Pallas kernels: 12.7 us -> 12.7 us  [call(): pl.pallas_call(body, in_specs=[VMEM] * len(flat) + [pl.BlockSpec(memory_s...]
  transfers between devices with their start and end apart: 38 -> 36, of which waited for: 24 -> 22; matrix products, arithmetic and copies ran while one was open for 0% -> 0% of each run, Pallas kernels for 12% -> 12%
where the time goes in v11:
time: 98.4 us; the launch traced here: 97.8 us
  waiting for transfers between devices  43.5 us (44%)
  starting transfers between devices  34.7 us (35%)
  Pallas kernels  18.4 us (19%)
    ppermute x34, waiting for transfers between devices, permute(): return lax.ppermute(value, AXES, pairs)  40.4 us
    ppermute x34, starting transfers between devices, permute(): return lax.ppermute(value, AXES, pairs)  32.2 us
    pallas_call x27, Pallas kernels, call(): pl.pallas_call(body, in_specs=[VMEM] * len(flat) + [pl.BlockSpec(memory_s...  12.7 us
    pallas_call x1, Pallas kernels, staged(): pl.pallas_call(body, in_specs=[pl.BlockSpec(memory_space=pltpu.HBM)] * co...  3.16 us
    ppermute x2, waiting for transfers between devices, shift(): return lax.ppermute(value, AXES, pairs)  3.04 us
    ppermute x2, starting transfers between devices, shift(): return lax.ppermute(value, AXES, pairs)  2.57 us
    pallas_call x2, Pallas kernels, fetched(): pl.pallas_call(body, in_specs=[pl.BlockSpec(memory_space=pltpu.HBM)] * co...  2.48 us
  transfers between devices with their start and end apart: 36, of which 22 were waited for; matrix products, arithmetic and copies ran while one was open for 0% of the time, Pallas kernels for 12%

profile of v11, /device:TPU:0, one launch (start us, length us, event | category | flops | bytes accessed | tf_op | source)
XLA Modules:
  0.0 97.8 jit_solution(4668165145969016549)
XLA Ops:
  0.6 1.3 %shard_map.217 = (f32[64,512]{1,0:T(8,128)S(1)}, f32[64,128]{1,0:T(8,128)S(1)}) custom-call(s32[1,64]{1,0:T(1,128)} %bitcast.86, f32[1,512]{1,0:T(1,128)} %bitcast.85, f32[1,512]{1,0:T(1,128)} %refs_2_.1, f32[1,512]{1,0:T(1,128)} %refs_3_.1, f32[64,512]{1,0:T(8,128)} %bitcast.73, f32[64,512]{1,0:T(8,128)} %bitcast.75, f32[64,512]{1,0:T(8,128)} %bitcast.77), custom_call_target="tpu_custom_call" | custom-call | tf_op jit(solution)/shard_map/pallas_call | solution.py:189
  2.0 3.0 %collective-permute-start.1 = (f32[64,512]{1,0:T(8,128)S(1)}, f32[64,512]{1,0:T(8,128)S(1)}, u32[]{:S(2)}, u32[]{:S(2)}) collective-permute-start(f32[64,512]{1,0:T(8,128)S(1)} %get-tuple-element.68.refs_0_), channel_id=1, source_target_pairs={{0,2},{1,3},{2,0},{3,1},{4,6},{5,7},{6,4},{7,5},{8,10},{9,11},{10,... | collective-permute-start | bytes 393224 | tf_op jit(solution)/shard_map/ppermute | solution.py:377
  5.0 3.2 %shard_map.218.refs_4_ = f32[512,3584]{1,0:T(8,128)S(1)} custom-call(f32[512,2048]{1,0:T(8,128)} %bitcast.58, f32[512,1536]{1,0:T(8,128)} %bitcast.62), custom_call_target="tpu_custom_call" | custom-call | tf_op jit(solution)/shard_map/pallas_call | solution.py:136
  8.7 1.1 %collective-permute-done.2.refs_3_ = f32[64,512]{1,0:T(8,128)S(1)} collective-permute-done((f32[64,512]{1,0:T(8,128)S(1)}, f32[64,512]{1,0:T(8,128)S(1)}, u32[]{:S(2)}, u32[]{:S(2)}) %collective-permute-start.2) | collective-permute-done | bytes 131104 | tf_op jit(solution)/shard_map/ppermute | solution.py:377
  9.8 2.8 %shard_map.219 = (f32[2,32,1536]{2,1,0:T(8,128)S(1)}, f32[2,32,1536]{2,1,0:T(8,128)S(1)}) custom-call(f32[64,512]{1,0:T(8,128)S(1)} %get-tuple-element.68.refs_0_, f32[64,512]{1,0:T(8,128)S(1)} %collective-permute-done.refs_1_, f32[64,512]{1,0:T(8,128)S(1)} %collective-permute-done.1.refs_2_, f32[64,512]{1,0:T(8,128)S(1)} %collective-permute-done.2.refs_3_, ...), custom_call_target="tpu_custom_call" | custom-call | tf_op jit(solution)/shard_map/pallas_call | solution.py:98
  12.9 1.5 %collective-permute-done.3.refs_1_ = f32[2,32,1536]{2,1,0:T(8,128)S(1)} collective-permute-done((f32[2,32,1536]{2,1,0:T(8,128)S(1)}, f32[2,32,1536]{2,1,0:T(8,128)S(1)}, u32[]{:S(2)}, u32[]{:S(2)}) %collective-permute-start.3) | collective-permute-done | bytes 393248 | tf_op jit(solution)/shard_map/ppermute | solution.py:377
  14.5 1.3 %collective-permute-start.6 = (f32[32,768]{1,0:T(8,128)S(1)}, f32[32,768]{1,0:T(8,128)S(1)}, u32[]{:S(2)}, u32[]{:S(2)}) collective-permute-start(f32[32,768]{1,0:T(8,128)S(1)} %get-tuple-element.77), channel_id=1, source_target_pairs={{4,0},{5,1},{6,2},{7,3},{8,4},{9,5},{10,6},{11,7},{12,8},{13,9},{1... | collective-permute-start | bytes 294920 | tf_op jit(solution)/shard_map/ppermute | solution.py:423
  15.8 1.8 %collective-permute-start.7 = (f32[32,768]{1,0:T(8,128)S(1)}, f32[32,768]{1,0:T(8,128)S(1)}, u32[]{:S(2)}, u32[]{:S(2)}) collective-permute-start(f32[32,768]{1,0:T(8,128)S(1)} %get-tuple-element.78), channel_id=1, source_target_pairs={{0,2},{1,3},{2,0},{3,1},{4,6},{5,7},{6,4},{7,5},{8,10},{9,11},{10,... | collective-permute-start | bytes 294920 | tf_op jit(solution)/shard_map/ppermute | solution.py:377
  17.6 1.3 %collective-permute-start.8 = (f32[32,768]{1,0:T(8,128)S(1)}, f32[32,768]{1,0:T(8,128)S(1)}, u32[]{:S(2)}, u32[]{:S(2)}) collective-permute-start(f32[32,768]{1,0:T(8,128)S(1)} %get-tuple-element.79), channel_id=1, source_target_pairs={{4,2},{5,3},{6,0},{7,1},{8,6},{9,7},{10,4},{11,5},{12,10},{13,11},... | collective-permute-start | bytes 294920 | tf_op jit(solution)/shard_map/ppermute | solution.py:423
  19.0 1.2 %shard_map.222 = (f32[32,384]{1,0:T(8,128)S(1)}, f32[32,384]{1,0:T(8,128)S(1)}) custom-call(f32[1,384]{1,0:T(1,128)} %refs_0_.1, f32[1,384]{1,0:T(1,128)} %refs_1_.1, f32[64,384]{1,0:T(8,128)} %bitcast.79, f32[64,384]{1,0:T(8,128)} %bitcast.81, f32[64,384]{1,0:T(8,128)} %bitcast.83, f32[64,128]{1,0:T(8,128)S(1)} %get-tuple-element.71.refs_5_), custom_call_target="tpu_custom_call" | custom-call | tf_op jit(solution)/shard_map/pallas_call | solution.py:189
  20.7 0.9 collective-permute-done.4.refs_1_
  21.9 3.0 %collective-permute-done.8.refs_5_ = f32[32,768]{1,0:T(8,128)S(1)} collective-permute-done((f32[32,768]{1,0:T(8,128)S(1)}, f32[32,768]{1,0:T(8,128)S(1)}, u32[]{:S(2)}, u32[]{:S(2)}) %collective-permute-start.8) | collective-permute-done | bytes 98336 | tf_op jit(solution)/shard_map/ppermute | solution.py:423
  25.1 2.7 %collective-permute-start.11 = (f32[32,768]{1,0:T(8,128)S(1)}, f32[32,768]{1,0:T(8,128)S(1)}, u32[]{:S(2)}, u32[]{:S(2)}) collective-permute-start(f32[32,768]{1,0:T(8,128)S(1)} %shard_map.223.refs_4_.refs_5_), channel_id=1, source_target_pairs={{0,4},{1,5},{2,6},{3,7},{4,0},{5,1},{6,2},{7,3},{8,12},{9,13},{10,... | collective-permute-start | bytes 294920 | tf_op jit(solution)/shard_map/ppermute | solution.py:377
  27.8 3.6 %collective-permute-done.11.refs_0_ = f32[32,768]{1,0:T(8,128)S(1)} collective-permute-done((f32[32,768]{1,0:T(8,128)S(1)}, f32[32,768]{1,0:T(8,128)S(1)}, u32[]{:S(2)}, u32[]{:S(2)}) %collective-permute-start.11) | collective-permute-done | bytes 98336 | tf_op jit(solution)/shard_map/ppermute | solution.py:377
  31.4 2.1 %collective-permute-done.9.refs_0_ = f32[32,768]{1,0:T(8,128)S(1)} collective-permute-done((f32[32,768]{1,0:T(8,128)S(1)}, f32[32,768]{1,0:T(8,128)S(1)}, u32[]{:S(2)}, u32[]{:S(2)}) %collective-permute-start.9) | collective-permute-done | bytes 98336 | tf_op jit(solution)/shard_map/ppermute | solution.py:377
  33.7 1.3 %collective-permute-start.14 = (f32[32,768]{1,0:T(8,128)S(1)}, f32[32,768]{1,0:T(8,128)S(1)}, u32[]{:S(2)}, u32[]{:S(2)}) collective-permute-start(f32[32,768]{1,0:T(8,128)S(1)} %shard_map.225.refs_5_), channel_id=1, source_target_pairs={{0,2},{1,3},{2,0},{3,1},{4,8},{5,9},{6,10},{7,11},{8,4},{9,5},{10,... | collective-permute-start | bytes 294920 | tf_op jit(solution)/shard_map/ppermute | solution.py:377
  35.8 3.6 %collective-permute-done.14.refs_0_ = f32[32,768]{1,0:T(8,128)S(1)} collective-permute-done((f32[32,768]{1,0:T(8,128)S(1)}, f32[32,768]{1,0:T(8,128)S(1)}, u32[]{:S(2)}, u32[]{:S(2)}) %collective-permute-start.14) | collective-permute-done | bytes 98336 | tf_op jit(solution)/shard_map/ppermute | solution.py:377
  39.3 1.7 %collective-permute-done.12.refs_0_ = f32[32,768]{1,0:T(8,128)S(1)} collective-permute-done((f32[32,768]{1,0:T(8,128)S(1)}, f32[32,768]{1,0:T(8,128)S(1)}, u32[]{:S(2)}, u32[]{:S(2)}) %collective-permute-start.12) | collective-permute-done | bytes 98336 | tf_op jit(solution)/shard_map/ppermute | solution.py:377
  41.2 3.2 %collective-permute-start.17 = (f32[32,768]{1,0:T(8,128)S(1)}, f32[32,768]{1,0:T(8,128)S(1)}, u32[]{:S(2)}, u32[]{:S(2)}) collective-permute-start(f32[32,768]{1,0:T(8,128)S(1)} %shard_map.227.refs_5_), channel_id=1, source_target_pairs={{0,4},{1,5},{2,6},{3,7},{4,0},{5,1},{6,2},{7,3},{8,12},{9,13},{10,... | collective-permute-start | bytes 294920 | tf_op jit(solution)/shard_map/ppermute | solution.py:377
  44.5 3.6 %collective-permute-done.17.refs_0_ = f32[32,768]{1,0:T(8,128)S(1)} collective-permute-done((f32[32,768]{1,0:T(8,128)S(1)}, f32[32,768]{1,0:T(8,128)S(1)}, u32[]{:S(2)}, u32[]{:S(2)}) %collective-permute-start.17) | collective-permute-done | bytes 98336 | tf_op jit(solution)/shard_map/ppermute | solution.py:377
  48.0 2.1 %collective-permute-done.15.refs_0_ = f32[32,768]{1,0:T(8,128)S(1)} collective-permute-done((f32[32,768]{1,0:T(8,128)S(1)}, f32[32,768]{1,0:T(8,128)S(1)}, u32[]{:S(2)}, u32[]{:S(2)}) %collective-permute-start.15) | collective-permute-done | bytes 98336 | tf_op jit(solution)/shard_map/ppermute | solution.py:377
  50.2 1.3 %collective-permute-start.18 = (f32[32,768]{1,0:T(8,128)S(1)}, f32[32,768]{1,0:T(8,128)S(1)}, u32[]{:S(2)}, u32[]{:S(2)}) collective-permute-start(f32[32,768]{1,0:T(8,128)S(1)} %shard_map.229.refs_0_), channel_id=1, source_target_pairs={{0,2},{1,3},{2,0},{3,1},{4,6},{5,7},{6,4},{7,5},{8,10},{9,11},{10,... | collective-permute-start | bytes 294920 | tf_op jit(solution)/shard_map/ppermute | solution.py:377
  52.3 2.6 %collective-permute-done.18.refs_0_ = f32[32,768]{1,0:T(8,128)S(1)} collective-permute-done((f32[32,768]{1,0:T(8,128)S(1)}, f32[32,768]{1,0:T(8,128)S(1)}, u32[]{:S(2)}, u32[]{:S(2)}) %collective-permute-start.18) | collective-permute-done | bytes 98336 | tf_op jit(solution)/shard_map/ppermute | solution.py:377
  55.8 1.7 %collective-permute-start.21 = (f32[32,768]{1,0:T(8,128)S(1)}, f32[32,768]{1,0:T(8,128)S(1)}, u32[]{:S(2)}, u32[]{:S(2)}) collective-permute-start(f32[32,768]{1,0:T(8,128)S(1)} %shard_map.231.refs_4_.refs_5_), channel_id=1, source_target_pairs={{0,4},{1,5},{2,6},{3,7},{4,0},{5,1},{6,2},{7,3},{8,12},{9,13},{10,... | collective-permute-start | bytes 294920 | tf_op jit(solution)/shard_map/ppermute | solution.py:377
  57.5 1.0 %collective-permute-start.19 = (f32[32,768]{1,0:T(8,128)S(1)}, f32[32,768]{1,0:T(8,128)S(1)}, u32[]{:S(2)}, u32[]{:S(2)}) collective-permute-start(f32[32,768]{1,0:T(8,128)S(1)} %shard_map.231.refs_4_.refs_5_), channel_id=1, source_target_pairs={{0,6},{1,7},{2,4},{3,5},{4,2},{5,3},{6,0},{7,1},{8,14},{9,15},{10,... | collective-permute-start | bytes 294920 | tf_op jit(solution)/shard_map/ppermute | solution.py:377
  58.5 2.5 %collective-permute-done.21.refs_0_ = f32[32,768]{1,0:T(8,128)S(1)} collective-permute-done((f32[32,768]{1,0:T(8,128)S(1)}, f32[32,768]{1,0:T(8,128)S(1)}, u32[]{:S(2)}, u32[]{:S(2)}) %collective-permute-start.21) | collective-permute-done | bytes 98336 | tf_op jit(solution)/shard_map/ppermute | solution.py:377
  61.0 2.7 %collective-permute-done.19.refs_0_ = f32[32,768]{1,0:T(8,128)S(1)} collective-permute-done((f32[32,768]{1,0:T(8,128)S(1)}, f32[32,768]{1,0:T(8,128)S(1)}, u32[]{:S(2)}, u32[]{:S(2)}) %collective-permute-start.19) | collective-permute-done | bytes 98336 | tf_op jit(solution)/shard_map/ppermute | solution.py:377
  63.8 1.0 %collective-permute-start.24 = (f32[32,768]{1,0:T(8,128)S(1)}, f32[32,768]{1,0:T(8,128)S(1)}, u32[]{:S(2)}, u32[]{:S(2)}) collective-permute-start(f32[32,768]{1,0:T(8,128)S(1)} %shard_map.233.refs_5_), channel_id=1, source_target_pairs={{0,2},{1,3},{2,0},{3,1},{4,8},{5,9},{6,10},{7,11},{8,4},{9,5},{10,... | collective-permute-start | bytes 294920 | tf_op jit(solution)/shard_map/ppermute | solution.py:377
  64.8 1.1 %collective-permute-start.22 = (f32[32,768]{1,0:T(8,128)S(1)}, f32[32,768]{1,0:T(8,128)S(1)}, u32[]{:S(2)}, u32[]{:S(2)}) collective-permute-start(f32[32,768]{1,0:T(8,128)S(1)} %shard_map.233.refs_5_), channel_id=1, source_target_pairs={{0,2},{1,3},{2,0},{3,1},{4,10},{5,11},{6,8},{7,9},{8,6},{9,7},{10,... | collective-permute-start | bytes 294920 | tf_op jit(solution)/shard_map/ppermute | solution.py:377
  65.9 3.6 %collective-permute-done.24.refs_0_ = f32[32,768]{1,0:T(8,128)S(1)} collective-permute-done((f32[32,768]{1,0:T(8,128)S(1)}, f32[32,768]{1,0:T(8,128)S(1)}, u32[]{:S(2)}, u32[]{:S(2)}) %collective-permute-start.24) | collective-permute-done | bytes 98336 | tf_op jit(solution)/shard_map/ppermute | solution.py:377
  69.5 1.7 %collective-permute-done.22.refs_0_ = f32[32,768]{1,0:T(8,128)S(1)} collective-permute-done((f32[32,768]{1,0:T(8,128)S(1)}, f32[32,768]{1,0:T(8,128)S(1)}, u32[]{:S(2)}, u32[]{:S(2)}) %collective-permute-start.22) | collective-permute-done | bytes 98336 | tf_op jit(solution)/shard_map/ppermute | solution.py:377
  71.2 3.8 %collective-permute-start.26 = (f32[32,768]{1,0:T(8,128)S(1)}, f32[32,768]{1,0:T(8,128)S(1)}, u32[]{:S(2)}, u32[]{:S(2)}) collective-permute-start(f32[32,768]{1,0:T(8,128)S(1)} %shard_map.235.refs_5_), channel_id=1, source_target_pairs={{0,4},{1,5},{2,6},{3,7},{4,0},{5,1},{6,2},{7,3},{8,12},{9,13},{10,... | collective-permute-start | bytes 294920 | tf_op jit(solution)/shard_map/ppermute | solution.py:377
  75.5 2.3 %collective-permute-done.26.refs_0_ = f32[32,768]{1,0:T(8,128)S(1)} collective-permute-done((f32[32,768]{1,0:T(8,128)S(1)}, f32[32,768]{1,0:T(8,128)S(1)}, u32[]{:S(2)}, u32[]{:S(2)}) %collective-permute-start.26) | collective-permute-done | bytes 98336 | tf_op jit(solution)/shard_map/ppermute | solution.py:377
  77.8 1.2 %collective-permute-start.29 = (f32[32,768]{1,0:T(8,128)S(1)}, f32[32,768]{1,0:T(8,128)S(1)}, u32[]{:S(2)}, u32[]{:S(2)}) collective-permute-start(f32[32,768]{1,0:T(8,128)S(1)} %shard_map.235.refs_5_), channel_id=1, source_target_pairs={{0,2},{1,3},{2,0},{3,1},{4,8},{5,9},{6,10},{7,11},{8,4},{9,5},{10,... | collective-permute-start | bytes 294920 | tf_op jit(solution)/shard_map/ppermute | solution.py:377
  78.9 0.9 collective-permute-start.30
  79.8 0.9 shard_map.236.refs_3_
  80.7 0.9 shard_map.237.refs_0_
  81.6 1.2 %collective-permute-start.32 = (f32[32,768]{1,0:T(8,128)S(1)}, f32[32,768]{1,0:T(8,128)S(1)}, u32[]{:S(2)}, u32[]{:S(2)}) collective-permute-start(f32[32,768]{1,0:T(8,128)S(1)} %shard_map.237.refs_0_), channel_id=1, source_target_pairs={{0,2},{1,3},{2,0},{3,1},{4,6},{5,7},{6,4},{7,5},{8,10},{9,11},{10,... | collective-permute-start | bytes 294920 | tf_op jit(solution)/shard_map/ppermute | solution.py:377
  82.8 0.9 collective-permute-start.31
  83.8 1.6 %collective-permute-start.27 = (f32[32,768]{1,0:T(8,128)S(1)}, f32[32,768]{1,0:T(8,128)S(1)}, u32[]{:S(2)}, u32[]{:S(2)}) collective-permute-start(f32[32,768]{1,0:T(8,128)S(1)} %shard_map.237.refs_0_), channel_id=1, source_target_pairs={{0,6},{1,7},{2,4},{3,5},{4,2},{5,3},{6,0},{7,1},{8,14},{9,15},{10,... | collective-permute-start | bytes 294920 | tf_op jit(solution)/shard_map/ppermute | solution.py:377
  85.4 1.0 %collective-permute-done.30.refs_3_ = f32[32,768]{1,0:T(8,128)S(1)} collective-permute-done((f32[32,768]{1,0:T(8,128)S(1)}, f32[32,768]{1,0:T(8,128)S(1)}, u32[]{:S(2)}, u32[]{:S(2)}) %collective-permute-start.30) | collective-permute-done | bytes 98336 | tf_op jit(solution)/shard_map/ppermute | solution.py:377
  86.4 1.0 %shard_map.238.refs_3_ = f32[32,1024]{1,0:T(8,128)S(1)} custom-call(f32[32,768]{1,0:T(8,128)S(1)} %shard_map.237.refs_0_, f32[512,1536]{1,0:T(8,128)S(1)} %bitcast.64, f32[512,1536]{1,0:T(8,128)S(1)} %collective-permute-done.20.refs_2_), custom_call_target="tpu_custom_call" | custom-call | bytes 4194304 | tf_op jit(solution)/shard_map/pallas_call | solution.py:98
  87.5 1.1 %shard_map.239.refs_4_ = f32[32,1024]{1,0:T(8,128)S(1)} custom-call(f32[32,768]{1,0:T(8,128)S(1)} %collective-permute-done.32.refs_0_, f32[512,1536]{1,0:T(8,128)S(1)} %bitcast.65, f32[512,1536]{1,0:T(8,128)S(1)} %collective-permute-done.20.refs_2_, f32[32,1024]{1,0:T(8,128)S(1)} %shard_map.238.refs_3_), custom_call_target="tpu_custom_call" | custom-call | bytes 4194304 | tf_op jit(solution)/shard_map/pallas_call | solution.py:98
  89.4 1.2 %collective-permute-start.33 = (f32[32,1024]{1,0:T(8,128)S(1)}, f32[32,1024]{1,0:T(8,128)S(1)}, u32[]{:S(2)}, u32[]{:S(2)}) collective-permute-start(f32[32,1024]{1,0:T(8,128)S(1)} %shard_map.241.refs_0_), channel_id=1, source_target_pairs={{0,2},{1,3},{2,0},{3,1},{4,6},{5,7},{6,4},{7,5},{8,10},{9,11},{10,... | collective-permute-start | bytes 393224 | tf_op jit(solution)/shard_map/ppermute | solution.py:377
  90.6 1.2 %collective-permute-done.34.refs_1_ = f32[32,384]{1,0:T(8,128)S(1)} collective-permute-done((f32[32,384]{1,0:T(8,128)S(1)}, f32[32,384]{1,0:T(8,128)S(1)}, u32[]{:S(2)}, u32[]{:S(2)}) %collective-permute-start.34) | collective-permute-done | bytes 49184 | tf_op jit(solution)/shard_map/ppermute | solution.py:377
  92.6 1.3 %shard_map.244.refs_3_ = f32[32,1024]{1,0:T(8,128)S(1)} custom-call(f32[32,1024]{1,0:T(8,128)S(1)} %shard_map.241.refs_0_, f32[512,2048]{1,0:T(8,128)S(1)} %bitcast.60, f32[512,2048]{1,0:T(8,128)S(1)} %collective-permute-done.28.refs_2_), custom_call_target="tpu_custom_call" | custom-call | bytes 4194304 | tf_op jit(solution)/shard_map/pallas_call | solution.py:98
  94.4 1.3 %shard_map.245 = (f32[32,512]{1,0:T(8,128)S(1)}, f32[32,512]{1,0:T(8,128)S(1)}) custom-call(f32[32,1024]{1,0:T(8,128)S(1)} %collective-permute-done.33.refs_0_, f32[512,2048]{1,0:T(8,128)S(1)} %bitcast.61, f32[512,2048]{1,0:T(8,128)S(1)} %collective-permute-done.28.refs_2_, f32[32,1024]{1,0:T(8,128)S(1)} %shard_map.244.refs_3_), custom_call_target="tpu_custom_call" | custom-call | tf_op jit(solution)/shard_map/pallas_call | solution.py:98
  95.8 1.2 %collective-permute-done.35.refs_1_ = f32[32,512]{1,0:T(8,128)S(1)} collective-permute-done((f32[32,512]{1,0:T(8,128)S(1)}, f32[32,512]{1,0:T(8,128)S(1)}, u32[]{:S(2)}, u32[]{:S(2)}) %collective-permute-start.35) | collective-permute-done | bytes 65568 | tf_op jit(solution)/shard_map/ppermute | solution.py:377
  (78 shorter events, 8.6 us)
Async XLA Ops:
  2.0 6.5 %collective-permute-start.1 = (f32[64,512]{1,0:T(8,128)S(1)}, f32[64,512]{1,0:T(8,128)S(1)}, u32[]{:S(2)}, u32[]{:S(2)}) collective-permute-start(f32[64,512]{1,0:T(8,128)S(1)} %get-tuple-element.68.refs_0_), channel_id=1, source_target_pairs={{0,2},{1,3},{2,0},{3,1},{4,6},{5,7},{6,4},{7,5},{8,10},{9,11},{10,... | collective-permute-start | bytes 393224 | tf_op jit(solution)/shard_map/ppermute | solution.py:377
  5.0 3.8 %collective-permute-start = (f32[64,512]{1,0:T(8,128)S(1)}, f32[64,512]{1,0:T(8,128)S(1)}, u32[]{:S(2)}, u32[]{:S(2)}) collective-permute-start(f32[64,512]{1,0:T(8,128)S(1)} %get-tuple-element.68.refs_0_), channel_id=1, source_target_pairs={{0,1},{1,0},{2,3},{3,2},{4,5},{5,4},{6,7},{7,6},{8,9},{9,8},{10,11... | collective-permute-start | bytes 393224 | tf_op jit(solution)/shard_map/ppermute | solution.py:377
  8.5 1.3 %collective-permute-start.2 = (f32[64,512]{1,0:T(8,128)S(1)}, f32[64,512]{1,0:T(8,128)S(1)}, u32[]{:S(2)}, u32[]{:S(2)}) collective-permute-start(f32[64,512]{1,0:T(8,128)S(1)} %collective-permute-done.1.refs_2_), channel_id=1, source_target_pairs={{0,1},{1,0},{2,3},{3,2},{4,5},{5,4},{6,7},{7,6},{8,9},{9,8},{10,11... | collective-permute-start | bytes 393224 | tf_op jit(solution)/shard_map/ppermute | solution.py:377
  9.8 11.7 %copy-start = (f32[1,384,1536]{2,1,0:T(8,128)S(1)}, f32[1,384,1536]{2,1,0:T(8,128)}, u32[]{:S(2)}) copy-start(f32[1,384,1536]{2,1,0:T(8,128)} %param.33) | copy-start | bytes 7077892
  9.8 15.2 %copy-start.5 = (f32[1,384,1536]{2,1,0:T(8,128)S(1)}, f32[1,384,1536]{2,1,0:T(8,128)}, u32[]{:S(2)}) copy-start(f32[1,384,1536]{2,1,0:T(8,128)} %param.34) | copy-start | bytes 7077892
  12.6 1.8 %collective-permute-start.3 = (f32[2,32,1536]{2,1,0:T(8,128)S(1)}, f32[2,32,1536]{2,1,0:T(8,128)S(1)}, u32[]{:S(2)}, u32[]{:S(2)}) collective-permute-start(f32[2,32,1536]{2,1,0:T(8,128)S(1)} %get-tuple-element.66), channel_id=1, source_target_pairs={{0,1},{1,0},{2,3},{3,2},{4,5},{5,4},{6,7},{7,6},{8,9},{9,8},{10,11... | collective-permute-start | bytes 1179656 | tf_op jit(solution)/shard_map/ppermute | solution.py:377
  14.5 7.5 %collective-permute-start.6 = (f32[32,768]{1,0:T(8,128)S(1)}, f32[32,768]{1,0:T(8,128)S(1)}, u32[]{:S(2)}, u32[]{:S(2)}) collective-permute-start(f32[32,768]{1,0:T(8,128)S(1)} %get-tuple-element.77), channel_id=1, source_target_pairs={{4,0},{5,1},{6,2},{7,3},{8,4},{9,5},{10,6},{11,7},{12,8},{13,9},{1... | collective-permute-start | bytes 294920 | tf_op jit(solution)/shard_map/ppermute | solution.py:423
  15.8 6.2 %collective-permute-start.7 = (f32[32,768]{1,0:T(8,128)S(1)}, f32[32,768]{1,0:T(8,128)S(1)}, u32[]{:S(2)}, u32[]{:S(2)}) collective-permute-start(f32[32,768]{1,0:T(8,128)S(1)} %get-tuple-element.78), channel_id=1, source_target_pairs={{0,2},{1,3},{2,0},{3,1},{4,6},{5,7},{6,4},{7,5},{8,10},{9,11},{10,... | collective-permute-start | bytes 294920 | tf_op jit(solution)/shard_map/ppermute | solution.py:377
  17.6 7.4 %collective-permute-start.8 = (f32[32,768]{1,0:T(8,128)S(1)}, f32[32,768]{1,0:T(8,128)S(1)}, u32[]{:S(2)}, u32[]{:S(2)}) collective-permute-start(f32[32,768]{1,0:T(8,128)S(1)} %get-tuple-element.79), channel_id=1, source_target_pairs={{4,2},{5,3},{6,0},{7,1},{8,6},{9,7},{10,4},{11,5},{12,10},{13,11},... | collective-permute-start | bytes 294920 | tf_op jit(solution)/shard_map/ppermute | solution.py:423
  18.9 3.0 %collective-permute-start.5 = (f32[32,512]{1,0:T(8,128)S(1)}, f32[32,512]{1,0:T(8,128)S(1)}, u32[]{:S(2)}, u32[]{:S(2)}) collective-permute-start(f32[32,512]{1,0:T(8,128)S(1)} %get-tuple-element.73), channel_id=1, source_target_pairs={{0,1},{1,0},{2,3},{3,2},{4,5},{5,4},{6,7},{7,6},{8,9},{9,8},{10,11... | collective-permute-start | bytes 196616 | tf_op jit(solution)/shard_map/ppermute | solution.py:377
  20.1 1.4 %collective-permute-start.4 = (f32[32,384]{1,0:T(8,128)S(1)}, f32[32,384]{1,0:T(8,128)S(1)}, u32[]{:S(2)}, u32[]{:S(2)}) collective-permute-start(f32[32,384]{1,0:T(8,128)S(1)} %get-tuple-element.72), channel_id=1, source_target_pairs={{0,1},{1,0},{2,3},{3,2},{4,5},{5,4},{6,7},{7,6},{8,9},{9,8},{10,11... | collective-permute-start | bytes 147464 | tf_op jit(solution)/shard_map/ppermute | solution.py:377
  21.6 9.9 %collective-permute-start.10 = (f32[384,1536]{1,0:T(8,128)S(1)}, f32[384,1536]{1,0:T(8,128)S(1)}, u32[]{:S(2)}, u32[]{:S(2)}) collective-permute-start(f32[384,1536]{1,0:T(8,128)S(1)} %bitcast.44), channel_id=1, source_target_pairs={{0,1},{1,0},{2,3},{3,2},{4,5},{5,4},{6,7},{7,6},{8,9},{9,8},{10,11... | collective-permute-start | bytes 7077896 | tf_op jit(solution)/shard_map/ppermute | solution.py:377
  25.0 8.6 %collective-permute-start.13 = (f32[384,1536]{1,0:T(8,128)S(1)}, f32[384,1536]{1,0:T(8,128)S(1)}, u32[]{:S(2)}, u32[]{:S(2)}) collective-permute-start(f32[384,1536]{1,0:T(8,128)S(1)} %bitcast.70), channel_id=1, source_target_pairs={{0,1},{1,0},{2,3},{3,2},{4,5},{5,4},{6,7},{7,6},{8,9},{9,8},{10,11... | collective-permute-start | bytes 7077896 | tf_op jit(solution)/shard_map/ppermute | solution.py:377
  25.1 6.4 %collective-permute-start.11 = (f32[32,768]{1,0:T(8,128)S(1)}, f32[32,768]{1,0:T(8,128)S(1)}, u32[]{:S(2)}, u32[]{:S(2)}) collective-permute-start(f32[32,768]{1,0:T(8,128)S(1)} %shard_map.223.refs_4_.refs_5_), channel_id=1, source_target_pairs={{0,4},{1,5},{2,6},{3,7},{4,0},{5,1},{6,2},{7,3},{8,12},{9,13},{10,... | collective-permute-start | bytes 294920 | tf_op jit(solution)/shard_map/ppermute | solution.py:377
  27.8 5.8 %collective-permute-start.9 = (f32[32,768]{1,0:T(8,128)S(1)}, f32[32,768]{1,0:T(8,128)S(1)}, u32[]{:S(2)}, u32[]{:S(2)}) collective-permute-start(f32[32,768]{1,0:T(8,128)S(1)} %shard_map.223.refs_4_.refs_5_), channel_id=1, source_target_pairs={{0,6},{1,7},{2,4},{3,5},{4,2},{5,3},{6,0},{7,1},{8,14},{9,15},{10,... | collective-permute-start | bytes 294920 | tf_op jit(solution)/shard_map/ppermute | solution.py:377
  31.4 2.1 %copy-start.1 = (f32[1,384,1536]{2,1,0:T(8,128)S(1)}, f32[1,384,1536]{2,1,0:T(8,128)}, u32[]{:S(2)}) copy-start(f32[1,384,1536]{2,1,0:T(8,128)} %param.35) | copy-start | bytes 7077892
  33.6 7.4 %collective-permute-start.16 = (f32[384,1536]{1,0:T(8,128)S(1)}, f32[384,1536]{1,0:T(8,128)S(1)}, u32[]{:S(2)}, u32[]{:S(2)}) collective-permute-start(f32[384,1536]{1,0:T(8,128)S(1)} %bitcast.51), channel_id=1, source_target_pairs={{0,1},{1,0},{2,3},{3,2},{4,5},{5,4},{6,7},{7,6},{8,9},{9,8},{10,11... | collective-permute-start | bytes 7077896 | tf_op jit(solution)/shard_map/ppermute | solution.py:377
  33.7 5.7 %collective-permute-start.14 = (f32[32,768]{1,0:T(8,128)S(1)}, f32[32,768]{1,0:T(8,128)S(1)}, u32[]{:S(2)}, u32[]{:S(2)}) collective-permute-start(f32[32,768]{1,0:T(8,128)S(1)} %shard_map.225.refs_5_), channel_id=1, source_target_pairs={{0,2},{1,3},{2,0},{3,1},{4,8},{5,9},{6,10},{7,11},{8,4},{9,5},{10,... | collective-permute-start | bytes 294920 | tf_op jit(solution)/shard_map/ppermute | solution.py:377
  34.9 6.1 %collective-permute-start.12 = (f32[32,768]{1,0:T(8,128)S(1)}, f32[32,768]{1,0:T(8,128)S(1)}, u32[]{:S(2)}, u32[]{:S(2)}) collective-permute-start(f32[32,768]{1,0:T(8,128)S(1)} %shard_map.225.refs_5_), channel_id=1, source_target_pairs={{0,2},{1,3},{2,0},{3,1},{4,10},{5,11},{6,8},{7,9},{8,6},{9,7},{10,... | collective-permute-start | bytes 294920 | tf_op jit(solution)/shard_map/ppermute | solution.py:377
  39.3 1.9 %copy-start.3 = (f32[1,512,1536]{2,1,0:T(8,128)S(1)}, f32[1,512,1536]{2,1,0:T(8,128)}, u32[]{:S(2)}) copy-start(f32[1,512,1536]{2,1,0:T(8,128)} %param.32) | copy-start | bytes 9437188
  41.2 14.5 %collective-permute-start.20 = (f32[512,1536]{1,0:T(8,128)S(1)}, f32[512,1536]{1,0:T(8,128)S(1)}, u32[]{:S(2)}, u32[]{:S(2)}) collective-permute-start(f32[512,1536]{1,0:T(8,128)S(1)} %bitcast.63), channel_id=1, source_target_pairs={{0,1},{1,0},{2,3},{3,2},{4,5},{5,4},{6,7},{7,6},{8,9},{9,8},{10,11... | collective-permute-start | bytes 9437192 | tf_op jit(solution)/shard_map/ppermute | solution.py:377
  41.2 6.8 %collective-permute-start.17 = (f32[32,768]{1,0:T(8,128)S(1)}, f32[32,768]{1,0:T(8,128)S(1)}, u32[]{:S(2)}, u32[]{:S(2)}) collective-permute-start(f32[32,768]{1,0:T(8,128)S(1)} %shard_map.227.refs_5_), channel_id=1, source_target_pairs={{0,4},{1,5},{2,6},{3,7},{4,0},{5,1},{6,2},{7,3},{8,12},{9,13},{10,... | collective-permute-start | bytes 294920 | tf_op jit(solution)/shard_map/ppermute | solution.py:377
  44.4 5.8 %collective-permute-start.15 = (f32[32,768]{1,0:T(8,128)S(1)}, f32[32,768]{1,0:T(8,128)S(1)}, u32[]{:S(2)}, u32[]{:S(2)}) collective-permute-start(f32[32,768]{1,0:T(8,128)S(1)} %shard_map.227.refs_5_), channel_id=1, source_target_pairs={{0,6},{1,7},{2,4},{3,5},{4,2},{5,3},{6,0},{7,1},{8,14},{9,15},{10,... | collective-permute-start | bytes 294920 | tf_op jit(solution)/shard_map/ppermute | solution.py:377
  50.2 4.7 %collective-permute-start.18 = (f32[32,768]{1,0:T(8,128)S(1)}, f32[32,768]{1,0:T(8,128)S(1)}, u32[]{:S(2)}, u32[]{:S(2)}) collective-permute-start(f32[32,768]{1,0:T(8,128)S(1)} %shard_map.229.refs_0_), channel_id=1, source_target_pairs={{0,2},{1,3},{2,0},{3,1},{4,6},{5,7},{6,4},{7,5},{8,10},{9,11},{10,... | collective-permute-start | bytes 294920 | tf_op jit(solution)/shard_map/ppermute | solution.py:377
  52.2 3.5 %copy-start.4 = (f32[1,512,1536]{2,1,0:T(8,128)S(1)}, f32[1,512,1536]{2,1,0:T(8,128)}, u32[]{:S(2)}) copy-start(f32[1,512,1536]{2,1,0:T(8,128)} %param.31) | copy-start | bytes 9437188
  55.7 8.0 %collective-permute-start.23 = (f32[512,1536]{1,0:T(8,128)S(1)}, f32[512,1536]{1,0:T(8,128)S(1)}, u32[]{:S(2)}, u32[]{:S(2)}) collective-permute-start(f32[512,1536]{1,0:T(8,128)S(1)} %bitcast.67), channel_id=1, source_target_pairs={{0,1},{1,0},{2,3},{3,2},{4,5},{5,4},{6,7},{7,6},{8,9},{9,8},{10,11... | collective-permute-start | bytes 9437192 | tf_op jit(solution)/shard_map/ppermute | solution.py:377
  55.8 5.2 %collective-permute-start.21 = (f32[32,768]{1,0:T(8,128)S(1)}, f32[32,768]{1,0:T(8,128)S(1)}, u32[]{:S(2)}, u32[]{:S(2)}) collective-permute-start(f32[32,768]{1,0:T(8,128)S(1)} %shard_map.231.refs_4_.refs_5_), channel_id=1, source_target_pairs={{0,4},{1,5},{2,6},{3,7},{4,0},{5,1},{6,2},{7,3},{8,12},{9,13},{10,... | collective-permute-start | bytes 294920 | tf_op jit(solution)/shard_map/ppermute | solution.py:377
  57.5 6.3 %collective-permute-start.19 = (f32[32,768]{1,0:T(8,128)S(1)}, f32[32,768]{1,0:T(8,128)S(1)}, u32[]{:S(2)}, u32[]{:S(2)}) collective-permute-start(f32[32,768]{1,0:T(8,128)S(1)} %shard_map.231.refs_4_.refs_5_), channel_id=1, source_target_pairs={{0,6},{1,7},{2,4},{3,5},{4,2},{5,3},{6,0},{7,1},{8,14},{9,15},{10,... | collective-permute-start | bytes 294920 | tf_op jit(solution)/shard_map/ppermute | solution.py:377
  61.0 2.8 %copy-start.2 = (f32[1,512,2048]{2,1,0:T(8,128)S(1)}, f32[1,512,2048]{2,1,0:T(8,128)}, u32[]{:S(2)}) copy-start(f32[1,512,2048]{2,1,0:T(8,128)} %param.30) | copy-start | bytes 12582916
  63.8 25.5 %collective-permute-start.28 = (f32[512,2048]{1,0:T(8,128)S(1)}, f32[512,2048]{1,0:T(8,128)S(1)}, u32[]{:S(2)}, u32[]{:S(2)}) collective-permute-start(f32[512,2048]{1,0:T(8,128)S(1)} %bitcast.59), channel_id=1, source_target_pairs={{0,1},{1,0},{2,3},{3,2},{4,5},{5,4},{6,7},{7,6},{8,9},{9,8},{10,11... | collective-permute-start | bytes 12582920 | tf_op jit(solution)/shard_map/ppermute | solution.py:377
  63.8 5.7 %collective-permute-start.24 = (f32[32,768]{1,0:T(8,128)S(1)}, f32[32,768]{1,0:T(8,128)S(1)}, u32[]{:S(2)}, u32[]{:S(2)}) collective-permute-start(f32[32,768]{1,0:T(8,128)S(1)} %shard_map.233.refs_5_), channel_id=1, source_target_pairs={{0,2},{1,3},{2,0},{3,1},{4,8},{5,9},{6,10},{7,11},{8,4},{9,5},{10,... | collective-permute-start | bytes 294920 | tf_op jit(solution)/shard_map/ppermute | solution.py:377
  64.8 6.3 %collective-permute-start.22 = (f32[32,768]{1,0:T(8,128)S(1)}, f32[32,768]{1,0:T(8,128)S(1)}, u32[]{:S(2)}, u32[]{:S(2)}) collective-permute-start(f32[32,768]{1,0:T(8,128)S(1)} %shard_map.233.refs_5_), channel_id=1, source_target_pairs={{0,2},{1,3},{2,0},{3,1},{4,10},{5,11},{6,8},{7,9},{8,6},{9,7},{10,... | collective-permute-start | bytes 294920 | tf_op jit(solution)/shard_map/ppermute | solution.py:377
  71.2 6.6 %collective-permute-start.26 = (f32[32,768]{1,0:T(8,128)S(1)}, f32[32,768]{1,0:T(8,128)S(1)}, u32[]{:S(2)}, u32[]{:S(2)}) collective-permute-start(f32[32,768]{1,0:T(8,128)S(1)} %shard_map.235.refs_5_), channel_id=1, source_target_pairs={{0,4},{1,5},{2,6},{3,7},{4,0},{5,1},{6,2},{7,3},{8,12},{9,13},{10,... | collective-permute-start | bytes 294920 | tf_op jit(solution)/shard_map/ppermute | solution.py:377
  74.9 5.8 %collective-permute-start.25 = (f32[32,768]{1,0:T(8,128)S(1)}, f32[32,768]{1,0:T(8,128)S(1)}, u32[]{:S(2)}, u32[]{:S(2)}) collective-permute-start(f32[32,768]{1,0:T(8,128)S(1)} %shard_map.235.refs_5_), channel_id=1, source_target_pairs={{0,6},{1,7},{2,4},{3,5},{4,2},{5,3},{6,0},{7,1},{8,14},{9,15},{10,... | collective-permute-start | bytes 294920 | tf_op jit(solution)/shard_map/ppermute | solution.py:377
  77.8 6.0 %collective-permute-start.29 = (f32[32,768]{1,0:T(8,128)S(1)}, f32[32,768]{1,0:T(8,128)S(1)}, u32[]{:S(2)}, u32[]{:S(2)}) collective-permute-start(f32[32,768]{1,0:T(8,128)S(1)} %shard_map.235.refs_5_), channel_id=1, source_target_pairs={{0,2},{1,3},{2,0},{3,1},{4,8},{5,9},{6,10},{7,11},{8,4},{9,5},{10,... | collective-permute-start | bytes 294920 | tf_op jit(solution)/shard_map/ppermute | solution.py:377
  78.9 7.5 %collective-permute-start.30 = (f32[32,768]{1,0:T(8,128)S(1)}, f32[32,768]{1,0:T(8,128)S(1)}, u32[]{:S(2)}, u32[]{:S(2)}) collective-permute-start(f32[32,768]{1,0:T(8,128)S(1)} %shard_map.235.refs_5_), channel_id=1, source_target_pairs={{0,2},{1,3},{2,0},{3,1},{4,10},{5,11},{6,8},{7,9},{8,6},{9,7},{10,... | collective-permute-start | bytes 294920 | tf_op jit(solution)/shard_map/ppermute | solution.py:377
  81.6 5.8 %collective-permute-start.32 = (f32[32,768]{1,0:T(8,128)S(1)}, f32[32,768]{1,0:T(8,128)S(1)}, u32[]{:S(2)}, u32[]{:S(2)}) collective-permute-start(f32[32,768]{1,0:T(8,128)S(1)} %shard_map.237.refs_0_), channel_id=1, source_target_pairs={{0,2},{1,3},{2,0},{3,1},{4,6},{5,7},{6,4},{7,5},{8,10},{9,11},{10,... | collective-permute-start | bytes 294920 | tf_op jit(solution)/shard_map/ppermute | solution.py:377
  82.8 5.7 %collective-permute-start.31 = (f32[32,768]{1,0:T(8,128)S(1)}, f32[32,768]{1,0:T(8,128)S(1)}, u32[]{:S(2)}, u32[]{:S(2)}) collective-permute-start(f32[32,768]{1,0:T(8,128)S(1)} %shard_map.237.refs_0_), channel_id=1, source_target_pairs={{0,4},{1,5},{2,6},{3,7},{4,0},{5,1},{6,2},{7,3},{8,12},{9,13},{10,... | collective-permute-start | bytes 294920 | tf_op jit(solution)/shard_map/ppermute | solution.py:377
  83.8 5.5 %collective-permute-start.27 = (f32[32,768]{1,0:T(8,128)S(1)}, f32[32,768]{1,0:T(8,128)S(1)}, u32[]{:S(2)}, u32[]{:S(2)}) collective-permute-start(f32[32,768]{1,0:T(8,128)S(1)} %shard_map.237.refs_0_), channel_id=1, source_target_pairs={{0,6},{1,7},{2,4},{3,5},{4,2},{5,3},{6,0},{7,1},{8,14},{9,15},{10,... | collective-permute-start | bytes 294920 | tf_op jit(solution)/shard_map/ppermute | solution.py:377
  89.3 2.6 %copy-start.9 = (f32[1,384,64]{1,2,0:T(8,128)S(1)}, f32[1,384,64]{1,2,0:T(8,128)}, u32[]{:S(2)}) copy-start(f32[1,384,64]{1,2,0:T(8,128)} %param.27) | copy-start | bytes 294916
  89.3 2.6 %copy-start.10 = (f32[1,384,64]{1,2,0:T(8,128)S(1)}, f32[1,384,64]{1,2,0:T(8,128)}, u32[]{:S(2)}) copy-start(f32[1,384,64]{1,2,0:T(8,128)} %param.28) | copy-start | bytes 294916
  89.3 2.6 %copy-start.11 = (f32[1,384,64]{1,2,0:T(8,128)S(1)}, f32[1,384,64]{1,2,0:T(8,128)}, u32[]{:S(2)}) copy-start(f32[1,384,64]{1,2,0:T(8,128)} %param.29) | copy-start | bytes 294916
  89.4 5.0 %collective-permute-start.33 = (f32[32,1024]{1,0:T(8,128)S(1)}, f32[32,1024]{1,0:T(8,128)S(1)}, u32[]{:S(2)}, u32[]{:S(2)}) collective-permute-start(f32[32,1024]{1,0:T(8,128)S(1)} %shard_map.241.refs_0_), channel_id=1, source_target_pairs={{0,2},{1,3},{2,0},{3,1},{4,6},{5,7},{6,4},{7,5},{8,10},{9,11},{10,... | collective-permute-start | bytes 393224 | tf_op jit(solution)/shard_map/ppermute | solution.py:377
  90.6 1.3 %collective-permute-start.34 = (f32[32,384]{1,0:T(8,128)S(1)}, f32[32,384]{1,0:T(8,128)S(1)}, u32[]{:S(2)}, u32[]{:S(2)}) collective-permute-start(f32[32,384]{1,0:T(8,128)S(1)} %get-tuple-element.100), channel_id=1, source_target_pairs={{0,1},{1,0},{2,3},{3,2},{4,5},{5,4},{6,7},{7,6},{8,9},{9,8},{10,11... | collective-permute-start | bytes 147464 | tf_op jit(solution)/shard_map/ppermute | solution.py:377
  94.4 2.7 %copy-start.6 = (f32[1,512,64]{1,2,0:T(8,128)S(1)}, f32[1,512,64]{1,2,0:T(8,128)}, u32[]{:S(2)}) copy-start(f32[1,512,64]{1,2,0:T(8,128)} %param.24) | copy-start | bytes 393220
  94.4 2.7 %copy-start.7 = (f32[1,512,64]{1,2,0:T(8,128)S(1)}, f32[1,512,64]{1,2,0:T(8,128)}, u32[]{:S(2)}) copy-start(f32[1,512,64]{1,2,0:T(8,128)} %param.25) | copy-start | bytes 393220
  94.4 2.7 %copy-start.8 = (f32[1,512,64]{1,2,0:T(8,128)S(1)}, f32[1,512,64]{1,2,0:T(8,128)}, u32[]{:S(2)}) copy-start(f32[1,512,64]{1,2,0:T(8,128)} %param.26) | copy-start | bytes 393220
  95.7 1.3 %collective-permute-start.35 = (f32[32,512]{1,0:T(8,128)S(1)}, f32[32,512]{1,0:T(8,128)S(1)}, u32[]{:S(2)}, u32[]{:S(2)}) collective-permute-start(f32[32,512]{1,0:T(8,128)S(1)} %get-tuple-element.107), channel_id=1, source_target_pairs={{0,1},{1,0},{2,3},{3,2},{4,5},{5,4},{6,7},{7,6},{8,9},{9,8},{10,11... | collective-permute-start | bytes 196616 | tf_op jit(solution)/shard_map/ppermute | solution.py:377

commit v12 on v11

--- a/solution.py
+++ b/solution.py
@@ -313,6 +313,17 @@
 def end_kernel(columns, piece, rows, sofar, out):
     value = piece[0][...]
     store_rows(out, plus(times_rows(value, *rows, columns=columns(value.shape[1])), sofar))
+
+
+def first_kernel(columns, piece, rows, early, out):
+    @pl.when(lax.axis_index("story") == 0)
+    def _():
+        value = piece[0][...]
+        out[...] = times_rows(value, *rows, columns=columns(value.shape[1]))
+
+    @pl.when(lax.axis_index("story") > 0)
+    def _():
+        out[...] = early[0][...]
 
 
 def coupled_kernel(columns, final, load, pair, rows, sofar, out):
@@ -538,7 +549,12 @@
             inverse_other = others(interior_inverse[0], [below_other, face])
             came[-1], below_other = lax.optimization_barrier([came[-1], below_other])
         if k == 0:
-            late, came[0] = lax.optimization_barrier([face, came[0]])
+            early = []
+            if face.shape[1] % 128 == 0:
+                kernel = functools.partial(part_kernel, from_chip(mv.chips, 0), None)
+                rows = [couple_above[0], above_other]
+                early = call(kernel, shape_int, [face], rows, [], cost=4 << 20)
+            late, came[0], *early = lax.optimization_barrier([face, came[0], *early])
             odd = mv.gather_story(late, 1)
         (face,) = call(
             functools.partial(step_kernel, from_chip(len(came), len(came) - 1), k),
@@ -555,6 +571,8 @@
     sofar = []
     for j, piece in enumerate(here):
         kernel = functools.partial(part_kernel, from_chip(len(here), j), None)
+        if j == 0 and early:
+            kernel, sofar = functools.partial(first_kernel, from_chip(len(here), j)), early
         sofar = call(kernel, shape_int, [piece], rows, sofar, cost=4 << 20)
     rows = [couple_below[0], below_other]
     for j, pair in enumerate(zip(even, odd)):

time: 98.4 us -> 98.3 us (level)
  waiting for transfers between devices: 43.5 us -> 42.4 us
    ppermute x34, waiting for transfers between devices: 40.4 us -> 39.4 us  [permute(): return lax.ppermute(value, AXES, pairs)]
    pallas_call x27 -> x28, Pallas kernels: 12.7 us -> 13.7 us  [call(): pl.pallas_call(body, in_specs=[VMEM] * len(flat) + [pl.BlockSpec(memory_s...]
  transfers between devices with their start and end apart: 36 -> 36, of which waited for: 22 -> 22; matrix products, arithmetic and copies ran while one was open for 0% -> 0% of each run, Pallas kernels for 12% -> 13%
where the time goes in v12:
time: 98.3 us; the launch traced here: 98 us
  waiting for transfers between devices  42.4 us (43%)
  starting transfers between devices  35 us (36%)
  Pallas kernels  19.3 us (20%)
    ppermute x34, waiting for transfers between devices, permute(): return lax.ppermute(value, AXES, pairs)  39.4 us
    ppermute x34, starting transfers between devices, permute(): return lax.ppermute(value, AXES, pairs)  32.5 us
    pallas_call x28, Pallas kernels, call(): pl.pallas_call(body, in_specs=[VMEM] * len(flat) + [pl.BlockSpec(memory_s...  13.7 us
    pallas_call x1, Pallas kernels, staged(): pl.pallas_call(body, in_specs=[pl.BlockSpec(memory_space=pltpu.HBM)] * co...  3.16 us
    ppermute x2, waiting for transfers between devices, shift(): return lax.ppermute(value, AXES, pairs)  3.04 us
    ppermute x2, starting transfers between devices, shift(): return lax.ppermute(value, AXES, pairs)  2.57 us
    pallas_call x2, Pallas kernels, fetched(): pl.pallas_call(body, in_specs=[pl.BlockSpec(memory_space=pltpu.HBM)] * co...  2.48 us
  transfers between devices with their start and end apart: 36, of which 22 were waited for; matrix products, arithmetic and copies ran while one was open for 0% of the time, Pallas kernels for 13%

profile of v12, /device:TPU:0, one launch (start us, length us, event | category | flops | bytes accessed | tf_op | source)
XLA Modules:
  0.0 98.0 jit_solution(11471580985646455017)
XLA Ops:
  0.6 1.3 %shard_map.217 = (f32[64,512]{1,0:T(8,128)S(1)}, f32[64,128]{1,0:T(8,128)S(1)}) custom-call(s32[1,64]{1,0:T(1,128)} %bitcast.87, f32[1,512]{1,0:T(1,128)} %bitcast.86, f32[1,512]{1,0:T(1,128)} %refs_2_.1, f32[1,512]{1,0:T(1,128)} %refs_3_.1, f32[64,512]{1,0:T(8,128)} %bitcast.74, f32[64,512]{1,0:T(8,128)} %bitcast.76, f32[64,512]{1,0:T(8,128)} %bitcast.78), custom_call_target="tpu_custom_call" | custom-call | tf_op jit(solution)/shard_map/pallas_call | solution.py:189
  2.0 3.0 %collective-permute-start.1 = (f32[64,512]{1,0:T(8,128)S(1)}, f32[64,512]{1,0:T(8,128)S(1)}, u32[]{:S(2)}, u32[]{:S(2)}) collective-permute-start(f32[64,512]{1,0:T(8,128)S(1)} %get-tuple-element.69.refs_0_), channel_id=1, source_target_pairs={{0,2},{1,3},{2,0},{3,1},{4,6},{5,7},{6,4},{7,5},{8,10},{9,11},{10,... | collective-permute-start | bytes 393224 | tf_op jit(solution)/shard_map/ppermute | solution.py:388
  5.0 3.2 %shard_map.218.refs_4_ = f32[512,3584]{1,0:T(8,128)S(1)} custom-call(f32[512,2048]{1,0:T(8,128)} %bitcast.63, f32[512,1536]{1,0:T(8,128)} %bitcast.58), custom_call_target="tpu_custom_call" | custom-call | tf_op jit(solution)/shard_map/pallas_call | solution.py:136
  8.7 1.1 %collective-permute-done.2.refs_3_ = f32[64,512]{1,0:T(8,128)S(1)} collective-permute-done((f32[64,512]{1,0:T(8,128)S(1)}, f32[64,512]{1,0:T(8,128)S(1)}, u32[]{:S(2)}, u32[]{:S(2)}) %collective-permute-start.2) | collective-permute-done | bytes 131104 | tf_op jit(solution)/shard_map/ppermute | solution.py:388
  9.8 2.8 %shard_map.219 = (f32[2,32,1536]{2,1,0:T(8,128)S(1)}, f32[2,32,1536]{2,1,0:T(8,128)S(1)}) custom-call(f32[64,512]{1,0:T(8,128)S(1)} %get-tuple-element.69.refs_0_, f32[64,512]{1,0:T(8,128)S(1)} %collective-permute-done.refs_1_, f32[64,512]{1,0:T(8,128)S(1)} %collective-permute-done.1.refs_2_, f32[64,512]{1,0:T(8,128)S(1)} %collective-permute-done.2.refs_3_, ...), custom_call_target="tpu_custom_call" | custom-call | tf_op jit(solution)/shard_map/pallas_call | solution.py:98
  12.9 1.5 %collective-permute-done.3.refs_1_ = f32[2,32,1536]{2,1,0:T(8,128)S(1)} collective-permute-done((f32[2,32,1536]{2,1,0:T(8,128)S(1)}, f32[2,32,1536]{2,1,0:T(8,128)S(1)}, u32[]{:S(2)}, u32[]{:S(2)}) %collective-permute-start.3) | collective-permute-done | bytes 393248 | tf_op jit(solution)/shard_map/ppermute | solution.py:388
  14.5 1.3 %collective-permute-start.6 = (f32[32,768]{1,0:T(8,128)S(1)}, f32[32,768]{1,0:T(8,128)S(1)}, u32[]{:S(2)}, u32[]{:S(2)}) collective-permute-start(f32[32,768]{1,0:T(8,128)S(1)} %get-tuple-element.78), channel_id=1, source_target_pairs={{4,0},{5,1},{6,2},{7,3},{8,4},{9,5},{10,6},{11,7},{12,8},{13,9},{1... | collective-permute-start | bytes 294920 | tf_op jit(solution)/shard_map/ppermute | solution.py:434
  15.8 1.8 %collective-permute-start.7 = (f32[32,768]{1,0:T(8,128)S(1)}, f32[32,768]{1,0:T(8,128)S(1)}, u32[]{:S(2)}, u32[]{:S(2)}) collective-permute-start(f32[32,768]{1,0:T(8,128)S(1)} %get-tuple-element.79), channel_id=1, source_target_pairs={{0,2},{1,3},{2,0},{3,1},{4,6},{5,7},{6,4},{7,5},{8,10},{9,11},{10,... | collective-permute-start | bytes 294920 | tf_op jit(solution)/shard_map/ppermute | solution.py:388
  17.6 1.3 %collective-permute-start.8 = (f32[32,768]{1,0:T(8,128)S(1)}, f32[32,768]{1,0:T(8,128)S(1)}, u32[]{:S(2)}, u32[]{:S(2)}) collective-permute-start(f32[32,768]{1,0:T(8,128)S(1)} %get-tuple-element.80), channel_id=1, source_target_pairs={{4,2},{5,3},{6,0},{7,1},{8,6},{9,7},{10,4},{11,5},{12,10},{13,11},... | collective-permute-start | bytes 294920 | tf_op jit(solution)/shard_map/ppermute | solution.py:434
  19.0 1.2 %shard_map.222 = (f32[32,384]{1,0:T(8,128)S(1)}, f32[32,384]{1,0:T(8,128)S(1)}) custom-call(f32[1,384]{1,0:T(1,128)} %refs_0_.1, f32[1,384]{1,0:T(1,128)} %refs_1_.1, f32[64,384]{1,0:T(8,128)} %bitcast.80, f32[64,384]{1,0:T(8,128)} %bitcast.82, f32[64,384]{1,0:T(8,128)} %bitcast.84, f32[64,128]{1,0:T(8,128)S(1)} %get-tuple-element.72.refs_5_), custom_call_target="tpu_custom_call" | custom-call | tf_op jit(solution)/shard_map/pallas_call | solution.py:189
  20.7 0.9 collective-permute-done.4.refs_1_
  21.9 3.0 %collective-permute-done.8.refs_5_ = f32[32,768]{1,0:T(8,128)S(1)} collective-permute-done((f32[32,768]{1,0:T(8,128)S(1)}, f32[32,768]{1,0:T(8,128)S(1)}, u32[]{:S(2)}, u32[]{:S(2)}) %collective-permute-start.8) | collective-permute-done | bytes 98336 | tf_op jit(solution)/shard_map/ppermute | solution.py:434
  25.1 2.7 %collective-permute-start.11 = (f32[32,768]{1,0:T(8,128)S(1)}, f32[32,768]{1,0:T(8,128)S(1)}, u32[]{:S(2)}, u32[]{:S(2)}) collective-permute-start(f32[32,768]{1,0:T(8,128)S(1)} %shard_map.223.refs_4_.refs_5_), channel_id=1, source_target_pairs={{0,4},{1,5},{2,6},{3,7},{4,0},{5,1},{6,2},{7,3},{8,12},{9,13},{10,... | collective-permute-start | bytes 294920 | tf_op jit(solution)/shard_map/ppermute | solution.py:388
  27.8 3.6 %collective-permute-done.11.refs_0_ = f32[32,768]{1,0:T(8,128)S(1)} collective-permute-done((f32[32,768]{1,0:T(8,128)S(1)}, f32[32,768]{1,0:T(8,128)S(1)}, u32[]{:S(2)}, u32[]{:S(2)}) %collective-permute-start.11) | collective-permute-done | bytes 98336 | tf_op jit(solution)/shard_map/ppermute | solution.py:388
  31.4 2.1 %collective-permute-done.9.refs_0_ = f32[32,768]{1,0:T(8,128)S(1)} collective-permute-done((f32[32,768]{1,0:T(8,128)S(1)}, f32[32,768]{1,0:T(8,128)S(1)}, u32[]{:S(2)}, u32[]{:S(2)}) %collective-permute-start.9) | collective-permute-done | bytes 98336 | tf_op jit(solution)/shard_map/ppermute | solution.py:388
  33.7 1.3 %collective-permute-start.14 = (f32[32,768]{1,0:T(8,128)S(1)}, f32[32,768]{1,0:T(8,128)S(1)}, u32[]{:S(2)}, u32[]{:S(2)}) collective-permute-start(f32[32,768]{1,0:T(8,128)S(1)} %shard_map.225.refs_5_), channel_id=1, source_target_pairs={{0,2},{1,3},{2,0},{3,1},{4,8},{5,9},{6,10},{7,11},{8,4},{9,5},{10,... | collective-permute-start | bytes 294920 | tf_op jit(solution)/shard_map/ppermute | solution.py:388
  35.8 3.6 %collective-permute-done.14.refs_0_ = f32[32,768]{1,0:T(8,128)S(1)} collective-permute-done((f32[32,768]{1,0:T(8,128)S(1)}, f32[32,768]{1,0:T(8,128)S(1)}, u32[]{:S(2)}, u32[]{:S(2)}) %collective-permute-start.14) | collective-permute-done | bytes 98336 | tf_op jit(solution)/shard_map/ppermute | solution.py:388
  39.3 1.7 %collective-permute-done.12.refs_0_ = f32[32,768]{1,0:T(8,128)S(1)} collective-permute-done((f32[32,768]{1,0:T(8,128)S(1)}, f32[32,768]{1,0:T(8,128)S(1)}, u32[]{:S(2)}, u32[]{:S(2)}) %collective-permute-start.12) | collective-permute-done | bytes 98336 | tf_op jit(solution)/shard_map/ppermute | solution.py:388
  41.2 3.2 %collective-permute-start.17 = (f32[32,768]{1,0:T(8,128)S(1)}, f32[32,768]{1,0:T(8,128)S(1)}, u32[]{:S(2)}, u32[]{:S(2)}) collective-permute-start(f32[32,768]{1,0:T(8,128)S(1)} %shard_map.227.refs_5_), channel_id=1, source_target_pairs={{0,4},{1,5},{2,6},{3,7},{4,0},{5,1},{6,2},{7,3},{8,12},{9,13},{10,... | collective-permute-start | bytes 294920 | tf_op jit(solution)/shard_map/ppermute | solution.py:388
  44.5 3.6 %collective-permute-done.17.refs_0_ = f32[32,768]{1,0:T(8,128)S(1)} collective-permute-done((f32[32,768]{1,0:T(8,128)S(1)}, f32[32,768]{1,0:T(8,128)S(1)}, u32[]{:S(2)}, u32[]{:S(2)}) %collective-permute-start.17) | collective-permute-done | bytes 98336 | tf_op jit(solution)/shard_map/ppermute | solution.py:388
  48.0 2.1 %collective-permute-done.15.refs_0_ = f32[32,768]{1,0:T(8,128)S(1)} collective-permute-done((f32[32,768]{1,0:T(8,128)S(1)}, f32[32,768]{1,0:T(8,128)S(1)}, u32[]{:S(2)}, u32[]{:S(2)}) %collective-permute-start.15) | collective-permute-done | bytes 98336 | tf_op jit(solution)/shard_map/ppermute | solution.py:388
  50.2 1.3 %collective-permute-start.18 = (f32[32,768]{1,0:T(8,128)S(1)}, f32[32,768]{1,0:T(8,128)S(1)}, u32[]{:S(2)}, u32[]{:S(2)}) collective-permute-start(f32[32,768]{1,0:T(8,128)S(1)} %shard_map.229.refs_0_), channel_id=1, source_target_pairs={{0,2},{1,3},{2,0},{3,1},{4,6},{5,7},{6,4},{7,5},{8,10},{9,11},{10,... | collective-permute-start | bytes 294920 | tf_op jit(solution)/shard_map/ppermute | solution.py:388
  52.3 2.6 %collective-permute-done.18.refs_0_ = f32[32,768]{1,0:T(8,128)S(1)} collective-permute-done((f32[32,768]{1,0:T(8,128)S(1)}, f32[32,768]{1,0:T(8,128)S(1)}, u32[]{:S(2)}, u32[]{:S(2)}) %collective-permute-start.18) | collective-permute-done | bytes 98336 | tf_op jit(solution)/shard_map/ppermute | solution.py:388
  55.8 1.7 %collective-permute-start.21 = (f32[32,768]{1,0:T(8,128)S(1)}, f32[32,768]{1,0:T(8,128)S(1)}, u32[]{:S(2)}, u32[]{:S(2)}) collective-permute-start(f32[32,768]{1,0:T(8,128)S(1)} %shard_map.231.refs_4_.refs_5_), channel_id=1, source_target_pairs={{0,4},{1,5},{2,6},{3,7},{4,0},{5,1},{6,2},{7,3},{8,12},{9,13},{10,... | collective-permute-start | bytes 294920 | tf_op jit(solution)/shard_map/ppermute | solution.py:388
  57.5 1.0 %collective-permute-start.19 = (f32[32,768]{1,0:T(8,128)S(1)}, f32[32,768]{1,0:T(8,128)S(1)}, u32[]{:S(2)}, u32[]{:S(2)}) collective-permute-start(f32[32,768]{1,0:T(8,128)S(1)} %shard_map.231.refs_4_.refs_5_), channel_id=1, source_target_pairs={{0,6},{1,7},{2,4},{3,5},{4,2},{5,3},{6,0},{7,1},{8,14},{9,15},{10,... | collective-permute-start | bytes 294920 | tf_op jit(solution)/shard_map/ppermute | solution.py:388
  58.5 2.5 %collective-permute-done.21.refs_0_ = f32[32,768]{1,0:T(8,128)S(1)} collective-permute-done((f32[32,768]{1,0:T(8,128)S(1)}, f32[32,768]{1,0:T(8,128)S(1)}, u32[]{:S(2)}, u32[]{:S(2)}) %collective-permute-start.21) | collective-permute-done | bytes 98336 | tf_op jit(solution)/shard_map/ppermute | solution.py:388
  61.0 2.7 %collective-permute-done.19.refs_0_ = f32[32,768]{1,0:T(8,128)S(1)} collective-permute-done((f32[32,768]{1,0:T(8,128)S(1)}, f32[32,768]{1,0:T(8,128)S(1)}, u32[]{:S(2)}, u32[]{:S(2)}) %collective-permute-start.19) | collective-permute-done | bytes 98336 | tf_op jit(solution)/shard_map/ppermute | solution.py:388
  63.8 1.0 %collective-permute-start.24 = (f32[32,768]{1,0:T(8,128)S(1)}, f32[32,768]{1,0:T(8,128)S(1)}, u32[]{:S(2)}, u32[]{:S(2)}) collective-permute-start(f32[32,768]{1,0:T(8,128)S(1)} %shard_map.233.refs_5_), channel_id=1, source_target_pairs={{0,2},{1,3},{2,0},{3,1},{4,8},{5,9},{6,10},{7,11},{8,4},{9,5},{10,... | collective-permute-start | bytes 294920 | tf_op jit(solution)/shard_map/ppermute | solution.py:388
  64.8 1.1 %collective-permute-start.22 = (f32[32,768]{1,0:T(8,128)S(1)}, f32[32,768]{1,0:T(8,128)S(1)}, u32[]{:S(2)}, u32[]{:S(2)}) collective-permute-start(f32[32,768]{1,0:T(8,128)S(1)} %shard_map.233.refs_5_), channel_id=1, source_target_pairs={{0,2},{1,3},{2,0},{3,1},{4,10},{5,11},{6,8},{7,9},{8,6},{9,7},{10,... | collective-permute-start | bytes 294920 | tf_op jit(solution)/shard_map/ppermute | solution.py:388
  65.9 3.6 %collective-permute-done.24.refs_0_ = f32[32,768]{1,0:T(8,128)S(1)} collective-permute-done((f32[32,768]{1,0:T(8,128)S(1)}, f32[32,768]{1,0:T(8,128)S(1)}, u32[]{:S(2)}, u32[]{:S(2)}) %collective-permute-start.24) | collective-permute-done | bytes 98336 | tf_op jit(solution)/shard_map/ppermute | solution.py:388
  69.5 1.7 %collective-permute-done.22.refs_0_ = f32[32,768]{1,0:T(8,128)S(1)} collective-permute-done((f32[32,768]{1,0:T(8,128)S(1)}, f32[32,768]{1,0:T(8,128)S(1)}, u32[]{:S(2)}, u32[]{:S(2)}) %collective-permute-start.22) | collective-permute-done | bytes 98336 | tf_op jit(solution)/shard_map/ppermute | solution.py:388
  71.2 3.9 %collective-permute-start.26 = (f32[32,768]{1,0:T(8,128)S(1)}, f32[32,768]{1,0:T(8,128)S(1)}, u32[]{:S(2)}, u32[]{:S(2)}) collective-permute-start(f32[32,768]{1,0:T(8,128)S(1)} %shard_map.235.refs_0_.refs_5_), channel_id=1, source_target_pairs={{0,4},{1,5},{2,6},{3,7},{4,0},{5,1},{6,2},{7,3},{8,12},{9,13},{10,... | collective-permute-start | bytes 294920 | tf_op jit(solution)/shard_map/ppermute | solution.py:388
  75.7 1.0 %shard_map.236.refs_3_ = f32[32,1024]{1,0:T(8,128)S(1)} custom-call(f32[32,768]{1,0:T(8,128)S(1)} %shard_map.235.refs_0_.refs_5_, f32[512,1536]{1,0:T(8,128)S(1)} %bitcast.60, f32[512,1536]{1,0:T(8,128)S(1)} %collective-permute-done.20.refs_2_), custom_call_target="tpu_custom_call" | custom-call | bytes 4194304 | tf_op jit(solution)/shard_map/pallas_call | solution.py:98
  76.7 1.3 %collective-permute-done.26.refs_0_ = f32[32,768]{1,0:T(8,128)S(1)} collective-permute-done((f32[32,768]{1,0:T(8,128)S(1)}, f32[32,768]{1,0:T(8,128)S(1)}, u32[]{:S(2)}, u32[]{:S(2)}) %collective-permute-start.26) | collective-permute-done | bytes 98336 | tf_op jit(solution)/shard_map/ppermute | solution.py:388
  78.0 1.2 %collective-permute-start.29 = (f32[32,768]{1,0:T(8,128)S(1)}, f32[32,768]{1,0:T(8,128)S(1)}, u32[]{:S(2)}, u32[]{:S(2)}) collective-permute-start(f32[32,768]{1,0:T(8,128)S(1)} %shard_map.235.refs_0_.refs_5_), channel_id=1, source_target_pairs={{0,2},{1,3},{2,0},{3,1},{4,8},{5,9},{6,10},{7,11},{8,4},{9,5},{10,... | collective-permute-start | bytes 294920 | tf_op jit(solution)/shard_map/ppermute | solution.py:388
  79.1 0.9 collective-permute-start.30
  80.8 0.9 shard_map.238.refs_0_
  81.7 1.2 %collective-permute-start.32 = (f32[32,768]{1,0:T(8,128)S(1)}, f32[32,768]{1,0:T(8,128)S(1)}, u32[]{:S(2)}, u32[]{:S(2)}) collective-permute-start(f32[32,768]{1,0:T(8,128)S(1)} %shard_map.238.refs_0_), channel_id=1, source_target_pairs={{0,2},{1,3},{2,0},{3,1},{4,6},{5,7},{6,4},{7,5},{8,10},{9,11},{10,... | collective-permute-start | bytes 294920 | tf_op jit(solution)/shard_map/ppermute | solution.py:388
  82.9 1.0 %collective-permute-start.31 = (f32[32,768]{1,0:T(8,128)S(1)}, f32[32,768]{1,0:T(8,128)S(1)}, u32[]{:S(2)}, u32[]{:S(2)}) collective-permute-start(f32[32,768]{1,0:T(8,128)S(1)} %shard_map.238.refs_0_), channel_id=1, source_target_pairs={{0,4},{1,5},{2,6},{3,7},{4,0},{5,1},{6,2},{7,3},{8,12},{9,13},{10,... | collective-permute-start | bytes 294920 | tf_op jit(solution)/shard_map/ppermute | solution.py:388
  83.9 1.6 %collective-permute-start.27 = (f32[32,768]{1,0:T(8,128)S(1)}, f32[32,768]{1,0:T(8,128)S(1)}, u32[]{:S(2)}, u32[]{:S(2)}) collective-permute-start(f32[32,768]{1,0:T(8,128)S(1)} %shard_map.238.refs_0_), channel_id=1, source_target_pairs={{0,6},{1,7},{2,4},{3,5},{4,2},{5,3},{6,0},{7,1},{8,14},{9,15},{10,... | collective-permute-start | bytes 294920 | tf_op jit(solution)/shard_map/ppermute | solution.py:388
  85.6 1.0 %collective-permute-done.30.refs_3_ = f32[32,768]{1,0:T(8,128)S(1)} collective-permute-done((f32[32,768]{1,0:T(8,128)S(1)}, f32[32,768]{1,0:T(8,128)S(1)}, u32[]{:S(2)}, u32[]{:S(2)}) %collective-permute-start.30) | collective-permute-done | bytes 98336 | tf_op jit(solution)/shard_map/ppermute | solution.py:388
  86.6 1.0 %shard_map.239.refs_3_ = f32[32,1024]{1,0:T(8,128)S(1)} custom-call(f32[32,768]{1,0:T(8,128)S(1)} %shard_map.238.refs_0_, f32[512,1536]{1,0:T(8,128)S(1)} %bitcast.61, f32[512,1536]{1,0:T(8,128)S(1)} %collective-permute-done.20.refs_2_, f32[32,1024]{1,0:T(8,128)S(1)} %shard_map.236.refs_3_), custom_call_target="tpu_custom_call" | custom-call | bytes 4194304 | tf_op jit(solution)/shard_map/pallas_call | solution.py:98
  87.7 1.1 %shard_map.240.refs_4_ = f32[32,1024]{1,0:T(8,128)S(1)} custom-call(f32[32,768]{1,0:T(8,128)S(1)} %collective-permute-done.32.refs_0_, f32[512,1536]{1,0:T(8,128)S(1)} %bitcast.62, f32[512,1536]{1,0:T(8,128)S(1)} %collective-permute-done.20.refs_2_, f32[32,1024]{1,0:T(8,128)S(1)} %shard_map.239.refs_3_), custom_call_target="tpu_custom_call" | custom-call | bytes 4194304 | tf_op jit(solution)/shard_map/pallas_call | solution.py:98
  89.5 1.2 %collective-permute-start.33 = (f32[32,1024]{1,0:T(8,128)S(1)}, f32[32,1024]{1,0:T(8,128)S(1)}, u32[]{:S(2)}, u32[]{:S(2)}) collective-permute-start(f32[32,1024]{1,0:T(8,128)S(1)} %shard_map.242.refs_0_), channel_id=1, source_target_pairs={{0,2},{1,3},{2,0},{3,1},{4,6},{5,7},{6,4},{7,5},{8,10},{9,11},{10,... | collective-permute-start | bytes 393224 | tf_op jit(solution)/shard_map/ppermute | solution.py:388
  90.8 1.2 %collective-permute-done.34.refs_1_ = f32[32,384]{1,0:T(8,128)S(1)} collective-permute-done((f32[32,384]{1,0:T(8,128)S(1)}, f32[32,384]{1,0:T(8,128)S(1)}, u32[]{:S(2)}, u32[]{:S(2)}) %collective-permute-start.34) | collective-permute-done | bytes 49184 | tf_op jit(solution)/shard_map/ppermute | solution.py:388
  92.8 1.4 %shard_map.245.refs_3_ = f32[32,1024]{1,0:T(8,128)S(1)} custom-call(f32[32,1024]{1,0:T(8,128)S(1)} %shard_map.242.refs_0_, f32[512,2048]{1,0:T(8,128)S(1)} %bitcast.65, f32[512,2048]{1,0:T(8,128)S(1)} %collective-permute-done.28.refs_2_), custom_call_target="tpu_custom_call" | custom-call | bytes 4194304 | tf_op jit(solution)/shard_map/pallas_call | solution.py:98
  94.6 1.4 %shard_map.246 = (f32[32,512]{1,0:T(8,128)S(1)}, f32[32,512]{1,0:T(8,128)S(1)}) custom-call(f32[32,1024]{1,0:T(8,128)S(1)} %collective-permute-done.33.refs_0_, f32[512,2048]{1,0:T(8,128)S(1)} %bitcast.66, f32[512,2048]{1,0:T(8,128)S(1)} %collective-permute-done.28.refs_2_, f32[32,1024]{1,0:T(8,128)S(1)} %shard_map.245.refs_3_), custom_call_target="tpu_custom_call" | custom-call | tf_op jit(solution)/shard_map/pallas_call | solution.py:98
  96.0 1.2 %collective-permute-done.35.refs_1_ = f32[32,512]{1,0:T(8,128)S(1)} collective-permute-done((f32[32,512]{1,0:T(8,128)S(1)}, f32[32,512]{1,0:T(8,128)S(1)}, u32[]{:S(2)}, u32[]{:S(2)}) %collective-permute-start.35) | collective-permute-done | bytes 65568 | tf_op jit(solution)/shard_map/ppermute | solution.py:388
  (79 shorter events, 9.4 us)
Async XLA Ops:
  2.0 6.5 %collective-permute-start.1 = (f32[64,512]{1,0:T(8,128)S(1)}, f32[64,512]{1,0:T(8,128)S(1)}, u32[]{:S(2)}, u32[]{:S(2)}) collective-permute-start(f32[64,512]{1,0:T(8,128)S(1)} %get-tuple-element.69.refs_0_), channel_id=1, source_target_pairs={{0,2},{1,3},{2,0},{3,1},{4,6},{5,7},{6,4},{7,5},{8,10},{9,11},{10,... | collective-permute-start | bytes 393224 | tf_op jit(solution)/shard_map/ppermute | solution.py:388
  5.0 3.8 %collective-permute-start = (f32[64,512]{1,0:T(8,128)S(1)}, f32[64,512]{1,0:T(8,128)S(1)}, u32[]{:S(2)}, u32[]{:S(2)}) collective-permute-start(f32[64,512]{1,0:T(8,128)S(1)} %get-tuple-element.69.refs_0_), channel_id=1, source_target_pairs={{0,1},{1,0},{2,3},{3,2},{4,5},{5,4},{6,7},{7,6},{8,9},{9,8},{10,11... | collective-permute-start | bytes 393224 | tf_op jit(solution)/shard_map/ppermute | solution.py:388
  8.5 1.3 %collective-permute-start.2 = (f32[64,512]{1,0:T(8,128)S(1)}, f32[64,512]{1,0:T(8,128)S(1)}, u32[]{:S(2)}, u32[]{:S(2)}) collective-permute-start(f32[64,512]{1,0:T(8,128)S(1)} %collective-permute-done.1.refs_2_), channel_id=1, source_target_pairs={{0,1},{1,0},{2,3},{3,2},{4,5},{5,4},{6,7},{7,6},{8,9},{9,8},{10,11... | collective-permute-start | bytes 393224 | tf_op jit(solution)/shard_map/ppermute | solution.py:388
  9.8 11.7 %copy-start = (f32[1,384,1536]{2,1,0:T(8,128)S(1)}, f32[1,384,1536]{2,1,0:T(8,128)}, u32[]{:S(2)}) copy-start(f32[1,384,1536]{2,1,0:T(8,128)} %param.33) | copy-start | bytes 7077892
  9.8 15.2 %copy-start.5 = (f32[1,384,1536]{2,1,0:T(8,128)S(1)}, f32[1,384,1536]{2,1,0:T(8,128)}, u32[]{:S(2)}) copy-start(f32[1,384,1536]{2,1,0:T(8,128)} %param.34) | copy-start | bytes 7077892
  12.6 1.8 %collective-permute-start.3 = (f32[2,32,1536]{2,1,0:T(8,128)S(1)}, f32[2,32,1536]{2,1,0:T(8,128)S(1)}, u32[]{:S(2)}, u32[]{:S(2)}) collective-permute-start(f32[2,32,1536]{2,1,0:T(8,128)S(1)} %get-tuple-element.67), channel_id=1, source_target_pairs={{0,1},{1,0},{2,3},{3,2},{4,5},{5,4},{6,7},{7,6},{8,9},{9,8},{10,11... | collective-permute-start | bytes 1179656 | tf_op jit(solution)/shard_map/ppermute | solution.py:388
  14.5 7.5 %collective-permute-start.6 = (f32[32,768]{1,0:T(8,128)S(1)}, f32[32,768]{1,0:T(8,128)S(1)}, u32[]{:S(2)}, u32[]{:S(2)}) collective-permute-start(f32[32,768]{1,0:T(8,128)S(1)} %get-tuple-element.78), channel_id=1, source_target_pairs={{4,0},{5,1},{6,2},{7,3},{8,4},{9,5},{10,6},{11,7},{12,8},{13,9},{1... | collective-permute-start | bytes 294920 | tf_op jit(solution)/shard_map/ppermute | solution.py:434
  15.8 6.2 %collective-permute-start.7 = (f32[32,768]{1,0:T(8,128)S(1)}, f32[32,768]{1,0:T(8,128)S(1)}, u32[]{:S(2)}, u32[]{:S(2)}) collective-permute-start(f32[32,768]{1,0:T(8,128)S(1)} %get-tuple-element.79), channel_id=1, source_target_pairs={{0,2},{1,3},{2,0},{3,1},{4,6},{5,7},{6,4},{7,5},{8,10},{9,11},{10,... | collective-permute-start | bytes 294920 | tf_op jit(solution)/shard_map/ppermute | solution.py:388
  17.6 7.4 %collective-permute-start.8 = (f32[32,768]{1,0:T(8,128)S(1)}, f32[32,768]{1,0:T(8,128)S(1)}, u32[]{:S(2)}, u32[]{:S(2)}) collective-permute-start(f32[32,768]{1,0:T(8,128)S(1)} %get-tuple-element.80), channel_id=1, source_target_pairs={{4,2},{5,3},{6,0},{7,1},{8,6},{9,7},{10,4},{11,5},{12,10},{13,11},... | collective-permute-start | bytes 294920 | tf_op jit(solution)/shard_map/ppermute | solution.py:434
  18.9 3.0 %collective-permute-start.5 = (f32[32,512]{1,0:T(8,128)S(1)}, f32[32,512]{1,0:T(8,128)S(1)}, u32[]{:S(2)}, u32[]{:S(2)}) collective-permute-start(f32[32,512]{1,0:T(8,128)S(1)} %get-tuple-element.74), channel_id=1, source_target_pairs={{0,1},{1,0},{2,3},{3,2},{4,5},{5,4},{6,7},{7,6},{8,9},{9,8},{10,11... | collective-permute-start | bytes 196616 | tf_op jit(solution)/shard_map/ppermute | solution.py:388
  20.1 1.4 %collective-permute-start.4 = (f32[32,384]{1,0:T(8,128)S(1)}, f32[32,384]{1,0:T(8,128)S(1)}, u32[]{:S(2)}, u32[]{:S(2)}) collective-permute-start(f32[32,384]{1,0:T(8,128)S(1)} %get-tuple-element.73), channel_id=1, source_target_pairs={{0,1},{1,0},{2,3},{3,2},{4,5},{5,4},{6,7},{7,6},{8,9},{9,8},{10,11... | collective-permute-start | bytes 147464 | tf_op jit(solution)/shard_map/ppermute | solution.py:388
  21.6 9.9 %collective-permute-start.10 = (f32[384,1536]{1,0:T(8,128)S(1)}, f32[384,1536]{1,0:T(8,128)S(1)}, u32[]{:S(2)}, u32[]{:S(2)}) collective-permute-start(f32[384,1536]{1,0:T(8,128)S(1)} %bitcast.44), channel_id=1, source_target_pairs={{0,1},{1,0},{2,3},{3,2},{4,5},{5,4},{6,7},{7,6},{8,9},{9,8},{10,11... | collective-permute-start | bytes 7077896 | tf_op jit(solution)/shard_map/ppermute | solution.py:388
  25.0 8.6 %collective-permute-start.13 = (f32[384,1536]{1,0:T(8,128)S(1)}, f32[384,1536]{1,0:T(8,128)S(1)}, u32[]{:S(2)}, u32[]{:S(2)}) collective-permute-start(f32[384,1536]{1,0:T(8,128)S(1)} %bitcast.71), channel_id=1, source_target_pairs={{0,1},{1,0},{2,3},{3,2},{4,5},{5,4},{6,7},{7,6},{8,9},{9,8},{10,11... | collective-permute-start | bytes 7077896 | tf_op jit(solution)/shard_map/ppermute | solution.py:388
  25.1 6.4 %collective-permute-start.11 = (f32[32,768]{1,0:T(8,128)S(1)}, f32[32,768]{1,0:T(8,128)S(1)}, u32[]{:S(2)}, u32[]{:S(2)}) collective-permute-start(f32[32,768]{1,0:T(8,128)S(1)} %shard_map.223.refs_4_.refs_5_), channel_id=1, source_target_pairs={{0,4},{1,5},{2,6},{3,7},{4,0},{5,1},{6,2},{7,3},{8,12},{9,13},{10,... | collective-permute-start | bytes 294920 | tf_op jit(solution)/shard_map/ppermute | solution.py:388
  27.8 5.8 %collective-permute-start.9 = (f32[32,768]{1,0:T(8,128)S(1)}, f32[32,768]{1,0:T(8,128)S(1)}, u32[]{:S(2)}, u32[]{:S(2)}) collective-permute-start(f32[32,768]{1,0:T(8,128)S(1)} %shard_map.223.refs_4_.refs_5_), channel_id=1, source_target_pairs={{0,6},{1,7},{2,4},{3,5},{4,2},{5,3},{6,0},{7,1},{8,14},{9,15},{10,... | collective-permute-start | bytes 294920 | tf_op jit(solution)/shard_map/ppermute | solution.py:388
  31.4 2.1 %copy-start.1 = (f32[1,384,1536]{2,1,0:T(8,128)S(1)}, f32[1,384,1536]{2,1,0:T(8,128)}, u32[]{:S(2)}) copy-start(f32[1,384,1536]{2,1,0:T(8,128)} %param.35) | copy-start | bytes 7077892
  33.6 7.4 %collective-permute-start.16 = (f32[384,1536]{1,0:T(8,128)S(1)}, f32[384,1536]{1,0:T(8,128)S(1)}, u32[]{:S(2)}, u32[]{:S(2)}) collective-permute-start(f32[384,1536]{1,0:T(8,128)S(1)} %bitcast.51), channel_id=1, source_target_pairs={{0,1},{1,0},{2,3},{3,2},{4,5},{5,4},{6,7},{7,6},{8,9},{9,8},{10,11... | collective-permute-start | bytes 7077896 | tf_op jit(solution)/shard_map/ppermute | solution.py:388
  33.7 5.7 %collective-permute-start.14 = (f32[32,768]{1,0:T(8,128)S(1)}, f32[32,768]{1,0:T(8,128)S(1)}, u32[]{:S(2)}, u32[]{:S(2)}) collective-permute-start(f32[32,768]{1,0:T(8,128)S(1)} %shard_map.225.refs_5_), channel_id=1, source_target_pairs={{0,2},{1,3},{2,0},{3,1},{4,8},{5,9},{6,10},{7,11},{8,4},{9,5},{10,... | collective-permute-start | bytes 294920 | tf_op jit(solution)/shard_map/ppermute | solution.py:388
  34.9 6.1 %collective-permute-start.12 = (f32[32,768]{1,0:T(8,128)S(1)}, f32[32,768]{1,0:T(8,128)S(1)}, u32[]{:S(2)}, u32[]{:S(2)}) collective-permute-start(f32[32,768]{1,0:T(8,128)S(1)} %shard_map.225.refs_5_), channel_id=1, source_target_pairs={{0,2},{1,3},{2,0},{3,1},{4,10},{5,11},{6,8},{7,9},{8,6},{9,7},{10,... | collective-permute-start | bytes 294920 | tf_op jit(solution)/shard_map/ppermute | solution.py:388
  39.3 1.9 %copy-start.2 = (f32[1,512,1536]{2,1,0:T(8,128)S(1)}, f32[1,512,1536]{2,1,0:T(8,128)}, u32[]{:S(2)}) copy-start(f32[1,512,1536]{2,1,0:T(8,128)} %param.32) | copy-start | bytes 9437188
  41.2 14.5 %collective-permute-start.20 = (f32[512,1536]{1,0:T(8,128)S(1)}, f32[512,1536]{1,0:T(8,128)S(1)}, u32[]{:S(2)}, u32[]{:S(2)}) collective-permute-start(f32[512,1536]{1,0:T(8,128)S(1)} %bitcast.59), channel_id=1, source_target_pairs={{0,1},{1,0},{2,3},{3,2},{4,5},{5,4},{6,7},{7,6},{8,9},{9,8},{10,11... | collective-permute-start | bytes 9437192 | tf_op jit(solution)/shard_map/ppermute | solution.py:388
  41.2 6.8 %collective-permute-start.17 = (f32[32,768]{1,0:T(8,128)S(1)}, f32[32,768]{1,0:T(8,128)S(1)}, u32[]{:S(2)}, u32[]{:S(2)}) collective-permute-start(f32[32,768]{1,0:T(8,128)S(1)} %shard_map.227.refs_5_), channel_id=1, source_target_pairs={{0,4},{1,5},{2,6},{3,7},{4,0},{5,1},{6,2},{7,3},{8,12},{9,13},{10,... | collective-permute-start | bytes 294920 | tf_op jit(solution)/shard_map/ppermute | solution.py:388
  44.4 5.8 %collective-permute-start.15 = (f32[32,768]{1,0:T(8,128)S(1)}, f32[32,768]{1,0:T(8,128)S(1)}, u32[]{:S(2)}, u32[]{:S(2)}) collective-permute-start(f32[32,768]{1,0:T(8,128)S(1)} %shard_map.227.refs_5_), channel_id=1, source_target_pairs={{0,6},{1,7},{2,4},{3,5},{4,2},{5,3},{6,0},{7,1},{8,14},{9,15},{10,... | collective-permute-start | bytes 294920 | tf_op jit(solution)/shard_map/ppermute | solution.py:388
  50.2 4.7 %collective-permute-start.18 = (f32[32,768]{1,0:T(8,128)S(1)}, f32[32,768]{1,0:T(8,128)S(1)}, u32[]{:S(2)}, u32[]{:S(2)}) collective-permute-start(f32[32,768]{1,0:T(8,128)S(1)} %shard_map.229.refs_0_), channel_id=1, source_target_pairs={{0,2},{1,3},{2,0},{3,1},{4,6},{5,7},{6,4},{7,5},{8,10},{9,11},{10,... | collective-permute-start | bytes 294920 | tf_op jit(solution)/shard_map/ppermute | solution.py:388
  52.2 3.5 %copy-start.4 = (f32[1,512,1536]{2,1,0:T(8,128)S(1)}, f32[1,512,1536]{2,1,0:T(8,128)}, u32[]{:S(2)}) copy-start(f32[1,512,1536]{2,1,0:T(8,128)} %param.31) | copy-start | bytes 9437188
  55.7 8.0 %collective-permute-start.23 = (f32[512,1536]{1,0:T(8,128)S(1)}, f32[512,1536]{1,0:T(8,128)S(1)}, u32[]{:S(2)}, u32[]{:S(2)}) collective-permute-start(f32[512,1536]{1,0:T(8,128)S(1)} %bitcast.68), channel_id=1, source_target_pairs={{0,1},{1,0},{2,3},{3,2},{4,5},{5,4},{6,7},{7,6},{8,9},{9,8},{10,11... | collective-permute-start | bytes 9437192 | tf_op jit(solution)/shard_map/ppermute | solution.py:388
  55.8 5.2 %collective-permute-start.21 = (f32[32,768]{1,0:T(8,128)S(1)}, f32[32,768]{1,0:T(8,128)S(1)}, u32[]{:S(2)}, u32[]{:S(2)}) collective-permute-start(f32[32,768]{1,0:T(8,128)S(1)} %shard_map.231.refs_4_.refs_5_), channel_id=1, source_target_pairs={{0,4},{1,5},{2,6},{3,7},{4,0},{5,1},{6,2},{7,3},{8,12},{9,13},{10,... | collective-permute-start | bytes 294920 | tf_op jit(solution)/shard_map/ppermute | solution.py:388
  57.5 6.3 %collective-permute-start.19 = (f32[32,768]{1,0:T(8,128)S(1)}, f32[32,768]{1,0:T(8,128)S(1)}, u32[]{:S(2)}, u32[]{:S(2)}) collective-permute-start(f32[32,768]{1,0:T(8,128)S(1)} %shard_map.231.refs_4_.refs_5_), channel_id=1, source_target_pairs={{0,6},{1,7},{2,4},{3,5},{4,2},{5,3},{6,0},{7,1},{8,14},{9,15},{10,... | collective-permute-start | bytes 294920 | tf_op jit(solution)/shard_map/ppermute | solution.py:388
  61.0 2.8 %copy-start.3 = (f32[1,512,2048]{2,1,0:T(8,128)S(1)}, f32[1,512,2048]{2,1,0:T(8,128)}, u32[]{:S(2)}) copy-start(f32[1,512,2048]{2,1,0:T(8,128)} %param.30) | copy-start | bytes 12582916
  63.8 25.7 %collective-permute-start.28 = (f32[512,2048]{1,0:T(8,128)S(1)}, f32[512,2048]{1,0:T(8,128)S(1)}, u32[]{:S(2)}, u32[]{:S(2)}) collective-permute-start(f32[512,2048]{1,0:T(8,128)S(1)} %bitcast.64), channel_id=1, source_target_pairs={{0,1},{1,0},{2,3},{3,2},{4,5},{5,4},{6,7},{7,6},{8,9},{9,8},{10,11... | collective-permute-start | bytes 12582920 | tf_op jit(solution)/shard_map/ppermute | solution.py:388
  63.8 5.7 %collective-permute-start.24 = (f32[32,768]{1,0:T(8,128)S(1)}, f32[32,768]{1,0:T(8,128)S(1)}, u32[]{:S(2)}, u32[]{:S(2)}) collective-permute-start(f32[32,768]{1,0:T(8,128)S(1)} %shard_map.233.refs_5_), channel_id=1, source_target_pairs={{0,2},{1,3},{2,0},{3,1},{4,8},{5,9},{6,10},{7,11},{8,4},{9,5},{10,... | collective-permute-start | bytes 294920 | tf_op jit(solution)/shard_map/ppermute | solution.py:388
  64.8 6.3 %collective-permute-start.22 = (f32[32,768]{1,0:T(8,128)S(1)}, f32[32,768]{1,0:T(8,128)S(1)}, u32[]{:S(2)}, u32[]{:S(2)}) collective-permute-start(f32[32,768]{1,0:T(8,128)S(1)} %shard_map.233.refs_5_), channel_id=1, source_target_pairs={{0,2},{1,3},{2,0},{3,1},{4,10},{5,11},{6,8},{7,9},{8,6},{9,7},{10,... | collective-permute-start | bytes 294920 | tf_op jit(solution)/shard_map/ppermute | solution.py:388
  71.2 6.8 %collective-permute-start.26 = (f32[32,768]{1,0:T(8,128)S(1)}, f32[32,768]{1,0:T(8,128)S(1)}, u32[]{:S(2)}, u32[]{:S(2)}) collective-permute-start(f32[32,768]{1,0:T(8,128)S(1)} %shard_map.235.refs_0_.refs_5_), channel_id=1, source_target_pairs={{0,4},{1,5},{2,6},{3,7},{4,0},{5,1},{6,2},{7,3},{8,12},{9,13},{10,... | collective-permute-start | bytes 294920 | tf_op jit(solution)/shard_map/ppermute | solution.py:388
  75.1 5.7 %collective-permute-start.25 = (f32[32,768]{1,0:T(8,128)S(1)}, f32[32,768]{1,0:T(8,128)S(1)}, u32[]{:S(2)}, u32[]{:S(2)}) collective-permute-start(f32[32,768]{1,0:T(8,128)S(1)} %shard_map.235.refs_0_.refs_5_), channel_id=1, source_target_pairs={{0,6},{1,7},{2,4},{3,5},{4,2},{5,3},{6,0},{7,1},{8,14},{9,15},{10,... | collective-permute-start | bytes 294920 | tf_op jit(solution)/shard_map/ppermute | solution.py:388
  78.0 6.0 %collective-permute-start.29 = (f32[32,768]{1,0:T(8,128)S(1)}, f32[32,768]{1,0:T(8,128)S(1)}, u32[]{:S(2)}, u32[]{:S(2)}) collective-permute-start(f32[32,768]{1,0:T(8,128)S(1)} %shard_map.235.refs_0_.refs_5_), channel_id=1, source_target_pairs={{0,2},{1,3},{2,0},{3,1},{4,8},{5,9},{6,10},{7,11},{8,4},{9,5},{10,... | collective-permute-start | bytes 294920 | tf_op jit(solution)/shard_map/ppermute | solution.py:388
  79.1 7.5 %collective-permute-start.30 = (f32[32,768]{1,0:T(8,128)S(1)}, f32[32,768]{1,0:T(8,128)S(1)}, u32[]{:S(2)}, u32[]{:S(2)}) collective-permute-start(f32[32,768]{1,0:T(8,128)S(1)} %shard_map.235.refs_0_.refs_5_), channel_id=1, source_target_pairs={{0,2},{1,3},{2,0},{3,1},{4,10},{5,11},{6,8},{7,9},{8,6},{9,7},{10,... | collective-permute-start | bytes 294920 | tf_op jit(solution)/shard_map/ppermute | solution.py:388
  81.7 6.0 %collective-permute-start.32 = (f32[32,768]{1,0:T(8,128)S(1)}, f32[32,768]{1,0:T(8,128)S(1)}, u32[]{:S(2)}, u32[]{:S(2)}) collective-permute-start(f32[32,768]{1,0:T(8,128)S(1)} %shard_map.238.refs_0_), channel_id=1, source_target_pairs={{0,2},{1,3},{2,0},{3,1},{4,6},{5,7},{6,4},{7,5},{8,10},{9,11},{10,... | collective-permute-start | bytes 294920 | tf_op jit(solution)/shard_map/ppermute | solution.py:388
  82.9 5.8 %collective-permute-start.31 = (f32[32,768]{1,0:T(8,128)S(1)}, f32[32,768]{1,0:T(8,128)S(1)}, u32[]{:S(2)}, u32[]{:S(2)}) collective-permute-start(f32[32,768]{1,0:T(8,128)S(1)} %shard_map.238.refs_0_), channel_id=1, source_target_pairs={{0,4},{1,5},{2,6},{3,7},{4,0},{5,1},{6,2},{7,3},{8,12},{9,13},{10,... | collective-permute-start | bytes 294920 | tf_op jit(solution)/shard_map/ppermute | solution.py:388
  83.9 5.5 %collective-permute-start.27 = (f32[32,768]{1,0:T(8,128)S(1)}, f32[32,768]{1,0:T(8,128)S(1)}, u32[]{:S(2)}, u32[]{:S(2)}) collective-permute-start(f32[32,768]{1,0:T(8,128)S(1)} %shard_map.238.refs_0_), channel_id=1, source_target_pairs={{0,6},{1,7},{2,4},{3,5},{4,2},{5,3},{6,0},{7,1},{8,14},{9,15},{10,... | collective-permute-start | bytes 294920 | tf_op jit(solution)/shard_map/ppermute | solution.py:388
  89.5 2.6 %copy-start.9 = (f32[1,384,64]{1,2,0:T(8,128)S(1)}, f32[1,384,64]{1,2,0:T(8,128)}, u32[]{:S(2)}) copy-start(f32[1,384,64]{1,2,0:T(8,128)} %param.27) | copy-start | bytes 294916
  89.5 2.6 %copy-start.10 = (f32[1,384,64]{1,2,0:T(8,128)S(1)}, f32[1,384,64]{1,2,0:T(8,128)}, u32[]{:S(2)}) copy-start(f32[1,384,64]{1,2,0:T(8,128)} %param.28) | copy-start | bytes 294916
  89.5 2.6 %copy-start.11 = (f32[1,384,64]{1,2,0:T(8,128)S(1)}, f32[1,384,64]{1,2,0:T(8,128)}, u32[]{:S(2)}) copy-start(f32[1,384,64]{1,2,0:T(8,128)} %param.29) | copy-start | bytes 294916
  89.5 5.0 %collective-permute-start.33 = (f32[32,1024]{1,0:T(8,128)S(1)}, f32[32,1024]{1,0:T(8,128)S(1)}, u32[]{:S(2)}, u32[]{:S(2)}) collective-permute-start(f32[32,1024]{1,0:T(8,128)S(1)} %shard_map.242.refs_0_), channel_id=1, source_target_pairs={{0,2},{1,3},{2,0},{3,1},{4,6},{5,7},{6,4},{7,5},{8,10},{9,11},{10,... | collective-permute-start | bytes 393224 | tf_op jit(solution)/shard_map/ppermute | solution.py:388
  90.7 1.3 %collective-permute-start.34 = (f32[32,384]{1,0:T(8,128)S(1)}, f32[32,384]{1,0:T(8,128)S(1)}, u32[]{:S(2)}, u32[]{:S(2)}) collective-permute-start(f32[32,384]{1,0:T(8,128)S(1)} %get-tuple-element.102), channel_id=1, source_target_pairs={{0,1},{1,0},{2,3},{3,2},{4,5},{5,4},{6,7},{7,6},{8,9},{9,8},{10,11... | collective-permute-start | bytes 147464 | tf_op jit(solution)/shard_map/ppermute | solution.py:388
  94.6 2.7 %copy-start.6 = (f32[1,512,64]{1,2,0:T(8,128)S(1)}, f32[1,512,64]{1,2,0:T(8,128)}, u32[]{:S(2)}) copy-start(f32[1,512,64]{1,2,0:T(8,128)} %param.24) | copy-start | bytes 393220
  94.6 2.7 %copy-start.7 = (f32[1,512,64]{1,2,0:T(8,128)S(1)}, f32[1,512,64]{1,2,0:T(8,128)}, u32[]{:S(2)}) copy-start(f32[1,512,64]{1,2,0:T(8,128)} %param.25) | copy-start | bytes 393220
  94.6 2.7 %copy-start.8 = (f32[1,512,64]{1,2,0:T(8,128)S(1)}, f32[1,512,64]{1,2,0:T(8,128)}, u32[]{:S(2)}) copy-start(f32[1,512,64]{1,2,0:T(8,128)} %param.26) | copy-start | bytes 393220
  95.9 1.3 %collective-permute-start.35 = (f32[32,512]{1,0:T(8,128)S(1)}, f32[32,512]{1,0:T(8,128)S(1)}, u32[]{:S(2)}, u32[]{:S(2)}) collective-permute-start(f32[32,512]{1,0:T(8,128)S(1)} %get-tuple-element.109), channel_id=1, source_target_pairs={{0,1},{1,0},{2,3},{3,2},{4,5},{5,4},{6,7},{7,6},{8,9},{9,8},{10,11... | collective-permute-start | bytes 196616 | tf_op jit(solution)/shard_map/ppermute | solution.py:388

commit v13 on v12

--- a/solution.py
+++ b/solution.py
@@ -143,21 +143,28 @@
     )(*held)
 
 
-def forces_kernel(swap_chips, pieces, matrices, mine, theirs, copy, below):
+def load_columns(chip, core, width):
+    place = (lax.axis_index("rec") ^ chip) * 2 + (lax.axis_index("blk") ^ core)
+    return pl.ds(pl.multiple_of(place * width, 128), width)
+
+
+def loads_kernel(places, pieces, matrices, out):
+    total = None
+    for (chip, core), piece in zip(places, pieces):
+        value = piece[...]
+        part = times_rows(value, matrices[0], columns=load_columns(chip, core, value.shape[1]))
+        total = part if total is None else total + part
+    out[...] = total
+
+
+def forces_kernel(place, pieces, matrices, sofar, mine, theirs, copy, below):
     (rows,) = matrices
     faces = mine.shape[2]
     inner = rows.shape[1] - faces
-    inverse = rows.at[:, :inner]
     above = rows.at[:, inner:]
-    if swap_chips:
-        chips = len(pieces) // 2
-        core = lax.axis_index("blk")
-        sets = [in_order([pieces[2 * j][...], pieces[2 * j + 1][...]], core) for j in range(chips)]
-        sets = [jnp.concatenate(pair, axis=1) for pair in sets]
-        full = jnp.concatenate(in_order(sets, lax.axis_index("rec")), axis=1)
-    else:
-        full = pieces[0][...]
-    part = times_rows(full, inverse)
+    value = pieces[0][...]
+    columns = slice(0, inner) if place is None else load_columns(*place, value.shape[1])
+    part = plus(times_rows(value, rows, columns=columns), sofar)
     half = part.shape[0] // 2
     second = lax.axis_index("blk") == 1
     for i, matrix in enumerate((above, below)):
@@ -484,16 +491,24 @@
     phase_rows, *across = lax.optimization_barrier([phase_rows, *across])
     beside = [mv.core(piece) for piece in [load_int] + across]
     pieces = [piece for pair in zip([load_int] + across, beside) for piece in pair]
-    aligned = load_int.shape[1] % 128 == 0
-    if not aligned:
+    sofar, place = [], None
+    if load_int.shape[1] % 128 == 0:
+        places = [(j, i) for j in range(mv.chips) for i in range(2)]
+        place, last_piece = places[-1], pieces[-1]
+        kernel = functools.partial(loads_kernel, places[:-1])
+        shape = [(records, own_int)]
+        sofar = call(kernel, shape, pieces[:-1], [phase_rows], cost=4 << 20)
+        pieces = [last_piece]
+    else:
         pieces = [
             mv.by_chip([mv.by_core(pieces[2 * j], pieces[2 * j + 1], 1) for j in range(mv.chips)])
         ]
     mine, theirs = call(
-        functools.partial(forces_kernel, aligned),
+        functools.partial(forces_kernel, place),
         [(2, half, faces)] * 2,
         pieces,
         [phase_rows],
+        sofar,
         late=couple_below[0],
     )
     chunks = call(

time: 98.3 us -> 98.9 us (level)
  Pallas kernels: 19.3 us -> 21.1 us
  waiting for transfers between devices: 42.4 us -> 41.4 us
    pallas_call x28 -> x29, Pallas kernels: 13.7 us -> 15.4 us  [call(): pl.pallas_call(body, in_specs=[VMEM] * len(flat) + [pl.BlockSpec(memory_s...]
    ppermute x34, waiting for transfers between devices: 39.4 us -> 38.2 us  [permute(): return lax.ppermute(value, AXES, pairs)]
  transfers between devices with their start and end apart: 36 -> 36, of which waited for: 22 -> 21; matrix products, arithmetic and copies ran while one was open for 0% -> 0% of each run, Pallas kernels for 13% -> 14%
where the time goes in v13:
time: 98.9 us; the launch traced here: 98.6 us
  waiting for transfers between devices  41.4 us (42%)
  starting transfers between devices  34.9 us (35%)
  Pallas kernels  21.1 us (21%)
    ppermute x34, waiting for transfers between devices, permute(): return lax.ppermute(value, AXES, pairs)  38.2 us
    ppermute x34, starting transfers between devices, permute(): return lax.ppermute(value, AXES, pairs)  32.3 us
    pallas_call x29, Pallas kernels, call(): pl.pallas_call(body, in_specs=[VMEM] * len(flat) + [pl.BlockSpec(memory_s...  15.4 us
    ppermute x2, waiting for transfers between devices, shift(): return lax.ppermute(value, AXES, pairs)  3.21 us
    pallas_call x1, Pallas kernels, staged(): pl.pallas_call(body, in_specs=[pl.BlockSpec(memory_space=pltpu.HBM)] * co...  3.16 us
    ppermute x2, starting transfers between devices, shift(): return lax.ppermute(value, AXES, pairs)  2.57 us
    pallas_call x2, Pallas kernels, fetched(): pl.pallas_call(body, in_specs=[pl.BlockSpec(memory_space=pltpu.HBM)] * co...  2.48 us
  transfers between devices with their start and end apart: 36, of which 21 were waited for; matrix products, arithmetic and copies ran while one was open for 0% of the time, Pallas kernels for 14%

profile of v13, /device:TPU:0, one launch (start us, length us, event | category | flops | bytes accessed | tf_op | source)
XLA Modules:
  0.0 98.6 jit_solution(16887209863750048227)
XLA Ops:
  0.6 1.3 %shard_map.217 = (f32[64,512]{1,0:T(8,128)S(1)}, f32[64,128]{1,0:T(8,128)S(1)}) custom-call(s32[1,64]{1,0:T(1,128)} %bitcast.87, f32[1,512]{1,0:T(1,128)} %bitcast.86, f32[1,512]{1,0:T(1,128)} %refs_2_.1, f32[1,512]{1,0:T(1,128)} %refs_3_.1, f32[64,512]{1,0:T(8,128)} %bitcast.74, f32[64,512]{1,0:T(8,128)} %bitcast.76, f32[64,512]{1,0:T(8,128)} %bitcast.78), custom_call_target="tpu_custom_call" | custom-call | tf_op jit(solution)/shard_map/pallas_call | solution.py:196
  2.0 3.0 %collective-permute-start = (f32[64,512]{1,0:T(8,128)S(1)}, f32[64,512]{1,0:T(8,128)S(1)}, u32[]{:S(2)}, u32[]{:S(2)}) collective-permute-start(f32[64,512]{1,0:T(8,128)S(1)} %get-tuple-element.69.refs_0_), channel_id=1, source_target_pairs={{0,2},{1,3},{2,0},{3,1},{4,6},{5,7},{6,4},{7,5},{8,10},{9,11},{10,... | collective-permute-start | bytes 393224 | tf_op jit(solution)/shard_map/ppermute | solution.py:395
  5.0 3.2 %shard_map.218.refs_3_.refs_1_ = f32[512,3584]{1,0:T(8,128)S(1)} custom-call(f32[512,2048]{1,0:T(8,128)} %bitcast.63, f32[512,1536]{1,0:T(8,128)} %bitcast.58), custom_call_target="tpu_custom_call" | custom-call | tf_op jit(solution)/shard_map/pallas_call | solution.py:136
  8.7 1.2 %shard_map.219.refs_2_ = f32[64,512]{1,0:T(8,128)S(1)} custom-call(f32[64,512]{1,0:T(8,128)S(1)} %get-tuple-element.69.refs_0_, f32[64,512]{1,0:T(8,128)S(1)} %collective-permute-done.2.refs_1_, f32[64,512]{1,0:T(8,128)S(1)} %collective-permute-done.refs_2_, f32[512,3584]{1,0:T(8,128)S(1)} %shard_map.218.refs_3_.refs_1_), custom_call_target="tpu_custom_call" | custom-call | bytes 4194304 | tf_op jit(solution)/shard_map/pallas_call | solution.py:98
  9.9 3.3 %shard_map.220 = (f32[2,32,1536]{2,1,0:T(8,128)S(1)}, f32[2,32,1536]{2,1,0:T(8,128)S(1)}) custom-call(f32[64,512]{1,0:T(8,128)S(1)} %collective-permute-done.1.refs_0_, f32[512,3584]{1,0:T(8,128)S(1)} %shard_map.218.refs_3_.refs_1_, f32[64,512]{1,0:T(8,128)S(1)} %shard_map.219.refs_2_, f32[512,1536]{1,0:T(8,128)} %bitcast.67), custom_call_target="tpu_custom_call" | custom-call | tf_op jit(solution)/shard_map/pallas_call | solution.py:98
  13.6 1.5 %collective-permute-done.3.refs_1_ = f32[2,32,1536]{2,1,0:T(8,128)S(1)} collective-permute-done((f32[2,32,1536]{2,1,0:T(8,128)S(1)}, f32[2,32,1536]{2,1,0:T(8,128)S(1)}, u32[]{:S(2)}, u32[]{:S(2)}) %collective-permute-start.3) | collective-permute-done | bytes 393248 | tf_op jit(solution)/shard_map/ppermute | solution.py:395
  15.1 1.3 %collective-permute-start.6 = (f32[32,768]{1,0:T(8,128)S(1)}, f32[32,768]{1,0:T(8,128)S(1)}, u32[]{:S(2)}, u32[]{:S(2)}) collective-permute-start(f32[32,768]{1,0:T(8,128)S(1)} %get-tuple-element.78), channel_id=1, source_target_pairs={{4,0},{5,1},{6,2},{7,3},{8,4},{9,5},{10,6},{11,7},{12,8},{13,9},{1... | collective-permute-start | bytes 294920 | tf_op jit(solution)/shard_map/ppermute | solution.py:441
  16.4 1.7 %collective-permute-start.7 = (f32[32,768]{1,0:T(8,128)S(1)}, f32[32,768]{1,0:T(8,128)S(1)}, u32[]{:S(2)}, u32[]{:S(2)}) collective-permute-start(f32[32,768]{1,0:T(8,128)S(1)} %get-tuple-element.79), channel_id=1, source_target_pairs={{0,2},{1,3},{2,0},{3,1},{4,6},{5,7},{6,4},{7,5},{8,10},{9,11},{10,... | collective-permute-start | bytes 294920 | tf_op jit(solution)/shard_map/ppermute | solution.py:395
  18.1 1.3 %collective-permute-start.8 = (f32[32,768]{1,0:T(8,128)S(1)}, f32[32,768]{1,0:T(8,128)S(1)}, u32[]{:S(2)}, u32[]{:S(2)}) collective-permute-start(f32[32,768]{1,0:T(8,128)S(1)} %get-tuple-element.80), channel_id=1, source_target_pairs={{4,2},{5,3},{6,0},{7,1},{8,6},{9,7},{10,4},{11,5},{12,10},{13,11},... | collective-permute-start | bytes 294920 | tf_op jit(solution)/shard_map/ppermute | solution.py:441
  19.6 1.1 %shard_map.223 = (f32[32,384]{1,0:T(8,128)S(1)}, f32[32,384]{1,0:T(8,128)S(1)}) custom-call(f32[1,384]{1,0:T(1,128)} %refs_0_.1, f32[1,384]{1,0:T(1,128)} %refs_1_.1, f32[64,384]{1,0:T(8,128)} %bitcast.80, f32[64,384]{1,0:T(8,128)} %bitcast.82, f32[64,384]{1,0:T(8,128)} %bitcast.84, f32[64,128]{1,0:T(8,128)S(1)} %get-tuple-element.72.refs_5_), custom_call_target="tpu_custom_call" | custom-call | tf_op jit(solution)/shard_map/pallas_call | solution.py:196
  21.2 0.9 collective-permute-done.4.refs_1_
  22.5 3.2 %collective-permute-done.8.refs_5_ = f32[32,768]{1,0:T(8,128)S(1)} collective-permute-done((f32[32,768]{1,0:T(8,128)S(1)}, f32[32,768]{1,0:T(8,128)S(1)}, u32[]{:S(2)}, u32[]{:S(2)}) %collective-permute-start.8) | collective-permute-done | bytes 98336 | tf_op jit(solution)/shard_map/ppermute | solution.py:441
  25.8 2.5 %collective-permute-start.11 = (f32[32,768]{1,0:T(8,128)S(1)}, f32[32,768]{1,0:T(8,128)S(1)}, u32[]{:S(2)}, u32[]{:S(2)}) collective-permute-start(f32[32,768]{1,0:T(8,128)S(1)} %shard_map.224.refs_4_.refs_5_), channel_id=1, source_target_pairs={{0,4},{1,5},{2,6},{3,7},{4,0},{5,1},{6,2},{7,3},{8,12},{9,13},{10,... | collective-permute-start | bytes 294920 | tf_op jit(solution)/shard_map/ppermute | solution.py:395
  28.5 3.5 %collective-permute-done.11.refs_0_ = f32[32,768]{1,0:T(8,128)S(1)} collective-permute-done((f32[32,768]{1,0:T(8,128)S(1)}, f32[32,768]{1,0:T(8,128)S(1)}, u32[]{:S(2)}, u32[]{:S(2)}) %collective-permute-start.11) | collective-permute-done | bytes 98336 | tf_op jit(solution)/shard_map/ppermute | solution.py:395
  32.0 2.1 %collective-permute-done.9.refs_0_ = f32[32,768]{1,0:T(8,128)S(1)} collective-permute-done((f32[32,768]{1,0:T(8,128)S(1)}, f32[32,768]{1,0:T(8,128)S(1)}, u32[]{:S(2)}, u32[]{:S(2)}) %collective-permute-start.9) | collective-permute-done | bytes 98336 | tf_op jit(solution)/shard_map/ppermute | solution.py:395
  34.2 1.3 %collective-permute-start.14 = (f32[32,768]{1,0:T(8,128)S(1)}, f32[32,768]{1,0:T(8,128)S(1)}, u32[]{:S(2)}, u32[]{:S(2)}) collective-permute-start(f32[32,768]{1,0:T(8,128)S(1)} %shard_map.226.refs_5_), channel_id=1, source_target_pairs={{0,2},{1,3},{2,0},{3,1},{4,8},{5,9},{6,10},{7,11},{8,4},{9,5},{10,... | collective-permute-start | bytes 294920 | tf_op jit(solution)/shard_map/ppermute | solution.py:395
  36.3 3.6 %collective-permute-done.14.refs_0_ = f32[32,768]{1,0:T(8,128)S(1)} collective-permute-done((f32[32,768]{1,0:T(8,128)S(1)}, f32[32,768]{1,0:T(8,128)S(1)}, u32[]{:S(2)}, u32[]{:S(2)}) %collective-permute-start.14) | collective-permute-done | bytes 98336 | tf_op jit(solution)/shard_map/ppermute | solution.py:395
  39.9 1.7 %collective-permute-done.12.refs_0_ = f32[32,768]{1,0:T(8,128)S(1)} collective-permute-done((f32[32,768]{1,0:T(8,128)S(1)}, f32[32,768]{1,0:T(8,128)S(1)}, u32[]{:S(2)}, u32[]{:S(2)}) %collective-permute-start.12) | collective-permute-done | bytes 98336 | tf_op jit(solution)/shard_map/ppermute | solution.py:395
  41.8 3.2 %collective-permute-start.17 = (f32[32,768]{1,0:T(8,128)S(1)}, f32[32,768]{1,0:T(8,128)S(1)}, u32[]{:S(2)}, u32[]{:S(2)}) collective-permute-start(f32[32,768]{1,0:T(8,128)S(1)} %shard_map.228.refs_5_), channel_id=1, source_target_pairs={{0,4},{1,5},{2,6},{3,7},{4,0},{5,1},{6,2},{7,3},{8,12},{9,13},{10,... | collective-permute-start | bytes 294920 | tf_op jit(solution)/shard_map/ppermute | solution.py:395
  45.0 3.6 %collective-permute-done.17.refs_0_ = f32[32,768]{1,0:T(8,128)S(1)} collective-permute-done((f32[32,768]{1,0:T(8,128)S(1)}, f32[32,768]{1,0:T(8,128)S(1)}, u32[]{:S(2)}, u32[]{:S(2)}) %collective-permute-start.17) | collective-permute-done | bytes 98336 | tf_op jit(solution)/shard_map/ppermute | solution.py:395
  48.6 2.1 %collective-permute-done.15.refs_0_ = f32[32,768]{1,0:T(8,128)S(1)} collective-permute-done((f32[32,768]{1,0:T(8,128)S(1)}, f32[32,768]{1,0:T(8,128)S(1)}, u32[]{:S(2)}, u32[]{:S(2)}) %collective-permute-start.15) | collective-permute-done | bytes 98336 | tf_op jit(solution)/shard_map/ppermute | solution.py:395
  50.7 1.3 %collective-permute-start.18 = (f32[32,768]{1,0:T(8,128)S(1)}, f32[32,768]{1,0:T(8,128)S(1)}, u32[]{:S(2)}, u32[]{:S(2)}) collective-permute-start(f32[32,768]{1,0:T(8,128)S(1)} %shard_map.230.refs_0_), channel_id=1, source_target_pairs={{0,2},{1,3},{2,0},{3,1},{4,6},{5,7},{6,4},{7,5},{8,10},{9,11},{10,... | collective-permute-start | bytes 294920 | tf_op jit(solution)/shard_map/ppermute | solution.py:395
  52.8 2.6 %collective-permute-done.18.refs_0_ = f32[32,768]{1,0:T(8,128)S(1)} collective-permute-done((f32[32,768]{1,0:T(8,128)S(1)}, f32[32,768]{1,0:T(8,128)S(1)}, u32[]{:S(2)}, u32[]{:S(2)}) %collective-permute-start.18) | collective-permute-done | bytes 98336 | tf_op jit(solution)/shard_map/ppermute | solution.py:395
  56.3 1.7 %collective-permute-start.21 = (f32[32,768]{1,0:T(8,128)S(1)}, f32[32,768]{1,0:T(8,128)S(1)}, u32[]{:S(2)}, u32[]{:S(2)}) collective-permute-start(f32[32,768]{1,0:T(8,128)S(1)} %shard_map.232.refs_4_.refs_5_), channel_id=1, source_target_pairs={{0,4},{1,5},{2,6},{3,7},{4,0},{5,1},{6,2},{7,3},{8,12},{9,13},{10,... | collective-permute-start | bytes 294920 | tf_op jit(solution)/shard_map/ppermute | solution.py:395
  58.0 1.0 %collective-permute-start.19 = (f32[32,768]{1,0:T(8,128)S(1)}, f32[32,768]{1,0:T(8,128)S(1)}, u32[]{:S(2)}, u32[]{:S(2)}) collective-permute-start(f32[32,768]{1,0:T(8,128)S(1)} %shard_map.232.refs_4_.refs_5_), channel_id=1, source_target_pairs={{0,6},{1,7},{2,4},{3,5},{4,2},{5,3},{6,0},{7,1},{8,14},{9,15},{10,... | collective-permute-start | bytes 294920 | tf_op jit(solution)/shard_map/ppermute | solution.py:395
  59.1 2.5 %collective-permute-done.21.refs_0_ = f32[32,768]{1,0:T(8,128)S(1)} collective-permute-done((f32[32,768]{1,0:T(8,128)S(1)}, f32[32,768]{1,0:T(8,128)S(1)}, u32[]{:S(2)}, u32[]{:S(2)}) %collective-permute-start.21) | collective-permute-done | bytes 98336 | tf_op jit(solution)/shard_map/ppermute | solution.py:395
  61.6 2.7 %collective-permute-done.19.refs_0_ = f32[32,768]{1,0:T(8,128)S(1)} collective-permute-done((f32[32,768]{1,0:T(8,128)S(1)}, f32[32,768]{1,0:T(8,128)S(1)}, u32[]{:S(2)}, u32[]{:S(2)}) %collective-permute-start.19) | collective-permute-done | bytes 98336 | tf_op jit(solution)/shard_map/ppermute | solution.py:395
  64.4 1.0 %collective-permute-start.24 = (f32[32,768]{1,0:T(8,128)S(1)}, f32[32,768]{1,0:T(8,128)S(1)}, u32[]{:S(2)}, u32[]{:S(2)}) collective-permute-start(f32[32,768]{1,0:T(8,128)S(1)} %shard_map.234.refs_5_), channel_id=1, source_target_pairs={{0,2},{1,3},{2,0},{3,1},{4,8},{5,9},{6,10},{7,11},{8,4},{9,5},{10,... | collective-permute-start | bytes 294920 | tf_op jit(solution)/shard_map/ppermute | solution.py:395
  65.4 1.1 %collective-permute-start.22 = (f32[32,768]{1,0:T(8,128)S(1)}, f32[32,768]{1,0:T(8,128)S(1)}, u32[]{:S(2)}, u32[]{:S(2)}) collective-permute-start(f32[32,768]{1,0:T(8,128)S(1)} %shard_map.234.refs_5_), channel_id=1, source_target_pairs={{0,2},{1,3},{2,0},{3,1},{4,10},{5,11},{6,8},{7,9},{8,6},{9,7},{10,... | collective-permute-start | bytes 294920 | tf_op jit(solution)/shard_map/ppermute | solution.py:395
  66.5 3.6 %collective-permute-done.24.refs_0_ = f32[32,768]{1,0:T(8,128)S(1)} collective-permute-done((f32[32,768]{1,0:T(8,128)S(1)}, f32[32,768]{1,0:T(8,128)S(1)}, u32[]{:S(2)}, u32[]{:S(2)}) %collective-permute-start.24) | collective-permute-done | bytes 98336 | tf_op jit(solution)/shard_map/ppermute | solution.py:395
  70.1 1.7 %collective-permute-done.22.refs_0_ = f32[32,768]{1,0:T(8,128)S(1)} collective-permute-done((f32[32,768]{1,0:T(8,128)S(1)}, f32[32,768]{1,0:T(8,128)S(1)}, u32[]{:S(2)}, u32[]{:S(2)}) %collective-permute-start.22) | collective-permute-done | bytes 98336 | tf_op jit(solution)/shard_map/ppermute | solution.py:395
  71.7 3.9 %collective-permute-start.26 = (f32[32,768]{1,0:T(8,128)S(1)}, f32[32,768]{1,0:T(8,128)S(1)}, u32[]{:S(2)}, u32[]{:S(2)}) collective-permute-start(f32[32,768]{1,0:T(8,128)S(1)} %shard_map.236.refs_0_.refs_5_), channel_id=1, source_target_pairs={{0,4},{1,5},{2,6},{3,7},{4,0},{5,1},{6,2},{7,3},{8,12},{9,13},{10,... | collective-permute-start | bytes 294920 | tf_op jit(solution)/shard_map/ppermute | solution.py:395
  76.2 1.0 %shard_map.237.refs_3_ = f32[32,1024]{1,0:T(8,128)S(1)} custom-call(f32[32,768]{1,0:T(8,128)S(1)} %shard_map.236.refs_0_.refs_5_, f32[512,1536]{1,0:T(8,128)S(1)} %bitcast.60, f32[512,1536]{1,0:T(8,128)S(1)} %collective-permute-done.20.refs_2_), custom_call_target="tpu_custom_call" | custom-call | bytes 4194304 | tf_op jit(solution)/shard_map/pallas_call | solution.py:98
  77.2 1.3 %collective-permute-done.26.refs_0_ = f32[32,768]{1,0:T(8,128)S(1)} collective-permute-done((f32[32,768]{1,0:T(8,128)S(1)}, f32[32,768]{1,0:T(8,128)S(1)}, u32[]{:S(2)}, u32[]{:S(2)}) %collective-permute-start.26) | collective-permute-done | bytes 98336 | tf_op jit(solution)/shard_map/ppermute | solution.py:395
  78.5 1.2 %collective-permute-start.29 = (f32[32,768]{1,0:T(8,128)S(1)}, f32[32,768]{1,0:T(8,128)S(1)}, u32[]{:S(2)}, u32[]{:S(2)}) collective-permute-start(f32[32,768]{1,0:T(8,128)S(1)} %shard_map.236.refs_0_.refs_5_), channel_id=1, source_target_pairs={{0,2},{1,3},{2,0},{3,1},{4,8},{5,9},{6,10},{7,11},{8,4},{9,5},{10,... | collective-permute-start | bytes 294920 | tf_op jit(solution)/shard_map/ppermute | solution.py:395
  79.7 0.9 collective-permute-start.30
  81.4 0.9 shard_map.239.refs_0_
  82.2 1.2 %collective-permute-start.32 = (f32[32,768]{1,0:T(8,128)S(1)}, f32[32,768]{1,0:T(8,128)S(1)}, u32[]{:S(2)}, u32[]{:S(2)}) collective-permute-start(f32[32,768]{1,0:T(8,128)S(1)} %shard_map.239.refs_0_), channel_id=1, source_target_pairs={{0,2},{1,3},{2,0},{3,1},{4,6},{5,7},{6,4},{7,5},{8,10},{9,11},{10,... | collective-permute-start | bytes 294920 | tf_op jit(solution)/shard_map/ppermute | solution.py:395
  83.5 1.0 %collective-permute-start.31 = (f32[32,768]{1,0:T(8,128)S(1)}, f32[32,768]{1,0:T(8,128)S(1)}, u32[]{:S(2)}, u32[]{:S(2)}) collective-permute-start(f32[32,768]{1,0:T(8,128)S(1)} %shard_map.239.refs_0_), channel_id=1, source_target_pairs={{0,4},{1,5},{2,6},{3,7},{4,0},{5,1},{6,2},{7,3},{8,12},{9,13},{10,... | collective-permute-start | bytes 294920 | tf_op jit(solution)/shard_map/ppermute | solution.py:395
  84.5 1.6 %collective-permute-start.27 = (f32[32,768]{1,0:T(8,128)S(1)}, f32[32,768]{1,0:T(8,128)S(1)}, u32[]{:S(2)}, u32[]{:S(2)}) collective-permute-start(f32[32,768]{1,0:T(8,128)S(1)} %shard_map.239.refs_0_), channel_id=1, source_target_pairs={{0,6},{1,7},{2,4},{3,5},{4,2},{5,3},{6,0},{7,1},{8,14},{9,15},{10,... | collective-permute-start | bytes 294920 | tf_op jit(solution)/shard_map/ppermute | solution.py:395
  86.1 1.0 %collective-permute-done.30.refs_3_ = f32[32,768]{1,0:T(8,128)S(1)} collective-permute-done((f32[32,768]{1,0:T(8,128)S(1)}, f32[32,768]{1,0:T(8,128)S(1)}, u32[]{:S(2)}, u32[]{:S(2)}) %collective-permute-start.30) | collective-permute-done | bytes 98336 | tf_op jit(solution)/shard_map/ppermute | solution.py:395
  87.2 1.0 %shard_map.240.refs_3_ = f32[32,1024]{1,0:T(8,128)S(1)} custom-call(f32[32,768]{1,0:T(8,128)S(1)} %shard_map.239.refs_0_, f32[512,1536]{1,0:T(8,128)S(1)} %bitcast.61, f32[512,1536]{1,0:T(8,128)S(1)} %collective-permute-done.20.refs_2_, f32[32,1024]{1,0:T(8,128)S(1)} %shard_map.237.refs_3_), custom_call_target="tpu_custom_call" | custom-call | bytes 4194304 | tf_op jit(solution)/shard_map/pallas_call | solution.py:98
  88.2 1.1 %shard_map.241.refs_4_ = f32[32,1024]{1,0:T(8,128)S(1)} custom-call(f32[32,768]{1,0:T(8,128)S(1)} %collective-permute-done.32.refs_0_, f32[512,1536]{1,0:T(8,128)S(1)} %bitcast.62, f32[512,1536]{1,0:T(8,128)S(1)} %collective-permute-done.20.refs_2_, f32[32,1024]{1,0:T(8,128)S(1)} %shard_map.240.refs_3_), custom_call_target="tpu_custom_call" | custom-call | bytes 4194304 | tf_op jit(solution)/shard_map/pallas_call | solution.py:98
  90.1 1.2 %collective-permute-start.33 = (f32[32,1024]{1,0:T(8,128)S(1)}, f32[32,1024]{1,0:T(8,128)S(1)}, u32[]{:S(2)}, u32[]{:S(2)}) collective-permute-start(f32[32,1024]{1,0:T(8,128)S(1)} %shard_map.243.refs_0_), channel_id=1, source_target_pairs={{0,2},{1,3},{2,0},{3,1},{4,6},{5,7},{6,4},{7,5},{8,10},{9,11},{10,... | collective-permute-start | bytes 393224 | tf_op jit(solution)/shard_map/ppermute | solution.py:395
  91.4 1.2 %collective-permute-done.34.refs_1_ = f32[32,384]{1,0:T(8,128)S(1)} collective-permute-done((f32[32,384]{1,0:T(8,128)S(1)}, f32[32,384]{1,0:T(8,128)S(1)}, u32[]{:S(2)}, u32[]{:S(2)}) %collective-permute-start.34) | collective-permute-done | bytes 49184 | tf_op jit(solution)/shard_map/ppermute | solution.py:395
  93.3 1.4 %shard_map.246.refs_3_ = f32[32,1024]{1,0:T(8,128)S(1)} custom-call(f32[32,1024]{1,0:T(8,128)S(1)} %shard_map.243.refs_0_, f32[512,2048]{1,0:T(8,128)S(1)} %bitcast.65, f32[512,2048]{1,0:T(8,128)S(1)} %collective-permute-done.28.refs_2_), custom_call_target="tpu_custom_call" | custom-call | bytes 4194304 | tf_op jit(solution)/shard_map/pallas_call | solution.py:98
  95.1 1.4 %shard_map.247 = (f32[32,512]{1,0:T(8,128)S(1)}, f32[32,512]{1,0:T(8,128)S(1)}) custom-call(f32[32,1024]{1,0:T(8,128)S(1)} %collective-permute-done.33.refs_0_, f32[512,2048]{1,0:T(8,128)S(1)} %bitcast.66, f32[512,2048]{1,0:T(8,128)S(1)} %collective-permute-done.28.refs_2_, f32[32,1024]{1,0:T(8,128)S(1)} %shard_map.246.refs_3_), custom_call_target="tpu_custom_call" | custom-call | tf_op jit(solution)/shard_map/pallas_call | solution.py:98
  96.5 1.2 %collective-permute-done.35.refs_1_ = f32[32,512]{1,0:T(8,128)S(1)} collective-permute-done((f32[32,512]{1,0:T(8,128)S(1)}, f32[32,512]{1,0:T(8,128)S(1)}, u32[]{:S(2)}, u32[]{:S(2)}) %collective-permute-start.35) | collective-permute-done | bytes 65568 | tf_op jit(solution)/shard_map/ppermute | solution.py:395
  (80 shorter events, 9.6 us)
Async XLA Ops:
  2.0 6.5 %collective-permute-start = (f32[64,512]{1,0:T(8,128)S(1)}, f32[64,512]{1,0:T(8,128)S(1)}, u32[]{:S(2)}, u32[]{:S(2)}) collective-permute-start(f32[64,512]{1,0:T(8,128)S(1)} %get-tuple-element.69.refs_0_), channel_id=1, source_target_pairs={{0,2},{1,3},{2,0},{3,1},{4,6},{5,7},{6,4},{7,5},{8,10},{9,11},{10,... | collective-permute-start | bytes 393224 | tf_op jit(solution)/shard_map/ppermute | solution.py:395
  5.0 3.8 %collective-permute-start.2 = (f32[64,512]{1,0:T(8,128)S(1)}, f32[64,512]{1,0:T(8,128)S(1)}, u32[]{:S(2)}, u32[]{:S(2)}) collective-permute-start(f32[64,512]{1,0:T(8,128)S(1)} %get-tuple-element.69.refs_0_), channel_id=1, source_target_pairs={{0,1},{1,0},{2,3},{3,2},{4,5},{5,4},{6,7},{7,6},{8,9},{9,8},{10,11... | collective-permute-start | bytes 393224 | tf_op jit(solution)/shard_map/ppermute | solution.py:395
  8.5 1.4 %collective-permute-start.1 = (f32[64,512]{1,0:T(8,128)S(1)}, f32[64,512]{1,0:T(8,128)S(1)}, u32[]{:S(2)}, u32[]{:S(2)}) collective-permute-start(f32[64,512]{1,0:T(8,128)S(1)} %collective-permute-done.refs_2_), channel_id=1, source_target_pairs={{0,1},{1,0},{2,3},{3,2},{4,5},{5,4},{6,7},{7,6},{8,9},{9,8},{10,11... | collective-permute-start | bytes 393224 | tf_op jit(solution)/shard_map/ppermute | solution.py:395
  9.9 12.2 %copy-start = (f32[1,384,1536]{2,1,0:T(8,128)S(1)}, f32[1,384,1536]{2,1,0:T(8,128)}, u32[]{:S(2)}) copy-start(f32[1,384,1536]{2,1,0:T(8,128)} %param.33) | copy-start | bytes 7077892
  9.9 15.8 %copy-start.5 = (f32[1,384,1536]{2,1,0:T(8,128)S(1)}, f32[1,384,1536]{2,1,0:T(8,128)}, u32[]{:S(2)}) copy-start(f32[1,384,1536]{2,1,0:T(8,128)} %param.34) | copy-start | bytes 7077892
  13.3 1.8 %collective-permute-start.3 = (f32[2,32,1536]{2,1,0:T(8,128)S(1)}, f32[2,32,1536]{2,1,0:T(8,128)S(1)}, u32[]{:S(2)}, u32[]{:S(2)}) collective-permute-start(f32[2,32,1536]{2,1,0:T(8,128)S(1)} %get-tuple-element.67), channel_id=1, source_target_pairs={{0,1},{1,0},{2,3},{3,2},{4,5},{5,4},{6,7},{7,6},{8,9},{9,8},{10,11... | collective-permute-start | bytes 1179656 | tf_op jit(solution)/shard_map/ppermute | solution.py:395
  15.1 7.3 %collective-permute-start.6 = (f32[32,768]{1,0:T(8,128)S(1)}, f32[32,768]{1,0:T(8,128)S(1)}, u32[]{:S(2)}, u32[]{:S(2)}) collective-permute-start(f32[32,768]{1,0:T(8,128)S(1)} %get-tuple-element.78), channel_id=1, source_target_pairs={{4,0},{5,1},{6,2},{7,3},{8,4},{9,5},{10,6},{11,7},{12,8},{13,9},{1... | collective-permute-start | bytes 294920 | tf_op jit(solution)/shard_map/ppermute | solution.py:441
  16.4 6.1 %collective-permute-start.7 = (f32[32,768]{1,0:T(8,128)S(1)}, f32[32,768]{1,0:T(8,128)S(1)}, u32[]{:S(2)}, u32[]{:S(2)}) collective-permute-start(f32[32,768]{1,0:T(8,128)S(1)} %get-tuple-element.79), channel_id=1, source_target_pairs={{0,2},{1,3},{2,0},{3,1},{4,6},{5,7},{6,4},{7,5},{8,10},{9,11},{10,... | collective-permute-start | bytes 294920 | tf_op jit(solution)/shard_map/ppermute | solution.py:395
  18.1 7.6 %collective-permute-start.8 = (f32[32,768]{1,0:T(8,128)S(1)}, f32[32,768]{1,0:T(8,128)S(1)}, u32[]{:S(2)}, u32[]{:S(2)}) collective-permute-start(f32[32,768]{1,0:T(8,128)S(1)} %get-tuple-element.80), channel_id=1, source_target_pairs={{4,2},{5,3},{6,0},{7,1},{8,6},{9,7},{10,4},{11,5},{12,10},{13,11},... | collective-permute-start | bytes 294920 | tf_op jit(solution)/shard_map/ppermute | solution.py:441
  19.4 3.0 %collective-permute-start.5 = (f32[32,512]{1,0:T(8,128)S(1)}, f32[32,512]{1,0:T(8,128)S(1)}, u32[]{:S(2)}, u32[]{:S(2)}) collective-permute-start(f32[32,512]{1,0:T(8,128)S(1)} %get-tuple-element.74), channel_id=1, source_target_pairs={{0,1},{1,0},{2,3},{3,2},{4,5},{5,4},{6,7},{7,6},{8,9},{9,8},{10,11... | collective-permute-start | bytes 196616 | tf_op jit(solution)/shard_map/ppermute | solution.py:395
  20.7 1.4 %collective-permute-start.4 = (f32[32,384]{1,0:T(8,128)S(1)}, f32[32,384]{1,0:T(8,128)S(1)}, u32[]{:S(2)}, u32[]{:S(2)}) collective-permute-start(f32[32,384]{1,0:T(8,128)S(1)} %get-tuple-element.73), channel_id=1, source_target_pairs={{0,1},{1,0},{2,3},{3,2},{4,5},{5,4},{6,7},{7,6},{8,9},{9,8},{10,11... | collective-permute-start | bytes 147464 | tf_op jit(solution)/shard_map/ppermute | solution.py:395
  22.1 9.9 %collective-permute-start.10 = (f32[384,1536]{1,0:T(8,128)S(1)}, f32[384,1536]{1,0:T(8,128)S(1)}, u32[]{:S(2)}, u32[]{:S(2)}) collective-permute-start(f32[384,1536]{1,0:T(8,128)S(1)} %bitcast.44), channel_id=1, source_target_pairs={{0,1},{1,0},{2,3},{3,2},{4,5},{5,4},{6,7},{7,6},{8,9},{9,8},{10,11... | collective-permute-start | bytes 7077896 | tf_op jit(solution)/shard_map/ppermute | solution.py:395
  25.7 8.4 %collective-permute-start.13 = (f32[384,1536]{1,0:T(8,128)S(1)}, f32[384,1536]{1,0:T(8,128)S(1)}, u32[]{:S(2)}, u32[]{:S(2)}) collective-permute-start(f32[384,1536]{1,0:T(8,128)S(1)} %bitcast.71), channel_id=1, source_target_pairs={{0,1},{1,0},{2,3},{3,2},{4,5},{5,4},{6,7},{7,6},{8,9},{9,8},{10,11... | collective-permute-start | bytes 7077896 | tf_op jit(solution)/shard_map/ppermute | solution.py:395
  25.8 6.2 %collective-permute-start.11 = (f32[32,768]{1,0:T(8,128)S(1)}, f32[32,768]{1,0:T(8,128)S(1)}, u32[]{:S(2)}, u32[]{:S(2)}) collective-permute-start(f32[32,768]{1,0:T(8,128)S(1)} %shard_map.224.refs_4_.refs_5_), channel_id=1, source_target_pairs={{0,4},{1,5},{2,6},{3,7},{4,0},{5,1},{6,2},{7,3},{8,12},{9,13},{10,... | collective-permute-start | bytes 294920 | tf_op jit(solution)/shard_map/ppermute | solution.py:395
  28.4 5.8 %collective-permute-start.9 = (f32[32,768]{1,0:T(8,128)S(1)}, f32[32,768]{1,0:T(8,128)S(1)}, u32[]{:S(2)}, u32[]{:S(2)}) collective-permute-start(f32[32,768]{1,0:T(8,128)S(1)} %shard_map.224.refs_4_.refs_5_), channel_id=1, source_target_pairs={{0,6},{1,7},{2,4},{3,5},{4,2},{5,3},{6,0},{7,1},{8,14},{9,15},{10,... | collective-permute-start | bytes 294920 | tf_op jit(solution)/shard_map/ppermute | solution.py:395
  32.0 2.1 %copy-start.1 = (f32[1,384,1536]{2,1,0:T(8,128)S(1)}, f32[1,384,1536]{2,1,0:T(8,128)}, u32[]{:S(2)}) copy-start(f32[1,384,1536]{2,1,0:T(8,128)} %param.35) | copy-start | bytes 7077892
  34.1 7.4 %collective-permute-start.16 = (f32[384,1536]{1,0:T(8,128)S(1)}, f32[384,1536]{1,0:T(8,128)S(1)}, u32[]{:S(2)}, u32[]{:S(2)}) collective-permute-start(f32[384,1536]{1,0:T(8,128)S(1)} %bitcast.51), channel_id=1, source_target_pairs={{0,1},{1,0},{2,3},{3,2},{4,5},{5,4},{6,7},{7,6},{8,9},{9,8},{10,11... | collective-permute-start | bytes 7077896 | tf_op jit(solution)/shard_map/ppermute | solution.py:395
  34.2 5.7 %collective-permute-start.14 = (f32[32,768]{1,0:T(8,128)S(1)}, f32[32,768]{1,0:T(8,128)S(1)}, u32[]{:S(2)}, u32[]{:S(2)}) collective-permute-start(f32[32,768]{1,0:T(8,128)S(1)} %shard_map.226.refs_5_), channel_id=1, source_target_pairs={{0,2},{1,3},{2,0},{3,1},{4,8},{5,9},{6,10},{7,11},{8,4},{9,5},{10,... | collective-permute-start | bytes 294920 | tf_op jit(solution)/shard_map/ppermute | solution.py:395
  35.5 6.1 %collective-permute-start.12 = (f32[32,768]{1,0:T(8,128)S(1)}, f32[32,768]{1,0:T(8,128)S(1)}, u32[]{:S(2)}, u32[]{:S(2)}) collective-permute-start(f32[32,768]{1,0:T(8,128)S(1)} %shard_map.226.refs_5_), channel_id=1, source_target_pairs={{0,2},{1,3},{2,0},{3,1},{4,10},{5,11},{6,8},{7,9},{8,6},{9,7},{10,... | collective-permute-start | bytes 294920 | tf_op jit(solution)/shard_map/ppermute | solution.py:395
  39.9 1.9 %copy-start.2 = (f32[1,512,1536]{2,1,0:T(8,128)S(1)}, f32[1,512,1536]{2,1,0:T(8,128)}, u32[]{:S(2)}) copy-start(f32[1,512,1536]{2,1,0:T(8,128)} %param.32) | copy-start | bytes 9437188
  41.8 14.5 %collective-permute-start.20 = (f32[512,1536]{1,0:T(8,128)S(1)}, f32[512,1536]{1,0:T(8,128)S(1)}, u32[]{:S(2)}, u32[]{:S(2)}) collective-permute-start(f32[512,1536]{1,0:T(8,128)S(1)} %bitcast.59), channel_id=1, source_target_pairs={{0,1},{1,0},{2,3},{3,2},{4,5},{5,4},{6,7},{7,6},{8,9},{9,8},{10,11... | collective-permute-start | bytes 9437192 | tf_op jit(solution)/shard_map/ppermute | solution.py:395
  41.8 6.8 %collective-permute-start.17 = (f32[32,768]{1,0:T(8,128)S(1)}, f32[32,768]{1,0:T(8,128)S(1)}, u32[]{:S(2)}, u32[]{:S(2)}) collective-permute-start(f32[32,768]{1,0:T(8,128)S(1)} %shard_map.228.refs_5_), channel_id=1, source_target_pairs={{0,4},{1,5},{2,6},{3,7},{4,0},{5,1},{6,2},{7,3},{8,12},{9,13},{10,... | collective-permute-start | bytes 294920 | tf_op jit(solution)/shard_map/ppermute | solution.py:395
  44.9 5.8 %collective-permute-start.15 = (f32[32,768]{1,0:T(8,128)S(1)}, f32[32,768]{1,0:T(8,128)S(1)}, u32[]{:S(2)}, u32[]{:S(2)}) collective-permute-start(f32[32,768]{1,0:T(8,128)S(1)} %shard_map.228.refs_5_), channel_id=1, source_target_pairs={{0,6},{1,7},{2,4},{3,5},{4,2},{5,3},{6,0},{7,1},{8,14},{9,15},{10,... | collective-permute-start | bytes 294920 | tf_op jit(solution)/shard_map/ppermute | solution.py:395
  50.7 4.7 %collective-permute-start.18 = (f32[32,768]{1,0:T(8,128)S(1)}, f32[32,768]{1,0:T(8,128)S(1)}, u32[]{:S(2)}, u32[]{:S(2)}) collective-permute-start(f32[32,768]{1,0:T(8,128)S(1)} %shard_map.230.refs_0_), channel_id=1, source_target_pairs={{0,2},{1,3},{2,0},{3,1},{4,6},{5,7},{6,4},{7,5},{8,10},{9,11},{10,... | collective-permute-start | bytes 294920 | tf_op jit(solution)/shard_map/ppermute | solution.py:395
  52.8 3.5 %copy-start.4 = (f32[1,512,1536]{2,1,0:T(8,128)S(1)}, f32[1,512,1536]{2,1,0:T(8,128)}, u32[]{:S(2)}) copy-start(f32[1,512,1536]{2,1,0:T(8,128)} %param.31) | copy-start | bytes 9437188
  56.3 8.0 %collective-permute-start.23 = (f32[512,1536]{1,0:T(8,128)S(1)}, f32[512,1536]{1,0:T(8,128)S(1)}, u32[]{:S(2)}, u32[]{:S(2)}) collective-permute-start(f32[512,1536]{1,0:T(8,128)S(1)} %bitcast.68), channel_id=1, source_target_pairs={{0,1},{1,0},{2,3},{3,2},{4,5},{5,4},{6,7},{7,6},{8,9},{9,8},{10,11... | collective-permute-start | bytes 9437192 | tf_op jit(solution)/shard_map/ppermute | solution.py:395
  56.3 5.2 %collective-permute-start.21 = (f32[32,768]{1,0:T(8,128)S(1)}, f32[32,768]{1,0:T(8,128)S(1)}, u32[]{:S(2)}, u32[]{:S(2)}) collective-permute-start(f32[32,768]{1,0:T(8,128)S(1)} %shard_map.232.refs_4_.refs_5_), channel_id=1, source_target_pairs={{0,4},{1,5},{2,6},{3,7},{4,0},{5,1},{6,2},{7,3},{8,12},{9,13},{10,... | collective-permute-start | bytes 294920 | tf_op jit(solution)/shard_map/ppermute | solution.py:395
  58.0 6.3 %collective-permute-start.19 = (f32[32,768]{1,0:T(8,128)S(1)}, f32[32,768]{1,0:T(8,128)S(1)}, u32[]{:S(2)}, u32[]{:S(2)}) collective-permute-start(f32[32,768]{1,0:T(8,128)S(1)} %shard_map.232.refs_4_.refs_5_), channel_id=1, source_target_pairs={{0,6},{1,7},{2,4},{3,5},{4,2},{5,3},{6,0},{7,1},{8,14},{9,15},{10,... | collective-permute-start | bytes 294920 | tf_op jit(solution)/shard_map/ppermute | solution.py:395
  61.6 2.8 %copy-start.3 = (f32[1,512,2048]{2,1,0:T(8,128)S(1)}, f32[1,512,2048]{2,1,0:T(8,128)}, u32[]{:S(2)}) copy-start(f32[1,512,2048]{2,1,0:T(8,128)} %param.30) | copy-start | bytes 12582916
  64.3 25.7 %collective-permute-start.28 = (f32[512,2048]{1,0:T(8,128)S(1)}, f32[512,2048]{1,0:T(8,128)S(1)}, u32[]{:S(2)}, u32[]{:S(2)}) collective-permute-start(f32[512,2048]{1,0:T(8,128)S(1)} %bitcast.64), channel_id=1, source_target_pairs={{0,1},{1,0},{2,3},{3,2},{4,5},{5,4},{6,7},{7,6},{8,9},{9,8},{10,11... | collective-permute-start | bytes 12582920 | tf_op jit(solution)/shard_map/ppermute | solution.py:395
  64.4 5.7 %collective-permute-start.24 = (f32[32,768]{1,0:T(8,128)S(1)}, f32[32,768]{1,0:T(8,128)S(1)}, u32[]{:S(2)}, u32[]{:S(2)}) collective-permute-start(f32[32,768]{1,0:T(8,128)S(1)} %shard_map.234.refs_5_), channel_id=1, source_target_pairs={{0,2},{1,3},{2,0},{3,1},{4,8},{5,9},{6,10},{7,11},{8,4},{9,5},{10,... | collective-permute-start | bytes 294920 | tf_op jit(solution)/shard_map/ppermute | solution.py:395
  65.4 6.3 %collective-permute-start.22 = (f32[32,768]{1,0:T(8,128)S(1)}, f32[32,768]{1,0:T(8,128)S(1)}, u32[]{:S(2)}, u32[]{:S(2)}) collective-permute-start(f32[32,768]{1,0:T(8,128)S(1)} %shard_map.234.refs_5_), channel_id=1, source_target_pairs={{0,2},{1,3},{2,0},{3,1},{4,10},{5,11},{6,8},{7,9},{8,6},{9,7},{10,... | collective-permute-start | bytes 294920 | tf_op jit(solution)/shard_map/ppermute | solution.py:395
  71.7 6.8 %collective-permute-start.26 = (f32[32,768]{1,0:T(8,128)S(1)}, f32[32,768]{1,0:T(8,128)S(1)}, u32[]{:S(2)}, u32[]{:S(2)}) collective-permute-start(f32[32,768]{1,0:T(8,128)S(1)} %shard_map.236.refs_0_.refs_5_), channel_id=1, source_target_pairs={{0,4},{1,5},{2,6},{3,7},{4,0},{5,1},{6,2},{7,3},{8,12},{9,13},{10,... | collective-permute-start | bytes 294920 | tf_op jit(solution)/shard_map/ppermute | solution.py:395
  75.7 5.7 %collective-permute-start.25 = (f32[32,768]{1,0:T(8,128)S(1)}, f32[32,768]{1,0:T(8,128)S(1)}, u32[]{:S(2)}, u32[]{:S(2)}) collective-permute-start(f32[32,768]{1,0:T(8,128)S(1)} %shard_map.236.refs_0_.refs_5_), channel_id=1, source_target_pairs={{0,6},{1,7},{2,4},{3,5},{4,2},{5,3},{6,0},{7,1},{8,14},{9,15},{10,... | collective-permute-start | bytes 294920 | tf_op jit(solution)/shard_map/ppermute | solution.py:395
  78.5 6.0 %collective-permute-start.29 = (f32[32,768]{1,0:T(8,128)S(1)}, f32[32,768]{1,0:T(8,128)S(1)}, u32[]{:S(2)}, u32[]{:S(2)}) collective-permute-start(f32[32,768]{1,0:T(8,128)S(1)} %shard_map.236.refs_0_.refs_5_), channel_id=1, source_target_pairs={{0,2},{1,3},{2,0},{3,1},{4,8},{5,9},{6,10},{7,11},{8,4},{9,5},{10,... | collective-permute-start | bytes 294920 | tf_op jit(solution)/shard_map/ppermute | solution.py:395
  79.7 7.5 %collective-permute-start.30 = (f32[32,768]{1,0:T(8,128)S(1)}, f32[32,768]{1,0:T(8,128)S(1)}, u32[]{:S(2)}, u32[]{:S(2)}) collective-permute-start(f32[32,768]{1,0:T(8,128)S(1)} %shard_map.236.refs_0_.refs_5_), channel_id=1, source_target_pairs={{0,2},{1,3},{2,0},{3,1},{4,10},{5,11},{6,8},{7,9},{8,6},{9,7},{10,... | collective-permute-start | bytes 294920 | tf_op jit(solution)/shard_map/ppermute | solution.py:395
  82.2 6.0 %collective-permute-start.32 = (f32[32,768]{1,0:T(8,128)S(1)}, f32[32,768]{1,0:T(8,128)S(1)}, u32[]{:S(2)}, u32[]{:S(2)}) collective-permute-start(f32[32,768]{1,0:T(8,128)S(1)} %shard_map.239.refs_0_), channel_id=1, source_target_pairs={{0,2},{1,3},{2,0},{3,1},{4,6},{5,7},{6,4},{7,5},{8,10},{9,11},{10,... | collective-permute-start | bytes 294920 | tf_op jit(solution)/shard_map/ppermute | solution.py:395
  83.5 5.8 %collective-permute-start.31 = (f32[32,768]{1,0:T(8,128)S(1)}, f32[32,768]{1,0:T(8,128)S(1)}, u32[]{:S(2)}, u32[]{:S(2)}) collective-permute-start(f32[32,768]{1,0:T(8,128)S(1)} %shard_map.239.refs_0_), channel_id=1, source_target_pairs={{0,4},{1,5},{2,6},{3,7},{4,0},{5,1},{6,2},{7,3},{8,12},{9,13},{10,... | collective-permute-start | bytes 294920 | tf_op jit(solution)/shard_map/ppermute | solution.py:395
  84.5 5.5 %collective-permute-start.27 = (f32[32,768]{1,0:T(8,128)S(1)}, f32[32,768]{1,0:T(8,128)S(1)}, u32[]{:S(2)}, u32[]{:S(2)}) collective-permute-start(f32[32,768]{1,0:T(8,128)S(1)} %shard_map.239.refs_0_), channel_id=1, source_target_pairs={{0,6},{1,7},{2,4},{3,5},{4,2},{5,3},{6,0},{7,1},{8,14},{9,15},{10,... | collective-permute-start | bytes 294920 | tf_op jit(solution)/shard_map/ppermute | solution.py:395
  90.0 2.6 %copy-start.9 = (f32[1,384,64]{1,2,0:T(8,128)S(1)}, f32[1,384,64]{1,2,0:T(8,128)}, u32[]{:S(2)}) copy-start(f32[1,384,64]{1,2,0:T(8,128)} %param.27) | copy-start | bytes 294916
  90.0 2.6 %copy-start.10 = (f32[1,384,64]{1,2,0:T(8,128)S(1)}, f32[1,384,64]{1,2,0:T(8,128)}, u32[]{:S(2)}) copy-start(f32[1,384,64]{1,2,0:T(8,128)} %param.28) | copy-start | bytes 294916
  90.0 2.6 %copy-start.11 = (f32[1,384,64]{1,2,0:T(8,128)S(1)}, f32[1,384,64]{1,2,0:T(8,128)}, u32[]{:S(2)}) copy-start(f32[1,384,64]{1,2,0:T(8,128)} %param.29) | copy-start | bytes 294916
  90.1 5.0 %collective-permute-start.33 = (f32[32,1024]{1,0:T(8,128)S(1)}, f32[32,1024]{1,0:T(8,128)S(1)}, u32[]{:S(2)}, u32[]{:S(2)}) collective-permute-start(f32[32,1024]{1,0:T(8,128)S(1)} %shard_map.243.refs_0_), channel_id=1, source_target_pairs={{0,2},{1,3},{2,0},{3,1},{4,6},{5,7},{6,4},{7,5},{8,10},{9,11},{10,... | collective-permute-start | bytes 393224 | tf_op jit(solution)/shard_map/ppermute | solution.py:395
  91.3 1.3 %collective-permute-start.34 = (f32[32,384]{1,0:T(8,128)S(1)}, f32[32,384]{1,0:T(8,128)S(1)}, u32[]{:S(2)}, u32[]{:S(2)}) collective-permute-start(f32[32,384]{1,0:T(8,128)S(1)} %get-tuple-element.102), channel_id=1, source_target_pairs={{0,1},{1,0},{2,3},{3,2},{4,5},{5,4},{6,7},{7,6},{8,9},{9,8},{10,11... | collective-permute-start | bytes 147464 | tf_op jit(solution)/shard_map/ppermute | solution.py:395
  95.1 2.7 %copy-start.6 = (f32[1,512,64]{1,2,0:T(8,128)S(1)}, f32[1,512,64]{1,2,0:T(8,128)}, u32[]{:S(2)}) copy-start(f32[1,512,64]{1,2,0:T(8,128)} %param.24) | copy-start | bytes 393220
  95.1 2.7 %copy-start.7 = (f32[1,512,64]{1,2,0:T(8,128)S(1)}, f32[1,512,64]{1,2,0:T(8,128)}, u32[]{:S(2)}) copy-start(f32[1,512,64]{1,2,0:T(8,128)} %param.25) | copy-start | bytes 393220
  95.1 2.7 %copy-start.8 = (f32[1,512,64]{1,2,0:T(8,128)S(1)}, f32[1,512,64]{1,2,0:T(8,128)}, u32[]{:S(2)}) copy-start(f32[1,512,64]{1,2,0:T(8,128)} %param.26) | copy-start | bytes 393220
  96.5 1.3 %collective-permute-start.35 = (f32[32,512]{1,0:T(8,128)S(1)}, f32[32,512]{1,0:T(8,128)S(1)}, u32[]{:S(2)}, u32[]{:S(2)}) collective-permute-start(f32[32,512]{1,0:T(8,128)S(1)} %get-tuple-element.109), channel_id=1, source_target_pairs={{0,1},{1,0},{2,3},{3,2},{4,5},{5,4},{6,7},{7,6},{8,9},{9,8},{10,11... | collective-permute-start | bytes 196616 | tf_op jit(solution)/shard_map/ppermute | solution.py:395

commit v14 on v13

--- a/solution.py
+++ b/solution.py
@@ -157,19 +157,18 @@
     out[...] = total
 
 
-def forces_kernel(place, pieces, matrices, sofar, mine, theirs, copy, below):
+def forces_kernel(place, pieces, matrices, sofar, mine, theirs):
     (rows,) = matrices
     faces = mine.shape[2]
-    inner = rows.shape[1] - faces
-    above = rows.at[:, inner:]
+    inner = rows.shape[1] - 2 * faces
+    above = rows.at[:, inner : inner + faces]
+    below = rows.at[:, inner + faces :]
     value = pieces[0][...]
     columns = slice(0, inner) if place is None else load_columns(*place, value.shape[1])
     part = plus(times_rows(value, rows, columns=columns), sofar)
     half = part.shape[0] // 2
     second = lax.axis_index("blk") == 1
     for i, matrix in enumerate((above, below)):
-        if i == 1:
-            copy.wait()
         force = times(part, matrix)
         mine[i] = jnp.where(second, force[half:], force[:half])
         theirs[i] = jnp.where(second, force[:half], force[half:])
@@ -487,7 +486,9 @@
 
     lower_other = mv.core(lower[0])
     across = [mv.chip(load_int, j) for j in range(1, mv.chips)]
-    phase_rows = staged(interior_inverse[0], couple_above[0], after=[load_int])
+    phase_rows = staged(
+        interior_inverse[0], couple_above[0], couple_below[0], after=[load_int]
+    )
     phase_rows, *across = lax.optimization_barrier([phase_rows, *across])
     beside = [mv.core(piece) for piece in [load_int] + across]
     pieces = [piece for pair in zip([load_int] + across, beside) for piece in pair]
@@ -509,7 +510,6 @@
         pieces,
         [phase_rows],
         sofar,
-        late=couple_below[0],
     )
     chunks = call(
         chunks_kernel,

time: 98.9 us -> 97.5 us (0.986)
  starting transfers between devices: 34.9 us -> 33.4 us
    pallas_call x29, Pallas kernels: 15.4 us -> 13.6 us  [call(): pl.pallas_call(body, in_specs=[VMEM] * len(flat) + [pl.BlockSpec(memory_s...]
    ppermute x34, starting transfers between devices: 32.3 us -> 30.9 us  [permute(): return lax.ppermute(value, AXES, pairs)]
  transfers between devices with their start and end apart: 36 -> 36, of which waited for: 21 -> 21; matrix products, arithmetic and copies ran while one was open for 0% -> 0% of each run, Pallas kernels for 14% -> 15%
where the time goes in v14:
time: 97.5 us; the launch traced here: 97.2 us
  waiting for transfers between devices  42.1 us (43%)
  starting transfers between devices  33.4 us (34%)
  Pallas kernels  20.2 us (21%)
    ppermute x34, waiting for transfers between devices, permute(): return lax.ppermute(value, AXES, pairs)  38.6 us
    ppermute x34, starting transfers between devices, permute(): return lax.ppermute(value, AXES, pairs)  30.9 us
    pallas_call x29, Pallas kernels, call(): pl.pallas_call(body, in_specs=[VMEM] * len(flat) + [pl.BlockSpec(memory_s...  13.6 us
    pallas_call x1, Pallas kernels, staged(): pl.pallas_call(body, in_specs=[pl.BlockSpec(memory_space=pltpu.HBM)] * co...  4.08 us
    ppermute x2, waiting for transfers between devices, shift(): return lax.ppermute(value, AXES, pairs)  3.51 us
    ppermute x2, starting transfers between devices, shift(): return lax.ppermute(value, AXES, pairs)  2.57 us
    pallas_call x2, Pallas kernels, fetched(): pl.pallas_call(body, in_specs=[pl.BlockSpec(memory_space=pltpu.HBM)] * co...  2.48 us
  transfers between devices with their start and end apart: 36, of which 21 were waited for; matrix products, arithmetic and copies ran while one was open for 0% of the time, Pallas kernels for 15%

profile of v14, /device:TPU:0, one launch (start us, length us, event | category | flops | bytes accessed | tf_op | source)
XLA Modules:
  0.0 97.2 jit_solution(319221255593974637)
XLA Ops:
  0.6 1.3 %shard_map.217 = (f32[64,512]{1,0:T(8,128)S(1)}, f32[64,128]{1,0:T(8,128)S(1)}) custom-call(s32[1,64]{1,0:T(1,128)} %bitcast.87, f32[1,512]{1,0:T(1,128)} %bitcast.86, f32[1,512]{1,0:T(1,128)} %refs_2_.1, f32[1,512]{1,0:T(1,128)} %refs_3_.1, f32[64,512]{1,0:T(8,128)} %bitcast.74, f32[64,512]{1,0:T(8,128)} %bitcast.76, f32[64,512]{1,0:T(8,128)} %bitcast.78), custom_call_target="tpu_custom_call" | custom-call | tf_op jit(solution)/shard_map/pallas_call | solution.py:195
  2.0 3.0 %collective-permute-start = (f32[64,512]{1,0:T(8,128)S(1)}, f32[64,512]{1,0:T(8,128)S(1)}, u32[]{:S(2)}, u32[]{:S(2)}) collective-permute-start(f32[64,512]{1,0:T(8,128)S(1)} %get-tuple-element.71.refs_0_), channel_id=1, source_target_pairs={{0,2},{1,3},{2,0},{3,1},{4,6},{5,7},{6,4},{7,5},{8,10},{9,11},{10,... | collective-permute-start | bytes 393224 | tf_op jit(solution)/shard_map/ppermute | solution.py:394
  5.0 4.1 %shard_map.218.refs_3_.refs_1_ = f32[512,5120]{1,0:T(8,128)S(1)} custom-call(f32[512,2048]{1,0:T(8,128)} %bitcast.63, f32[512,1536]{1,0:T(8,128)} %bitcast.58, f32[512,1536]{1,0:T(8,128)} %bitcast.67), custom_call_target="tpu_custom_call" | custom-call | tf_op jit(solution)/shard_map/pallas_call | solution.py:136
  9.7 1.2 %shard_map.219.refs_2_ = f32[64,512]{1,0:T(8,128)S(1)} custom-call(f32[64,512]{1,0:T(8,128)S(1)} %get-tuple-element.71.refs_0_, f32[64,512]{1,0:T(8,128)S(1)} %collective-permute-done.2.refs_1_, f32[64,512]{1,0:T(8,128)S(1)} %collective-permute-done.refs_2_, f32[512,5120]{1,0:T(8,128)S(1)} %shard_map.218.refs_3_.refs_1_), custom_call_target="tpu_custom_call" | custom-call | bytes 4194304 | tf_op jit(solution)/shard_map/pallas_call | solution.py:98
  10.8 1.6 %shard_map.220 = (f32[2,32,1536]{2,1,0:T(8,128)S(1)}, f32[2,32,1536]{2,1,0:T(8,128)S(1)}) custom-call(f32[64,512]{1,0:T(8,128)S(1)} %collective-permute-done.1.refs_0_, f32[512,5120]{1,0:T(8,128)S(1)} %shard_map.218.refs_3_.refs_1_, f32[64,512]{1,0:T(8,128)S(1)} %shard_map.219.refs_2_), custom_call_target="tpu_custom_call" | custom-call | tf_op jit(solution)/shard_map/pallas_call | solution.py:98
  12.6 1.6 %collective-permute-done.3.refs_1_ = f32[2,32,1536]{2,1,0:T(8,128)S(1)} collective-permute-done((f32[2,32,1536]{2,1,0:T(8,128)S(1)}, f32[2,32,1536]{2,1,0:T(8,128)S(1)}, u32[]{:S(2)}, u32[]{:S(2)}) %collective-permute-start.3) | collective-permute-done | bytes 393248 | tf_op jit(solution)/shard_map/ppermute | solution.py:394
  14.2 1.3 %collective-permute-start.6 = (f32[32,768]{1,0:T(8,128)S(1)}, f32[32,768]{1,0:T(8,128)S(1)}, u32[]{:S(2)}, u32[]{:S(2)}) collective-permute-start(f32[32,768]{1,0:T(8,128)S(1)} %get-tuple-element.80), channel_id=1, source_target_pairs={{4,0},{5,1},{6,2},{7,3},{8,4},{9,5},{10,6},{11,7},{12,8},{13,9},{1... | collective-permute-start | bytes 294920 | tf_op jit(solution)/shard_map/ppermute | solution.py:440
  16.3 1.3 %collective-permute-start.8 = (f32[32,768]{1,0:T(8,128)S(1)}, f32[32,768]{1,0:T(8,128)S(1)}, u32[]{:S(2)}, u32[]{:S(2)}) collective-permute-start(f32[32,768]{1,0:T(8,128)S(1)} %get-tuple-element.82), channel_id=1, source_target_pairs={{4,2},{5,3},{6,0},{7,1},{8,6},{9,7},{10,4},{11,5},{12,10},{13,11},... | collective-permute-start | bytes 294920 | tf_op jit(solution)/shard_map/ppermute | solution.py:440
  17.8 1.1 %shard_map.223 = (f32[32,384]{1,0:T(8,128)S(1)}, f32[32,384]{1,0:T(8,128)S(1)}) custom-call(f32[1,384]{1,0:T(1,128)} %refs_0_.1, f32[1,384]{1,0:T(1,128)} %refs_1_.1, f32[64,384]{1,0:T(8,128)} %bitcast.80, f32[64,384]{1,0:T(8,128)} %bitcast.82, f32[64,384]{1,0:T(8,128)} %bitcast.84, f32[64,128]{1,0:T(8,128)S(1)} %get-tuple-element.74.refs_5_), custom_call_target="tpu_custom_call" | custom-call | tf_op jit(solution)/shard_map/pallas_call | solution.py:195
  19.4 0.9 collective-permute-done.4.refs_1_
  21.0 3.2 %collective-permute-done.8.refs_5_ = f32[32,768]{1,0:T(8,128)S(1)} collective-permute-done((f32[32,768]{1,0:T(8,128)S(1)}, f32[32,768]{1,0:T(8,128)S(1)}, u32[]{:S(2)}, u32[]{:S(2)}) %collective-permute-start.8) | collective-permute-done | bytes 98336 | tf_op jit(solution)/shard_map/ppermute | solution.py:440
  24.3 2.2 %collective-permute-start.11 = (f32[32,768]{1,0:T(8,128)S(1)}, f32[32,768]{1,0:T(8,128)S(1)}, u32[]{:S(2)}, u32[]{:S(2)}) collective-permute-start(f32[32,768]{1,0:T(8,128)S(1)} %shard_map.224.refs_4_.refs_5_), channel_id=1, source_target_pairs={{0,4},{1,5},{2,6},{3,7},{4,0},{5,1},{6,2},{7,3},{8,12},{9,13},{10,... | collective-permute-start | bytes 294920 | tf_op jit(solution)/shard_map/ppermute | solution.py:394
  27.4 2.6 %collective-permute-done.11.refs_0_ = f32[32,768]{1,0:T(8,128)S(1)} collective-permute-done((f32[32,768]{1,0:T(8,128)S(1)}, f32[32,768]{1,0:T(8,128)S(1)}, u32[]{:S(2)}, u32[]{:S(2)}) %collective-permute-start.11) | collective-permute-done | bytes 98336 | tf_op jit(solution)/shard_map/ppermute | solution.py:394
  30.0 2.8 %collective-permute-done.9.refs_0_ = f32[32,768]{1,0:T(8,128)S(1)} collective-permute-done((f32[32,768]{1,0:T(8,128)S(1)}, f32[32,768]{1,0:T(8,128)S(1)}, u32[]{:S(2)}, u32[]{:S(2)}) %collective-permute-start.9) | collective-permute-done | bytes 98336 | tf_op jit(solution)/shard_map/ppermute | solution.py:394
  32.9 0.9 collective-permute-start.14
  33.8 1.2 %collective-permute-start.12 = (f32[32,768]{1,0:T(8,128)S(1)}, f32[32,768]{1,0:T(8,128)S(1)}, u32[]{:S(2)}, u32[]{:S(2)}) collective-permute-start(f32[32,768]{1,0:T(8,128)S(1)} %shard_map.226.refs_5_), channel_id=1, source_target_pairs={{0,2},{1,3},{2,0},{3,1},{4,10},{5,11},{6,8},{7,9},{8,6},{9,7},{10,... | collective-permute-start | bytes 294920 | tf_op jit(solution)/shard_map/ppermute | solution.py:394
  35.0 3.6 %collective-permute-done.14.refs_0_ = f32[32,768]{1,0:T(8,128)S(1)} collective-permute-done((f32[32,768]{1,0:T(8,128)S(1)}, f32[32,768]{1,0:T(8,128)S(1)}, u32[]{:S(2)}, u32[]{:S(2)}) %collective-permute-start.14) | collective-permute-done | bytes 98336 | tf_op jit(solution)/shard_map/ppermute | solution.py:394
  38.6 1.7 %collective-permute-done.12.refs_0_ = f32[32,768]{1,0:T(8,128)S(1)} collective-permute-done((f32[32,768]{1,0:T(8,128)S(1)}, f32[32,768]{1,0:T(8,128)S(1)}, u32[]{:S(2)}, u32[]{:S(2)}) %collective-permute-start.12) | collective-permute-done | bytes 98336 | tf_op jit(solution)/shard_map/ppermute | solution.py:394
  40.5 2.7 %collective-permute-start.17 = (f32[32,768]{1,0:T(8,128)S(1)}, f32[32,768]{1,0:T(8,128)S(1)}, u32[]{:S(2)}, u32[]{:S(2)}) collective-permute-start(f32[32,768]{1,0:T(8,128)S(1)} %shard_map.228.refs_5_), channel_id=1, source_target_pairs={{0,4},{1,5},{2,6},{3,7},{4,0},{5,1},{6,2},{7,3},{8,12},{9,13},{10,... | collective-permute-start | bytes 294920 | tf_op jit(solution)/shard_map/ppermute | solution.py:394
  44.0 2.6 %collective-permute-done.17.refs_0_ = f32[32,768]{1,0:T(8,128)S(1)} collective-permute-done((f32[32,768]{1,0:T(8,128)S(1)}, f32[32,768]{1,0:T(8,128)S(1)}, u32[]{:S(2)}, u32[]{:S(2)}) %collective-permute-start.17) | collective-permute-done | bytes 98336 | tf_op jit(solution)/shard_map/ppermute | solution.py:394
  46.5 2.8 %collective-permute-done.15.refs_0_ = f32[32,768]{1,0:T(8,128)S(1)} collective-permute-done((f32[32,768]{1,0:T(8,128)S(1)}, f32[32,768]{1,0:T(8,128)S(1)}, u32[]{:S(2)}, u32[]{:S(2)}) %collective-permute-start.15) | collective-permute-done | bytes 98336 | tf_op jit(solution)/shard_map/ppermute | solution.py:394
  49.4 0.9 collective-permute-start.18
  51.1 2.9 %collective-permute-done.18.refs_0_ = f32[32,768]{1,0:T(8,128)S(1)} collective-permute-done((f32[32,768]{1,0:T(8,128)S(1)}, f32[32,768]{1,0:T(8,128)S(1)}, u32[]{:S(2)}, u32[]{:S(2)}) %collective-permute-start.18) | collective-permute-done | bytes 98336 | tf_op jit(solution)/shard_map/ppermute | solution.py:394
  54.1 0.8 shard_map.232.refs_4_.refs_5_
  55.0 1.8 %collective-permute-start.21 = (f32[32,768]{1,0:T(8,128)S(1)}, f32[32,768]{1,0:T(8,128)S(1)}, u32[]{:S(2)}, u32[]{:S(2)}) collective-permute-start(f32[32,768]{1,0:T(8,128)S(1)} %shard_map.232.refs_4_.refs_5_), channel_id=1, source_target_pairs={{0,4},{1,5},{2,6},{3,7},{4,0},{5,1},{6,2},{7,3},{8,12},{9,13},{10,... | collective-permute-start | bytes 294920 | tf_op jit(solution)/shard_map/ppermute | solution.py:394
  57.4 3.3 %collective-permute-done.21.refs_0_ = f32[32,768]{1,0:T(8,128)S(1)} collective-permute-done((f32[32,768]{1,0:T(8,128)S(1)}, f32[32,768]{1,0:T(8,128)S(1)}, u32[]{:S(2)}, u32[]{:S(2)}) %collective-permute-start.21) | collective-permute-done | bytes 98336 | tf_op jit(solution)/shard_map/ppermute | solution.py:394
  60.7 1.9 %collective-permute-done.19.refs_0_ = f32[32,768]{1,0:T(8,128)S(1)} collective-permute-done((f32[32,768]{1,0:T(8,128)S(1)}, f32[32,768]{1,0:T(8,128)S(1)}, u32[]{:S(2)}, u32[]{:S(2)}) %collective-permute-start.19) | collective-permute-done | bytes 98336 | tf_op jit(solution)/shard_map/ppermute | solution.py:394
  62.9 1.1 %collective-permute-start.24 = (f32[32,768]{1,0:T(8,128)S(1)}, f32[32,768]{1,0:T(8,128)S(1)}, u32[]{:S(2)}, u32[]{:S(2)}) collective-permute-start(f32[32,768]{1,0:T(8,128)S(1)} %shard_map.234.refs_5_), channel_id=1, source_target_pairs={{0,2},{1,3},{2,0},{3,1},{4,8},{5,9},{6,10},{7,11},{8,4},{9,5},{10,... | collective-permute-start | bytes 294920 | tf_op jit(solution)/shard_map/ppermute | solution.py:394
  64.0 0.9 collective-permute-start.22
  64.9 3.6 %collective-permute-done.24.refs_0_ = f32[32,768]{1,0:T(8,128)S(1)} collective-permute-done((f32[32,768]{1,0:T(8,128)S(1)}, f32[32,768]{1,0:T(8,128)S(1)}, u32[]{:S(2)}, u32[]{:S(2)}) %collective-permute-start.24) | collective-permute-done | bytes 98336 | tf_op jit(solution)/shard_map/ppermute | solution.py:394
  68.5 1.7 %collective-permute-done.22.refs_0_ = f32[32,768]{1,0:T(8,128)S(1)} collective-permute-done((f32[32,768]{1,0:T(8,128)S(1)}, f32[32,768]{1,0:T(8,128)S(1)}, u32[]{:S(2)}, u32[]{:S(2)}) %collective-permute-start.22) | collective-permute-done | bytes 98336 | tf_op jit(solution)/shard_map/ppermute | solution.py:394
  70.2 4.0 %collective-permute-start.26 = (f32[32,768]{1,0:T(8,128)S(1)}, f32[32,768]{1,0:T(8,128)S(1)}, u32[]{:S(2)}, u32[]{:S(2)}) collective-permute-start(f32[32,768]{1,0:T(8,128)S(1)} %shard_map.236.refs_0_.refs_5_), channel_id=1, source_target_pairs={{0,4},{1,5},{2,6},{3,7},{4,0},{5,1},{6,2},{7,3},{8,12},{9,13},{10,... | collective-permute-start | bytes 294920 | tf_op jit(solution)/shard_map/ppermute | solution.py:394
  74.7 1.0 %shard_map.237.refs_3_ = f32[32,1024]{1,0:T(8,128)S(1)} custom-call(f32[32,768]{1,0:T(8,128)S(1)} %shard_map.236.refs_0_.refs_5_, f32[512,1536]{1,0:T(8,128)S(1)} %bitcast.60, f32[512,1536]{1,0:T(8,128)S(1)} %collective-permute-done.20.refs_2_), custom_call_target="tpu_custom_call" | custom-call | bytes 4194304 | tf_op jit(solution)/shard_map/pallas_call | solution.py:98
  75.7 1.4 %collective-permute-done.26.refs_0_ = f32[32,768]{1,0:T(8,128)S(1)} collective-permute-done((f32[32,768]{1,0:T(8,128)S(1)}, f32[32,768]{1,0:T(8,128)S(1)}, u32[]{:S(2)}, u32[]{:S(2)}) %collective-permute-start.26) | collective-permute-done | bytes 98336 | tf_op jit(solution)/shard_map/ppermute | solution.py:394
  78.0 1.2 %collective-permute-start.30 = (f32[32,768]{1,0:T(8,128)S(1)}, f32[32,768]{1,0:T(8,128)S(1)}, u32[]{:S(2)}, u32[]{:S(2)}) collective-permute-start(f32[32,768]{1,0:T(8,128)S(1)} %shard_map.236.refs_0_.refs_5_), channel_id=1, source_target_pairs={{0,2},{1,3},{2,0},{3,1},{4,10},{5,11},{6,8},{7,9},{8,6},{9,7},{10,... | collective-permute-start | bytes 294920 | tf_op jit(solution)/shard_map/ppermute | solution.py:394
  80.0 0.9 shard_map.239.refs_0_
  80.9 0.9 collective-permute-start.32
  81.8 1.3 %collective-permute-start.31 = (f32[32,768]{1,0:T(8,128)S(1)}, f32[32,768]{1,0:T(8,128)S(1)}, u32[]{:S(2)}, u32[]{:S(2)}) collective-permute-start(f32[32,768]{1,0:T(8,128)S(1)} %shard_map.239.refs_0_), channel_id=1, source_target_pairs={{0,4},{1,5},{2,6},{3,7},{4,0},{5,1},{6,2},{7,3},{8,12},{9,13},{10,... | collective-permute-start | bytes 294920 | tf_op jit(solution)/shard_map/ppermute | solution.py:394
  83.1 1.3 %collective-permute-start.27 = (f32[32,768]{1,0:T(8,128)S(1)}, f32[32,768]{1,0:T(8,128)S(1)}, u32[]{:S(2)}, u32[]{:S(2)}) collective-permute-start(f32[32,768]{1,0:T(8,128)S(1)} %shard_map.239.refs_0_), channel_id=1, source_target_pairs={{0,6},{1,7},{2,4},{3,5},{4,2},{5,3},{6,0},{7,1},{8,14},{9,15},{10,... | collective-permute-start | bytes 294920 | tf_op jit(solution)/shard_map/ppermute | solution.py:394
  84.5 1.2 %collective-permute-done.30.refs_3_ = f32[32,768]{1,0:T(8,128)S(1)} collective-permute-done((f32[32,768]{1,0:T(8,128)S(1)}, f32[32,768]{1,0:T(8,128)S(1)}, u32[]{:S(2)}, u32[]{:S(2)}) %collective-permute-start.30) | collective-permute-done | bytes 98336 | tf_op jit(solution)/shard_map/ppermute | solution.py:394
  85.6 1.0 %shard_map.240.refs_3_ = f32[32,1024]{1,0:T(8,128)S(1)} custom-call(f32[32,768]{1,0:T(8,128)S(1)} %shard_map.239.refs_0_, f32[512,1536]{1,0:T(8,128)S(1)} %bitcast.61, f32[512,1536]{1,0:T(8,128)S(1)} %collective-permute-done.20.refs_2_, f32[32,1024]{1,0:T(8,128)S(1)} %shard_map.237.refs_3_), custom_call_target="tpu_custom_call" | custom-call | bytes 4194304 | tf_op jit(solution)/shard_map/pallas_call | solution.py:98
  86.7 1.1 %shard_map.241.refs_4_ = f32[32,1024]{1,0:T(8,128)S(1)} custom-call(f32[32,768]{1,0:T(8,128)S(1)} %collective-permute-done.32.refs_0_, f32[512,1536]{1,0:T(8,128)S(1)} %bitcast.62, f32[512,1536]{1,0:T(8,128)S(1)} %collective-permute-done.20.refs_2_, f32[32,1024]{1,0:T(8,128)S(1)} %shard_map.240.refs_3_), custom_call_target="tpu_custom_call" | custom-call | bytes 4194304 | tf_op jit(solution)/shard_map/pallas_call | solution.py:98
  87.8 0.8 collective-permute-done.27.refs_2_
  88.7 0.9 collective-permute-start.33
  89.7 1.2 %collective-permute-done.34.refs_1_ = f32[32,384]{1,0:T(8,128)S(1)} collective-permute-done((f32[32,384]{1,0:T(8,128)S(1)}, f32[32,384]{1,0:T(8,128)S(1)}, u32[]{:S(2)}, u32[]{:S(2)}) %collective-permute-start.34) | collective-permute-done | bytes 49184 | tf_op jit(solution)/shard_map/ppermute | solution.py:394
  91.7 1.4 %shard_map.246.refs_3_ = f32[32,1024]{1,0:T(8,128)S(1)} custom-call(f32[32,1024]{1,0:T(8,128)S(1)} %shard_map.243.refs_0_, f32[512,2048]{1,0:T(8,128)S(1)} %bitcast.65, f32[512,2048]{1,0:T(8,128)S(1)} %collective-permute-done.28.refs_2_), custom_call_target="tpu_custom_call" | custom-call | bytes 4194304 | tf_op jit(solution)/shard_map/pallas_call | solution.py:98
  93.8 1.4 %shard_map.247 = (f32[32,512]{1,0:T(8,128)S(1)}, f32[32,512]{1,0:T(8,128)S(1)}) custom-call(f32[32,1024]{1,0:T(8,128)S(1)} %collective-permute-done.33.refs_0_, f32[512,2048]{1,0:T(8,128)S(1)} %bitcast.66, f32[512,2048]{1,0:T(8,128)S(1)} %collective-permute-done.28.refs_2_, f32[32,1024]{1,0:T(8,128)S(1)} %shard_map.246.refs_3_), custom_call_target="tpu_custom_call" | custom-call | tf_op jit(solution)/shard_map/pallas_call | solution.py:98
  95.2 1.2 %collective-permute-done.35.refs_1_ = f32[32,512]{1,0:T(8,128)S(1)} collective-permute-done((f32[32,512]{1,0:T(8,128)S(1)}, f32[32,512]{1,0:T(8,128)S(1)}, u32[]{:S(2)}, u32[]{:S(2)}) %collective-permute-start.35) | collective-permute-done | bytes 65568 | tf_op jit(solution)/shard_map/ppermute | solution.py:394
  (80 shorter events, 11.3 us)
Async XLA Ops:
  2.0 7.1 %collective-permute-start = (f32[64,512]{1,0:T(8,128)S(1)}, f32[64,512]{1,0:T(8,128)S(1)}, u32[]{:S(2)}, u32[]{:S(2)}) collective-permute-start(f32[64,512]{1,0:T(8,128)S(1)} %get-tuple-element.71.refs_0_), channel_id=1, source_target_pairs={{0,2},{1,3},{2,0},{3,1},{4,6},{5,7},{6,4},{7,5},{8,10},{9,11},{10,... | collective-permute-start | bytes 393224 | tf_op jit(solution)/shard_map/ppermute | solution.py:394
  5.0 4.7 %collective-permute-start.2 = (f32[64,512]{1,0:T(8,128)S(1)}, f32[64,512]{1,0:T(8,128)S(1)}, u32[]{:S(2)}, u32[]{:S(2)}) collective-permute-start(f32[64,512]{1,0:T(8,128)S(1)} %get-tuple-element.71.refs_0_), channel_id=1, source_target_pairs={{0,1},{1,0},{2,3},{3,2},{4,5},{5,4},{6,7},{7,6},{8,9},{9,8},{10,11... | collective-permute-start | bytes 393224 | tf_op jit(solution)/shard_map/ppermute | solution.py:394
  9.1 1.8 %collective-permute-start.1 = (f32[64,512]{1,0:T(8,128)S(1)}, f32[64,512]{1,0:T(8,128)S(1)}, u32[]{:S(2)}, u32[]{:S(2)}) collective-permute-start(f32[64,512]{1,0:T(8,128)S(1)} %collective-permute-done.refs_2_), channel_id=1, source_target_pairs={{0,1},{1,0},{2,3},{3,2},{4,5},{5,4},{6,7},{7,6},{8,9},{9,8},{10,11... | collective-permute-start | bytes 393224 | tf_op jit(solution)/shard_map/ppermute | solution.py:394
  10.8 9.5 %copy-start = (f32[1,384,1536]{2,1,0:T(8,128)S(1)}, f32[1,384,1536]{2,1,0:T(8,128)}, u32[]{:S(2)}) copy-start(f32[1,384,1536]{2,1,0:T(8,128)} %param.33) | copy-start | bytes 7077892
  10.8 13.4 %copy-start.5 = (f32[1,384,1536]{2,1,0:T(8,128)S(1)}, f32[1,384,1536]{2,1,0:T(8,128)}, u32[]{:S(2)}) copy-start(f32[1,384,1536]{2,1,0:T(8,128)} %param.34) | copy-start | bytes 7077892
  12.4 1.8 %collective-permute-start.3 = (f32[2,32,1536]{2,1,0:T(8,128)S(1)}, f32[2,32,1536]{2,1,0:T(8,128)S(1)}, u32[]{:S(2)}, u32[]{:S(2)}) collective-permute-start(f32[2,32,1536]{2,1,0:T(8,128)S(1)} %get-tuple-element.69), channel_id=1, source_target_pairs={{0,1},{1,0},{2,3},{3,2},{4,5},{5,4},{6,7},{7,6},{8,9},{9,8},{10,11... | collective-permute-start | bytes 1179656 | tf_op jit(solution)/shard_map/ppermute | solution.py:394
  14.2 6.7 %collective-permute-start.6 = (f32[32,768]{1,0:T(8,128)S(1)}, f32[32,768]{1,0:T(8,128)S(1)}, u32[]{:S(2)}, u32[]{:S(2)}) collective-permute-start(f32[32,768]{1,0:T(8,128)S(1)} %get-tuple-element.80), channel_id=1, source_target_pairs={{4,0},{5,1},{6,2},{7,3},{8,4},{9,5},{10,6},{11,7},{12,8},{13,9},{1... | collective-permute-start | bytes 294920 | tf_op jit(solution)/shard_map/ppermute | solution.py:440
  15.5 5.4 %collective-permute-start.7 = (f32[32,768]{1,0:T(8,128)S(1)}, f32[32,768]{1,0:T(8,128)S(1)}, u32[]{:S(2)}, u32[]{:S(2)}) collective-permute-start(f32[32,768]{1,0:T(8,128)S(1)} %get-tuple-element.81), channel_id=1, source_target_pairs={{0,2},{1,3},{2,0},{3,1},{4,6},{5,7},{6,4},{7,5},{8,10},{9,11},{10,... | collective-permute-start | bytes 294920 | tf_op jit(solution)/shard_map/ppermute | solution.py:394
  16.3 7.9 %collective-permute-start.8 = (f32[32,768]{1,0:T(8,128)S(1)}, f32[32,768]{1,0:T(8,128)S(1)}, u32[]{:S(2)}, u32[]{:S(2)}) collective-permute-start(f32[32,768]{1,0:T(8,128)S(1)} %get-tuple-element.82), channel_id=1, source_target_pairs={{4,2},{5,3},{6,0},{7,1},{8,6},{9,7},{10,4},{11,5},{12,10},{13,11},... | collective-permute-start | bytes 294920 | tf_op jit(solution)/shard_map/ppermute | solution.py:440
  17.7 3.0 %collective-permute-start.5 = (f32[32,512]{1,0:T(8,128)S(1)}, f32[32,512]{1,0:T(8,128)S(1)}, u32[]{:S(2)}, u32[]{:S(2)}) collective-permute-start(f32[32,512]{1,0:T(8,128)S(1)} %get-tuple-element.76), channel_id=1, source_target_pairs={{0,1},{1,0},{2,3},{3,2},{4,5},{5,4},{6,7},{7,6},{8,9},{9,8},{10,11... | collective-permute-start | bytes 196616 | tf_op jit(solution)/shard_map/ppermute | solution.py:394
  19.0 1.4 %collective-permute-start.4 = (f32[32,384]{1,0:T(8,128)S(1)}, f32[32,384]{1,0:T(8,128)S(1)}, u32[]{:S(2)}, u32[]{:S(2)}) collective-permute-start(f32[32,384]{1,0:T(8,128)S(1)} %get-tuple-element.75), channel_id=1, source_target_pairs={{0,1},{1,0},{2,3},{3,2},{4,5},{5,4},{6,7},{7,6},{8,9},{9,8},{10,11... | collective-permute-start | bytes 147464 | tf_op jit(solution)/shard_map/ppermute | solution.py:394
  20.3 9.6 %collective-permute-start.10 = (f32[384,1536]{1,0:T(8,128)S(1)}, f32[384,1536]{1,0:T(8,128)S(1)}, u32[]{:S(2)}, u32[]{:S(2)}) collective-permute-start(f32[384,1536]{1,0:T(8,128)S(1)} %bitcast.44), channel_id=1, source_target_pairs={{0,1},{1,0},{2,3},{3,2},{4,5},{5,4},{6,7},{7,6},{8,9},{9,8},{10,11... | collective-permute-start | bytes 7077896 | tf_op jit(solution)/shard_map/ppermute | solution.py:394
  24.2 8.6 %collective-permute-start.13 = (f32[384,1536]{1,0:T(8,128)S(1)}, f32[384,1536]{1,0:T(8,128)S(1)}, u32[]{:S(2)}, u32[]{:S(2)}) collective-permute-start(f32[384,1536]{1,0:T(8,128)S(1)} %bitcast.71), channel_id=1, source_target_pairs={{0,1},{1,0},{2,3},{3,2},{4,5},{5,4},{6,7},{7,6},{8,9},{9,8},{10,11... | collective-permute-start | bytes 7077896 | tf_op jit(solution)/shard_map/ppermute | solution.py:394
  24.3 5.6 %collective-permute-start.11 = (f32[32,768]{1,0:T(8,128)S(1)}, f32[32,768]{1,0:T(8,128)S(1)}, u32[]{:S(2)}, u32[]{:S(2)}) collective-permute-start(f32[32,768]{1,0:T(8,128)S(1)} %shard_map.224.refs_4_.refs_5_), channel_id=1, source_target_pairs={{0,4},{1,5},{2,6},{3,7},{4,0},{5,1},{6,2},{7,3},{8,12},{9,13},{10,... | collective-permute-start | bytes 294920 | tf_op jit(solution)/shard_map/ppermute | solution.py:394
  26.6 6.2 %collective-permute-start.9 = (f32[32,768]{1,0:T(8,128)S(1)}, f32[32,768]{1,0:T(8,128)S(1)}, u32[]{:S(2)}, u32[]{:S(2)}) collective-permute-start(f32[32,768]{1,0:T(8,128)S(1)} %shard_map.224.refs_4_.refs_5_), channel_id=1, source_target_pairs={{0,6},{1,7},{2,4},{3,5},{4,2},{5,3},{6,0},{7,1},{8,14},{9,15},{10,... | collective-permute-start | bytes 294920 | tf_op jit(solution)/shard_map/ppermute | solution.py:394
  30.0 2.9 %copy-start.1 = (f32[1,384,1536]{2,1,0:T(8,128)S(1)}, f32[1,384,1536]{2,1,0:T(8,128)}, u32[]{:S(2)}) copy-start(f32[1,384,1536]{2,1,0:T(8,128)} %param.35) | copy-start | bytes 7077892
  32.8 7.4 %collective-permute-start.16 = (f32[384,1536]{1,0:T(8,128)S(1)}, f32[384,1536]{1,0:T(8,128)S(1)}, u32[]{:S(2)}, u32[]{:S(2)}) collective-permute-start(f32[384,1536]{1,0:T(8,128)S(1)} %bitcast.51), channel_id=1, source_target_pairs={{0,1},{1,0},{2,3},{3,2},{4,5},{5,4},{6,7},{7,6},{8,9},{9,8},{10,11... | collective-permute-start | bytes 7077896 | tf_op jit(solution)/shard_map/ppermute | solution.py:394
  32.9 5.7 %collective-permute-start.14 = (f32[32,768]{1,0:T(8,128)S(1)}, f32[32,768]{1,0:T(8,128)S(1)}, u32[]{:S(2)}, u32[]{:S(2)}) collective-permute-start(f32[32,768]{1,0:T(8,128)S(1)} %shard_map.226.refs_5_), channel_id=1, source_target_pairs={{0,2},{1,3},{2,0},{3,1},{4,8},{5,9},{6,10},{7,11},{8,4},{9,5},{10,... | collective-permute-start | bytes 294920 | tf_op jit(solution)/shard_map/ppermute | solution.py:394
  33.8 6.4 %collective-permute-start.12 = (f32[32,768]{1,0:T(8,128)S(1)}, f32[32,768]{1,0:T(8,128)S(1)}, u32[]{:S(2)}, u32[]{:S(2)}) collective-permute-start(f32[32,768]{1,0:T(8,128)S(1)} %shard_map.226.refs_5_), channel_id=1, source_target_pairs={{0,2},{1,3},{2,0},{3,1},{4,10},{5,11},{6,8},{7,9},{8,6},{9,7},{10,... | collective-permute-start | bytes 294920 | tf_op jit(solution)/shard_map/ppermute | solution.py:394
  38.6 1.9 %copy-start.2 = (f32[1,512,1536]{2,1,0:T(8,128)S(1)}, f32[1,512,1536]{2,1,0:T(8,128)}, u32[]{:S(2)}) copy-start(f32[1,512,1536]{2,1,0:T(8,128)} %param.32) | copy-start | bytes 9437188
  40.5 14.5 %collective-permute-start.20 = (f32[512,1536]{1,0:T(8,128)S(1)}, f32[512,1536]{1,0:T(8,128)S(1)}, u32[]{:S(2)}, u32[]{:S(2)}) collective-permute-start(f32[512,1536]{1,0:T(8,128)S(1)} %bitcast.59), channel_id=1, source_target_pairs={{0,1},{1,0},{2,3},{3,2},{4,5},{5,4},{6,7},{7,6},{8,9},{9,8},{10,11... | collective-permute-start | bytes 9437192 | tf_op jit(solution)/shard_map/ppermute | solution.py:394
  40.5 6.1 %collective-permute-start.17 = (f32[32,768]{1,0:T(8,128)S(1)}, f32[32,768]{1,0:T(8,128)S(1)}, u32[]{:S(2)}, u32[]{:S(2)}) collective-permute-start(f32[32,768]{1,0:T(8,128)S(1)} %shard_map.228.refs_5_), channel_id=1, source_target_pairs={{0,4},{1,5},{2,6},{3,7},{4,0},{5,1},{6,2},{7,3},{8,12},{9,13},{10,... | collective-permute-start | bytes 294920 | tf_op jit(solution)/shard_map/ppermute | solution.py:394
  43.2 6.2 %collective-permute-start.15 = (f32[32,768]{1,0:T(8,128)S(1)}, f32[32,768]{1,0:T(8,128)S(1)}, u32[]{:S(2)}, u32[]{:S(2)}) collective-permute-start(f32[32,768]{1,0:T(8,128)S(1)} %shard_map.228.refs_5_), channel_id=1, source_target_pairs={{0,6},{1,7},{2,4},{3,5},{4,2},{5,3},{6,0},{7,1},{8,14},{9,15},{10,... | collective-permute-start | bytes 294920 | tf_op jit(solution)/shard_map/ppermute | solution.py:394
  49.4 4.7 %collective-permute-start.18 = (f32[32,768]{1,0:T(8,128)S(1)}, f32[32,768]{1,0:T(8,128)S(1)}, u32[]{:S(2)}, u32[]{:S(2)}) collective-permute-start(f32[32,768]{1,0:T(8,128)S(1)} %shard_map.230.refs_0_), channel_id=1, source_target_pairs={{0,2},{1,3},{2,0},{3,1},{4,6},{5,7},{6,4},{7,5},{8,10},{9,11},{10,... | collective-permute-start | bytes 294920 | tf_op jit(solution)/shard_map/ppermute | solution.py:394
  51.1 3.8 %copy-start.4 = (f32[1,512,1536]{2,1,0:T(8,128)S(1)}, f32[1,512,1536]{2,1,0:T(8,128)}, u32[]{:S(2)}) copy-start(f32[1,512,1536]{2,1,0:T(8,128)} %param.31) | copy-start | bytes 9437188
  54.9 7.7 %collective-permute-start.23 = (f32[512,1536]{1,0:T(8,128)S(1)}, f32[512,1536]{1,0:T(8,128)S(1)}, u32[]{:S(2)}, u32[]{:S(2)}) collective-permute-start(f32[512,1536]{1,0:T(8,128)S(1)} %bitcast.68), channel_id=1, source_target_pairs={{0,1},{1,0},{2,3},{3,2},{4,5},{5,4},{6,7},{7,6},{8,9},{9,8},{10,11... | collective-permute-start | bytes 9437192 | tf_op jit(solution)/shard_map/ppermute | solution.py:394
  55.0 5.7 %collective-permute-start.21 = (f32[32,768]{1,0:T(8,128)S(1)}, f32[32,768]{1,0:T(8,128)S(1)}, u32[]{:S(2)}, u32[]{:S(2)}) collective-permute-start(f32[32,768]{1,0:T(8,128)S(1)} %shard_map.232.refs_4_.refs_5_), channel_id=1, source_target_pairs={{0,4},{1,5},{2,6},{3,7},{4,0},{5,1},{6,2},{7,3},{8,12},{9,13},{10,... | collective-permute-start | bytes 294920 | tf_op jit(solution)/shard_map/ppermute | solution.py:394
  56.8 5.8 %collective-permute-start.19 = (f32[32,768]{1,0:T(8,128)S(1)}, f32[32,768]{1,0:T(8,128)S(1)}, u32[]{:S(2)}, u32[]{:S(2)}) collective-permute-start(f32[32,768]{1,0:T(8,128)S(1)} %shard_map.232.refs_4_.refs_5_), channel_id=1, source_target_pairs={{0,6},{1,7},{2,4},{3,5},{4,2},{5,3},{6,0},{7,1},{8,14},{9,15},{10,... | collective-permute-start | bytes 294920 | tf_op jit(solution)/shard_map/ppermute | solution.py:394
  60.7 2.2 %copy-start.3 = (f32[1,512,2048]{2,1,0:T(8,128)S(1)}, f32[1,512,2048]{2,1,0:T(8,128)}, u32[]{:S(2)}) copy-start(f32[1,512,2048]{2,1,0:T(8,128)} %param.30) | copy-start | bytes 12582916
  62.9 25.8 %collective-permute-start.28 = (f32[512,2048]{1,0:T(8,128)S(1)}, f32[512,2048]{1,0:T(8,128)S(1)}, u32[]{:S(2)}, u32[]{:S(2)}) collective-permute-start(f32[512,2048]{1,0:T(8,128)S(1)} %bitcast.64), channel_id=1, source_target_pairs={{0,1},{1,0},{2,3},{3,2},{4,5},{5,4},{6,7},{7,6},{8,9},{9,8},{10,11... | collective-permute-start | bytes 12582920 | tf_op jit(solution)/shard_map/ppermute | solution.py:394
  62.9 5.6 %collective-permute-start.24 = (f32[32,768]{1,0:T(8,128)S(1)}, f32[32,768]{1,0:T(8,128)S(1)}, u32[]{:S(2)}, u32[]{:S(2)}) collective-permute-start(f32[32,768]{1,0:T(8,128)S(1)} %shard_map.234.refs_5_), channel_id=1, source_target_pairs={{0,2},{1,3},{2,0},{3,1},{4,8},{5,9},{6,10},{7,11},{8,4},{9,5},{10,... | collective-permute-start | bytes 294920 | tf_op jit(solution)/shard_map/ppermute | solution.py:394
  64.0 6.2 %collective-permute-start.22 = (f32[32,768]{1,0:T(8,128)S(1)}, f32[32,768]{1,0:T(8,128)S(1)}, u32[]{:S(2)}, u32[]{:S(2)}) collective-permute-start(f32[32,768]{1,0:T(8,128)S(1)} %shard_map.234.refs_5_), channel_id=1, source_target_pairs={{0,2},{1,3},{2,0},{3,1},{4,10},{5,11},{6,8},{7,9},{8,6},{9,7},{10,... | collective-permute-start | bytes 294920 | tf_op jit(solution)/shard_map/ppermute | solution.py:394
  70.2 7.0 %collective-permute-start.26 = (f32[32,768]{1,0:T(8,128)S(1)}, f32[32,768]{1,0:T(8,128)S(1)}, u32[]{:S(2)}, u32[]{:S(2)}) collective-permute-start(f32[32,768]{1,0:T(8,128)S(1)} %shard_map.236.refs_0_.refs_5_), channel_id=1, source_target_pairs={{0,4},{1,5},{2,6},{3,7},{4,0},{5,1},{6,2},{7,3},{8,12},{9,13},{10,... | collective-permute-start | bytes 294920 | tf_op jit(solution)/shard_map/ppermute | solution.py:394
  74.2 5.9 %collective-permute-start.25 = (f32[32,768]{1,0:T(8,128)S(1)}, f32[32,768]{1,0:T(8,128)S(1)}, u32[]{:S(2)}, u32[]{:S(2)}) collective-permute-start(f32[32,768]{1,0:T(8,128)S(1)} %shard_map.236.refs_0_.refs_5_), channel_id=1, source_target_pairs={{0,6},{1,7},{2,4},{3,5},{4,2},{5,3},{6,0},{7,1},{8,14},{9,15},{10,... | collective-permute-start | bytes 294920 | tf_op jit(solution)/shard_map/ppermute | solution.py:394
  77.2 6.0 %collective-permute-start.29 = (f32[32,768]{1,0:T(8,128)S(1)}, f32[32,768]{1,0:T(8,128)S(1)}, u32[]{:S(2)}, u32[]{:S(2)}) collective-permute-start(f32[32,768]{1,0:T(8,128)S(1)} %shard_map.236.refs_0_.refs_5_), channel_id=1, source_target_pairs={{0,2},{1,3},{2,0},{3,1},{4,8},{5,9},{6,10},{7,11},{8,4},{9,5},{10,... | collective-permute-start | bytes 294920 | tf_op jit(solution)/shard_map/ppermute | solution.py:394
  78.0 7.7 %collective-permute-start.30 = (f32[32,768]{1,0:T(8,128)S(1)}, f32[32,768]{1,0:T(8,128)S(1)}, u32[]{:S(2)}, u32[]{:S(2)}) collective-permute-start(f32[32,768]{1,0:T(8,128)S(1)} %shard_map.236.refs_0_.refs_5_), channel_id=1, source_target_pairs={{0,2},{1,3},{2,0},{3,1},{4,10},{5,11},{6,8},{7,9},{8,6},{9,7},{10,... | collective-permute-start | bytes 294920 | tf_op jit(solution)/shard_map/ppermute | solution.py:394
  80.9 5.8 %collective-permute-start.32 = (f32[32,768]{1,0:T(8,128)S(1)}, f32[32,768]{1,0:T(8,128)S(1)}, u32[]{:S(2)}, u32[]{:S(2)}) collective-permute-start(f32[32,768]{1,0:T(8,128)S(1)} %shard_map.239.refs_0_), channel_id=1, source_target_pairs={{0,2},{1,3},{2,0},{3,1},{4,6},{5,7},{6,4},{7,5},{8,10},{9,11},{10,... | collective-permute-start | bytes 294920 | tf_op jit(solution)/shard_map/ppermute | solution.py:394
  81.8 6.0 %collective-permute-start.31 = (f32[32,768]{1,0:T(8,128)S(1)}, f32[32,768]{1,0:T(8,128)S(1)}, u32[]{:S(2)}, u32[]{:S(2)}) collective-permute-start(f32[32,768]{1,0:T(8,128)S(1)} %shard_map.239.refs_0_), channel_id=1, source_target_pairs={{0,4},{1,5},{2,6},{3,7},{4,0},{5,1},{6,2},{7,3},{8,12},{9,13},{10,... | collective-permute-start | bytes 294920 | tf_op jit(solution)/shard_map/ppermute | solution.py:394
  83.1 5.5 %collective-permute-start.27 = (f32[32,768]{1,0:T(8,128)S(1)}, f32[32,768]{1,0:T(8,128)S(1)}, u32[]{:S(2)}, u32[]{:S(2)}) collective-permute-start(f32[32,768]{1,0:T(8,128)S(1)} %shard_map.239.refs_0_), channel_id=1, source_target_pairs={{0,6},{1,7},{2,4},{3,5},{4,2},{5,3},{6,0},{7,1},{8,14},{9,15},{10,... | collective-permute-start | bytes 294920 | tf_op jit(solution)/shard_map/ppermute | solution.py:394
  88.7 2.3 %copy-start.9 = (f32[1,384,64]{1,2,0:T(8,128)S(1)}, f32[1,384,64]{1,2,0:T(8,128)}, u32[]{:S(2)}) copy-start(f32[1,384,64]{1,2,0:T(8,128)} %param.27) | copy-start | bytes 294916
  88.7 2.3 %copy-start.10 = (f32[1,384,64]{1,2,0:T(8,128)S(1)}, f32[1,384,64]{1,2,0:T(8,128)}, u32[]{:S(2)}) copy-start(f32[1,384,64]{1,2,0:T(8,128)} %param.28) | copy-start | bytes 294916
  88.7 2.3 %copy-start.11 = (f32[1,384,64]{1,2,0:T(8,128)S(1)}, f32[1,384,64]{1,2,0:T(8,128)}, u32[]{:S(2)}) copy-start(f32[1,384,64]{1,2,0:T(8,128)} %param.29) | copy-start | bytes 294916
  88.7 5.0 %collective-permute-start.33 = (f32[32,1024]{1,0:T(8,128)S(1)}, f32[32,1024]{1,0:T(8,128)S(1)}, u32[]{:S(2)}, u32[]{:S(2)}) collective-permute-start(f32[32,1024]{1,0:T(8,128)S(1)} %shard_map.243.refs_0_), channel_id=1, source_target_pairs={{0,2},{1,3},{2,0},{3,1},{4,6},{5,7},{6,4},{7,5},{8,10},{9,11},{10,... | collective-permute-start | bytes 393224 | tf_op jit(solution)/shard_map/ppermute | solution.py:394
  89.7 1.3 %collective-permute-start.34 = (f32[32,384]{1,0:T(8,128)S(1)}, f32[32,384]{1,0:T(8,128)S(1)}, u32[]{:S(2)}, u32[]{:S(2)}) collective-permute-start(f32[32,384]{1,0:T(8,128)S(1)} %get-tuple-element.104), channel_id=1, source_target_pairs={{0,1},{1,0},{2,3},{3,2},{4,5},{5,4},{6,7},{7,6},{8,9},{9,8},{10,11... | collective-permute-start | bytes 147464 | tf_op jit(solution)/shard_map/ppermute | solution.py:394
  93.8 2.7 %copy-start.6 = (f32[1,512,64]{1,2,0:T(8,128)S(1)}, f32[1,512,64]{1,2,0:T(8,128)}, u32[]{:S(2)}) copy-start(f32[1,512,64]{1,2,0:T(8,128)} %param.24) | copy-start | bytes 393220
  93.8 2.7 %copy-start.7 = (f32[1,512,64]{1,2,0:T(8,128)S(1)}, f32[1,512,64]{1,2,0:T(8,128)}, u32[]{:S(2)}) copy-start(f32[1,512,64]{1,2,0:T(8,128)} %param.25) | copy-start | bytes 393220
  93.8 2.7 %copy-start.8 = (f32[1,512,64]{1,2,0:T(8,128)S(1)}, f32[1,512,64]{1,2,0:T(8,128)}, u32[]{:S(2)}) copy-start(f32[1,512,64]{1,2,0:T(8,128)} %param.26) | copy-start | bytes 393220
  95.1 1.3 %collective-permute-start.35 = (f32[32,512]{1,0:T(8,128)S(1)}, f32[32,512]{1,0:T(8,128)S(1)}, u32[]{:S(2)}, u32[]{:S(2)}) collective-permute-start(f32[32,512]{1,0:T(8,128)S(1)} %get-tuple-element.111), channel_id=1, source_target_pairs={{0,1},{1,0},{2,3},{3,2},{4,5},{5,4},{6,7},{7,6},{8,9},{9,8},{10,11... | collective-permute-start | bytes 196616 | tf_op jit(solution)/shard_map/ppermute | solution.py:394
